TPU v7x, 32 devices: a whole 2x2x4 slice. The times are simulated.
32 devices in a mesh: ctx: 8 (over z, y), uly: 4 (over x, core).
Axes of the slice: x: 2, y: 2, z: 4, core: 2. Of those that a mesh axis runs over, the one named last changes fastest.
Arguments:
- queries: bfloat16 [4096, 32, 128], P(('ctx', 'uly')), may hold values from -20 to 20
- keys: bfloat16 [4096, 8, 128], P(('ctx', 'uly')), may hold values from -20 to 20
- values: bfloat16 [4096, 8, 128], P(('ctx', 'uly')), may hold values from -6 to 6
- grad_out: bfloat16 [4096, 32, 128], P(('ctx', 'uly')), may hold values from -6 to 6
- doc_lengths: int32 [16], replicated, may hold values from 1 to 512, 4096 in all
Outputs:
- grad_queries: bfloat16 [4096, 32, 128], P(('ctx', 'uly'))
- grad_keys: bfloat16 [4096, 8, 128], P(('ctx', 'uly'))
- grad_values: bfloat16 [4096, 8, 128], P(('ctx', 'uly'))
Inputs may be any that keep to these rules, and one draw needn't show every extreme that they name: `doc_lengths`: positive lengths that sum to 4096; the longest document has exactly 512 tokens.
All inputs are finite; a program needn't handle non-finite values.
Results may differ from a plain program's by a relative error of at most 0.0069.
Values may be sent and summed in bfloat16 or wider, within the bound.
No kernel may reach another device: no remote copies, remote signals or barrier semaphores. Data moves between devices by JAX's collectives and lax.ppermute only.
A program may use at most 64 MiB of HBM per device.

v0:
```python
import jax
import jax.numpy as jnp
from jax import lax
from jax.sharding import PartitionSpec as P

neg_large = -1e30


def passed_along(array, axis, by):
    count = lax.axis_size(axis)
    pairs = [(i, i + by) for i in range(count) if 0 <= i + by < count]
    return lax.ppermute(array, axis, pairs)


def doc_number(positions, doc_ends):
    return jnp.sum((positions[:, None] >= doc_ends[None, :]).astype(jnp.int32), axis=1)


def tile_grads(
    grouped_query_rows,
    grouped_output_gradient,
    query_pos,
    all_keys,
    all_values,
    key_pos,
    doc_ends,
    block_rows,
    grad_k,
    grad_v,
):
    shard_rows, key_heads, group_size, head_dim = grouped_query_rows.shape
    block_count = all_keys.shape[0] // block_rows
    softmax_scale = head_dim ** (-0.5)
    query_doc = doc_number(query_pos, doc_ends)

    def take(block_number):
        offset = block_number * block_rows
        key_tile_rows = lax.dynamic_slice_in_dim(all_keys, offset, block_rows, 0)
        value_tile_rows = lax.dynamic_slice_in_dim(all_values, offset, block_rows, 0)
        block_pos = lax.dynamic_slice_in_dim(key_pos, offset, block_rows, 0)
        key_doc = doc_number(block_pos, doc_ends)
        allowed = (
            (key_doc[None, :] == query_doc[:, None])
            & (block_pos[None, :] <= query_pos[:, None])
            & (block_pos[None, :] >= 0)
        )
        return (key_tile_rows, value_tile_rows, allowed)

    def products(key_tile_rows, value_tile_rows):
        logit_scores = (
            jnp.einsum(
                "nyej,xyj->yenx",
                grouped_query_rows,
                key_tile_rows,
                preferred_element_type=jnp.float32,
            )
            * softmax_scale
        )
        probability_gradient = jnp.einsum(
            "nyej,xyj->yenx",
            grouped_output_gradient,
            value_tile_rows,
            preferred_element_type=jnp.float32,
        )
        return (logit_scores, probability_gradient)

    def unchanged(carry):
        return carry

    def first_turn(block_number, carry):
        key_tile_rows, value_tile_rows, allowed = take(block_number)

        def first_update(state):
            running_max, weight_sum, weighted = state
            logit_scores, probability_gradient = products(key_tile_rows, value_tile_rows)
            new_max = jnp.maximum(
                running_max, jnp.max(jnp.where(allowed, logit_scores, neg_large), axis=-1)
            )
            factor = jnp.exp(running_max - new_max)
            prob = jnp.where(allowed, jnp.exp(logit_scores - new_max[..., None]), 0.0)
            return (
                new_max,
                weight_sum * factor + jnp.sum(prob, axis=-1),
                weighted * factor + jnp.sum(prob * probability_gradient, axis=-1),
            )

        return lax.cond(jnp.any(allowed), first_update, unchanged, carry)

    stat_shape = (key_heads, group_size, shard_rows)
    start_stats = (
        jnp.full(stat_shape, neg_large, jnp.float32),
        jnp.zeros(stat_shape, jnp.float32),
        jnp.zeros(stat_shape, jnp.float32),
    )
    running_max, weight_sum, weighted = lax.fori_loop(0, block_count, first_turn, start_stats)
    log_total = running_max + jnp.log(weight_sum)
    delta = weighted / weight_sum

    def second_turn(block_number, carry):
        key_tile_rows, value_tile_rows, allowed = take(block_number)

        def second_update(state):
            query_gradient, grad_k, grad_v = state
            logit_scores, probability_gradient = products(key_tile_rows, value_tile_rows)
            prob = jnp.where(allowed, jnp.exp(logit_scores - log_total[..., None]), 0.0)
            dscore = prob * (probability_gradient - delta[..., None])
            probability_block = prob.astype(jnp.bfloat16)
            score_gradient_block = dscore.astype(jnp.bfloat16)
            query_gradient = query_gradient + jnp.einsum(
                "evnz,zej->nevj",
                score_gradient_block,
                key_tile_rows,
                preferred_element_type=jnp.float32,
            )
            partial_key_gradient = (
                jnp.einsum(
                    "etpr,peti->rei",
                    score_gradient_block,
                    grouped_query_rows,
                    preferred_element_type=jnp.float32,
                )
                * softmax_scale
            )
            partial_value_gradient = jnp.einsum(
                "etpr,peti->rei",
                probability_block,
                grouped_output_gradient,
                preferred_element_type=jnp.float32,
            )
            offset = block_number * block_rows
            grad_k = lax.dynamic_update_slice_in_dim(
                grad_k,
                lax.dynamic_slice_in_dim(grad_k, offset, block_rows, 0) + partial_key_gradient,
                offset,
                0,
            )
            grad_v = lax.dynamic_update_slice_in_dim(
                grad_v,
                lax.dynamic_slice_in_dim(grad_v, offset, block_rows, 0) + partial_value_gradient,
                offset,
                0,
            )
            return (query_gradient, grad_k, grad_v)

        return lax.cond(jnp.any(allowed), second_update, unchanged, carry)

    start_grads = (jnp.zeros(grouped_query_rows.shape, jnp.float32), grad_k, grad_v)
    query_gradient, grad_k, grad_v = lax.fori_loop(0, block_count, second_turn, start_grads)
    return (query_gradient * softmax_scale, grad_k, grad_v)


def local(queries, keys, values, grad_out, doc_lengths):
    doc_ends = jnp.cumsum(doc_lengths)
    query_heads, dout_heads, key_rows, value_rows = (
        lax.all_to_all(queries, "uly", split_axis=1, concat_axis=0, tiled=True),
        lax.all_to_all(grad_out, "uly", split_axis=1, concat_axis=0, tiled=True),
        lax.all_to_all(keys, "uly", split_axis=1, concat_axis=0, tiled=True),
        lax.all_to_all(values, "uly", split_axis=1, concat_axis=0, tiled=True),
    )
    prior_keys, prior_values = passed_along((key_rows, value_rows), "ctx", 1)
    shard_rows, heads_local, head_dim = query_heads.shape
    key_heads = key_rows.shape[1]
    group_size = heads_local // key_heads
    grouped_query_rows = query_heads.reshape(shard_rows, key_heads, group_size, head_dim)
    grouped_output_gradient = dout_heads.reshape(shard_rows, key_heads, group_size, head_dim)
    window_keys = jnp.concatenate([prior_keys, key_rows], axis=0)
    window_values = jnp.concatenate([prior_values, value_rows], axis=0)
    block_place = lax.axis_index("ctx")
    key_pos = (block_place - 1) * shard_rows + jnp.arange(2 * shard_rows, dtype=jnp.int32)
    half_rows = shard_rows // 2
    grad_k = jnp.zeros(window_keys.shape, jnp.float32)
    grad_v = jnp.zeros(window_values.shape, jnp.float32)
    query_tiles = []
    for tile_number in range(2):
        start = tile_number * half_rows
        query_pos = block_place * shard_rows + start + jnp.arange(half_rows, dtype=jnp.int32)
        tile_q, grad_k, grad_v = tile_grads(
            grouped_query_rows[start : start + half_rows],
            grouped_output_gradient[start : start + half_rows],
            query_pos,
            window_keys,
            window_values,
            key_pos,
            doc_ends,
            half_rows,
            grad_k,
            grad_v,
        )
        query_tiles.append(tile_q)
    query_gradient = jnp.concatenate(query_tiles, axis=0)
    back_k, back_v = passed_along((grad_k[:shard_rows], grad_v[:shard_rows]), "ctx", -1)
    own_k = grad_k[shard_rows:] + back_k
    own_v = grad_v[shard_rows:] + back_v
    rounded_q = query_gradient.astype(jnp.bfloat16).reshape(shard_rows, heads_local, head_dim)
    rounded_k = own_k.astype(jnp.bfloat16)
    rounded_v = own_v.astype(jnp.bfloat16)
    grad_queries, grad_keys, grad_values = (
        lax.all_to_all(rounded_q, "uly", split_axis=0, concat_axis=1, tiled=True),
        lax.all_to_all(rounded_k, "uly", split_axis=0, concat_axis=1, tiled=True),
        lax.all_to_all(rounded_v, "uly", split_axis=0, concat_axis=1, tiled=True),
    )
    return (grad_queries, grad_keys, grad_values)


def solution(mesh):
    in_specs = (
        P(("ctx", "uly"), None, None),
        P(("ctx", "uly"), None, None),
        P(("ctx", "uly"), None, None),
        P(("ctx", "uly"), None, None),
        P(),
    )
    out_specs = (
        P(("ctx", "uly"), None, None),
        P(("ctx", "uly"), None, None),
        P(("ctx", "uly"), None, None),
    )
    return jax.shard_map(local, mesh=mesh, in_specs=in_specs, out_specs=out_specs, check_vma=False)
```

profile of v0, /device:TPU:23, one launch (start us, length us, event | category | flops | bytes accessed | tf_op | source)
XLA Modules:
  0.0 224.4 jit_solution(16070076230977734371)
XLA Ops:
  2.4 4.2 %all-to-all-start = ((bf16[128,8,128]{2,0,1:T(8,128)(2,1)}), bf16[128,8,128]{2,0,1:T(8,128)(2,1)S(1)}, u32[]{:S(2)}, u32[]{:S(2)}) async-start(bf16[128,8,128]{2,0,1:T(8,128)(2,1)} %copy.65), calls=%async_computation | async-start | bytes 524288 | tf_op jit(solution)/shard_map/all_to_all | solution.py:157
  10.8 5.3 %all-to-all-start.2 = ((bf16[128,8,128]{2,0,1:T(8,128)(2,1)}), bf16[128,8,128]{2,0,1:T(8,128)(2,1)S(1)}, u32[]{:S(2)}, u32[]{:S(2)}) async-start(bf16[128,8,128]{2,0,1:T(8,128)(2,1)} %copy.69), calls=%async_computation.2 | async-start | bytes 524288 | tf_op jit(solution)/shard_map/all_to_all | solution.py:158
  20.2 5.4 %all-to-all-start.1 = ((bf16[128,32,128]{2,0,1:T(8,128)(2,1)}), bf16[128,32,128]{2,0,1:T(8,128)(2,1)S(1)}, u32[]{:S(2)}, u32[]{:S(2)}) async-start(bf16[128,32,128]{2,0,1:T(8,128)(2,1)} %copy.67), calls=%async_computation.1 | async-start | bytes 2097152 | tf_op jit(solution)/shard_map/all_to_all | solution.py:155
  27.0 3.1 %collective-permute-start = (bf16[512,2,128]{2,0,1:T(8,128)(2,1)S(1)}, bf16[512,2,128]{2,0,1:T(8,128)(2,1)S(1)}, u32[]{:S(2)}, u32[]{:S(2)}) collective-permute-start(bf16[512,2,128]{2,0,1:T(8,128)(2,1)S(1)} %bitcast.261), channel_id=1, source_target_pairs={{0,4},{4,8},{8,12},{12,16},{16,20},{20,24},{24,28},{1,5},{5,9},{9,... | collective-permute-start | bytes 786440 | tf_op jit(solution)/shard_map/ppermute | solution.py:12
  30.1 8.0 %all-to-all-done.1 = bf16[128,32,128]{2,0,1:T(8,128)(2,1)S(1)} async-done(((bf16[128,32,128]{2,0,1:T(8,128)(2,1)}), bf16[128,32,128]{2,0,1:T(8,128)(2,1)S(1)}, u32[]{:S(2)}, u32[]{:S(2)}) %all-to-all-start.1) | async-done | bytes 1048608 | tf_op jit(solution)/shard_map/all_to_all | solution.py:155
  38.1 5.4 %all-to-all-start.3 = ((bf16[128,32,128]{2,0,1:T(8,128)(2,1)}), bf16[128,32,128]{2,0,1:T(8,128)(2,1)S(1)}, u32[]{:S(2)}, u32[]{:S(2)}) async-start(bf16[128,32,128]{2,0,1:T(8,128)(2,1)} %copy.71), calls=%async_computation.3 | async-start | bytes 2097152 | tf_op jit(solution)/shard_map/all_to_all | solution.py:156
  43.6 3.1 %collective-permute-start.1 = (bf16[512,2,128]{2,0,1:T(8,128)(2,1)S(1)}, bf16[512,2,128]{2,0,1:T(8,128)(2,1)S(1)}, u32[]{:S(2)}, u32[]{:S(2)}) collective-permute-start(bf16[512,2,128]{2,0,1:T(8,128)(2,1)S(1)} %bitcast.263), channel_id=1, source_target_pairs={{0,4},{4,8},{8,12},{12,16},{16,20},{20,24},{24,28},{1,5},{5,9},{9,... | collective-permute-start | bytes 786440 | tf_op jit(solution)/shard_map/ppermute | solution.py:12
  47.9 5.1 %collective-permute-done.1 = bf16[512,2,128]{2,0,1:T(8,128)(2,1)S(1)} collective-permute-done((bf16[512,2,128]{2,0,1:T(8,128)(2,1)S(1)}, bf16[512,2,128]{2,0,1:T(8,128)(2,1)S(1)}, u32[]{:S(2)}, u32[]{:S(2)}) %collective-permute-start.1) | collective-permute-done | bytes 262176 | tf_op jit(solution)/shard_map/ppermute | solution.py:12
  56.3 14.2 %while.74 = (s32[]{:T(128)}, f32[2,4,256]{2,1,0:T(4,128)S(1)}, f32[2,4,256]{2,1,0:T(4,128)S(1)}, f32[2,4,256]{2,1,0:T(4,128)S(1)}, s32[1024]{0:T(1024)S(1)}, /*i...) while((s32[]{:T(128)}, f32[2,4,256]{2,1,0:T(4,128)S(1)}, ...), condition=%wide.region_26.27_spmd.clone, body=%wide.region_18.26_spmd.clone.sunk | while | flops 275073280 | bytes 8022929 | solution.py:95
  61.7 3.5 %conditional.14 = ((f32[2,4,256]{2,1,0:T(4,128)S(1)}, f32[2,4,256]{2,1,0:T(4,128)S(1)}, f32[2,4,256]{2,1,0:T(4,128)S(1)})) conditional(s32[]{:T(128)} %convert_element_type.129, (f32[2,4,256]{2,1,0:T(4,128)S(1)}, f32[2,4,256]{2,1,0:T(4,128)S(1)}, f32[2,4,256]{2,1,0:T(4,128)S(1)}) %tuple.212, (pred[256,256]{0,1:T(8,128)(4,1)S(1)}, ...), branch_computations={%region_21.21_spmd, %region_22.25_spmd} | conditional | flops 274733056 | bytes 7947296 | solution.py:87
  67.0 3.5 %conditional.14 = ((f32[2,4,256]{2,1,0:T(4,128)S(1)}, f32[2,4,256]{2,1,0:T(4,128)S(1)}, f32[2,4,256]{2,1,0:T(4,128)S(1)})) conditional(s32[]{:T(128)} %convert_element_type.129, (f32[2,4,256]{2,1,0:T(4,128)S(1)}, f32[2,4,256]{2,1,0:T(4,128)S(1)}, f32[2,4,256]{2,1,0:T(4,128)S(1)}) %tuple.212, (pred[256,256]{0,1:T(8,128)(4,1)S(1)}, ...), branch_computations={%region_21.21_spmd, %region_22.25_spmd} | conditional | flops 274733056 | bytes 7947296 | solution.py:87
  72.3 18.7 %while.72 = (s32[]{:T(128)}, f32[2,4,256]{2,1,0:T(4,128)S(1)}, f32[2,4,256]{2,1,0:T(4,128)S(1)}, f32[2,4,256]{2,1,0:T(4,128)S(1)}, s32[1024]{0:T(1024)S(1)}, /*i...) while((s32[]{:T(128)}, f32[2,4,256]{2,1,0:T(4,128)S(1)}, ...), condition=%wide.region_10.11_spmd.clone, body=%wide.region_2.10_spmd.clone.sunk | while | flops 275073280 | bytes 8022929 | solution.py:95
  74.0 4.0 %conditional.12 = ((f32[2,4,256]{2,1,0:T(4,128)S(1)}, f32[2,4,256]{2,1,0:T(4,128)S(1)}, f32[2,4,256]{2,1,0:T(4,128)S(1)})) conditional(s32[]{:T(128)} %convert_element_type.125, (f32[2,4,256]{2,1,0:T(4,128)S(1)}, f32[2,4,256]{2,1,0:T(4,128)S(1)}, f32[2,4,256]{2,1,0:T(4,128)S(1)}) %tuple.202, (pred[256,256]{0,1:T(8,128)(4,1)S(1)}, ...), branch_computations={%region_5.5_spmd, %region_6.9_spmd} | conditional | flops 274733056 | bytes 7947296 | solution.py:87
  79.7 4.0 %conditional.12 = ((f32[2,4,256]{2,1,0:T(4,128)S(1)}, f32[2,4,256]{2,1,0:T(4,128)S(1)}, f32[2,4,256]{2,1,0:T(4,128)S(1)})) conditional(s32[]{:T(128)} %convert_element_type.125, (f32[2,4,256]{2,1,0:T(4,128)S(1)}, f32[2,4,256]{2,1,0:T(4,128)S(1)}, f32[2,4,256]{2,1,0:T(4,128)S(1)}) %tuple.202, (pred[256,256]{0,1:T(8,128)(4,1)S(1)}, ...), branch_computations={%region_5.5_spmd, %region_6.9_spmd} | conditional | flops 274733056 | bytes 7947296 | solution.py:87
  85.3 4.0 %conditional.12 = ((f32[2,4,256]{2,1,0:T(4,128)S(1)}, f32[2,4,256]{2,1,0:T(4,128)S(1)}, f32[2,4,256]{2,1,0:T(4,128)S(1)})) conditional(s32[]{:T(128)} %convert_element_type.125, (f32[2,4,256]{2,1,0:T(4,128)S(1)}, f32[2,4,256]{2,1,0:T(4,128)S(1)}, f32[2,4,256]{2,1,0:T(4,128)S(1)}) %tuple.202, (pred[256,256]{0,1:T(8,128)(4,1)S(1)}, ...), branch_computations={%region_5.5_spmd, %region_6.9_spmd} | conditional | flops 274733056 | bytes 7947296 | solution.py:87
  93.3 41.5 %while.73 = (s32[]{:T(128)}, f32[256,2,4,128]{3,0,2,1:T(8,128)}, f32[1024,2,128]{2,0,1:T(8,128)S(1)}, f32[1024,2,128]{2,0,1:T(8,128)}, s32[1024]{0:T(1024)S(1)},...) while((s32[]{:T(128)}, f32[256,2,4,128]{3,0,2,1:T(8,128)}, ...), condition=%wide.region_16.17_spmd.clone, body=%wide.region_11.16_spmd.clone.sunk | while | flops 675557632 | bytes 23621160 | solution.py:148
  94.9 11.7 %conditional.13 = ((f32[256,2,4,128]{3,0,2,1:T(8,128)}, f32[1024,2,128]{2,0,1:T(8,128)S(1)}, f32[1024,2,128]{2,0,1:T(8,128)})) conditional(s32[]{:T(128)} %convert_element_type.127, (f32[256,2,4,128]{3,0,2,1:T(8,128)}, f32[1024,2,128]{2,0,1:T(8,128)S(1)}, f32[1024,2,128]{2,0,1:T(8,128)}) %tuple.207, (pred[256,256]{0,1:T(8,128)(4,1)S(1)}, ...), branch_computations={%region_14.14_spmd, %region_15.15_spmd} | conditional | flops 675217408 | bytes 23545486 | solution.py:145
  108.2 11.7 %conditional.13 = ((f32[256,2,4,128]{3,0,2,1:T(8,128)}, f32[1024,2,128]{2,0,1:T(8,128)S(1)}, f32[1024,2,128]{2,0,1:T(8,128)})) conditional(s32[]{:T(128)} %convert_element_type.127, (f32[256,2,4,128]{3,0,2,1:T(8,128)}, f32[1024,2,128]{2,0,1:T(8,128)S(1)}, f32[1024,2,128]{2,0,1:T(8,128)}) %tuple.207, (pred[256,256]{0,1:T(8,128)(4,1)S(1)}, ...), branch_computations={%region_14.14_spmd, %region_15.15_spmd} | conditional | flops 675217408 | bytes 23545486 | solution.py:145
  116.9 2.9 %fusion.24 = f32[256,2,4,128]{3,0,2,1:T(8,128)} fusion(f32[256,2,4,128]{3,0,2,1:T(8,128)} %get-tuple-element.1157, bf16[2,4,256,256]{2,3,1,0:T(8,128)(2,1)S(1)} %fusion.21, bf16[1024,2,128]{2,0,1:T(8,128)(2,1)} %get-tuple-element.1159, s32[]{:T(128)} %get-tuple-element.1160), kind=kOutput, calls=%fused_computation.29 | convolution fusion | flops 134479872 | bytes 3277312 | tf_op jit(solution)/shard_map/while/body/eval_jaxpr/cond/branch_1_fun/evnz,zej->nevj/dot_general | solution.py:109
  121.5 11.7 %conditional.13 = ((f32[256,2,4,128]{3,0,2,1:T(8,128)}, f32[1024,2,128]{2,0,1:T(8,128)S(1)}, f32[1024,2,128]{2,0,1:T(8,128)})) conditional(s32[]{:T(128)} %convert_element_type.127, (f32[256,2,4,128]{3,0,2,1:T(8,128)}, f32[1024,2,128]{2,0,1:T(8,128)S(1)}, f32[1024,2,128]{2,0,1:T(8,128)}) %tuple.207, (pred[256,256]{0,1:T(8,128)(4,1)S(1)}, ...), branch_computations={%region_14.14_spmd, %region_15.15_spmd} | conditional | flops 675217408 | bytes 23545486 | solution.py:145
  135.9 29.5 %while.75 = (s32[]{:T(128)}, f32[256,2,4,128]{3,0,2,1:T(8,128)}, f32[1024,2,128]{2,0,1:T(8,128)S(1)}, f32[1024,2,128]{2,0,1:T(8,128)}, s32[1024]{0:T(1024)S(1)},...) while((s32[]{:T(128)}, f32[256,2,4,128]{3,0,2,1:T(8,128)}, ...), condition=%wide.region_32.33_spmd.clone, body=%wide.region_27.32_spmd.clone.sunk | while | flops 675557632 | bytes 27815520 | solution.py:148
  140.9 11.4 %conditional.15 = ((f32[256,2,4,128]{3,0,2,1:T(8,128)}, f32[1024,2,128]{2,0,1:T(8,128)S(1)}, f32[1024,2,128]{2,0,1:T(8,128)})) conditional(s32[]{:T(128)} %convert_element_type.131, (f32[256,2,4,128]{3,0,2,1:T(8,128)}, f32[1024,2,128]{2,0,1:T(8,128)S(1)}, f32[1024,2,128]{2,0,1:T(8,128)}) %tuple.217, (pred[256,256]{0,1:T(8,128)(4,1)S(1)}, ...), branch_computations={%region_30.30_spmd, %region_31.31_spmd} | conditional | flops 675217408 | bytes 27739846 | solution.py:145
  149.4 2.9 %fusion.57 = f32[256,2,4,128]{3,0,2,1:T(8,128)} fusion(f32[256,2,4,128]{3,0,2,1:T(8,128)} %get-tuple-element.1212, bf16[2,4,256,256]{2,3,1,0:T(8,128)(2,1)S(1)} %fusion.54, bf16[1024,2,128]{2,0,1:T(8,128)(2,1)} %get-tuple-element.1214, s32[]{:T(128)} %get-tuple-element.1215), kind=kOutput, calls=%fused_computation.73 | convolution fusion | flops 134479872 | bytes 3277312 | tf_op jit(solution)/shard_map/while/body/eval_jaxpr/cond/branch_1_fun/evnz,zej->nevj/dot_general | solution.py:109
  153.9 11.4 %conditional.15 = ((f32[256,2,4,128]{3,0,2,1:T(8,128)}, f32[1024,2,128]{2,0,1:T(8,128)S(1)}, f32[1024,2,128]{2,0,1:T(8,128)})) conditional(s32[]{:T(128)} %convert_element_type.131, (f32[256,2,4,128]{3,0,2,1:T(8,128)}, f32[1024,2,128]{2,0,1:T(8,128)S(1)}, f32[1024,2,128]{2,0,1:T(8,128)}) %tuple.217, (pred[256,256]{0,1:T(8,128)(4,1)S(1)}, ...), branch_computations={%region_30.30_spmd, %region_31.31_spmd} | conditional | flops 675217408 | bytes 27739846 | solution.py:145
  162.4 2.9 %fusion.57 = f32[256,2,4,128]{3,0,2,1:T(8,128)} fusion(f32[256,2,4,128]{3,0,2,1:T(8,128)} %get-tuple-element.1212, bf16[2,4,256,256]{2,3,1,0:T(8,128)(2,1)S(1)} %fusion.54, bf16[1024,2,128]{2,0,1:T(8,128)(2,1)} %get-tuple-element.1214, s32[]{:T(128)} %get-tuple-element.1215), kind=kOutput, calls=%fused_computation.73 | convolution fusion | flops 134479872 | bytes 3277312 | tf_op jit(solution)/shard_map/while/body/eval_jaxpr/cond/branch_1_fun/evnz,zej->nevj/dot_general | solution.py:109
  170.2 3.4 %collective-permute-start.2 = (f32[512,2,128]{2,1,0:T(2,128)S(1)}, f32[512,2,128]{2,1,0:T(2,128)S(1)}, u32[]{:S(2)}, u32[]{:S(2)}) collective-permute-start(f32[512,2,128]{2,1,0:T(2,128)S(1)} %slice.53), channel_id=1, source_target_pairs={{4,0},{8,4},{12,8},{16,12},{20,16},{24,20},{28,24},{5,1},{9,5},{13... | collective-permute-start | bytes 1572872 | tf_op jit(solution)/shard_map/ppermute | solution.py:12
  175.0 8.1 %collective-permute-done.3 = f32[512,2,128]{2,1,0:T(2,128)S(1)} collective-permute-done((f32[512,2,128]{2,1,0:T(2,128)S(1)}, f32[512,2,128]{2,1,0:T(2,128)S(1)}, u32[]{:S(2)}, u32[]{:S(2)}) %collective-permute-start.3) | collective-permute-done | bytes 524320 | tf_op jit(solution)/shard_map/ppermute | solution.py:12
  184.1 7.3 %all-to-all-start.6 = ((bf16[512,2,128]{2,1,0:T(2,128)(2,1)}), bf16[512,2,128]{2,1,0:T(2,128)(2,1)S(1)}, u32[]{:S(2)}, u32[]{:S(2)}) async-start(bf16[512,2,128]{2,1,0:T(2,128)(2,1)} %fusion.74), calls=%async_computation.6 | async-start | bytes 524288 | tf_op jit(solution)/shard_map/all_to_all | solution.py:200
  191.3 3.0 %collective-permute-done.2 = f32[512,2,128]{2,1,0:T(2,128)S(1)} collective-permute-done((f32[512,2,128]{2,1,0:T(2,128)S(1)}, f32[512,2,128]{2,1,0:T(2,128)S(1)}, u32[]{:S(2)}, u32[]{:S(2)}) %collective-permute-start.2) | collective-permute-done | bytes 524320 | tf_op jit(solution)/shard_map/ppermute | solution.py:12
  195.4 5.7 %all-to-all-start.5 = ((bf16[512,2,128]{2,1,0:T(2,128)(2,1)}), bf16[512,2,128]{2,1,0:T(2,128)(2,1)S(1)}, u32[]{:S(2)}, u32[]{:S(2)}) async-start(bf16[512,2,128]{2,1,0:T(2,128)(2,1)} %fusion.75), calls=%async_computation.5 | async-start | bytes 524288 | tf_op jit(solution)/shard_map/all_to_all | solution.py:199
  205.3 5.4 %all-to-all-start.4 = ((bf16[512,8,128]{2,1,0:T(8,128)(2,1)}), bf16[512,8,128]{2,1,0:T(8,128)(2,1)S(1)}, u32[]{:S(2)}, u32[]{:S(2)}) async-start(bf16[512,8,128]{2,1,0:T(8,128)(2,1)} %pad_maximum_fusion), calls=%async_computation.4 | async-start | bytes 2097152 | tf_op jit(solution)/shard_map/all_to_all | solution.py:198
  212.5 10.8 %all-to-all-done.4 = bf16[512,8,128]{2,1,0:T(8,128)(2,1)S(1)} async-done(((bf16[512,8,128]{2,1,0:T(8,128)(2,1)}), bf16[512,8,128]{2,1,0:T(8,128)(2,1)S(1)}, u32[]{:S(2)}, u32[]{:S(2)}) %all-to-all-start.4) | async-done | bytes 1048608 | tf_op jit(solution)/shard_map/all_to_all | solution.py:198
  (213 shorter events, 120.1 us)
Async XLA Ops:
  0.6 15.4 %copy-start.8 = (bf16[128,32,128]{2,1,0:T(8,128)(2,1)S(1)}, bf16[128,32,128]{2,1,0:T(8,128)(2,1)}, u32[]{:S(2)}) copy-start(bf16[128,32,128]{2,1,0:T(8,128)(2,1)} %param.21) | copy-start | bytes 3145732
  2.4 8.4 %all-to-all-start = ((bf16[128,8,128]{2,0,1:T(8,128)(2,1)}), bf16[128,8,128]{2,0,1:T(8,128)(2,1)S(1)}, u32[]{:S(2)}, u32[]{:S(2)}) async-start(bf16[128,8,128]{2,0,1:T(8,128)(2,1)} %copy.65), calls=%async_computation | async-start | bytes 524288 | tf_op jit(solution)/shard_map/all_to_all | solution.py:157
  10.8 9.4 %all-to-all-start.2 = ((bf16[128,8,128]{2,0,1:T(8,128)(2,1)}), bf16[128,8,128]{2,0,1:T(8,128)(2,1)S(1)}, u32[]{:S(2)}, u32[]{:S(2)}) async-start(bf16[128,8,128]{2,0,1:T(8,128)(2,1)} %copy.69), calls=%async_computation.2 | async-start | bytes 524288 | tf_op jit(solution)/shard_map/all_to_all | solution.py:158
  16.1 9.5 %copy-start.9 = (bf16[128,32,128]{2,1,0:T(8,128)(2,1)S(1)}, bf16[128,32,128]{2,1,0:T(8,128)(2,1)}, u32[]{:S(2)}) copy-start(bf16[128,32,128]{2,1,0:T(8,128)(2,1)} %param.24) | copy-start | bytes 3145732
  20.2 18.0 %all-to-all-start.1 = ((bf16[128,32,128]{2,0,1:T(8,128)(2,1)}), bf16[128,32,128]{2,0,1:T(8,128)(2,1)S(1)}, u32[]{:S(2)}, u32[]{:S(2)}) async-start(bf16[128,32,128]{2,0,1:T(8,128)(2,1)} %copy.67), calls=%async_computation.1 | async-start | bytes 2097152 | tf_op jit(solution)/shard_map/all_to_all | solution.py:155
  27.0 19.8 %copy-start.10 = (s32[16]{0:T(128)S(1)}, s32[16]{0:T(128)}, u32[]{:S(2)}) copy-start(s32[16]{0:T(128)} %param.25) | copy-start | bytes 196
  27.0 20.1 %collective-permute-start = (bf16[512,2,128]{2,0,1:T(8,128)(2,1)S(1)}, bf16[512,2,128]{2,0,1:T(8,128)(2,1)S(1)}, u32[]{:S(2)}, u32[]{:S(2)}) collective-permute-start(bf16[512,2,128]{2,0,1:T(8,128)(2,1)S(1)} %bitcast.261), channel_id=1, source_target_pairs={{0,4},{4,8},{8,12},{12,16},{16,20},{20,24},{24,28},{1,5},{5,9},{9,... | collective-permute-start | bytes 786440 | tf_op jit(solution)/shard_map/ppermute | solution.py:12
  38.1 18.0 %all-to-all-start.3 = ((bf16[128,32,128]{2,0,1:T(8,128)(2,1)}), bf16[128,32,128]{2,0,1:T(8,128)(2,1)S(1)}, u32[]{:S(2)}, u32[]{:S(2)}) async-start(bf16[128,32,128]{2,0,1:T(8,128)(2,1)} %copy.71), calls=%async_computation.3 | async-start | bytes 2097152 | tf_op jit(solution)/shard_map/all_to_all | solution.py:156
  43.6 9.4 %collective-permute-start.1 = (bf16[512,2,128]{2,0,1:T(8,128)(2,1)S(1)}, bf16[512,2,128]{2,0,1:T(8,128)(2,1)S(1)}, u32[]{:S(2)}, u32[]{:S(2)}) collective-permute-start(bf16[512,2,128]{2,0,1:T(8,128)(2,1)S(1)} %bitcast.263), channel_id=1, source_target_pairs={{0,4},{4,8},{8,12},{12,16},{16,20},{20,24},{24,28},{1,5},{5,9},{9,... | collective-permute-start | bytes 786440 | tf_op jit(solution)/shard_map/ppermute | solution.py:12
  70.5 1.8 copy-start
  70.5 1.8 copy-start.1
  94.9 1.0 copy-start.4
  103.6 2.9 %copy-start.5 = (f32[1024,2,128]{2,0,1:T(8,128)S(1)}, f32[1024,2,128]{2,0,1:T(8,128)}, u32[]{:S(2)}) copy-start(f32[1024,2,128]{2,0,1:T(8,128)} %fusion.28) | copy-start | bytes 3145732 | tf_op jit(solution)/shard_map/while/body/eval_jaxpr/cond
  108.2 1.0 copy-start.4
  116.9 2.9 %copy-start.5 = (f32[1024,2,128]{2,0,1:T(8,128)S(1)}, f32[1024,2,128]{2,0,1:T(8,128)}, u32[]{:S(2)}) copy-start(f32[1024,2,128]{2,0,1:T(8,128)} %fusion.28) | copy-start | bytes 3145732 | tf_op jit(solution)/shard_map/while/body/eval_jaxpr/cond
  121.5 1.0 copy-start.4
  130.2 2.9 %copy-start.5 = (f32[1024,2,128]{2,0,1:T(8,128)S(1)}, f32[1024,2,128]{2,0,1:T(8,128)}, u32[]{:S(2)}) copy-start(f32[1024,2,128]{2,0,1:T(8,128)} %fusion.28) | copy-start | bytes 3145732 | tf_op jit(solution)/shard_map/while/body/eval_jaxpr/cond
  140.9 1.0 copy-start.6
  140.9 2.7 %copy-start.2 = (bf16[256,2,4,128]{3,0,2,1:T(8,128)(2,1)S(1)}, bf16[256,2,4,128]{3,0,2,1:T(8,128)(2,1)}, u32[]{:S(2)}) copy-start(bf16[256,2,4,128]{3,0,2,1:T(8,128)(2,1)} %get-tuple-element.1219) | copy-start | bytes 1572868 | tf_op jit(solution)/shard_map/while/body/eval_jaxpr/cond
  145.0 2.3 %copy-start.3 = (bf16[256,2,4,128]{3,0,2,1:T(8,128)(2,1)S(1)}, bf16[256,2,4,128]{3,0,2,1:T(8,128)(2,1)}, u32[]{:S(2)}) copy-start(bf16[256,2,4,128]{3,0,2,1:T(8,128)(2,1)} %get-tuple-element.1219) | copy-start | bytes 1572868 | tf_op jit(solution)/shard_map/while/body/eval_jaxpr/cond
  149.4 2.9 %copy-start.7 = (f32[1024,2,128]{2,0,1:T(8,128)S(1)}, f32[1024,2,128]{2,0,1:T(8,128)}, u32[]{:S(2)}) copy-start(f32[1024,2,128]{2,0,1:T(8,128)} %fusion.61) | copy-start | bytes 3145732 | tf_op jit(solution)/shard_map/while/body/eval_jaxpr/cond
  154.0 1.0 copy-start.6
  154.0 2.7 %copy-start.2 = (bf16[256,2,4,128]{3,0,2,1:T(8,128)(2,1)S(1)}, bf16[256,2,4,128]{3,0,2,1:T(8,128)(2,1)}, u32[]{:S(2)}) copy-start(bf16[256,2,4,128]{3,0,2,1:T(8,128)(2,1)} %get-tuple-element.1219) | copy-start | bytes 1572868 | tf_op jit(solution)/shard_map/while/body/eval_jaxpr/cond
  158.0 2.3 %copy-start.3 = (bf16[256,2,4,128]{3,0,2,1:T(8,128)(2,1)S(1)}, bf16[256,2,4,128]{3,0,2,1:T(8,128)(2,1)}, u32[]{:S(2)}) copy-start(bf16[256,2,4,128]{3,0,2,1:T(8,128)(2,1)} %get-tuple-element.1219) | copy-start | bytes 1572868 | tf_op jit(solution)/shard_map/while/body/eval_jaxpr/cond
  162.4 2.9 %copy-start.7 = (f32[1024,2,128]{2,0,1:T(8,128)S(1)}, f32[1024,2,128]{2,0,1:T(8,128)}, u32[]{:S(2)}) copy-start(f32[1024,2,128]{2,0,1:T(8,128)} %fusion.61) | copy-start | bytes 3145732 | tf_op jit(solution)/shard_map/while/body/eval_jaxpr/cond
  167.4 15.7 %collective-permute-start.3 = (f32[512,2,128]{2,1,0:T(2,128)S(1)}, f32[512,2,128]{2,1,0:T(2,128)S(1)}, u32[]{:S(2)}, u32[]{:S(2)}) collective-permute-start(f32[512,2,128]{2,1,0:T(2,128)S(1)} %slice.55), channel_id=1, source_target_pairs={{4,0},{8,4},{12,8},{16,12},{20,16},{24,20},{28,24},{5,1},{9,5},{13... | collective-permute-start | bytes 1572872 | tf_op jit(solution)/shard_map/ppermute | solution.py:12
  170.2 24.1 %collective-permute-start.2 = (f32[512,2,128]{2,1,0:T(2,128)S(1)}, f32[512,2,128]{2,1,0:T(2,128)S(1)}, u32[]{:S(2)}, u32[]{:S(2)}) collective-permute-start(f32[512,2,128]{2,1,0:T(2,128)S(1)} %slice.53), channel_id=1, source_target_pairs={{4,0},{8,4},{12,8},{16,12},{20,16},{24,20},{28,24},{5,1},{9,5},{13... | collective-permute-start | bytes 1572872 | tf_op jit(solution)/shard_map/ppermute | solution.py:12
  184.1 11.4 %all-to-all-start.6 = ((bf16[512,2,128]{2,1,0:T(2,128)(2,1)}), bf16[512,2,128]{2,1,0:T(2,128)(2,1)S(1)}, u32[]{:S(2)}, u32[]{:S(2)}) async-start(bf16[512,2,128]{2,1,0:T(2,128)(2,1)} %fusion.74), calls=%async_computation.6 | async-start | bytes 524288 | tf_op jit(solution)/shard_map/all_to_all | solution.py:200
  195.4 9.9 %all-to-all-start.5 = ((bf16[512,2,128]{2,1,0:T(2,128)(2,1)}), bf16[512,2,128]{2,1,0:T(2,128)(2,1)S(1)}, u32[]{:S(2)}, u32[]{:S(2)}) async-start(bf16[512,2,128]{2,1,0:T(2,128)(2,1)} %fusion.75), calls=%async_computation.5 | async-start | bytes 524288 | tf_op jit(solution)/shard_map/all_to_all | solution.py:199
  205.3 18.0 %all-to-all-start.4 = ((bf16[512,8,128]{2,1,0:T(8,128)(2,1)}), bf16[512,8,128]{2,1,0:T(8,128)(2,1)S(1)}, u32[]{:S(2)}, u32[]{:S(2)}) async-start(bf16[512,8,128]{2,1,0:T(8,128)(2,1)} %pad_maximum_fusion), calls=%async_computation.4 | async-start | bytes 2097152 | tf_op jit(solution)/shard_map/all_to_all | solution.py:198
where the time goes:
time: 228 us; the launch traced here: 224 us
  matrix products  68.9 us (30%)
  starting transfers between devices  50.3 us (22%)
  waiting for transfers between devices  43.3 us (19%)
  other arithmetic  26.4 us (12%)
  local copies, waits for them, and re-layouts  23.2 us (10%)
  loops' own time  11.4 us (5%)
    ppermute x4, waiting for transfers between devices, passed_along(): return lax.ppermute(array, axis, pairs)  16.2 us
    dot_general x10, matrix products, products(): jnp.einsum('nyej,xyj->yenx', grouped_output_gradient, value_tile_rows, pr...  16.1 us
    dot_general x10, matrix products, products(): jnp.einsum('nyej,xyj->yenx', grouped_query_rows, key_tile_rows, preferred...  16.1 us
    dot_general x5, matrix products, second_update(): jnp.einsum('evnz,zej->nevj', score_gradient_block, key_tile_rows, preferr...  14.5 us
    ppermute x4, starting transfers between devices, passed_along(): return lax.ppermute(array, axis, pairs)  11.6 us
    dot_general x5, matrix products, second_update(): jnp.einsum('etpr,peti->rei', score_gradient_block, grouped_query_rows, pr...  11.3 us
    dot_general x5, matrix products, second_update(): jnp.einsum('etpr,peti->rei', probability_block, grouped_output_gradient,...  10.9 us
    all_to_all x1, waiting for transfers between devices, local(): lax.all_to_all(rounded_q, 'uly', split_axis=0, concat_axis=1, tiled=True)  10.8 us
  transfers between devices with their start and end apart: 11, of which 10 were waited for; matrix products, arithmetic and copies ran while one was open for 7% of the time, Pallas kernels for 0%

commit v1 on v0

v1 whole, which is shorter than its diff:
```python
import functools

import jax
import jax.numpy as jnp
from jax import lax
from jax.experimental import pallas as pl
from jax.experimental.pallas import tpu as pltpu
from jax.sharding import PartitionSpec as P

AXES = ("ctx", "uly")
LOG2E = 1.4426950408889634
MASKED = -1e30


def shifted(array, device_count, by, swap):
    pairs = []
    for d in range(device_count):
        to = (d ^ 1 if swap else d) + by
        if 0 <= to < device_count:
            pairs.append((d, to))
    return lax.ppermute(array, AXES, pairs)


def grads_kernel(halo, group, place_ref, lengths_ref, *refs):
    kv_refs = refs[: 2 * (halo + 1)]
    qd_refs = refs[2 * (halo + 1) : 2 * (halo + 1) + 2]
    outs = refs[2 * (halo + 1) + 2 : -3]
    dkv_refs, dq_refs = outs[: 2 * (halo + 1)], outs[2 * (halo + 1) :]
    kv_scr, qd_scr, acc = refs[-3:]
    tokens, dim = kv_refs[0].shape[2:]
    core, window_start = place_ref[0], place_ref[1]
    blocks = 2 * halo + 1
    keys = blocks * tokens
    scale = dim**-0.5

    for back in range(halo + 1):
        at = 2 * (halo - back)
        kv_scr[at + core] = kv_refs[2 * back][0]
        kv_scr[at + 1 - core] = kv_refs[2 * back + 1][0]
    qd_scr[core] = qd_refs[0][0]
    qd_scr[1 - core] = qd_refs[1][0]

    lane = lax.broadcasted_iota(jnp.int32, (1, tokens), 1)
    for e in range(2):
        query_pos = lane + (2 * halo + e) * tokens

        def start_of(d, carry):
            start, first = carry
            first = jnp.where(query_pos + window_start >= start, start, first)
            return start + lengths_ref[d], first

        _, first = lax.fori_loop(
            0, lengths_ref.shape[0], start_of, (jnp.int32(0), jnp.zeros((1, tokens), jnp.int32))
        )
        first = first - window_start
        key_pos = lax.broadcasted_iota(jnp.int32, (keys, tokens), 0) + e * tokens
        allowed = (key_pos >= first) & (key_pos <= query_pos)
        k = kv_scr[pl.ds(e, blocks), 0].reshape(keys, dim)
        v = kv_scr[pl.ds(e, blocks), 1].reshape(keys, dim)
        q = qd_scr[e, 0].reshape(group * tokens, dim)
        do = qd_scr[e, 1].reshape(group * tokens, dim)
        probs, dscores = [], []
        for g in range(group):
            rows = slice(g * tokens, (g + 1) * tokens)
            nt = (((1,), (1,)), ((), ()))
            s = lax.dot_general(k, q[rows], nt, preferred_element_type=jnp.float32)
            dp = lax.dot_general(v, do[rows], nt, preferred_element_type=jnp.float32)
            s = jnp.where(allowed, s, MASKED)
            top = jnp.max(s, axis=0, keepdims=True)
            w = jnp.exp2((s - top) * (scale * LOG2E))
            inv = 1.0 / jnp.sum(w, axis=0, keepdims=True)
            delta = jnp.sum(w * dp, axis=0, keepdims=True) * inv
            p = w * inv
            probs.append(p.astype(jnp.bfloat16))
            dscores.append((p * (dp - delta)).astype(jnp.bfloat16))
        p = jnp.concatenate(probs, axis=1)
        ds = jnp.concatenate(dscores, axis=1)
        dv = jnp.dot(p, do, preferred_element_type=jnp.float32)
        dk = jnp.dot(ds, q, preferred_element_type=jnp.float32) * scale
        dqt = jnp.dot(k.T, ds, preferred_element_type=jnp.float32) * scale
        for g in range(group):
            dq = dqt[:, g * tokens : (g + 1) * tokens].T
            qd_scr[e, 0, g] = dq.astype(jnp.bfloat16)
        dk = dk.reshape(blocks, tokens, dim)
        dv = dv.reshape(blocks, tokens, dim)
        if e == 0:
            acc[:blocks, 0] = dk
            acc[:blocks, 1] = dv
            acc[blocks] = jnp.zeros_like(acc[blocks])
        else:
            acc[1:, 0] += dk
            acc[1:, 1] += dv

    for back in range(halo + 1):
        at = 2 * (halo - back)
        for swap in range(2):
            out = dkv_refs[2 * back + swap]
            out[0] = acc[at + (1 - core if swap else core)].astype(out.dtype)
    dq_refs[0][0] = qd_scr[core, 0]
    dq_refs[1][0] = qd_scr[1 - core, 0]


def grads(place, lengths, kvs, qds):
    heads, _, group, tokens, dim = qds[0].shape
    halo = len(kvs) // 2 - 1
    kv_spec = pl.BlockSpec((1, 2, tokens, dim), lambda h, *_: (h, 0, 0, 0))
    qd_spec = pl.BlockSpec((1, 2, group, tokens, dim), lambda h, *_: (h, 0, 0, 0, 0))
    dq_spec = pl.BlockSpec((1, group, tokens, dim), lambda h, *_: (h, 0, 0, 0))
    dkv_shape = (heads, 2, tokens, dim)
    outs = [jax.ShapeDtypeStruct(dkv_shape, jnp.float32 if i == 0 else jnp.bfloat16) for i in range(len(kvs))]
    outs += [jax.ShapeDtypeStruct((heads, group, tokens, dim), jnp.bfloat16)] * 2
    window = 2 * halo + 2
    products = 5 * 2 * heads * group * 2 * tokens * (window - 1) * tokens * dim
    return pl.pallas_call(
        functools.partial(grads_kernel, halo, group),
        out_shape=outs,
        grid_spec=pltpu.PrefetchScalarGridSpec(
            num_scalar_prefetch=2,
            grid=(heads,),
            in_specs=[kv_spec] * len(kvs) + [qd_spec] * 2,
            out_specs=[kv_spec] * len(kvs) + [dq_spec] * 2,
            scratch_shapes=[
                pltpu.VMEM((window, 2, tokens, dim), jnp.bfloat16),
                pltpu.VMEM((2, 2, group, tokens, dim), jnp.bfloat16),
                pltpu.VMEM((window, 2, tokens, dim), jnp.float32),
            ],
        ),
        compiler_params=pltpu.CompilerParams(vmem_limit_bytes=48 * 2**20),
        cost_estimate=pl.CostEstimate(flops=products, bytes_accessed=8 * 2**20, transcendentals=0),
        name="grads",
    )(place, lengths, *kvs, *qds)


def local(queries, keys, values, grad_out, doc_lengths):
    uly_count = lax.axis_size("uly")
    device_count = lax.axis_size("ctx") * uly_count
    halo = uly_count // 2
    device = lax.axis_index("ctx") * uly_count + lax.axis_index("uly")
    core = device % 2
    tokens, heads, dim = queries.shape
    key_heads = keys.shape[1]
    group = heads // key_heads
    half = key_heads // 2

    kv = jnp.stack([keys, values]).reshape(2, tokens, 2, half, dim).transpose(2, 3, 0, 1, 4)
    kv_same = lax.dynamic_index_in_dim(kv, core, 0, keepdims=False)
    kv_cross = lax.dynamic_index_in_dim(kv, 1 - core, 0, keepdims=False)
    qd = jnp.stack([queries, grad_out]).reshape(2, tokens, 2, half, group, dim).transpose(2, 3, 0, 4, 1, 5)
    qd_same = lax.dynamic_index_in_dim(qd, core, 0, keepdims=False)
    qd_cross = lax.dynamic_index_in_dim(qd, 1 - core, 0, keepdims=False)

    kvs = [kv_same, shifted(kv_cross, device_count, 0, True)]
    for back in range(1, halo + 1):
        kvs.append(shifted(kv_same, device_count, 2 * back, False))
        kvs.append(shifted(kv_cross, device_count, 2 * back, True))
    qds = [qd_same, shifted(qd_cross, device_count, 0, True)]

    place = jnp.stack([core, (device // 2 - halo) * (2 * tokens)]).astype(jnp.int32)
    outs = grads(place, doc_lengths, kvs, qds)
    dkvs, (dq_same, dq_cross) = outs[:-2], outs[-2:]

    dkv_same = dkvs[0]
    dkv_cross = shifted(dkvs[1], device_count, 0, True).astype(jnp.float32)
    for back in range(1, halo + 1):
        dkv_same = dkv_same + shifted(dkvs[2 * back], device_count, -2 * back, False).astype(jnp.float32)
        dkv_cross = dkv_cross + shifted(dkvs[2 * back + 1], device_count, -2 * back, True).astype(jnp.float32)
    dq_cross = shifted(dq_cross, device_count, 0, True)

    def ordered(same, cross):
        low = jnp.where(core == 0, same, cross)
        high = jnp.where(core == 0, cross, same)
        return jnp.concatenate([low, high], axis=0)

    dkv = ordered(dkv_same, dkv_cross).astype(jnp.bfloat16).transpose(1, 2, 0, 3)
    dq = ordered(dq_same, dq_cross).transpose(2, 0, 1, 3).reshape(tokens, heads, dim)
    return dq, dkv[0], dkv[1]


def solution(mesh):
    spec = P(AXES, None, None)
    return jax.shard_map(
        local, mesh=mesh, in_specs=(spec,) * 4 + (P(),), out_specs=(spec,) * 3, check_vma=False
    )
```

time: 228 us -> 86.7 us (0.38)
  the two profiles are of different devices: /device:TPU:23 before, /device:TPU:5 now
where the time goes in v1:
time: 86.7 us; the launch traced here: 86.3 us
  waiting for transfers between devices  35.3 us (41%)
  starting transfers between devices  22.7 us (26%)
  Pallas kernels  15.1 us (17%)
  local copies, waits for them, and re-layouts  10.6 us (12%)
  other arithmetic  1.74 us (2%)
  between operations  0.88 us (1%)
    ppermute x12, waiting for transfers between devices, shifted(): return lax.ppermute(array, AXES, pairs)  35.3 us
    ppermute x12, starting transfers between devices, shifted(): return lax.ppermute(array, AXES, pairs)  22.7 us
    pallas_call x1, Pallas kernels, grads(): pl.pallas_call(functools.partial(grads_kernel, halo, group), out_shape=ou...  15.1 us
    unnamed x27, local copies, waits for them, and re-layouts  10.6 us
  transfers between devices with their start and end apart: 12, of which 6 were waited for; matrix products, arithmetic and copies ran while one was open for 3% of the time, Pallas kernels for 0%

profile of v1, /device:TPU:5, one launch (start us, length us, event | category | flops | bytes accessed | tf_op | source)
XLA Modules:
  0.0 86.3 jit_solution(2360222392520530083)
XLA Ops:
  0.7 1.7 %copy.10 = bf16[128,32,128]{2,0,1:T(8,128)(2,1)S(1)} copy(bf16[128,32,128]{2,1,0:T(8,128)(2,1)} %param.5) | data formatting | bytes 2097152 | tf_op args[0]
  2.4 0.4 copy.11
  2.8 1.2 %fusion.1 = (bf16[4,2,4,128,128]{4,3,2,1,0:T(8,128)(2,1)}, bf16[4,2,4,128,128]{4,3,2,1,0:T(8,128)(2,1)S(1)}) fusion(s32[]{:T(128)S(6)} %select_n.49, bf16[1,128,2,4,4,128]{5,1,4,0,3,2:T(8,128)(2,1)S(1)} %bitcast.31, bf16[1,128,2,4,4,128]{5,1,4,0,3,2:T(8,128)(2,1)S(1)} %bitcast.32, s32[]{:T(128)S(6)} %select_n.48), kind=kLoop, calls=%fused_computation.5 | loop fusion | flops 1048576 | bytes 4194312 | tf_op jit(solution)/shard_map/jit(dynamic_index_in_dim)/squeeze | solution.py:150
  4.0 0.7 collective-permute-start.5
  4.8 3.0 %collective-permute-start.4 = (bf16[4,2,128,128]{3,2,1,0:T(8,128)(2,1)S(1)}, bf16[4,2,128,128]{3,2,1,0:T(8,128)(2,1)S(1)}, u32[]{:S(2)}, u32[]{:S(2)}) collective-permute-start(bf16[4,2,128,128]{3,2,1,0:T(8,128)(2,1)S(1)} %get-tuple-element.30), channel_id=1, source_target_pairs={{0,5},{1,4},{2,7},{3,6},{4,9},{5,8},{6,11},{7,10},{8,13},{9,12},{1... | collective-permute-start | bytes 786440 | tf_op jit(solution)/shard_map/ppermute | solution.py:21
  7.9 3.5 %collective-permute-start.2 = (bf16[4,2,128,128]{3,2,1,0:T(8,128)(2,1)S(1)}, bf16[4,2,128,128]{3,2,1,0:T(8,128)(2,1)S(1)}, u32[]{:S(2)}, u32[]{:S(2)}) collective-permute-start(bf16[4,2,128,128]{3,2,1,0:T(8,128)(2,1)S(1)} %get-tuple-element.30), channel_id=1, source_target_pairs={{0,3},{1,2},{2,5},{3,4},{4,7},{5,6},{6,9},{7,8},{8,11},{9,10},{10,... | collective-permute-start | bytes 786440 | tf_op jit(solution)/shard_map/ppermute | solution.py:21
  11.5 3.1 %collective-permute-start.3 = (bf16[4,2,128,128]{3,2,1,0:T(8,128)(2,1)S(1)}, bf16[4,2,128,128]{3,2,1,0:T(8,128)(2,1)S(1)}, u32[]{:S(2)}, u32[]{:S(2)}) collective-permute-start(bf16[4,2,128,128]{3,2,1,0:T(8,128)(2,1)S(1)} %get-tuple-element.31.refs_0_), channel_id=1, source_target_pairs={{0,4},{1,5},{2,6},{3,7},{4,8},{5,9},{6,10},{7,11},{8,12},{9,13},{1... | collective-permute-start | bytes 786440 | tf_op jit(solution)/shard_map/ppermute | solution.py:21
  14.6 6.3 %collective-permute-done.4.refs_5_ = bf16[4,2,128,128]{3,2,1,0:T(8,128)(2,1)S(1)} collective-permute-done((bf16[4,2,128,128]{3,2,1,0:T(8,128)(2,1)S(1)}, bf16[4,2,128,128]{3,2,1,0:T(8,128)(2,1)S(1)}, u32[]{:S(2)}, u32[]{:S(2)}) %collective-permute-start.4) | collective-permute-done | bytes 262176 | tf_op jit(solution)/shard_map/ppermute | solution.py:21
  20.9 1.9 %collective-permute-start.1 = (bf16[4,2,128,128]{3,2,1,0:T(8,128)(2,1)S(1)}, bf16[4,2,128,128]{3,2,1,0:T(8,128)(2,1)S(1)}, u32[]{:S(2)}, u32[]{:S(2)}) collective-permute-start(bf16[4,2,128,128]{3,2,1,0:T(8,128)(2,1)S(1)} %get-tuple-element.31.refs_0_), channel_id=1, source_target_pairs={{0,2},{1,3},{2,4},{3,5},{4,6},{5,7},{6,8},{7,9},{8,10},{9,11},{10,... | collective-permute-start | bytes 786440 | tf_op jit(solution)/shard_map/ppermute | solution.py:21
  22.9 0.7 copy-done
  23.6 1.9 %collective-permute-done.3.refs_4_ = bf16[4,2,128,128]{3,2,1,0:T(8,128)(2,1)S(1)} collective-permute-done((bf16[4,2,128,128]{3,2,1,0:T(8,128)(2,1)S(1)}, bf16[4,2,128,128]{3,2,1,0:T(8,128)(2,1)S(1)}, u32[]{:S(2)}, u32[]{:S(2)}) %collective-permute-start.3) | collective-permute-done | bytes 262176 | tf_op jit(solution)/shard_map/ppermute | solution.py:21
  25.5 0.7 copy-done.2
  26.2 5.5 %collective-permute-done.1.refs_2_ = bf16[4,2,128,128]{3,2,1,0:T(8,128)(2,1)S(1)} collective-permute-done((bf16[4,2,128,128]{3,2,1,0:T(8,128)(2,1)S(1)}, bf16[4,2,128,128]{3,2,1,0:T(8,128)(2,1)S(1)}, u32[]{:S(2)}, u32[]{:S(2)}) %collective-permute-start.1) | collective-permute-done | bytes 262176 | tf_op jit(solution)/shard_map/ppermute | solution.py:21
  31.7 0.7 copy-done.4
  32.5 0.9 %copy-done.1 = bf16[4,2,128,128]{3,2,1,0:T(8,128)(2,1)S(1)} copy-done((bf16[4,2,128,128]{3,2,1,0:T(8,128)(2,1)S(1)}, bf16[4,2,128,128]{3,2,1,0:T(8,128)(2,1)}, u32[]{:S(2)}) %copy-start.1) | copy-done | bytes 262168
  33.4 0.9 %copy-done.3 = bf16[4,2,128,128]{3,2,1,0:T(8,128)(2,1)S(1)} copy-done((bf16[4,2,128,128]{3,2,1,0:T(8,128)(2,1)S(1)}, bf16[4,2,128,128]{3,2,1,0:T(8,128)(2,1)}, u32[]{:S(2)}) %copy-start.3) | copy-done | bytes 262168
  34.4 0.9 %copy-done.5 = bf16[4,2,128,128]{3,2,1,0:T(8,128)(2,1)S(1)} copy-done((bf16[4,2,128,128]{3,2,1,0:T(8,128)(2,1)S(1)}, bf16[4,2,128,128]{3,2,1,0:T(8,128)(2,1)}, u32[]{:S(2)}) %copy-start.5) | copy-done | bytes 262168
  35.3 15.1 %grads.1 = (f32[4,2,128,128]{3,2,1,0:T(8,128)S(1)}, bf16[4,2,128,128]{3,2,1,0:T(8,128)(2,1)}, bf16[4,2,128,128]{3,2,1,0:T(8,128)(2,1)}, bf16[4,2,128,128]{3,2,1,...) custom-call(s32[2]{0:T(128)S(1)} %pad_add_fusion.place_ref, ...), custom_call_target="tpu_custom_call" | custom-call | flops 3355443200 | bytes 8388608 | tf_op jit(solution)/shard_map/grads/pallas_call | solution.py:114
  50.4 1.9 %collective-permute-start.7 = (bf16[4,2,128,128]{3,2,1,0:T(8,128)(2,1)}, bf16[4,2,128,128]{3,2,1,0:T(8,128)(2,1)S(1)}, u32[]{:S(2)}, u32[]{:S(2)}) collective-permute-start(bf16[4,2,128,128]{3,2,1,0:T(8,128)(2,1)} %get-tuple-element.14), channel_id=1, source_target_pairs={{2,0},{3,1},{4,2},{5,3},{6,4},{7,5},{8,6},{9,7},{10,8},{11,9},{12,... | collective-permute-start | bytes 786440 | tf_op jit(solution)/shard_map/ppermute | solution.py:21
  52.3 1.9 %collective-permute-start.8 = (bf16[4,2,128,128]{3,2,1,0:T(8,128)(2,1)}, bf16[4,2,128,128]{3,2,1,0:T(8,128)(2,1)S(1)}, u32[]{:S(2)}, u32[]{:S(2)}) collective-permute-start(bf16[4,2,128,128]{3,2,1,0:T(8,128)(2,1)} %get-tuple-element.15), channel_id=1, source_target_pairs={{4,0},{5,1},{6,2},{7,3},{8,4},{9,5},{10,6},{11,7},{12,8},{13,9},{1... | collective-permute-start | bytes 786440 | tf_op jit(solution)/shard_map/ppermute | solution.py:21
  54.2 0.5 collective-permute-start.9
  54.7 1.9 %collective-permute-start.10 = (bf16[4,2,128,128]{3,2,1,0:T(8,128)(2,1)}, bf16[4,2,128,128]{3,2,1,0:T(8,128)(2,1)S(1)}, u32[]{:S(2)}, u32[]{:S(2)}) collective-permute-start(bf16[4,2,128,128]{3,2,1,0:T(8,128)(2,1)} %get-tuple-element.17), channel_id=1, source_target_pairs={{2,1},{3,0},{4,3},{5,2},{6,5},{7,4},{8,7},{9,6},{10,9},{11,8},{12,... | collective-permute-start | bytes 786440 | tf_op jit(solution)/shard_map/ppermute | solution.py:21
  56.6 1.9 %collective-permute-start.11 = (bf16[4,2,128,128]{3,2,1,0:T(8,128)(2,1)}, bf16[4,2,128,128]{3,2,1,0:T(8,128)(2,1)S(1)}, u32[]{:S(2)}, u32[]{:S(2)}) collective-permute-start(bf16[4,2,128,128]{3,2,1,0:T(8,128)(2,1)} %get-tuple-element.18), channel_id=1, source_target_pairs={{4,1},{5,0},{6,3},{7,2},{8,5},{9,4},{10,7},{11,6},{12,9},{13,8},{1... | collective-permute-start | bytes 786440 | tf_op jit(solution)/shard_map/ppermute | solution.py:21
  58.5 1.4 %collective-permute-done.7 = bf16[4,2,128,128]{3,2,1,0:T(8,128)(2,1)S(1)} collective-permute-done((bf16[4,2,128,128]{3,2,1,0:T(8,128)(2,1)}, bf16[4,2,128,128]{3,2,1,0:T(8,128)(2,1)S(1)}, u32[]{:S(2)}, u32[]{:S(2)}) %collective-permute-start.7) | collective-permute-done | bytes 262176 | tf_op jit(solution)/shard_map/ppermute | solution.py:21
  59.9 2.2 %collective-permute-start.6 = (bf16[4,4,128,128]{3,2,1,0:T(8,128)(2,1)S(1)}, bf16[4,4,128,128]{3,2,1,0:T(8,128)(2,1)S(1)}, u32[]{:S(2)}, u32[]{:S(2)}) collective-permute-start(bf16[4,4,128,128]{3,2,1,0:T(8,128)(2,1)S(1)} %get-tuple-element.12), channel_id=1, source_target_pairs={{0,1},{1,0},{2,3},{3,2},{4,5},{5,4},{6,7},{7,6},{8,9},{9,8},{10,11... | collective-permute-start | bytes 1572872 | tf_op jit(solution)/shard_map/ppermute | solution.py:21
  62.2 6.4 %collective-permute-done.8 = bf16[4,2,128,128]{3,2,1,0:T(8,128)(2,1)S(1)} collective-permute-done((bf16[4,2,128,128]{3,2,1,0:T(8,128)(2,1)}, bf16[4,2,128,128]{3,2,1,0:T(8,128)(2,1)S(1)}, u32[]{:S(2)}, u32[]{:S(2)}) %collective-permute-start.8) | collective-permute-done | bytes 262176 | tf_op jit(solution)/shard_map/ppermute | solution.py:21
  68.5 13.8 %collective-permute-done.11 = bf16[4,2,128,128]{3,2,1,0:T(8,128)(2,1)S(1)} collective-permute-done((bf16[4,2,128,128]{3,2,1,0:T(8,128)(2,1)}, bf16[4,2,128,128]{3,2,1,0:T(8,128)(2,1)S(1)}, u32[]{:S(2)}, u32[]{:S(2)}) %collective-permute-start.11) | collective-permute-done | bytes 262176 | tf_op jit(solution)/shard_map/ppermute | solution.py:21
  82.3 0.2 select_convert_fusion.1
  82.7 0.9 %copy.14 = bf16[128,8,128]{2,1,0:T(8,128)(2,1)} copy(bf16[128,8,128]{2,0,1:T(8,128)(2,1)S(1)} %get-tuple-element.28) | data formatting | bytes 524288
  83.6 0.9 %copy.13 = bf16[128,8,128]{2,1,0:T(8,128)(2,1)} copy(bf16[128,8,128]{2,0,1:T(8,128)(2,1)S(1)} %get-tuple-element.29) | data formatting | bytes 524288
  84.5 0.1 pad_maximum_fusion
  84.6 1.6 %copy.12 = bf16[128,32,128]{2,1,0:T(8,128)(2,1)} copy(bf16[128,32,128]{2,0,1:T(8,128)(2,1)S(1)} %bitcast.33) | data formatting | bytes 2097152
  (28 shorter events, 0.5 us)
Async XLA Ops:
  0.7 1.7 %copy-start.7 = (bf16[128,32,128]{2,1,0:T(8,128)(2,1)S(1)}, bf16[128,32,128]{2,1,0:T(8,128)(2,1)}, u32[]{:S(2)}) copy-start(bf16[128,32,128]{2,1,0:T(8,128)(2,1)} %param.8) | copy-start | bytes 3145732
  2.8 1.9 %copy-start.8 = (bf16[128,8,128]{2,1,0:T(8,128)(2,1)S(1)}, bf16[128,8,128]{2,1,0:T(8,128)(2,1)}, u32[]{:S(2)}) copy-start(bf16[128,8,128]{2,1,0:T(8,128)(2,1)} %param.6) | copy-start | bytes 786436
  2.8 1.9 %copy-start.9 = (bf16[128,8,128]{2,1,0:T(8,128)(2,1)S(1)}, bf16[128,8,128]{2,1,0:T(8,128)(2,1)}, u32[]{:S(2)}) copy-start(bf16[128,8,128]{2,1,0:T(8,128)(2,1)} %param.7) | copy-start | bytes 786436
  4.0 28.4 %copy-start.6 = (s32[16]{0:T(128)S(1)}, s32[16]{0:T(128)}, u32[]{:S(2)}) copy-start(s32[16]{0:T(128)} %lengths_ref.1) | copy-start | bytes 196
  4.0 28.4 %collective-permute-start.5 = (bf16[4,2,4,128,128]{4,3,2,1,0:T(8,128)(2,1)}, bf16[4,2,4,128,128]{4,3,2,1,0:T(8,128)(2,1)}, u32[]{:S(2)}, u32[]{:S(2)}) collective-permute-start(bf16[4,2,4,128,128]{4,3,2,1,0:T(8,128)(2,1)} %get-tuple-element.22), channel_id=1, source_target_pairs={{0,1},{1,0},{2,3},{3,2},{4,5},{5,4},{6,7},{7,6},{8,9},{9,8},{10,11... | collective-permute-start | bytes 3145736 | tf_op jit(solution)/shard_map/ppermute | solution.py:21
  4.8 16.1 %collective-permute-start.4 = (bf16[4,2,128,128]{3,2,1,0:T(8,128)(2,1)S(1)}, bf16[4,2,128,128]{3,2,1,0:T(8,128)(2,1)S(1)}, u32[]{:S(2)}, u32[]{:S(2)}) collective-permute-start(bf16[4,2,128,128]{3,2,1,0:T(8,128)(2,1)S(1)} %get-tuple-element.30), channel_id=1, source_target_pairs={{0,5},{1,4},{2,7},{3,6},{4,9},{5,8},{6,11},{7,10},{8,13},{9,12},{1... | collective-permute-start | bytes 786440 | tf_op jit(solution)/shard_map/ppermute | solution.py:21
  7.9 15.0 %collective-permute-start.2 = (bf16[4,2,128,128]{3,2,1,0:T(8,128)(2,1)S(1)}, bf16[4,2,128,128]{3,2,1,0:T(8,128)(2,1)S(1)}, u32[]{:S(2)}, u32[]{:S(2)}) collective-permute-start(bf16[4,2,128,128]{3,2,1,0:T(8,128)(2,1)S(1)} %get-tuple-element.30), channel_id=1, source_target_pairs={{0,3},{1,2},{2,5},{3,4},{4,7},{5,6},{6,9},{7,8},{8,11},{9,10},{10,... | collective-permute-start | bytes 786440 | tf_op jit(solution)/shard_map/ppermute | solution.py:21
  11.4 11.5 %collective-permute-start = (bf16[4,2,128,128]{3,2,1,0:T(8,128)(2,1)S(1)}, bf16[4,2,128,128]{3,2,1,0:T(8,128)(2,1)S(1)}, u32[]{:S(2)}, u32[]{:S(2)}) collective-permute-start(bf16[4,2,128,128]{3,2,1,0:T(8,128)(2,1)S(1)} %get-tuple-element.30), channel_id=1, source_target_pairs={{0,1},{1,0},{2,3},{3,2},{4,5},{5,4},{6,7},{7,6},{8,9},{9,8},{10,11... | collective-permute-start | bytes 786440 | tf_op jit(solution)/shard_map/ppermute | solution.py:21
  11.5 14.1 %collective-permute-start.3 = (bf16[4,2,128,128]{3,2,1,0:T(8,128)(2,1)S(1)}, bf16[4,2,128,128]{3,2,1,0:T(8,128)(2,1)S(1)}, u32[]{:S(2)}, u32[]{:S(2)}) collective-permute-start(bf16[4,2,128,128]{3,2,1,0:T(8,128)(2,1)S(1)} %get-tuple-element.31.refs_0_), channel_id=1, source_target_pairs={{0,4},{1,5},{2,6},{3,7},{4,8},{5,9},{6,10},{7,11},{8,12},{9,13},{1... | collective-permute-start | bytes 786440 | tf_op jit(solution)/shard_map/ppermute | solution.py:21
  20.9 10.8 %collective-permute-start.1 = (bf16[4,2,128,128]{3,2,1,0:T(8,128)(2,1)S(1)}, bf16[4,2,128,128]{3,2,1,0:T(8,128)(2,1)S(1)}, u32[]{:S(2)}, u32[]{:S(2)}) collective-permute-start(bf16[4,2,128,128]{3,2,1,0:T(8,128)(2,1)S(1)} %get-tuple-element.31.refs_0_), channel_id=1, source_target_pairs={{0,2},{1,3},{2,4},{3,5},{4,6},{5,7},{6,8},{7,9},{8,10},{9,11},{10,... | collective-permute-start | bytes 786440 | tf_op jit(solution)/shard_map/ppermute | solution.py:21
  22.9 0.7 copy-start
  25.5 0.7 copy-start.2
  31.7 0.7 copy-start.4
  32.5 1.0 %copy-start.1 = (bf16[4,2,128,128]{3,2,1,0:T(8,128)(2,1)S(1)}, bf16[4,2,128,128]{3,2,1,0:T(8,128)(2,1)}, u32[]{:S(2)}) copy-start(bf16[4,2,128,128]{3,2,1,0:T(8,128)(2,1)} %copy-done) | copy-start | bytes 786436
  33.4 0.9 %copy-start.3 = (bf16[4,2,128,128]{3,2,1,0:T(8,128)(2,1)S(1)}, bf16[4,2,128,128]{3,2,1,0:T(8,128)(2,1)}, u32[]{:S(2)}) copy-start(bf16[4,2,128,128]{3,2,1,0:T(8,128)(2,1)} %copy-done.2) | copy-start | bytes 786436
  34.4 0.9 %copy-start.5 = (bf16[4,2,128,128]{3,2,1,0:T(8,128)(2,1)S(1)}, bf16[4,2,128,128]{3,2,1,0:T(8,128)(2,1)}, u32[]{:S(2)}) copy-start(bf16[4,2,128,128]{3,2,1,0:T(8,128)(2,1)} %copy-done.4) | copy-start | bytes 786436
  50.4 9.5 %collective-permute-start.7 = (bf16[4,2,128,128]{3,2,1,0:T(8,128)(2,1)}, bf16[4,2,128,128]{3,2,1,0:T(8,128)(2,1)S(1)}, u32[]{:S(2)}, u32[]{:S(2)}) collective-permute-start(bf16[4,2,128,128]{3,2,1,0:T(8,128)(2,1)} %get-tuple-element.14), channel_id=1, source_target_pairs={{2,0},{3,1},{4,2},{5,3},{6,4},{7,5},{8,6},{9,7},{10,8},{11,9},{12,... | collective-permute-start | bytes 786440 | tf_op jit(solution)/shard_map/ppermute | solution.py:21
  52.3 16.2 %collective-permute-start.8 = (bf16[4,2,128,128]{3,2,1,0:T(8,128)(2,1)}, bf16[4,2,128,128]{3,2,1,0:T(8,128)(2,1)S(1)}, u32[]{:S(2)}, u32[]{:S(2)}) collective-permute-start(bf16[4,2,128,128]{3,2,1,0:T(8,128)(2,1)} %get-tuple-element.15), channel_id=1, source_target_pairs={{4,0},{5,1},{6,2},{7,3},{8,4},{9,5},{10,6},{11,7},{12,8},{13,9},{1... | collective-permute-start | bytes 786440 | tf_op jit(solution)/shard_map/ppermute | solution.py:21
  54.2 14.3 %collective-permute-start.9 = (bf16[4,2,128,128]{3,2,1,0:T(8,128)(2,1)}, bf16[4,2,128,128]{3,2,1,0:T(8,128)(2,1)S(1)}, u32[]{:S(2)}, u32[]{:S(2)}) collective-permute-start(bf16[4,2,128,128]{3,2,1,0:T(8,128)(2,1)} %get-tuple-element.16), channel_id=1, source_target_pairs={{0,1},{1,0},{2,3},{3,2},{4,5},{5,4},{6,7},{7,6},{8,9},{9,8},{10,11... | collective-permute-start | bytes 786440 | tf_op jit(solution)/shard_map/ppermute | solution.py:21
  54.7 13.9 %collective-permute-start.10 = (bf16[4,2,128,128]{3,2,1,0:T(8,128)(2,1)}, bf16[4,2,128,128]{3,2,1,0:T(8,128)(2,1)S(1)}, u32[]{:S(2)}, u32[]{:S(2)}) collective-permute-start(bf16[4,2,128,128]{3,2,1,0:T(8,128)(2,1)} %get-tuple-element.17), channel_id=1, source_target_pairs={{2,1},{3,0},{4,3},{5,2},{6,5},{7,4},{8,7},{9,6},{10,9},{11,8},{12,... | collective-permute-start | bytes 786440 | tf_op jit(solution)/shard_map/ppermute | solution.py:21
  56.6 25.7 %collective-permute-start.11 = (bf16[4,2,128,128]{3,2,1,0:T(8,128)(2,1)}, bf16[4,2,128,128]{3,2,1,0:T(8,128)(2,1)S(1)}, u32[]{:S(2)}, u32[]{:S(2)}) collective-permute-start(bf16[4,2,128,128]{3,2,1,0:T(8,128)(2,1)} %get-tuple-element.18), channel_id=1, source_target_pairs={{4,1},{5,0},{6,3},{7,2},{8,5},{9,4},{10,7},{11,6},{12,9},{13,8},{1... | collective-permute-start | bytes 786440 | tf_op jit(solution)/shard_map/ppermute | solution.py:21
  59.9 24.5 %collective-permute-start.6 = (bf16[4,4,128,128]{3,2,1,0:T(8,128)(2,1)S(1)}, bf16[4,4,128,128]{3,2,1,0:T(8,128)(2,1)S(1)}, u32[]{:S(2)}, u32[]{:S(2)}) collective-permute-start(bf16[4,4,128,128]{3,2,1,0:T(8,128)(2,1)S(1)} %get-tuple-element.12), channel_id=1, source_target_pairs={{0,1},{1,0},{2,3},{3,2},{4,5},{5,4},{6,7},{7,6},{8,9},{9,8},{10,11... | collective-permute-start | bytes 1572872 | tf_op jit(solution)/shard_map/ppermute | solution.py:21

commit v2 on v1

v2 whole, which is shorter than its diff:
```python
import functools

import jax
import jax.numpy as jnp
from jax import lax
from jax.experimental import pallas as pl
from jax.experimental.pallas import tpu as pltpu
from jax.sharding import PartitionSpec as P

AXES = ("ctx", "uly")
LOG2E = 1.4426950408889634
MASKED = -1e30
BF16, F32 = jnp.bfloat16, jnp.float32
NT = (((1,), (1,)), ((), ()))
VMEM_BYTES = 40 * 2**20


def moved(array, device_count, by):
    pairs = [(d, d + by) for d in range(device_count) if 0 <= d + by < device_count]
    return lax.ppermute(array, AXES, pairs)


def swapped(array, device_count):
    return lax.ppermute(array, AXES, [(d, d ^ 1) for d in range(device_count)])


def call(kernel, name, grid, place, inputs, in_specs, outs, out_specs, scratch, flops):
    scalars = place if isinstance(place, tuple) else (place,)
    return pl.pallas_call(
        kernel,
        out_shape=outs,
        grid_spec=pltpu.PrefetchScalarGridSpec(
            num_scalar_prefetch=len(scalars),
            grid=grid,
            in_specs=in_specs,
            out_specs=out_specs,
            scratch_shapes=scratch,
        ),
        compiler_params=pltpu.CompilerParams(vmem_limit_bytes=VMEM_BYTES),
        cost_estimate=pl.CostEstimate(flops=flops, bytes_accessed=2**20, transcendentals=0),
        name=name,
    )(*scalars, *inputs)


def arrange_kernel(group, place_ref, q_ref, do_ref, q_other_ref, do_other_ref, out_ref, scr):
    core = place_ref[0]
    rows, heads, dim = q_ref.shape
    for kind, (own, other) in enumerate([(q_ref, q_other_ref), (do_ref, do_other_ref)]):
        for which, ref in enumerate([own, other]):
            block = 1 - core if which else core
            scr[...] = ref[...].astype(F32).reshape(rows * heads, dim)
            for h in range(heads):
                out_ref[h // group, block, kind, h % group] = scr[pl.ds(h, rows, stride=heads), :].astype(BF16)


def arrange(place, queries, grad_out, q_other, do_other, key_heads):
    tokens, heads, dim = queries.shape
    half, group = heads // 2, heads // key_heads
    rows = 32
    in_spec = pl.BlockSpec((rows, half, dim), lambda i, place: (i, place[0], 0))
    out = (key_heads // 2, 2, 2, group, tokens, dim)
    return call(
        functools.partial(arrange_kernel, group),
        "arrange",
        (tokens // rows,),
        place,
        (queries, grad_out, q_other, do_other),
        [in_spec] * 4,
        jax.ShapeDtypeStruct(out, BF16),
        pl.BlockSpec(out[:4] + (rows, dim), lambda i, place: (0, 0, 0, 0, i, 0)),
        [pltpu.VMEM((rows * half, dim), F32)],
        10**9,
    )


def spread(block_refs, core, wide):
    tokens, heads, dim = block_refs[0].shape
    halo = len(block_refs) // 2 - 1
    for back in range(halo + 1):
        at = 2 * (halo - back)
        wide[at + core] = block_refs[2 * back][...].astype(F32).reshape(tokens * heads, dim)
        wide[at + 1 - core] = block_refs[2 * back + 1][...].astype(F32).reshape(tokens * heads, dim)


def one_head(wide, core, heads, narrow):
    head = core * (heads // 2) + pl.program_id(0)
    for r in range(narrow.shape[0]):
        narrow[r] = wide[r, pl.ds(head, narrow.shape[1], stride=heads), :].astype(BF16)


def first_allowed(lengths_ref, query_pos, window_start):
    def step(d, carry):
        start, first = carry
        first = jnp.where(query_pos + window_start >= start, start, first)
        return start + lengths_ref[d], first

    zero = jnp.zeros(query_pos.shape, jnp.int32)
    _, first = lax.fori_loop(0, lengths_ref.shape[0], step, (jnp.int32(0), zero))
    return first - window_start


def prob_kernel(halo, place_ref, lengths_ref, qd_ref, *refs):
    blocks = refs[: 2 * (halo + 1)]
    k_out, p_ref = refs[2 * (halo + 1) : 2 * (halo + 1) + 2]
    dv_refs = refs[2 * (halo + 1) + 2 : -2]
    wide, acc = refs[-2:]
    core, window_start = place_ref[0], place_ref[1]
    tokens, heads, dim = blocks[0].shape
    _, _, _, group, _, _ = qd_ref.shape
    count = 2 * halo + 1

    @pl.when(pl.program_id(0) == 0)
    def _():
        spread(blocks, core, wide)

    one_head(wide, core, heads, k_out.at[0])
    pair = 2 * tokens
    lane = lax.broadcasted_iota(jnp.int32, (1, pair), 1) % tokens
    row = lax.broadcasted_iota(jnp.int32, (tokens, pair), 0)
    for e in range(2):
        query_pos = lane + (2 * halo + e) * tokens
        first = first_allowed(lengths_ref, query_pos, window_start)
        k = k_out[0, pl.ds(e, count)].reshape(count * tokens, dim)
        q = qd_ref[0, e, 0].reshape(group * tokens, dim)
        do = qd_ref[0, e, 1].reshape(group * tokens, dim)
        for at in range(0, group * tokens, pair):
            s = lax.dot_general(k, q[at : at + pair], NT, preferred_element_type=F32)
            tiles = []
            for j in range(count):
                key_pos = row + (e + j) * tokens
                allowed = key_pos >= first
                if j == count - 1:
                    allowed &= key_pos <= query_pos
                tiles.append(jnp.where(allowed, s[j * tokens : (j + 1) * tokens], MASKED))
            s = jnp.concatenate(tiles, axis=0)
            top = jnp.max(s, axis=0, keepdims=True)
            w = jnp.exp2((s - top) * (dim**-0.5 * LOG2E))
            inv = 1.0 / jnp.sum(w, axis=0, keepdims=True)
            p_ref[0, e, :, at : at + pair] = (w * inv).astype(BF16)
        keep = (2 * halo - e) * tokens
        dv = jnp.dot(p_ref[0, e, :keep], do, preferred_element_type=F32).reshape(2 * halo - e, tokens, dim)
        if e == 0:
            acc[...] = dv
        else:
            acc[1:] += dv
    for back, ref in zip(range(1, halo + 1), dv_refs):
        ref[0] = acc[pl.ds(2 * (halo - back), 2)].astype(BF16)


def dscore_kernel(halo, place_ref, qd_ref, p_ref, *refs):
    blocks = refs[: 2 * (halo + 1)]
    ds_ref = refs[2 * (halo + 1)]
    dk_refs = refs[2 * (halo + 1) + 1 : -3]
    wide, narrow, acc = refs[-3:]
    core = place_ref[0]
    tokens, heads, dim = blocks[0].shape
    _, _, _, group, _, _ = qd_ref.shape
    count = 2 * halo + 1

    @pl.when(pl.program_id(0) == 0)
    def _():
        spread(blocks, core, wide)

    one_head(wide, core, heads, narrow)
    pair = 2 * tokens
    for e in range(2):
        v = narrow[pl.ds(e, count)].reshape(count * tokens, dim)
        q = qd_ref[0, e, 0].reshape(group * tokens, dim)
        do = qd_ref[0, e, 1].reshape(group * tokens, dim)
        for at in range(0, group * tokens, pair):
            dp = lax.dot_general(v, do[at : at + pair], NT, preferred_element_type=F32)
            p = p_ref[0, e, :, at : at + pair].astype(F32)
            delta = jnp.sum(p * dp, axis=0, keepdims=True)
            ds_ref[0, e, :, at : at + pair] = (p * (dp - delta)).astype(BF16)
        keep = (2 * halo - e) * tokens
        dk = jnp.dot(ds_ref[0, e, :keep], q, preferred_element_type=F32).reshape(2 * halo - e, tokens, dim)
        if e == 0:
            acc[...] = dk
        else:
            acc[1:] += dk
    for back, ref in zip(range(1, halo + 1), dk_refs):
        ref[0] = (acc[pl.ds(2 * (halo - back), 2)] * dim**-0.5).astype(BF16)


def own_kernel(halo, place_ref, qd_ref, k_ref, p_ref, ds_ref, dq_ref, dq_other_ref, dk_ref, dv_ref, scr):
    core = place_ref[0]
    _, _, _, group, tokens, dim = qd_ref.shape
    count = 2 * halo + 1
    scale = dim**-0.5
    for e in range(2):
        q = qd_ref[0, e, 0].reshape(group * tokens, dim)
        do = qd_ref[0, e, 1].reshape(group * tokens, dim)
        k = k_ref[0, pl.ds(e, count)].reshape(count * tokens, dim)
        dqt = jnp.dot(k.T, ds_ref[0, e], preferred_element_type=F32) * scale
        for g in range(group):
            scr[e, g] = dqt[:, g * tokens : (g + 1) * tokens].T.astype(BF16)
        keep = (2 * halo - e) * tokens
        dk = jnp.dot(ds_ref[0, e, keep:], q, preferred_element_type=F32) * scale
        dv = jnp.dot(p_ref[0, e, keep:], do, preferred_element_type=F32)
        if e == 0:
            dk_ref[0, 0], dv_ref[0, 0] = dk, dv
        else:
            dk_ref[0, 0] += dk[:tokens]
            dv_ref[0, 0] += dv[:tokens]
            dk_ref[0, 1], dv_ref[0, 1] = dk[tokens:], dv[tokens:]
    dq_ref[0] = scr[core]
    dq_other_ref[0] = scr[1 - core]


def merge_kernel(place_ref, own_ref, other_ref, out_ref, scr):
    core = place_ref[0]
    rows, heads, dim = out_ref.shape
    half = heads // 2
    for which, ref in enumerate([own_ref, other_ref]):
        side = 1 - core if which else core
        for h in range(half):
            scr[pl.ds(side * half + h, rows, stride=heads), :] = ref[h].astype(F32)
    out_ref[...] = scr[...].astype(BF16).reshape(rows, heads, dim)


def merge(place, own, other, rows, name):
    half, tokens, dim = own.shape
    in_spec = pl.BlockSpec((half, rows, dim), lambda i, place: (0, i, 0))
    return call(
        merge_kernel,
        name,
        (tokens // rows,),
        place,
        (own, other),
        [in_spec] * 2,
        jax.ShapeDtypeStruct((tokens, 2 * half, dim), BF16),
        pl.BlockSpec((rows, 2 * half, dim), lambda i, place: (i, 0, 0)),
        [pltpu.VMEM((rows * 2 * half, dim), F32)],
        10**9,
    )


def local(queries, keys, values, grad_out, doc_lengths):
    uly_count = lax.axis_size("uly")
    device_count = lax.axis_size("ctx") * uly_count
    halo = uly_count // 2
    device = lax.axis_index("ctx") * uly_count + lax.axis_index("uly")
    core = device % 2
    tokens, heads, dim = queries.shape
    key_heads = keys.shape[1]
    group = heads // key_heads
    half = key_heads // 2
    window, count = 2 * halo + 2, 2 * halo + 1
    place = jnp.stack([core, (device // 2 - halo) * (2 * tokens)]).astype(jnp.int32)

    far_first = range(halo, 0, -1)
    k_halo = {back: moved(keys, device_count, 2 * back) for back in far_first}
    v_halo = {back: moved(values, device_count, 2 * back) for back in far_first}

    def all_blocks(own, halos):
        blocks = [own, swapped(own, device_count)]
        for back in range(1, halo + 1):
            blocks += [halos[back], swapped(halos[back], device_count)]
        return blocks

    qd = arrange(
        place, queries, grad_out, swapped(queries, device_count), swapped(grad_out, device_count), key_heads
    )

    def per_head(*shape):
        return pl.BlockSpec((1,) + shape, lambda h, *_: (h,) + (0,) * len(shape))

    raw_spec = pl.BlockSpec(keys.shape, lambda h, *_: (0, 0, 0))
    qd_spec = per_head(2, 2, group, tokens, dim)
    k_spec = per_head(window, tokens, dim)
    p_spec = per_head(2, count * tokens, group * tokens)
    pair_spec = per_head(2, tokens, dim)
    p_shape = jax.ShapeDtypeStruct((half, 2, count * tokens, group * tokens), BF16)
    pair = (half, 2, tokens, dim)
    wide = pltpu.VMEM((window, tokens * key_heads, dim), F32)
    acc = pltpu.VMEM((2 * halo, tokens, dim), F32)
    product = 2 * half * 2 * count * tokens * group * tokens * dim

    k_arranged, prob, *dv_halo = call(
        functools.partial(prob_kernel, halo),
        "prob",
        (half,),
        (place, doc_lengths),
        (qd, *all_blocks(keys, k_halo)),
        [qd_spec] + [raw_spec] * window,
        [jax.ShapeDtypeStruct((half, window, tokens, dim), BF16), p_shape] + [jax.ShapeDtypeStruct(pair, BF16)] * halo,
        [k_spec, p_spec] + [pair_spec] * halo,
        [wide, acc],
        4 * product,
    )
    dv_back = [moved(dv_halo[back - 1], device_count, -2 * back) for back in far_first]
    dscore, *dk_halo = call(
        functools.partial(dscore_kernel, halo),
        "dscore",
        (half,),
        place,
        (qd, prob, *all_blocks(values, v_halo)),
        [qd_spec, p_spec] + [raw_spec] * window,
        [p_shape] + [jax.ShapeDtypeStruct(pair, BF16)] * halo,
        [p_spec] + [pair_spec] * halo,
        [wide, pltpu.VMEM((window, tokens, dim), BF16), acc],
        4 * product,
    )
    dk_back = [moved(dk_halo[back - 1], device_count, -2 * back) for back in far_first]
    dq_spec = per_head(group, tokens, dim)
    dq_shape = jax.ShapeDtypeStruct((half, group, tokens, dim), BF16)
    dq, dq_other, dk_own, dv_own = call(
        functools.partial(own_kernel, halo),
        "own",
        (half,),
        place,
        (qd, k_arranged, prob, dscore),
        [qd_spec, k_spec, p_spec, p_spec],
        [dq_shape] * 2 + [jax.ShapeDtypeStruct(pair, F32)] * 2,
        [dq_spec] * 2 + [pair_spec] * 2,
        [pltpu.VMEM((2, group, tokens, dim), BF16)],
        4 * product,
    )
    dq_other = swapped(dq_other, device_count)
    flat = (half * group, tokens, dim)
    grad_queries = merge(place, dq.reshape(flat), dq_other.reshape(flat), 32, "merge_dq")

    def summed(own, backs, name):
        total = own
        for back in backs:
            total = total + back.astype(F32)
        total = total.astype(BF16)
        mine = lax.dynamic_index_in_dim(total, core, 1, keepdims=False)
        other = lax.dynamic_index_in_dim(total, 1 - core, 1, keepdims=False)
        return merge(place, mine, swapped(other, device_count), tokens, name)

    grad_values = summed(dv_own, dv_back, "merge_dv")
    grad_keys = summed(dk_own, dk_back, "merge_dk")
    return grad_queries, grad_keys, grad_values


def solution(mesh):
    spec = P(AXES, None, None)
    return jax.shard_map(
        local, mesh=mesh, in_specs=(spec,) * 4 + (P(),), out_specs=(spec,) * 3, check_vma=False
    )
```

time: 86.7 us -> 104 us (1.20)
  the two profiles are of different devices: /device:TPU:5 before, /device:TPU:23 now
where the time goes in v2:
time: 104 us
  Pallas kernels  33.9 us (33%)
  starting transfers between devices  33 us (32%)
  waiting for transfers between devices  22.1 us (21%)
  local copies, waits for them, and re-layouts  12.6 us (12%)
  other arithmetic  1.31 us (1%)
    pallas_call x7, Pallas kernels, call(): pl.pallas_call(kernel, out_shape=outs, grid_spec=pltpu.PrefetchScalarGrid...  33.9 us
    ppermute x8, starting transfers between devices, moved(): return lax.ppermute(array, AXES, pairs)  25.5 us
    ppermute x8, waiting for transfers between devices, moved(): return lax.ppermute(array, AXES, pairs)  21.2 us
    unnamed x24, local copies, waits for them, and re-layouts  12.6 us
    ppermute x11, starting transfers between devices, swapped(): return lax.ppermute(array, AXES, [(d, d ^ 1) for d in range(device_count)])  7.47 us
  transfers between devices with their start and end apart: 19, of which 7 were waited for; matrix products, arithmetic and copies ran while one was open for 1% of the time, Pallas kernels for 21%

profile of v2, /device:TPU:23, one launch (start us, length us, event | category | flops | bytes accessed | tf_op | source)
XLA Modules:
  0.0 103.7 jit_solution(3077158573323059688)
XLA Ops:
  1.5 3.1 %collective-permute-start.3 = (bf16[128,8,128]{2,1,0:T(8,128)(2,1)}, bf16[128,8,128]{2,1,0:T(8,128)(2,1)}, u32[]{:S(2)}, u32[]{:S(2)}) collective-permute-start(bf16[128,8,128]{2,1,0:T(8,128)(2,1)} %refs_0_.2), channel_id=1, source_target_pairs={{0,2},{1,3},{2,4},{3,5},{4,6},{5,7},{6,8},{7,9},{8,10},{9,11},{10,... | collective-permute-start | bytes 786440 | tf_op jit(solution)/shard_map/ppermute | solution.py:20
  4.6 3.2 %collective-permute-start.5 = (bf16[128,8,128]{2,1,0:T(8,128)(2,1)}, bf16[128,8,128]{2,1,0:T(8,128)(2,1)}, u32[]{:S(2)}, u32[]{:S(2)}) collective-permute-start(bf16[128,8,128]{2,1,0:T(8,128)(2,1)} %refs_0_.2), channel_id=1, source_target_pairs={{0,4},{1,5},{2,6},{3,7},{4,8},{5,9},{6,10},{7,11},{8,12},{9,13},{1... | collective-permute-start | bytes 786440 | tf_op jit(solution)/shard_map/ppermute | solution.py:20
  7.7 1.1 %collective-permute-start.2 = (bf16[128,8,128]{2,1,0:T(8,128)(2,1)}, bf16[128,8,128]{2,1,0:T(8,128)(2,1)S(1)}, u32[]{:S(2)}, u32[]{:S(2)}) collective-permute-start(bf16[128,8,128]{2,1,0:T(8,128)(2,1)} %refs_0_.2), channel_id=1, source_target_pairs={{0,1},{1,0},{2,3},{3,2},{4,5},{5,4},{6,7},{7,6},{8,9},{9,8},{10,11... | collective-permute-start | bytes 786440 | tf_op jit(solution)/shard_map/ppermute | solution.py:24
  8.8 2.3 %collective-permute-done.3.refs_2_ = bf16[128,8,128]{2,1,0:T(8,128)(2,1)} collective-permute-done((bf16[128,8,128]{2,1,0:T(8,128)(2,1)}, bf16[128,8,128]{2,1,0:T(8,128)(2,1)}, u32[]{:S(2)}, u32[]{:S(2)}) %collective-permute-start.3) | collective-permute-done | bytes 262176 | tf_op jit(solution)/shard_map/ppermute | solution.py:20
  11.1 3.1 %collective-permute-start.10 = (bf16[128,8,128]{2,1,0:T(8,128)(2,1)}, bf16[128,8,128]{2,1,0:T(8,128)(2,1)S(1)}, u32[]{:S(2)}, u32[]{:S(2)}) collective-permute-start(bf16[128,8,128]{2,1,0:T(8,128)(2,1)} %refs_0_.3), channel_id=1, source_target_pairs={{0,4},{1,5},{2,6},{3,7},{4,8},{5,9},{6,10},{7,11},{8,12},{9,13},{1... | collective-permute-start | bytes 786440 | tf_op jit(solution)/shard_map/ppermute | solution.py:20
  14.3 2.0 %collective-permute-done.5.refs_4_ = bf16[128,8,128]{2,1,0:T(8,128)(2,1)} collective-permute-done((bf16[128,8,128]{2,1,0:T(8,128)(2,1)}, bf16[128,8,128]{2,1,0:T(8,128)(2,1)}, u32[]{:S(2)}, u32[]{:S(2)}) %collective-permute-start.5) | collective-permute-done | bytes 262176 | tf_op jit(solution)/shard_map/ppermute | solution.py:20
  16.2 5.1 %collective-permute-start.8 = (bf16[128,8,128]{2,1,0:T(8,128)(2,1)}, bf16[128,8,128]{2,1,0:T(8,128)(2,1)}, u32[]{:S(2)}, u32[]{:S(2)}) collective-permute-start(bf16[128,8,128]{2,1,0:T(8,128)(2,1)} %refs_0_.3), channel_id=1, source_target_pairs={{0,2},{1,3},{2,4},{3,5},{4,6},{5,7},{6,8},{7,9},{8,10},{9,11},{10,... | collective-permute-start | bytes 786440 | tf_op jit(solution)/shard_map/ppermute | solution.py:20
  22.1 1.8 %collective-permute-start.4 = (bf16[128,8,128]{2,1,0:T(8,128)(2,1)}, bf16[128,8,128]{2,1,0:T(8,128)(2,1)}, u32[]{:S(2)}, u32[]{:S(2)}) collective-permute-start(bf16[128,8,128]{2,1,0:T(8,128)(2,1)} %collective-permute-done.3.refs_2_), channel_id=1, source_target_pairs={{0,1},{1,0},{2,3},{3,2},{4,5},{5,4},{6,7},{7,6},{8,9},{9,8},{10,11... | collective-permute-start | bytes 786440 | tf_op jit(solution)/shard_map/ppermute | solution.py:24
  24.0 3.4 %collective-permute-done.8.refs_2_ = bf16[128,8,128]{2,1,0:T(8,128)(2,1)} collective-permute-done((bf16[128,8,128]{2,1,0:T(8,128)(2,1)}, bf16[128,8,128]{2,1,0:T(8,128)(2,1)}, u32[]{:S(2)}, u32[]{:S(2)}) %collective-permute-start.8) | collective-permute-done | bytes 262176 | tf_op jit(solution)/shard_map/ppermute | solution.py:20
  27.4 1.9 %collective-permute-start.7 = (bf16[128,8,128]{2,1,0:T(8,128)(2,1)}, bf16[128,8,128]{2,1,0:T(8,128)(2,1)S(1)}, u32[]{:S(2)}, u32[]{:S(2)}) collective-permute-start(bf16[128,8,128]{2,1,0:T(8,128)(2,1)} %refs_0_.3), channel_id=1, source_target_pairs={{0,1},{1,0},{2,3},{3,2},{4,5},{5,4},{6,7},{7,6},{8,9},{9,8},{10,11... | collective-permute-start | bytes 786440 | tf_op jit(solution)/shard_map/ppermute | solution.py:24
  29.4 1.0 copy-done.5
  30.8 1.2 %copy-done.3 = bf16[128,32,128]{2,1,0:T(8,128)(2,1)S(1)} copy-done((bf16[128,32,128]{2,1,0:T(8,128)(2,1)S(1)}, bf16[128,32,128]{2,1,0:T(8,128)(2,1)}, u32[]{:S(2)}) %copy-start.3) | copy-done | bytes 1048600
  32.1 1.2 %copy-done.4 = bf16[128,32,128]{2,1,0:T(8,128)(2,1)S(1)} copy-done((bf16[128,32,128]{2,1,0:T(8,128)(2,1)S(1)}, bf16[128,32,128]{2,1,0:T(8,128)(2,1)}, u32[]{:S(2)}) %copy-start.4) | copy-done | bytes 1048600
  33.3 1.2 %copy-done.6 = bf16[128,32,128]{2,1,0:T(8,128)(2,1)S(1)} copy-done((bf16[128,32,128]{2,1,0:T(8,128)(2,1)S(1)}, bf16[128,32,128]{2,1,0:T(8,128)(2,1)}, u32[]{:S(2)}) %copy-start.6) | copy-done | bytes 1048600
  34.5 2.5 %arrange.1.qd_ref = bf16[4,2,2,4,128,128]{5,4,3,2,1,0:T(8,128)(2,1)S(1)} custom-call(s32[2]{0:T(128)S(1)} %pad_add_fusion.place_ref, bf16[128,32,128]{2,1,0:T(8,128)(2,1)S(1)} %copy-done.3, bf16[128,32,128]{2,1,0:T(8,128)(2,1)S(1)} %copy-done.4, bf16[128,32,128]{2,1,0:T(8,128)(2,1)S(1)} %collective-permute-done.q_other_ref, bf16[128,32,128]{2,1,0:T(8,128)(2,1)S(1)} %copy-done.6), custom_call_target="tpu_custom_call" | custom-call | flops 1000000000 | bytes 1048576 | tf_op jit(solution)/shard_map/arrange/pallas_call | solution.py:29
  37.1 11.4 %prob.1 = (bf16[4,6,128,128]{3,2,1,0:T(8,128)(2,1)S(1)}, bf16[4,2,640,512]{3,2,1,0:T(8,128)(2,1)S(1)}, bf16[4,2,128,128]{3,2,1,0:T(8,128)(2,1)}, bf16[4,2,128,128]{3,2,1,0:T(8,128)(2,1)}) custom-call(s32[2]{0:T(128)S(1)} %pad_add_fusion.place_ref, s32[16]{0:T(128)S(1)} %copy-done.11, bf16[4,2,2,4,128,128]{5,4,3,2,1,0:T(8,128)(2,1)S(1)} %arrange.1.qd_ref, ...), custom_call_target="tpu_custom_call" | custom-call | flops 2684354560 | bytes 1048576 | tf_op jit(solution)/shard_map/prob/pallas_call | solution.py:29
  48.5 2.3 %copy-done = bf16[4,2,640,512]{3,2,1,0:T(8,128)(2,1)} copy-done((bf16[4,2,640,512]{3,2,1,0:T(8,128)(2,1)}, bf16[4,2,640,512]{3,2,1,0:T(8,128)(2,1)S(1)}, u32[]{:S(2)}) %copy-start) | copy-done | bytes 5242904
  50.8 8.5 %dscore.1 = (bf16[4,2,640,512]{3,2,1,0:T(8,128)(2,1)S(1)}, bf16[4,2,128,128]{3,2,1,0:T(8,128)(2,1)}, bf16[4,2,128,128]{3,2,1,0:T(8,128)(2,1)}) custom-call(s32[2]{0:T(128)S(1)} %pad_add_fusion.place_ref, bf16[4,2,2,4,128,128]{5,4,3,2,1,0:T(8,128)(2,1)S(1)} %arrange.1.qd_ref, bf16[4,2,640,512]{3,2,1,0:T(8,128)(2,1)} %copy-done, ...), custom_call_target="tpu_custom_call" | custom-call | flops 2684354560 | bytes 1048576 | tf_op jit(solution)/shard_map/dscore/pallas_call | solution.py:29
  59.3 2.4 %copy-done.2 = bf16[4,2,640,512]{3,2,1,0:T(8,128)(2,1)} copy-done((bf16[4,2,640,512]{3,2,1,0:T(8,128)(2,1)}, bf16[4,2,640,512]{3,2,1,0:T(8,128)(2,1)S(1)}, u32[]{:S(2)}) %copy-start.2) | copy-done | bytes 5242904
  61.7 1.9 %collective-permute-start.13 = (bf16[4,2,128,128]{3,2,1,0:T(8,128)(2,1)}, bf16[4,2,128,128]{3,2,1,0:T(8,128)(2,1)S(1)}, u32[]{:S(2)}, u32[]{:S(2)}) collective-permute-start(bf16[4,2,128,128]{3,2,1,0:T(8,128)(2,1)} %get-tuple-element.20), channel_id=1, source_target_pairs={{4,0},{5,1},{6,2},{7,3},{8,4},{9,5},{10,6},{11,7},{12,8},{13,9},{1... | collective-permute-start | bytes 786440 | tf_op jit(solution)/shard_map/ppermute | solution.py:20
  63.6 5.3 %collective-permute-start.14 = (bf16[4,2,128,128]{3,2,1,0:T(8,128)(2,1)}, bf16[4,2,128,128]{3,2,1,0:T(8,128)(2,1)S(1)}, u32[]{:S(2)}, u32[]{:S(2)}) collective-permute-start(bf16[4,2,128,128]{3,2,1,0:T(8,128)(2,1)} %get-tuple-element.21), channel_id=1, source_target_pairs={{2,0},{3,1},{4,2},{5,3},{6,4},{7,5},{8,6},{9,7},{10,8},{11,9},{12,... | collective-permute-start | bytes 786440 | tf_op jit(solution)/shard_map/ppermute | solution.py:20
  68.9 1.9 %collective-permute-start.16 = (bf16[4,2,128,128]{3,2,1,0:T(8,128)(2,1)}, bf16[4,2,128,128]{3,2,1,0:T(8,128)(2,1)}, u32[]{:S(2)}, u32[]{:S(2)}) collective-permute-start(bf16[4,2,128,128]{3,2,1,0:T(8,128)(2,1)} %get-tuple-element.23), channel_id=1, source_target_pairs={{4,0},{5,1},{6,2},{7,3},{8,4},{9,5},{10,6},{11,7},{12,8},{13,9},{1... | collective-permute-start | bytes 786440 | tf_op jit(solution)/shard_map/ppermute | solution.py:20
  70.8 1.9 %collective-permute-start.17 = (bf16[4,2,128,128]{3,2,1,0:T(8,128)(2,1)}, bf16[4,2,128,128]{3,2,1,0:T(8,128)(2,1)}, u32[]{:S(2)}, u32[]{:S(2)}) collective-permute-start(bf16[4,2,128,128]{3,2,1,0:T(8,128)(2,1)} %get-tuple-element.24), channel_id=1, source_target_pairs={{2,0},{3,1},{4,2},{5,3},{6,4},{7,5},{8,6},{9,7},{10,8},{11,9},{12,... | collective-permute-start | bytes 786440 | tf_op jit(solution)/shard_map/ppermute | solution.py:20
  72.8 2.5 %copy-done.1 = bf16[4,2,640,512]{3,2,1,0:T(8,128)(2,1)S(1)} copy-done((bf16[4,2,640,512]{3,2,1,0:T(8,128)(2,1)S(1)}, bf16[4,2,640,512]{3,2,1,0:T(8,128)(2,1)}, u32[]{:S(2)}) %copy-start.1) | copy-done | bytes 5242904
  75.2 5.1 %own.1 = (bf16[4,4,128,128]{3,2,1,0:T(8,128)(2,1)S(1)}, bf16[4,4,128,128]{3,2,1,0:T(8,128)(2,1)S(1)}, f32[4,2,128,128]{3,2,1,0:T(8,128)S(1)}, f32[4,2,128,128]{3,2,1,0:T(8,128)S(1)}) custom-call(s32[2]{0:T(128)S(1)} %pad_add_fusion.place_ref, bf16[4,2,2,4,128,128]{5,4,3,2,1,0:T(8,128)(2,1)S(1)} %arrange.1.qd_ref, ...), custom_call_target="tpu_custom_call" | custom-call | flops 2684354560 | bytes 1048576 | tf_op jit(solution)/shard_map/own/pallas_call | solution.py:29
  81.0 3.5 %collective-permute-done.14 = bf16[4,2,128,128]{3,2,1,0:T(8,128)(2,1)S(1)} collective-permute-done((bf16[4,2,128,128]{3,2,1,0:T(8,128)(2,1)}, bf16[4,2,128,128]{3,2,1,0:T(8,128)(2,1)S(1)}, u32[]{:S(2)}, u32[]{:S(2)}) %collective-permute-start.14) | collective-permute-done | bytes 262176 | tf_op jit(solution)/shard_map/ppermute | solution.py:20
  84.5 2.1 %collective-permute-done.16 = bf16[4,2,128,128]{3,2,1,0:T(8,128)(2,1)} collective-permute-done((bf16[4,2,128,128]{3,2,1,0:T(8,128)(2,1)}, bf16[4,2,128,128]{3,2,1,0:T(8,128)(2,1)}, u32[]{:S(2)}, u32[]{:S(2)}) %collective-permute-start.16) | collective-permute-done | bytes 262176 | tf_op jit(solution)/shard_map/ppermute | solution.py:20
  86.6 7.9 %collective-permute-done.17 = bf16[4,2,128,128]{3,2,1,0:T(8,128)(2,1)} collective-permute-done((bf16[4,2,128,128]{3,2,1,0:T(8,128)(2,1)}, bf16[4,2,128,128]{3,2,1,0:T(8,128)(2,1)}, u32[]{:S(2)}, u32[]{:S(2)}) %collective-permute-start.17) | collective-permute-done | bytes 262176 | tf_op jit(solution)/shard_map/ppermute | solution.py:20
  94.5 1.2 %add_convert_fusion = (bf16[4,2,128,128]{3,2,1,0:T(8,128)(2,1)S(1)}, bf16[4,2,128,128]{3,2,1,0:T(8,128)(2,1)S(1)}) fusion(bf16[4,2,128,128]{3,2,1,0:T(8,128)(2,1)} %collective-permute-done.17, f32[4,2,128,128]{3,2,1,0:T(8,128)S(1)} %get-tuple-element.22, bf16[4,2,128,128]{3,2,1,0:T(8,128)(2,1)} %collective-permute-done.16, ...), kind=kLoop, calls=%fused_computation | loop fusion | flops 1310720 | bytes 2621440 | tf_op jit(solution)/shard_map/convert_element_type | solution.py:327
  97.4 1.4 %merge_dv.1 = bf16[128,8,128]{2,1,0:T(8,128)(2,1)} custom-call(s32[2]{0:T(128)S(1)} %pad_add_fusion.place_ref, bf16[4,128,128]{2,1,0:T(8,128)(2,1)S(1)} %get-tuple-element.26.own_ref, bf16[4,128,128]{2,1,0:T(8,128)(2,1)S(1)} %collective-permute-done.18.other_ref), custom_call_target="tpu_custom_call" | custom-call | flops 1000000000 | bytes 1048576 | tf_op jit(solution)/shard_map/merge_dv/pallas_call | solution.py:29
  98.8 1.4 %merge_dk.1 = bf16[128,8,128]{2,1,0:T(8,128)(2,1)} custom-call(s32[2]{0:T(128)S(1)} %pad_add_fusion.place_ref, bf16[4,128,128]{2,1,0:T(8,128)(2,1)S(1)} %get-tuple-element.28.own_ref, bf16[4,128,128]{2,1,0:T(8,128)(2,1)S(1)} %collective-permute-done.15.other_ref), custom_call_target="tpu_custom_call" | custom-call | flops 1000000000 | bytes 1048576 | tf_op jit(solution)/shard_map/merge_dk/pallas_call | solution.py:29
  100.2 3.6 %merge_dq.1 = bf16[128,32,128]{2,1,0:T(8,128)(2,1)} custom-call(s32[2]{0:T(128)S(1)} %pad_add_fusion.place_ref, bf16[16,128,128]{2,1,0:T(8,128)(2,1)S(1)} %bitcast.12, bf16[16,128,128]{2,1,0:T(8,128)(2,1)S(1)} %bitcast.13), custom_call_target="tpu_custom_call" | custom-call | flops 1000000000 | bytes 1048576 | tf_op jit(solution)/shard_map/merge_dq/pallas_call | solution.py:29
  (41 shorter events, 4.4 us)
Async XLA Ops:
  0.6 36.4 %copy-start.11 = (s32[16]{0:T(128)S(1)}, s32[16]{0:T(128)}, u32[]{:S(2)}) copy-start(s32[16]{0:T(128)} %lengths_ref.1) | copy-start | bytes 196
  0.6 28.7 %collective-permute-start = (bf16[128,32,128]{2,1,0:T(8,128)(2,1)}, bf16[128,32,128]{2,1,0:T(8,128)(2,1)S(1)}, u32[]{:S(2)}, u32[]{:S(2)}) collective-permute-start(bf16[128,32,128]{2,1,0:T(8,128)(2,1)} %q_ref.1), channel_id=1, source_target_pairs={{0,1},{1,0},{2,3},{3,2},{4,5},{5,4},{6,7},{7,6},{8,9},{9,8},{10,11... | collective-permute-start | bytes 3145736 | tf_op jit(solution)/shard_map/ppermute | solution.py:24
  1.4 28.0 %collective-permute-start.1 = (bf16[128,32,128]{2,1,0:T(8,128)(2,1)}, bf16[128,32,128]{2,1,0:T(8,128)(2,1)S(1)}, u32[]{:S(2)}, u32[]{:S(2)}) collective-permute-start(bf16[128,32,128]{2,1,0:T(8,128)(2,1)} %do_ref.1), channel_id=1, source_target_pairs={{0,1},{1,0},{2,3},{3,2},{4,5},{5,4},{6,7},{7,6},{8,9},{9,8},{10,11... | collective-permute-start | bytes 3145736 | tf_op jit(solution)/shard_map/ppermute | solution.py:24
  1.5 9.6 %collective-permute-start.3 = (bf16[128,8,128]{2,1,0:T(8,128)(2,1)}, bf16[128,8,128]{2,1,0:T(8,128)(2,1)}, u32[]{:S(2)}, u32[]{:S(2)}) collective-permute-start(bf16[128,8,128]{2,1,0:T(8,128)(2,1)} %refs_0_.2), channel_id=1, source_target_pairs={{0,2},{1,3},{2,4},{3,5},{4,6},{5,7},{6,8},{7,9},{8,10},{9,11},{10,... | collective-permute-start | bytes 786440 | tf_op jit(solution)/shard_map/ppermute | solution.py:20
  4.6 11.7 %collective-permute-start.5 = (bf16[128,8,128]{2,1,0:T(8,128)(2,1)}, bf16[128,8,128]{2,1,0:T(8,128)(2,1)}, u32[]{:S(2)}, u32[]{:S(2)}) collective-permute-start(bf16[128,8,128]{2,1,0:T(8,128)(2,1)} %refs_0_.2), channel_id=1, source_target_pairs={{0,4},{1,5},{2,6},{3,7},{4,8},{5,9},{6,10},{7,11},{8,12},{9,13},{1... | collective-permute-start | bytes 786440 | tf_op jit(solution)/shard_map/ppermute | solution.py:20
  7.7 13.6 %collective-permute-start.2 = (bf16[128,8,128]{2,1,0:T(8,128)(2,1)}, bf16[128,8,128]{2,1,0:T(8,128)(2,1)S(1)}, u32[]{:S(2)}, u32[]{:S(2)}) collective-permute-start(bf16[128,8,128]{2,1,0:T(8,128)(2,1)} %refs_0_.2), channel_id=1, source_target_pairs={{0,1},{1,0},{2,3},{3,2},{4,5},{5,4},{6,7},{7,6},{8,9},{9,8},{10,11... | collective-permute-start | bytes 786440 | tf_op jit(solution)/shard_map/ppermute | solution.py:24
  11.1 12.8 %collective-permute-start.10 = (bf16[128,8,128]{2,1,0:T(8,128)(2,1)}, bf16[128,8,128]{2,1,0:T(8,128)(2,1)S(1)}, u32[]{:S(2)}, u32[]{:S(2)}) collective-permute-start(bf16[128,8,128]{2,1,0:T(8,128)(2,1)} %refs_0_.3), channel_id=1, source_target_pairs={{0,4},{1,5},{2,6},{3,7},{4,8},{5,9},{6,10},{7,11},{8,12},{9,13},{1... | collective-permute-start | bytes 786440 | tf_op jit(solution)/shard_map/ppermute | solution.py:20
  16.2 11.2 %collective-permute-start.8 = (bf16[128,8,128]{2,1,0:T(8,128)(2,1)}, bf16[128,8,128]{2,1,0:T(8,128)(2,1)}, u32[]{:S(2)}, u32[]{:S(2)}) collective-permute-start(bf16[128,8,128]{2,1,0:T(8,128)(2,1)} %refs_0_.3), channel_id=1, source_target_pairs={{0,2},{1,3},{2,4},{3,5},{4,6},{5,7},{6,8},{7,9},{8,10},{9,11},{10,... | collective-permute-start | bytes 786440 | tf_op jit(solution)/shard_map/ppermute | solution.py:20
  21.4 0.7 copy-start.9
  22.1 15.0 %collective-permute-start.4 = (bf16[128,8,128]{2,1,0:T(8,128)(2,1)}, bf16[128,8,128]{2,1,0:T(8,128)(2,1)}, u32[]{:S(2)}, u32[]{:S(2)}) collective-permute-start(bf16[128,8,128]{2,1,0:T(8,128)(2,1)} %collective-permute-done.3.refs_2_), channel_id=1, source_target_pairs={{0,1},{1,0},{2,3},{3,2},{4,5},{5,4},{6,7},{7,6},{8,9},{9,8},{10,11... | collective-permute-start | bytes 786440 | tf_op jit(solution)/shard_map/ppermute | solution.py:24
  23.9 13.1 %collective-permute-start.6 = (bf16[128,8,128]{2,1,0:T(8,128)(2,1)}, bf16[128,8,128]{2,1,0:T(8,128)(2,1)}, u32[]{:S(2)}, u32[]{:S(2)}) collective-permute-start(bf16[128,8,128]{2,1,0:T(8,128)(2,1)} %collective-permute-done.5.refs_4_), channel_id=1, source_target_pairs={{0,1},{1,0},{2,3},{3,2},{4,5},{5,4},{6,7},{7,6},{8,9},{9,8},{10,11... | collective-permute-start | bytes 786440 | tf_op jit(solution)/shard_map/ppermute | solution.py:24
  27.4 23.4 %collective-permute-start.7 = (bf16[128,8,128]{2,1,0:T(8,128)(2,1)}, bf16[128,8,128]{2,1,0:T(8,128)(2,1)S(1)}, u32[]{:S(2)}, u32[]{:S(2)}) collective-permute-start(bf16[128,8,128]{2,1,0:T(8,128)(2,1)} %refs_0_.3), channel_id=1, source_target_pairs={{0,1},{1,0},{2,3},{3,2},{4,5},{5,4},{6,7},{7,6},{8,9},{9,8},{10,11... | collective-permute-start | bytes 786440 | tf_op jit(solution)/shard_map/ppermute | solution.py:24
  29.3 21.4 %collective-permute-start.11 = (bf16[128,8,128]{2,1,0:T(8,128)(2,1)S(1)}, bf16[128,8,128]{2,1,0:T(8,128)(2,1)S(1)}, u32[]{:S(2)}, u32[]{:S(2)}) collective-permute-start(bf16[128,8,128]{2,1,0:T(8,128)(2,1)S(1)} %collective-permute-done.10.refs_4_), channel_id=1, source_target_pairs={{0,1},{1,0},{2,3},{3,2},{4,5},{5,4},{6,7},{7,6},{8,9},{9,8},{10,11... | collective-permute-start | bytes 786440 | tf_op jit(solution)/shard_map/ppermute | solution.py:24
  29.3 1.0 copy-start.5
  30.3 20.5 %collective-permute-start.9 = (bf16[128,8,128]{2,1,0:T(8,128)(2,1)}, bf16[128,8,128]{2,1,0:T(8,128)(2,1)S(1)}, u32[]{:S(2)}, u32[]{:S(2)}) collective-permute-start(bf16[128,8,128]{2,1,0:T(8,128)(2,1)} %collective-permute-done.8.refs_2_), channel_id=1, source_target_pairs={{0,1},{1,0},{2,3},{3,2},{4,5},{5,4},{6,7},{7,6},{8,9},{9,8},{10,11... | collective-permute-start | bytes 786440 | tf_op jit(solution)/shard_map/ppermute | solution.py:24
  30.8 1.2 %copy-start.3 = (bf16[128,32,128]{2,1,0:T(8,128)(2,1)S(1)}, bf16[128,32,128]{2,1,0:T(8,128)(2,1)}, u32[]{:S(2)}) copy-start(bf16[128,32,128]{2,1,0:T(8,128)(2,1)} %q_ref.1) | copy-start | bytes 3145732
  32.1 1.2 %copy-start.4 = (bf16[128,32,128]{2,1,0:T(8,128)(2,1)S(1)}, bf16[128,32,128]{2,1,0:T(8,128)(2,1)}, u32[]{:S(2)}) copy-start(bf16[128,32,128]{2,1,0:T(8,128)(2,1)} %do_ref.1) | copy-start | bytes 3145732
  33.3 1.2 %copy-start.6 = (bf16[128,32,128]{2,1,0:T(8,128)(2,1)S(1)}, bf16[128,32,128]{2,1,0:T(8,128)(2,1)}, u32[]{:S(2)}) copy-start(bf16[128,32,128]{2,1,0:T(8,128)(2,1)} %copy-done.5) | copy-start | bytes 3145732
  34.5 2.6 %copy-start.7 = (bf16[128,8,128]{2,1,0:T(8,128)(2,1)S(1)}, bf16[128,8,128]{2,1,0:T(8,128)(2,1)}, u32[]{:S(2)}) copy-start(bf16[128,8,128]{2,1,0:T(8,128)(2,1)} %refs_0_.2) | copy-start | bytes 786436
  34.5 2.6 %copy-start.10 = (bf16[128,8,128]{2,1,0:T(8,128)(2,1)S(1)}, bf16[128,8,128]{2,1,0:T(8,128)(2,1)}, u32[]{:S(2)}) copy-start(bf16[128,8,128]{2,1,0:T(8,128)(2,1)} %copy-done.9) | copy-start | bytes 786436
  37.0 13.8 %copy-start.8 = (bf16[128,8,128]{2,1,0:T(8,128)(2,1)S(1)}, bf16[128,8,128]{2,1,0:T(8,128)(2,1)}, u32[]{:S(2)}) copy-start(bf16[128,8,128]{2,1,0:T(8,128)(2,1)} %refs_0_.3) | copy-start | bytes 786436
  48.4 2.3 %copy-start = (bf16[4,2,640,512]{3,2,1,0:T(8,128)(2,1)}, bf16[4,2,640,512]{3,2,1,0:T(8,128)(2,1)S(1)}, u32[]{:S(2)}) copy-start(bf16[4,2,640,512]{3,2,1,0:T(8,128)(2,1)S(1)} %get-tuple-element.15.p_ref) | copy-start | bytes 15728644
  59.3 2.4 %copy-start.2 = (bf16[4,2,640,512]{3,2,1,0:T(8,128)(2,1)}, bf16[4,2,640,512]{3,2,1,0:T(8,128)(2,1)S(1)}, u32[]{:S(2)}) copy-start(bf16[4,2,640,512]{3,2,1,0:T(8,128)(2,1)S(1)} %get-tuple-element.16.ds_ref) | copy-start | bytes 15728644
  61.7 19.3 %collective-permute-start.13 = (bf16[4,2,128,128]{3,2,1,0:T(8,128)(2,1)}, bf16[4,2,128,128]{3,2,1,0:T(8,128)(2,1)S(1)}, u32[]{:S(2)}, u32[]{:S(2)}) collective-permute-start(bf16[4,2,128,128]{3,2,1,0:T(8,128)(2,1)} %get-tuple-element.20), channel_id=1, source_target_pairs={{4,0},{5,1},{6,2},{7,3},{8,4},{9,5},{10,6},{11,7},{12,8},{13,9},{1... | collective-permute-start | bytes 786440 | tf_op jit(solution)/shard_map/ppermute | solution.py:20
  63.6 20.9 %collective-permute-start.14 = (bf16[4,2,128,128]{3,2,1,0:T(8,128)(2,1)}, bf16[4,2,128,128]{3,2,1,0:T(8,128)(2,1)S(1)}, u32[]{:S(2)}, u32[]{:S(2)}) collective-permute-start(bf16[4,2,128,128]{3,2,1,0:T(8,128)(2,1)} %get-tuple-element.21), channel_id=1, source_target_pairs={{2,0},{3,1},{4,2},{5,3},{6,4},{7,5},{8,6},{9,7},{10,8},{11,9},{12,... | collective-permute-start | bytes 786440 | tf_op jit(solution)/shard_map/ppermute | solution.py:20
  68.9 17.7 %collective-permute-start.16 = (bf16[4,2,128,128]{3,2,1,0:T(8,128)(2,1)}, bf16[4,2,128,128]{3,2,1,0:T(8,128)(2,1)}, u32[]{:S(2)}, u32[]{:S(2)}) collective-permute-start(bf16[4,2,128,128]{3,2,1,0:T(8,128)(2,1)} %get-tuple-element.23), channel_id=1, source_target_pairs={{4,0},{5,1},{6,2},{7,3},{8,4},{9,5},{10,6},{11,7},{12,8},{13,9},{1... | collective-permute-start | bytes 786440 | tf_op jit(solution)/shard_map/ppermute | solution.py:20
  70.8 23.6 %collective-permute-start.17 = (bf16[4,2,128,128]{3,2,1,0:T(8,128)(2,1)}, bf16[4,2,128,128]{3,2,1,0:T(8,128)(2,1)}, u32[]{:S(2)}, u32[]{:S(2)}) collective-permute-start(bf16[4,2,128,128]{3,2,1,0:T(8,128)(2,1)} %get-tuple-element.24), channel_id=1, source_target_pairs={{2,0},{3,1},{4,2},{5,3},{6,4},{7,5},{8,6},{9,7},{10,8},{11,9},{12,... | collective-permute-start | bytes 786440 | tf_op jit(solution)/shard_map/ppermute | solution.py:20
  72.8 2.5 %copy-start.1 = (bf16[4,2,640,512]{3,2,1,0:T(8,128)(2,1)S(1)}, bf16[4,2,640,512]{3,2,1,0:T(8,128)(2,1)}, u32[]{:S(2)}) copy-start(bf16[4,2,640,512]{3,2,1,0:T(8,128)(2,1)} %copy-done) | copy-start | bytes 15728644
  80.4 19.8 %collective-permute-start.12 = (bf16[4,4,128,128]{3,2,1,0:T(8,128)(2,1)S(1)}, bf16[4,4,128,128]{3,2,1,0:T(8,128)(2,1)S(1)}, u32[]{:S(2)}, u32[]{:S(2)}) collective-permute-start(bf16[4,4,128,128]{3,2,1,0:T(8,128)(2,1)S(1)} %get-tuple-element.18), channel_id=1, source_target_pairs={{0,1},{1,0},{2,3},{3,2},{4,5},{5,4},{6,7},{7,6},{8,9},{9,8},{10,11... | collective-permute-start | bytes 1572872 | tf_op jit(solution)/shard_map/ppermute | solution.py:24
  95.7 1.6 %collective-permute-start.18 = (bf16[4,128,128]{2,1,0:T(8,128)(2,1)S(1)}, bf16[4,128,128]{2,1,0:T(8,128)(2,1)S(1)}, u32[]{:S(2)}, u32[]{:S(2)}) collective-permute-start(bf16[4,128,128]{2,1,0:T(8,128)(2,1)S(1)} %get-tuple-element.25), channel_id=1, source_target_pairs={{0,1},{1,0},{2,3},{3,2},{4,5},{5,4},{6,7},{7,6},{8,9},{9,8},{10,11... | collective-permute-start | bytes 393224 | tf_op jit(solution)/shard_map/ppermute | solution.py:24
  96.4 2.4 %collective-permute-start.15 = (bf16[4,128,128]{2,1,0:T(8,128)(2,1)S(1)}, bf16[4,128,128]{2,1,0:T(8,128)(2,1)S(1)}, u32[]{:S(2)}, u32[]{:S(2)}) collective-permute-start(bf16[4,128,128]{2,1,0:T(8,128)(2,1)S(1)} %get-tuple-element.27), channel_id=1, source_target_pairs={{0,1},{1,0},{2,3},{3,2},{4,5},{5,4},{6,7},{7,6},{8,9},{9,8},{10,11... | collective-permute-start | bytes 393224 | tf_op jit(solution)/shard_map/ppermute | solution.py:24

commit v3 on v2

--- a/solution.py
+++ b/solution.py
@@ -12,7 +12,7 @@
 MASKED = -1e30
 BF16, F32 = jnp.bfloat16, jnp.float32
 NT = (((1,), (1,)), ((), ()))
-VMEM_BYTES = 40 * 2**20
+VMEM_BYTES = 24 * 2**20
 
 
 def moved(array, device_count, by):
@@ -73,19 +73,33 @@
     )
 
 
-def spread(block_refs, core, wide):
-    tokens, heads, dim = block_refs[0].shape
-    halo = len(block_refs) // 2 - 1
-    for back in range(halo + 1):
-        at = 2 * (halo - back)
-        wide[at + core] = block_refs[2 * back][...].astype(F32).reshape(tokens * heads, dim)
-        wide[at + 1 - core] = block_refs[2 * back + 1][...].astype(F32).reshape(tokens * heads, dim)
-
-
-def one_head(wide, core, heads, narrow):
-    head = core * (heads // 2) + pl.program_id(0)
-    for r in range(narrow.shape[0]):
-        narrow[r] = wide[r, pl.ds(head, narrow.shape[1], stride=heads), :].astype(BF16)
+def pack_kernel(place_ref, own_ref, other_ref, out_ref, scr):
+    core = place_ref[0]
+    tokens, heads, dim = own_ref.shape
+    half = heads // 2
+    for which, ref in enumerate([own_ref, other_ref]):
+        block = 1 - core if which else core
+        scr[...] = ref[...].astype(F32).reshape(tokens * heads, dim)
+        for h in range(half):
+            out_ref[h, block] = scr[pl.ds(core * half + h, tokens, stride=heads), :].astype(BF16)
+
+
+def pack(place, own, other, name):
+    tokens, heads, dim = own.shape
+    spec = pl.BlockSpec(own.shape, lambda i, place: (0, 0, 0))
+    out = (heads // 2, 2, tokens, dim)
+    return call(
+        pack_kernel,
+        name,
+        (1,),
+        place,
+        (own, other),
+        [spec] * 2,
+        jax.ShapeDtypeStruct(out, BF16),
+        pl.BlockSpec(out, lambda i, place: (0, 0, 0, 0)),
+        [pltpu.VMEM((tokens * heads, dim), F32)],
+        10**9,
+    )
 
 
 def first_allowed(lengths_ref, query_pos, window_start):
@@ -99,38 +113,42 @@
     return first - window_start
 
 
+def window_of(pair_refs, scr):
+    halo = len(pair_refs) - 1
+    for back, ref in enumerate(pair_refs):
+        scr[pl.ds(2 * (halo - back), 2)] = ref[0]
+
+
 def prob_kernel(halo, place_ref, lengths_ref, qd_ref, *refs):
-    blocks = refs[: 2 * (halo + 1)]
-    k_out, p_ref = refs[2 * (halo + 1) : 2 * (halo + 1) + 2]
-    dv_refs = refs[2 * (halo + 1) + 2 : -2]
-    wide, acc = refs[-2:]
-    core, window_start = place_ref[0], place_ref[1]
-    tokens, heads, dim = blocks[0].shape
-    _, _, _, group, _, _ = qd_ref.shape
+    k_refs = refs[: halo + 1]
+    p_ref = refs[halo + 1]
+    dv_refs = refs[halo + 2 : -3]
+    k_scr, acc, firsts = refs[-3:]
+    _, _, _, group, tokens, dim = qd_ref.shape
     count = 2 * halo + 1
+    pair = 2 * tokens
+    lane = lax.broadcasted_iota(jnp.int32, (1, pair), 1) % tokens
 
     @pl.when(pl.program_id(0) == 0)
     def _():
-        spread(blocks, core, wide)
-
-    one_head(wide, core, heads, k_out.at[0])
-    pair = 2 * tokens
-    lane = lax.broadcasted_iota(jnp.int32, (1, pair), 1) % tokens
+        for e in range(2):
+            query_pos = lane + (2 * halo + e) * tokens
+            firsts[e] = first_allowed(lengths_ref, query_pos, place_ref[1])
+
+    window_of(k_refs, k_scr)
     row = lax.broadcasted_iota(jnp.int32, (tokens, pair), 0)
     for e in range(2):
-        query_pos = lane + (2 * halo + e) * tokens
-        first = first_allowed(lengths_ref, query_pos, window_start)
-        k = k_out[0, pl.ds(e, count)].reshape(count * tokens, dim)
+        first = firsts[e] - row
+        k = k_scr[pl.ds(e, count)].reshape(count * tokens, dim)
         q = qd_ref[0, e, 0].reshape(group * tokens, dim)
         do = qd_ref[0, e, 1].reshape(group * tokens, dim)
         for at in range(0, group * tokens, pair):
             s = lax.dot_general(k, q[at : at + pair], NT, preferred_element_type=F32)
             tiles = []
             for j in range(count):
-                key_pos = row + (e + j) * tokens
-                allowed = key_pos >= first
+                allowed = first <= (e + j) * tokens
                 if j == count - 1:
-                    allowed &= key_pos <= query_pos
+                    allowed &= row <= lane
                 tiles.append(jnp.where(allowed, s[j * tokens : (j + 1) * tokens], MASKED))
             s = jnp.concatenate(tiles, axis=0)
             top = jnp.max(s, axis=0, keepdims=True)
@@ -148,23 +166,16 @@
 
 
 def dscore_kernel(halo, place_ref, qd_ref, p_ref, *refs):
-    blocks = refs[: 2 * (halo + 1)]
-    ds_ref = refs[2 * (halo + 1)]
-    dk_refs = refs[2 * (halo + 1) + 1 : -3]
-    wide, narrow, acc = refs[-3:]
-    core = place_ref[0]
-    tokens, heads, dim = blocks[0].shape
-    _, _, _, group, _, _ = qd_ref.shape
+    v_refs = refs[: halo + 1]
+    ds_ref = refs[halo + 1]
+    dk_refs = refs[halo + 2 : -2]
+    v_scr, acc = refs[-2:]
+    _, _, _, group, tokens, dim = qd_ref.shape
     count = 2 * halo + 1
-
-    @pl.when(pl.program_id(0) == 0)
-    def _():
-        spread(blocks, core, wide)
-
-    one_head(wide, core, heads, narrow)
     pair = 2 * tokens
+    window_of(v_refs, v_scr)
     for e in range(2):
-        v = narrow[pl.ds(e, count)].reshape(count * tokens, dim)
+        v = v_scr[pl.ds(e, count)].reshape(count * tokens, dim)
         q = qd_ref[0, e, 0].reshape(group * tokens, dim)
         do = qd_ref[0, e, 1].reshape(group * tokens, dim)
         for at in range(0, group * tokens, pair):
@@ -182,29 +193,36 @@
         ref[0] = (acc[pl.ds(2 * (halo - back), 2)] * dim**-0.5).astype(BF16)
 
 
-def own_kernel(halo, place_ref, qd_ref, k_ref, p_ref, ds_ref, dq_ref, dq_other_ref, dk_ref, dv_ref, scr):
+def own_kernel(halo, place_ref, qd_ref, p_ref, ds_ref, *refs):
+    k_refs, back_refs = refs[: halo + 1], refs[halo + 1 : 2 * halo + 1]
+    dq_ref, dq_other_ref, dk_ref, dv_ref, dv_other_ref, k_scr, dq_scr, dv_scr = refs[2 * halo + 1 :]
     core = place_ref[0]
     _, _, _, group, tokens, dim = qd_ref.shape
     count = 2 * halo + 1
     scale = dim**-0.5
+    window_of(k_refs, k_scr)
     for e in range(2):
         q = qd_ref[0, e, 0].reshape(group * tokens, dim)
         do = qd_ref[0, e, 1].reshape(group * tokens, dim)
-        k = k_ref[0, pl.ds(e, count)].reshape(count * tokens, dim)
+        k = k_scr[pl.ds(e, count)].reshape(count * tokens, dim)
         dqt = jnp.dot(k.T, ds_ref[0, e], preferred_element_type=F32) * scale
         for g in range(group):
-            scr[e, g] = dqt[:, g * tokens : (g + 1) * tokens].T.astype(BF16)
+            dq_scr[e, g] = dqt[:, g * tokens : (g + 1) * tokens].T.astype(BF16)
         keep = (2 * halo - e) * tokens
         dk = jnp.dot(ds_ref[0, e, keep:], q, preferred_element_type=F32) * scale
         dv = jnp.dot(p_ref[0, e, keep:], do, preferred_element_type=F32)
         if e == 0:
-            dk_ref[0, 0], dv_ref[0, 0] = dk, dv
+            dk_ref[0, 0], dv_scr[0] = dk, dv
         else:
             dk_ref[0, 0] += dk[:tokens]
-            dv_ref[0, 0] += dv[:tokens]
-            dk_ref[0, 1], dv_ref[0, 1] = dk[tokens:], dv[tokens:]
-    dq_ref[0] = scr[core]
-    dq_other_ref[0] = scr[1 - core]
+            dv_scr[0] += dv[:tokens]
+            dk_ref[0, 1], dv_scr[1] = dk[tokens:], dv[tokens:]
+    for ref in back_refs:
+        dv_scr[...] += ref[0].astype(F32)
+    dq_ref[0] = dq_scr[core]
+    dq_other_ref[0] = dq_scr[1 - core]
+    dv_ref[0] = dv_scr[core].astype(BF16)
+    dv_other_ref[0] = dv_scr[1 - core].astype(BF16)
 
 
 def merge_kernel(place_ref, own_ref, other_ref, out_ref, scr):
@@ -249,88 +267,92 @@
     place = jnp.stack([core, (device // 2 - halo) * (2 * tokens)]).astype(jnp.int32)
 
     far_first = range(halo, 0, -1)
-    k_halo = {back: moved(keys, device_count, 2 * back) for back in far_first}
-    v_halo = {back: moved(values, device_count, 2 * back) for back in far_first}
-
-    def all_blocks(own, halos):
-        blocks = [own, swapped(own, device_count)]
-        for back in range(1, halo + 1):
-            blocks += [halos[back], swapped(halos[back], device_count)]
-        return blocks
-
+    k_own = pack(place, keys, swapped(keys, device_count), "pack_k")
+    v_own = pack(place, values, swapped(values, device_count), "pack_v")
     qd = arrange(
         place, queries, grad_out, swapped(queries, device_count), swapped(grad_out, device_count), key_heads
     )
 
+    def halo_of(own):
+        received = {back: moved(own, device_count, 2 * back) for back in far_first}
+        return [own] + [received[back] for back in range(1, halo + 1)]
+
+    def sent_back(partials):
+        return [moved(partials[back - 1], device_count, -2 * back) for back in far_first]
+
     def per_head(*shape):
         return pl.BlockSpec((1,) + shape, lambda h, *_: (h,) + (0,) * len(shape))
 
-    raw_spec = pl.BlockSpec(keys.shape, lambda h, *_: (0, 0, 0))
     qd_spec = per_head(2, 2, group, tokens, dim)
-    k_spec = per_head(window, tokens, dim)
     p_spec = per_head(2, count * tokens, group * tokens)
+    p_shape = jax.ShapeDtypeStruct((half, 2, count * tokens, group * tokens), BF16)
     pair_spec = per_head(2, tokens, dim)
-    p_shape = jax.ShapeDtypeStruct((half, 2, count * tokens, group * tokens), BF16)
     pair = (half, 2, tokens, dim)
-    wide = pltpu.VMEM((window, tokens * key_heads, dim), F32)
+    one_spec = per_head(tokens, dim)
+    one_shape = jax.ShapeDtypeStruct((half, tokens, dim), BF16)
+    dq_spec = per_head(group, tokens, dim)
+    dq_shape = jax.ShapeDtypeStruct((half, group, tokens, dim), BF16)
+    run = pltpu.VMEM((window, tokens, dim), BF16)
     acc = pltpu.VMEM((2 * halo, tokens, dim), F32)
     product = 2 * half * 2 * count * tokens * group * tokens * dim
 
-    k_arranged, prob, *dv_halo = call(
+    k_pairs = halo_of(k_own)
+    v_pairs = halo_of(v_own)
+    prob, *dv_halo = call(
         functools.partial(prob_kernel, halo),
         "prob",
         (half,),
         (place, doc_lengths),
-        (qd, *all_blocks(keys, k_halo)),
-        [qd_spec] + [raw_spec] * window,
-        [jax.ShapeDtypeStruct((half, window, tokens, dim), BF16), p_shape] + [jax.ShapeDtypeStruct(pair, BF16)] * halo,
-        [k_spec, p_spec] + [pair_spec] * halo,
-        [wide, acc],
+        (qd, *k_pairs),
+        [qd_spec] + [pair_spec] * (halo + 1),
+        [p_shape] + [jax.ShapeDtypeStruct(pair, BF16)] * halo,
+        [p_spec] + [pair_spec] * halo,
+        [run, acc, pltpu.VMEM((2, 1, 2 * tokens), jnp.int32)],
         4 * product,
     )
-    dv_back = [moved(dv_halo[back - 1], device_count, -2 * back) for back in far_first]
+    dv_back = sent_back(dv_halo)
     dscore, *dk_halo = call(
         functools.partial(dscore_kernel, halo),
         "dscore",
         (half,),
         place,
-        (qd, prob, *all_blocks(values, v_halo)),
-        [qd_spec, p_spec] + [raw_spec] * window,
+        (qd, prob, *v_pairs),
+        [qd_spec, p_spec] + [pair_spec] * (halo + 1),
         [p_shape] + [jax.ShapeDtypeStruct(pair, BF16)] * halo,
         [p_spec] + [pair_spec] * halo,
-        [wide, pltpu.VMEM((window, tokens, dim), BF16), acc],
+        [run, acc],
         4 * product,
     )
-    dk_back = [moved(dk_halo[back - 1], device_count, -2 * back) for back in far_first]
-    dq_spec = per_head(group, tokens, dim)
-    dq_shape = jax.ShapeDtypeStruct((half, group, tokens, dim), BF16)
-    dq, dq_other, dk_own, dv_own = call(
+    dk_back = sent_back(dk_halo)
+    dq, dq_other, dk_own, dv, dv_other = call(
         functools.partial(own_kernel, halo),
         "own",
         (half,),
         place,
-        (qd, k_arranged, prob, dscore),
-        [qd_spec, k_spec, p_spec, p_spec],
-        [dq_shape] * 2 + [jax.ShapeDtypeStruct(pair, F32)] * 2,
-        [dq_spec] * 2 + [pair_spec] * 2,
-        [pltpu.VMEM((2, group, tokens, dim), BF16)],
+        (qd, prob, dscore, *k_pairs, *dv_back),
+        [qd_spec, p_spec, p_spec] + [pair_spec] * (2 * halo + 1),
+        [dq_shape] * 2 + [jax.ShapeDtypeStruct(pair, F32)] + [one_shape] * 2,
+        [dq_spec] * 2 + [pair_spec] + [one_spec] * 2,
+        [
+            run,
+            pltpu.VMEM((2, group, tokens, dim), BF16),
+            pltpu.VMEM((2, tokens, dim), F32),
+        ],
         4 * product,
     )
     dq_other = swapped(dq_other, device_count)
+    dv_other = swapped(dv_other, device_count)
     flat = (half * group, tokens, dim)
     grad_queries = merge(place, dq.reshape(flat), dq_other.reshape(flat), 32, "merge_dq")
-
-    def summed(own, backs, name):
-        total = own
-        for back in backs:
-            total = total + back.astype(F32)
-        total = total.astype(BF16)
-        mine = lax.dynamic_index_in_dim(total, core, 1, keepdims=False)
-        other = lax.dynamic_index_in_dim(total, 1 - core, 1, keepdims=False)
-        return merge(place, mine, swapped(other, device_count), tokens, name)
-
-    grad_values = summed(dv_own, dv_back, "merge_dv")
-    grad_keys = summed(dk_own, dk_back, "merge_dk")
+    grad_values = merge(place, dv, dv_other, tokens, "merge_dv")
+
+    total, grad_queries, grad_values = lax.optimization_barrier((dk_own, grad_queries, grad_values))
+    for back in dk_back:
+        total = total + back.astype(F32)
+    total = total.astype(BF16)
+    mine = lax.dynamic_index_in_dim(total, core, 1, keepdims=False)
+    other = lax.dynamic_index_in_dim(total, 1 - core, 1, keepdims=False)
+    grad_keys = merge(place, mine, swapped(other, device_count), tokens, "merge_dk")
     return grad_queries, grad_keys, grad_values
 
 

time: 104 us -> 79.7 us (0.77)
  local copies, waits for them, and re-layouts: 12.6 us -> 1.93 us
  Pallas kernels: 33.9 us -> 28.7 us
  waiting for transfers between devices: 22.1 us -> 17.5 us
  starting transfers between devices: 33 us -> 29.1 us
    unnamed x24 -> x10, local copies, waits for them, and re-layouts: 12.6 us -> 1.91 us
    ppermute x8, waiting for transfers between devices: 21.2 us -> 12.3 us  [moved(): return lax.ppermute(array, AXES, pairs)]
    pallas_call x7 -> x9, Pallas kernels: 33.9 us -> 28.7 us  [call(): pl.pallas_call(kernel, out_shape=outs, grid_spec=pltpu.PrefetchScalarGrid...]
    ppermute x11 -> x7, waiting for transfers between devices: 0.9 us -> 5.21 us  [swapped(): return lax.ppermute(array, AXES, [(d, d ^ 1) for d in range(device_count)])]
    ppermute x11 -> x7, starting transfers between devices: 7.47 us -> 4.53 us  [swapped(): return lax.ppermute(array, AXES, [(d, d ^ 1) for d in range(device_count)])]
  transfers between devices with their start and end apart: 19 -> 15, of which waited for: 7 -> 5; matrix products, arithmetic and copies ran while one was open for 1% -> 0% of each run, Pallas kernels for 21% -> 30%
where the time goes in v3:
time: 79.7 us; the launch traced here: 79.2 us
  starting transfers between devices  29.1 us (37%)
  Pallas kernels  28.7 us (36%)
  waiting for transfers between devices  17.5 us (22%)
  local copies, waits for them, and re-layouts  1.93 us (2%)
  other arithmetic  1.12 us (1%)
  between operations  0.88 us (1%)
    pallas_call x9, Pallas kernels, call(): pl.pallas_call(kernel, out_shape=outs, grid_spec=pltpu.PrefetchScalarGrid...  28.7 us
    ppermute x8, starting transfers between devices, moved(): return lax.ppermute(array, AXES, pairs)  24.6 us
    ppermute x8, waiting for transfers between devices, moved(): return lax.ppermute(array, AXES, pairs)  12.3 us
    ppermute x7, waiting for transfers between devices, swapped(): return lax.ppermute(array, AXES, [(d, d ^ 1) for d in range(device_count)])  5.21 us
    ppermute x7, starting transfers between devices, swapped(): return lax.ppermute(array, AXES, [(d, d ^ 1) for d in range(device_count)])  4.53 us
    unnamed x10, local copies, waits for them, and re-layouts  1.91 us
  transfers between devices with their start and end apart: 15, of which 5 were waited for; matrix products, arithmetic and copies ran while one was open for 0% of the time, Pallas kernels for 30%

profile of v3, /device:TPU:23, one launch (start us, length us, event | category | flops | bytes accessed | tf_op | source)
XLA Modules:
  0.0 79.2 jit_solution(13587399695943692090)
XLA Ops:
  0.6 0.7 collective-permute-start
  1.4 0.1 collective-permute-start.1
  1.5 0.4 collective-permute-start.2
  1.9 0.1 collective-permute-start.5
  2.1 4.2 %collective-permute-done.2.other_ref = bf16[128,8,128]{2,1,0:T(8,128)(2,1)} collective-permute-done((bf16[128,8,128]{2,1,0:T(8,128)(2,1)}, bf16[128,8,128]{2,1,0:T(8,128)(2,1)}, u32[]{:S(2)}, u32[]{:S(2)}) %collective-permute-start.2) | collective-permute-done | bytes 262176 | tf_op jit(solution)/shard_map/ppermute | solution.py:24
  6.3 0.9 %copy-done.2 = bf16[128,8,128]{2,1,0:T(8,128)(2,1)S(1)} copy-done((bf16[128,8,128]{2,1,0:T(8,128)(2,1)S(1)}, bf16[128,8,128]{2,1,0:T(8,128)(2,1)}, u32[]{:S(2)}) %copy-start.2) | copy-done | bytes 262168
  7.2 1.7 %pack_k.1.refs_0_ = bf16[4,2,128,128]{3,2,1,0:T(8,128)(2,1)S(1)} custom-call(s32[2]{0:T(128)S(1)} %pad_add_fusion.place_ref, bf16[128,8,128]{2,1,0:T(8,128)(2,1)S(1)} %copy-done.2, bf16[128,8,128]{2,1,0:T(8,128)(2,1)} %collective-permute-done.2.other_ref), custom_call_target="tpu_custom_call" | custom-call | flops 1000000000 | bytes 1048576 | tf_op jit(solution)/shard_map/pack_k/pallas_call | solution.py:29
  8.9 3.1 %collective-permute-start.3 = (bf16[4,2,128,128]{3,2,1,0:T(8,128)(2,1)S(1)}, bf16[4,2,128,128]{3,2,1,0:T(8,128)(2,1)S(1)}, u32[]{:S(2)}, u32[]{:S(2)}) collective-permute-start(bf16[4,2,128,128]{3,2,1,0:T(8,128)(2,1)S(1)} %pack_k.1.refs_0_), channel_id=1, source_target_pairs={{0,2},{1,3},{2,4},{3,5},{4,6},{5,7},{6,8},{7,9},{8,10},{9,11},{10,... | collective-permute-start | bytes 786440 | tf_op jit(solution)/shard_map/ppermute | solution.py:20
  12.0 3.1 %collective-permute-start.4 = (bf16[4,2,128,128]{3,2,1,0:T(8,128)(2,1)S(1)}, bf16[4,2,128,128]{3,2,1,0:T(8,128)(2,1)S(1)}, u32[]{:S(2)}, u32[]{:S(2)}) collective-permute-start(bf16[4,2,128,128]{3,2,1,0:T(8,128)(2,1)S(1)} %pack_k.1.refs_0_), channel_id=1, source_target_pairs={{0,4},{1,5},{2,6},{3,7},{4,8},{5,9},{6,10},{7,11},{8,12},{9,13},{1... | collective-permute-start | bytes 786440 | tf_op jit(solution)/shard_map/ppermute | solution.py:20
  15.2 0.9 %copy-done.3 = bf16[128,8,128]{2,1,0:T(8,128)(2,1)S(1)} copy-done((bf16[128,8,128]{2,1,0:T(8,128)(2,1)S(1)}, bf16[128,8,128]{2,1,0:T(8,128)(2,1)}, u32[]{:S(2)}) %copy-start.3) | copy-done | bytes 262168
  16.1 0.7 pack_v.1.refs_0_
  16.8 3.1 %collective-permute-start.6 = (bf16[4,2,128,128]{3,2,1,0:T(8,128)(2,1)S(1)}, bf16[4,2,128,128]{3,2,1,0:T(8,128)(2,1)S(1)}, u32[]{:S(2)}, u32[]{:S(2)}) collective-permute-start(bf16[4,2,128,128]{3,2,1,0:T(8,128)(2,1)S(1)} %pack_v.1.refs_0_), channel_id=1, source_target_pairs={{0,2},{1,3},{2,4},{3,5},{4,6},{5,7},{6,8},{7,9},{8,10},{9,11},{10,... | collective-permute-start | bytes 786440 | tf_op jit(solution)/shard_map/ppermute | solution.py:20
  20.0 1.9 %collective-permute-start.7 = (bf16[4,2,128,128]{3,2,1,0:T(8,128)(2,1)S(1)}, bf16[4,2,128,128]{3,2,1,0:T(8,128)(2,1)S(1)}, u32[]{:S(2)}, u32[]{:S(2)}) collective-permute-start(bf16[4,2,128,128]{3,2,1,0:T(8,128)(2,1)S(1)} %pack_v.1.refs_0_), channel_id=1, source_target_pairs={{0,4},{1,5},{2,6},{3,7},{4,8},{5,9},{6,10},{7,11},{8,12},{9,13},{1... | collective-permute-start | bytes 786440 | tf_op jit(solution)/shard_map/ppermute | solution.py:20
  21.9 3.8 %arrange.1.qd_ref = bf16[4,2,2,4,128,128]{5,4,3,2,1,0:T(8,128)(2,1)S(1)} custom-call(s32[2]{0:T(128)S(1)} %pad_add_fusion.place_ref, bf16[128,32,128]{2,1,0:T(8,128)(2,1)S(1)} %copy-done, bf16[128,32,128]{2,1,0:T(8,128)(2,1)S(1)} %copy-done.1, bf16[128,32,128]{2,1,0:T(8,128)(2,1)S(1)} %collective-permute-done.q_other_ref, ...), custom_call_target="tpu_custom_call" | custom-call | flops 1000000000 | bytes 1048576 | tf_op jit(solution)/shard_map/arrange/pallas_call | solution.py:29
  25.8 6.9 %prob.1 = (bf16[4,2,640,512]{3,2,1,0:T(8,128)(2,1)S(1)}, bf16[4,2,128,128]{3,2,1,0:T(8,128)(2,1)S(1)}, bf16[4,2,128,128]{3,2,1,0:T(8,128)(2,1)S(1)}) custom-call(s32[2]{0:T(128)S(1)} %pad_add_fusion.place_ref, s32[16]{0:T(128)S(1)} %copy-done.4, bf16[4,2,2,4,128,128]{5,4,3,2,1,0:T(8,128)(2,1)S(1)} %arrange.1.qd_ref, ...), custom_call_target="tpu_custom_call" | custom-call | flops 2684354560 | bytes 1048576 | tf_op jit(solution)/shard_map/prob/pallas_call | solution.py:29
  32.7 3.4 %collective-permute-start.8 = (bf16[4,2,128,128]{3,2,1,0:T(8,128)(2,1)S(1)}, bf16[4,2,128,128]{3,2,1,0:T(8,128)(2,1)S(1)}, u32[]{:S(2)}, u32[]{:S(2)}) collective-permute-start(bf16[4,2,128,128]{3,2,1,0:T(8,128)(2,1)S(1)} %get-tuple-element.19), channel_id=1, source_target_pairs={{4,0},{5,1},{6,2},{7,3},{8,4},{9,5},{10,6},{11,7},{12,8},{13,9},{1... | collective-permute-start | bytes 786440 | tf_op jit(solution)/shard_map/ppermute | solution.py:20
  36.1 6.1 %collective-permute-start.9 = (bf16[4,2,128,128]{3,2,1,0:T(8,128)(2,1)S(1)}, bf16[4,2,128,128]{3,2,1,0:T(8,128)(2,1)S(1)}, u32[]{:S(2)}, u32[]{:S(2)}) collective-permute-start(bf16[4,2,128,128]{3,2,1,0:T(8,128)(2,1)S(1)} %get-tuple-element.20), channel_id=1, source_target_pairs={{2,0},{3,1},{4,2},{5,3},{6,4},{7,5},{8,6},{9,7},{10,8},{11,9},{12,... | collective-permute-start | bytes 786440 | tf_op jit(solution)/shard_map/ppermute | solution.py:20
  42.2 6.1 %dscore.1 = (bf16[4,2,640,512]{3,2,1,0:T(8,128)(2,1)S(1)}, bf16[4,2,128,128]{3,2,1,0:T(8,128)(2,1)S(1)}, bf16[4,2,128,128]{3,2,1,0:T(8,128)(2,1)S(1)}) custom-call(s32[2]{0:T(128)S(1)} %pad_add_fusion.place_ref, bf16[4,2,2,4,128,128]{5,4,3,2,1,0:T(8,128)(2,1)S(1)} %arrange.1.qd_ref, bf16[4,2,640,512]{3,2,1,0:T(8,128)(2,1)S(1)} %get-tuple-element.17.p_ref, ...), custom_call_target="tpu_custom_call" | custom-call | flops 2684354560 | bytes 1048576 | tf_op jit(solution)/shard_map/dscore/pallas_call | solution.py:29
  48.3 5.5 %collective-permute-done.9.refs_4_ = bf16[4,2,128,128]{3,2,1,0:T(8,128)(2,1)S(1)} collective-permute-done((bf16[4,2,128,128]{3,2,1,0:T(8,128)(2,1)S(1)}, bf16[4,2,128,128]{3,2,1,0:T(8,128)(2,1)S(1)}, u32[]{:S(2)}, u32[]{:S(2)}) %collective-permute-start.9) | collective-permute-done | bytes 262176 | tf_op jit(solution)/shard_map/ppermute | solution.py:20
  53.8 3.1 %own.1 = (bf16[4,4,128,128]{3,2,1,0:T(8,128)(2,1)S(1)}, bf16[4,4,128,128]{3,2,1,0:T(8,128)(2,1)S(1)}, f32[4,2,128,128]{3,2,1,0:T(8,128)S(1)}, bf16[4,128,128]{2,1,0:T(8,128)(2,1)S(1)}, bf16[4,128,128]{2,1,0:T(8,128)(2,1)S(1)}) custom-call(s32[2]{0:T(128)S(1)} %pad_add_fusion.place_ref, bf16[4,2,2,4,128,128]{5,4,3,2,1,0:T(8,128)(2,1)S(1)} %arrange.1.qd_ref, ...), custom_call_target="tpu_custom_call" | custom-call | flops 2684354560 | bytes 1048576 | tf_op jit(solution)/shard_map/own/pallas_call | solution.py:29
  56.9 1.5 %collective-permute-start.10 = (bf16[4,4,128,128]{3,2,1,0:T(8,128)(2,1)S(1)}, bf16[4,4,128,128]{3,2,1,0:T(8,128)(2,1)S(1)}, u32[]{:S(2)}, u32[]{:S(2)}) collective-permute-start(bf16[4,4,128,128]{3,2,1,0:T(8,128)(2,1)S(1)} %get-tuple-element.23), channel_id=1, source_target_pairs={{0,1},{1,0},{2,3},{3,2},{4,5},{5,4},{6,7},{7,6},{8,9},{9,8},{10,11... | collective-permute-start | bytes 1572872 | tf_op jit(solution)/shard_map/ppermute | solution.py:24
  58.4 0.1 collective-permute-start.11
  58.5 1.9 %collective-permute-start.12 = (bf16[4,2,128,128]{3,2,1,0:T(8,128)(2,1)S(1)}, bf16[4,2,128,128]{3,2,1,0:T(8,128)(2,1)S(1)}, u32[]{:S(2)}, u32[]{:S(2)}) collective-permute-start(bf16[4,2,128,128]{3,2,1,0:T(8,128)(2,1)S(1)} %get-tuple-element.28), channel_id=1, source_target_pairs={{4,0},{5,1},{6,2},{7,3},{8,4},{9,5},{10,6},{11,7},{12,8},{13,9},{1... | collective-permute-start | bytes 786440 | tf_op jit(solution)/shard_map/ppermute | solution.py:20
  60.4 1.9 %collective-permute-start.13 = (bf16[4,2,128,128]{3,2,1,0:T(8,128)(2,1)S(1)}, bf16[4,2,128,128]{3,2,1,0:T(8,128)(2,1)}, u32[]{:S(2)}, u32[]{:S(2)}) collective-permute-start(bf16[4,2,128,128]{3,2,1,0:T(8,128)(2,1)S(1)} %get-tuple-element.29), channel_id=1, source_target_pairs={{2,0},{3,1},{4,2},{5,3},{6,4},{7,5},{8,6},{9,7},{10,8},{11,9},{12,... | collective-permute-start | bytes 786440 | tf_op jit(solution)/shard_map/ppermute | solution.py:20
  62.3 1.4 %merge_dv.1 = bf16[128,8,128]{2,1,0:T(8,128)(2,1)} custom-call(s32[2]{0:T(128)S(1)} %pad_add_fusion.place_ref, bf16[4,128,128]{2,1,0:T(8,128)(2,1)S(1)} %get-tuple-element.24.own_ref, bf16[4,128,128]{2,1,0:T(8,128)(2,1)S(1)} %collective-permute-done.11.other_ref), custom_call_target="tpu_custom_call" | custom-call | flops 1000000000 | bytes 1048576 | tf_op jit(solution)/shard_map/merge_dv/pallas_call | solution.py:29
  63.7 3.6 %merge_dq.1 = bf16[128,32,128]{2,1,0:T(8,128)(2,1)} custom-call(s32[2]{0:T(128)S(1)} %pad_add_fusion.place_ref, bf16[16,128,128]{2,1,0:T(8,128)(2,1)S(1)} %bitcast.8, bf16[16,128,128]{2,1,0:T(8,128)(2,1)S(1)} %bitcast.9), custom_call_target="tpu_custom_call" | custom-call | flops 1000000000 | bytes 1048576 | tf_op jit(solution)/shard_map/merge_dq/pallas_call | solution.py:29
  67.3 4.2 %collective-permute-done.12 = bf16[4,2,128,128]{3,2,1,0:T(8,128)(2,1)S(1)} collective-permute-done((bf16[4,2,128,128]{3,2,1,0:T(8,128)(2,1)S(1)}, bf16[4,2,128,128]{3,2,1,0:T(8,128)(2,1)S(1)}, u32[]{:S(2)}, u32[]{:S(2)}) %collective-permute-start.12) | collective-permute-done | bytes 262176 | tf_op jit(solution)/shard_map/ppermute | solution.py:20
  71.5 2.6 %collective-permute-done.13 = bf16[4,2,128,128]{3,2,1,0:T(8,128)(2,1)} collective-permute-done((bf16[4,2,128,128]{3,2,1,0:T(8,128)(2,1)S(1)}, bf16[4,2,128,128]{3,2,1,0:T(8,128)(2,1)}, u32[]{:S(2)}, u32[]{:S(2)}) %collective-permute-start.13) | collective-permute-done | bytes 262176 | tf_op jit(solution)/shard_map/ppermute | solution.py:20
  74.1 1.0 %add_convert_fusion = bf16[4,2,128,128]{3,2,1,0:T(8,128)(2,1)S(1)} fusion(bf16[4,2,128,128]{3,2,1,0:T(8,128)(2,1)} %collective-permute-done.13, f32[4,2,128,128]{3,2,1,0:T(8,128)S(1)} %get-tuple-element.27, bf16[4,2,128,128]{3,2,1,0:T(8,128)(2,1)S(1)} %collective-permute-done.12), kind=kLoop, calls=%fused_computation | loop fusion | flops 655360 | bytes 1310720 | tf_op jit(solution)/shard_map/convert_element_type | solution.py:352
  75.2 1.6 %collective-permute-start.14 = (bf16[4,128,128]{2,1,0:T(8,128)(2,1)S(1)}, bf16[4,128,128]{2,1,0:T(8,128)(2,1)S(1)}, u32[]{:S(2)}, u32[]{:S(2)}) collective-permute-start(bf16[4,128,128]{2,1,0:T(8,128)(2,1)S(1)} %get-tuple-element.31), channel_id=1, source_target_pairs={{0,1},{1,0},{2,3},{3,2},{4,5},{5,4},{6,7},{7,6},{8,9},{9,8},{10,11... | collective-permute-start | bytes 393224 | tf_op jit(solution)/shard_map/ppermute | solution.py:24
  76.8 1.0 %collective-permute-done.14.other_ref = bf16[4,128,128]{2,1,0:T(8,128)(2,1)S(1)} collective-permute-done((bf16[4,128,128]{2,1,0:T(8,128)(2,1)S(1)}, bf16[4,128,128]{2,1,0:T(8,128)(2,1)S(1)}, u32[]{:S(2)}, u32[]{:S(2)}) %collective-permute-start.14) | collective-permute-done | bytes 131104 | tf_op jit(solution)/shard_map/ppermute | solution.py:24
  77.8 1.4 %merge_dk.1 = bf16[128,8,128]{2,1,0:T(8,128)(2,1)} custom-call(s32[2]{0:T(128)S(1)} %pad_add_fusion.place_ref, bf16[4,128,128]{2,1,0:T(8,128)(2,1)S(1)} %get-tuple-element.32.own_ref, bf16[4,128,128]{2,1,0:T(8,128)(2,1)S(1)} %collective-permute-done.14.other_ref), custom_call_target="tpu_custom_call" | custom-call | flops 1000000000 | bytes 1048576 | tf_op jit(solution)/shard_map/merge_dk/pallas_call | solution.py:29
  (20 shorter events, 0.1 us)
Async XLA Ops:
  0.6 21.3 %copy-start = (bf16[128,32,128]{2,1,0:T(8,128)(2,1)S(1)}, bf16[128,32,128]{2,1,0:T(8,128)(2,1)}, u32[]{:S(2)}) copy-start(bf16[128,32,128]{2,1,0:T(8,128)(2,1)} %q_ref.1) | copy-start | bytes 3145732
  0.6 21.3 %copy-start.1 = (bf16[128,32,128]{2,1,0:T(8,128)(2,1)S(1)}, bf16[128,32,128]{2,1,0:T(8,128)(2,1)}, u32[]{:S(2)}) copy-start(bf16[128,32,128]{2,1,0:T(8,128)(2,1)} %do_ref.1) | copy-start | bytes 3145732
  0.6 19.3 %collective-permute-start = (bf16[128,32,128]{2,1,0:T(8,128)(2,1)}, bf16[128,32,128]{2,1,0:T(8,128)(2,1)S(1)}, u32[]{:S(2)}, u32[]{:S(2)}) collective-permute-start(bf16[128,32,128]{2,1,0:T(8,128)(2,1)} %q_ref.1), channel_id=1, source_target_pairs={{0,1},{1,0},{2,3},{3,2},{4,5},{5,4},{6,7},{7,6},{8,9},{9,8},{10,11... | collective-permute-start | bytes 3145736 | tf_op jit(solution)/shard_map/ppermute | solution.py:24
  1.4 20.5 %collective-permute-start.1 = (bf16[128,32,128]{2,1,0:T(8,128)(2,1)}, bf16[128,32,128]{2,1,0:T(8,128)(2,1)}, u32[]{:S(2)}, u32[]{:S(2)}) collective-permute-start(bf16[128,32,128]{2,1,0:T(8,128)(2,1)} %do_ref.1), channel_id=1, source_target_pairs={{0,1},{1,0},{2,3},{3,2},{4,5},{5,4},{6,7},{7,6},{8,9},{9,8},{10,11... | collective-permute-start | bytes 3145736 | tf_op jit(solution)/shard_map/ppermute | solution.py:24
  1.5 4.8 %collective-permute-start.2 = (bf16[128,8,128]{2,1,0:T(8,128)(2,1)}, bf16[128,8,128]{2,1,0:T(8,128)(2,1)}, u32[]{:S(2)}, u32[]{:S(2)}) collective-permute-start(bf16[128,8,128]{2,1,0:T(8,128)(2,1)} %own_ref.2), channel_id=1, source_target_pairs={{0,1},{1,0},{2,3},{3,2},{4,5},{5,4},{6,7},{7,6},{8,9},{9,8},{10,11... | collective-permute-start | bytes 786440 | tf_op jit(solution)/shard_map/ppermute | solution.py:24
  1.9 13.3 %collective-permute-start.5 = (bf16[128,8,128]{2,1,0:T(8,128)(2,1)}, bf16[128,8,128]{2,1,0:T(8,128)(2,1)S(1)}, u32[]{:S(2)}, u32[]{:S(2)}) collective-permute-start(bf16[128,8,128]{2,1,0:T(8,128)(2,1)} %own_ref.3), channel_id=1, source_target_pairs={{0,1},{1,0},{2,3},{3,2},{4,5},{5,4},{6,7},{7,6},{8,9},{9,8},{10,11... | collective-permute-start | bytes 786440 | tf_op jit(solution)/shard_map/ppermute | solution.py:24
  6.3 0.9 %copy-start.2 = (bf16[128,8,128]{2,1,0:T(8,128)(2,1)S(1)}, bf16[128,8,128]{2,1,0:T(8,128)(2,1)}, u32[]{:S(2)}) copy-start(bf16[128,8,128]{2,1,0:T(8,128)(2,1)} %own_ref.2) | copy-start | bytes 786436
  7.2 18.6 %copy-start.4 = (s32[16]{0:T(128)S(1)}, s32[16]{0:T(128)}, u32[]{:S(2)}) copy-start(s32[16]{0:T(128)} %lengths_ref.1) | copy-start | bytes 196
  8.9 16.9 %collective-permute-start.3 = (bf16[4,2,128,128]{3,2,1,0:T(8,128)(2,1)S(1)}, bf16[4,2,128,128]{3,2,1,0:T(8,128)(2,1)S(1)}, u32[]{:S(2)}, u32[]{:S(2)}) collective-permute-start(bf16[4,2,128,128]{3,2,1,0:T(8,128)(2,1)S(1)} %pack_k.1.refs_0_), channel_id=1, source_target_pairs={{0,2},{1,3},{2,4},{3,5},{4,6},{5,7},{6,8},{7,9},{8,10},{9,11},{10,... | collective-permute-start | bytes 786440 | tf_op jit(solution)/shard_map/ppermute | solution.py:20
  12.0 13.8 %collective-permute-start.4 = (bf16[4,2,128,128]{3,2,1,0:T(8,128)(2,1)S(1)}, bf16[4,2,128,128]{3,2,1,0:T(8,128)(2,1)S(1)}, u32[]{:S(2)}, u32[]{:S(2)}) collective-permute-start(bf16[4,2,128,128]{3,2,1,0:T(8,128)(2,1)S(1)} %pack_k.1.refs_0_), channel_id=1, source_target_pairs={{0,4},{1,5},{2,6},{3,7},{4,8},{5,9},{6,10},{7,11},{8,12},{9,13},{1... | collective-permute-start | bytes 786440 | tf_op jit(solution)/shard_map/ppermute | solution.py:20
  15.2 1.0 %copy-start.3 = (bf16[128,8,128]{2,1,0:T(8,128)(2,1)S(1)}, bf16[128,8,128]{2,1,0:T(8,128)(2,1)}, u32[]{:S(2)}) copy-start(bf16[128,8,128]{2,1,0:T(8,128)(2,1)} %own_ref.3) | copy-start | bytes 786436
  16.8 25.3 %collective-permute-start.6 = (bf16[4,2,128,128]{3,2,1,0:T(8,128)(2,1)S(1)}, bf16[4,2,128,128]{3,2,1,0:T(8,128)(2,1)S(1)}, u32[]{:S(2)}, u32[]{:S(2)}) collective-permute-start(bf16[4,2,128,128]{3,2,1,0:T(8,128)(2,1)S(1)} %pack_v.1.refs_0_), channel_id=1, source_target_pairs={{0,2},{1,3},{2,4},{3,5},{4,6},{5,7},{6,8},{7,9},{8,10},{9,11},{10,... | collective-permute-start | bytes 786440 | tf_op jit(solution)/shard_map/ppermute | solution.py:20
  20.0 22.2 %collective-permute-start.7 = (bf16[4,2,128,128]{3,2,1,0:T(8,128)(2,1)S(1)}, bf16[4,2,128,128]{3,2,1,0:T(8,128)(2,1)S(1)}, u32[]{:S(2)}, u32[]{:S(2)}) collective-permute-start(bf16[4,2,128,128]{3,2,1,0:T(8,128)(2,1)S(1)} %pack_v.1.refs_0_), channel_id=1, source_target_pairs={{0,4},{1,5},{2,6},{3,7},{4,8},{5,9},{6,10},{7,11},{8,12},{9,13},{1... | collective-permute-start | bytes 786440 | tf_op jit(solution)/shard_map/ppermute | solution.py:20
  32.7 15.6 %collective-permute-start.8 = (bf16[4,2,128,128]{3,2,1,0:T(8,128)(2,1)S(1)}, bf16[4,2,128,128]{3,2,1,0:T(8,128)(2,1)S(1)}, u32[]{:S(2)}, u32[]{:S(2)}) collective-permute-start(bf16[4,2,128,128]{3,2,1,0:T(8,128)(2,1)S(1)} %get-tuple-element.19), channel_id=1, source_target_pairs={{4,0},{5,1},{6,2},{7,3},{8,4},{9,5},{10,6},{11,7},{12,8},{13,9},{1... | collective-permute-start | bytes 786440 | tf_op jit(solution)/shard_map/ppermute | solution.py:20
  36.1 17.7 %collective-permute-start.9 = (bf16[4,2,128,128]{3,2,1,0:T(8,128)(2,1)S(1)}, bf16[4,2,128,128]{3,2,1,0:T(8,128)(2,1)S(1)}, u32[]{:S(2)}, u32[]{:S(2)}) collective-permute-start(bf16[4,2,128,128]{3,2,1,0:T(8,128)(2,1)S(1)} %get-tuple-element.20), channel_id=1, source_target_pairs={{2,0},{3,1},{4,2},{5,3},{6,4},{7,5},{8,6},{9,7},{10,8},{11,9},{12,... | collective-permute-start | bytes 786440 | tf_op jit(solution)/shard_map/ppermute | solution.py:20
  56.9 6.8 %collective-permute-start.10 = (bf16[4,4,128,128]{3,2,1,0:T(8,128)(2,1)S(1)}, bf16[4,4,128,128]{3,2,1,0:T(8,128)(2,1)S(1)}, u32[]{:S(2)}, u32[]{:S(2)}) collective-permute-start(bf16[4,4,128,128]{3,2,1,0:T(8,128)(2,1)S(1)} %get-tuple-element.23), channel_id=1, source_target_pairs={{0,1},{1,0},{2,3},{3,2},{4,5},{5,4},{6,7},{7,6},{8,9},{9,8},{10,11... | collective-permute-start | bytes 1572872 | tf_op jit(solution)/shard_map/ppermute | solution.py:24
  58.4 3.9 %collective-permute-start.11 = (bf16[4,128,128]{2,1,0:T(8,128)(2,1)S(1)}, bf16[4,128,128]{2,1,0:T(8,128)(2,1)S(1)}, u32[]{:S(2)}, u32[]{:S(2)}) collective-permute-start(bf16[4,128,128]{2,1,0:T(8,128)(2,1)S(1)} %get-tuple-element.25), channel_id=1, source_target_pairs={{0,1},{1,0},{2,3},{3,2},{4,5},{5,4},{6,7},{7,6},{8,9},{9,8},{10,11... | collective-permute-start | bytes 393224 | tf_op jit(solution)/shard_map/ppermute | solution.py:24
  58.5 13.1 %collective-permute-start.12 = (bf16[4,2,128,128]{3,2,1,0:T(8,128)(2,1)S(1)}, bf16[4,2,128,128]{3,2,1,0:T(8,128)(2,1)S(1)}, u32[]{:S(2)}, u32[]{:S(2)}) collective-permute-start(bf16[4,2,128,128]{3,2,1,0:T(8,128)(2,1)S(1)} %get-tuple-element.28), channel_id=1, source_target_pairs={{4,0},{5,1},{6,2},{7,3},{8,4},{9,5},{10,6},{11,7},{12,8},{13,9},{1... | collective-permute-start | bytes 786440 | tf_op jit(solution)/shard_map/ppermute | solution.py:20
  60.4 13.7 %collective-permute-start.13 = (bf16[4,2,128,128]{3,2,1,0:T(8,128)(2,1)S(1)}, bf16[4,2,128,128]{3,2,1,0:T(8,128)(2,1)}, u32[]{:S(2)}, u32[]{:S(2)}) collective-permute-start(bf16[4,2,128,128]{3,2,1,0:T(8,128)(2,1)S(1)} %get-tuple-element.29), channel_id=1, source_target_pairs={{2,0},{3,1},{4,2},{5,3},{6,4},{7,5},{8,6},{9,7},{10,8},{11,9},{12,... | collective-permute-start | bytes 786440 | tf_op jit(solution)/shard_map/ppermute | solution.py:20
  75.2 2.6 %collective-permute-start.14 = (bf16[4,128,128]{2,1,0:T(8,128)(2,1)S(1)}, bf16[4,128,128]{2,1,0:T(8,128)(2,1)S(1)}, u32[]{:S(2)}, u32[]{:S(2)}) collective-permute-start(bf16[4,128,128]{2,1,0:T(8,128)(2,1)S(1)} %get-tuple-element.31), channel_id=1, source_target_pairs={{0,1},{1,0},{2,3},{3,2},{4,5},{5,4},{6,7},{7,6},{8,9},{9,8},{10,11... | collective-permute-start | bytes 393224 | tf_op jit(solution)/shard_map/ppermute | solution.py:24

commit v4 on v3

--- a/solution.py
+++ b/solution.py
@@ -37,7 +37,7 @@
             scratch_shapes=scratch,
         ),
         compiler_params=pltpu.CompilerParams(vmem_limit_bytes=VMEM_BYTES),
-        cost_estimate=pl.CostEstimate(flops=flops, bytes_accessed=2**20, transcendentals=0),
+        cost_estimate=pl.CostEstimate(flops=flops, bytes_accessed=0, transcendentals=0),
         name=name,
     )(*scalars, *inputs)
 
@@ -249,7 +249,7 @@
         jax.ShapeDtypeStruct((tokens, 2 * half, dim), BF16),
         pl.BlockSpec((rows, 2 * half, dim), lambda i, place: (i, 0, 0)),
         [pltpu.VMEM((rows * 2 * half, dim), F32)],
-        10**9,
+        4 * 10**9,
     )
 
 
@@ -268,6 +268,7 @@
 
     far_first = range(halo, 0, -1)
     k_own = pack(place, keys, swapped(keys, device_count), "pack_k")
+    k_own, queries, grad_out = lax.optimization_barrier((k_own, queries, grad_out))
     v_own = pack(place, values, swapped(values, device_count), "pack_v")
     qd = arrange(
         place, queries, grad_out, swapped(queries, device_count), swapped(grad_out, device_count), key_heads
@@ -338,7 +339,7 @@
             pltpu.VMEM((2, group, tokens, dim), BF16),
             pltpu.VMEM((2, tokens, dim), F32),
         ],
-        4 * product,
+        0,
     )
     dq_other = swapped(dq_other, device_count)
     dv_other = swapped(dv_other, device_count)
@@ -346,7 +347,7 @@
     grad_queries = merge(place, dq.reshape(flat), dq_other.reshape(flat), 32, "merge_dq")
     grad_values = merge(place, dv, dv_other, tokens, "merge_dv")
 
-    total, grad_queries, grad_values = lax.optimization_barrier((dk_own, grad_queries, grad_values))
+    total = dk_own
     for back in dk_back:
         total = total + back.astype(F32)
     total = total.astype(BF16)

time: 79.7 us -> 77.7 us (0.975)
  the two profiles are of different devices: /device:TPU:23 before, /device:TPU:25 now
where the time goes in v4:
time: 77.7 us; the launch traced here: 77.2 us
  Pallas kernels  27 us (35%)
  starting transfers between devices  26.4 us (34%)
  local copies, waits for them, and re-layouts  13.5 us (17%)
  waiting for transfers between devices  8.24 us (11%)
  other arithmetic  1.21 us (2%)
  between operations  0.88 us (1%)
    pallas_call x9, Pallas kernels, call(): pl.pallas_call(kernel, out_shape=outs, grid_spec=pltpu.PrefetchScalarGrid...  27 us
    ppermute x8, starting transfers between devices, moved(): return lax.ppermute(array, AXES, pairs)  22.3 us
    unnamed x26, local copies, waits for them, and re-layouts  13.5 us
    ppermute x8, waiting for transfers between devices, moved(): return lax.ppermute(array, AXES, pairs)  6.93 us
    ppermute x7, starting transfers between devices, swapped(): return lax.ppermute(array, AXES, [(d, d ^ 1) for d in range(device_count)])  4.01 us
  transfers between devices with their start and end apart: 15, of which 2 were waited for; matrix products, arithmetic and copies ran while one was open for 2% of the time, Pallas kernels for 29%

profile of v4, /device:TPU:25, one launch (start us, length us, event | category | flops | bytes accessed | tf_op | source)
XLA Modules:
  0.0 77.2 jit_solution(10509038420325404494)
XLA Ops:
  0.6 0.7 collective-permute-start
  1.5 1.3 %collective-permute-done.other_ref = bf16[128,8,128]{2,1,0:T(8,128)(2,1)S(1)} collective-permute-done((bf16[128,8,128]{2,1,0:T(8,128)(2,1)}, bf16[128,8,128]{2,1,0:T(8,128)(2,1)S(1)}, u32[]{:S(2)}, u32[]{:S(2)}) %collective-permute-start) | collective-permute-done | bytes 262176 | tf_op jit(solution)/shard_map/ppermute | solution.py:24
  2.8 0.9 %copy-done.10 = bf16[128,8,128]{2,1,0:T(8,128)(2,1)S(1)} copy-done((bf16[128,8,128]{2,1,0:T(8,128)(2,1)S(1)}, bf16[128,8,128]{2,1,0:T(8,128)(2,1)}, u32[]{:S(2)}) %copy-start.10) | copy-done | bytes 262168
  3.7 0.7 pack_k.1.refs_0_
  4.4 0.4 collective-permute-start.1
  5.4 3.1 %collective-permute-start.3 = (bf16[4,2,128,128]{3,2,1,0:T(8,128)(2,1)S(1)}, bf16[4,2,128,128]{3,2,1,0:T(8,128)(2,1)S(1)}, u32[]{:S(2)}, u32[]{:S(2)}) collective-permute-start(bf16[4,2,128,128]{3,2,1,0:T(8,128)(2,1)S(1)} %pack_k.1.refs_0_), channel_id=1, source_target_pairs={{0,2},{1,3},{2,4},{3,5},{4,6},{5,7},{6,8},{7,9},{8,10},{9,11},{10,... | collective-permute-start | bytes 786440 | tf_op jit(solution)/shard_map/ppermute | solution.py:20
  8.5 3.1 %collective-permute-start.4 = (bf16[4,2,128,128]{3,2,1,0:T(8,128)(2,1)S(1)}, bf16[4,2,128,128]{3,2,1,0:T(8,128)(2,1)S(1)}, u32[]{:S(2)}, u32[]{:S(2)}) collective-permute-start(bf16[4,2,128,128]{3,2,1,0:T(8,128)(2,1)S(1)} %pack_k.1.refs_0_), channel_id=1, source_target_pairs={{0,4},{1,5},{2,6},{3,7},{4,8},{5,9},{6,10},{7,11},{8,12},{9,13},{1... | collective-permute-start | bytes 786440 | tf_op jit(solution)/shard_map/ppermute | solution.py:20
  11.7 0.9 %copy-done.11 = bf16[128,8,128]{2,1,0:T(8,128)(2,1)S(1)} copy-done((bf16[128,8,128]{2,1,0:T(8,128)(2,1)S(1)}, bf16[128,8,128]{2,1,0:T(8,128)(2,1)}, u32[]{:S(2)}) %copy-start.11) | copy-done | bytes 262168
  12.6 0.7 pack_v.1.refs_0_
  13.3 1.9 %collective-permute-start.6 = (bf16[4,2,128,128]{3,2,1,0:T(8,128)(2,1)S(1)}, bf16[4,2,128,128]{3,2,1,0:T(8,128)(2,1)S(1)}, u32[]{:S(2)}, u32[]{:S(2)}) collective-permute-start(bf16[4,2,128,128]{3,2,1,0:T(8,128)(2,1)S(1)} %pack_v.1.refs_0_), channel_id=1, source_target_pairs={{0,2},{1,3},{2,4},{3,5},{4,6},{5,7},{6,8},{7,9},{8,10},{9,11},{10,... | collective-permute-start | bytes 786440 | tf_op jit(solution)/shard_map/ppermute | solution.py:20
  15.3 1.9 %collective-permute-start.7 = (bf16[4,2,128,128]{3,2,1,0:T(8,128)(2,1)S(1)}, bf16[4,2,128,128]{3,2,1,0:T(8,128)(2,1)S(1)}, u32[]{:S(2)}, u32[]{:S(2)}) collective-permute-start(bf16[4,2,128,128]{3,2,1,0:T(8,128)(2,1)S(1)} %pack_v.1.refs_0_), channel_id=1, source_target_pairs={{0,4},{1,5},{2,6},{3,7},{4,8},{5,9},{6,10},{7,11},{8,12},{9,13},{1... | collective-permute-start | bytes 786440 | tf_op jit(solution)/shard_map/ppermute | solution.py:20
  17.2 2.5 %arrange.1.qd_ref = bf16[4,2,2,4,128,128]{5,4,3,2,1,0:T(8,128)(2,1)S(1)} custom-call(s32[2]{0:T(128)S(1)} %pad_add_fusion.place_ref, bf16[128,32,128]{2,1,0:T(8,128)(2,1)S(1)} %copy-done.4, bf16[128,32,128]{2,1,0:T(8,128)(2,1)S(1)} %copy-done.5, bf16[128,32,128]{2,1,0:T(8,128)(2,1)S(1)} %collective-permute-done.1.q_other_ref, ...), custom_call_target="tpu_custom_call" | custom-call | flops 1000000000 | tf_op jit(solution)/shard_map/arrange/pallas_call | solution.py:29
  19.8 6.9 %collective-permute-done.4.refs_2_ = bf16[4,2,128,128]{3,2,1,0:T(8,128)(2,1)S(1)} collective-permute-done((bf16[4,2,128,128]{3,2,1,0:T(8,128)(2,1)S(1)}, bf16[4,2,128,128]{3,2,1,0:T(8,128)(2,1)S(1)}, u32[]{:S(2)}, u32[]{:S(2)}) %collective-permute-start.4) | collective-permute-done | bytes 262176 | tf_op jit(solution)/shard_map/ppermute | solution.py:20
  26.7 6.9 %prob.1 = (bf16[4,2,640,512]{3,2,1,0:T(8,128)(2,1)S(1)}, bf16[4,2,128,128]{3,2,1,0:T(8,128)(2,1)S(1)}, bf16[4,2,128,128]{3,2,1,0:T(8,128)(2,1)S(1)}) custom-call(s32[2]{0:T(128)S(1)} %pad_add_fusion.place_ref, s32[16]{0:T(128)S(1)} %copy-done.12, bf16[4,2,2,4,128,128]{5,4,3,2,1,0:T(8,128)(2,1)S(1)} %arrange.1.qd_ref, ...), custom_call_target="tpu_custom_call" | custom-call | flops 2684354560 | tf_op jit(solution)/shard_map/prob/pallas_call | solution.py:29
  33.6 4.0 %collective-permute-start.8 = (bf16[4,2,128,128]{3,2,1,0:T(8,128)(2,1)S(1)}, bf16[4,2,128,128]{3,2,1,0:T(8,128)(2,1)S(1)}, u32[]{:S(2)}, u32[]{:S(2)}) collective-permute-start(bf16[4,2,128,128]{3,2,1,0:T(8,128)(2,1)S(1)} %get-tuple-element.22), channel_id=1, source_target_pairs={{4,0},{5,1},{6,2},{7,3},{8,4},{9,5},{10,6},{11,7},{12,8},{13,9},{1... | collective-permute-start | bytes 786440 | tf_op jit(solution)/shard_map/ppermute | solution.py:20
  37.6 1.9 %collective-permute-start.9 = (bf16[4,2,128,128]{3,2,1,0:T(8,128)(2,1)S(1)}, bf16[4,2,128,128]{3,2,1,0:T(8,128)(2,1)S(1)}, u32[]{:S(2)}, u32[]{:S(2)}) collective-permute-start(bf16[4,2,128,128]{3,2,1,0:T(8,128)(2,1)S(1)} %get-tuple-element.23), channel_id=1, source_target_pairs={{2,0},{3,1},{4,2},{5,3},{6,4},{7,5},{8,6},{9,7},{10,8},{11,9},{12,... | collective-permute-start | bytes 786440 | tf_op jit(solution)/shard_map/ppermute | solution.py:20
  39.5 6.7 %dscore.1 = (bf16[4,2,640,512]{3,2,1,0:T(8,128)(2,1)S(1)}, bf16[4,2,128,128]{3,2,1,0:T(8,128)(2,1)}, bf16[4,2,128,128]{3,2,1,0:T(8,128)(2,1)}) custom-call(s32[2]{0:T(128)S(1)} %pad_add_fusion.place_ref, bf16[4,2,2,4,128,128]{5,4,3,2,1,0:T(8,128)(2,1)S(1)} %arrange.1.qd_ref, bf16[4,2,640,512]{3,2,1,0:T(8,128)(2,1)S(1)} %get-tuple-element.20.p_ref, ...), custom_call_target="tpu_custom_call" | custom-call | flops 2684354560 | tf_op jit(solution)/shard_map/dscore/pallas_call | solution.py:29
  46.2 2.3 %copy-done = bf16[4,2,640,512]{3,2,1,0:T(8,128)(2,1)} copy-done((bf16[4,2,640,512]{3,2,1,0:T(8,128)(2,1)}, bf16[4,2,640,512]{3,2,1,0:T(8,128)(2,1)S(1)}, u32[]{:S(2)}) %copy-start) | copy-done | bytes 5242904
  48.5 2.4 %copy-done.2 = bf16[4,2,640,512]{3,2,1,0:T(8,128)(2,1)} copy-done((bf16[4,2,640,512]{3,2,1,0:T(8,128)(2,1)}, bf16[4,2,640,512]{3,2,1,0:T(8,128)(2,1)S(1)}, u32[]{:S(2)}) %copy-start.2) | copy-done | bytes 5242904
  50.9 1.9 %collective-permute-start.11 = (bf16[4,2,128,128]{3,2,1,0:T(8,128)(2,1)}, bf16[4,2,128,128]{3,2,1,0:T(8,128)(2,1)}, u32[]{:S(2)}, u32[]{:S(2)}) collective-permute-start(bf16[4,2,128,128]{3,2,1,0:T(8,128)(2,1)} %get-tuple-element.27), channel_id=1, source_target_pairs={{4,0},{5,1},{6,2},{7,3},{8,4},{9,5},{10,6},{11,7},{12,8},{13,9},{1... | collective-permute-start | bytes 786440 | tf_op jit(solution)/shard_map/ppermute | solution.py:20
  52.8 4.4 %collective-permute-start.12 = (bf16[4,2,128,128]{3,2,1,0:T(8,128)(2,1)}, bf16[4,2,128,128]{3,2,1,0:T(8,128)(2,1)}, u32[]{:S(2)}, u32[]{:S(2)}) collective-permute-start(bf16[4,2,128,128]{3,2,1,0:T(8,128)(2,1)} %get-tuple-element.28), channel_id=1, source_target_pairs={{2,0},{3,1},{4,2},{5,3},{6,4},{7,5},{8,6},{9,7},{10,8},{11,9},{12,... | collective-permute-start | bytes 786440 | tf_op jit(solution)/shard_map/ppermute | solution.py:20
  57.3 2.5 %copy-done.1 = bf16[4,2,640,512]{3,2,1,0:T(8,128)(2,1)S(1)} copy-done((bf16[4,2,640,512]{3,2,1,0:T(8,128)(2,1)S(1)}, bf16[4,2,640,512]{3,2,1,0:T(8,128)(2,1)}, u32[]{:S(2)}) %copy-start.1) | copy-done | bytes 5242904
  59.8 2.5 %copy-done.3 = bf16[4,2,640,512]{3,2,1,0:T(8,128)(2,1)S(1)} copy-done((bf16[4,2,640,512]{3,2,1,0:T(8,128)(2,1)S(1)}, bf16[4,2,640,512]{3,2,1,0:T(8,128)(2,1)}, u32[]{:S(2)}) %copy-start.3) | copy-done | bytes 5242904
  62.3 0.9 %copy-done.7 = bf16[4,2,128,128]{3,2,1,0:T(8,128)(2,1)S(1)} copy-done((bf16[4,2,128,128]{3,2,1,0:T(8,128)(2,1)S(1)}, bf16[4,2,128,128]{3,2,1,0:T(8,128)(2,1)}, u32[]{:S(2)}) %copy-start.7) | copy-done | bytes 262168
  63.2 0.9 %copy-done.9 = bf16[4,2,128,128]{3,2,1,0:T(8,128)(2,1)S(1)} copy-done((bf16[4,2,128,128]{3,2,1,0:T(8,128)(2,1)S(1)}, bf16[4,2,128,128]{3,2,1,0:T(8,128)(2,1)}, u32[]{:S(2)}) %copy-start.9) | copy-done | bytes 262168
  64.2 3.2 %own.1 = (bf16[4,4,128,128]{3,2,1,0:T(8,128)(2,1)S(1)}, bf16[4,4,128,128]{3,2,1,0:T(8,128)(2,1)S(1)}, f32[4,2,128,128]{3,2,1,0:T(8,128)S(1)}, bf16[4,128,128]{2,1,0:T(8,128)(2,1)S(1)}, bf16[4,128,128]{2,1,0:T(8,128)(2,1)S(1)}) custom-call(s32[2]{0:T(128)S(1)} %pad_add_fusion.place_ref, bf16[4,2,2,4,128,128]{5,4,3,2,1,0:T(8,128)(2,1)S(1)} %arrange.1.qd_ref, ...), custom_call_target="tpu_custom_call" | custom-call | tf_op jit(solution)/shard_map/own/pallas_call | solution.py:29
  67.3 1.7 %collective-permute-start.14 = (bf16[4,128,128]{2,1,0:T(8,128)(2,1)S(1)}, bf16[4,128,128]{2,1,0:T(8,128)(2,1)S(1)}, u32[]{:S(2)}, u32[]{:S(2)}) collective-permute-start(bf16[4,128,128]{2,1,0:T(8,128)(2,1)S(1)} %get-tuple-element.30), channel_id=1, source_target_pairs={{0,1},{1,0},{2,3},{3,2},{4,5},{5,4},{6,7},{7,6},{8,9},{9,8},{10,11... | collective-permute-start | bytes 393224 | tf_op jit(solution)/shard_map/ppermute | solution.py:24
  69.1 1.1 %add_convert_fusion = bf16[4,2,128,128]{3,2,1,0:T(8,128)(2,1)S(1)} fusion(bf16[4,2,128,128]{3,2,1,0:T(8,128)(2,1)} %collective-permute-done.12, f32[4,2,128,128]{3,2,1,0:T(8,128)S(1)} %get-tuple-element.26, bf16[4,2,128,128]{3,2,1,0:T(8,128)(2,1)} %collective-permute-done.11), kind=kLoop, calls=%fused_computation | loop fusion | flops 655360 | bytes 1310720 | tf_op jit(solution)/shard_map/convert_element_type | solution.py:353
  70.3 0.5 collective-permute-start.10
  70.8 1.4 %merge_dv.1 = bf16[128,8,128]{2,1,0:T(8,128)(2,1)} custom-call(s32[2]{0:T(128)S(1)} %pad_add_fusion.place_ref, bf16[4,128,128]{2,1,0:T(8,128)(2,1)S(1)} %get-tuple-element.29.own_ref, bf16[4,128,128]{2,1,0:T(8,128)(2,1)S(1)} %collective-permute-done.14.other_ref), custom_call_target="tpu_custom_call" | custom-call | flops 4000000000 | tf_op jit(solution)/shard_map/merge_dv/pallas_call | solution.py:29
  72.2 1.4 %merge_dk.1 = bf16[128,8,128]{2,1,0:T(8,128)(2,1)} custom-call(s32[2]{0:T(128)S(1)} %pad_add_fusion.place_ref, bf16[4,128,128]{2,1,0:T(8,128)(2,1)S(1)} %get-tuple-element.32.own_ref, bf16[4,128,128]{2,1,0:T(8,128)(2,1)S(1)} %collective-permute-done.13.other_ref), custom_call_target="tpu_custom_call" | custom-call | flops 4000000000 | tf_op jit(solution)/shard_map/merge_dk/pallas_call | solution.py:29
  73.6 3.6 %merge_dq.1 = bf16[128,32,128]{2,1,0:T(8,128)(2,1)} custom-call(s32[2]{0:T(128)S(1)} %pad_add_fusion.place_ref, bf16[16,128,128]{2,1,0:T(8,128)(2,1)S(1)} %bitcast.8, bf16[16,128,128]{2,1,0:T(8,128)(2,1)S(1)} %bitcast.9), custom_call_target="tpu_custom_call" | custom-call | flops 4000000000 | tf_op jit(solution)/shard_map/merge_dq/pallas_call | solution.py:29
  (36 shorter events, 0.8 us)
Async XLA Ops:
  0.6 16.6 %copy-start.4 = (bf16[128,32,128]{2,1,0:T(8,128)(2,1)S(1)}, bf16[128,32,128]{2,1,0:T(8,128)(2,1)}, u32[]{:S(2)}) copy-start(bf16[128,32,128]{2,1,0:T(8,128)(2,1)} %q_ref) | copy-start | bytes 3145732
  0.6 2.1 %collective-permute-start = (bf16[128,8,128]{2,1,0:T(8,128)(2,1)}, bf16[128,8,128]{2,1,0:T(8,128)(2,1)S(1)}, u32[]{:S(2)}, u32[]{:S(2)}) collective-permute-start(bf16[128,8,128]{2,1,0:T(8,128)(2,1)} %own_ref.2), channel_id=1, source_target_pairs={{0,1},{1,0},{2,3},{3,2},{4,5},{5,4},{6,7},{7,6},{8,9},{9,8},{10,11... | collective-permute-start | bytes 786440 | tf_op jit(solution)/shard_map/ppermute | solution.py:24
  1.4 15.8 %copy-start.5 = (bf16[128,32,128]{2,1,0:T(8,128)(2,1)S(1)}, bf16[128,32,128]{2,1,0:T(8,128)(2,1)}, u32[]{:S(2)}) copy-start(bf16[128,32,128]{2,1,0:T(8,128)(2,1)} %do_ref) | copy-start | bytes 3145732
  2.8 0.9 %copy-start.10 = (bf16[128,8,128]{2,1,0:T(8,128)(2,1)S(1)}, bf16[128,8,128]{2,1,0:T(8,128)(2,1)}, u32[]{:S(2)}) copy-start(bf16[128,8,128]{2,1,0:T(8,128)(2,1)} %own_ref.2) | copy-start | bytes 786436
  3.7 23.0 %copy-start.12 = (s32[16]{0:T(128)S(1)}, s32[16]{0:T(128)}, u32[]{:S(2)}) copy-start(s32[16]{0:T(128)} %lengths_ref.1) | copy-start | bytes 196
  4.4 10.8 %collective-permute-start.1 = (bf16[128,32,128]{2,1,0:T(8,128)(2,1)}, bf16[128,32,128]{2,1,0:T(8,128)(2,1)S(1)}, u32[]{:S(2)}, u32[]{:S(2)}) collective-permute-start(bf16[128,32,128]{2,1,0:T(8,128)(2,1)} %q_ref), channel_id=1, source_target_pairs={{0,1},{1,0},{2,3},{3,2},{4,5},{5,4},{6,7},{7,6},{8,9},{9,8},{10,11... | collective-permute-start | bytes 3145736 | tf_op jit(solution)/shard_map/ppermute | solution.py:24
  4.9 12.3 %collective-permute-start.2 = (bf16[128,32,128]{2,1,0:T(8,128)(2,1)}, bf16[128,32,128]{2,1,0:T(8,128)(2,1)S(1)}, u32[]{:S(2)}, u32[]{:S(2)}) collective-permute-start(bf16[128,32,128]{2,1,0:T(8,128)(2,1)} %do_ref), channel_id=1, source_target_pairs={{0,1},{1,0},{2,3},{3,2},{4,5},{5,4},{6,7},{7,6},{8,9},{9,8},{10,11... | collective-permute-start | bytes 3145736 | tf_op jit(solution)/shard_map/ppermute | solution.py:24
  5.0 6.6 %collective-permute-start.5 = (bf16[128,8,128]{2,1,0:T(8,128)(2,1)}, bf16[128,8,128]{2,1,0:T(8,128)(2,1)S(1)}, u32[]{:S(2)}, u32[]{:S(2)}) collective-permute-start(bf16[128,8,128]{2,1,0:T(8,128)(2,1)} %own_ref.3), channel_id=1, source_target_pairs={{0,1},{1,0},{2,3},{3,2},{4,5},{5,4},{6,7},{7,6},{8,9},{9,8},{10,11... | collective-permute-start | bytes 786440 | tf_op jit(solution)/shard_map/ppermute | solution.py:24
  5.4 14.4 %collective-permute-start.3 = (bf16[4,2,128,128]{3,2,1,0:T(8,128)(2,1)S(1)}, bf16[4,2,128,128]{3,2,1,0:T(8,128)(2,1)S(1)}, u32[]{:S(2)}, u32[]{:S(2)}) collective-permute-start(bf16[4,2,128,128]{3,2,1,0:T(8,128)(2,1)S(1)} %pack_k.1.refs_0_), channel_id=1, source_target_pairs={{0,2},{1,3},{2,4},{3,5},{4,6},{5,7},{6,8},{7,9},{8,10},{9,11},{10,... | collective-permute-start | bytes 786440 | tf_op jit(solution)/shard_map/ppermute | solution.py:20
  8.5 18.2 %collective-permute-start.4 = (bf16[4,2,128,128]{3,2,1,0:T(8,128)(2,1)S(1)}, bf16[4,2,128,128]{3,2,1,0:T(8,128)(2,1)S(1)}, u32[]{:S(2)}, u32[]{:S(2)}) collective-permute-start(bf16[4,2,128,128]{3,2,1,0:T(8,128)(2,1)S(1)} %pack_k.1.refs_0_), channel_id=1, source_target_pairs={{0,4},{1,5},{2,6},{3,7},{4,8},{5,9},{6,10},{7,11},{8,12},{9,13},{1... | collective-permute-start | bytes 786440 | tf_op jit(solution)/shard_map/ppermute | solution.py:20
  11.7 1.0 %copy-start.11 = (bf16[128,8,128]{2,1,0:T(8,128)(2,1)S(1)}, bf16[128,8,128]{2,1,0:T(8,128)(2,1)}, u32[]{:S(2)}) copy-start(bf16[128,8,128]{2,1,0:T(8,128)(2,1)} %own_ref.3) | copy-start | bytes 786436
  13.3 26.2 %collective-permute-start.6 = (bf16[4,2,128,128]{3,2,1,0:T(8,128)(2,1)S(1)}, bf16[4,2,128,128]{3,2,1,0:T(8,128)(2,1)S(1)}, u32[]{:S(2)}, u32[]{:S(2)}) collective-permute-start(bf16[4,2,128,128]{3,2,1,0:T(8,128)(2,1)S(1)} %pack_v.1.refs_0_), channel_id=1, source_target_pairs={{0,2},{1,3},{2,4},{3,5},{4,6},{5,7},{6,8},{7,9},{8,10},{9,11},{10,... | collective-permute-start | bytes 786440 | tf_op jit(solution)/shard_map/ppermute | solution.py:20
  15.3 24.2 %collective-permute-start.7 = (bf16[4,2,128,128]{3,2,1,0:T(8,128)(2,1)S(1)}, bf16[4,2,128,128]{3,2,1,0:T(8,128)(2,1)S(1)}, u32[]{:S(2)}, u32[]{:S(2)}) collective-permute-start(bf16[4,2,128,128]{3,2,1,0:T(8,128)(2,1)S(1)} %pack_v.1.refs_0_), channel_id=1, source_target_pairs={{0,4},{1,5},{2,6},{3,7},{4,8},{5,9},{6,10},{7,11},{8,12},{9,13},{1... | collective-permute-start | bytes 786440 | tf_op jit(solution)/shard_map/ppermute | solution.py:20
  19.8 26.4 %copy-start.6 = (bf16[4,2,128,128]{3,2,1,0:T(8,128)(2,1)}, bf16[4,2,128,128]{3,2,1,0:T(8,128)(2,1)S(1)}, u32[]{:S(2)}) copy-start(bf16[4,2,128,128]{3,2,1,0:T(8,128)(2,1)S(1)} %collective-permute-done.3.refs_1_) | copy-start | bytes 786436
  26.7 19.5 %copy-start.8 = (bf16[4,2,128,128]{3,2,1,0:T(8,128)(2,1)}, bf16[4,2,128,128]{3,2,1,0:T(8,128)(2,1)S(1)}, u32[]{:S(2)}) copy-start(bf16[4,2,128,128]{3,2,1,0:T(8,128)(2,1)S(1)} %collective-permute-done.4.refs_2_) | copy-start | bytes 786436
  33.6 23.7 %collective-permute-start.8 = (bf16[4,2,128,128]{3,2,1,0:T(8,128)(2,1)S(1)}, bf16[4,2,128,128]{3,2,1,0:T(8,128)(2,1)S(1)}, u32[]{:S(2)}, u32[]{:S(2)}) collective-permute-start(bf16[4,2,128,128]{3,2,1,0:T(8,128)(2,1)S(1)} %get-tuple-element.22), channel_id=1, source_target_pairs={{4,0},{5,1},{6,2},{7,3},{8,4},{9,5},{10,6},{11,7},{12,8},{13,9},{1... | collective-permute-start | bytes 786440 | tf_op jit(solution)/shard_map/ppermute | solution.py:20
  37.6 19.7 %collective-permute-start.9 = (bf16[4,2,128,128]{3,2,1,0:T(8,128)(2,1)S(1)}, bf16[4,2,128,128]{3,2,1,0:T(8,128)(2,1)S(1)}, u32[]{:S(2)}, u32[]{:S(2)}) collective-permute-start(bf16[4,2,128,128]{3,2,1,0:T(8,128)(2,1)S(1)} %get-tuple-element.23), channel_id=1, source_target_pairs={{2,0},{3,1},{4,2},{5,3},{6,4},{7,5},{8,6},{9,7},{10,8},{11,9},{12,... | collective-permute-start | bytes 786440 | tf_op jit(solution)/shard_map/ppermute | solution.py:20
  46.2 2.3 %copy-start = (bf16[4,2,640,512]{3,2,1,0:T(8,128)(2,1)}, bf16[4,2,640,512]{3,2,1,0:T(8,128)(2,1)S(1)}, u32[]{:S(2)}) copy-start(bf16[4,2,640,512]{3,2,1,0:T(8,128)(2,1)S(1)} %get-tuple-element.20.p_ref) | copy-start | bytes 15728644
  48.5 2.4 %copy-start.2 = (bf16[4,2,640,512]{3,2,1,0:T(8,128)(2,1)}, bf16[4,2,640,512]{3,2,1,0:T(8,128)(2,1)S(1)}, u32[]{:S(2)}) copy-start(bf16[4,2,640,512]{3,2,1,0:T(8,128)(2,1)S(1)} %get-tuple-element.21.ds_ref) | copy-start | bytes 15728644
  50.9 18.2 %collective-permute-start.11 = (bf16[4,2,128,128]{3,2,1,0:T(8,128)(2,1)}, bf16[4,2,128,128]{3,2,1,0:T(8,128)(2,1)}, u32[]{:S(2)}, u32[]{:S(2)}) collective-permute-start(bf16[4,2,128,128]{3,2,1,0:T(8,128)(2,1)} %get-tuple-element.27), channel_id=1, source_target_pairs={{4,0},{5,1},{6,2},{7,3},{8,4},{9,5},{10,6},{11,7},{12,8},{13,9},{1... | collective-permute-start | bytes 786440 | tf_op jit(solution)/shard_map/ppermute | solution.py:20
  52.8 16.3 %collective-permute-start.12 = (bf16[4,2,128,128]{3,2,1,0:T(8,128)(2,1)}, bf16[4,2,128,128]{3,2,1,0:T(8,128)(2,1)}, u32[]{:S(2)}, u32[]{:S(2)}) collective-permute-start(bf16[4,2,128,128]{3,2,1,0:T(8,128)(2,1)} %get-tuple-element.28), channel_id=1, source_target_pairs={{2,0},{3,1},{4,2},{5,3},{6,4},{7,5},{8,6},{9,7},{10,8},{11,9},{12,... | collective-permute-start | bytes 786440 | tf_op jit(solution)/shard_map/ppermute | solution.py:20
  57.3 2.5 %copy-start.1 = (bf16[4,2,640,512]{3,2,1,0:T(8,128)(2,1)S(1)}, bf16[4,2,640,512]{3,2,1,0:T(8,128)(2,1)}, u32[]{:S(2)}) copy-start(bf16[4,2,640,512]{3,2,1,0:T(8,128)(2,1)} %copy-done) | copy-start | bytes 15728644
  59.8 2.5 %copy-start.3 = (bf16[4,2,640,512]{3,2,1,0:T(8,128)(2,1)S(1)}, bf16[4,2,640,512]{3,2,1,0:T(8,128)(2,1)}, u32[]{:S(2)}) copy-start(bf16[4,2,640,512]{3,2,1,0:T(8,128)(2,1)} %copy-done.2) | copy-start | bytes 15728644
  62.3 0.9 %copy-start.7 = (bf16[4,2,128,128]{3,2,1,0:T(8,128)(2,1)S(1)}, bf16[4,2,128,128]{3,2,1,0:T(8,128)(2,1)}, u32[]{:S(2)}) copy-start(bf16[4,2,128,128]{3,2,1,0:T(8,128)(2,1)} %copy-done.6) | copy-start | bytes 786436
  63.2 0.9 %copy-start.9 = (bf16[4,2,128,128]{3,2,1,0:T(8,128)(2,1)S(1)}, bf16[4,2,128,128]{3,2,1,0:T(8,128)(2,1)}, u32[]{:S(2)}) copy-start(bf16[4,2,128,128]{3,2,1,0:T(8,128)(2,1)} %copy-done.8) | copy-start | bytes 786436
  67.3 3.5 %collective-permute-start.14 = (bf16[4,128,128]{2,1,0:T(8,128)(2,1)S(1)}, bf16[4,128,128]{2,1,0:T(8,128)(2,1)S(1)}, u32[]{:S(2)}, u32[]{:S(2)}) collective-permute-start(bf16[4,128,128]{2,1,0:T(8,128)(2,1)S(1)} %get-tuple-element.30), channel_id=1, source_target_pairs={{0,1},{1,0},{2,3},{3,2},{4,5},{5,4},{6,7},{7,6},{8,9},{9,8},{10,11... | collective-permute-start | bytes 393224 | tf_op jit(solution)/shard_map/ppermute | solution.py:24
  70.3 2.0 %collective-permute-start.13 = (bf16[4,128,128]{2,1,0:T(8,128)(2,1)S(1)}, bf16[4,128,128]{2,1,0:T(8,128)(2,1)S(1)}, u32[]{:S(2)}, u32[]{:S(2)}) collective-permute-start(bf16[4,128,128]{2,1,0:T(8,128)(2,1)S(1)} %get-tuple-element.31), channel_id=1, source_target_pairs={{0,1},{1,0},{2,3},{3,2},{4,5},{5,4},{6,7},{7,6},{8,9},{9,8},{10,11... | collective-permute-start | bytes 393224 | tf_op jit(solution)/shard_map/ppermute | solution.py:24
  70.3 3.3 %collective-permute-start.10 = (bf16[4,4,128,128]{3,2,1,0:T(8,128)(2,1)S(1)}, bf16[4,4,128,128]{3,2,1,0:T(8,128)(2,1)S(1)}, u32[]{:S(2)}, u32[]{:S(2)}) collective-permute-start(bf16[4,4,128,128]{3,2,1,0:T(8,128)(2,1)S(1)} %get-tuple-element.25), channel_id=1, source_target_pairs={{0,1},{1,0},{2,3},{3,2},{4,5},{5,4},{6,7},{7,6},{8,9},{9,8},{10,11... | collective-permute-start | bytes 1572872 | tf_op jit(solution)/shard_map/ppermute | solution.py:24

commit v5 on v4

--- a/solution.py
+++ b/solution.py
@@ -66,7 +66,7 @@
         place,
         (queries, grad_out, q_other, do_other),
         [in_spec] * 4,
-        jax.ShapeDtypeStruct(out, BF16),
+        pltpu.VMEM(out, BF16),
         pl.BlockSpec(out[:4] + (rows, dim), lambda i, place: (0, 0, 0, 0, i, 0)),
         [pltpu.VMEM((rows * half, dim), F32)],
         10**9,
@@ -119,6 +119,15 @@
         scr[pl.ds(2 * (halo - back), 2)] = ref[0]
 
 
+def split_tile(tile):
+    tokens, lanes = tile.shape
+    row = lax.broadcasted_iota(jnp.int32, tile.shape, 0)
+    lane = lax.broadcasted_iota(jnp.int32, tile.shape, 1) % tokens
+    diagonal = row <= lane
+    zero = jnp.zeros_like(tile)
+    return jnp.where(diagonal, zero, tile), jnp.where(diagonal, tile, zero)
+
+
 def prob_kernel(halo, place_ref, lengths_ref, qd_ref, *refs):
     k_refs = refs[: halo + 1]
     p_ref = refs[halo + 1]
@@ -137,6 +146,7 @@
 
     window_of(k_refs, k_scr)
     row = lax.broadcasted_iota(jnp.int32, (tokens, pair), 0)
+    diagonal = row <= lane
     for e in range(2):
         first = firsts[e] - row
         k = k_scr[pl.ds(e, count)].reshape(count * tokens, dim)
@@ -144,23 +154,27 @@
         do = qd_ref[0, e, 1].reshape(group * tokens, dim)
         for at in range(0, group * tokens, pair):
             s = lax.dot_general(k, q[at : at + pair], NT, preferred_element_type=F32)
-            tiles = []
-            for j in range(count):
-                allowed = first <= (e + j) * tokens
-                if j == count - 1:
-                    allowed &= row <= lane
-                tiles.append(jnp.where(allowed, s[j * tokens : (j + 1) * tokens], MASKED))
+            tiles = [s[j * tokens : (j + 1) * tokens] for j in range(count)]
+            last = (e + count - 1) * tokens
+            bound = jnp.where(diagonal, last, e * tokens)
+            tiles[0] = jnp.where(first <= bound, jnp.where(diagonal, tiles.pop(), tiles[0]), MASKED)
+            for j in range(1, count - 1):
+                tiles[j] = jnp.where(first <= (e + j) * tokens, tiles[j], MASKED)
             s = jnp.concatenate(tiles, axis=0)
             top = jnp.max(s, axis=0, keepdims=True)
             w = jnp.exp2((s - top) * (dim**-0.5 * LOG2E))
             inv = 1.0 / jnp.sum(w, axis=0, keepdims=True)
             p_ref[0, e, :, at : at + pair] = (w * inv).astype(BF16)
+        far, _ = split_tile(p_ref[0, e, :tokens])
         keep = (2 * halo - e) * tokens
-        dv = jnp.dot(p_ref[0, e, :keep], do, preferred_element_type=F32).reshape(2 * halo - e, tokens, dim)
+        dv = jnp.dot(far, do, preferred_element_type=F32)
+        near = jnp.dot(p_ref[0, e, tokens:keep], do, preferred_element_type=F32)
+        near = near.reshape(2 * halo - e - 1, tokens, dim)
         if e == 0:
-            acc[...] = dv
+            acc[0], acc[1:] = dv, near
         else:
-            acc[1:] += dv
+            acc[1] += dv
+            acc[2:] += near
     for back, ref in zip(range(1, halo + 1), dv_refs):
         ref[0] = acc[pl.ds(2 * (halo - back), 2)].astype(BF16)
 
@@ -174,21 +188,30 @@
     count = 2 * halo + 1
     pair = 2 * tokens
     window_of(v_refs, v_scr)
+    row = lax.broadcasted_iota(jnp.int32, (tokens, pair), 0)
+    diagonal = row <= lax.broadcasted_iota(jnp.int32, (tokens, pair), 1) % tokens
     for e in range(2):
         v = v_scr[pl.ds(e, count)].reshape(count * tokens, dim)
         q = qd_ref[0, e, 0].reshape(group * tokens, dim)
         do = qd_ref[0, e, 1].reshape(group * tokens, dim)
         for at in range(0, group * tokens, pair):
             dp = lax.dot_general(v, do[at : at + pair], NT, preferred_element_type=F32)
+            last = (count - 1) * tokens
+            shared = jnp.where(diagonal, dp[last:], dp[:tokens])
+            dp = jnp.concatenate([shared, dp[tokens:last]], axis=0)
             p = p_ref[0, e, :, at : at + pair].astype(F32)
             delta = jnp.sum(p * dp, axis=0, keepdims=True)
             ds_ref[0, e, :, at : at + pair] = (p * (dp - delta)).astype(BF16)
+        far, _ = split_tile(ds_ref[0, e, :tokens])
         keep = (2 * halo - e) * tokens
-        dk = jnp.dot(ds_ref[0, e, :keep], q, preferred_element_type=F32).reshape(2 * halo - e, tokens, dim)
+        dk = jnp.dot(far, q, preferred_element_type=F32)
+        near = jnp.dot(ds_ref[0, e, tokens:keep], q, preferred_element_type=F32)
+        near = near.reshape(2 * halo - e - 1, tokens, dim)
         if e == 0:
-            acc[...] = dk
+            acc[0], acc[1:] = dk, near
         else:
-            acc[1:] += dk
+            acc[1] += dk
+            acc[2:] += near
     for back, ref in zip(range(1, halo + 1), dk_refs):
         ref[0] = (acc[pl.ds(2 * (halo - back), 2)] * dim**-0.5).astype(BF16)
 
@@ -196,8 +219,9 @@
 def own_kernel(halo, place_ref, qd_ref, p_ref, ds_ref, *refs):
     k_refs, back_refs = refs[: halo + 1], refs[halo + 1 : 2 * halo + 1]
     dq_ref, dq_other_ref, dk_ref, dv_ref, dv_other_ref, k_scr, dq_scr, dv_scr = refs[2 * halo + 1 :]
-    core = place_ref[0]
+    core, head = place_ref[0], pl.program_id(0)
     _, _, _, group, tokens, dim = qd_ref.shape
+    rows = dq_ref.shape[1]
     count = 2 * halo + 1
     scale = dim**-0.5
     window_of(k_refs, k_scr)
@@ -205,24 +229,58 @@
         q = qd_ref[0, e, 0].reshape(group * tokens, dim)
         do = qd_ref[0, e, 1].reshape(group * tokens, dim)
         k = k_scr[pl.ds(e, count)].reshape(count * tokens, dim)
-        dqt = jnp.dot(k.T, ds_ref[0, e], preferred_element_type=F32) * scale
+        far, diagonal = split_tile(ds_ref[0, e, :tokens])
+        ds = jnp.concatenate([far, ds_ref[0, e, tokens:], diagonal], axis=0)
+        dqt = jnp.dot(k.T, ds, preferred_element_type=F32) * scale
         for g in range(group):
-            dq_scr[e, g] = dqt[:, g * tokens : (g + 1) * tokens].T.astype(BF16)
-        keep = (2 * halo - e) * tokens
-        dk = jnp.dot(ds_ref[0, e, keep:], q, preferred_element_type=F32) * scale
-        dv = jnp.dot(p_ref[0, e, keep:], do, preferred_element_type=F32)
-        if e == 0:
-            dk_ref[0, 0], dv_scr[0] = dk, dv
-        else:
-            dk_ref[0, 0] += dk[:tokens]
-            dv_scr[0] += dv[:tokens]
-            dk_ref[0, 1], dv_scr[1] = dk[tokens:], dv[tokens:]
+            dq_scr[e, pl.ds(head * group + g, tokens, stride=rows), :] = dqt[:, g * tokens : (g + 1) * tokens].T
+        _, p_diagonal = split_tile(p_ref[0, e, :tokens])
+        dk = jnp.dot(diagonal, q, preferred_element_type=F32) * scale
+        dv = jnp.dot(p_diagonal, do, preferred_element_type=F32)
+        dk_ref[0, e], dv_scr[e] = dk, dv
+        if e == 1:
+            last = (count - 2) * tokens
+            dk_ref[0, 0] += jnp.dot(ds_ref[0, e, last:], q, preferred_element_type=F32) * scale
+            dv_scr[0] += jnp.dot(p_ref[0, e, last:], do, preferred_element_type=F32)
     for ref in back_refs:
         dv_scr[...] += ref[0].astype(F32)
-    dq_ref[0] = dq_scr[core]
-    dq_other_ref[0] = dq_scr[1 - core]
     dv_ref[0] = dv_scr[core].astype(BF16)
     dv_other_ref[0] = dv_scr[1 - core].astype(BF16)
+
+    @pl.when(head == pl.num_programs(0) - 1)
+    def _():
+        dq_ref[...] = dq_scr[core].astype(BF16).reshape(dq_ref.shape)
+        dq_other_ref[...] = dq_scr[1 - core].astype(BF16).reshape(dq_ref.shape)
+
+
+def join_kernel(place_ref, own_ref, other_ref, out_ref, own_sem, other_sem):
+    core = place_ref[0]
+    half = own_ref.shape[1]
+    own = pltpu.make_async_copy(own_ref, out_ref.at[:, pl.ds(pl.multiple_of(core * half, half), half)], own_sem)
+    other = pltpu.make_async_copy(
+        other_ref, out_ref.at[:, pl.ds(pl.multiple_of((1 - core) * half, half), half)], other_sem
+    )
+    own.start()
+    other.start()
+    own.wait()
+    other.wait()
+
+
+def join(place, own, other):
+    tokens, half, dim = own.shape
+    anywhere = pl.BlockSpec(memory_space=pl.ANY)
+    return call(
+        join_kernel,
+        "join",
+        (1,),
+        place,
+        (own, other),
+        [anywhere] * 2,
+        jax.ShapeDtypeStruct((tokens, 2 * half, dim), BF16),
+        anywhere,
+        [pltpu.SemaphoreType.DMA, pltpu.SemaphoreType.DMA],
+        10**9,
+    )
 
 
 def merge_kernel(place_ref, own_ref, other_ref, out_ref, scr):
@@ -269,10 +327,12 @@
     far_first = range(halo, 0, -1)
     k_own = pack(place, keys, swapped(keys, device_count), "pack_k")
     k_own, queries, grad_out = lax.optimization_barrier((k_own, queries, grad_out))
-    v_own = pack(place, values, swapped(values, device_count), "pack_v")
     qd = arrange(
         place, queries, grad_out, swapped(queries, device_count), swapped(grad_out, device_count), key_heads
     )
+    v_other = swapped(values, device_count)
+    qd, values, v_other = lax.optimization_barrier((qd, values, v_other))
+    v_own = pack(place, values, v_other, "pack_v")
 
     def halo_of(own):
         received = {back: moved(own, device_count, 2 * back) for back in far_first}
@@ -285,14 +345,14 @@
         return pl.BlockSpec((1,) + shape, lambda h, *_: (h,) + (0,) * len(shape))
 
     qd_spec = per_head(2, 2, group, tokens, dim)
-    p_spec = per_head(2, count * tokens, group * tokens)
-    p_shape = jax.ShapeDtypeStruct((half, 2, count * tokens, group * tokens), BF16)
+    p_spec = per_head(2, (count - 1) * tokens, group * tokens)
+    p_shape = pltpu.VMEM((half, 2, (count - 1) * tokens, group * tokens), BF16)
     pair_spec = per_head(2, tokens, dim)
     pair = (half, 2, tokens, dim)
     one_spec = per_head(tokens, dim)
     one_shape = jax.ShapeDtypeStruct((half, tokens, dim), BF16)
-    dq_spec = per_head(group, tokens, dim)
-    dq_shape = jax.ShapeDtypeStruct((half, group, tokens, dim), BF16)
+    dq_shape = jax.ShapeDtypeStruct((tokens, heads // 2, dim), BF16)
+    dq_spec = pl.BlockSpec(dq_shape.shape, lambda h, *_: (0, 0, 0))
     run = pltpu.VMEM((window, tokens, dim), BF16)
     acc = pltpu.VMEM((2 * halo, tokens, dim), F32)
     product = 2 * half * 2 * count * tokens * group * tokens * dim
@@ -336,15 +396,14 @@
         [dq_spec] * 2 + [pair_spec] + [one_spec] * 2,
         [
             run,
-            pltpu.VMEM((2, group, tokens, dim), BF16),
+            pltpu.VMEM((2, tokens * heads // 2, dim), F32),
             pltpu.VMEM((2, tokens, dim), F32),
         ],
         0,
     )
     dq_other = swapped(dq_other, device_count)
     dv_other = swapped(dv_other, device_count)
-    flat = (half * group, tokens, dim)
-    grad_queries = merge(place, dq.reshape(flat), dq_other.reshape(flat), 32, "merge_dq")
+    grad_queries = join(place, dq, dq_other)
     grad_values = merge(place, dv, dv_other, tokens, "merge_dv")
 
     total = dk_own

time: 77.7 us -> 72.9 us (0.938)
  the two profiles are of different devices: /device:TPU:25 before, /device:TPU:23 now
where the time goes in v5:
time: 72.9 us; the launch traced here: 72.3 us
  starting transfers between devices  32.5 us (45%)
  Pallas kernels  27.2 us (37%)
  local copies, waits for them, and re-layouts  7.4 us (10%)
  waiting for transfers between devices  3.06 us (4%)
  other arithmetic  1.21 us (2%)
  between operations  0.91 us (1%)
    ppermute x8, starting transfers between devices, moved(): return lax.ppermute(array, AXES, pairs)  27.7 us
    pallas_call x9, Pallas kernels, call(): pl.pallas_call(kernel, out_shape=outs, grid_spec=pltpu.PrefetchScalarGrid...  27.2 us
    unnamed x26, local copies, waits for them, and re-layouts  7.37 us
    ppermute x7, starting transfers between devices, swapped(): return lax.ppermute(array, AXES, [(d, d ^ 1) for d in range(device_count)])  4.84 us
    ppermute x8, waiting for transfers between devices, moved(): return lax.ppermute(array, AXES, pairs)  1.74 us
  transfers between devices with their start and end apart: 15, of which 3 were waited for; matrix products, arithmetic and copies ran while one was open for 2% of the time, Pallas kernels for 34%

profile of v5, /device:TPU:23, one launch (start us, length us, event | category | flops | bytes accessed | tf_op | source)
XLA Modules:
  0.0 72.3 jit_solution(17306667029584573683)
XLA Ops:
  0.6 0.7 %collective-permute-start = (bf16[128,8,128]{2,1,0:T(8,128)(2,1)}, bf16[128,8,128]{2,1,0:T(8,128)(2,1)S(1)}, u32[]{:S(2)}, u32[]{:S(2)}) collective-permute-start(bf16[128,8,128]{2,1,0:T(8,128)(2,1)} %own_ref.1), channel_id=1, source_target_pairs={{0,1},{1,0},{2,3},{3,2},{4,5},{5,4},{6,7},{7,6},{8,9},{9,8},{10,11... | collective-permute-start | bytes 786440 | tf_op jit(solution)/shard_map/ppermute | solution.py:24
  1.5 1.3 %collective-permute-done.other_ref = bf16[128,8,128]{2,1,0:T(8,128)(2,1)S(1)} collective-permute-done((bf16[128,8,128]{2,1,0:T(8,128)(2,1)}, bf16[128,8,128]{2,1,0:T(8,128)(2,1)S(1)}, u32[]{:S(2)}, u32[]{:S(2)}) %collective-permute-start) | collective-permute-done | bytes 262176 | tf_op jit(solution)/shard_map/ppermute | solution.py:24
  2.8 0.9 %copy-done.10 = bf16[128,8,128]{2,1,0:T(8,128)(2,1)S(1)} copy-done((bf16[128,8,128]{2,1,0:T(8,128)(2,1)S(1)}, bf16[128,8,128]{2,1,0:T(8,128)(2,1)}, u32[]{:S(2)}) %copy-start.10) | copy-done | bytes 262168
  3.7 0.7 pack_k.1.refs_0_
  4.4 0.4 collective-permute-start.1
  4.9 0.1 collective-permute-start.2
  5.0 0.4 collective-permute-start.3
  5.4 3.1 %collective-permute-start.4 = (bf16[4,2,128,128]{3,2,1,0:T(8,128)(2,1)S(1)}, bf16[4,2,128,128]{3,2,1,0:T(8,128)(2,1)S(1)}, u32[]{:S(2)}, u32[]{:S(2)}) collective-permute-start(bf16[4,2,128,128]{3,2,1,0:T(8,128)(2,1)S(1)} %pack_k.1.refs_0_), channel_id=1, source_target_pairs={{0,2},{1,3},{2,4},{3,5},{4,6},{5,7},{6,8},{7,9},{8,10},{9,11},{10,... | collective-permute-start | bytes 786440 | tf_op jit(solution)/shard_map/ppermute | solution.py:20
  8.5 3.1 %collective-permute-start.5 = (bf16[4,2,128,128]{3,2,1,0:T(8,128)(2,1)S(1)}, bf16[4,2,128,128]{3,2,1,0:T(8,128)(2,1)S(1)}, u32[]{:S(2)}, u32[]{:S(2)}) collective-permute-start(bf16[4,2,128,128]{3,2,1,0:T(8,128)(2,1)S(1)} %pack_k.1.refs_0_), channel_id=1, source_target_pairs={{0,4},{1,5},{2,6},{3,7},{4,8},{5,9},{6,10},{7,11},{8,12},{9,13},{1... | collective-permute-start | bytes 786440 | tf_op jit(solution)/shard_map/ppermute | solution.py:20
  11.7 2.5 %arrange.1.qd_ref = bf16[4,2,2,4,128,128]{5,4,3,2,1,0:T(8,128)(2,1)S(1)} custom-call(s32[2]{0:T(128)S(1)} %pad_add_fusion.place_ref, bf16[128,32,128]{2,1,0:T(8,128)(2,1)S(1)} %copy-done.4, bf16[128,32,128]{2,1,0:T(8,128)(2,1)S(1)} %copy-done.5, bf16[128,32,128]{2,1,0:T(8,128)(2,1)S(1)} %collective-permute-done.1.q_other_ref, ...), custom_call_target="tpu_custom_call" | custom-call | flops 1000000000 | tf_op jit(solution)/shard_map/arrange/pallas_call | solution.py:29
  14.2 0.7 pack_v.1.refs_0_
  15.0 3.1 %collective-permute-start.6 = (bf16[4,2,128,128]{3,2,1,0:T(8,128)(2,1)S(1)}, bf16[4,2,128,128]{3,2,1,0:T(8,128)(2,1)S(1)}, u32[]{:S(2)}, u32[]{:S(2)}) collective-permute-start(bf16[4,2,128,128]{3,2,1,0:T(8,128)(2,1)S(1)} %pack_v.1.refs_0_), channel_id=1, source_target_pairs={{0,2},{1,3},{2,4},{3,5},{4,6},{5,7},{6,8},{7,9},{8,10},{9,11},{10,... | collective-permute-start | bytes 786440 | tf_op jit(solution)/shard_map/ppermute | solution.py:20
  18.1 1.9 %collective-permute-start.7 = (bf16[4,2,128,128]{3,2,1,0:T(8,128)(2,1)S(1)}, bf16[4,2,128,128]{3,2,1,0:T(8,128)(2,1)S(1)}, u32[]{:S(2)}, u32[]{:S(2)}) collective-permute-start(bf16[4,2,128,128]{3,2,1,0:T(8,128)(2,1)S(1)} %pack_v.1.refs_0_), channel_id=1, source_target_pairs={{0,4},{1,5},{2,6},{3,7},{4,8},{5,9},{6,10},{7,11},{8,12},{9,13},{1... | collective-permute-start | bytes 786440 | tf_op jit(solution)/shard_map/ppermute | solution.py:20
  20.0 0.4 collective-permute-done.5.refs_2_
  20.5 7.7 %prob.1 = (bf16[4,2,512,512]{3,2,1,0:T(8,128)(2,1)S(1)}, bf16[4,2,128,128]{3,2,1,0:T(8,128)(2,1)}, bf16[4,2,128,128]{3,2,1,0:T(8,128)(2,1)}) custom-call(s32[2]{0:T(128)S(1)} %pad_add_fusion.place_ref, s32[16]{0:T(128)S(1)} %copy-done.12, bf16[4,2,2,4,128,128]{5,4,3,2,1,0:T(8,128)(2,1)S(1)} %arrange.1.qd_ref, bf16[4,2,128,128]{3,2,1,0:T(8,128)(2,1)S(1)} %pack_k.1.refs_0_, ...), custom_call_target="tpu_custom_call" | custom-call | flops 2684354560 | tf_op jit(solution)/shard_map/prob/pallas_call | solution.py:29
  28.2 4.0 %collective-permute-start.8 = (bf16[4,2,128,128]{3,2,1,0:T(8,128)(2,1)}, bf16[4,2,128,128]{3,2,1,0:T(8,128)(2,1)S(1)}, u32[]{:S(2)}, u32[]{:S(2)}) collective-permute-start(bf16[4,2,128,128]{3,2,1,0:T(8,128)(2,1)} %get-tuple-element.28), channel_id=1, source_target_pairs={{4,0},{5,1},{6,2},{7,3},{8,4},{9,5},{10,6},{11,7},{12,8},{13,9},{1... | collective-permute-start | bytes 786440 | tf_op jit(solution)/shard_map/ppermute | solution.py:20
  32.2 7.3 %collective-permute-start.9 = (bf16[4,2,128,128]{3,2,1,0:T(8,128)(2,1)}, bf16[4,2,128,128]{3,2,1,0:T(8,128)(2,1)S(1)}, u32[]{:S(2)}, u32[]{:S(2)}) collective-permute-start(bf16[4,2,128,128]{3,2,1,0:T(8,128)(2,1)} %get-tuple-element.29), channel_id=1, source_target_pairs={{2,0},{3,1},{4,2},{5,3},{6,4},{7,5},{8,6},{9,7},{10,8},{11,9},{12,... | collective-permute-start | bytes 786440 | tf_op jit(solution)/shard_map/ppermute | solution.py:20
  39.5 7.8 %dscore.1 = (bf16[4,2,512,512]{3,2,1,0:T(8,128)(2,1)S(1)}, bf16[4,2,128,128]{3,2,1,0:T(8,128)(2,1)}, bf16[4,2,128,128]{3,2,1,0:T(8,128)(2,1)}) custom-call(s32[2]{0:T(128)S(1)} %pad_add_fusion.place_ref, bf16[4,2,2,4,128,128]{5,4,3,2,1,0:T(8,128)(2,1)S(1)} %arrange.1.qd_ref, bf16[4,2,512,512]{3,2,1,0:T(8,128)(2,1)S(1)} %get-tuple-element.24.p_ref, ...), custom_call_target="tpu_custom_call" | custom-call | flops 2684354560 | tf_op jit(solution)/shard_map/dscore/pallas_call | solution.py:29
  47.3 2.0 %copy-done.2 = bf16[4,2,512,512]{3,2,1,0:T(8,128)(2,1)} copy-done((bf16[4,2,512,512]{3,2,1,0:T(8,128)(2,1)}, bf16[4,2,512,512]{3,2,1,0:T(8,128)(2,1)S(1)}, u32[]{:S(2)}) %copy-start.2) | copy-done | bytes 4194328
  49.3 3.2 %collective-permute-start.11 = (bf16[4,2,128,128]{3,2,1,0:T(8,128)(2,1)}, bf16[4,2,128,128]{3,2,1,0:T(8,128)(2,1)}, u32[]{:S(2)}, u32[]{:S(2)}) collective-permute-start(bf16[4,2,128,128]{3,2,1,0:T(8,128)(2,1)} %get-tuple-element.33), channel_id=1, source_target_pairs={{4,0},{5,1},{6,2},{7,3},{8,4},{9,5},{10,6},{11,7},{12,8},{13,9},{1... | collective-permute-start | bytes 786440 | tf_op jit(solution)/shard_map/ppermute | solution.py:20
  52.5 1.9 %collective-permute-start.12 = (bf16[4,2,128,128]{3,2,1,0:T(8,128)(2,1)}, bf16[4,2,128,128]{3,2,1,0:T(8,128)(2,1)}, u32[]{:S(2)}, u32[]{:S(2)}) collective-permute-start(bf16[4,2,128,128]{3,2,1,0:T(8,128)(2,1)} %get-tuple-element.34), channel_id=1, source_target_pairs={{2,0},{3,1},{4,2},{5,3},{6,4},{7,5},{8,6},{9,7},{10,8},{11,9},{12,... | collective-permute-start | bytes 786440 | tf_op jit(solution)/shard_map/ppermute | solution.py:20
  54.5 2.2 %copy-done.1 = bf16[4,2,512,512]{3,2,1,0:T(8,128)(2,1)S(1)} copy-done((bf16[4,2,512,512]{3,2,1,0:T(8,128)(2,1)S(1)}, bf16[4,2,512,512]{3,2,1,0:T(8,128)(2,1)}, u32[]{:S(2)}) %copy-start.1) | copy-done | bytes 4194328
  56.7 2.2 %copy-done.3 = bf16[4,2,512,512]{3,2,1,0:T(8,128)(2,1)S(1)} copy-done((bf16[4,2,512,512]{3,2,1,0:T(8,128)(2,1)S(1)}, bf16[4,2,512,512]{3,2,1,0:T(8,128)(2,1)}, u32[]{:S(2)}) %copy-start.3) | copy-done | bytes 4194328
  58.9 3.4 %own.1 = (bf16[128,16,128]{2,1,0:T(8,128)(2,1)S(1)}, bf16[128,16,128]{2,1,0:T(8,128)(2,1)S(1)}, f32[4,2,128,128]{3,2,1,0:T(8,128)S(1)}, bf16[4,128,128]{2,1,0:T(8,128)(2,1)S(1)}, bf16[4,128,128]{2,1,0:T(8,128)(2,1)S(1)}) custom-call(s32[2]{0:T(128)S(1)} %pad_add_fusion.place_ref, bf16[4,2,2,4,128,128]{5,4,3,2,1,0:T(8,128)(2,1)S(1)} %arrange.1.qd_ref, ...), custom_call_target="tpu_custom_call" | custom-call | tf_op jit(solution)/shard_map/own/pallas_call | solution.py:29
  62.3 1.5 %collective-permute-start.14 = (bf16[4,128,128]{2,1,0:T(8,128)(2,1)S(1)}, bf16[4,128,128]{2,1,0:T(8,128)(2,1)S(1)}, u32[]{:S(2)}, u32[]{:S(2)}) collective-permute-start(bf16[4,128,128]{2,1,0:T(8,128)(2,1)S(1)} %get-tuple-element.36), channel_id=1, source_target_pairs={{0,1},{1,0},{2,3},{3,2},{4,5},{5,4},{6,7},{7,6},{8,9},{9,8},{10,11... | collective-permute-start | bytes 393224 | tf_op jit(solution)/shard_map/ppermute | solution.py:24
  63.8 0.1 collective-permute-start.10
  63.9 1.3 %collective-permute-done.12 = bf16[4,2,128,128]{3,2,1,0:T(8,128)(2,1)} collective-permute-done((bf16[4,2,128,128]{3,2,1,0:T(8,128)(2,1)}, bf16[4,2,128,128]{3,2,1,0:T(8,128)(2,1)}, u32[]{:S(2)}, u32[]{:S(2)}) %collective-permute-start.12) | collective-permute-done | bytes 262176 | tf_op jit(solution)/shard_map/ppermute | solution.py:20
  65.2 1.1 %add_convert_fusion = bf16[4,2,128,128]{3,2,1,0:T(8,128)(2,1)S(1)} fusion(bf16[4,2,128,128]{3,2,1,0:T(8,128)(2,1)} %collective-permute-done.12, f32[4,2,128,128]{3,2,1,0:T(8,128)S(1)} %get-tuple-element.32, bf16[4,2,128,128]{3,2,1,0:T(8,128)(2,1)} %collective-permute-done.11), kind=kLoop, calls=%fused_computation | loop fusion | flops 655360 | bytes 1310720 | tf_op jit(solution)/shard_map/convert_element_type | solution.py:412
  66.4 1.6 %collective-permute-start.13 = (bf16[4,128,128]{2,1,0:T(8,128)(2,1)S(1)}, bf16[4,128,128]{2,1,0:T(8,128)(2,1)S(1)}, u32[]{:S(2)}, u32[]{:S(2)}) collective-permute-start(bf16[4,128,128]{2,1,0:T(8,128)(2,1)S(1)} %get-tuple-element.37), channel_id=1, source_target_pairs={{0,1},{1,0},{2,3},{3,2},{4,5},{5,4},{6,7},{7,6},{8,9},{9,8},{10,11... | collective-permute-start | bytes 393224 | tf_op jit(solution)/shard_map/ppermute | solution.py:24
  68.0 1.4 %merge_dv.1 = bf16[128,8,128]{2,1,0:T(8,128)(2,1)} custom-call(s32[2]{0:T(128)S(1)} %pad_add_fusion.place_ref, bf16[4,128,128]{2,1,0:T(8,128)(2,1)S(1)} %get-tuple-element.35.own_ref, bf16[4,128,128]{2,1,0:T(8,128)(2,1)S(1)} %collective-permute-done.14.other_ref), custom_call_target="tpu_custom_call" | custom-call | flops 4000000000 | tf_op jit(solution)/shard_map/merge_dv/pallas_call | solution.py:29
  69.4 1.4 %merge_dk.1 = bf16[128,8,128]{2,1,0:T(8,128)(2,1)} custom-call(s32[2]{0:T(128)S(1)} %pad_add_fusion.place_ref, bf16[4,128,128]{2,1,0:T(8,128)(2,1)S(1)} %get-tuple-element.38.own_ref, bf16[4,128,128]{2,1,0:T(8,128)(2,1)S(1)} %collective-permute-done.13.other_ref), custom_call_target="tpu_custom_call" | custom-call | flops 4000000000 | tf_op jit(solution)/shard_map/merge_dk/pallas_call | solution.py:29
  70.8 1.5 %join.1 = bf16[128,32,128]{2,1,0:T(8,128)(2,1)} custom-call(s32[2]{0:T(128)S(1)} %pad_add_fusion.place_ref, bf16[128,16,128]{2,1,0:T(8,128)(2,1)S(1)} %get-tuple-element.30.own_ref, bf16[128,16,128]{2,1,0:T(8,128)(2,1)S(1)} %collective-permute-done.10.other_ref), custom_call_target="tpu_custom_call" | custom-call | flops 1000000000 | tf_op jit(solution)/shard_map/join/pallas_call | solution.py:29
  (36 shorter events, 0.2 us)
Async XLA Ops:
  0.6 11.1 %copy-start.4 = (bf16[128,32,128]{2,1,0:T(8,128)(2,1)S(1)}, bf16[128,32,128]{2,1,0:T(8,128)(2,1)}, u32[]{:S(2)}) copy-start(bf16[128,32,128]{2,1,0:T(8,128)(2,1)} %q_ref) | copy-start | bytes 3145732
  0.6 2.1 %collective-permute-start = (bf16[128,8,128]{2,1,0:T(8,128)(2,1)}, bf16[128,8,128]{2,1,0:T(8,128)(2,1)S(1)}, u32[]{:S(2)}, u32[]{:S(2)}) collective-permute-start(bf16[128,8,128]{2,1,0:T(8,128)(2,1)} %own_ref.1), channel_id=1, source_target_pairs={{0,1},{1,0},{2,3},{3,2},{4,5},{5,4},{6,7},{7,6},{8,9},{9,8},{10,11... | collective-permute-start | bytes 786440 | tf_op jit(solution)/shard_map/ppermute | solution.py:24
  1.4 10.3 %copy-start.5 = (bf16[128,32,128]{2,1,0:T(8,128)(2,1)S(1)}, bf16[128,32,128]{2,1,0:T(8,128)(2,1)}, u32[]{:S(2)}) copy-start(bf16[128,32,128]{2,1,0:T(8,128)(2,1)} %do_ref) | copy-start | bytes 3145732
  2.8 0.9 %copy-start.10 = (bf16[128,8,128]{2,1,0:T(8,128)(2,1)S(1)}, bf16[128,8,128]{2,1,0:T(8,128)(2,1)}, u32[]{:S(2)}) copy-start(bf16[128,8,128]{2,1,0:T(8,128)(2,1)} %own_ref.1) | copy-start | bytes 786436
  3.7 10.5 %copy-start.11 = (bf16[128,8,128]{2,1,0:T(8,128)(2,1)S(1)}, bf16[128,8,128]{2,1,0:T(8,128)(2,1)}, u32[]{:S(2)}) copy-start(bf16[128,8,128]{2,1,0:T(8,128)(2,1)} %own_ref.2) | copy-start | bytes 786436
  4.4 16.1 %copy-start.12 = (s32[16]{0:T(128)S(1)}, s32[16]{0:T(128)}, u32[]{:S(2)}) copy-start(s32[16]{0:T(128)} %lengths_ref.1) | copy-start | bytes 196
  4.4 7.2 %collective-permute-start.1 = (bf16[128,32,128]{2,1,0:T(8,128)(2,1)}, bf16[128,32,128]{2,1,0:T(8,128)(2,1)S(1)}, u32[]{:S(2)}, u32[]{:S(2)}) collective-permute-start(bf16[128,32,128]{2,1,0:T(8,128)(2,1)} %q_ref), channel_id=1, source_target_pairs={{0,1},{1,0},{2,3},{3,2},{4,5},{5,4},{6,7},{7,6},{8,9},{9,8},{10,11... | collective-permute-start | bytes 3145736 | tf_op jit(solution)/shard_map/ppermute | solution.py:24
  4.9 6.8 %collective-permute-start.2 = (bf16[128,32,128]{2,1,0:T(8,128)(2,1)}, bf16[128,32,128]{2,1,0:T(8,128)(2,1)S(1)}, u32[]{:S(2)}, u32[]{:S(2)}) collective-permute-start(bf16[128,32,128]{2,1,0:T(8,128)(2,1)} %do_ref), channel_id=1, source_target_pairs={{0,1},{1,0},{2,3},{3,2},{4,5},{5,4},{6,7},{7,6},{8,9},{9,8},{10,11... | collective-permute-start | bytes 3145736 | tf_op jit(solution)/shard_map/ppermute | solution.py:24
  5.0 9.2 %collective-permute-start.3 = (bf16[128,8,128]{2,1,0:T(8,128)(2,1)}, bf16[128,8,128]{2,1,0:T(8,128)(2,1)S(1)}, u32[]{:S(2)}, u32[]{:S(2)}) collective-permute-start(bf16[128,8,128]{2,1,0:T(8,128)(2,1)} %own_ref.2), channel_id=1, source_target_pairs={{0,1},{1,0},{2,3},{3,2},{4,5},{5,4},{6,7},{7,6},{8,9},{9,8},{10,11... | collective-permute-start | bytes 786440 | tf_op jit(solution)/shard_map/ppermute | solution.py:24
  5.4 14.6 %collective-permute-start.4 = (bf16[4,2,128,128]{3,2,1,0:T(8,128)(2,1)S(1)}, bf16[4,2,128,128]{3,2,1,0:T(8,128)(2,1)S(1)}, u32[]{:S(2)}, u32[]{:S(2)}) collective-permute-start(bf16[4,2,128,128]{3,2,1,0:T(8,128)(2,1)S(1)} %pack_k.1.refs_0_), channel_id=1, source_target_pairs={{0,2},{1,3},{2,4},{3,5},{4,6},{5,7},{6,8},{7,9},{8,10},{9,11},{10,... | collective-permute-start | bytes 786440 | tf_op jit(solution)/shard_map/ppermute | solution.py:20
  8.5 12.0 %collective-permute-start.5 = (bf16[4,2,128,128]{3,2,1,0:T(8,128)(2,1)S(1)}, bf16[4,2,128,128]{3,2,1,0:T(8,128)(2,1)S(1)}, u32[]{:S(2)}, u32[]{:S(2)}) collective-permute-start(bf16[4,2,128,128]{3,2,1,0:T(8,128)(2,1)S(1)} %pack_k.1.refs_0_), channel_id=1, source_target_pairs={{0,4},{1,5},{2,6},{3,7},{4,8},{5,9},{6,10},{7,11},{8,12},{9,13},{1... | collective-permute-start | bytes 786440 | tf_op jit(solution)/shard_map/ppermute | solution.py:20
  15.0 24.5 %collective-permute-start.6 = (bf16[4,2,128,128]{3,2,1,0:T(8,128)(2,1)S(1)}, bf16[4,2,128,128]{3,2,1,0:T(8,128)(2,1)S(1)}, u32[]{:S(2)}, u32[]{:S(2)}) collective-permute-start(bf16[4,2,128,128]{3,2,1,0:T(8,128)(2,1)S(1)} %pack_v.1.refs_0_), channel_id=1, source_target_pairs={{0,2},{1,3},{2,4},{3,5},{4,6},{5,7},{6,8},{7,9},{8,10},{9,11},{10,... | collective-permute-start | bytes 786440 | tf_op jit(solution)/shard_map/ppermute | solution.py:20
  18.1 21.4 %collective-permute-start.7 = (bf16[4,2,128,128]{3,2,1,0:T(8,128)(2,1)S(1)}, bf16[4,2,128,128]{3,2,1,0:T(8,128)(2,1)S(1)}, u32[]{:S(2)}, u32[]{:S(2)}) collective-permute-start(bf16[4,2,128,128]{3,2,1,0:T(8,128)(2,1)S(1)} %pack_v.1.refs_0_), channel_id=1, source_target_pairs={{0,4},{1,5},{2,6},{3,7},{4,8},{5,9},{6,10},{7,11},{8,12},{9,13},{1... | collective-permute-start | bytes 786440 | tf_op jit(solution)/shard_map/ppermute | solution.py:20
  20.0 8.2 %copy-start.6 = (bf16[4,2,128,128]{3,2,1,0:T(8,128)(2,1)}, bf16[4,2,128,128]{3,2,1,0:T(8,128)(2,1)S(1)}, u32[]{:S(2)}) copy-start(bf16[4,2,128,128]{3,2,1,0:T(8,128)(2,1)S(1)} %collective-permute-done.4.refs_1_) | copy-start | bytes 786436
  20.5 7.7 %copy-start.8 = (bf16[4,2,128,128]{3,2,1,0:T(8,128)(2,1)}, bf16[4,2,128,128]{3,2,1,0:T(8,128)(2,1)S(1)}, u32[]{:S(2)}) copy-start(bf16[4,2,128,128]{3,2,1,0:T(8,128)(2,1)S(1)} %collective-permute-done.5.refs_2_) | copy-start | bytes 786436
  28.2 19.1 %copy-start = (bf16[4,2,512,512]{3,2,1,0:T(8,128)(2,1)}, bf16[4,2,512,512]{3,2,1,0:T(8,128)(2,1)S(1)}, u32[]{:S(2)}) copy-start(bf16[4,2,512,512]{3,2,1,0:T(8,128)(2,1)S(1)} %get-tuple-element.24.p_ref) | copy-start | bytes 12582916
  28.2 26.3 %collective-permute-start.8 = (bf16[4,2,128,128]{3,2,1,0:T(8,128)(2,1)}, bf16[4,2,128,128]{3,2,1,0:T(8,128)(2,1)S(1)}, u32[]{:S(2)}, u32[]{:S(2)}) collective-permute-start(bf16[4,2,128,128]{3,2,1,0:T(8,128)(2,1)} %get-tuple-element.28), channel_id=1, source_target_pairs={{4,0},{5,1},{6,2},{7,3},{8,4},{9,5},{10,6},{11,7},{12,8},{13,9},{1... | collective-permute-start | bytes 786440 | tf_op jit(solution)/shard_map/ppermute | solution.py:20
  32.2 22.3 %collective-permute-start.9 = (bf16[4,2,128,128]{3,2,1,0:T(8,128)(2,1)}, bf16[4,2,128,128]{3,2,1,0:T(8,128)(2,1)S(1)}, u32[]{:S(2)}, u32[]{:S(2)}) collective-permute-start(bf16[4,2,128,128]{3,2,1,0:T(8,128)(2,1)} %get-tuple-element.29), channel_id=1, source_target_pairs={{2,0},{3,1},{4,2},{5,3},{6,4},{7,5},{8,6},{9,7},{10,8},{11,9},{12,... | collective-permute-start | bytes 786440 | tf_op jit(solution)/shard_map/ppermute | solution.py:20
  39.5 15.0 %copy-start.7 = (bf16[4,2,128,128]{3,2,1,0:T(8,128)(2,1)S(1)}, bf16[4,2,128,128]{3,2,1,0:T(8,128)(2,1)}, u32[]{:S(2)}) copy-start(bf16[4,2,128,128]{3,2,1,0:T(8,128)(2,1)} %copy-done.6) | copy-start | bytes 786436
  39.5 15.0 %copy-start.9 = (bf16[4,2,128,128]{3,2,1,0:T(8,128)(2,1)S(1)}, bf16[4,2,128,128]{3,2,1,0:T(8,128)(2,1)}, u32[]{:S(2)}) copy-start(bf16[4,2,128,128]{3,2,1,0:T(8,128)(2,1)} %copy-done.8) | copy-start | bytes 786436
  47.3 2.0 %copy-start.2 = (bf16[4,2,512,512]{3,2,1,0:T(8,128)(2,1)}, bf16[4,2,512,512]{3,2,1,0:T(8,128)(2,1)S(1)}, u32[]{:S(2)}) copy-start(bf16[4,2,512,512]{3,2,1,0:T(8,128)(2,1)S(1)} %get-tuple-element.27.ds_ref) | copy-start | bytes 12582916
  49.3 14.6 %collective-permute-start.11 = (bf16[4,2,128,128]{3,2,1,0:T(8,128)(2,1)}, bf16[4,2,128,128]{3,2,1,0:T(8,128)(2,1)}, u32[]{:S(2)}, u32[]{:S(2)}) collective-permute-start(bf16[4,2,128,128]{3,2,1,0:T(8,128)(2,1)} %get-tuple-element.33), channel_id=1, source_target_pairs={{4,0},{5,1},{6,2},{7,3},{8,4},{9,5},{10,6},{11,7},{12,8},{13,9},{1... | collective-permute-start | bytes 786440 | tf_op jit(solution)/shard_map/ppermute | solution.py:20
  52.5 12.7 %collective-permute-start.12 = (bf16[4,2,128,128]{3,2,1,0:T(8,128)(2,1)}, bf16[4,2,128,128]{3,2,1,0:T(8,128)(2,1)}, u32[]{:S(2)}, u32[]{:S(2)}) collective-permute-start(bf16[4,2,128,128]{3,2,1,0:T(8,128)(2,1)} %get-tuple-element.34), channel_id=1, source_target_pairs={{2,0},{3,1},{4,2},{5,3},{6,4},{7,5},{8,6},{9,7},{10,8},{11,9},{12,... | collective-permute-start | bytes 786440 | tf_op jit(solution)/shard_map/ppermute | solution.py:20
  54.5 2.2 %copy-start.1 = (bf16[4,2,512,512]{3,2,1,0:T(8,128)(2,1)S(1)}, bf16[4,2,512,512]{3,2,1,0:T(8,128)(2,1)}, u32[]{:S(2)}) copy-start(bf16[4,2,512,512]{3,2,1,0:T(8,128)(2,1)} %copy-done) | copy-start | bytes 12582916
  56.7 2.2 %copy-start.3 = (bf16[4,2,512,512]{3,2,1,0:T(8,128)(2,1)S(1)}, bf16[4,2,512,512]{3,2,1,0:T(8,128)(2,1)}, u32[]{:S(2)}) copy-start(bf16[4,2,512,512]{3,2,1,0:T(8,128)(2,1)} %copy-done.2) | copy-start | bytes 12582916
  62.3 5.6 %collective-permute-start.14 = (bf16[4,128,128]{2,1,0:T(8,128)(2,1)S(1)}, bf16[4,128,128]{2,1,0:T(8,128)(2,1)S(1)}, u32[]{:S(2)}, u32[]{:S(2)}) collective-permute-start(bf16[4,128,128]{2,1,0:T(8,128)(2,1)S(1)} %get-tuple-element.36), channel_id=1, source_target_pairs={{0,1},{1,0},{2,3},{3,2},{4,5},{5,4},{6,7},{7,6},{8,9},{9,8},{10,11... | collective-permute-start | bytes 393224 | tf_op jit(solution)/shard_map/ppermute | solution.py:24
  63.8 6.9 %collective-permute-start.10 = (bf16[128,16,128]{2,1,0:T(8,128)(2,1)S(1)}, bf16[128,16,128]{2,1,0:T(8,128)(2,1)S(1)}, u32[]{:S(2)}, u32[]{:S(2)}) collective-permute-start(bf16[128,16,128]{2,1,0:T(8,128)(2,1)S(1)} %get-tuple-element.31), channel_id=1, source_target_pairs={{0,1},{1,0},{2,3},{3,2},{4,5},{5,4},{6,7},{7,6},{8,9},{9,8},{10,11... | collective-permute-start | bytes 1572872 | tf_op jit(solution)/shard_map/ppermute | solution.py:24
  66.4 3.0 %collective-permute-start.13 = (bf16[4,128,128]{2,1,0:T(8,128)(2,1)S(1)}, bf16[4,128,128]{2,1,0:T(8,128)(2,1)S(1)}, u32[]{:S(2)}, u32[]{:S(2)}) collective-permute-start(bf16[4,128,128]{2,1,0:T(8,128)(2,1)S(1)} %get-tuple-element.37), channel_id=1, source_target_pairs={{0,1},{1,0},{2,3},{3,2},{4,5},{5,4},{6,7},{7,6},{8,9},{9,8},{10,11... | collective-permute-start | bytes 393224 | tf_op jit(solution)/shard_map/ppermute | solution.py:24

commit v6 on v4

--- a/solution.py
+++ b/solution.py
@@ -12,7 +12,7 @@
 MASKED = -1e30
 BF16, F32 = jnp.bfloat16, jnp.float32
 NT = (((1,), (1,)), ((), ()))
-VMEM_BYTES = 24 * 2**20
+VMEM_BYTES = 16 * 2**20
 
 
 def moved(array, device_count, by):
@@ -22,6 +22,10 @@
 
 def swapped(array, device_count):
     return lax.ppermute(array, AXES, [(d, d ^ 1) for d in range(device_count)])
+
+
+def in_vmem(array):
+    return pltpu.with_memory_space_constraint(array, pltpu.VMEM)
 
 
 def call(kernel, name, grid, place, inputs, in_specs, outs, out_specs, scratch, flops):
@@ -66,19 +70,23 @@
         place,
         (queries, grad_out, q_other, do_other),
         [in_spec] * 4,
-        jax.ShapeDtypeStruct(out, BF16),
+        pltpu.VMEM(out, BF16),
         pl.BlockSpec(out[:4] + (rows, dim), lambda i, place: (0, 0, 0, 0, i, 0)),
         [pltpu.VMEM((rows * half, dim), F32)],
         10**9,
     )
 
 
-def pack_kernel(place_ref, own_ref, other_ref, out_ref, scr):
+def pack_kernel(place_ref, own_ref, other_ref, out_ref, own_scr, scr, sem):
     core = place_ref[0]
-    tokens, heads, dim = own_ref.shape
+    tokens, heads, dim = other_ref.shape
     half = heads // 2
-    for which, ref in enumerate([own_ref, other_ref]):
-        block = 1 - core if which else core
+    fetch = pltpu.make_async_copy(own_ref, own_scr, sem)
+    fetch.start()
+    for which, ref in enumerate([other_ref, own_scr]):
+        if which:
+            fetch.wait()
+        block = core if which else 1 - core
         scr[...] = ref[...].astype(F32).reshape(tokens * heads, dim)
         for h in range(half):
             out_ref[h, block] = scr[pl.ds(core * half + h, tokens, stride=heads), :].astype(BF16)
@@ -86,18 +94,21 @@
 
 def pack(place, own, other, name):
     tokens, heads, dim = own.shape
-    spec = pl.BlockSpec(own.shape, lambda i, place: (0, 0, 0))
     out = (heads // 2, 2, tokens, dim)
     return call(
         pack_kernel,
         name,
         (1,),
         place,
-        (own, other),
-        [spec] * 2,
+        (pltpu.with_memory_space_constraint(own, pltpu.HBM), other),
+        [pl.BlockSpec(memory_space=pltpu.HBM), pl.BlockSpec(own.shape, lambda i, place: (0, 0, 0))],
         jax.ShapeDtypeStruct(out, BF16),
         pl.BlockSpec(out, lambda i, place: (0, 0, 0, 0)),
-        [pltpu.VMEM((tokens * heads, dim), F32)],
+        [
+            pltpu.VMEM(own.shape, BF16),
+            pltpu.VMEM((tokens * heads, dim), F32),
+            pltpu.SemaphoreType.DMA,
+        ],
         10**9,
     )
 
@@ -117,6 +128,21 @@
     halo = len(pair_refs) - 1
     for back, ref in enumerate(pair_refs):
         scr[pl.ds(2 * (halo - back), 2)] = ref[0]
+
+
+def on_diagonal(tokens, copies):
+    row = lax.broadcasted_iota(jnp.int32, (tokens, tokens), 0)
+    lane = lax.broadcasted_iota(jnp.int32, (tokens, tokens), 1)
+    return jnp.concatenate([row] * copies, axis=1), jnp.concatenate([lane] * copies, axis=1)
+
+
+def store_tiles(ref, e, at, tile, diagonal):
+    tokens, pair = diagonal.shape
+    lanes = slice(at, at + pair)
+    shared, rest = tile[:tokens], tile[tokens:]
+    ref[0, e, :tokens, lanes] = jnp.where(diagonal, 0.0, shared).astype(BF16)
+    ref[0, e, tokens:-tokens, lanes] = rest.astype(BF16)
+    ref[0, e, -tokens:, lanes] = jnp.where(diagonal, shared, 0.0).astype(BF16)
 
 
 def prob_kernel(halo, place_ref, lengths_ref, qd_ref, *refs):
@@ -127,16 +153,16 @@
     _, _, _, group, tokens, dim = qd_ref.shape
     count = 2 * halo + 1
     pair = 2 * tokens
-    lane = lax.broadcasted_iota(jnp.int32, (1, pair), 1) % tokens
+    row, lane = on_diagonal(tokens, 2)
+    diagonal = row <= lane
 
     @pl.when(pl.program_id(0) == 0)
     def _():
         for e in range(2):
-            query_pos = lane + (2 * halo + e) * tokens
+            query_pos = lane[:1] + (2 * halo + e) * tokens
             firsts[e] = first_allowed(lengths_ref, query_pos, place_ref[1])
 
     window_of(k_refs, k_scr)
-    row = lax.broadcasted_iota(jnp.int32, (tokens, pair), 0)
     for e in range(2):
         first = firsts[e] - row
         k = k_scr[pl.ds(e, count)].reshape(count * tokens, dim)
@@ -144,17 +170,17 @@
         do = qd_ref[0, e, 1].reshape(group * tokens, dim)
         for at in range(0, group * tokens, pair):
             s = lax.dot_general(k, q[at : at + pair], NT, preferred_element_type=F32)
-            tiles = []
-            for j in range(count):
-                allowed = first <= (e + j) * tokens
-                if j == count - 1:
-                    allowed &= row <= lane
-                tiles.append(jnp.where(allowed, s[j * tokens : (j + 1) * tokens], MASKED))
+            tiles = [s[j * tokens : (j + 1) * tokens] for j in range(count)]
+            last = (e + count - 1) * tokens
+            bound = jnp.where(diagonal, last, e * tokens)
+            tiles[0] = jnp.where(first <= bound, jnp.where(diagonal, tiles.pop(), tiles[0]), MASKED)
+            for j in range(1, count - 1):
+                tiles[j] = jnp.where(first <= (e + j) * tokens, tiles[j], MASKED)
             s = jnp.concatenate(tiles, axis=0)
             top = jnp.max(s, axis=0, keepdims=True)
             w = jnp.exp2((s - top) * (dim**-0.5 * LOG2E))
             inv = 1.0 / jnp.sum(w, axis=0, keepdims=True)
-            p_ref[0, e, :, at : at + pair] = (w * inv).astype(BF16)
+            store_tiles(p_ref, e, at, w * inv, diagonal)
         keep = (2 * halo - e) * tokens
         dv = jnp.dot(p_ref[0, e, :keep], do, preferred_element_type=F32).reshape(2 * halo - e, tokens, dim)
         if e == 0:
@@ -174,15 +200,21 @@
     count = 2 * halo + 1
     pair = 2 * tokens
     window_of(v_refs, v_scr)
+    row, lane = on_diagonal(tokens, 2)
+    diagonal = row <= lane
     for e in range(2):
         v = v_scr[pl.ds(e, count)].reshape(count * tokens, dim)
         q = qd_ref[0, e, 0].reshape(group * tokens, dim)
         do = qd_ref[0, e, 1].reshape(group * tokens, dim)
         for at in range(0, group * tokens, pair):
             dp = lax.dot_general(v, do[at : at + pair], NT, preferred_element_type=F32)
-            p = p_ref[0, e, :, at : at + pair].astype(F32)
+            last = (count - 1) * tokens
+            shared = jnp.where(diagonal, dp[last:], dp[:tokens])
+            dp = jnp.concatenate([shared, dp[tokens:last]], axis=0)
+            p = p_ref[0, e, :, at : at + pair]
+            p = jnp.concatenate([p[:tokens] + p[last:], p[tokens:last]], axis=0).astype(F32)
             delta = jnp.sum(p * dp, axis=0, keepdims=True)
-            ds_ref[0, e, :, at : at + pair] = (p * (dp - delta)).astype(BF16)
+            store_tiles(ds_ref, e, at, p * (dp - delta), diagonal)
         keep = (2 * halo - e) * tokens
         dk = jnp.dot(ds_ref[0, e, :keep], q, preferred_element_type=F32).reshape(2 * halo - e, tokens, dim)
         if e == 0:
@@ -196,8 +228,9 @@
 def own_kernel(halo, place_ref, qd_ref, p_ref, ds_ref, *refs):
     k_refs, back_refs = refs[: halo + 1], refs[halo + 1 : 2 * halo + 1]
     dq_ref, dq_other_ref, dk_ref, dv_ref, dv_other_ref, k_scr, dq_scr, dv_scr = refs[2 * halo + 1 :]
-    core = place_ref[0]
+    core, head = place_ref[0], pl.program_id(0)
     _, _, _, group, tokens, dim = qd_ref.shape
+    rows = dq_ref.shape[1]
     count = 2 * halo + 1
     scale = dim**-0.5
     window_of(k_refs, k_scr)
@@ -207,7 +240,7 @@
         k = k_scr[pl.ds(e, count)].reshape(count * tokens, dim)
         dqt = jnp.dot(k.T, ds_ref[0, e], preferred_element_type=F32) * scale
         for g in range(group):
-            dq_scr[e, g] = dqt[:, g * tokens : (g + 1) * tokens].T.astype(BF16)
+            dq_scr[e, pl.ds(head * group + g, tokens, stride=rows), :] = dqt[:, g * tokens : (g + 1) * tokens].T
         keep = (2 * halo - e) * tokens
         dk = jnp.dot(ds_ref[0, e, keep:], q, preferred_element_type=F32) * scale
         dv = jnp.dot(p_ref[0, e, keep:], do, preferred_element_type=F32)
@@ -219,10 +252,71 @@
             dk_ref[0, 1], dv_scr[1] = dk[tokens:], dv[tokens:]
     for ref in back_refs:
         dv_scr[...] += ref[0].astype(F32)
-    dq_ref[0] = dq_scr[core]
-    dq_other_ref[0] = dq_scr[1 - core]
     dv_ref[0] = dv_scr[core].astype(BF16)
     dv_other_ref[0] = dv_scr[1 - core].astype(BF16)
+
+    @pl.when(head == pl.num_programs(0) - 1)
+    def _():
+        dq_ref[...] = dq_scr[core].astype(BF16).reshape(dq_ref.shape)
+        dq_other_ref[...] = dq_scr[1 - core].astype(BF16).reshape(dq_ref.shape)
+
+
+def sum_kernel(place_ref, own_ref, *refs):
+    back_refs, (mine_ref, other_ref) = refs[:-2], refs[-2:]
+    core = place_ref[0]
+    for block, ref in [(1 - core, other_ref), (core, mine_ref)]:
+        total = own_ref[:, block]
+        for back in back_refs:
+            total += back[:, block].astype(F32)
+        ref[...] = total.astype(BF16)
+
+
+def summed(place, own, backs):
+    half, _, tokens, dim = own.shape
+    pair_spec = pl.BlockSpec(own.shape, lambda i, place: (0, 0, 0, 0))
+    one = (half, tokens, dim)
+    return call(
+        sum_kernel,
+        "sum_dk",
+        (1,),
+        place,
+        (own, *backs),
+        [pair_spec] * (1 + len(backs)),
+        [jax.ShapeDtypeStruct(one, BF16)] * 2,
+        [pl.BlockSpec(one, lambda i, place: (0, 0, 0))] * 2,
+        [],
+        10**8,
+    )
+
+
+def join_kernel(place_ref, own_ref, other_ref, out_ref, sems):
+    core = place_ref[0]
+    half = own_ref.shape[1]
+    copies = []
+    for which, ref in enumerate([own_ref, other_ref]):
+        side = 1 - core if which else core
+        at = pl.multiple_of(side * half, half)
+        copies.append(pltpu.make_async_copy(ref, out_ref.at[:, pl.ds(at, half)], sems.at[which]))
+        copies[-1].start()
+    for copy in copies:
+        copy.wait()
+
+
+def join(place, own, other):
+    tokens, half, dim = own.shape
+    anywhere = pl.BlockSpec(memory_space=pl.ANY)
+    return call(
+        join_kernel,
+        "join",
+        (1,),
+        place,
+        (own, other),
+        [anywhere] * 2,
+        jax.ShapeDtypeStruct((tokens, 2 * half, dim), BF16),
+        anywhere,
+        [pltpu.SemaphoreType.DMA((2,))],
+        10**9,
+    )
 
 
 def merge_kernel(place_ref, own_ref, other_ref, out_ref, scr):
@@ -236,19 +330,20 @@
     out_ref[...] = scr[...].astype(BF16).reshape(rows, heads, dim)
 
 
-def merge(place, own, other, rows, name):
+def merge(place, own, other, name):
     half, tokens, dim = own.shape
-    in_spec = pl.BlockSpec((half, rows, dim), lambda i, place: (0, i, 0))
+    spec = pl.BlockSpec(own.shape, lambda i, place: (0, 0, 0))
+    out = (tokens, 2 * half, dim)
     return call(
         merge_kernel,
         name,
-        (tokens // rows,),
+        (1,),
         place,
         (own, other),
-        [in_spec] * 2,
-        jax.ShapeDtypeStruct((tokens, 2 * half, dim), BF16),
-        pl.BlockSpec((rows, 2 * half, dim), lambda i, place: (i, 0, 0)),
-        [pltpu.VMEM((rows * 2 * half, dim), F32)],
+        [spec] * 2,
+        jax.ShapeDtypeStruct(out, BF16),
+        pl.BlockSpec(out, lambda i, place: (0, 0, 0)),
+        [pltpu.VMEM((tokens * 2 * half, dim), F32)],
         4 * 10**9,
     )
 
@@ -269,10 +364,12 @@
     far_first = range(halo, 0, -1)
     k_own = pack(place, keys, swapped(keys, device_count), "pack_k")
     k_own, queries, grad_out = lax.optimization_barrier((k_own, queries, grad_out))
-    v_own = pack(place, values, swapped(values, device_count), "pack_v")
     qd = arrange(
         place, queries, grad_out, swapped(queries, device_count), swapped(grad_out, device_count), key_heads
     )
+    v_other = swapped(values, device_count)
+    qd, values, v_other = lax.optimization_barrier((qd, values, v_other))
+    v_own = pack(place, values, v_other, "pack_v")
 
     def halo_of(own):
         received = {back: moved(own, device_count, 2 * back) for back in far_first}
@@ -286,13 +383,13 @@
 
     qd_spec = per_head(2, 2, group, tokens, dim)
     p_spec = per_head(2, count * tokens, group * tokens)
-    p_shape = jax.ShapeDtypeStruct((half, 2, count * tokens, group * tokens), BF16)
+    p_shape = pltpu.VMEM((half, 2, count * tokens, group * tokens), BF16)
     pair_spec = per_head(2, tokens, dim)
     pair = (half, 2, tokens, dim)
     one_spec = per_head(tokens, dim)
     one_shape = jax.ShapeDtypeStruct((half, tokens, dim), BF16)
-    dq_spec = per_head(group, tokens, dim)
-    dq_shape = jax.ShapeDtypeStruct((half, group, tokens, dim), BF16)
+    dq_shape = jax.ShapeDtypeStruct((tokens, heads // 2, dim), BF16)
+    dq_spec = pl.BlockSpec(dq_shape.shape, lambda h, *_: (0, 0, 0))
     run = pltpu.VMEM((window, tokens, dim), BF16)
     acc = pltpu.VMEM((2 * halo, tokens, dim), F32)
     product = 2 * half * 2 * count * tokens * group * tokens * dim
@@ -304,7 +401,7 @@
         "prob",
         (half,),
         (place, doc_lengths),
-        (qd, *k_pairs),
+        (in_vmem(qd), *k_pairs),
         [qd_spec] + [pair_spec] * (halo + 1),
         [p_shape] + [jax.ShapeDtypeStruct(pair, BF16)] * halo,
         [p_spec] + [pair_spec] * halo,
@@ -317,7 +414,7 @@
         "dscore",
         (half,),
         place,
-        (qd, prob, *v_pairs),
+        (in_vmem(qd), in_vmem(prob), *v_pairs),
         [qd_spec, p_spec] + [pair_spec] * (halo + 1),
         [p_shape] + [jax.ShapeDtypeStruct(pair, BF16)] * halo,
         [p_spec] + [pair_spec] * halo,
@@ -330,30 +427,23 @@
         "own",
         (half,),
         place,
-        (qd, prob, dscore, *k_pairs, *dv_back),
+        (in_vmem(qd), in_vmem(prob), in_vmem(dscore), *k_pairs, *dv_back),
         [qd_spec, p_spec, p_spec] + [pair_spec] * (2 * halo + 1),
         [dq_shape] * 2 + [jax.ShapeDtypeStruct(pair, F32)] + [one_shape] * 2,
         [dq_spec] * 2 + [pair_spec] + [one_spec] * 2,
         [
             run,
-            pltpu.VMEM((2, group, tokens, dim), BF16),
+            pltpu.VMEM((2, tokens * heads // 2, dim), F32),
             pltpu.VMEM((2, tokens, dim), F32),
         ],
         0,
     )
     dq_other = swapped(dq_other, device_count)
     dv_other = swapped(dv_other, device_count)
-    flat = (half * group, tokens, dim)
-    grad_queries = merge(place, dq.reshape(flat), dq_other.reshape(flat), 32, "merge_dq")
-    grad_values = merge(place, dv, dv_other, tokens, "merge_dv")
-
-    total = dk_own
-    for back in dk_back:
-        total = total + back.astype(F32)
-    total = total.astype(BF16)
-    mine = lax.dynamic_index_in_dim(total, core, 1, keepdims=False)
-    other = lax.dynamic_index_in_dim(total, 1 - core, 1, keepdims=False)
-    grad_keys = merge(place, mine, swapped(other, device_count), tokens, "merge_dk")
+    dk, dk_other = summed(place, dk_own, dk_back)
+    grad_queries = join(place, dq, dq_other)
+    grad_values = merge(place, dv, dv_other, "merge_dv")
+    grad_keys = merge(place, dk, swapped(dk_other, device_count), "merge_dk")
     return grad_queries, grad_keys, grad_values
 
 

time: 77.7 us -> 65.7 us (0.85)
  the two profiles are of different devices: /device:TPU:25 before, /device:TPU:23 now
where the time goes in v6:
time: 65.7 us; the launch traced here: 65.3 us
  starting transfers between devices  30 us (46%)
  Pallas kernels  26.5 us (40%)
  waiting for transfers between devices  5.43 us (8%)
  local copies, waits for them, and re-layouts  2.45 us (4%)
  between operations  0.84 us (1%)
    pallas_call x10, Pallas kernels, call(): pl.pallas_call(kernel, out_shape=outs, grid_spec=pltpu.PrefetchScalarGrid...  26.5 us
    ppermute x8, starting transfers between devices, moved(): return lax.ppermute(array, AXES, pairs)  22.9 us
    ppermute x7, starting transfers between devices, swapped(): return lax.ppermute(array, AXES, [(d, d ^ 1) for d in range(device_count)])  7.09 us
    ppermute x8, waiting for transfers between devices, moved(): return lax.ppermute(array, AXES, pairs)  4.11 us
    unnamed x6, local copies, waits for them, and re-layouts  2.45 us
  transfers between devices with their start and end apart: 15, of which 2 were waited for; matrix products, arithmetic and copies ran while one was open for 0% of the time, Pallas kernels for 36%

profile of v6, /device:TPU:23, one launch (start us, length us, event | category | flops | bytes accessed | tf_op | source)
XLA Modules:
  0.0 65.3 jit_solution(5751209813686734506)
XLA Ops:
  0.6 0.7 %collective-permute-start = (bf16[128,8,128]{2,1,0:T(8,128)(2,1)}, bf16[128,8,128]{2,1,0:T(8,128)(2,1)S(1)}, u32[]{:S(2)}, u32[]{:S(2)}) collective-permute-start(bf16[128,8,128]{2,1,0:T(8,128)(2,1)} %own_ref.1), channel_id=1, source_target_pairs={{0,1},{1,0},{2,3},{3,2},{4,5},{5,4},{6,7},{7,6},{8,9},{9,8},{10,11... | collective-permute-start | bytes 786440 | tf_op jit(solution)/shard_map/ppermute | solution.py:24
  1.4 0.1 pad_add_fusion.place_ref
  1.4 1.3 %collective-permute-done.other_ref = bf16[128,8,128]{2,1,0:T(8,128)(2,1)S(1)} collective-permute-done((bf16[128,8,128]{2,1,0:T(8,128)(2,1)}, bf16[128,8,128]{2,1,0:T(8,128)(2,1)S(1)}, u32[]{:S(2)}, u32[]{:S(2)}) %collective-permute-start) | collective-permute-done | bytes 262176 | tf_op jit(solution)/shard_map/ppermute | solution.py:24
  2.7 1.6 %pack_k.1.refs_0_ = bf16[4,2,128,128]{3,2,1,0:T(8,128)(2,1)S(1)} custom-call(s32[2]{0:T(128)S(1)} %pad_add_fusion.place_ref, bf16[128,8,128]{2,1,0:T(8,128)(2,1)} %own_ref.1, bf16[128,8,128]{2,1,0:T(8,128)(2,1)S(1)} %collective-permute-done.other_ref), custom_call_target="tpu_custom_call" | custom-call | flops 1000000000 | tf_op jit(solution)/shard_map/pack_k/pallas_call | solution.py:33
  4.3 0.4 collective-permute-start.1
  4.8 0.1 collective-permute-start.2
  4.9 0.4 collective-permute-start.3
  5.3 3.1 %collective-permute-start.5 = (bf16[4,2,128,128]{3,2,1,0:T(8,128)(2,1)S(1)}, bf16[4,2,128,128]{3,2,1,0:T(8,128)(2,1)S(1)}, u32[]{:S(2)}, u32[]{:S(2)}) collective-permute-start(bf16[4,2,128,128]{3,2,1,0:T(8,128)(2,1)S(1)} %pack_k.1.refs_0_), channel_id=1, source_target_pairs={{0,4},{1,5},{2,6},{3,7},{4,8},{5,9},{6,10},{7,11},{8,12},{9,13},{1... | collective-permute-start | bytes 786440 | tf_op jit(solution)/shard_map/ppermute | solution.py:20
  8.4 3.1 %collective-permute-start.4 = (bf16[4,2,128,128]{3,2,1,0:T(8,128)(2,1)S(1)}, bf16[4,2,128,128]{3,2,1,0:T(8,128)(2,1)S(1)}, u32[]{:S(2)}, u32[]{:S(2)}) collective-permute-start(bf16[4,2,128,128]{3,2,1,0:T(8,128)(2,1)S(1)} %pack_k.1.refs_0_), channel_id=1, source_target_pairs={{0,2},{1,3},{2,4},{3,5},{4,6},{5,7},{6,8},{7,9},{8,10},{9,11},{10,... | collective-permute-start | bytes 786440 | tf_op jit(solution)/shard_map/ppermute | solution.py:20
  11.6 0.0 collective-permute-done.1.q_other_ref
  11.6 0.0 copy-start
  11.6 1.2 %copy-done = bf16[128,32,128]{2,1,0:T(8,128)(2,1)S(1)} copy-done((bf16[128,32,128]{2,1,0:T(8,128)(2,1)S(1)}, bf16[128,32,128]{2,1,0:T(8,128)(2,1)}, u32[]{:S(2)}) %copy-start) | copy-done | bytes 1048600
  12.8 1.2 %copy-done.1 = bf16[128,32,128]{2,1,0:T(8,128)(2,1)S(1)} copy-done((bf16[128,32,128]{2,1,0:T(8,128)(2,1)S(1)}, bf16[128,32,128]{2,1,0:T(8,128)(2,1)}, u32[]{:S(2)}) %copy-start.1) | copy-done | bytes 1048600
  14.0 2.5 %arrange.1.qd_ref = bf16[4,2,2,4,128,128]{5,4,3,2,1,0:T(8,128)(2,1)S(1)} custom-call(s32[2]{0:T(128)S(1)} %pad_add_fusion.place_ref, bf16[128,32,128]{2,1,0:T(8,128)(2,1)S(1)} %copy-done, bf16[128,32,128]{2,1,0:T(8,128)(2,1)S(1)} %copy-done.1, bf16[128,32,128]{2,1,0:T(8,128)(2,1)S(1)} %collective-permute-done.1.q_other_ref, ...), custom_call_target="tpu_custom_call" | custom-call | flops 1000000000 | tf_op jit(solution)/shard_map/arrange/pallas_call | solution.py:33
  16.5 1.6 %pack_v.1.refs_0_ = bf16[4,2,128,128]{3,2,1,0:T(8,128)(2,1)S(1)} custom-call(s32[2]{0:T(128)S(1)} %pad_add_fusion.place_ref, bf16[128,8,128]{2,1,0:T(8,128)(2,1)} %own_ref.2, bf16[128,8,128]{2,1,0:T(8,128)(2,1)S(1)} %collective-permute-done.3.other_ref), custom_call_target="tpu_custom_call" | custom-call | flops 1000000000 | tf_op jit(solution)/shard_map/pack_v/pallas_call | solution.py:33
  18.1 1.9 %collective-permute-start.7 = (bf16[4,2,128,128]{3,2,1,0:T(8,128)(2,1)S(1)}, bf16[4,2,128,128]{3,2,1,0:T(8,128)(2,1)S(1)}, u32[]{:S(2)}, u32[]{:S(2)}) collective-permute-start(bf16[4,2,128,128]{3,2,1,0:T(8,128)(2,1)S(1)} %pack_v.1.refs_0_), channel_id=1, source_target_pairs={{0,4},{1,5},{2,6},{3,7},{4,8},{5,9},{6,10},{7,11},{8,12},{9,13},{1... | collective-permute-start | bytes 786440 | tf_op jit(solution)/shard_map/ppermute | solution.py:20
  20.1 3.1 %collective-permute-start.6 = (bf16[4,2,128,128]{3,2,1,0:T(8,128)(2,1)S(1)}, bf16[4,2,128,128]{3,2,1,0:T(8,128)(2,1)S(1)}, u32[]{:S(2)}, u32[]{:S(2)}) collective-permute-start(bf16[4,2,128,128]{3,2,1,0:T(8,128)(2,1)S(1)} %pack_v.1.refs_0_), channel_id=1, source_target_pairs={{0,2},{1,3},{2,4},{3,5},{4,6},{5,7},{6,8},{7,9},{8,10},{9,11},{10,... | collective-permute-start | bytes 786440 | tf_op jit(solution)/shard_map/ppermute | solution.py:20
  23.2 6.5 %prob.1 = (bf16[4,2,640,512]{3,2,1,0:T(8,128)(2,1)S(1)}, bf16[4,2,128,128]{3,2,1,0:T(8,128)(2,1)S(1)}, bf16[4,2,128,128]{3,2,1,0:T(8,128)(2,1)S(1)}) custom-call(s32[2]{0:T(128)S(1)} %pad_add_fusion.place_ref, s32[16]{0:T(128)S(1)} %copy-done.2, bf16[4,2,2,4,128,128]{5,4,3,2,1,0:T(8,128)(2,1)S(1)} %arrange.1.qd_ref, ...), custom_call_target="tpu_custom_call" | custom-call | flops 2684354560 | tf_op jit(solution)/shard_map/prob/pallas_call | solution.py:33
  29.7 3.4 %collective-permute-start.8 = (bf16[4,2,128,128]{3,2,1,0:T(8,128)(2,1)S(1)}, bf16[4,2,128,128]{3,2,1,0:T(8,128)(2,1)S(1)}, u32[]{:S(2)}, u32[]{:S(2)}) collective-permute-start(bf16[4,2,128,128]{3,2,1,0:T(8,128)(2,1)S(1)} %get-tuple-element.30), channel_id=1, source_target_pairs={{4,0},{5,1},{6,2},{7,3},{8,4},{9,5},{10,6},{11,7},{12,8},{13,9},{1... | collective-permute-start | bytes 786440 | tf_op jit(solution)/shard_map/ppermute | solution.py:20
  33.1 2.2 %collective-permute-start.9 = (bf16[4,2,128,128]{3,2,1,0:T(8,128)(2,1)S(1)}, bf16[4,2,128,128]{3,2,1,0:T(8,128)(2,1)S(1)}, u32[]{:S(2)}, u32[]{:S(2)}) collective-permute-start(bf16[4,2,128,128]{3,2,1,0:T(8,128)(2,1)S(1)} %get-tuple-element.31), channel_id=1, source_target_pairs={{2,0},{3,1},{4,2},{5,3},{6,4},{7,5},{8,6},{9,7},{10,8},{11,9},{12,... | collective-permute-start | bytes 786440 | tf_op jit(solution)/shard_map/ppermute | solution.py:20
  35.3 6.1 %dscore.1 = (bf16[4,2,640,512]{3,2,1,0:T(8,128)(2,1)S(1)}, bf16[4,2,128,128]{3,2,1,0:T(8,128)(2,1)S(1)}, bf16[4,2,128,128]{3,2,1,0:T(8,128)(2,1)S(1)}) custom-call(s32[2]{0:T(128)S(1)} %pad_add_fusion.place_ref, bf16[4,2,2,4,128,128]{5,4,3,2,1,0:T(8,128)(2,1)S(1)} %arrange.1.qd_ref, bf16[4,2,640,512]{3,2,1,0:T(8,128)(2,1)S(1)} %get-tuple-element.26.p_ref, ...), custom_call_target="tpu_custom_call" | custom-call | flops 2684354560 | tf_op jit(solution)/shard_map/dscore/pallas_call | solution.py:33
  41.4 3.0 %collective-permute-start.11 = (bf16[4,2,128,128]{3,2,1,0:T(8,128)(2,1)S(1)}, bf16[4,2,128,128]{3,2,1,0:T(8,128)(2,1)S(1)}, u32[]{:S(2)}, u32[]{:S(2)}) collective-permute-start(bf16[4,2,128,128]{3,2,1,0:T(8,128)(2,1)S(1)} %get-tuple-element.35), channel_id=1, source_target_pairs={{4,0},{5,1},{6,2},{7,3},{8,4},{9,5},{10,6},{11,7},{12,8},{13,9},{1... | collective-permute-start | bytes 786440 | tf_op jit(solution)/shard_map/ppermute | solution.py:20
  44.4 3.0 %collective-permute-start.12 = (bf16[4,2,128,128]{3,2,1,0:T(8,128)(2,1)S(1)}, bf16[4,2,128,128]{3,2,1,0:T(8,128)(2,1)S(1)}, u32[]{:S(2)}, u32[]{:S(2)}) collective-permute-start(bf16[4,2,128,128]{3,2,1,0:T(8,128)(2,1)S(1)} %get-tuple-element.36), channel_id=1, source_target_pairs={{2,0},{3,1},{4,2},{5,3},{6,4},{7,5},{8,6},{9,7},{10,8},{11,9},{12,... | collective-permute-start | bytes 786440 | tf_op jit(solution)/shard_map/ppermute | solution.py:20
  47.5 3.3 %own.1 = (bf16[128,16,128]{2,1,0:T(8,128)(2,1)S(1)}, bf16[128,16,128]{2,1,0:T(8,128)(2,1)S(1)}, f32[4,2,128,128]{3,2,1,0:T(8,128)S(1)}, bf16[4,128,128]{2,1,0:T(8,128)(2,1)S(1)}, bf16[4,128,128]{2,1,0:T(8,128)(2,1)S(1)}) custom-call(s32[2]{0:T(128)S(1)} %pad_add_fusion.place_ref, bf16[4,2,2,4,128,128]{5,4,3,2,1,0:T(8,128)(2,1)S(1)} %arrange.1.qd_ref, ...), custom_call_target="tpu_custom_call" | custom-call | tf_op jit(solution)/shard_map/own/pallas_call | solution.py:33
  50.8 2.5 %collective-permute-start.14 = (bf16[4,128,128]{2,1,0:T(8,128)(2,1)S(1)}, bf16[4,128,128]{2,1,0:T(8,128)(2,1)S(1)}, u32[]{:S(2)}, u32[]{:S(2)}) collective-permute-start(bf16[4,128,128]{2,1,0:T(8,128)(2,1)S(1)} %get-tuple-element.40), channel_id=1, source_target_pairs={{0,1},{1,0},{2,3},{3,2},{4,5},{5,4},{6,7},{7,6},{8,9},{9,8},{10,11... | collective-permute-start | bytes 393224 | tf_op jit(solution)/shard_map/ppermute | solution.py:24
  53.3 0.1 collective-permute-start.10
  53.4 4.1 %collective-permute-done.12.refs_1_ = bf16[4,2,128,128]{3,2,1,0:T(8,128)(2,1)S(1)} collective-permute-done((bf16[4,2,128,128]{3,2,1,0:T(8,128)(2,1)S(1)}, bf16[4,2,128,128]{3,2,1,0:T(8,128)(2,1)S(1)}, u32[]{:S(2)}, u32[]{:S(2)}) %collective-permute-start.12) | collective-permute-done | bytes 262176 | tf_op jit(solution)/shard_map/ppermute | solution.py:20
  57.5 0.6 sum_dk.1
  58.1 2.8 %collective-permute-start.13 = (bf16[4,128,128]{2,1,0:T(8,128)(2,1)S(1)}, bf16[4,128,128]{2,1,0:T(8,128)(2,1)S(1)}, u32[]{:S(2)}, u32[]{:S(2)}) collective-permute-start(bf16[4,128,128]{2,1,0:T(8,128)(2,1)S(1)} %get-tuple-element.38), channel_id=1, source_target_pairs={{0,1},{1,0},{2,3},{3,2},{4,5},{5,4},{6,7},{7,6},{8,9},{9,8},{10,11... | collective-permute-start | bytes 393224 | tf_op jit(solution)/shard_map/ppermute | solution.py:24
  61.0 1.4 %merge_dv.1 = bf16[128,8,128]{2,1,0:T(8,128)(2,1)} custom-call(s32[2]{0:T(128)S(1)} %pad_add_fusion.place_ref, bf16[4,128,128]{2,1,0:T(8,128)(2,1)S(1)} %get-tuple-element.39.own_ref, bf16[4,128,128]{2,1,0:T(8,128)(2,1)S(1)} %collective-permute-done.14.other_ref), custom_call_target="tpu_custom_call" | custom-call | flops 4000000000 | tf_op jit(solution)/shard_map/merge_dv/pallas_call | solution.py:33
  62.4 1.4 %merge_dk.1 = bf16[128,8,128]{2,1,0:T(8,128)(2,1)} custom-call(s32[2]{0:T(128)S(1)} %pad_add_fusion.place_ref, bf16[4,128,128]{2,1,0:T(8,128)(2,1)S(1)} %get-tuple-element.37.own_ref, bf16[4,128,128]{2,1,0:T(8,128)(2,1)S(1)} %collective-permute-done.13.other_ref), custom_call_target="tpu_custom_call" | custom-call | flops 4000000000 | tf_op jit(solution)/shard_map/merge_dk/pallas_call | solution.py:33
  63.8 1.5 %join.1 = bf16[128,32,128]{2,1,0:T(8,128)(2,1)} custom-call(s32[2]{0:T(128)S(1)} %pad_add_fusion.place_ref, bf16[128,16,128]{2,1,0:T(8,128)(2,1)S(1)} %get-tuple-element.32.own_ref, bf16[128,16,128]{2,1,0:T(8,128)(2,1)S(1)} %collective-permute-done.10.other_ref), custom_call_target="tpu_custom_call" | custom-call | flops 1000000000 | tf_op jit(solution)/shard_map/join/pallas_call | solution.py:33
  (15 shorter events, 0.0 us)
Async XLA Ops:
  0.6 2.1 %collective-permute-start = (bf16[128,8,128]{2,1,0:T(8,128)(2,1)}, bf16[128,8,128]{2,1,0:T(8,128)(2,1)S(1)}, u32[]{:S(2)}, u32[]{:S(2)}) collective-permute-start(bf16[128,8,128]{2,1,0:T(8,128)(2,1)} %own_ref.1), channel_id=1, source_target_pairs={{0,1},{1,0},{2,3},{3,2},{4,5},{5,4},{6,7},{7,6},{8,9},{9,8},{10,11... | collective-permute-start | bytes 786440 | tf_op jit(solution)/shard_map/ppermute | solution.py:24
  2.7 20.5 %copy-start.2 = (s32[16]{0:T(128)S(1)}, s32[16]{0:T(128)}, u32[]{:S(2)}) copy-start(s32[16]{0:T(128)} %lengths_ref.1) | copy-start | bytes 196
  4.3 7.2 %collective-permute-start.1 = (bf16[128,32,128]{2,1,0:T(8,128)(2,1)}, bf16[128,32,128]{2,1,0:T(8,128)(2,1)S(1)}, u32[]{:S(2)}, u32[]{:S(2)}) collective-permute-start(bf16[128,32,128]{2,1,0:T(8,128)(2,1)} %q_ref), channel_id=1, source_target_pairs={{0,1},{1,0},{2,3},{3,2},{4,5},{5,4},{6,7},{7,6},{8,9},{9,8},{10,11... | collective-permute-start | bytes 3145736 | tf_op jit(solution)/shard_map/ppermute | solution.py:24
  4.8 6.8 %collective-permute-start.2 = (bf16[128,32,128]{2,1,0:T(8,128)(2,1)}, bf16[128,32,128]{2,1,0:T(8,128)(2,1)S(1)}, u32[]{:S(2)}, u32[]{:S(2)}) collective-permute-start(bf16[128,32,128]{2,1,0:T(8,128)(2,1)} %do_ref), channel_id=1, source_target_pairs={{0,1},{1,0},{2,3},{3,2},{4,5},{5,4},{6,7},{7,6},{8,9},{9,8},{10,11... | collective-permute-start | bytes 3145736 | tf_op jit(solution)/shard_map/ppermute | solution.py:24
  4.9 11.6 %collective-permute-start.3 = (bf16[128,8,128]{2,1,0:T(8,128)(2,1)}, bf16[128,8,128]{2,1,0:T(8,128)(2,1)S(1)}, u32[]{:S(2)}, u32[]{:S(2)}) collective-permute-start(bf16[128,8,128]{2,1,0:T(8,128)(2,1)} %own_ref.2), channel_id=1, source_target_pairs={{0,1},{1,0},{2,3},{3,2},{4,5},{5,4},{6,7},{7,6},{8,9},{9,8},{10,11... | collective-permute-start | bytes 786440 | tf_op jit(solution)/shard_map/ppermute | solution.py:24
  5.3 17.9 %collective-permute-start.5 = (bf16[4,2,128,128]{3,2,1,0:T(8,128)(2,1)S(1)}, bf16[4,2,128,128]{3,2,1,0:T(8,128)(2,1)S(1)}, u32[]{:S(2)}, u32[]{:S(2)}) collective-permute-start(bf16[4,2,128,128]{3,2,1,0:T(8,128)(2,1)S(1)} %pack_k.1.refs_0_), channel_id=1, source_target_pairs={{0,4},{1,5},{2,6},{3,7},{4,8},{5,9},{6,10},{7,11},{8,12},{9,13},{1... | collective-permute-start | bytes 786440 | tf_op jit(solution)/shard_map/ppermute | solution.py:20
  8.4 14.8 %collective-permute-start.4 = (bf16[4,2,128,128]{3,2,1,0:T(8,128)(2,1)S(1)}, bf16[4,2,128,128]{3,2,1,0:T(8,128)(2,1)S(1)}, u32[]{:S(2)}, u32[]{:S(2)}) collective-permute-start(bf16[4,2,128,128]{3,2,1,0:T(8,128)(2,1)S(1)} %pack_k.1.refs_0_), channel_id=1, source_target_pairs={{0,2},{1,3},{2,4},{3,5},{4,6},{5,7},{6,8},{7,9},{8,10},{9,11},{10,... | collective-permute-start | bytes 786440 | tf_op jit(solution)/shard_map/ppermute | solution.py:20
  11.6 1.2 %copy-start = (bf16[128,32,128]{2,1,0:T(8,128)(2,1)S(1)}, bf16[128,32,128]{2,1,0:T(8,128)(2,1)}, u32[]{:S(2)}) copy-start(bf16[128,32,128]{2,1,0:T(8,128)(2,1)} %q_ref) | copy-start | bytes 3145732
  12.8 1.2 %copy-start.1 = (bf16[128,32,128]{2,1,0:T(8,128)(2,1)S(1)}, bf16[128,32,128]{2,1,0:T(8,128)(2,1)}, u32[]{:S(2)}) copy-start(bf16[128,32,128]{2,1,0:T(8,128)(2,1)} %do_ref) | copy-start | bytes 3145732
  18.1 17.1 %collective-permute-start.7 = (bf16[4,2,128,128]{3,2,1,0:T(8,128)(2,1)S(1)}, bf16[4,2,128,128]{3,2,1,0:T(8,128)(2,1)S(1)}, u32[]{:S(2)}, u32[]{:S(2)}) collective-permute-start(bf16[4,2,128,128]{3,2,1,0:T(8,128)(2,1)S(1)} %pack_v.1.refs_0_), channel_id=1, source_target_pairs={{0,4},{1,5},{2,6},{3,7},{4,8},{5,9},{6,10},{7,11},{8,12},{9,13},{1... | collective-permute-start | bytes 786440 | tf_op jit(solution)/shard_map/ppermute | solution.py:20
  20.1 15.2 %collective-permute-start.6 = (bf16[4,2,128,128]{3,2,1,0:T(8,128)(2,1)S(1)}, bf16[4,2,128,128]{3,2,1,0:T(8,128)(2,1)S(1)}, u32[]{:S(2)}, u32[]{:S(2)}) collective-permute-start(bf16[4,2,128,128]{3,2,1,0:T(8,128)(2,1)S(1)} %pack_v.1.refs_0_), channel_id=1, source_target_pairs={{0,2},{1,3},{2,4},{3,5},{4,6},{5,7},{6,8},{7,9},{8,10},{9,11},{10,... | collective-permute-start | bytes 786440 | tf_op jit(solution)/shard_map/ppermute | solution.py:20
  29.7 17.8 %collective-permute-start.8 = (bf16[4,2,128,128]{3,2,1,0:T(8,128)(2,1)S(1)}, bf16[4,2,128,128]{3,2,1,0:T(8,128)(2,1)S(1)}, u32[]{:S(2)}, u32[]{:S(2)}) collective-permute-start(bf16[4,2,128,128]{3,2,1,0:T(8,128)(2,1)S(1)} %get-tuple-element.30), channel_id=1, source_target_pairs={{4,0},{5,1},{6,2},{7,3},{8,4},{9,5},{10,6},{11,7},{12,8},{13,9},{1... | collective-permute-start | bytes 786440 | tf_op jit(solution)/shard_map/ppermute | solution.py:20
  33.1 14.4 %collective-permute-start.9 = (bf16[4,2,128,128]{3,2,1,0:T(8,128)(2,1)S(1)}, bf16[4,2,128,128]{3,2,1,0:T(8,128)(2,1)S(1)}, u32[]{:S(2)}, u32[]{:S(2)}) collective-permute-start(bf16[4,2,128,128]{3,2,1,0:T(8,128)(2,1)S(1)} %get-tuple-element.31), channel_id=1, source_target_pairs={{2,0},{3,1},{4,2},{5,3},{6,4},{7,5},{8,6},{9,7},{10,8},{11,9},{12,... | collective-permute-start | bytes 786440 | tf_op jit(solution)/shard_map/ppermute | solution.py:20
  41.4 12.0 %collective-permute-start.11 = (bf16[4,2,128,128]{3,2,1,0:T(8,128)(2,1)S(1)}, bf16[4,2,128,128]{3,2,1,0:T(8,128)(2,1)S(1)}, u32[]{:S(2)}, u32[]{:S(2)}) collective-permute-start(bf16[4,2,128,128]{3,2,1,0:T(8,128)(2,1)S(1)} %get-tuple-element.35), channel_id=1, source_target_pairs={{4,0},{5,1},{6,2},{7,3},{8,4},{9,5},{10,6},{11,7},{12,8},{13,9},{1... | collective-permute-start | bytes 786440 | tf_op jit(solution)/shard_map/ppermute | solution.py:20
  44.4 13.1 %collective-permute-start.12 = (bf16[4,2,128,128]{3,2,1,0:T(8,128)(2,1)S(1)}, bf16[4,2,128,128]{3,2,1,0:T(8,128)(2,1)S(1)}, u32[]{:S(2)}, u32[]{:S(2)}) collective-permute-start(bf16[4,2,128,128]{3,2,1,0:T(8,128)(2,1)S(1)} %get-tuple-element.36), channel_id=1, source_target_pairs={{2,0},{3,1},{4,2},{5,3},{6,4},{7,5},{8,6},{9,7},{10,8},{11,9},{12,... | collective-permute-start | bytes 786440 | tf_op jit(solution)/shard_map/ppermute | solution.py:20
  50.8 10.1 %collective-permute-start.14 = (bf16[4,128,128]{2,1,0:T(8,128)(2,1)S(1)}, bf16[4,128,128]{2,1,0:T(8,128)(2,1)S(1)}, u32[]{:S(2)}, u32[]{:S(2)}) collective-permute-start(bf16[4,128,128]{2,1,0:T(8,128)(2,1)S(1)} %get-tuple-element.40), channel_id=1, source_target_pairs={{0,1},{1,0},{2,3},{3,2},{4,5},{5,4},{6,7},{7,6},{8,9},{9,8},{10,11... | collective-permute-start | bytes 393224 | tf_op jit(solution)/shard_map/ppermute | solution.py:24
  53.3 10.5 %collective-permute-start.10 = (bf16[128,16,128]{2,1,0:T(8,128)(2,1)S(1)}, bf16[128,16,128]{2,1,0:T(8,128)(2,1)S(1)}, u32[]{:S(2)}, u32[]{:S(2)}) collective-permute-start(bf16[128,16,128]{2,1,0:T(8,128)(2,1)S(1)} %get-tuple-element.33), channel_id=1, source_target_pairs={{0,1},{1,0},{2,3},{3,2},{4,5},{5,4},{6,7},{7,6},{8,9},{9,8},{10,11... | collective-permute-start | bytes 1572872 | tf_op jit(solution)/shard_map/ppermute | solution.py:24
  58.1 4.2 %collective-permute-start.13 = (bf16[4,128,128]{2,1,0:T(8,128)(2,1)S(1)}, bf16[4,128,128]{2,1,0:T(8,128)(2,1)S(1)}, u32[]{:S(2)}, u32[]{:S(2)}) collective-permute-start(bf16[4,128,128]{2,1,0:T(8,128)(2,1)S(1)} %get-tuple-element.38), channel_id=1, source_target_pairs={{0,1},{1,0},{2,3},{3,2},{4,5},{5,4},{6,7},{7,6},{8,9},{9,8},{10,11... | collective-permute-start | bytes 393224 | tf_op jit(solution)/shard_map/ppermute | solution.py:24

commit v7 on v6

--- a/solution.py
+++ b/solution.py
@@ -28,7 +28,7 @@
     return pltpu.with_memory_space_constraint(array, pltpu.VMEM)
 
 
-def call(kernel, name, grid, place, inputs, in_specs, outs, out_specs, scratch, flops):
+def call(kernel, name, grid, place, inputs, in_specs, outs, out_specs, scratch, flops, aliases={}):
     scalars = place if isinstance(place, tuple) else (place,)
     return pl.pallas_call(
         kernel,
@@ -42,6 +42,7 @@
         ),
         compiler_params=pltpu.CompilerParams(vmem_limit_bytes=VMEM_BYTES),
         cost_estimate=pl.CostEstimate(flops=flops, bytes_accessed=0, transcendentals=0),
+        input_output_aliases=aliases,
         name=name,
     )(*scalars, *inputs)
 
@@ -77,40 +78,102 @@
     )
 
 
-def pack_kernel(place_ref, own_ref, other_ref, out_ref, own_scr, scr, sem):
+def pack_block(raw, core, block, out_ref, scr):
+    tokens, heads, dim = raw.shape
+    half = heads // 2
+    scr[...] = raw[...].astype(F32).reshape(tokens * heads, dim)
+    for h in range(half):
+        out_ref[h, block] = scr[pl.ds(core * half + h, tokens, stride=heads), :].astype(BF16)
+
+
+def fetch_kernel(place_ref, key_ref, *refs):
+    count = (len(refs) - 4) // 2
+    sources, out_ref, targets = refs[:count], refs[count], refs[count + 1 : 2 * count + 1]
+    raw, scr, sems = refs[-3:]
+    first = pltpu.make_async_copy(key_ref, raw, sems.at[0])
+    first.start()
+    copies = [pltpu.make_async_copy(s, t, sems.at[i + 1]) for i, (s, t) in enumerate(zip(sources, targets))]
+    for copy in copies:
+        copy.start()
+    first.wait()
+    pack_block(raw, place_ref[0], place_ref[0], out_ref, scr)
+    for copy in copies:
+        copy.wait()
+
+
+def fetch(place, keys, arrays):
+    tokens, heads, dim = keys.shape
+    out = (heads // 2, 2, tokens, dim)
+    return call(
+        fetch_kernel,
+        "fetch",
+        (1,),
+        place,
+        [pltpu.with_memory_space_constraint(x, pltpu.HBM) for x in (keys, *arrays)],
+        [pl.BlockSpec(memory_space=pltpu.HBM)] * (1 + len(arrays)),
+        [pltpu.VMEM(out, BF16)] + [pltpu.VMEM(x.shape, x.dtype) for x in arrays],
+        [pl.BlockSpec(memory_space=pltpu.VMEM)] * (1 + len(arrays)),
+        [
+            pltpu.VMEM(keys.shape, BF16),
+            pltpu.VMEM((tokens * heads, dim), F32),
+            pltpu.SemaphoreType.DMA((1 + len(arrays),)),
+        ],
+        10**9,
+    )
+
+
+def pack_other_kernel(place_ref, other_ref, _, out_ref, scr):
+    pack_block(other_ref, place_ref[0], 1 - place_ref[0], out_ref, scr)
+
+
+def pack_other(place, other, packed):
+    tokens, heads, dim = other.shape
+    whole = pl.BlockSpec(memory_space=pltpu.VMEM)
+    return call(
+        pack_other_kernel,
+        "pack_other",
+        (1,),
+        place,
+        (in_vmem(other), in_vmem(packed)),
+        [whole] * 2,
+        pltpu.VMEM(packed.shape, BF16),
+        whole,
+        [pltpu.VMEM((tokens * heads, dim), F32)],
+        10**9,
+        {2: 0},
+    )
+
+
+def pack_both_kernel(place_ref, own_ref, other_ref, out_ref, scr):
     core = place_ref[0]
-    tokens, heads, dim = other_ref.shape
-    half = heads // 2
-    fetch = pltpu.make_async_copy(own_ref, own_scr, sem)
-    fetch.start()
-    for which, ref in enumerate([other_ref, own_scr]):
-        if which:
-            fetch.wait()
-        block = core if which else 1 - core
-        scr[...] = ref[...].astype(F32).reshape(tokens * heads, dim)
-        for h in range(half):
-            out_ref[h, block] = scr[pl.ds(core * half + h, tokens, stride=heads), :].astype(BF16)
-
-
-def pack(place, own, other, name):
+    pack_block(own_ref, core, core, out_ref, scr)
+    pack_block(other_ref, core, 1 - core, out_ref, scr)
+
+
+def pack_both(place, own, other):
     tokens, heads, dim = own.shape
     out = (heads // 2, 2, tokens, dim)
-    return call(
-        pack_kernel,
-        name,
+    whole = pl.BlockSpec(memory_space=pltpu.VMEM)
+    return call(
+        pack_both_kernel,
+        "pack_both",
         (1,),
         place,
-        (pltpu.with_memory_space_constraint(own, pltpu.HBM), other),
-        [pl.BlockSpec(memory_space=pltpu.HBM), pl.BlockSpec(own.shape, lambda i, place: (0, 0, 0))],
-        jax.ShapeDtypeStruct(out, BF16),
-        pl.BlockSpec(out, lambda i, place: (0, 0, 0, 0)),
-        [
-            pltpu.VMEM(own.shape, BF16),
-            pltpu.VMEM((tokens * heads, dim), F32),
-            pltpu.SemaphoreType.DMA,
-        ],
+        (in_vmem(own), in_vmem(other)),
+        [whole] * 2,
+        pltpu.VMEM(out, BF16),
+        whole,
+        [pltpu.VMEM((tokens * heads, dim), F32)],
         10**9,
     )
+
+
+def folded(op, x):
+    while x.shape[0] > 8:
+        half = x.shape[0] // 2
+        x = op(x[:half], x[half:])
+    reduce = jnp.max if op is jnp.maximum else jnp.sum
+    return reduce(x, axis=0, keepdims=True)
 
 
 def first_allowed(lengths_ref, query_pos, window_start):
@@ -136,13 +199,13 @@
     return jnp.concatenate([row] * copies, axis=1), jnp.concatenate([lane] * copies, axis=1)
 
 
-def store_tiles(ref, e, at, tile, diagonal):
+def store_tiles(ref, e, at, tiles, diagonal):
     tokens, pair = diagonal.shape
     lanes = slice(at, at + pair)
-    shared, rest = tile[:tokens], tile[tokens:]
-    ref[0, e, :tokens, lanes] = jnp.where(diagonal, 0.0, shared).astype(BF16)
-    ref[0, e, tokens:-tokens, lanes] = rest.astype(BF16)
-    ref[0, e, -tokens:, lanes] = jnp.where(diagonal, shared, 0.0).astype(BF16)
+    ref[0, e, :tokens, lanes] = jnp.where(diagonal, 0.0, tiles[0]).astype(BF16)
+    for j, tile in enumerate(tiles[1:], 1):
+        ref[0, e, j * tokens : (j + 1) * tokens, lanes] = tile.astype(BF16)
+    ref[0, e, -tokens:, lanes] = jnp.where(diagonal, tiles[0], 0.0).astype(BF16)
 
 
 def prob_kernel(halo, place_ref, lengths_ref, qd_ref, *refs):
@@ -176,11 +239,10 @@
             tiles[0] = jnp.where(first <= bound, jnp.where(diagonal, tiles.pop(), tiles[0]), MASKED)
             for j in range(1, count - 1):
                 tiles[j] = jnp.where(first <= (e + j) * tokens, tiles[j], MASKED)
-            s = jnp.concatenate(tiles, axis=0)
-            top = jnp.max(s, axis=0, keepdims=True)
-            w = jnp.exp2((s - top) * (dim**-0.5 * LOG2E))
-            inv = 1.0 / jnp.sum(w, axis=0, keepdims=True)
-            store_tiles(p_ref, e, at, w * inv, diagonal)
+            top = folded(jnp.maximum, functools.reduce(jnp.maximum, tiles))
+            tiles = [jnp.exp2((tile - top) * (dim**-0.5 * LOG2E)) for tile in tiles]
+            inv = 1.0 / folded(jnp.add, functools.reduce(jnp.add, tiles))
+            store_tiles(p_ref, e, at, [tile * inv for tile in tiles], diagonal)
         keep = (2 * halo - e) * tokens
         dv = jnp.dot(p_ref[0, e, :keep], do, preferred_element_type=F32).reshape(2 * halo - e, tokens, dim)
         if e == 0:
@@ -208,13 +270,13 @@
         do = qd_ref[0, e, 1].reshape(group * tokens, dim)
         for at in range(0, group * tokens, pair):
             dp = lax.dot_general(v, do[at : at + pair], NT, preferred_element_type=F32)
-            last = (count - 1) * tokens
-            shared = jnp.where(diagonal, dp[last:], dp[:tokens])
-            dp = jnp.concatenate([shared, dp[tokens:last]], axis=0)
-            p = p_ref[0, e, :, at : at + pair]
-            p = jnp.concatenate([p[:tokens] + p[last:], p[tokens:last]], axis=0).astype(F32)
-            delta = jnp.sum(p * dp, axis=0, keepdims=True)
-            store_tiles(ds_ref, e, at, p * (dp - delta), diagonal)
+            dps = [dp[j * tokens : (j + 1) * tokens] for j in range(count)]
+            dps[0] = jnp.where(diagonal, dps.pop(), dps[0])
+            ps = [p_ref[0, e, j * tokens : (j + 1) * tokens, at : at + pair] for j in range(count)]
+            ps[0] += ps.pop()
+            ps = [p.astype(F32) for p in ps]
+            delta = folded(jnp.add, functools.reduce(jnp.add, [p * dp for p, dp in zip(ps, dps)]))
+            store_tiles(ds_ref, e, at, [p * (dp - delta) for p, dp in zip(ps, dps)], diagonal)
         keep = (2 * halo - e) * tokens
         dk = jnp.dot(ds_ref[0, e, :keep], q, preferred_element_type=F32).reshape(2 * halo - e, tokens, dim)
         if e == 0:
@@ -362,14 +424,14 @@
     place = jnp.stack([core, (device // 2 - halo) * (2 * tokens)]).astype(jnp.int32)
 
     far_first = range(halo, 0, -1)
-    k_own = pack(place, keys, swapped(keys, device_count), "pack_k")
-    k_own, queries, grad_out = lax.optimization_barrier((k_own, queries, grad_out))
-    qd = arrange(
-        place, queries, grad_out, swapped(queries, device_count), swapped(grad_out, device_count), key_heads
-    )
-    v_other = swapped(values, device_count)
-    qd, values, v_other = lax.optimization_barrier((qd, values, v_other))
-    v_own = pack(place, values, v_other, "pack_v")
+    k_other = swapped(keys, device_count)
+    k_mine, v_mine, q_mine, do_mine = fetch(place, keys, (values, queries, grad_out))
+    k_own = pack_other(place, k_other, k_mine)
+    k_own, q_mine, do_mine, v_mine = lax.optimization_barrier((k_own, q_mine, do_mine, v_mine))
+    q_other, do_other, v_other = (swapped(x, device_count) for x in (q_mine, do_mine, v_mine))
+    qd = arrange(place, in_vmem(q_mine), in_vmem(do_mine), q_other, do_other, key_heads)
+    qd, v_mine, v_other = lax.optimization_barrier((qd, v_mine, v_other))
+    v_own = pack_both(place, v_mine, v_other)
 
     def halo_of(own):
         received = {back: moved(own, device_count, 2 * back) for back in far_first}

time: 65.7 us -> 62.7 us (0.954)
  local copies, waits for them, and re-layouts: 2.45 us -> 0.01 us
  waiting for transfers between devices: 5.43 us -> 3.71 us
  starting transfers between devices: 30 us -> 30.8 us
    unnamed x6 -> x2, local copies, waits for them, and re-layouts: 2.45 us -> 0.01 us
    ppermute x7, waiting for transfers between devices: 1.31 us -> 0.02 us  [swapped(): return lax.ppermute(array, AXES, [(d, d ^ 1) for d in range(device_count)])]
    ppermute x7, starting transfers between devices: 7.09 us -> 7.89 us  [swapped(): return lax.ppermute(array, AXES, [(d, d ^ 1) for d in range(device_count)])]
    pallas_call x10 -> x11, Pallas kernels: 26.5 us -> 26.9 us  [call(): pl.pallas_call(kernel, out_shape=outs, grid_spec=pltpu.PrefetchScalarGrid...]
  transfers between devices with their start and end apart: 15 -> 15, of which waited for: 2 -> 1; matrix products, arithmetic and copies ran while one was open for 0% -> 0% of each run, Pallas kernels for 36% -> 40%
where the time goes in v7:
time: 62.7 us; the launch traced here: 62.4 us
  starting transfers between devices  30.8 us (49%)
  Pallas kernels  26.9 us (43%)
  waiting for transfers between devices  3.71 us (6%)
  between operations  0.85 us (1%)
    pallas_call x11, Pallas kernels, call(): pl.pallas_call(kernel, out_shape=outs, grid_spec=pltpu.PrefetchScalarGrid...  26.9 us
    ppermute x8, starting transfers between devices, moved(): return lax.ppermute(array, AXES, pairs)  22.9 us
    ppermute x7, starting transfers between devices, swapped(): return lax.ppermute(array, AXES, [(d, d ^ 1) for d in range(device_count)])  7.89 us
    ppermute x8, waiting for transfers between devices, moved(): return lax.ppermute(array, AXES, pairs)  3.69 us
  transfers between devices with their start and end apart: 15, of which 1 were waited for; matrix products, arithmetic and copies ran while one was open for 0% of the time, Pallas kernels for 40%

profile of v7, /device:TPU:23, one launch (start us, length us, event | category | flops | bytes accessed | tf_op | source)
XLA Modules:
  0.0 62.4 jit_solution(1985015326379445758)
XLA Ops:
  0.6 0.7 %collective-permute-start = (bf16[128,8,128]{2,1,0:T(8,128)(2,1)}, bf16[128,8,128]{2,1,0:T(8,128)(2,1)S(1)}, u32[]{:S(2)}, u32[]{:S(2)}) collective-permute-start(bf16[128,8,128]{2,1,0:T(8,128)(2,1)} %key_ref.1), channel_id=1, source_target_pairs={{0,1},{1,0},{2,3},{3,2},{4,5},{5,4},{6,7},{7,6},{8,9},{9,8},{10,11... | collective-permute-start | bytes 786440 | tf_op jit(solution)/shard_map/ppermute | solution.py:24
  1.4 0.1 pad_add_fusion.place_ref
  1.4 2.3 %fetch.1 = (bf16[4,2,128,128]{3,2,1,0:T(8,128)(2,1)S(1)}, bf16[128,8,128]{2,1,0:T(8,128)(2,1)S(1)}, bf16[128,32,128]{2,1,0:T(8,128)(2,1)S(1)}, bf16[128,32,128]{2,1,0:T(8,128)(2,1)S(1)}) custom-call(s32[2]{0:T(128)S(1)} %pad_add_fusion.place_ref, bf16[128,8,128]{2,1,0:T(8,128)(2,1)} %key_ref.1, bf16[128,8,128]{2,1,0:T(8,128)(2,1)} %refs_0_.1, ...), custom_call_target="tpu_custom_call" | custom-call | flops 1000000000 | tf_op jit(solution)/shard_map/fetch/pallas_call | solution.py:33
  3.7 0.0 collective-permute-done.other_ref
  3.7 0.6 pack_other.1.refs_0_
  4.4 0.0 copy-start
  4.4 0.1 collective-permute-start.1
  4.5 0.5 collective-permute-start.2
  5.0 0.1 collective-permute-start.3
  5.0 3.1 %collective-permute-start.5 = (bf16[4,2,128,128]{3,2,1,0:T(8,128)(2,1)S(1)}, bf16[4,2,128,128]{3,2,1,0:T(8,128)(2,1)S(1)}, u32[]{:S(2)}, u32[]{:S(2)}) collective-permute-start(bf16[4,2,128,128]{3,2,1,0:T(8,128)(2,1)S(1)} %pack_other.1.refs_0_), channel_id=1, source_target_pairs={{0,4},{1,5},{2,6},{3,7},{4,8},{5,9},{6,10},{7,11},{8,12},{9,13},{1... | collective-permute-start | bytes 786440 | tf_op jit(solution)/shard_map/ppermute | solution.py:20
  8.2 3.1 %collective-permute-start.4 = (bf16[4,2,128,128]{3,2,1,0:T(8,128)(2,1)S(1)}, bf16[4,2,128,128]{3,2,1,0:T(8,128)(2,1)S(1)}, u32[]{:S(2)}, u32[]{:S(2)}) collective-permute-start(bf16[4,2,128,128]{3,2,1,0:T(8,128)(2,1)S(1)} %pack_other.1.refs_0_), channel_id=1, source_target_pairs={{0,2},{1,3},{2,4},{3,5},{4,6},{5,7},{6,8},{7,9},{8,10},{9,11},{10,... | collective-permute-start | bytes 786440 | tf_op jit(solution)/shard_map/ppermute | solution.py:20
  11.3 0.0 collective-permute-done.1.q_other_ref
  11.3 2.5 %arrange.1.qd_ref = bf16[4,2,2,4,128,128]{5,4,3,2,1,0:T(8,128)(2,1)S(1)} custom-call(s32[2]{0:T(128)S(1)} %pad_add_fusion.place_ref, bf16[128,32,128]{2,1,0:T(8,128)(2,1)S(1)} %get-tuple-element.31.q_ref, bf16[128,32,128]{2,1,0:T(8,128)(2,1)S(1)} %get-tuple-element.32.do_ref, bf16[128,32,128]{2,1,0:T(8,128)(2,1)S(1)} %collective-permute-done.1.q_other_ref, ...), custom_call_target="tpu_custom_call" | custom-call | flops 1000000000 | tf_op jit(solution)/shard_map/arrange/pallas_call | solution.py:33
  13.8 0.0 collective-permute-done.3.other_ref
  13.9 0.7 %pack_both.1.refs_0_ = bf16[4,2,128,128]{3,2,1,0:T(8,128)(2,1)S(1)} custom-call(s32[2]{0:T(128)S(1)} %pad_add_fusion.place_ref, bf16[128,8,128]{2,1,0:T(8,128)(2,1)S(1)} %get-tuple-element.37.own_ref, bf16[128,8,128]{2,1,0:T(8,128)(2,1)S(1)} %collective-permute-done.3.other_ref), custom_call_target="tpu_custom_call" | custom-call | flops 1000000000 | tf_op jit(solution)/shard_map/pack_both/pallas_call | solution.py:33
  14.6 1.9 %collective-permute-start.7 = (bf16[4,2,128,128]{3,2,1,0:T(8,128)(2,1)S(1)}, bf16[4,2,128,128]{3,2,1,0:T(8,128)(2,1)S(1)}, u32[]{:S(2)}, u32[]{:S(2)}) collective-permute-start(bf16[4,2,128,128]{3,2,1,0:T(8,128)(2,1)S(1)} %pack_both.1.refs_0_), channel_id=1, source_target_pairs={{0,4},{1,5},{2,6},{3,7},{4,8},{5,9},{6,10},{7,11},{8,12},{9,13},{1... | collective-permute-start | bytes 786440 | tf_op jit(solution)/shard_map/ppermute | solution.py:20
  16.5 3.1 %collective-permute-start.6 = (bf16[4,2,128,128]{3,2,1,0:T(8,128)(2,1)S(1)}, bf16[4,2,128,128]{3,2,1,0:T(8,128)(2,1)S(1)}, u32[]{:S(2)}, u32[]{:S(2)}) collective-permute-start(bf16[4,2,128,128]{3,2,1,0:T(8,128)(2,1)S(1)} %pack_both.1.refs_0_), channel_id=1, source_target_pairs={{0,2},{1,3},{2,4},{3,5},{4,6},{5,7},{6,8},{7,9},{8,10},{9,11},{10,... | collective-permute-start | bytes 786440 | tf_op jit(solution)/shard_map/ppermute | solution.py:20
  19.7 6.5 %prob.1 = (bf16[4,2,640,512]{3,2,1,0:T(8,128)(2,1)S(1)}, bf16[4,2,128,128]{3,2,1,0:T(8,128)(2,1)S(1)}, bf16[4,2,128,128]{3,2,1,0:T(8,128)(2,1)S(1)}) custom-call(s32[2]{0:T(128)S(1)} %pad_add_fusion.place_ref, s32[16]{0:T(128)S(1)} %copy-done, bf16[4,2,2,4,128,128]{5,4,3,2,1,0:T(8,128)(2,1)S(1)} %arrange.1.qd_ref, ...), custom_call_target="tpu_custom_call" | custom-call | flops 2684354560 | tf_op jit(solution)/shard_map/prob/pallas_call | solution.py:33
  26.2 3.4 %collective-permute-start.8 = (bf16[4,2,128,128]{3,2,1,0:T(8,128)(2,1)S(1)}, bf16[4,2,128,128]{3,2,1,0:T(8,128)(2,1)S(1)}, u32[]{:S(2)}, u32[]{:S(2)}) collective-permute-start(bf16[4,2,128,128]{3,2,1,0:T(8,128)(2,1)S(1)} %get-tuple-element.40), channel_id=1, source_target_pairs={{4,0},{5,1},{6,2},{7,3},{8,4},{9,5},{10,6},{11,7},{12,8},{13,9},{1... | collective-permute-start | bytes 786440 | tf_op jit(solution)/shard_map/ppermute | solution.py:20
  29.5 4.3 %collective-permute-start.9 = (bf16[4,2,128,128]{3,2,1,0:T(8,128)(2,1)S(1)}, bf16[4,2,128,128]{3,2,1,0:T(8,128)(2,1)S(1)}, u32[]{:S(2)}, u32[]{:S(2)}) collective-permute-start(bf16[4,2,128,128]{3,2,1,0:T(8,128)(2,1)S(1)} %get-tuple-element.41), channel_id=1, source_target_pairs={{2,0},{3,1},{4,2},{5,3},{6,4},{7,5},{8,6},{9,7},{10,8},{11,9},{12,... | collective-permute-start | bytes 786440 | tf_op jit(solution)/shard_map/ppermute | solution.py:20
  33.9 6.0 %dscore.1 = (bf16[4,2,640,512]{3,2,1,0:T(8,128)(2,1)S(1)}, bf16[4,2,128,128]{3,2,1,0:T(8,128)(2,1)S(1)}, bf16[4,2,128,128]{3,2,1,0:T(8,128)(2,1)S(1)}) custom-call(s32[2]{0:T(128)S(1)} %pad_add_fusion.place_ref, bf16[4,2,2,4,128,128]{5,4,3,2,1,0:T(8,128)(2,1)S(1)} %arrange.1.qd_ref, bf16[4,2,640,512]{3,2,1,0:T(8,128)(2,1)S(1)} %get-tuple-element.36.p_ref, ...), custom_call_target="tpu_custom_call" | custom-call | flops 2684354560 | tf_op jit(solution)/shard_map/dscore/pallas_call | solution.py:33
  39.9 1.9 %collective-permute-start.11 = (bf16[4,2,128,128]{3,2,1,0:T(8,128)(2,1)S(1)}, bf16[4,2,128,128]{3,2,1,0:T(8,128)(2,1)S(1)}, u32[]{:S(2)}, u32[]{:S(2)}) collective-permute-start(bf16[4,2,128,128]{3,2,1,0:T(8,128)(2,1)S(1)} %get-tuple-element.45), channel_id=1, source_target_pairs={{4,0},{5,1},{6,2},{7,3},{8,4},{9,5},{10,6},{11,7},{12,8},{13,9},{1... | collective-permute-start | bytes 786440 | tf_op jit(solution)/shard_map/ppermute | solution.py:20
  41.9 2.0 %collective-permute-start.12 = (bf16[4,2,128,128]{3,2,1,0:T(8,128)(2,1)S(1)}, bf16[4,2,128,128]{3,2,1,0:T(8,128)(2,1)S(1)}, u32[]{:S(2)}, u32[]{:S(2)}) collective-permute-start(bf16[4,2,128,128]{3,2,1,0:T(8,128)(2,1)S(1)} %get-tuple-element.46), channel_id=1, source_target_pairs={{2,0},{3,1},{4,2},{5,3},{6,4},{7,5},{8,6},{9,7},{10,8},{11,9},{12,... | collective-permute-start | bytes 786440 | tf_op jit(solution)/shard_map/ppermute | solution.py:20
  43.9 3.3 %own.1 = (bf16[128,16,128]{2,1,0:T(8,128)(2,1)S(1)}, bf16[128,16,128]{2,1,0:T(8,128)(2,1)S(1)}, f32[4,2,128,128]{3,2,1,0:T(8,128)S(1)}, bf16[4,128,128]{2,1,0:T(8,128)(2,1)S(1)}, bf16[4,128,128]{2,1,0:T(8,128)(2,1)S(1)}) custom-call(s32[2]{0:T(128)S(1)} %pad_add_fusion.place_ref, bf16[4,2,2,4,128,128]{5,4,3,2,1,0:T(8,128)(2,1)S(1)} %arrange.1.qd_ref, ...), custom_call_target="tpu_custom_call" | custom-call | tf_op jit(solution)/shard_map/own/pallas_call | solution.py:33
  47.2 2.9 %collective-permute-start.14 = (bf16[4,128,128]{2,1,0:T(8,128)(2,1)S(1)}, bf16[4,128,128]{2,1,0:T(8,128)(2,1)S(1)}, u32[]{:S(2)}, u32[]{:S(2)}) collective-permute-start(bf16[4,128,128]{2,1,0:T(8,128)(2,1)S(1)} %get-tuple-element.50), channel_id=1, source_target_pairs={{0,1},{1,0},{2,3},{3,2},{4,5},{5,4},{6,7},{7,6},{8,9},{9,8},{10,11... | collective-permute-start | bytes 393224 | tf_op jit(solution)/shard_map/ppermute | solution.py:24
  50.1 0.1 collective-permute-start.10
  50.2 3.7 %collective-permute-done.12.refs_1_ = bf16[4,2,128,128]{3,2,1,0:T(8,128)(2,1)S(1)} collective-permute-done((bf16[4,2,128,128]{3,2,1,0:T(8,128)(2,1)S(1)}, bf16[4,2,128,128]{3,2,1,0:T(8,128)(2,1)S(1)}, u32[]{:S(2)}, u32[]{:S(2)}) %collective-permute-start.12) | collective-permute-done | bytes 262176 | tf_op jit(solution)/shard_map/ppermute | solution.py:20
  53.9 0.6 sum_dk.1
  54.5 3.5 %collective-permute-start.13 = (bf16[4,128,128]{2,1,0:T(8,128)(2,1)S(1)}, bf16[4,128,128]{2,1,0:T(8,128)(2,1)S(1)}, u32[]{:S(2)}, u32[]{:S(2)}) collective-permute-start(bf16[4,128,128]{2,1,0:T(8,128)(2,1)S(1)} %get-tuple-element.48), channel_id=1, source_target_pairs={{0,1},{1,0},{2,3},{3,2},{4,5},{5,4},{6,7},{7,6},{8,9},{9,8},{10,11... | collective-permute-start | bytes 393224 | tf_op jit(solution)/shard_map/ppermute | solution.py:24
  58.0 1.4 %merge_dv.1 = bf16[128,8,128]{2,1,0:T(8,128)(2,1)} custom-call(s32[2]{0:T(128)S(1)} %pad_add_fusion.place_ref, bf16[4,128,128]{2,1,0:T(8,128)(2,1)S(1)} %get-tuple-element.49.own_ref, bf16[4,128,128]{2,1,0:T(8,128)(2,1)S(1)} %collective-permute-done.14.other_ref), custom_call_target="tpu_custom_call" | custom-call | flops 4000000000 | tf_op jit(solution)/shard_map/merge_dv/pallas_call | solution.py:33
  59.4 1.4 %merge_dk.1 = bf16[128,8,128]{2,1,0:T(8,128)(2,1)} custom-call(s32[2]{0:T(128)S(1)} %pad_add_fusion.place_ref, bf16[4,128,128]{2,1,0:T(8,128)(2,1)S(1)} %get-tuple-element.47.own_ref, bf16[4,128,128]{2,1,0:T(8,128)(2,1)S(1)} %collective-permute-done.13.other_ref), custom_call_target="tpu_custom_call" | custom-call | flops 4000000000 | tf_op jit(solution)/shard_map/merge_dk/pallas_call | solution.py:33
  60.8 1.5 %join.1 = bf16[128,32,128]{2,1,0:T(8,128)(2,1)} custom-call(s32[2]{0:T(128)S(1)} %pad_add_fusion.place_ref, bf16[128,16,128]{2,1,0:T(8,128)(2,1)S(1)} %get-tuple-element.42.own_ref, bf16[128,16,128]{2,1,0:T(8,128)(2,1)S(1)} %collective-permute-done.10.other_ref), custom_call_target="tpu_custom_call" | custom-call | flops 1000000000 | tf_op jit(solution)/shard_map/join/pallas_call | solution.py:33
  (12 shorter events, 0.0 us)
Async XLA Ops:
  0.6 3.1 %collective-permute-start = (bf16[128,8,128]{2,1,0:T(8,128)(2,1)}, bf16[128,8,128]{2,1,0:T(8,128)(2,1)S(1)}, u32[]{:S(2)}, u32[]{:S(2)}) collective-permute-start(bf16[128,8,128]{2,1,0:T(8,128)(2,1)} %key_ref.1), channel_id=1, source_target_pairs={{0,1},{1,0},{2,3},{3,2},{4,5},{5,4},{6,7},{7,6},{8,9},{9,8},{10,11... | collective-permute-start | bytes 786440 | tf_op jit(solution)/shard_map/ppermute | solution.py:24
  4.4 15.3 %copy-start = (s32[16]{0:T(128)S(1)}, s32[16]{0:T(128)}, u32[]{:S(2)}) copy-start(s32[16]{0:T(128)} %lengths_ref.1) | copy-start | bytes 196
  4.4 6.9 %collective-permute-start.1 = (bf16[128,32,128]{2,1,0:T(8,128)(2,1)S(1)}, bf16[128,32,128]{2,1,0:T(8,128)(2,1)S(1)}, u32[]{:S(2)}, u32[]{:S(2)}) collective-permute-start(bf16[128,32,128]{2,1,0:T(8,128)(2,1)S(1)} %get-tuple-element.31.q_ref), channel_id=1, source_target_pairs={{0,1},{1,0},{2,3},{3,2},{4,5},{5,4},{6,7},{7,6},{8,9},{9,8},{10,11... | collective-permute-start | bytes 3145736 | tf_op jit(solution)/shard_map/ppermute | solution.py:24
  4.5 6.8 %collective-permute-start.2 = (bf16[128,32,128]{2,1,0:T(8,128)(2,1)S(1)}, bf16[128,32,128]{2,1,0:T(8,128)(2,1)S(1)}, u32[]{:S(2)}, u32[]{:S(2)}) collective-permute-start(bf16[128,32,128]{2,1,0:T(8,128)(2,1)S(1)} %get-tuple-element.32.do_ref), channel_id=1, source_target_pairs={{0,1},{1,0},{2,3},{3,2},{4,5},{5,4},{6,7},{7,6},{8,9},{9,8},{10,11... | collective-permute-start | bytes 3145736 | tf_op jit(solution)/shard_map/ppermute | solution.py:24
  5.0 8.9 %collective-permute-start.3 = (bf16[128,8,128]{2,1,0:T(8,128)(2,1)S(1)}, bf16[128,8,128]{2,1,0:T(8,128)(2,1)S(1)}, u32[]{:S(2)}, u32[]{:S(2)}) collective-permute-start(bf16[128,8,128]{2,1,0:T(8,128)(2,1)S(1)} %get-tuple-element.37.own_ref), channel_id=1, source_target_pairs={{0,1},{1,0},{2,3},{3,2},{4,5},{5,4},{6,7},{7,6},{8,9},{9,8},{10,11... | collective-permute-start | bytes 786440 | tf_op jit(solution)/shard_map/ppermute | solution.py:24
  5.0 14.6 %collective-permute-start.5 = (bf16[4,2,128,128]{3,2,1,0:T(8,128)(2,1)S(1)}, bf16[4,2,128,128]{3,2,1,0:T(8,128)(2,1)S(1)}, u32[]{:S(2)}, u32[]{:S(2)}) collective-permute-start(bf16[4,2,128,128]{3,2,1,0:T(8,128)(2,1)S(1)} %pack_other.1.refs_0_), channel_id=1, source_target_pairs={{0,4},{1,5},{2,6},{3,7},{4,8},{5,9},{6,10},{7,11},{8,12},{9,13},{1... | collective-permute-start | bytes 786440 | tf_op jit(solution)/shard_map/ppermute | solution.py:20
  8.2 11.5 %collective-permute-start.4 = (bf16[4,2,128,128]{3,2,1,0:T(8,128)(2,1)S(1)}, bf16[4,2,128,128]{3,2,1,0:T(8,128)(2,1)S(1)}, u32[]{:S(2)}, u32[]{:S(2)}) collective-permute-start(bf16[4,2,128,128]{3,2,1,0:T(8,128)(2,1)S(1)} %pack_other.1.refs_0_), channel_id=1, source_target_pairs={{0,2},{1,3},{2,4},{3,5},{4,6},{5,7},{6,8},{7,9},{8,10},{9,11},{10,... | collective-permute-start | bytes 786440 | tf_op jit(solution)/shard_map/ppermute | solution.py:20
  14.6 19.3 %collective-permute-start.7 = (bf16[4,2,128,128]{3,2,1,0:T(8,128)(2,1)S(1)}, bf16[4,2,128,128]{3,2,1,0:T(8,128)(2,1)S(1)}, u32[]{:S(2)}, u32[]{:S(2)}) collective-permute-start(bf16[4,2,128,128]{3,2,1,0:T(8,128)(2,1)S(1)} %pack_both.1.refs_0_), channel_id=1, source_target_pairs={{0,4},{1,5},{2,6},{3,7},{4,8},{5,9},{6,10},{7,11},{8,12},{9,13},{1... | collective-permute-start | bytes 786440 | tf_op jit(solution)/shard_map/ppermute | solution.py:20
  16.5 17.4 %collective-permute-start.6 = (bf16[4,2,128,128]{3,2,1,0:T(8,128)(2,1)S(1)}, bf16[4,2,128,128]{3,2,1,0:T(8,128)(2,1)S(1)}, u32[]{:S(2)}, u32[]{:S(2)}) collective-permute-start(bf16[4,2,128,128]{3,2,1,0:T(8,128)(2,1)S(1)} %pack_both.1.refs_0_), channel_id=1, source_target_pairs={{0,2},{1,3},{2,4},{3,5},{4,6},{5,7},{6,8},{7,9},{8,10},{9,11},{10,... | collective-permute-start | bytes 786440 | tf_op jit(solution)/shard_map/ppermute | solution.py:20
  26.2 17.7 %collective-permute-start.8 = (bf16[4,2,128,128]{3,2,1,0:T(8,128)(2,1)S(1)}, bf16[4,2,128,128]{3,2,1,0:T(8,128)(2,1)S(1)}, u32[]{:S(2)}, u32[]{:S(2)}) collective-permute-start(bf16[4,2,128,128]{3,2,1,0:T(8,128)(2,1)S(1)} %get-tuple-element.40), channel_id=1, source_target_pairs={{4,0},{5,1},{6,2},{7,3},{8,4},{9,5},{10,6},{11,7},{12,8},{13,9},{1... | collective-permute-start | bytes 786440 | tf_op jit(solution)/shard_map/ppermute | solution.py:20
  29.5 14.3 %collective-permute-start.9 = (bf16[4,2,128,128]{3,2,1,0:T(8,128)(2,1)S(1)}, bf16[4,2,128,128]{3,2,1,0:T(8,128)(2,1)S(1)}, u32[]{:S(2)}, u32[]{:S(2)}) collective-permute-start(bf16[4,2,128,128]{3,2,1,0:T(8,128)(2,1)S(1)} %get-tuple-element.41), channel_id=1, source_target_pairs={{2,0},{3,1},{4,2},{5,3},{6,4},{7,5},{8,6},{9,7},{10,8},{11,9},{12,... | collective-permute-start | bytes 786440 | tf_op jit(solution)/shard_map/ppermute | solution.py:20
  39.9 10.3 %collective-permute-start.11 = (bf16[4,2,128,128]{3,2,1,0:T(8,128)(2,1)S(1)}, bf16[4,2,128,128]{3,2,1,0:T(8,128)(2,1)S(1)}, u32[]{:S(2)}, u32[]{:S(2)}) collective-permute-start(bf16[4,2,128,128]{3,2,1,0:T(8,128)(2,1)S(1)} %get-tuple-element.45), channel_id=1, source_target_pairs={{4,0},{5,1},{6,2},{7,3},{8,4},{9,5},{10,6},{11,7},{12,8},{13,9},{1... | collective-permute-start | bytes 786440 | tf_op jit(solution)/shard_map/ppermute | solution.py:20
  41.9 12.0 %collective-permute-start.12 = (bf16[4,2,128,128]{3,2,1,0:T(8,128)(2,1)S(1)}, bf16[4,2,128,128]{3,2,1,0:T(8,128)(2,1)S(1)}, u32[]{:S(2)}, u32[]{:S(2)}) collective-permute-start(bf16[4,2,128,128]{3,2,1,0:T(8,128)(2,1)S(1)} %get-tuple-element.46), channel_id=1, source_target_pairs={{2,0},{3,1},{4,2},{5,3},{6,4},{7,5},{8,6},{9,7},{10,8},{11,9},{12,... | collective-permute-start | bytes 786440 | tf_op jit(solution)/shard_map/ppermute | solution.py:20
  47.2 10.8 %collective-permute-start.14 = (bf16[4,128,128]{2,1,0:T(8,128)(2,1)S(1)}, bf16[4,128,128]{2,1,0:T(8,128)(2,1)S(1)}, u32[]{:S(2)}, u32[]{:S(2)}) collective-permute-start(bf16[4,128,128]{2,1,0:T(8,128)(2,1)S(1)} %get-tuple-element.50), channel_id=1, source_target_pairs={{0,1},{1,0},{2,3},{3,2},{4,5},{5,4},{6,7},{7,6},{8,9},{9,8},{10,11... | collective-permute-start | bytes 393224 | tf_op jit(solution)/shard_map/ppermute | solution.py:24
  50.1 10.7 %collective-permute-start.10 = (bf16[128,16,128]{2,1,0:T(8,128)(2,1)S(1)}, bf16[128,16,128]{2,1,0:T(8,128)(2,1)S(1)}, u32[]{:S(2)}, u32[]{:S(2)}) collective-permute-start(bf16[128,16,128]{2,1,0:T(8,128)(2,1)S(1)} %get-tuple-element.43), channel_id=1, source_target_pairs={{0,1},{1,0},{2,3},{3,2},{4,5},{5,4},{6,7},{7,6},{8,9},{9,8},{10,11... | collective-permute-start | bytes 1572872 | tf_op jit(solution)/shard_map/ppermute | solution.py:24
  54.5 4.9 %collective-permute-start.13 = (bf16[4,128,128]{2,1,0:T(8,128)(2,1)S(1)}, bf16[4,128,128]{2,1,0:T(8,128)(2,1)S(1)}, u32[]{:S(2)}, u32[]{:S(2)}) collective-permute-start(bf16[4,128,128]{2,1,0:T(8,128)(2,1)S(1)} %get-tuple-element.48), channel_id=1, source_target_pairs={{0,1},{1,0},{2,3},{3,2},{4,5},{5,4},{6,7},{7,6},{8,9},{9,8},{10,11... | collective-permute-start | bytes 393224 | tf_op jit(solution)/shard_map/ppermute | solution.py:24

commit v8 on v7

--- a/solution.py
+++ b/solution.py
@@ -8,8 +8,8 @@
 from jax.sharding import PartitionSpec as P
 
 AXES = ("ctx", "uly")
-LOG2E = 1.4426950408889634
 MASKED = -1e30
+HEADS_AT_ONCE = 4
 BF16, F32 = jnp.bfloat16, jnp.float32
 NT = (((1,), (1,)), ((), ()))
 VMEM_BYTES = 16 * 2**20
@@ -26,6 +26,10 @@
 
 def in_vmem(array):
     return pltpu.with_memory_space_constraint(array, pltpu.VMEM)
+
+
+def in_hbm(array):
+    return pltpu.with_memory_space_constraint(array, pltpu.HBM)
 
 
 def call(kernel, name, grid, place, inputs, in_specs, outs, out_specs, scratch, flops, aliases={}):
@@ -109,7 +113,7 @@
         "fetch",
         (1,),
         place,
-        [pltpu.with_memory_space_constraint(x, pltpu.HBM) for x in (keys, *arrays)],
+        [in_hbm(x) for x in (keys, *arrays)],
         [pl.BlockSpec(memory_space=pltpu.HBM)] * (1 + len(arrays)),
         [pltpu.VMEM(out, BF16)] + [pltpu.VMEM(x.shape, x.dtype) for x in arrays],
         [pl.BlockSpec(memory_space=pltpu.VMEM)] * (1 + len(arrays)),
@@ -215,8 +219,8 @@
     k_scr, acc, firsts = refs[-3:]
     _, _, _, group, tokens, dim = qd_ref.shape
     count = 2 * halo + 1
-    pair = 2 * tokens
-    row, lane = on_diagonal(tokens, 2)
+    pair = HEADS_AT_ONCE * tokens
+    row, lane = on_diagonal(tokens, HEADS_AT_ONCE)
     diagonal = row <= lane
 
     @pl.when(pl.program_id(0) == 0)
@@ -240,7 +244,7 @@
             for j in range(1, count - 1):
                 tiles[j] = jnp.where(first <= (e + j) * tokens, tiles[j], MASKED)
             top = folded(jnp.maximum, functools.reduce(jnp.maximum, tiles))
-            tiles = [jnp.exp2((tile - top) * (dim**-0.5 * LOG2E)) for tile in tiles]
+            tiles = [jnp.exp((tile - top) * dim**-0.5) for tile in tiles]
             inv = 1.0 / folded(jnp.add, functools.reduce(jnp.add, tiles))
             store_tiles(p_ref, e, at, [tile * inv for tile in tiles], diagonal)
         keep = (2 * halo - e) * tokens
@@ -260,9 +264,9 @@
     v_scr, acc = refs[-2:]
     _, _, _, group, tokens, dim = qd_ref.shape
     count = 2 * halo + 1
-    pair = 2 * tokens
+    pair = HEADS_AT_ONCE * tokens
     window_of(v_refs, v_scr)
-    row, lane = on_diagonal(tokens, 2)
+    row, lane = on_diagonal(tokens, HEADS_AT_ONCE)
     diagonal = row <= lane
     for e in range(2):
         v = v_scr[pl.ds(e, count)].reshape(count * tokens, dim)
@@ -289,7 +293,7 @@
 
 def own_kernel(halo, place_ref, qd_ref, p_ref, ds_ref, *refs):
     k_refs, back_refs = refs[: halo + 1], refs[halo + 1 : 2 * halo + 1]
-    dq_ref, dq_other_ref, dk_ref, dv_ref, dv_other_ref, k_scr, dq_scr, dv_scr = refs[2 * halo + 1 :]
+    dq_ref, *dq_other_refs, dk_ref, dv_ref, dv_other_ref, k_scr, dq_scr, dv_scr = refs[2 * halo + 1 :]
     core, head = place_ref[0], pl.program_id(0)
     _, _, _, group, tokens, dim = qd_ref.shape
     rows = dq_ref.shape[1]
@@ -320,7 +324,11 @@
     @pl.when(head == pl.num_programs(0) - 1)
     def _():
         dq_ref[...] = dq_scr[core].astype(BF16).reshape(dq_ref.shape)
-        dq_other_ref[...] = dq_scr[1 - core].astype(BF16).reshape(dq_ref.shape)
+        at = 0
+        for ref in dq_other_refs:
+            part = ref.shape[0] * rows
+            ref[...] = dq_scr[1 - core, at : at + part].astype(BF16).reshape(ref.shape)
+            at += part
 
 
 def sum_kernel(place_ref, own_ref, *refs):
@@ -347,66 +355,53 @@
         [jax.ShapeDtypeStruct(one, BF16)] * 2,
         [pl.BlockSpec(one, lambda i, place: (0, 0, 0))] * 2,
         [],
-        10**8,
-    )
-
-
-def join_kernel(place_ref, own_ref, other_ref, out_ref, sems):
+        0,
+    )
+
+
+def finish_kernel(parts, place_ref, *refs):
+    dq, others, (dk, dk_other, dv, dv_other) = refs[0], refs[1 : 1 + parts], refs[1 + parts : 5 + parts]
+    dq_out, dk_out, dv_out, scr, sems = refs[5 + parts :]
     core = place_ref[0]
-    half = own_ref.shape[1]
-    copies = []
-    for which, ref in enumerate([own_ref, other_ref]):
-        side = 1 - core if which else core
-        at = pl.multiple_of(side * half, half)
-        copies.append(pltpu.make_async_copy(ref, out_ref.at[:, pl.ds(at, half)], sems.at[which]))
-        copies[-1].start()
+    rows, heads, dim = dk_out.shape
+    half, q_half = heads // 2, dq.shape[1]
+    at = pl.multiple_of(core * q_half, q_half)
+    copies = [pltpu.make_async_copy(dq, dq_out.at[:, pl.ds(at, q_half)], sems.at[0])]
+    at = pl.multiple_of((1 - core) * q_half, q_half)
+    first = 0
+    for i, part in enumerate(others):
+        to = dq_out.at[pl.ds(first, part.shape[0]), pl.ds(at, q_half)]
+        copies.append(pltpu.make_async_copy(part, to, sems.at[1 + i]))
+        first += part.shape[0]
+    for copy in copies:
+        copy.start()
+    for n, (own, other, out) in enumerate([(dk, dk_other, dk_out), (dv, dv_other, dv_out)]):
+        for which, ref in enumerate([own, other]):
+            side = 1 - core if which else core
+            for h in range(half):
+                scr[n, pl.ds(side * half + h, rows, stride=heads), :] = ref[h].astype(F32)
+        out[...] = scr[n].astype(BF16).reshape(rows, heads, dim)
     for copy in copies:
         copy.wait()
 
 
-def join(place, own, other):
-    tokens, half, dim = own.shape
+def finish(place, dq, dq_others, dk, dk_other, dv, dv_other):
+    half, tokens, dim = dk.shape
     anywhere = pl.BlockSpec(memory_space=pl.ANY)
+    in_spec = pl.BlockSpec(dk.shape, lambda i, place: (0, 0, 0))
+    out = (tokens, 2 * half, dim)
+    parts = len(dq_others)
     return call(
-        join_kernel,
-        "join",
+        functools.partial(finish_kernel, parts),
+        "finish",
         (1,),
         place,
-        (own, other),
-        [anywhere] * 2,
-        jax.ShapeDtypeStruct((tokens, 2 * half, dim), BF16),
-        anywhere,
-        [pltpu.SemaphoreType.DMA((2,))],
-        10**9,
-    )
-
-
-def merge_kernel(place_ref, own_ref, other_ref, out_ref, scr):
-    core = place_ref[0]
-    rows, heads, dim = out_ref.shape
-    half = heads // 2
-    for which, ref in enumerate([own_ref, other_ref]):
-        side = 1 - core if which else core
-        for h in range(half):
-            scr[pl.ds(side * half + h, rows, stride=heads), :] = ref[h].astype(F32)
-    out_ref[...] = scr[...].astype(BF16).reshape(rows, heads, dim)
-
-
-def merge(place, own, other, name):
-    half, tokens, dim = own.shape
-    spec = pl.BlockSpec(own.shape, lambda i, place: (0, 0, 0))
-    out = (tokens, 2 * half, dim)
-    return call(
-        merge_kernel,
-        name,
-        (1,),
-        place,
-        (own, other),
-        [spec] * 2,
-        jax.ShapeDtypeStruct(out, BF16),
-        pl.BlockSpec(out, lambda i, place: (0, 0, 0)),
-        [pltpu.VMEM((tokens * 2 * half, dim), F32)],
-        4 * 10**9,
+        (dq, *dq_others, dk, dk_other, dv, dv_other),
+        [anywhere] * (1 + parts) + [in_spec] * 4,
+        [jax.ShapeDtypeStruct((tokens, 2 * dq.shape[1], dim), BF16)] + [jax.ShapeDtypeStruct(out, BF16)] * 2,
+        [anywhere] + [pl.BlockSpec(out, lambda i, place: (0, 0, 0))] * 2,
+        [pltpu.VMEM((2, tokens * 2 * half, dim), F32), pltpu.SemaphoreType.DMA((1 + parts,))],
+        0,
     )
 
 
@@ -425,11 +420,11 @@
 
     far_first = range(halo, 0, -1)
     k_other = swapped(keys, device_count)
-    k_mine, v_mine, q_mine, do_mine = fetch(place, keys, (values, queries, grad_out))
+    k_mine, v_mine = fetch(place, keys, (values,))
     k_own = pack_other(place, k_other, k_mine)
-    k_own, q_mine, do_mine, v_mine = lax.optimization_barrier((k_own, q_mine, do_mine, v_mine))
-    q_other, do_other, v_other = (swapped(x, device_count) for x in (q_mine, do_mine, v_mine))
-    qd = arrange(place, in_vmem(q_mine), in_vmem(do_mine), q_other, do_other, key_heads)
+    k_own, queries, grad_out, v_mine = lax.optimization_barrier((k_own, queries, grad_out, v_mine))
+    q_other, do_other, v_other = (swapped(x, device_count) for x in (queries, grad_out, v_mine))
+    qd = arrange(place, in_hbm(queries), in_hbm(grad_out), q_other, do_other, key_heads)
     qd, v_mine, v_other = lax.optimization_barrier((qd, v_mine, v_other))
     v_own = pack_both(place, v_mine, v_other)
 
@@ -452,6 +447,8 @@
     one_shape = jax.ShapeDtypeStruct((half, tokens, dim), BF16)
     dq_shape = jax.ShapeDtypeStruct((tokens, heads // 2, dim), BF16)
     dq_spec = pl.BlockSpec(dq_shape.shape, lambda h, *_: (0, 0, 0))
+    dq_part_shape = jax.ShapeDtypeStruct((tokens // 2, heads // 2, dim), BF16)
+    dq_part_spec = pl.BlockSpec(dq_part_shape.shape, lambda h, *_: (0, 0, 0))
     run = pltpu.VMEM((window, tokens, dim), BF16)
     acc = pltpu.VMEM((2 * halo, tokens, dim), F32)
     product = 2 * half * 2 * count * tokens * group * tokens * dim
@@ -467,7 +464,7 @@
         [qd_spec] + [pair_spec] * (halo + 1),
         [p_shape] + [jax.ShapeDtypeStruct(pair, BF16)] * halo,
         [p_spec] + [pair_spec] * halo,
-        [run, acc, pltpu.VMEM((2, 1, 2 * tokens), jnp.int32)],
+        [run, acc, pltpu.VMEM((2, 1, HEADS_AT_ONCE * tokens), jnp.int32)],
         4 * product,
     )
     dv_back = sent_back(dv_halo)
@@ -484,15 +481,15 @@
         4 * product,
     )
     dk_back = sent_back(dk_halo)
-    dq, dq_other, dk_own, dv, dv_other = call(
+    dq, *dq_others, dk_own, dv, dv_other = call(
         functools.partial(own_kernel, halo),
         "own",
         (half,),
         place,
         (in_vmem(qd), in_vmem(prob), in_vmem(dscore), *k_pairs, *dv_back),
         [qd_spec, p_spec, p_spec] + [pair_spec] * (2 * halo + 1),
-        [dq_shape] * 2 + [jax.ShapeDtypeStruct(pair, F32)] + [one_shape] * 2,
-        [dq_spec] * 2 + [pair_spec] + [one_spec] * 2,
+        [dq_shape] + [dq_part_shape] * 2 + [jax.ShapeDtypeStruct(pair, F32)] + [one_shape] * 2,
+        [dq_spec] + [dq_part_spec] * 2 + [pair_spec] + [one_spec] * 2,
         [
             run,
             pltpu.VMEM((2, tokens * heads // 2, dim), F32),
@@ -500,13 +497,10 @@
         ],
         0,
     )
-    dq_other = swapped(dq_other, device_count)
+    dq_others = [swapped(part, device_count) for part in dq_others]
     dv_other = swapped(dv_other, device_count)
     dk, dk_other = summed(place, dk_own, dk_back)
-    grad_queries = join(place, dq, dq_other)
-    grad_values = merge(place, dv, dv_other, "merge_dv")
-    grad_keys = merge(place, dk, swapped(dk_other, device_count), "merge_dk")
-    return grad_queries, grad_keys, grad_values
+    return tuple(finish(place, dq, dq_others, dk, swapped(dk_other, device_count), dv, dv_other))
 
 
 def solution(mesh):

time: 62.7 us -> 62.2 us (level)
  Pallas kernels: 26.9 us -> 26 us
    ppermute x7 -> x8, waiting for transfers between devices: 0.02 us -> 0.99 us  [swapped(): return lax.ppermute(array, AXES, [(d, d ^ 1) for d in range(device_count)])]
    pallas_call x11 -> x9, Pallas kernels: 26.9 us -> 26 us  [call(): pl.pallas_call(kernel, out_shape=outs, grid_spec=pltpu.PrefetchScalarGrid...]
    ppermute x7 -> x8, starting transfers between devices: 7.89 us -> 7.72 us  [swapped(): return lax.ppermute(array, AXES, [(d, d ^ 1) for d in range(device_count)])]
  transfers between devices with their start and end apart: 15 -> 16, of which waited for: 1 -> 2; matrix products, arithmetic and copies ran while one was open for 0% -> 0% of each run, Pallas kernels for 40% -> 37%
where the time goes in v8:
time: 62.2 us; the launch traced here: 61.8 us
  starting transfers between devices  30.7 us (49%)
  Pallas kernels  26 us (42%)
  waiting for transfers between devices  4.18 us (7%)
  between operations  0.88 us (1%)
    pallas_call x9, Pallas kernels, call(): pl.pallas_call(kernel, out_shape=outs, grid_spec=pltpu.PrefetchScalarGrid...  26 us
    ppermute x8, starting transfers between devices, moved(): return lax.ppermute(array, AXES, pairs)  22.9 us
    ppermute x8, starting transfers between devices, swapped(): return lax.ppermute(array, AXES, [(d, d ^ 1) for d in range(device_count)])  7.72 us
    ppermute x8, waiting for transfers between devices, moved(): return lax.ppermute(array, AXES, pairs)  3.19 us
  transfers between devices with their start and end apart: 16, of which 2 were waited for; matrix products, arithmetic and copies ran while one was open for 0% of the time, Pallas kernels for 37%

profile of v8, /device:TPU:23, one launch (start us, length us, event | category | flops | bytes accessed | tf_op | source)
XLA Modules:
  0.0 61.8 jit_solution(11958119794494254412)
XLA Ops:
  0.6 0.0 copy-start.2
  0.6 0.0 copy-start.1
  0.7 0.7 %collective-permute-start = (bf16[128,8,128]{2,1,0:T(8,128)(2,1)}, bf16[128,8,128]{2,1,0:T(8,128)(2,1)S(1)}, u32[]{:S(2)}, u32[]{:S(2)}) collective-permute-start(bf16[128,8,128]{2,1,0:T(8,128)(2,1)} %key_ref.1), channel_id=1, source_target_pairs={{0,1},{1,0},{2,3},{3,2},{4,5},{5,4},{6,7},{7,6},{8,9},{9,8},{10,11... | collective-permute-start | bytes 786440 | tf_op jit(solution)/shard_map/ppermute | solution.py:24
  1.4 0.1 pad_add_fusion.place_ref
  1.5 1.6 %fetch.1 = (bf16[4,2,128,128]{3,2,1,0:T(8,128)(2,1)S(1)}, bf16[128,8,128]{2,1,0:T(8,128)(2,1)S(1)}) custom-call(s32[2]{0:T(128)S(1)} %pad_add_fusion.place_ref, bf16[128,8,128]{2,1,0:T(8,128)(2,1)} %key_ref.1, bf16[128,8,128]{2,1,0:T(8,128)(2,1)} %refs_0_.1), custom_call_target="tpu_custom_call" | custom-call | flops 1000000000 | tf_op jit(solution)/shard_map/fetch/pallas_call | solution.py:37
  3.1 0.6 %pack_other.1.refs_0_ = bf16[4,2,128,128]{3,2,1,0:T(8,128)(2,1)S(1)} custom-call(s32[2]{0:T(128)S(1)} %pad_add_fusion.place_ref, bf16[128,8,128]{2,1,0:T(8,128)(2,1)S(1)} %collective-permute-done.other_ref, bf16[4,2,128,128]{3,2,1,0:T(8,128)(2,1)S(1)} %get-tuple-element.26._), custom_call_target="tpu_custom_call", output_to_operand_aliasing={{}: (2, {})} | custom-call | flops 1000000000 | tf_op jit(solution)/shard_map/pack_other/pallas_call | solution.py:37
  3.7 0.0 copy-start
  3.7 0.1 collective-permute-start.1
  3.9 0.4 collective-permute-start.2
  4.3 0.1 collective-permute-start.3
  4.4 3.1 %collective-permute-start.5 = (bf16[4,2,128,128]{3,2,1,0:T(8,128)(2,1)S(1)}, bf16[4,2,128,128]{3,2,1,0:T(8,128)(2,1)S(1)}, u32[]{:S(2)}, u32[]{:S(2)}) collective-permute-start(bf16[4,2,128,128]{3,2,1,0:T(8,128)(2,1)S(1)} %pack_other.1.refs_0_), channel_id=1, source_target_pairs={{0,4},{1,5},{2,6},{3,7},{4,8},{5,9},{6,10},{7,11},{8,12},{9,13},{1... | collective-permute-start | bytes 786440 | tf_op jit(solution)/shard_map/ppermute | solution.py:20
  7.5 3.1 %collective-permute-start.4 = (bf16[4,2,128,128]{3,2,1,0:T(8,128)(2,1)S(1)}, bf16[4,2,128,128]{3,2,1,0:T(8,128)(2,1)S(1)}, u32[]{:S(2)}, u32[]{:S(2)}) collective-permute-start(bf16[4,2,128,128]{3,2,1,0:T(8,128)(2,1)S(1)} %pack_other.1.refs_0_), channel_id=1, source_target_pairs={{0,2},{1,3},{2,4},{3,5},{4,6},{5,7},{6,8},{7,9},{8,10},{9,11},{10,... | collective-permute-start | bytes 786440 | tf_op jit(solution)/shard_map/ppermute | solution.py:20
  10.7 0.0 collective-permute-done.1.q_other_ref
  10.7 3.9 %arrange.1.qd_ref = bf16[4,2,2,4,128,128]{5,4,3,2,1,0:T(8,128)(2,1)S(1)} custom-call(s32[2]{0:T(128)S(1)} %pad_add_fusion.place_ref, bf16[128,32,128]{2,1,0:T(8,128)(2,1)} %q_ref, bf16[128,32,128]{2,1,0:T(8,128)(2,1)} %do_ref, bf16[128,32,128]{2,1,0:T(8,128)(2,1)S(1)} %collective-permute-done.1.q_other_ref, ...), custom_call_target="tpu_custom_call" | custom-call | flops 1000000000 | tf_op jit(solution)/shard_map/arrange/pallas_call | solution.py:37
  14.6 0.7 %pack_both.1.refs_0_ = bf16[4,2,128,128]{3,2,1,0:T(8,128)(2,1)S(1)} custom-call(s32[2]{0:T(128)S(1)} %pad_add_fusion.place_ref, bf16[128,8,128]{2,1,0:T(8,128)(2,1)S(1)} %get-tuple-element.34.own_ref, bf16[128,8,128]{2,1,0:T(8,128)(2,1)S(1)} %collective-permute-done.3.other_ref), custom_call_target="tpu_custom_call" | custom-call | flops 1000000000 | tf_op jit(solution)/shard_map/pack_both/pallas_call | solution.py:37
  15.3 1.9 %collective-permute-start.7 = (bf16[4,2,128,128]{3,2,1,0:T(8,128)(2,1)S(1)}, bf16[4,2,128,128]{3,2,1,0:T(8,128)(2,1)S(1)}, u32[]{:S(2)}, u32[]{:S(2)}) collective-permute-start(bf16[4,2,128,128]{3,2,1,0:T(8,128)(2,1)S(1)} %pack_both.1.refs_0_), channel_id=1, source_target_pairs={{0,4},{1,5},{2,6},{3,7},{4,8},{5,9},{6,10},{7,11},{8,12},{9,13},{1... | collective-permute-start | bytes 786440 | tf_op jit(solution)/shard_map/ppermute | solution.py:20
  17.2 3.1 %collective-permute-start.6 = (bf16[4,2,128,128]{3,2,1,0:T(8,128)(2,1)S(1)}, bf16[4,2,128,128]{3,2,1,0:T(8,128)(2,1)S(1)}, u32[]{:S(2)}, u32[]{:S(2)}) collective-permute-start(bf16[4,2,128,128]{3,2,1,0:T(8,128)(2,1)S(1)} %pack_both.1.refs_0_), channel_id=1, source_target_pairs={{0,2},{1,3},{2,4},{3,5},{4,6},{5,7},{6,8},{7,9},{8,10},{9,11},{10,... | collective-permute-start | bytes 786440 | tf_op jit(solution)/shard_map/ppermute | solution.py:20
  20.4 6.9 %prob.1 = (bf16[4,2,640,512]{3,2,1,0:T(8,128)(2,1)S(1)}, bf16[4,2,128,128]{3,2,1,0:T(8,128)(2,1)S(1)}, bf16[4,2,128,128]{3,2,1,0:T(8,128)(2,1)S(1)}) custom-call(s32[2]{0:T(128)S(1)} %pad_add_fusion.place_ref, s32[16]{0:T(128)S(1)} %copy-done, bf16[4,2,2,4,128,128]{5,4,3,2,1,0:T(8,128)(2,1)S(1)} %arrange.1.qd_ref, ...), custom_call_target="tpu_custom_call" | custom-call | flops 2684354560 | tf_op jit(solution)/shard_map/prob/pallas_call | solution.py:37
  27.3 3.4 %collective-permute-start.8 = (bf16[4,2,128,128]{3,2,1,0:T(8,128)(2,1)S(1)}, bf16[4,2,128,128]{3,2,1,0:T(8,128)(2,1)S(1)}, u32[]{:S(2)}, u32[]{:S(2)}) collective-permute-start(bf16[4,2,128,128]{3,2,1,0:T(8,128)(2,1)S(1)} %get-tuple-element.37), channel_id=1, source_target_pairs={{4,0},{5,1},{6,2},{7,3},{8,4},{9,5},{10,6},{11,7},{12,8},{13,9},{1... | collective-permute-start | bytes 786440 | tf_op jit(solution)/shard_map/ppermute | solution.py:20
  30.7 2.2 %collective-permute-start.9 = (bf16[4,2,128,128]{3,2,1,0:T(8,128)(2,1)S(1)}, bf16[4,2,128,128]{3,2,1,0:T(8,128)(2,1)S(1)}, u32[]{:S(2)}, u32[]{:S(2)}) collective-permute-start(bf16[4,2,128,128]{3,2,1,0:T(8,128)(2,1)S(1)} %get-tuple-element.38), channel_id=1, source_target_pairs={{2,0},{3,1},{4,2},{5,3},{6,4},{7,5},{8,6},{9,7},{10,8},{11,9},{12,... | collective-permute-start | bytes 786440 | tf_op jit(solution)/shard_map/ppermute | solution.py:20
  32.9 6.0 %dscore.1 = (bf16[4,2,640,512]{3,2,1,0:T(8,128)(2,1)S(1)}, bf16[4,2,128,128]{3,2,1,0:T(8,128)(2,1)S(1)}, bf16[4,2,128,128]{3,2,1,0:T(8,128)(2,1)S(1)}) custom-call(s32[2]{0:T(128)S(1)} %pad_add_fusion.place_ref, bf16[4,2,2,4,128,128]{5,4,3,2,1,0:T(8,128)(2,1)S(1)} %arrange.1.qd_ref, bf16[4,2,640,512]{3,2,1,0:T(8,128)(2,1)S(1)} %get-tuple-element.33.p_ref, ...), custom_call_target="tpu_custom_call" | custom-call | flops 2684354560 | tf_op jit(solution)/shard_map/dscore/pallas_call | solution.py:37
  38.9 3.0 %collective-permute-start.12 = (bf16[4,2,128,128]{3,2,1,0:T(8,128)(2,1)S(1)}, bf16[4,2,128,128]{3,2,1,0:T(8,128)(2,1)S(1)}, u32[]{:S(2)}, u32[]{:S(2)}) collective-permute-start(bf16[4,2,128,128]{3,2,1,0:T(8,128)(2,1)S(1)} %get-tuple-element.43), channel_id=1, source_target_pairs={{4,0},{5,1},{6,2},{7,3},{8,4},{9,5},{10,6},{11,7},{12,8},{13,9},{1... | collective-permute-start | bytes 786440 | tf_op jit(solution)/shard_map/ppermute | solution.py:20
  42.0 3.1 %collective-permute-start.13 = (bf16[4,2,128,128]{3,2,1,0:T(8,128)(2,1)S(1)}, bf16[4,2,128,128]{3,2,1,0:T(8,128)(2,1)S(1)}, u32[]{:S(2)}, u32[]{:S(2)}) collective-permute-start(bf16[4,2,128,128]{3,2,1,0:T(8,128)(2,1)S(1)} %get-tuple-element.44), channel_id=1, source_target_pairs={{2,0},{3,1},{4,2},{5,3},{6,4},{7,5},{8,6},{9,7},{10,8},{11,9},{12,... | collective-permute-start | bytes 786440 | tf_op jit(solution)/shard_map/ppermute | solution.py:20
  45.1 3.3 %own.1 = (bf16[128,16,128]{2,1,0:T(8,128)(2,1)S(1)}, bf16[64,16,128]{2,1,0:T(8,128)(2,1)S(1)}, bf16[64,16,128]{2,1,0:T(8,128)(2,1)S(1)}, f32[4,2,128,128]{3,2,1,...) custom-call(s32[2]{0:T(128)S(1)} %pad_add_fusion.place_ref, ...), custom_call_target="tpu_custom_call" | custom-call | tf_op jit(solution)/shard_map/own/pallas_call | solution.py:37
  48.4 2.7 %collective-permute-start.10 = (bf16[64,16,128]{2,1,0:T(8,128)(2,1)S(1)}, bf16[64,16,128]{2,1,0:T(8,128)(2,1)S(1)}, u32[]{:S(2)}, u32[]{:S(2)}) collective-permute-start(bf16[64,16,128]{2,1,0:T(8,128)(2,1)S(1)} %get-tuple-element.40), channel_id=1, source_target_pairs={{0,1},{1,0},{2,3},{3,2},{4,5},{5,4},{6,7},{7,6},{8,9},{9,8},{10,11... | collective-permute-start | bytes 786440 | tf_op jit(solution)/shard_map/ppermute | solution.py:24
  51.1 0.1 collective-permute-start.11
  51.2 0.4 collective-permute-start.15
  51.7 3.2 %collective-permute-done.13.refs_1_ = bf16[4,2,128,128]{3,2,1,0:T(8,128)(2,1)S(1)} collective-permute-done((bf16[4,2,128,128]{3,2,1,0:T(8,128)(2,1)S(1)}, bf16[4,2,128,128]{3,2,1,0:T(8,128)(2,1)S(1)}, u32[]{:S(2)}, u32[]{:S(2)}) %collective-permute-start.13) | collective-permute-done | bytes 262176 | tf_op jit(solution)/shard_map/ppermute | solution.py:20
  54.8 0.6 %sum_dk.1 = (bf16[4,128,128]{2,1,0:T(8,128)(2,1)S(1)}, bf16[4,128,128]{2,1,0:T(8,128)(2,1)S(1)}) custom-call(s32[2]{0:T(128)S(1)} %pad_add_fusion.place_ref, f32[4,2,128,128]{3,2,1,0:T(8,128)S(1)} %get-tuple-element.42.own_ref, bf16[4,2,128,128]{3,2,1,0:T(8,128)(2,1)S(1)} %collective-permute-done.12.refs_0_, ...), custom_call_target="tpu_custom_call" | custom-call | tf_op jit(solution)/shard_map/sum_dk/pallas_call | solution.py:37
  55.5 3.1 %collective-permute-start.14 = (bf16[4,128,128]{2,1,0:T(8,128)(2,1)S(1)}, bf16[4,128,128]{2,1,0:T(8,128)(2,1)S(1)}, u32[]{:S(2)}, u32[]{:S(2)}) collective-permute-start(bf16[4,128,128]{2,1,0:T(8,128)(2,1)S(1)} %get-tuple-element.46), channel_id=1, source_target_pairs={{0,1},{1,0},{2,3},{3,2},{4,5},{5,4},{6,7},{7,6},{8,9},{9,8},{10,11... | collective-permute-start | bytes 393224 | tf_op jit(solution)/shard_map/ppermute | solution.py:24
  58.6 1.0 %collective-permute-done.14.refs_4_ = bf16[4,128,128]{2,1,0:T(8,128)(2,1)S(1)} collective-permute-done((bf16[4,128,128]{2,1,0:T(8,128)(2,1)S(1)}, bf16[4,128,128]{2,1,0:T(8,128)(2,1)S(1)}, u32[]{:S(2)}, u32[]{:S(2)}) %collective-permute-start.14) | collective-permute-done | bytes 131104 | tf_op jit(solution)/shard_map/ppermute | solution.py:24
  59.5 2.3 %finish.1 = (bf16[128,32,128]{2,1,0:T(8,128)(2,1)}, bf16[128,8,128]{2,1,0:T(8,128)(2,1)}, bf16[128,8,128]{2,1,0:T(8,128)(2,1)}) custom-call(s32[2]{0:T(128)S(1)} %pad_add_fusion.place_ref, bf16[128,16,128]{2,1,0:T(8,128)(2,1)S(1)} %get-tuple-element.39.refs_0_, bf16[64,16,128]{2,1,0:T(8,128)(2,1)S(1)} %collective-permute-done.10.refs_1_, ...), custom_call_target="tpu_custom_call" | custom-call | tf_op jit(solution)/shard_map/finish/pallas_call | solution.py:37
  (16 shorter events, 0.0 us)
Async XLA Ops:
  0.6 3.2 %copy-start.2 = (bf16[128,32,128]{2,1,0:T(8,128)(2,1)S(1)}, bf16[128,32,128]{2,1,0:T(8,128)(2,1)}, u32[]{:S(2)}) copy-start(bf16[128,32,128]{2,1,0:T(8,128)(2,1)} %do_ref) | copy-start | bytes 3145732
  0.6 3.1 %copy-start.1 = (bf16[128,32,128]{2,1,0:T(8,128)(2,1)S(1)}, bf16[128,32,128]{2,1,0:T(8,128)(2,1)}, u32[]{:S(2)}) copy-start(bf16[128,32,128]{2,1,0:T(8,128)(2,1)} %q_ref) | copy-start | bytes 3145732
  0.7 2.4 %collective-permute-start = (bf16[128,8,128]{2,1,0:T(8,128)(2,1)}, bf16[128,8,128]{2,1,0:T(8,128)(2,1)S(1)}, u32[]{:S(2)}, u32[]{:S(2)}) collective-permute-start(bf16[128,8,128]{2,1,0:T(8,128)(2,1)} %key_ref.1), channel_id=1, source_target_pairs={{0,1},{1,0},{2,3},{3,2},{4,5},{5,4},{6,7},{7,6},{8,9},{9,8},{10,11... | collective-permute-start | bytes 786440 | tf_op jit(solution)/shard_map/ppermute | solution.py:24
  3.7 16.7 %copy-start = (s32[16]{0:T(128)S(1)}, s32[16]{0:T(128)}, u32[]{:S(2)}) copy-start(s32[16]{0:T(128)} %lengths_ref.1) | copy-start | bytes 196
  3.7 6.9 %collective-permute-start.1 = (bf16[128,32,128]{2,1,0:T(8,128)(2,1)S(1)}, bf16[128,32,128]{2,1,0:T(8,128)(2,1)S(1)}, u32[]{:S(2)}, u32[]{:S(2)}) collective-permute-start(bf16[128,32,128]{2,1,0:T(8,128)(2,1)S(1)} %copy-done.1), channel_id=1, source_target_pairs={{0,1},{1,0},{2,3},{3,2},{4,5},{5,4},{6,7},{7,6},{8,9},{9,8},{10,11... | collective-permute-start | bytes 3145736 | tf_op jit(solution)/shard_map/ppermute | solution.py:24
  3.9 6.8 %collective-permute-start.2 = (bf16[128,32,128]{2,1,0:T(8,128)(2,1)S(1)}, bf16[128,32,128]{2,1,0:T(8,128)(2,1)S(1)}, u32[]{:S(2)}, u32[]{:S(2)}) collective-permute-start(bf16[128,32,128]{2,1,0:T(8,128)(2,1)S(1)} %copy-done.2), channel_id=1, source_target_pairs={{0,1},{1,0},{2,3},{3,2},{4,5},{5,4},{6,7},{7,6},{8,9},{9,8},{10,11... | collective-permute-start | bytes 3145736 | tf_op jit(solution)/shard_map/ppermute | solution.py:24
  4.3 10.3 %collective-permute-start.3 = (bf16[128,8,128]{2,1,0:T(8,128)(2,1)S(1)}, bf16[128,8,128]{2,1,0:T(8,128)(2,1)S(1)}, u32[]{:S(2)}, u32[]{:S(2)}) collective-permute-start(bf16[128,8,128]{2,1,0:T(8,128)(2,1)S(1)} %get-tuple-element.34.own_ref), channel_id=1, source_target_pairs={{0,1},{1,0},{2,3},{3,2},{4,5},{5,4},{6,7},{7,6},{8,9},{9,8},{10,11... | collective-permute-start | bytes 786440 | tf_op jit(solution)/shard_map/ppermute | solution.py:24
  4.4 16.0 %collective-permute-start.5 = (bf16[4,2,128,128]{3,2,1,0:T(8,128)(2,1)S(1)}, bf16[4,2,128,128]{3,2,1,0:T(8,128)(2,1)S(1)}, u32[]{:S(2)}, u32[]{:S(2)}) collective-permute-start(bf16[4,2,128,128]{3,2,1,0:T(8,128)(2,1)S(1)} %pack_other.1.refs_0_), channel_id=1, source_target_pairs={{0,4},{1,5},{2,6},{3,7},{4,8},{5,9},{6,10},{7,11},{8,12},{9,13},{1... | collective-permute-start | bytes 786440 | tf_op jit(solution)/shard_map/ppermute | solution.py:20
  7.5 12.8 %collective-permute-start.4 = (bf16[4,2,128,128]{3,2,1,0:T(8,128)(2,1)S(1)}, bf16[4,2,128,128]{3,2,1,0:T(8,128)(2,1)S(1)}, u32[]{:S(2)}, u32[]{:S(2)}) collective-permute-start(bf16[4,2,128,128]{3,2,1,0:T(8,128)(2,1)S(1)} %pack_other.1.refs_0_), channel_id=1, source_target_pairs={{0,2},{1,3},{2,4},{3,5},{4,6},{5,7},{6,8},{7,9},{8,10},{9,11},{10,... | collective-permute-start | bytes 786440 | tf_op jit(solution)/shard_map/ppermute | solution.py:20
  15.3 17.6 %collective-permute-start.7 = (bf16[4,2,128,128]{3,2,1,0:T(8,128)(2,1)S(1)}, bf16[4,2,128,128]{3,2,1,0:T(8,128)(2,1)S(1)}, u32[]{:S(2)}, u32[]{:S(2)}) collective-permute-start(bf16[4,2,128,128]{3,2,1,0:T(8,128)(2,1)S(1)} %pack_both.1.refs_0_), channel_id=1, source_target_pairs={{0,4},{1,5},{2,6},{3,7},{4,8},{5,9},{6,10},{7,11},{8,12},{9,13},{1... | collective-permute-start | bytes 786440 | tf_op jit(solution)/shard_map/ppermute | solution.py:20
  17.2 15.6 %collective-permute-start.6 = (bf16[4,2,128,128]{3,2,1,0:T(8,128)(2,1)S(1)}, bf16[4,2,128,128]{3,2,1,0:T(8,128)(2,1)S(1)}, u32[]{:S(2)}, u32[]{:S(2)}) collective-permute-start(bf16[4,2,128,128]{3,2,1,0:T(8,128)(2,1)S(1)} %pack_both.1.refs_0_), channel_id=1, source_target_pairs={{0,2},{1,3},{2,4},{3,5},{4,6},{5,7},{6,8},{7,9},{8,10},{9,11},{10,... | collective-permute-start | bytes 786440 | tf_op jit(solution)/shard_map/ppermute | solution.py:20
  27.3 17.7 %collective-permute-start.8 = (bf16[4,2,128,128]{3,2,1,0:T(8,128)(2,1)S(1)}, bf16[4,2,128,128]{3,2,1,0:T(8,128)(2,1)S(1)}, u32[]{:S(2)}, u32[]{:S(2)}) collective-permute-start(bf16[4,2,128,128]{3,2,1,0:T(8,128)(2,1)S(1)} %get-tuple-element.37), channel_id=1, source_target_pairs={{4,0},{5,1},{6,2},{7,3},{8,4},{9,5},{10,6},{11,7},{12,8},{13,9},{1... | collective-permute-start | bytes 786440 | tf_op jit(solution)/shard_map/ppermute | solution.py:20
  30.7 14.4 %collective-permute-start.9 = (bf16[4,2,128,128]{3,2,1,0:T(8,128)(2,1)S(1)}, bf16[4,2,128,128]{3,2,1,0:T(8,128)(2,1)S(1)}, u32[]{:S(2)}, u32[]{:S(2)}) collective-permute-start(bf16[4,2,128,128]{3,2,1,0:T(8,128)(2,1)S(1)} %get-tuple-element.38), channel_id=1, source_target_pairs={{2,0},{3,1},{4,2},{5,3},{6,4},{7,5},{8,6},{9,7},{10,8},{11,9},{12,... | collective-permute-start | bytes 786440 | tf_op jit(solution)/shard_map/ppermute | solution.py:20
  38.9 12.7 %collective-permute-start.12 = (bf16[4,2,128,128]{3,2,1,0:T(8,128)(2,1)S(1)}, bf16[4,2,128,128]{3,2,1,0:T(8,128)(2,1)S(1)}, u32[]{:S(2)}, u32[]{:S(2)}) collective-permute-start(bf16[4,2,128,128]{3,2,1,0:T(8,128)(2,1)S(1)} %get-tuple-element.43), channel_id=1, source_target_pairs={{4,0},{5,1},{6,2},{7,3},{8,4},{9,5},{10,6},{11,7},{12,8},{13,9},{1... | collective-permute-start | bytes 786440 | tf_op jit(solution)/shard_map/ppermute | solution.py:20
  42.0 12.9 %collective-permute-start.13 = (bf16[4,2,128,128]{3,2,1,0:T(8,128)(2,1)S(1)}, bf16[4,2,128,128]{3,2,1,0:T(8,128)(2,1)S(1)}, u32[]{:S(2)}, u32[]{:S(2)}) collective-permute-start(bf16[4,2,128,128]{3,2,1,0:T(8,128)(2,1)S(1)} %get-tuple-element.44), channel_id=1, source_target_pairs={{2,0},{3,1},{4,2},{5,3},{6,4},{7,5},{8,6},{9,7},{10,8},{11,9},{12,... | collective-permute-start | bytes 786440 | tf_op jit(solution)/shard_map/ppermute | solution.py:20
  48.4 10.1 %collective-permute-start.10 = (bf16[64,16,128]{2,1,0:T(8,128)(2,1)S(1)}, bf16[64,16,128]{2,1,0:T(8,128)(2,1)S(1)}, u32[]{:S(2)}, u32[]{:S(2)}) collective-permute-start(bf16[64,16,128]{2,1,0:T(8,128)(2,1)S(1)} %get-tuple-element.40), channel_id=1, source_target_pairs={{0,1},{1,0},{2,3},{3,2},{4,5},{5,4},{6,7},{7,6},{8,9},{9,8},{10,11... | collective-permute-start | bytes 786440 | tf_op jit(solution)/shard_map/ppermute | solution.py:24
  51.1 7.4 %collective-permute-start.11 = (bf16[64,16,128]{2,1,0:T(8,128)(2,1)S(1)}, bf16[64,16,128]{2,1,0:T(8,128)(2,1)S(1)}, u32[]{:S(2)}, u32[]{:S(2)}) collective-permute-start(bf16[64,16,128]{2,1,0:T(8,128)(2,1)S(1)} %get-tuple-element.41), channel_id=1, source_target_pairs={{0,1},{1,0},{2,3},{3,2},{4,5},{5,4},{6,7},{7,6},{8,9},{9,8},{10,11... | collective-permute-start | bytes 786440 | tf_op jit(solution)/shard_map/ppermute | solution.py:24
  51.2 7.3 %collective-permute-start.15 = (bf16[4,128,128]{2,1,0:T(8,128)(2,1)S(1)}, bf16[4,128,128]{2,1,0:T(8,128)(2,1)S(1)}, u32[]{:S(2)}, u32[]{:S(2)}) collective-permute-start(bf16[4,128,128]{2,1,0:T(8,128)(2,1)S(1)} %get-tuple-element.48), channel_id=1, source_target_pairs={{0,1},{1,0},{2,3},{3,2},{4,5},{5,4},{6,7},{7,6},{8,9},{9,8},{10,11... | collective-permute-start | bytes 393224 | tf_op jit(solution)/shard_map/ppermute | solution.py:24
  55.5 4.1 %collective-permute-start.14 = (bf16[4,128,128]{2,1,0:T(8,128)(2,1)S(1)}, bf16[4,128,128]{2,1,0:T(8,128)(2,1)S(1)}, u32[]{:S(2)}, u32[]{:S(2)}) collective-permute-start(bf16[4,128,128]{2,1,0:T(8,128)(2,1)S(1)} %get-tuple-element.46), channel_id=1, source_target_pairs={{0,1},{1,0},{2,3},{3,2},{4,5},{5,4},{6,7},{7,6},{8,9},{9,8},{10,11... | collective-permute-start | bytes 393224 | tf_op jit(solution)/shard_map/ppermute | solution.py:24

commit v9 on v8

--- a/solution.py
+++ b/solution.py
@@ -9,7 +9,7 @@
 
 AXES = ("ctx", "uly")
 MASKED = -1e30
-HEADS_AT_ONCE = 4
+HEADS_AT_ONCE = 2
 BF16, F32 = jnp.bfloat16, jnp.float32
 NT = (((1,), (1,)), ((), ()))
 VMEM_BYTES = 16 * 2**20
@@ -53,31 +53,34 @@
 
 def arrange_kernel(group, place_ref, q_ref, do_ref, q_other_ref, do_other_ref, out_ref, scr):
     core = place_ref[0]
-    rows, heads, dim = q_ref.shape
+    tokens, heads, dim = q_ref.shape
+    half = heads // 2
+    mine = pl.ds(pl.multiple_of(core * half, half), half)
+    turn = 0
     for kind, (own, other) in enumerate([(q_ref, q_other_ref), (do_ref, do_other_ref)]):
         for which, ref in enumerate([own, other]):
             block = 1 - core if which else core
-            scr[...] = ref[...].astype(F32).reshape(rows * heads, dim)
-            for h in range(heads):
-                out_ref[h // group, block, kind, h % group] = scr[pl.ds(h, rows, stride=heads), :].astype(BF16)
+            wide = scr.at[turn % 2]
+            wide[...] = ref[:, mine].astype(F32).reshape(tokens * half, dim)
+            for h in range(half):
+                out_ref[h // group, block, kind, h % group] = wide[pl.ds(h, tokens, stride=half), :].astype(BF16)
+            turn += 1
 
 
 def arrange(place, queries, grad_out, q_other, do_other, key_heads):
     tokens, heads, dim = queries.shape
     half, group = heads // 2, heads // key_heads
-    rows = 32
-    in_spec = pl.BlockSpec((rows, half, dim), lambda i, place: (i, place[0], 0))
-    out = (key_heads // 2, 2, 2, group, tokens, dim)
+    whole = pl.BlockSpec(memory_space=pltpu.VMEM)
     return call(
         functools.partial(arrange_kernel, group),
         "arrange",
-        (tokens // rows,),
-        place,
-        (queries, grad_out, q_other, do_other),
-        [in_spec] * 4,
-        pltpu.VMEM(out, BF16),
-        pl.BlockSpec(out[:4] + (rows, dim), lambda i, place: (0, 0, 0, 0, i, 0)),
-        [pltpu.VMEM((rows * half, dim), F32)],
+        (1,),
+        place,
+        [in_vmem(x) for x in (queries, grad_out, q_other, do_other)],
+        [whole] * 4,
+        pltpu.VMEM((key_heads // 2, 2, 2, group, tokens, dim), BF16),
+        whole,
+        [pltpu.VMEM((2, tokens * half, dim), F32)],
         10**9,
     )
 
@@ -230,29 +233,37 @@
             firsts[e] = first_allowed(lengths_ref, query_pos, place_ref[1])
 
     window_of(k_refs, k_scr)
-    for e in range(2):
+    chunks = [(e, at) for e in range(2) for at in range(0, group * tokens, pair)]
+
+    def scores(e, at):
+        k = k_scr[pl.ds(e, count)].reshape(count * tokens, dim)
+        q = qd_ref[0, e, 0].reshape(group * tokens, dim)[at : at + pair]
+        return lax.dot_general(k, q, NT, preferred_element_type=F32)
+
+    ahead = scores(*chunks[0])
+    for i, (e, at) in enumerate(chunks):
+        s = ahead
+        if i + 1 < len(chunks):
+            ahead = scores(*chunks[i + 1])
         first = firsts[e] - row
-        k = k_scr[pl.ds(e, count)].reshape(count * tokens, dim)
-        q = qd_ref[0, e, 0].reshape(group * tokens, dim)
-        do = qd_ref[0, e, 1].reshape(group * tokens, dim)
-        for at in range(0, group * tokens, pair):
-            s = lax.dot_general(k, q[at : at + pair], NT, preferred_element_type=F32)
-            tiles = [s[j * tokens : (j + 1) * tokens] for j in range(count)]
-            last = (e + count - 1) * tokens
-            bound = jnp.where(diagonal, last, e * tokens)
-            tiles[0] = jnp.where(first <= bound, jnp.where(diagonal, tiles.pop(), tiles[0]), MASKED)
-            for j in range(1, count - 1):
-                tiles[j] = jnp.where(first <= (e + j) * tokens, tiles[j], MASKED)
-            top = folded(jnp.maximum, functools.reduce(jnp.maximum, tiles))
-            tiles = [jnp.exp((tile - top) * dim**-0.5) for tile in tiles]
-            inv = 1.0 / folded(jnp.add, functools.reduce(jnp.add, tiles))
-            store_tiles(p_ref, e, at, [tile * inv for tile in tiles], diagonal)
-        keep = (2 * halo - e) * tokens
-        dv = jnp.dot(p_ref[0, e, :keep], do, preferred_element_type=F32).reshape(2 * halo - e, tokens, dim)
-        if e == 0:
-            acc[...] = dv
-        else:
-            acc[1:] += dv
+        tiles = [s[j * tokens : (j + 1) * tokens] for j in range(count)]
+        last = (e + count - 1) * tokens
+        bound = jnp.where(diagonal, last, e * tokens)
+        tiles[0] = jnp.where(first <= bound, jnp.where(diagonal, tiles.pop(), tiles[0]), MASKED)
+        for j in range(1, count - 1):
+            tiles[j] = jnp.where(first <= (e + j) * tokens, tiles[j], MASKED)
+        top = folded(jnp.maximum, functools.reduce(jnp.maximum, tiles))
+        tiles = [jnp.exp((tile - top) * dim**-0.5) for tile in tiles]
+        inv = 1.0 / folded(jnp.add, functools.reduce(jnp.add, tiles))
+        store_tiles(p_ref, e, at, [tile * inv for tile in tiles], diagonal)
+        if at + pair == group * tokens:
+            do = qd_ref[0, e, 1].reshape(group * tokens, dim)
+            keep = (2 * halo - e) * tokens
+            dv = jnp.dot(p_ref[0, e, :keep], do, preferred_element_type=F32).reshape(2 * halo - e, tokens, dim)
+            if e == 0:
+                acc[...] = dv
+            else:
+                acc[1:] += dv
     for back, ref in zip(range(1, halo + 1), dv_refs):
         ref[0] = acc[pl.ds(2 * (halo - back), 2)].astype(BF16)
 
@@ -268,25 +279,33 @@
     window_of(v_refs, v_scr)
     row, lane = on_diagonal(tokens, HEADS_AT_ONCE)
     diagonal = row <= lane
-    for e in range(2):
+    chunks = [(e, at) for e in range(2) for at in range(0, group * tokens, pair)]
+
+    def dprobs(e, at):
         v = v_scr[pl.ds(e, count)].reshape(count * tokens, dim)
-        q = qd_ref[0, e, 0].reshape(group * tokens, dim)
-        do = qd_ref[0, e, 1].reshape(group * tokens, dim)
-        for at in range(0, group * tokens, pair):
-            dp = lax.dot_general(v, do[at : at + pair], NT, preferred_element_type=F32)
-            dps = [dp[j * tokens : (j + 1) * tokens] for j in range(count)]
-            dps[0] = jnp.where(diagonal, dps.pop(), dps[0])
-            ps = [p_ref[0, e, j * tokens : (j + 1) * tokens, at : at + pair] for j in range(count)]
-            ps[0] += ps.pop()
-            ps = [p.astype(F32) for p in ps]
-            delta = folded(jnp.add, functools.reduce(jnp.add, [p * dp for p, dp in zip(ps, dps)]))
-            store_tiles(ds_ref, e, at, [p * (dp - delta) for p, dp in zip(ps, dps)], diagonal)
-        keep = (2 * halo - e) * tokens
-        dk = jnp.dot(ds_ref[0, e, :keep], q, preferred_element_type=F32).reshape(2 * halo - e, tokens, dim)
-        if e == 0:
-            acc[...] = dk
-        else:
-            acc[1:] += dk
+        do = qd_ref[0, e, 1].reshape(group * tokens, dim)[at : at + pair]
+        return lax.dot_general(v, do, NT, preferred_element_type=F32)
+
+    ahead = dprobs(*chunks[0])
+    for i, (e, at) in enumerate(chunks):
+        dp = ahead
+        if i + 1 < len(chunks):
+            ahead = dprobs(*chunks[i + 1])
+        dps = [dp[j * tokens : (j + 1) * tokens] for j in range(count)]
+        dps[0] = jnp.where(diagonal, dps.pop(), dps[0])
+        ps = [p_ref[0, e, j * tokens : (j + 1) * tokens, at : at + pair] for j in range(count)]
+        ps[0] += ps.pop()
+        ps = [p.astype(F32) for p in ps]
+        delta = folded(jnp.add, functools.reduce(jnp.add, [p * dp for p, dp in zip(ps, dps)]))
+        store_tiles(ds_ref, e, at, [p * (dp - delta) for p, dp in zip(ps, dps)], diagonal)
+        if at + pair == group * tokens:
+            q = qd_ref[0, e, 0].reshape(group * tokens, dim)
+            keep = (2 * halo - e) * tokens
+            dk = jnp.dot(ds_ref[0, e, :keep], q, preferred_element_type=F32).reshape(2 * halo - e, tokens, dim)
+            if e == 0:
+                acc[...] = dk
+            else:
+                acc[1:] += dk
     for back, ref in zip(range(1, halo + 1), dk_refs):
         ref[0] = (acc[pl.ds(2 * (halo - back), 2)] * dim**-0.5).astype(BF16)
 
@@ -424,7 +443,7 @@
     k_own = pack_other(place, k_other, k_mine)
     k_own, queries, grad_out, v_mine = lax.optimization_barrier((k_own, queries, grad_out, v_mine))
     q_other, do_other, v_other = (swapped(x, device_count) for x in (queries, grad_out, v_mine))
-    qd = arrange(place, in_hbm(queries), in_hbm(grad_out), q_other, do_other, key_heads)
+    qd = arrange(place, queries, grad_out, q_other, do_other, key_heads)
     qd, v_mine, v_other = lax.optimization_barrier((qd, v_mine, v_other))
     v_own = pack_both(place, v_mine, v_other)
 

time: 62.2 us -> 62.6 us (level)
  starting transfers between devices: 30.7 us -> 32.4 us
  Pallas kernels: 26 us -> 24.5 us
    pallas_call x9, Pallas kernels: 26 us -> 24.5 us  [call(): pl.pallas_call(kernel, out_shape=outs, grid_spec=pltpu.PrefetchScalarGrid...]
    ppermute x8, starting transfers between devices: 7.72 us -> 8.71 us  [swapped(): return lax.ppermute(array, AXES, [(d, d ^ 1) for d in range(device_count)])]
    ppermute x8, starting transfers between devices: 22.9 us -> 23.7 us  [moved(): return lax.ppermute(array, AXES, pairs)]
  transfers between devices with their start and end apart: 16 -> 16, of which waited for: 2 -> 2; matrix products, arithmetic and copies ran while one was open for 0% -> 0% of each run, Pallas kernels for 37% -> 35%
where the time goes in v9:
time: 62.6 us; the launch traced here: 62.3 us
  starting transfers between devices  32.4 us (52%)
  Pallas kernels  24.5 us (39%)
  waiting for transfers between devices  4.34 us (7%)
  between operations  0.87 us (1%)
    pallas_call x9, Pallas kernels, call(): pl.pallas_call(kernel, out_shape=outs, grid_spec=pltpu.PrefetchScalarGrid...  24.5 us
    ppermute x8, starting transfers between devices, moved(): return lax.ppermute(array, AXES, pairs)  23.7 us
    ppermute x8, starting transfers between devices, swapped(): return lax.ppermute(array, AXES, [(d, d ^ 1) for d in range(device_count)])  8.71 us
    ppermute x8, waiting for transfers between devices, moved(): return lax.ppermute(array, AXES, pairs)  3.35 us
  transfers between devices with their start and end apart: 16, of which 2 were waited for; matrix products, arithmetic and copies ran while one was open for 0% of the time, Pallas kernels for 35%

profile of v9, /device:TPU:23, one launch (start us, length us, event | category | flops | bytes accessed | tf_op | source)
XLA Modules:
  0.0 62.3 jit_solution(11477143576859472561)
XLA Ops:
  0.6 0.7 %collective-permute-start = (bf16[128,8,128]{2,1,0:T(8,128)(2,1)}, bf16[128,8,128]{2,1,0:T(8,128)(2,1)S(1)}, u32[]{:S(2)}, u32[]{:S(2)}) collective-permute-start(bf16[128,8,128]{2,1,0:T(8,128)(2,1)} %key_ref.1), channel_id=1, source_target_pairs={{0,1},{1,0},{2,3},{3,2},{4,5},{5,4},{6,7},{7,6},{8,9},{9,8},{10,11... | collective-permute-start | bytes 786440 | tf_op jit(solution)/shard_map/ppermute | solution.py:24
  1.4 0.1 pad_add_fusion.place_ref
  1.5 1.6 %fetch.1 = (bf16[4,2,128,128]{3,2,1,0:T(8,128)(2,1)S(1)}, bf16[128,8,128]{2,1,0:T(8,128)(2,1)S(1)}) custom-call(s32[2]{0:T(128)S(1)} %pad_add_fusion.place_ref, bf16[128,8,128]{2,1,0:T(8,128)(2,1)} %key_ref.1, bf16[128,8,128]{2,1,0:T(8,128)(2,1)} %refs_0_.1), custom_call_target="tpu_custom_call" | custom-call | flops 1000000000 | tf_op jit(solution)/shard_map/fetch/pallas_call | solution.py:37
  3.1 0.0 collective-permute-done.other_ref
  3.1 0.6 pack_other.1.refs_0_
  3.7 0.0 copy-start.2
  3.7 0.1 collective-permute-start.1
  3.9 0.4 collective-permute-start.2
  4.3 0.1 collective-permute-start.3
  4.4 3.1 %collective-permute-start.5 = (bf16[4,2,128,128]{3,2,1,0:T(8,128)(2,1)S(1)}, bf16[4,2,128,128]{3,2,1,0:T(8,128)(2,1)S(1)}, u32[]{:S(2)}, u32[]{:S(2)}) collective-permute-start(bf16[4,2,128,128]{3,2,1,0:T(8,128)(2,1)S(1)} %pack_other.1.refs_0_), channel_id=1, source_target_pairs={{0,4},{1,5},{2,6},{3,7},{4,8},{5,9},{6,10},{7,11},{8,12},{9,13},{1... | collective-permute-start | bytes 786440 | tf_op jit(solution)/shard_map/ppermute | solution.py:20
  7.5 3.1 %collective-permute-start.4 = (bf16[4,2,128,128]{3,2,1,0:T(8,128)(2,1)S(1)}, bf16[4,2,128,128]{3,2,1,0:T(8,128)(2,1)S(1)}, u32[]{:S(2)}, u32[]{:S(2)}) collective-permute-start(bf16[4,2,128,128]{3,2,1,0:T(8,128)(2,1)S(1)} %pack_other.1.refs_0_), channel_id=1, source_target_pairs={{0,2},{1,3},{2,4},{3,5},{4,6},{5,7},{6,8},{7,9},{8,10},{9,11},{10,... | collective-permute-start | bytes 786440 | tf_op jit(solution)/shard_map/ppermute | solution.py:20
  10.7 0.0 collective-permute-done.1.q_other_ref
  10.7 0.0 collective-permute-done.2.do_other_ref
  10.7 2.0 %arrange.1.qd_ref = bf16[4,2,2,4,128,128]{5,4,3,2,1,0:T(8,128)(2,1)S(1)} custom-call(s32[2]{0:T(128)S(1)} %pad_add_fusion.place_ref, bf16[128,32,128]{2,1,0:T(8,128)(2,1)S(1)} %copy-done, bf16[128,32,128]{2,1,0:T(8,128)(2,1)S(1)} %copy-done.1, bf16[128,32,128]{2,1,0:T(8,128)(2,1)S(1)} %collective-permute-done.1.q_other_ref, ...), custom_call_target="tpu_custom_call" | custom-call | flops 1000000000 | tf_op jit(solution)/shard_map/arrange/pallas_call | solution.py:37
  12.7 0.7 %pack_both.1.refs_0_ = bf16[4,2,128,128]{3,2,1,0:T(8,128)(2,1)S(1)} custom-call(s32[2]{0:T(128)S(1)} %pad_add_fusion.place_ref, bf16[128,8,128]{2,1,0:T(8,128)(2,1)S(1)} %get-tuple-element.34.own_ref, bf16[128,8,128]{2,1,0:T(8,128)(2,1)S(1)} %collective-permute-done.3.other_ref), custom_call_target="tpu_custom_call" | custom-call | flops 1000000000 | tf_op jit(solution)/shard_map/pack_both/pallas_call | solution.py:37
  13.4 1.9 %collective-permute-start.7 = (bf16[4,2,128,128]{3,2,1,0:T(8,128)(2,1)S(1)}, bf16[4,2,128,128]{3,2,1,0:T(8,128)(2,1)S(1)}, u32[]{:S(2)}, u32[]{:S(2)}) collective-permute-start(bf16[4,2,128,128]{3,2,1,0:T(8,128)(2,1)S(1)} %pack_both.1.refs_0_), channel_id=1, source_target_pairs={{0,4},{1,5},{2,6},{3,7},{4,8},{5,9},{6,10},{7,11},{8,12},{9,13},{1... | collective-permute-start | bytes 786440 | tf_op jit(solution)/shard_map/ppermute | solution.py:20
  15.4 3.1 %collective-permute-start.6 = (bf16[4,2,128,128]{3,2,1,0:T(8,128)(2,1)S(1)}, bf16[4,2,128,128]{3,2,1,0:T(8,128)(2,1)S(1)}, u32[]{:S(2)}, u32[]{:S(2)}) collective-permute-start(bf16[4,2,128,128]{3,2,1,0:T(8,128)(2,1)S(1)} %pack_both.1.refs_0_), channel_id=1, source_target_pairs={{0,2},{1,3},{2,4},{3,5},{4,6},{5,7},{6,8},{7,9},{8,10},{9,11},{10,... | collective-permute-start | bytes 786440 | tf_op jit(solution)/shard_map/ppermute | solution.py:20
  18.5 7.1 %prob.1 = (bf16[4,2,640,512]{3,2,1,0:T(8,128)(2,1)S(1)}, bf16[4,2,128,128]{3,2,1,0:T(8,128)(2,1)S(1)}, bf16[4,2,128,128]{3,2,1,0:T(8,128)(2,1)S(1)}) custom-call(s32[2]{0:T(128)S(1)} %pad_add_fusion.place_ref, s32[16]{0:T(128)S(1)} %copy-done.2, bf16[4,2,2,4,128,128]{5,4,3,2,1,0:T(8,128)(2,1)S(1)} %arrange.1.qd_ref, ...), custom_call_target="tpu_custom_call" | custom-call | flops 2684354560 | tf_op jit(solution)/shard_map/prob/pallas_call | solution.py:37
  25.6 3.4 %collective-permute-start.8 = (bf16[4,2,128,128]{3,2,1,0:T(8,128)(2,1)S(1)}, bf16[4,2,128,128]{3,2,1,0:T(8,128)(2,1)S(1)}, u32[]{:S(2)}, u32[]{:S(2)}) collective-permute-start(bf16[4,2,128,128]{3,2,1,0:T(8,128)(2,1)S(1)} %get-tuple-element.37), channel_id=1, source_target_pairs={{4,0},{5,1},{6,2},{7,3},{8,4},{9,5},{10,6},{11,7},{12,8},{13,9},{1... | collective-permute-start | bytes 786440 | tf_op jit(solution)/shard_map/ppermute | solution.py:20
  29.0 5.2 %collective-permute-start.9 = (bf16[4,2,128,128]{3,2,1,0:T(8,128)(2,1)S(1)}, bf16[4,2,128,128]{3,2,1,0:T(8,128)(2,1)S(1)}, u32[]{:S(2)}, u32[]{:S(2)}) collective-permute-start(bf16[4,2,128,128]{3,2,1,0:T(8,128)(2,1)S(1)} %get-tuple-element.38), channel_id=1, source_target_pairs={{2,0},{3,1},{4,2},{5,3},{6,4},{7,5},{8,6},{9,7},{10,8},{11,9},{12,... | collective-permute-start | bytes 786440 | tf_op jit(solution)/shard_map/ppermute | solution.py:20
  34.2 6.2 %dscore.1 = (bf16[4,2,640,512]{3,2,1,0:T(8,128)(2,1)S(1)}, bf16[4,2,128,128]{3,2,1,0:T(8,128)(2,1)S(1)}, bf16[4,2,128,128]{3,2,1,0:T(8,128)(2,1)S(1)}) custom-call(s32[2]{0:T(128)S(1)} %pad_add_fusion.place_ref, bf16[4,2,2,4,128,128]{5,4,3,2,1,0:T(8,128)(2,1)S(1)} %arrange.1.qd_ref, bf16[4,2,640,512]{3,2,1,0:T(8,128)(2,1)S(1)} %get-tuple-element.33.p_ref, ...), custom_call_target="tpu_custom_call" | custom-call | flops 2684354560 | tf_op jit(solution)/shard_map/dscore/pallas_call | solution.py:37
  40.5 1.9 %collective-permute-start.12 = (bf16[4,2,128,128]{3,2,1,0:T(8,128)(2,1)S(1)}, bf16[4,2,128,128]{3,2,1,0:T(8,128)(2,1)S(1)}, u32[]{:S(2)}, u32[]{:S(2)}) collective-permute-start(bf16[4,2,128,128]{3,2,1,0:T(8,128)(2,1)S(1)} %get-tuple-element.43), channel_id=1, source_target_pairs={{4,0},{5,1},{6,2},{7,3},{8,4},{9,5},{10,6},{11,7},{12,8},{13,9},{1... | collective-permute-start | bytes 786440 | tf_op jit(solution)/shard_map/ppermute | solution.py:20
  42.4 1.9 %collective-permute-start.13 = (bf16[4,2,128,128]{3,2,1,0:T(8,128)(2,1)S(1)}, bf16[4,2,128,128]{3,2,1,0:T(8,128)(2,1)S(1)}, u32[]{:S(2)}, u32[]{:S(2)}) collective-permute-start(bf16[4,2,128,128]{3,2,1,0:T(8,128)(2,1)S(1)} %get-tuple-element.44), channel_id=1, source_target_pairs={{2,0},{3,1},{4,2},{5,3},{6,4},{7,5},{8,6},{9,7},{10,8},{11,9},{12,... | collective-permute-start | bytes 786440 | tf_op jit(solution)/shard_map/ppermute | solution.py:20
  44.3 3.3 %own.1 = (bf16[128,16,128]{2,1,0:T(8,128)(2,1)S(1)}, bf16[64,16,128]{2,1,0:T(8,128)(2,1)S(1)}, bf16[64,16,128]{2,1,0:T(8,128)(2,1)S(1)}, f32[4,2,128,128]{3,2,1,...) custom-call(s32[2]{0:T(128)S(1)} %pad_add_fusion.place_ref, ...), custom_call_target="tpu_custom_call" | custom-call | tf_op jit(solution)/shard_map/own/pallas_call | solution.py:37
  47.7 4.0 %collective-permute-start.10 = (bf16[64,16,128]{2,1,0:T(8,128)(2,1)S(1)}, bf16[64,16,128]{2,1,0:T(8,128)(2,1)S(1)}, u32[]{:S(2)}, u32[]{:S(2)}) collective-permute-start(bf16[64,16,128]{2,1,0:T(8,128)(2,1)S(1)} %get-tuple-element.40), channel_id=1, source_target_pairs={{0,1},{1,0},{2,3},{3,2},{4,5},{5,4},{6,7},{7,6},{8,9},{9,8},{10,11... | collective-permute-start | bytes 786440 | tf_op jit(solution)/shard_map/ppermute | solution.py:24
  51.7 0.1 collective-permute-start.11
  51.8 0.4 collective-permute-start.15
  52.2 3.3 %collective-permute-done.13.refs_1_ = bf16[4,2,128,128]{3,2,1,0:T(8,128)(2,1)S(1)} collective-permute-done((bf16[4,2,128,128]{3,2,1,0:T(8,128)(2,1)S(1)}, bf16[4,2,128,128]{3,2,1,0:T(8,128)(2,1)S(1)}, u32[]{:S(2)}, u32[]{:S(2)}) %collective-permute-start.13) | collective-permute-done | bytes 262176 | tf_op jit(solution)/shard_map/ppermute | solution.py:20
  55.5 0.6 %sum_dk.1 = (bf16[4,128,128]{2,1,0:T(8,128)(2,1)S(1)}, bf16[4,128,128]{2,1,0:T(8,128)(2,1)S(1)}) custom-call(s32[2]{0:T(128)S(1)} %pad_add_fusion.place_ref, f32[4,2,128,128]{3,2,1,0:T(8,128)S(1)} %get-tuple-element.42.own_ref, bf16[4,2,128,128]{3,2,1,0:T(8,128)(2,1)S(1)} %collective-permute-done.12.refs_0_, ...), custom_call_target="tpu_custom_call" | custom-call | tf_op jit(solution)/shard_map/sum_dk/pallas_call | solution.py:37
  56.1 2.8 %collective-permute-start.14 = (bf16[4,128,128]{2,1,0:T(8,128)(2,1)S(1)}, bf16[4,128,128]{2,1,0:T(8,128)(2,1)S(1)}, u32[]{:S(2)}, u32[]{:S(2)}) collective-permute-start(bf16[4,128,128]{2,1,0:T(8,128)(2,1)S(1)} %get-tuple-element.46), channel_id=1, source_target_pairs={{0,1},{1,0},{2,3},{3,2},{4,5},{5,4},{6,7},{7,6},{8,9},{9,8},{10,11... | collective-permute-start | bytes 393224 | tf_op jit(solution)/shard_map/ppermute | solution.py:24
  59.0 1.0 %collective-permute-done.14.refs_4_ = bf16[4,128,128]{2,1,0:T(8,128)(2,1)S(1)} collective-permute-done((bf16[4,128,128]{2,1,0:T(8,128)(2,1)S(1)}, bf16[4,128,128]{2,1,0:T(8,128)(2,1)S(1)}, u32[]{:S(2)}, u32[]{:S(2)}) %collective-permute-start.14) | collective-permute-done | bytes 131104 | tf_op jit(solution)/shard_map/ppermute | solution.py:24
  59.9 2.3 %finish.1 = (bf16[128,32,128]{2,1,0:T(8,128)(2,1)}, bf16[128,8,128]{2,1,0:T(8,128)(2,1)}, bf16[128,8,128]{2,1,0:T(8,128)(2,1)}) custom-call(s32[2]{0:T(128)S(1)} %pad_add_fusion.place_ref, bf16[128,16,128]{2,1,0:T(8,128)(2,1)S(1)} %get-tuple-element.39.refs_0_, bf16[64,16,128]{2,1,0:T(8,128)(2,1)S(1)} %collective-permute-done.10.refs_1_, ...), custom_call_target="tpu_custom_call" | custom-call | tf_op jit(solution)/shard_map/finish/pallas_call | solution.py:37
  (16 shorter events, 0.0 us)
Async XLA Ops:
  0.6 3.2 %copy-start.1 = (bf16[128,32,128]{2,1,0:T(8,128)(2,1)S(1)}, bf16[128,32,128]{2,1,0:T(8,128)(2,1)}, u32[]{:S(2)}) copy-start(bf16[128,32,128]{2,1,0:T(8,128)(2,1)} %do_ref) | copy-start | bytes 3145732
  0.6 3.1 %copy-start = (bf16[128,32,128]{2,1,0:T(8,128)(2,1)S(1)}, bf16[128,32,128]{2,1,0:T(8,128)(2,1)}, u32[]{:S(2)}) copy-start(bf16[128,32,128]{2,1,0:T(8,128)(2,1)} %q_ref) | copy-start | bytes 3145732
  0.6 2.4 %collective-permute-start = (bf16[128,8,128]{2,1,0:T(8,128)(2,1)}, bf16[128,8,128]{2,1,0:T(8,128)(2,1)S(1)}, u32[]{:S(2)}, u32[]{:S(2)}) collective-permute-start(bf16[128,8,128]{2,1,0:T(8,128)(2,1)} %key_ref.1), channel_id=1, source_target_pairs={{0,1},{1,0},{2,3},{3,2},{4,5},{5,4},{6,7},{7,6},{8,9},{9,8},{10,11... | collective-permute-start | bytes 786440 | tf_op jit(solution)/shard_map/ppermute | solution.py:24
  3.7 14.8 %copy-start.2 = (s32[16]{0:T(128)S(1)}, s32[16]{0:T(128)}, u32[]{:S(2)}) copy-start(s32[16]{0:T(128)} %lengths_ref.1) | copy-start | bytes 196
  3.7 6.9 %collective-permute-start.1 = (bf16[128,32,128]{2,1,0:T(8,128)(2,1)S(1)}, bf16[128,32,128]{2,1,0:T(8,128)(2,1)S(1)}, u32[]{:S(2)}, u32[]{:S(2)}) collective-permute-start(bf16[128,32,128]{2,1,0:T(8,128)(2,1)S(1)} %copy-done), channel_id=1, source_target_pairs={{0,1},{1,0},{2,3},{3,2},{4,5},{5,4},{6,7},{7,6},{8,9},{9,8},{10,11... | collective-permute-start | bytes 3145736 | tf_op jit(solution)/shard_map/ppermute | solution.py:24
  3.9 6.8 %collective-permute-start.2 = (bf16[128,32,128]{2,1,0:T(8,128)(2,1)S(1)}, bf16[128,32,128]{2,1,0:T(8,128)(2,1)S(1)}, u32[]{:S(2)}, u32[]{:S(2)}) collective-permute-start(bf16[128,32,128]{2,1,0:T(8,128)(2,1)S(1)} %copy-done.1), channel_id=1, source_target_pairs={{0,1},{1,0},{2,3},{3,2},{4,5},{5,4},{6,7},{7,6},{8,9},{9,8},{10,11... | collective-permute-start | bytes 3145736 | tf_op jit(solution)/shard_map/ppermute | solution.py:24
  4.3 8.4 %collective-permute-start.3 = (bf16[128,8,128]{2,1,0:T(8,128)(2,1)S(1)}, bf16[128,8,128]{2,1,0:T(8,128)(2,1)S(1)}, u32[]{:S(2)}, u32[]{:S(2)}) collective-permute-start(bf16[128,8,128]{2,1,0:T(8,128)(2,1)S(1)} %get-tuple-element.34.own_ref), channel_id=1, source_target_pairs={{0,1},{1,0},{2,3},{3,2},{4,5},{5,4},{6,7},{7,6},{8,9},{9,8},{10,11... | collective-permute-start | bytes 786440 | tf_op jit(solution)/shard_map/ppermute | solution.py:24
  4.4 14.1 %collective-permute-start.5 = (bf16[4,2,128,128]{3,2,1,0:T(8,128)(2,1)S(1)}, bf16[4,2,128,128]{3,2,1,0:T(8,128)(2,1)S(1)}, u32[]{:S(2)}, u32[]{:S(2)}) collective-permute-start(bf16[4,2,128,128]{3,2,1,0:T(8,128)(2,1)S(1)} %pack_other.1.refs_0_), channel_id=1, source_target_pairs={{0,4},{1,5},{2,6},{3,7},{4,8},{5,9},{6,10},{7,11},{8,12},{9,13},{1... | collective-permute-start | bytes 786440 | tf_op jit(solution)/shard_map/ppermute | solution.py:20
  7.5 11.0 %collective-permute-start.4 = (bf16[4,2,128,128]{3,2,1,0:T(8,128)(2,1)S(1)}, bf16[4,2,128,128]{3,2,1,0:T(8,128)(2,1)S(1)}, u32[]{:S(2)}, u32[]{:S(2)}) collective-permute-start(bf16[4,2,128,128]{3,2,1,0:T(8,128)(2,1)S(1)} %pack_other.1.refs_0_), channel_id=1, source_target_pairs={{0,2},{1,3},{2,4},{3,5},{4,6},{5,7},{6,8},{7,9},{8,10},{9,11},{10,... | collective-permute-start | bytes 786440 | tf_op jit(solution)/shard_map/ppermute | solution.py:20
  13.4 20.8 %collective-permute-start.7 = (bf16[4,2,128,128]{3,2,1,0:T(8,128)(2,1)S(1)}, bf16[4,2,128,128]{3,2,1,0:T(8,128)(2,1)S(1)}, u32[]{:S(2)}, u32[]{:S(2)}) collective-permute-start(bf16[4,2,128,128]{3,2,1,0:T(8,128)(2,1)S(1)} %pack_both.1.refs_0_), channel_id=1, source_target_pairs={{0,4},{1,5},{2,6},{3,7},{4,8},{5,9},{6,10},{7,11},{8,12},{9,13},{1... | collective-permute-start | bytes 786440 | tf_op jit(solution)/shard_map/ppermute | solution.py:20
  15.4 18.8 %collective-permute-start.6 = (bf16[4,2,128,128]{3,2,1,0:T(8,128)(2,1)S(1)}, bf16[4,2,128,128]{3,2,1,0:T(8,128)(2,1)S(1)}, u32[]{:S(2)}, u32[]{:S(2)}) collective-permute-start(bf16[4,2,128,128]{3,2,1,0:T(8,128)(2,1)S(1)} %pack_both.1.refs_0_), channel_id=1, source_target_pairs={{0,2},{1,3},{2,4},{3,5},{4,6},{5,7},{6,8},{7,9},{8,10},{9,11},{10,... | collective-permute-start | bytes 786440 | tf_op jit(solution)/shard_map/ppermute | solution.py:20
  25.6 18.7 %collective-permute-start.8 = (bf16[4,2,128,128]{3,2,1,0:T(8,128)(2,1)S(1)}, bf16[4,2,128,128]{3,2,1,0:T(8,128)(2,1)S(1)}, u32[]{:S(2)}, u32[]{:S(2)}) collective-permute-start(bf16[4,2,128,128]{3,2,1,0:T(8,128)(2,1)S(1)} %get-tuple-element.37), channel_id=1, source_target_pairs={{4,0},{5,1},{6,2},{7,3},{8,4},{9,5},{10,6},{11,7},{12,8},{13,9},{1... | collective-permute-start | bytes 786440 | tf_op jit(solution)/shard_map/ppermute | solution.py:20
  29.0 15.4 %collective-permute-start.9 = (bf16[4,2,128,128]{3,2,1,0:T(8,128)(2,1)S(1)}, bf16[4,2,128,128]{3,2,1,0:T(8,128)(2,1)S(1)}, u32[]{:S(2)}, u32[]{:S(2)}) collective-permute-start(bf16[4,2,128,128]{3,2,1,0:T(8,128)(2,1)S(1)} %get-tuple-element.38), channel_id=1, source_target_pairs={{2,0},{3,1},{4,2},{5,3},{6,4},{7,5},{8,6},{9,7},{10,8},{11,9},{12,... | collective-permute-start | bytes 786440 | tf_op jit(solution)/shard_map/ppermute | solution.py:20
  40.5 11.7 %collective-permute-start.12 = (bf16[4,2,128,128]{3,2,1,0:T(8,128)(2,1)S(1)}, bf16[4,2,128,128]{3,2,1,0:T(8,128)(2,1)S(1)}, u32[]{:S(2)}, u32[]{:S(2)}) collective-permute-start(bf16[4,2,128,128]{3,2,1,0:T(8,128)(2,1)S(1)} %get-tuple-element.43), channel_id=1, source_target_pairs={{4,0},{5,1},{6,2},{7,3},{8,4},{9,5},{10,6},{11,7},{12,8},{13,9},{1... | collective-permute-start | bytes 786440 | tf_op jit(solution)/shard_map/ppermute | solution.py:20
  42.4 13.1 %collective-permute-start.13 = (bf16[4,2,128,128]{3,2,1,0:T(8,128)(2,1)S(1)}, bf16[4,2,128,128]{3,2,1,0:T(8,128)(2,1)S(1)}, u32[]{:S(2)}, u32[]{:S(2)}) collective-permute-start(bf16[4,2,128,128]{3,2,1,0:T(8,128)(2,1)S(1)} %get-tuple-element.44), channel_id=1, source_target_pairs={{2,0},{3,1},{4,2},{5,3},{6,4},{7,5},{8,6},{9,7},{10,8},{11,9},{12,... | collective-permute-start | bytes 786440 | tf_op jit(solution)/shard_map/ppermute | solution.py:20
  47.7 11.3 %collective-permute-start.10 = (bf16[64,16,128]{2,1,0:T(8,128)(2,1)S(1)}, bf16[64,16,128]{2,1,0:T(8,128)(2,1)S(1)}, u32[]{:S(2)}, u32[]{:S(2)}) collective-permute-start(bf16[64,16,128]{2,1,0:T(8,128)(2,1)S(1)} %get-tuple-element.40), channel_id=1, source_target_pairs={{0,1},{1,0},{2,3},{3,2},{4,5},{5,4},{6,7},{7,6},{8,9},{9,8},{10,11... | collective-permute-start | bytes 786440 | tf_op jit(solution)/shard_map/ppermute | solution.py:24
  51.7 7.3 %collective-permute-start.11 = (bf16[64,16,128]{2,1,0:T(8,128)(2,1)S(1)}, bf16[64,16,128]{2,1,0:T(8,128)(2,1)S(1)}, u32[]{:S(2)}, u32[]{:S(2)}) collective-permute-start(bf16[64,16,128]{2,1,0:T(8,128)(2,1)S(1)} %get-tuple-element.41), channel_id=1, source_target_pairs={{0,1},{1,0},{2,3},{3,2},{4,5},{5,4},{6,7},{7,6},{8,9},{9,8},{10,11... | collective-permute-start | bytes 786440 | tf_op jit(solution)/shard_map/ppermute | solution.py:24
  51.8 7.2 %collective-permute-start.15 = (bf16[4,128,128]{2,1,0:T(8,128)(2,1)S(1)}, bf16[4,128,128]{2,1,0:T(8,128)(2,1)S(1)}, u32[]{:S(2)}, u32[]{:S(2)}) collective-permute-start(bf16[4,128,128]{2,1,0:T(8,128)(2,1)S(1)} %get-tuple-element.48), channel_id=1, source_target_pairs={{0,1},{1,0},{2,3},{3,2},{4,5},{5,4},{6,7},{7,6},{8,9},{9,8},{10,11... | collective-permute-start | bytes 393224 | tf_op jit(solution)/shard_map/ppermute | solution.py:24
  56.1 3.8 %collective-permute-start.14 = (bf16[4,128,128]{2,1,0:T(8,128)(2,1)S(1)}, bf16[4,128,128]{2,1,0:T(8,128)(2,1)S(1)}, u32[]{:S(2)}, u32[]{:S(2)}) collective-permute-start(bf16[4,128,128]{2,1,0:T(8,128)(2,1)S(1)} %get-tuple-element.46), channel_id=1, source_target_pairs={{0,1},{1,0},{2,3},{3,2},{4,5},{5,4},{6,7},{7,6},{8,9},{9,8},{10,11... | collective-permute-start | bytes 393224 | tf_op jit(solution)/shard_map/ppermute | solution.py:24

commit v10 on v8

--- a/solution.py
+++ b/solution.py
@@ -9,7 +9,7 @@
 
 AXES = ("ctx", "uly")
 MASKED = -1e30
-HEADS_AT_ONCE = 4
+HEADS_AT_ONCE = 2
 BF16, F32 = jnp.bfloat16, jnp.float32
 NT = (((1,), (1,)), ((), ()))
 VMEM_BYTES = 16 * 2**20
@@ -53,31 +53,34 @@
 
 def arrange_kernel(group, place_ref, q_ref, do_ref, q_other_ref, do_other_ref, out_ref, scr):
     core = place_ref[0]
-    rows, heads, dim = q_ref.shape
+    tokens, heads, dim = q_ref.shape
+    half = heads // 2
+    mine = pl.ds(pl.multiple_of(core * half, half), half)
+    turn = 0
     for kind, (own, other) in enumerate([(q_ref, q_other_ref), (do_ref, do_other_ref)]):
         for which, ref in enumerate([own, other]):
             block = 1 - core if which else core
-            scr[...] = ref[...].astype(F32).reshape(rows * heads, dim)
-            for h in range(heads):
-                out_ref[h // group, block, kind, h % group] = scr[pl.ds(h, rows, stride=heads), :].astype(BF16)
+            wide = scr.at[turn % 2]
+            wide[...] = ref[:, mine].astype(F32).reshape(tokens * half, dim)
+            for h in range(half):
+                out_ref[h // group, block, kind, h % group] = wide[pl.ds(h, tokens, stride=half), :].astype(BF16)
+            turn += 1
 
 
 def arrange(place, queries, grad_out, q_other, do_other, key_heads):
     tokens, heads, dim = queries.shape
     half, group = heads // 2, heads // key_heads
-    rows = 32
-    in_spec = pl.BlockSpec((rows, half, dim), lambda i, place: (i, place[0], 0))
-    out = (key_heads // 2, 2, 2, group, tokens, dim)
+    whole = pl.BlockSpec(memory_space=pltpu.VMEM)
     return call(
         functools.partial(arrange_kernel, group),
         "arrange",
-        (tokens // rows,),
-        place,
-        (queries, grad_out, q_other, do_other),
-        [in_spec] * 4,
-        pltpu.VMEM(out, BF16),
-        pl.BlockSpec(out[:4] + (rows, dim), lambda i, place: (0, 0, 0, 0, i, 0)),
-        [pltpu.VMEM((rows * half, dim), F32)],
+        (1,),
+        place,
+        [in_vmem(x) for x in (queries, grad_out, q_other, do_other)],
+        [whole] * 4,
+        pltpu.VMEM((key_heads // 2, 2, 2, group, tokens, dim), BF16),
+        whole,
+        [pltpu.VMEM((2, tokens * half, dim), F32)],
         10**9,
     )
 
@@ -192,9 +195,9 @@
 
 
 def window_of(pair_refs, scr):
-    halo = len(pair_refs) - 1
+    count = len(pair_refs)
     for back, ref in enumerate(pair_refs):
-        scr[pl.ds(2 * (halo - back), 2)] = ref[0]
+        scr[pl.ds(2 * (count - 1 - back), 2)] = ref[0]
 
 
 def on_diagonal(tokens, copies):
@@ -212,16 +215,10 @@
     ref[0, e, -tokens:, lanes] = jnp.where(diagonal, tiles[0], 0.0).astype(BF16)
 
 
-def prob_kernel(halo, place_ref, lengths_ref, qd_ref, *refs):
-    k_refs = refs[: halo + 1]
-    p_ref = refs[halo + 1]
-    dv_refs = refs[halo + 2 : -3]
-    k_scr, acc, firsts = refs[-3:]
+def near_kernel(halo, place_ref, lengths_ref, qd_ref, k_ref, v_ref, s_ref, dp_ref, firsts):
     _, _, _, group, tokens, dim = qd_ref.shape
-    count = 2 * halo + 1
-    pair = HEADS_AT_ONCE * tokens
-    row, lane = on_diagonal(tokens, HEADS_AT_ONCE)
-    diagonal = row <= lane
+    lanes = group * tokens
+    row, lane = on_diagonal(tokens, group)
 
     @pl.when(pl.program_id(0) == 0)
     def _():
@@ -229,26 +226,58 @@
             query_pos = lane[:1] + (2 * halo + e) * tokens
             firsts[e] = first_allowed(lengths_ref, query_pos, place_ref[1])
 
+    for e in range(2):
+        rows = (e + 1) * tokens
+        q = qd_ref[0, e, 0].reshape(lanes, dim)
+        do = qd_ref[0, e, 1].reshape(lanes, dim)
+        k = k_ref[0, : e + 1].reshape(rows, dim)
+        v = v_ref[0, : e + 1].reshape(rows, dim)
+        s = lax.dot_general(k, q, NT, preferred_element_type=F32)
+        dp_ref[0, e * tokens : e * tokens + rows] = lax.dot_general(v, do, NT, preferred_element_type=F32)
+        first = firsts[e] - row
+        for j in range(e + 1):
+            allowed = first <= (2 * halo + j) * tokens
+            if j == e:
+                allowed &= row <= lane
+            tile = jnp.where(allowed, s[j * tokens : (j + 1) * tokens], MASKED)
+            s_ref[0, (e + j) * tokens : (e + j + 1) * tokens] = tile
+
+
+def prob_kernel(halo, place_ref, lengths_ref, qd_ref, near_ref, *refs):
+    k_refs = refs[:halo]
+    p_ref = refs[halo]
+    dv_refs = refs[halo + 1 : -3]
+    k_scr, acc, firsts = refs[-3:]
+    _, _, _, group, tokens, dim = qd_ref.shape
+    pair = HEADS_AT_ONCE * tokens
+    row, lane = on_diagonal(tokens, HEADS_AT_ONCE)
+    diagonal = row <= lane
+
+    @pl.when(pl.program_id(0) == 0)
+    def _():
+        for e in range(2):
+            query_pos = lane[:1] + (2 * halo + e) * tokens
+            firsts[e] = first_allowed(lengths_ref, query_pos, place_ref[1])
+
     window_of(k_refs, k_scr)
     for e in range(2):
         first = firsts[e] - row
-        k = k_scr[pl.ds(e, count)].reshape(count * tokens, dim)
+        far = 2 * halo - e
+        k = k_scr[pl.ds(e, far)].reshape(far * tokens, dim)
         q = qd_ref[0, e, 0].reshape(group * tokens, dim)
         do = qd_ref[0, e, 1].reshape(group * tokens, dim)
         for at in range(0, group * tokens, pair):
             s = lax.dot_general(k, q[at : at + pair], NT, preferred_element_type=F32)
-            tiles = [s[j * tokens : (j + 1) * tokens] for j in range(count)]
-            last = (e + count - 1) * tokens
-            bound = jnp.where(diagonal, last, e * tokens)
-            tiles[0] = jnp.where(first <= bound, jnp.where(diagonal, tiles.pop(), tiles[0]), MASKED)
-            for j in range(1, count - 1):
-                tiles[j] = jnp.where(first <= (e + j) * tokens, tiles[j], MASKED)
+            tiles = [
+                jnp.where(first <= (e + j) * tokens, s[j * tokens : (j + 1) * tokens], MASKED) for j in range(far)
+            ]
+            tiles += near_tiles(near_ref, e, at, pair)
+            tiles[0] = jnp.where(diagonal, tiles.pop(), tiles[0])
             top = folded(jnp.maximum, functools.reduce(jnp.maximum, tiles))
             tiles = [jnp.exp((tile - top) * dim**-0.5) for tile in tiles]
             inv = 1.0 / folded(jnp.add, functools.reduce(jnp.add, tiles))
             store_tiles(p_ref, e, at, [tile * inv for tile in tiles], diagonal)
-        keep = (2 * halo - e) * tokens
-        dv = jnp.dot(p_ref[0, e, :keep], do, preferred_element_type=F32).reshape(2 * halo - e, tokens, dim)
+        dv = jnp.dot(p_ref[0, e, : far * tokens], do, preferred_element_type=F32).reshape(far, tokens, dim)
         if e == 0:
             acc[...] = dv
         else:
@@ -257,32 +286,38 @@
         ref[0] = acc[pl.ds(2 * (halo - back), 2)].astype(BF16)
 
 
-def dscore_kernel(halo, place_ref, qd_ref, p_ref, *refs):
-    v_refs = refs[: halo + 1]
-    ds_ref = refs[halo + 1]
-    dk_refs = refs[halo + 2 : -2]
+def near_tiles(ref, e, at, pair):
+    tokens = ref.shape[1] // 3
+    return [ref[0, (e + j) * tokens : (e + j + 1) * tokens, at : at + pair] for j in range(e + 1)]
+
+
+def dscore_kernel(halo, place_ref, qd_ref, p_ref, near_ref, *refs):
+    v_refs = refs[:halo]
+    ds_ref = refs[halo]
+    dk_refs = refs[halo + 1 : -2]
     v_scr, acc = refs[-2:]
     _, _, _, group, tokens, dim = qd_ref.shape
     count = 2 * halo + 1
     pair = HEADS_AT_ONCE * tokens
-    window_of(v_refs, v_scr)
     row, lane = on_diagonal(tokens, HEADS_AT_ONCE)
     diagonal = row <= lane
+    window_of(v_refs, v_scr)
     for e in range(2):
-        v = v_scr[pl.ds(e, count)].reshape(count * tokens, dim)
+        far = 2 * halo - e
+        v = v_scr[pl.ds(e, far)].reshape(far * tokens, dim)
         q = qd_ref[0, e, 0].reshape(group * tokens, dim)
         do = qd_ref[0, e, 1].reshape(group * tokens, dim)
         for at in range(0, group * tokens, pair):
             dp = lax.dot_general(v, do[at : at + pair], NT, preferred_element_type=F32)
-            dps = [dp[j * tokens : (j + 1) * tokens] for j in range(count)]
+            dps = [dp[j * tokens : (j + 1) * tokens] for j in range(far)]
+            dps += near_tiles(near_ref, e, at, pair)
             dps[0] = jnp.where(diagonal, dps.pop(), dps[0])
             ps = [p_ref[0, e, j * tokens : (j + 1) * tokens, at : at + pair] for j in range(count)]
             ps[0] += ps.pop()
             ps = [p.astype(F32) for p in ps]
             delta = folded(jnp.add, functools.reduce(jnp.add, [p * dp for p, dp in zip(ps, dps)]))
             store_tiles(ds_ref, e, at, [p * (dp - delta) for p, dp in zip(ps, dps)], diagonal)
-        keep = (2 * halo - e) * tokens
-        dk = jnp.dot(ds_ref[0, e, :keep], q, preferred_element_type=F32).reshape(2 * halo - e, tokens, dim)
+        dk = jnp.dot(ds_ref[0, e, : far * tokens], q, preferred_element_type=F32).reshape(far, tokens, dim)
         if e == 0:
             acc[...] = dk
         else:
@@ -424,9 +459,32 @@
     k_own = pack_other(place, k_other, k_mine)
     k_own, queries, grad_out, v_mine = lax.optimization_barrier((k_own, queries, grad_out, v_mine))
     q_other, do_other, v_other = (swapped(x, device_count) for x in (queries, grad_out, v_mine))
-    qd = arrange(place, in_hbm(queries), in_hbm(grad_out), q_other, do_other, key_heads)
-    qd, v_mine, v_other = lax.optimization_barrier((qd, v_mine, v_other))
+    qd = arrange(place, queries, grad_out, q_other, do_other, key_heads)
     v_own = pack_both(place, v_mine, v_other)
+
+    def per_head(*shape):
+        return pl.BlockSpec((1,) + shape, lambda h, *_: (h,) + (0,) * len(shape))
+
+    qd_spec = per_head(2, 2, group, tokens, dim)
+    pair_spec = per_head(2, tokens, dim)
+    near_spec = per_head(3 * tokens, group * tokens)
+    near_shape = pltpu.VMEM((half, 3 * tokens, group * tokens), F32)
+    firsts = pltpu.VMEM((2, 1, group * tokens), jnp.int32)
+    product = 2 * half * 2 * count * tokens * group * tokens * dim
+
+    s_near, dp_near = call(
+        functools.partial(near_kernel, halo),
+        "near",
+        (half,),
+        (place, doc_lengths),
+        (in_vmem(qd), in_vmem(k_own), in_vmem(v_own)),
+        [qd_spec] + [pair_spec] * 2,
+        [near_shape] * 2,
+        [near_spec] * 2,
+        [firsts],
+        2 * product,
+    )
+    s_near, dp_near, v_own = lax.optimization_barrier((s_near, dp_near, v_own))
 
     def halo_of(own):
         received = {back: moved(own, device_count, 2 * back) for back in far_first}
@@ -435,13 +493,8 @@
     def sent_back(partials):
         return [moved(partials[back - 1], device_count, -2 * back) for back in far_first]
 
-    def per_head(*shape):
-        return pl.BlockSpec((1,) + shape, lambda h, *_: (h,) + (0,) * len(shape))
-
-    qd_spec = per_head(2, 2, group, tokens, dim)
     p_spec = per_head(2, count * tokens, group * tokens)
     p_shape = pltpu.VMEM((half, 2, count * tokens, group * tokens), BF16)
-    pair_spec = per_head(2, tokens, dim)
     pair = (half, 2, tokens, dim)
     one_spec = per_head(tokens, dim)
     one_shape = jax.ShapeDtypeStruct((half, tokens, dim), BF16)
@@ -450,8 +503,8 @@
     dq_part_shape = jax.ShapeDtypeStruct((tokens // 2, heads // 2, dim), BF16)
     dq_part_spec = pl.BlockSpec(dq_part_shape.shape, lambda h, *_: (0, 0, 0))
     run = pltpu.VMEM((window, tokens, dim), BF16)
+    halo_run = pltpu.VMEM((2 * halo, tokens, dim), BF16)
     acc = pltpu.VMEM((2 * halo, tokens, dim), F32)
-    product = 2 * half * 2 * count * tokens * group * tokens * dim
 
     k_pairs = halo_of(k_own)
     v_pairs = halo_of(v_own)
@@ -460,11 +513,11 @@
         "prob",
         (half,),
         (place, doc_lengths),
-        (in_vmem(qd), *k_pairs),
-        [qd_spec] + [pair_spec] * (halo + 1),
+        (in_vmem(qd), in_vmem(s_near), *k_pairs[1:]),
+        [qd_spec, near_spec] + [pair_spec] * halo,
         [p_shape] + [jax.ShapeDtypeStruct(pair, BF16)] * halo,
         [p_spec] + [pair_spec] * halo,
-        [run, acc, pltpu.VMEM((2, 1, HEADS_AT_ONCE * tokens), jnp.int32)],
+        [halo_run, acc, pltpu.VMEM((2, 1, HEADS_AT_ONCE * tokens), jnp.int32)],
         4 * product,
     )
     dv_back = sent_back(dv_halo)
@@ -473,11 +526,11 @@
         "dscore",
         (half,),
         place,
-        (in_vmem(qd), in_vmem(prob), *v_pairs),
-        [qd_spec, p_spec] + [pair_spec] * (halo + 1),
+        (in_vmem(qd), in_vmem(prob), in_vmem(dp_near), *v_pairs[1:]),
+        [qd_spec, p_spec, near_spec] + [pair_spec] * halo,
         [p_shape] + [jax.ShapeDtypeStruct(pair, BF16)] * halo,
         [p_spec] + [pair_spec] * halo,
-        [run, acc],
+        [halo_run, acc],
         4 * product,
     )
     dk_back = sent_back(dk_halo)

time: 62.2 us -> 62.3 us (level)
    pallas_call x9 -> x10, Pallas kernels: 26 us -> 26.2 us  [call(): pl.pallas_call(kernel, out_shape=outs, grid_spec=pltpu.PrefetchScalarGrid...]
  transfers between devices with their start and end apart: 16 -> 16, of which waited for: 2 -> 2; matrix products, arithmetic and copies ran while one was open for 0% -> 0% of each run, Pallas kernels for 37% -> 38%
where the time goes in v10:
time: 62.3 us; the launch traced here: 62 us
  starting transfers between devices  30.7 us (49%)
  Pallas kernels  26.2 us (42%)
  waiting for transfers between devices  4.08 us (7%)
  between operations  0.87 us (1%)
    pallas_call x10, Pallas kernels, call(): pl.pallas_call(kernel, out_shape=outs, grid_spec=pltpu.PrefetchScalarGrid...  26.2 us
    ppermute x8, starting transfers between devices, moved(): return lax.ppermute(array, AXES, pairs)  22.9 us
    ppermute x8, starting transfers between devices, swapped(): return lax.ppermute(array, AXES, [(d, d ^ 1) for d in range(device_count)])  7.83 us
    ppermute x8, waiting for transfers between devices, moved(): return lax.ppermute(array, AXES, pairs)  3.08 us
  transfers between devices with their start and end apart: 16, of which 2 were waited for; matrix products, arithmetic and copies ran while one was open for 0% of the time, Pallas kernels for 38%

profile of v10, /device:TPU:23, one launch (start us, length us, event | category | flops | bytes accessed | tf_op | source)
XLA Modules:
  0.0 62.0 jit_solution(18204384483844166261)
XLA Ops:
  0.6 0.7 %collective-permute-start = (bf16[128,8,128]{2,1,0:T(8,128)(2,1)}, bf16[128,8,128]{2,1,0:T(8,128)(2,1)S(1)}, u32[]{:S(2)}, u32[]{:S(2)}) collective-permute-start(bf16[128,8,128]{2,1,0:T(8,128)(2,1)} %key_ref.1), channel_id=1, source_target_pairs={{0,1},{1,0},{2,3},{3,2},{4,5},{5,4},{6,7},{7,6},{8,9},{9,8},{10,11... | collective-permute-start | bytes 786440 | tf_op jit(solution)/shard_map/ppermute | solution.py:24
  1.4 0.1 pad_add_fusion.place_ref
  1.4 1.7 %fetch.1 = (bf16[4,2,128,128]{3,2,1,0:T(8,128)(2,1)S(1)}, bf16[128,8,128]{2,1,0:T(8,128)(2,1)S(1)}) custom-call(s32[2]{0:T(128)S(1)} %pad_add_fusion.place_ref, bf16[128,8,128]{2,1,0:T(8,128)(2,1)} %key_ref.1, bf16[128,8,128]{2,1,0:T(8,128)(2,1)} %refs_0_.1), custom_call_target="tpu_custom_call" | custom-call | flops 1000000000 | tf_op jit(solution)/shard_map/fetch/pallas_call | solution.py:37
  3.1 0.0 collective-permute-done.other_ref
  3.1 0.6 %pack_other.1.k_ref.refs_0_ = bf16[4,2,128,128]{3,2,1,0:T(8,128)(2,1)S(1)} custom-call(s32[2]{0:T(128)S(1)} %pad_add_fusion.place_ref, bf16[128,8,128]{2,1,0:T(8,128)(2,1)S(1)} %collective-permute-done.other_ref, bf16[4,2,128,128]{3,2,1,0:T(8,128)(2,1)S(1)} %get-tuple-element.28._), custom_call_target="tpu_custom_call", output_to_operand_aliasing={{}: (2, {})} | custom-call | flops 1000000000 | tf_op jit(solution)/shard_map/pack_other/pallas_call | solution.py:37
  3.8 0.1 collective-permute-start.1
  3.9 0.5 collective-permute-start.2
  4.4 0.1 collective-permute-start.3
  4.4 3.1 %collective-permute-start.5 = (bf16[4,2,128,128]{3,2,1,0:T(8,128)(2,1)S(1)}, bf16[4,2,128,128]{3,2,1,0:T(8,128)(2,1)S(1)}, u32[]{:S(2)}, u32[]{:S(2)}) collective-permute-start(bf16[4,2,128,128]{3,2,1,0:T(8,128)(2,1)S(1)} %pack_other.1.k_ref.refs_0_), channel_id=1, source_target_pairs={{0,4},{1,5},{2,6},{3,7},{4,8},{5,9},{6,10},{7,11},{8,12},{9,13},{1... | collective-permute-start | bytes 786440 | tf_op jit(solution)/shard_map/ppermute | solution.py:20
  7.6 3.1 %collective-permute-start.4 = (bf16[4,2,128,128]{3,2,1,0:T(8,128)(2,1)S(1)}, bf16[4,2,128,128]{3,2,1,0:T(8,128)(2,1)S(1)}, u32[]{:S(2)}, u32[]{:S(2)}) collective-permute-start(bf16[4,2,128,128]{3,2,1,0:T(8,128)(2,1)S(1)} %pack_other.1.k_ref.refs_0_), channel_id=1, source_target_pairs={{0,2},{1,3},{2,4},{3,5},{4,6},{5,7},{6,8},{7,9},{8,10},{9,11},{10,... | collective-permute-start | bytes 786440 | tf_op jit(solution)/shard_map/ppermute | solution.py:20
  10.7 0.7 %pack_both.1.v_ref = bf16[4,2,128,128]{3,2,1,0:T(8,128)(2,1)S(1)} custom-call(s32[2]{0:T(128)S(1)} %pad_add_fusion.place_ref, bf16[128,8,128]{2,1,0:T(8,128)(2,1)S(1)} %get-tuple-element.33.own_ref, bf16[128,8,128]{2,1,0:T(8,128)(2,1)S(1)} %collective-permute-done.3.other_ref), custom_call_target="tpu_custom_call" | custom-call | flops 1000000000 | tf_op jit(solution)/shard_map/pack_both/pallas_call | solution.py:37
  11.4 0.0 copy-start.2
  11.5 0.0 collective-permute-done.2.do_other_ref
  11.5 2.0 %arrange.1.qd_ref = bf16[4,2,2,4,128,128]{5,4,3,2,1,0:T(8,128)(2,1)S(1)} custom-call(s32[2]{0:T(128)S(1)} %pad_add_fusion.place_ref, bf16[128,32,128]{2,1,0:T(8,128)(2,1)S(1)} %copy-done, bf16[128,32,128]{2,1,0:T(8,128)(2,1)S(1)} %copy-done.1, bf16[128,32,128]{2,1,0:T(8,128)(2,1)S(1)} %collective-permute-done.1.q_other_ref, ...), custom_call_target="tpu_custom_call" | custom-call | flops 1000000000 | tf_op jit(solution)/shard_map/arrange/pallas_call | solution.py:37
  13.5 2.2 %near.1 = (f32[4,384,512]{2,1,0:T(8,128)S(1)}, f32[4,384,512]{2,1,0:T(8,128)S(1)}) custom-call(s32[2]{0:T(128)S(1)} %pad_add_fusion.place_ref, s32[16]{0:T(128)S(1)} %copy-done.2, bf16[4,2,2,4,128,128]{5,4,3,2,1,0:T(8,128)(2,1)S(1)} %arrange.1.qd_ref, bf16[4,2,128,128]{3,2,1,0:T(8,128)(2,1)S(1)} %pack_other.1.k_ref.refs_0_, ...), custom_call_target="tpu_custom_call" | custom-call | flops 1342177280 | tf_op jit(solution)/shard_map/near/pallas_call | solution.py:37
  15.8 1.9 %collective-permute-start.7 = (bf16[4,2,128,128]{3,2,1,0:T(8,128)(2,1)S(1)}, bf16[4,2,128,128]{3,2,1,0:T(8,128)(2,1)S(1)}, u32[]{:S(2)}, u32[]{:S(2)}) collective-permute-start(bf16[4,2,128,128]{3,2,1,0:T(8,128)(2,1)S(1)} %pack_both.1.v_ref), channel_id=1, source_target_pairs={{0,4},{1,5},{2,6},{3,7},{4,8},{5,9},{6,10},{7,11},{8,12},{9,13},{1... | collective-permute-start | bytes 786440 | tf_op jit(solution)/shard_map/ppermute | solution.py:20
  17.7 3.1 %collective-permute-start.6 = (bf16[4,2,128,128]{3,2,1,0:T(8,128)(2,1)S(1)}, bf16[4,2,128,128]{3,2,1,0:T(8,128)(2,1)S(1)}, u32[]{:S(2)}, u32[]{:S(2)}) collective-permute-start(bf16[4,2,128,128]{3,2,1,0:T(8,128)(2,1)S(1)} %pack_both.1.v_ref), channel_id=1, source_target_pairs={{0,2},{1,3},{2,4},{3,5},{4,6},{5,7},{6,8},{7,9},{8,10},{9,11},{10,... | collective-permute-start | bytes 786440 | tf_op jit(solution)/shard_map/ppermute | solution.py:20
  20.8 6.8 %prob.1 = (bf16[4,2,640,512]{3,2,1,0:T(8,128)(2,1)S(1)}, bf16[4,2,128,128]{3,2,1,0:T(8,128)(2,1)S(1)}, bf16[4,2,128,128]{3,2,1,0:T(8,128)(2,1)S(1)}) custom-call(s32[2]{0:T(128)S(1)} %pad_add_fusion.place_ref, s32[16]{0:T(128)S(1)} %copy-done.2, bf16[4,2,2,4,128,128]{5,4,3,2,1,0:T(8,128)(2,1)S(1)} %arrange.1.qd_ref, ...), custom_call_target="tpu_custom_call" | custom-call | flops 2684354560 | tf_op jit(solution)/shard_map/prob/pallas_call | solution.py:37
  27.7 3.4 %collective-permute-start.8 = (bf16[4,2,128,128]{3,2,1,0:T(8,128)(2,1)S(1)}, bf16[4,2,128,128]{3,2,1,0:T(8,128)(2,1)S(1)}, u32[]{:S(2)}, u32[]{:S(2)}) collective-permute-start(bf16[4,2,128,128]{3,2,1,0:T(8,128)(2,1)S(1)} %get-tuple-element.41), channel_id=1, source_target_pairs={{4,0},{5,1},{6,2},{7,3},{8,4},{9,5},{10,6},{11,7},{12,8},{13,9},{1... | collective-permute-start | bytes 786440 | tf_op jit(solution)/shard_map/ppermute | solution.py:20
  31.0 2.2 %collective-permute-start.9 = (bf16[4,2,128,128]{3,2,1,0:T(8,128)(2,1)S(1)}, bf16[4,2,128,128]{3,2,1,0:T(8,128)(2,1)S(1)}, u32[]{:S(2)}, u32[]{:S(2)}) collective-permute-start(bf16[4,2,128,128]{3,2,1,0:T(8,128)(2,1)S(1)} %get-tuple-element.42), channel_id=1, source_target_pairs={{2,0},{3,1},{4,2},{5,3},{6,4},{7,5},{8,6},{9,7},{10,8},{11,9},{12,... | collective-permute-start | bytes 786440 | tf_op jit(solution)/shard_map/ppermute | solution.py:20
  33.2 5.8 %dscore.1 = (bf16[4,2,640,512]{3,2,1,0:T(8,128)(2,1)S(1)}, bf16[4,2,128,128]{3,2,1,0:T(8,128)(2,1)S(1)}, bf16[4,2,128,128]{3,2,1,0:T(8,128)(2,1)S(1)}) custom-call(s32[2]{0:T(128)S(1)} %pad_add_fusion.place_ref, bf16[4,2,2,4,128,128]{5,4,3,2,1,0:T(8,128)(2,1)S(1)} %arrange.1.qd_ref, bf16[4,2,640,512]{3,2,1,0:T(8,128)(2,1)S(1)} %get-tuple-element.37.p_ref, ...), custom_call_target="tpu_custom_call" | custom-call | flops 2684354560 | tf_op jit(solution)/shard_map/dscore/pallas_call | solution.py:37
  39.1 3.0 %collective-permute-start.12 = (bf16[4,2,128,128]{3,2,1,0:T(8,128)(2,1)S(1)}, bf16[4,2,128,128]{3,2,1,0:T(8,128)(2,1)S(1)}, u32[]{:S(2)}, u32[]{:S(2)}) collective-permute-start(bf16[4,2,128,128]{3,2,1,0:T(8,128)(2,1)S(1)} %get-tuple-element.47), channel_id=1, source_target_pairs={{4,0},{5,1},{6,2},{7,3},{8,4},{9,5},{10,6},{11,7},{12,8},{13,9},{1... | collective-permute-start | bytes 786440 | tf_op jit(solution)/shard_map/ppermute | solution.py:20
  42.1 3.1 %collective-permute-start.13 = (bf16[4,2,128,128]{3,2,1,0:T(8,128)(2,1)S(1)}, bf16[4,2,128,128]{3,2,1,0:T(8,128)(2,1)S(1)}, u32[]{:S(2)}, u32[]{:S(2)}) collective-permute-start(bf16[4,2,128,128]{3,2,1,0:T(8,128)(2,1)S(1)} %get-tuple-element.48), channel_id=1, source_target_pairs={{2,0},{3,1},{4,2},{5,3},{6,4},{7,5},{8,6},{9,7},{10,8},{11,9},{12,... | collective-permute-start | bytes 786440 | tf_op jit(solution)/shard_map/ppermute | solution.py:20
  45.2 3.3 %own.1 = (bf16[128,16,128]{2,1,0:T(8,128)(2,1)S(1)}, bf16[64,16,128]{2,1,0:T(8,128)(2,1)S(1)}, bf16[64,16,128]{2,1,0:T(8,128)(2,1)S(1)}, f32[4,2,128,128]{3,2,1,...) custom-call(s32[2]{0:T(128)S(1)} %pad_add_fusion.place_ref, ...), custom_call_target="tpu_custom_call" | custom-call | tf_op jit(solution)/shard_map/own/pallas_call | solution.py:37
  48.6 2.8 %collective-permute-start.10 = (bf16[64,16,128]{2,1,0:T(8,128)(2,1)S(1)}, bf16[64,16,128]{2,1,0:T(8,128)(2,1)S(1)}, u32[]{:S(2)}, u32[]{:S(2)}) collective-permute-start(bf16[64,16,128]{2,1,0:T(8,128)(2,1)S(1)} %get-tuple-element.44), channel_id=1, source_target_pairs={{0,1},{1,0},{2,3},{3,2},{4,5},{5,4},{6,7},{7,6},{8,9},{9,8},{10,11... | collective-permute-start | bytes 786440 | tf_op jit(solution)/shard_map/ppermute | solution.py:24
  51.3 0.1 collective-permute-start.11
  51.4 0.4 collective-permute-start.15
  51.8 3.1 %collective-permute-done.13.refs_1_ = bf16[4,2,128,128]{3,2,1,0:T(8,128)(2,1)S(1)} collective-permute-done((bf16[4,2,128,128]{3,2,1,0:T(8,128)(2,1)S(1)}, bf16[4,2,128,128]{3,2,1,0:T(8,128)(2,1)S(1)}, u32[]{:S(2)}, u32[]{:S(2)}) %collective-permute-start.13) | collective-permute-done | bytes 262176 | tf_op jit(solution)/shard_map/ppermute | solution.py:20
  54.9 0.6 %sum_dk.1 = (bf16[4,128,128]{2,1,0:T(8,128)(2,1)S(1)}, bf16[4,128,128]{2,1,0:T(8,128)(2,1)S(1)}) custom-call(s32[2]{0:T(128)S(1)} %pad_add_fusion.place_ref, f32[4,2,128,128]{3,2,1,0:T(8,128)S(1)} %get-tuple-element.46.own_ref, bf16[4,2,128,128]{3,2,1,0:T(8,128)(2,1)S(1)} %collective-permute-done.12.refs_0_, ...), custom_call_target="tpu_custom_call" | custom-call | tf_op jit(solution)/shard_map/sum_dk/pallas_call | solution.py:37
  55.5 3.1 %collective-permute-start.14 = (bf16[4,128,128]{2,1,0:T(8,128)(2,1)S(1)}, bf16[4,128,128]{2,1,0:T(8,128)(2,1)S(1)}, u32[]{:S(2)}, u32[]{:S(2)}) collective-permute-start(bf16[4,128,128]{2,1,0:T(8,128)(2,1)S(1)} %get-tuple-element.50), channel_id=1, source_target_pairs={{0,1},{1,0},{2,3},{3,2},{4,5},{5,4},{6,7},{7,6},{8,9},{9,8},{10,11... | collective-permute-start | bytes 393224 | tf_op jit(solution)/shard_map/ppermute | solution.py:24
  58.7 1.0 %collective-permute-done.14.refs_4_ = bf16[4,128,128]{2,1,0:T(8,128)(2,1)S(1)} collective-permute-done((bf16[4,128,128]{2,1,0:T(8,128)(2,1)S(1)}, bf16[4,128,128]{2,1,0:T(8,128)(2,1)S(1)}, u32[]{:S(2)}, u32[]{:S(2)}) %collective-permute-start.14) | collective-permute-done | bytes 131104 | tf_op jit(solution)/shard_map/ppermute | solution.py:24
  59.7 2.3 %finish.1 = (bf16[128,32,128]{2,1,0:T(8,128)(2,1)}, bf16[128,8,128]{2,1,0:T(8,128)(2,1)}, bf16[128,8,128]{2,1,0:T(8,128)(2,1)}) custom-call(s32[2]{0:T(128)S(1)} %pad_add_fusion.place_ref, bf16[128,16,128]{2,1,0:T(8,128)(2,1)S(1)} %get-tuple-element.43.refs_0_, bf16[64,16,128]{2,1,0:T(8,128)(2,1)S(1)} %collective-permute-done.10.refs_1_, ...), custom_call_target="tpu_custom_call" | custom-call | tf_op jit(solution)/shard_map/finish/pallas_call | solution.py:37
  (17 shorter events, 0.0 us)
Async XLA Ops:
  0.6 2.5 %collective-permute-start = (bf16[128,8,128]{2,1,0:T(8,128)(2,1)}, bf16[128,8,128]{2,1,0:T(8,128)(2,1)S(1)}, u32[]{:S(2)}, u32[]{:S(2)}) collective-permute-start(bf16[128,8,128]{2,1,0:T(8,128)(2,1)} %key_ref.1), channel_id=1, source_target_pairs={{0,1},{1,0},{2,3},{3,2},{4,5},{5,4},{6,7},{7,6},{8,9},{9,8},{10,11... | collective-permute-start | bytes 786440 | tf_op jit(solution)/shard_map/ppermute | solution.py:24
  1.4 2.3 %copy-start = (bf16[128,32,128]{2,1,0:T(8,128)(2,1)S(1)}, bf16[128,32,128]{2,1,0:T(8,128)(2,1)}, u32[]{:S(2)}) copy-start(bf16[128,32,128]{2,1,0:T(8,128)(2,1)} %q_ref) | copy-start | bytes 3145732
  1.4 2.4 %copy-start.1 = (bf16[128,32,128]{2,1,0:T(8,128)(2,1)S(1)}, bf16[128,32,128]{2,1,0:T(8,128)(2,1)}, u32[]{:S(2)}) copy-start(bf16[128,32,128]{2,1,0:T(8,128)(2,1)} %do_ref) | copy-start | bytes 3145732
  3.8 7.7 %collective-permute-start.1 = (bf16[128,32,128]{2,1,0:T(8,128)(2,1)S(1)}, bf16[128,32,128]{2,1,0:T(8,128)(2,1)S(1)}, u32[]{:S(2)}, u32[]{:S(2)}) collective-permute-start(bf16[128,32,128]{2,1,0:T(8,128)(2,1)S(1)} %copy-done), channel_id=1, source_target_pairs={{0,1},{1,0},{2,3},{3,2},{4,5},{5,4},{6,7},{7,6},{8,9},{9,8},{10,11... | collective-permute-start | bytes 3145736 | tf_op jit(solution)/shard_map/ppermute | solution.py:24
  3.9 7.6 %collective-permute-start.2 = (bf16[128,32,128]{2,1,0:T(8,128)(2,1)S(1)}, bf16[128,32,128]{2,1,0:T(8,128)(2,1)S(1)}, u32[]{:S(2)}, u32[]{:S(2)}) collective-permute-start(bf16[128,32,128]{2,1,0:T(8,128)(2,1)S(1)} %copy-done.1), channel_id=1, source_target_pairs={{0,1},{1,0},{2,3},{3,2},{4,5},{5,4},{6,7},{7,6},{8,9},{9,8},{10,11... | collective-permute-start | bytes 3145736 | tf_op jit(solution)/shard_map/ppermute | solution.py:24
  4.4 6.4 %collective-permute-start.3 = (bf16[128,8,128]{2,1,0:T(8,128)(2,1)S(1)}, bf16[128,8,128]{2,1,0:T(8,128)(2,1)S(1)}, u32[]{:S(2)}, u32[]{:S(2)}) collective-permute-start(bf16[128,8,128]{2,1,0:T(8,128)(2,1)S(1)} %get-tuple-element.33.own_ref), channel_id=1, source_target_pairs={{0,1},{1,0},{2,3},{3,2},{4,5},{5,4},{6,7},{7,6},{8,9},{9,8},{10,11... | collective-permute-start | bytes 786440 | tf_op jit(solution)/shard_map/ppermute | solution.py:24
  4.4 16.4 %collective-permute-start.5 = (bf16[4,2,128,128]{3,2,1,0:T(8,128)(2,1)S(1)}, bf16[4,2,128,128]{3,2,1,0:T(8,128)(2,1)S(1)}, u32[]{:S(2)}, u32[]{:S(2)}) collective-permute-start(bf16[4,2,128,128]{3,2,1,0:T(8,128)(2,1)S(1)} %pack_other.1.k_ref.refs_0_), channel_id=1, source_target_pairs={{0,4},{1,5},{2,6},{3,7},{4,8},{5,9},{6,10},{7,11},{8,12},{9,13},{1... | collective-permute-start | bytes 786440 | tf_op jit(solution)/shard_map/ppermute | solution.py:20
  7.6 13.2 %collective-permute-start.4 = (bf16[4,2,128,128]{3,2,1,0:T(8,128)(2,1)S(1)}, bf16[4,2,128,128]{3,2,1,0:T(8,128)(2,1)S(1)}, u32[]{:S(2)}, u32[]{:S(2)}) collective-permute-start(bf16[4,2,128,128]{3,2,1,0:T(8,128)(2,1)S(1)} %pack_other.1.k_ref.refs_0_), channel_id=1, source_target_pairs={{0,2},{1,3},{2,4},{3,5},{4,6},{5,7},{6,8},{7,9},{8,10},{9,11},{10,... | collective-permute-start | bytes 786440 | tf_op jit(solution)/shard_map/ppermute | solution.py:20
  11.4 2.1 %copy-start.2 = (s32[16]{0:T(128)S(1)}, s32[16]{0:T(128)}, u32[]{:S(2)}) copy-start(s32[16]{0:T(128)} %lengths_ref.3) | copy-start | bytes 196
  15.8 17.4 %collective-permute-start.7 = (bf16[4,2,128,128]{3,2,1,0:T(8,128)(2,1)S(1)}, bf16[4,2,128,128]{3,2,1,0:T(8,128)(2,1)S(1)}, u32[]{:S(2)}, u32[]{:S(2)}) collective-permute-start(bf16[4,2,128,128]{3,2,1,0:T(8,128)(2,1)S(1)} %pack_both.1.v_ref), channel_id=1, source_target_pairs={{0,4},{1,5},{2,6},{3,7},{4,8},{5,9},{6,10},{7,11},{8,12},{9,13},{1... | collective-permute-start | bytes 786440 | tf_op jit(solution)/shard_map/ppermute | solution.py:20
  17.7 15.5 %collective-permute-start.6 = (bf16[4,2,128,128]{3,2,1,0:T(8,128)(2,1)S(1)}, bf16[4,2,128,128]{3,2,1,0:T(8,128)(2,1)S(1)}, u32[]{:S(2)}, u32[]{:S(2)}) collective-permute-start(bf16[4,2,128,128]{3,2,1,0:T(8,128)(2,1)S(1)} %pack_both.1.v_ref), channel_id=1, source_target_pairs={{0,2},{1,3},{2,4},{3,5},{4,6},{5,7},{6,8},{7,9},{8,10},{9,11},{10,... | collective-permute-start | bytes 786440 | tf_op jit(solution)/shard_map/ppermute | solution.py:20
  27.7 17.5 %collective-permute-start.8 = (bf16[4,2,128,128]{3,2,1,0:T(8,128)(2,1)S(1)}, bf16[4,2,128,128]{3,2,1,0:T(8,128)(2,1)S(1)}, u32[]{:S(2)}, u32[]{:S(2)}) collective-permute-start(bf16[4,2,128,128]{3,2,1,0:T(8,128)(2,1)S(1)} %get-tuple-element.41), channel_id=1, source_target_pairs={{4,0},{5,1},{6,2},{7,3},{8,4},{9,5},{10,6},{11,7},{12,8},{13,9},{1... | collective-permute-start | bytes 786440 | tf_op jit(solution)/shard_map/ppermute | solution.py:20
  31.0 14.2 %collective-permute-start.9 = (bf16[4,2,128,128]{3,2,1,0:T(8,128)(2,1)S(1)}, bf16[4,2,128,128]{3,2,1,0:T(8,128)(2,1)S(1)}, u32[]{:S(2)}, u32[]{:S(2)}) collective-permute-start(bf16[4,2,128,128]{3,2,1,0:T(8,128)(2,1)S(1)} %get-tuple-element.42), channel_id=1, source_target_pairs={{2,0},{3,1},{4,2},{5,3},{6,4},{7,5},{8,6},{9,7},{10,8},{11,9},{12,... | collective-permute-start | bytes 786440 | tf_op jit(solution)/shard_map/ppermute | solution.py:20
  39.1 12.8 %collective-permute-start.12 = (bf16[4,2,128,128]{3,2,1,0:T(8,128)(2,1)S(1)}, bf16[4,2,128,128]{3,2,1,0:T(8,128)(2,1)S(1)}, u32[]{:S(2)}, u32[]{:S(2)}) collective-permute-start(bf16[4,2,128,128]{3,2,1,0:T(8,128)(2,1)S(1)} %get-tuple-element.47), channel_id=1, source_target_pairs={{4,0},{5,1},{6,2},{7,3},{8,4},{9,5},{10,6},{11,7},{12,8},{13,9},{1... | collective-permute-start | bytes 786440 | tf_op jit(solution)/shard_map/ppermute | solution.py:20
  42.1 12.8 %collective-permute-start.13 = (bf16[4,2,128,128]{3,2,1,0:T(8,128)(2,1)S(1)}, bf16[4,2,128,128]{3,2,1,0:T(8,128)(2,1)S(1)}, u32[]{:S(2)}, u32[]{:S(2)}) collective-permute-start(bf16[4,2,128,128]{3,2,1,0:T(8,128)(2,1)S(1)} %get-tuple-element.48), channel_id=1, source_target_pairs={{2,0},{3,1},{4,2},{5,3},{6,4},{7,5},{8,6},{9,7},{10,8},{11,9},{12,... | collective-permute-start | bytes 786440 | tf_op jit(solution)/shard_map/ppermute | solution.py:20
  48.6 10.1 %collective-permute-start.10 = (bf16[64,16,128]{2,1,0:T(8,128)(2,1)S(1)}, bf16[64,16,128]{2,1,0:T(8,128)(2,1)S(1)}, u32[]{:S(2)}, u32[]{:S(2)}) collective-permute-start(bf16[64,16,128]{2,1,0:T(8,128)(2,1)S(1)} %get-tuple-element.44), channel_id=1, source_target_pairs={{0,1},{1,0},{2,3},{3,2},{4,5},{5,4},{6,7},{7,6},{8,9},{9,8},{10,11... | collective-permute-start | bytes 786440 | tf_op jit(solution)/shard_map/ppermute | solution.py:24
  51.3 7.4 %collective-permute-start.11 = (bf16[64,16,128]{2,1,0:T(8,128)(2,1)S(1)}, bf16[64,16,128]{2,1,0:T(8,128)(2,1)S(1)}, u32[]{:S(2)}, u32[]{:S(2)}) collective-permute-start(bf16[64,16,128]{2,1,0:T(8,128)(2,1)S(1)} %get-tuple-element.45), channel_id=1, source_target_pairs={{0,1},{1,0},{2,3},{3,2},{4,5},{5,4},{6,7},{7,6},{8,9},{9,8},{10,11... | collective-permute-start | bytes 786440 | tf_op jit(solution)/shard_map/ppermute | solution.py:24
  51.4 7.3 %collective-permute-start.15 = (bf16[4,128,128]{2,1,0:T(8,128)(2,1)S(1)}, bf16[4,128,128]{2,1,0:T(8,128)(2,1)S(1)}, u32[]{:S(2)}, u32[]{:S(2)}) collective-permute-start(bf16[4,128,128]{2,1,0:T(8,128)(2,1)S(1)} %get-tuple-element.52), channel_id=1, source_target_pairs={{0,1},{1,0},{2,3},{3,2},{4,5},{5,4},{6,7},{7,6},{8,9},{9,8},{10,11... | collective-permute-start | bytes 393224 | tf_op jit(solution)/shard_map/ppermute | solution.py:24
  55.5 4.1 %collective-permute-start.14 = (bf16[4,128,128]{2,1,0:T(8,128)(2,1)S(1)}, bf16[4,128,128]{2,1,0:T(8,128)(2,1)S(1)}, u32[]{:S(2)}, u32[]{:S(2)}) collective-permute-start(bf16[4,128,128]{2,1,0:T(8,128)(2,1)S(1)} %get-tuple-element.50), channel_id=1, source_target_pairs={{0,1},{1,0},{2,3},{3,2},{4,5},{5,4},{6,7},{7,6},{8,9},{9,8},{10,11... | collective-permute-start | bytes 393224 | tf_op jit(solution)/shard_map/ppermute | solution.py:24

commit v11 on v8

--- a/solution.py
+++ b/solution.py
@@ -9,7 +9,8 @@
 
 AXES = ("ctx", "uly")
 MASKED = -1e30
-HEADS_AT_ONCE = 4
+LOG2E = 1.4426950408889634
+HEADS_AT_ONCE = 2
 BF16, F32 = jnp.bfloat16, jnp.float32
 NT = (((1,), (1,)), ((), ()))
 VMEM_BYTES = 16 * 2**20
@@ -53,31 +54,34 @@
 
 def arrange_kernel(group, place_ref, q_ref, do_ref, q_other_ref, do_other_ref, out_ref, scr):
     core = place_ref[0]
-    rows, heads, dim = q_ref.shape
+    tokens, heads, dim = q_ref.shape
+    half = heads // 2
+    mine = pl.ds(pl.multiple_of(core * half, half), half)
+    turn = 0
     for kind, (own, other) in enumerate([(q_ref, q_other_ref), (do_ref, do_other_ref)]):
         for which, ref in enumerate([own, other]):
             block = 1 - core if which else core
-            scr[...] = ref[...].astype(F32).reshape(rows * heads, dim)
-            for h in range(heads):
-                out_ref[h // group, block, kind, h % group] = scr[pl.ds(h, rows, stride=heads), :].astype(BF16)
+            wide = scr.at[turn % 2]
+            wide[...] = ref[:, mine].astype(F32).reshape(tokens * half, dim)
+            for h in range(half):
+                out_ref[h // group, block, kind, h % group] = wide[pl.ds(h, tokens, stride=half), :].astype(BF16)
+            turn += 1
 
 
 def arrange(place, queries, grad_out, q_other, do_other, key_heads):
     tokens, heads, dim = queries.shape
     half, group = heads // 2, heads // key_heads
-    rows = 32
-    in_spec = pl.BlockSpec((rows, half, dim), lambda i, place: (i, place[0], 0))
-    out = (key_heads // 2, 2, 2, group, tokens, dim)
+    whole = pl.BlockSpec(memory_space=pltpu.VMEM)
     return call(
         functools.partial(arrange_kernel, group),
         "arrange",
-        (tokens // rows,),
-        place,
-        (queries, grad_out, q_other, do_other),
-        [in_spec] * 4,
-        pltpu.VMEM(out, BF16),
-        pl.BlockSpec(out[:4] + (rows, dim), lambda i, place: (0, 0, 0, 0, i, 0)),
-        [pltpu.VMEM((rows * half, dim), F32)],
+        (1,),
+        place,
+        [in_vmem(x) for x in (queries, grad_out, q_other, do_other)],
+        [whole] * 4,
+        pltpu.VMEM((key_heads // 2, 2, 2, group, tokens, dim), BF16),
+        whole,
+        [pltpu.VMEM((2, tokens * half, dim), F32)],
         10**9,
     )
 
@@ -214,8 +218,8 @@
 
 def prob_kernel(halo, place_ref, lengths_ref, qd_ref, *refs):
     k_refs = refs[: halo + 1]
-    p_ref = refs[halo + 1]
-    dv_refs = refs[halo + 2 : -3]
+    w_ref, inv_ref, do_ref = refs[halo + 1 : halo + 4]
+    dv_refs = refs[halo + 4 : -3]
     k_scr, acc, firsts = refs[-3:]
     _, _, _, group, tokens, dim = qd_ref.shape
     count = 2 * halo + 1
@@ -234,7 +238,6 @@
         first = firsts[e] - row
         k = k_scr[pl.ds(e, count)].reshape(count * tokens, dim)
         q = qd_ref[0, e, 0].reshape(group * tokens, dim)
-        do = qd_ref[0, e, 1].reshape(group * tokens, dim)
         for at in range(0, group * tokens, pair):
             s = lax.dot_general(k, q[at : at + pair], NT, preferred_element_type=F32)
             tiles = [s[j * tokens : (j + 1) * tokens] for j in range(count)]
@@ -244,11 +247,16 @@
             for j in range(1, count - 1):
                 tiles[j] = jnp.where(first <= (e + j) * tokens, tiles[j], MASKED)
             top = folded(jnp.maximum, functools.reduce(jnp.maximum, tiles))
-            tiles = [jnp.exp((tile - top) * dim**-0.5) for tile in tiles]
+            tiles = [jnp.exp2((tile - top) * (dim**-0.5 * LOG2E)) for tile in tiles]
+            store_tiles(w_ref, e, at, tiles, diagonal)
             inv = 1.0 / folded(jnp.add, functools.reduce(jnp.add, tiles))
-            store_tiles(p_ref, e, at, [tile * inv for tile in tiles], diagonal)
+            inv_ref[0, e, :, at : at + pair] = inv
+            for g in range(at // tokens, (at + pair) // tokens):
+                of_row = jnp.broadcast_to(inv[:, g * tokens - at : (g + 1) * tokens - at], (dim, tokens)).T
+                do_ref[0, e, g] = (qd_ref[0, e, 1, g].astype(F32) * of_row).astype(BF16)
+        do = do_ref[0, e].reshape(group * tokens, dim)
         keep = (2 * halo - e) * tokens
-        dv = jnp.dot(p_ref[0, e, :keep], do, preferred_element_type=F32).reshape(2 * halo - e, tokens, dim)
+        dv = jnp.dot(w_ref[0, e, :keep], do, preferred_element_type=F32).reshape(2 * halo - e, tokens, dim)
         if e == 0:
             acc[...] = dv
         else:
@@ -257,7 +265,7 @@
         ref[0] = acc[pl.ds(2 * (halo - back), 2)].astype(BF16)
 
 
-def dscore_kernel(halo, place_ref, qd_ref, p_ref, *refs):
+def dscore_kernel(halo, place_ref, qd_ref, w_ref, inv_ref, do_ref, *refs):
     v_refs = refs[: halo + 1]
     ds_ref = refs[halo + 1]
     dk_refs = refs[halo + 2 : -2]
@@ -265,22 +273,23 @@
     _, _, _, group, tokens, dim = qd_ref.shape
     count = 2 * halo + 1
     pair = HEADS_AT_ONCE * tokens
-    window_of(v_refs, v_scr)
     row, lane = on_diagonal(tokens, HEADS_AT_ONCE)
     diagonal = row <= lane
+    window_of(v_refs, v_scr)
     for e in range(2):
         v = v_scr[pl.ds(e, count)].reshape(count * tokens, dim)
         q = qd_ref[0, e, 0].reshape(group * tokens, dim)
-        do = qd_ref[0, e, 1].reshape(group * tokens, dim)
+        do = do_ref[0, e].reshape(group * tokens, dim)
         for at in range(0, group * tokens, pair):
             dp = lax.dot_general(v, do[at : at + pair], NT, preferred_element_type=F32)
             dps = [dp[j * tokens : (j + 1) * tokens] for j in range(count)]
             dps[0] = jnp.where(diagonal, dps.pop(), dps[0])
-            ps = [p_ref[0, e, j * tokens : (j + 1) * tokens, at : at + pair] for j in range(count)]
-            ps[0] += ps.pop()
-            ps = [p.astype(F32) for p in ps]
-            delta = folded(jnp.add, functools.reduce(jnp.add, [p * dp for p, dp in zip(ps, dps)]))
-            store_tiles(ds_ref, e, at, [p * (dp - delta) for p, dp in zip(ps, dps)], diagonal)
+            ws = [w_ref[0, e, j * tokens : (j + 1) * tokens, at : at + pair] for j in range(count)]
+            ws[0] += ws.pop()
+            ws = [w.astype(F32) for w in ws]
+            delta = folded(jnp.add, functools.reduce(jnp.add, [w * dp for w, dp in zip(ws, dps)]))
+            delta = delta * inv_ref[0, e, :, at : at + pair]
+            store_tiles(ds_ref, e, at, [w * (dp - delta) for w, dp in zip(ws, dps)], diagonal)
         keep = (2 * halo - e) * tokens
         dk = jnp.dot(ds_ref[0, e, :keep], q, preferred_element_type=F32).reshape(2 * halo - e, tokens, dim)
         if e == 0:
@@ -291,7 +300,7 @@
         ref[0] = (acc[pl.ds(2 * (halo - back), 2)] * dim**-0.5).astype(BF16)
 
 
-def own_kernel(halo, place_ref, qd_ref, p_ref, ds_ref, *refs):
+def own_kernel(halo, place_ref, qd_ref, w_ref, do_ref, ds_ref, *refs):
     k_refs, back_refs = refs[: halo + 1], refs[halo + 1 : 2 * halo + 1]
     dq_ref, *dq_other_refs, dk_ref, dv_ref, dv_other_ref, k_scr, dq_scr, dv_scr = refs[2 * halo + 1 :]
     core, head = place_ref[0], pl.program_id(0)
@@ -302,14 +311,14 @@
     window_of(k_refs, k_scr)
     for e in range(2):
         q = qd_ref[0, e, 0].reshape(group * tokens, dim)
-        do = qd_ref[0, e, 1].reshape(group * tokens, dim)
+        do = do_ref[0, e].reshape(group * tokens, dim)
         k = k_scr[pl.ds(e, count)].reshape(count * tokens, dim)
         dqt = jnp.dot(k.T, ds_ref[0, e], preferred_element_type=F32) * scale
         for g in range(group):
             dq_scr[e, pl.ds(head * group + g, tokens, stride=rows), :] = dqt[:, g * tokens : (g + 1) * tokens].T
         keep = (2 * halo - e) * tokens
         dk = jnp.dot(ds_ref[0, e, keep:], q, preferred_element_type=F32) * scale
-        dv = jnp.dot(p_ref[0, e, keep:], do, preferred_element_type=F32)
+        dv = jnp.dot(w_ref[0, e, keep:], do, preferred_element_type=F32)
         if e == 0:
             dk_ref[0, 0], dv_scr[0] = dk, dv
         else:
@@ -424,7 +433,7 @@
     k_own = pack_other(place, k_other, k_mine)
     k_own, queries, grad_out, v_mine = lax.optimization_barrier((k_own, queries, grad_out, v_mine))
     q_other, do_other, v_other = (swapped(x, device_count) for x in (queries, grad_out, v_mine))
-    qd = arrange(place, in_hbm(queries), in_hbm(grad_out), q_other, do_other, key_heads)
+    qd = arrange(place, queries, grad_out, q_other, do_other, key_heads)
     qd, v_mine, v_other = lax.optimization_barrier((qd, v_mine, v_other))
     v_own = pack_both(place, v_mine, v_other)
 
@@ -441,6 +450,10 @@
     qd_spec = per_head(2, 2, group, tokens, dim)
     p_spec = per_head(2, count * tokens, group * tokens)
     p_shape = pltpu.VMEM((half, 2, count * tokens, group * tokens), BF16)
+    inv_shape = pltpu.VMEM((half, 2, 1, group * tokens), F32)
+    inv_spec = per_head(2, 1, group * tokens)
+    do_shape = pltpu.VMEM((half, 2, group, tokens, dim), BF16)
+    do_spec = per_head(2, group, tokens, dim)
     pair_spec = per_head(2, tokens, dim)
     pair = (half, 2, tokens, dim)
     one_spec = per_head(tokens, dim)
@@ -455,15 +468,15 @@
 
     k_pairs = halo_of(k_own)
     v_pairs = halo_of(v_own)
-    prob, *dv_halo = call(
+    prob, inverse, scaled, *dv_halo = call(
         functools.partial(prob_kernel, halo),
         "prob",
         (half,),
         (place, doc_lengths),
         (in_vmem(qd), *k_pairs),
         [qd_spec] + [pair_spec] * (halo + 1),
-        [p_shape] + [jax.ShapeDtypeStruct(pair, BF16)] * halo,
-        [p_spec] + [pair_spec] * halo,
+        [p_shape, inv_shape, do_shape] + [jax.ShapeDtypeStruct(pair, BF16)] * halo,
+        [p_spec, inv_spec, do_spec] + [pair_spec] * halo,
         [run, acc, pltpu.VMEM((2, 1, HEADS_AT_ONCE * tokens), jnp.int32)],
         4 * product,
     )
@@ -473,8 +486,8 @@
         "dscore",
         (half,),
         place,
-        (in_vmem(qd), in_vmem(prob), *v_pairs),
-        [qd_spec, p_spec] + [pair_spec] * (halo + 1),
+        (in_vmem(qd), in_vmem(prob), in_vmem(inverse), in_vmem(scaled), *v_pairs),
+        [qd_spec, p_spec, inv_spec, do_spec] + [pair_spec] * (halo + 1),
         [p_shape] + [jax.ShapeDtypeStruct(pair, BF16)] * halo,
         [p_spec] + [pair_spec] * halo,
         [run, acc],
@@ -486,8 +499,8 @@
         "own",
         (half,),
         place,
-        (in_vmem(qd), in_vmem(prob), in_vmem(dscore), *k_pairs, *dv_back),
-        [qd_spec, p_spec, p_spec] + [pair_spec] * (2 * halo + 1),
+        (in_vmem(qd), in_vmem(prob), in_vmem(scaled), in_vmem(dscore), *k_pairs, *dv_back),
+        [qd_spec, p_spec, do_spec, p_spec] + [pair_spec] * (2 * halo + 1),
         [dq_shape] + [dq_part_shape] * 2 + [jax.ShapeDtypeStruct(pair, F32)] + [one_shape] * 2,
         [dq_spec] + [dq_part_spec] * 2 + [pair_spec] + [one_spec] * 2,
         [

time: 62.2 us -> 62.1 us (level)
  Pallas kernels: 26 us -> 23.8 us
  starting transfers between devices: 30.7 us -> 32.7 us
    pallas_call x9, Pallas kernels: 26 us -> 23.8 us  [call(): pl.pallas_call(kernel, out_shape=outs, grid_spec=pltpu.PrefetchScalarGrid...]
    ppermute x8, starting transfers between devices: 7.72 us -> 8.93 us  [swapped(): return lax.ppermute(array, AXES, [(d, d ^ 1) for d in range(device_count)])]
    ppermute x8, starting transfers between devices: 22.9 us -> 23.7 us  [moved(): return lax.ppermute(array, AXES, pairs)]
  transfers between devices with their start and end apart: 16 -> 16, of which waited for: 2 -> 2; matrix products, arithmetic and copies ran while one was open for 0% -> 0% of each run, Pallas kernels for 37% -> 34%
where the time goes in v11:
time: 62.1 us; the launch traced here: 61.8 us
  starting transfers between devices  32.7 us (53%)
  Pallas kernels  23.8 us (38%)
  waiting for transfers between devices  4.3 us (7%)
  between operations  0.87 us (1%)
    pallas_call x9, Pallas kernels, call(): pl.pallas_call(kernel, out_shape=outs, grid_spec=pltpu.PrefetchScalarGrid...  23.8 us
    ppermute x8, starting transfers between devices, moved(): return lax.ppermute(array, AXES, pairs)  23.7 us
    ppermute x8, starting transfers between devices, swapped(): return lax.ppermute(array, AXES, [(d, d ^ 1) for d in range(device_count)])  8.93 us
    ppermute x8, waiting for transfers between devices, moved(): return lax.ppermute(array, AXES, pairs)  3.3 us
  transfers between devices with their start and end apart: 16, of which 2 were waited for; matrix products, arithmetic and copies ran while one was open for 0% of the time, Pallas kernels for 34%

profile of v11, /device:TPU:23, one launch (start us, length us, event | category | flops | bytes accessed | tf_op | source)
XLA Modules:
  0.0 61.8 jit_solution(2664680673926461059)
XLA Ops:
  0.6 0.7 %collective-permute-start = (bf16[128,8,128]{2,1,0:T(8,128)(2,1)}, bf16[128,8,128]{2,1,0:T(8,128)(2,1)S(1)}, u32[]{:S(2)}, u32[]{:S(2)}) collective-permute-start(bf16[128,8,128]{2,1,0:T(8,128)(2,1)} %key_ref.1), channel_id=1, source_target_pairs={{0,1},{1,0},{2,3},{3,2},{4,5},{5,4},{6,7},{7,6},{8,9},{9,8},{10,11... | collective-permute-start | bytes 786440 | tf_op jit(solution)/shard_map/ppermute | solution.py:25
  1.4 0.1 pad_add_fusion.place_ref
  1.5 1.6 %fetch.1 = (bf16[4,2,128,128]{3,2,1,0:T(8,128)(2,1)S(1)}, bf16[128,8,128]{2,1,0:T(8,128)(2,1)S(1)}) custom-call(s32[2]{0:T(128)S(1)} %pad_add_fusion.place_ref, bf16[128,8,128]{2,1,0:T(8,128)(2,1)} %key_ref.1, bf16[128,8,128]{2,1,0:T(8,128)(2,1)} %refs_0_.1), custom_call_target="tpu_custom_call" | custom-call | flops 1000000000 | tf_op jit(solution)/shard_map/fetch/pallas_call | solution.py:38
  3.1 0.0 collective-permute-done.other_ref
  3.1 0.6 %pack_other.1.refs_0_ = bf16[4,2,128,128]{3,2,1,0:T(8,128)(2,1)S(1)} custom-call(s32[2]{0:T(128)S(1)} %pad_add_fusion.place_ref, bf16[128,8,128]{2,1,0:T(8,128)(2,1)S(1)} %collective-permute-done.other_ref, bf16[4,2,128,128]{3,2,1,0:T(8,128)(2,1)S(1)} %get-tuple-element.28._), custom_call_target="tpu_custom_call", output_to_operand_aliasing={{}: (2, {})} | custom-call | flops 1000000000 | tf_op jit(solution)/shard_map/pack_other/pallas_call | solution.py:38
  3.7 0.0 copy-start.2
  3.7 0.1 collective-permute-start.1
  3.9 0.4 collective-permute-start.2
  4.3 0.1 collective-permute-start.3
  4.4 3.1 %collective-permute-start.5 = (bf16[4,2,128,128]{3,2,1,0:T(8,128)(2,1)S(1)}, bf16[4,2,128,128]{3,2,1,0:T(8,128)(2,1)S(1)}, u32[]{:S(2)}, u32[]{:S(2)}) collective-permute-start(bf16[4,2,128,128]{3,2,1,0:T(8,128)(2,1)S(1)} %pack_other.1.refs_0_), channel_id=1, source_target_pairs={{0,4},{1,5},{2,6},{3,7},{4,8},{5,9},{6,10},{7,11},{8,12},{9,13},{1... | collective-permute-start | bytes 786440 | tf_op jit(solution)/shard_map/ppermute | solution.py:21
  7.5 3.1 %collective-permute-start.4 = (bf16[4,2,128,128]{3,2,1,0:T(8,128)(2,1)S(1)}, bf16[4,2,128,128]{3,2,1,0:T(8,128)(2,1)S(1)}, u32[]{:S(2)}, u32[]{:S(2)}) collective-permute-start(bf16[4,2,128,128]{3,2,1,0:T(8,128)(2,1)S(1)} %pack_other.1.refs_0_), channel_id=1, source_target_pairs={{0,2},{1,3},{2,4},{3,5},{4,6},{5,7},{6,8},{7,9},{8,10},{9,11},{10,... | collective-permute-start | bytes 786440 | tf_op jit(solution)/shard_map/ppermute | solution.py:21
  10.7 0.0 collective-permute-done.1.q_other_ref
  10.7 0.0 collective-permute-done.2.do_other_ref
  10.7 2.0 %arrange.1.qd_ref = bf16[4,2,2,4,128,128]{5,4,3,2,1,0:T(8,128)(2,1)S(1)} custom-call(s32[2]{0:T(128)S(1)} %pad_add_fusion.place_ref, bf16[128,32,128]{2,1,0:T(8,128)(2,1)S(1)} %copy-done, bf16[128,32,128]{2,1,0:T(8,128)(2,1)S(1)} %copy-done.1, bf16[128,32,128]{2,1,0:T(8,128)(2,1)S(1)} %collective-permute-done.1.q_other_ref, ...), custom_call_target="tpu_custom_call" | custom-call | flops 1000000000 | tf_op jit(solution)/shard_map/arrange/pallas_call | solution.py:38
  12.7 0.7 %pack_both.1.refs_0_ = bf16[4,2,128,128]{3,2,1,0:T(8,128)(2,1)S(1)} custom-call(s32[2]{0:T(128)S(1)} %pad_add_fusion.place_ref, bf16[128,8,128]{2,1,0:T(8,128)(2,1)S(1)} %get-tuple-element.38.own_ref, bf16[128,8,128]{2,1,0:T(8,128)(2,1)S(1)} %collective-permute-done.3.other_ref), custom_call_target="tpu_custom_call" | custom-call | flops 1000000000 | tf_op jit(solution)/shard_map/pack_both/pallas_call | solution.py:38
  13.4 1.9 %collective-permute-start.7 = (bf16[4,2,128,128]{3,2,1,0:T(8,128)(2,1)S(1)}, bf16[4,2,128,128]{3,2,1,0:T(8,128)(2,1)S(1)}, u32[]{:S(2)}, u32[]{:S(2)}) collective-permute-start(bf16[4,2,128,128]{3,2,1,0:T(8,128)(2,1)S(1)} %pack_both.1.refs_0_), channel_id=1, source_target_pairs={{0,4},{1,5},{2,6},{3,7},{4,8},{5,9},{6,10},{7,11},{8,12},{9,13},{1... | collective-permute-start | bytes 786440 | tf_op jit(solution)/shard_map/ppermute | solution.py:21
  15.4 3.1 %collective-permute-start.6 = (bf16[4,2,128,128]{3,2,1,0:T(8,128)(2,1)S(1)}, bf16[4,2,128,128]{3,2,1,0:T(8,128)(2,1)S(1)}, u32[]{:S(2)}, u32[]{:S(2)}) collective-permute-start(bf16[4,2,128,128]{3,2,1,0:T(8,128)(2,1)S(1)} %pack_both.1.refs_0_), channel_id=1, source_target_pairs={{0,2},{1,3},{2,4},{3,5},{4,6},{5,7},{6,8},{7,9},{8,10},{9,11},{10,... | collective-permute-start | bytes 786440 | tf_op jit(solution)/shard_map/ppermute | solution.py:21
  18.5 6.6 %prob.1 = (bf16[4,2,640,512]{3,2,1,0:T(8,128)(2,1)S(1)}, f32[4,2,1,512]{3,2,1,0:T(1,128)S(1)}, bf16[4,2,4,128,128]{4,3,2,1,0:T(8,128)(2,1)S(1)}, bf16[4,2,128,12...) custom-call(s32[2]{0:T(128)S(1)} %pad_add_fusion.place_ref, s32[16]{0:T(128)S(1)} %copy-done.2, ...), custom_call_target="tpu_custom_call" | custom-call | flops 2684354560 | tf_op jit(solution)/shard_map/prob/pallas_call | solution.py:38
  25.1 3.4 %collective-permute-start.8 = (bf16[4,2,128,128]{3,2,1,0:T(8,128)(2,1)S(1)}, bf16[4,2,128,128]{3,2,1,0:T(8,128)(2,1)S(1)}, u32[]{:S(2)}, u32[]{:S(2)}) collective-permute-start(bf16[4,2,128,128]{3,2,1,0:T(8,128)(2,1)S(1)} %get-tuple-element.41), channel_id=1, source_target_pairs={{4,0},{5,1},{6,2},{7,3},{8,4},{9,5},{10,6},{11,7},{12,8},{13,9},{1... | collective-permute-start | bytes 786440 | tf_op jit(solution)/shard_map/ppermute | solution.py:21
  28.5 5.2 %collective-permute-start.9 = (bf16[4,2,128,128]{3,2,1,0:T(8,128)(2,1)S(1)}, bf16[4,2,128,128]{3,2,1,0:T(8,128)(2,1)S(1)}, u32[]{:S(2)}, u32[]{:S(2)}) collective-permute-start(bf16[4,2,128,128]{3,2,1,0:T(8,128)(2,1)S(1)} %get-tuple-element.42), channel_id=1, source_target_pairs={{2,0},{3,1},{4,2},{5,3},{6,4},{7,5},{8,6},{9,7},{10,8},{11,9},{12,... | collective-permute-start | bytes 786440 | tf_op jit(solution)/shard_map/ppermute | solution.py:21
  33.7 6.0 %dscore.1 = (bf16[4,2,640,512]{3,2,1,0:T(8,128)(2,1)S(1)}, bf16[4,2,128,128]{3,2,1,0:T(8,128)(2,1)S(1)}, bf16[4,2,128,128]{3,2,1,0:T(8,128)(2,1)S(1)}) custom-call(s32[2]{0:T(128)S(1)} %pad_add_fusion.place_ref, bf16[4,2,2,4,128,128]{5,4,3,2,1,0:T(8,128)(2,1)S(1)} %arrange.1.qd_ref, bf16[4,2,640,512]{3,2,1,0:T(8,128)(2,1)S(1)} %get-tuple-element.35.w_ref, ...), custom_call_target="tpu_custom_call" | custom-call | flops 2684354560 | tf_op jit(solution)/shard_map/dscore/pallas_call | solution.py:38
  39.8 1.9 %collective-permute-start.12 = (bf16[4,2,128,128]{3,2,1,0:T(8,128)(2,1)S(1)}, bf16[4,2,128,128]{3,2,1,0:T(8,128)(2,1)S(1)}, u32[]{:S(2)}, u32[]{:S(2)}) collective-permute-start(bf16[4,2,128,128]{3,2,1,0:T(8,128)(2,1)S(1)} %get-tuple-element.47), channel_id=1, source_target_pairs={{4,0},{5,1},{6,2},{7,3},{8,4},{9,5},{10,6},{11,7},{12,8},{13,9},{1... | collective-permute-start | bytes 786440 | tf_op jit(solution)/shard_map/ppermute | solution.py:21
  41.7 1.9 %collective-permute-start.13 = (bf16[4,2,128,128]{3,2,1,0:T(8,128)(2,1)S(1)}, bf16[4,2,128,128]{3,2,1,0:T(8,128)(2,1)S(1)}, u32[]{:S(2)}, u32[]{:S(2)}) collective-permute-start(bf16[4,2,128,128]{3,2,1,0:T(8,128)(2,1)S(1)} %get-tuple-element.48), channel_id=1, source_target_pairs={{2,0},{3,1},{4,2},{5,3},{6,4},{7,5},{8,6},{9,7},{10,8},{11,9},{12,... | collective-permute-start | bytes 786440 | tf_op jit(solution)/shard_map/ppermute | solution.py:21
  43.7 3.3 %own.1 = (bf16[128,16,128]{2,1,0:T(8,128)(2,1)S(1)}, bf16[64,16,128]{2,1,0:T(8,128)(2,1)S(1)}, bf16[64,16,128]{2,1,0:T(8,128)(2,1)S(1)}, f32[4,2,128,128]{3,2,1,...) custom-call(s32[2]{0:T(128)S(1)} %pad_add_fusion.place_ref, ...), custom_call_target="tpu_custom_call" | custom-call | tf_op jit(solution)/shard_map/own/pallas_call | solution.py:38
  47.0 4.4 %collective-permute-start.10 = (bf16[64,16,128]{2,1,0:T(8,128)(2,1)S(1)}, bf16[64,16,128]{2,1,0:T(8,128)(2,1)S(1)}, u32[]{:S(2)}, u32[]{:S(2)}) collective-permute-start(bf16[64,16,128]{2,1,0:T(8,128)(2,1)S(1)} %get-tuple-element.44), channel_id=1, source_target_pairs={{0,1},{1,0},{2,3},{3,2},{4,5},{5,4},{6,7},{7,6},{8,9},{9,8},{10,11... | collective-permute-start | bytes 786440 | tf_op jit(solution)/shard_map/ppermute | solution.py:25
  51.4 0.1 collective-permute-start.11
  51.5 0.4 collective-permute-start.15
  51.9 3.3 %collective-permute-done.13.refs_1_ = bf16[4,2,128,128]{3,2,1,0:T(8,128)(2,1)S(1)} collective-permute-done((bf16[4,2,128,128]{3,2,1,0:T(8,128)(2,1)S(1)}, bf16[4,2,128,128]{3,2,1,0:T(8,128)(2,1)S(1)}, u32[]{:S(2)}, u32[]{:S(2)}) %collective-permute-start.13) | collective-permute-done | bytes 262176 | tf_op jit(solution)/shard_map/ppermute | solution.py:21
  55.2 0.6 %sum_dk.1 = (bf16[4,128,128]{2,1,0:T(8,128)(2,1)S(1)}, bf16[4,128,128]{2,1,0:T(8,128)(2,1)S(1)}) custom-call(s32[2]{0:T(128)S(1)} %pad_add_fusion.place_ref, f32[4,2,128,128]{3,2,1,0:T(8,128)S(1)} %get-tuple-element.46.own_ref, bf16[4,2,128,128]{3,2,1,0:T(8,128)(2,1)S(1)} %collective-permute-done.12.refs_0_, ...), custom_call_target="tpu_custom_call" | custom-call | tf_op jit(solution)/shard_map/sum_dk/pallas_call | solution.py:38
  55.9 2.6 %collective-permute-start.14 = (bf16[4,128,128]{2,1,0:T(8,128)(2,1)S(1)}, bf16[4,128,128]{2,1,0:T(8,128)(2,1)S(1)}, u32[]{:S(2)}, u32[]{:S(2)}) collective-permute-start(bf16[4,128,128]{2,1,0:T(8,128)(2,1)S(1)} %get-tuple-element.50), channel_id=1, source_target_pairs={{0,1},{1,0},{2,3},{3,2},{4,5},{5,4},{6,7},{7,6},{8,9},{9,8},{10,11... | collective-permute-start | bytes 393224 | tf_op jit(solution)/shard_map/ppermute | solution.py:25
  58.5 1.0 %collective-permute-done.14.refs_4_ = bf16[4,128,128]{2,1,0:T(8,128)(2,1)S(1)} collective-permute-done((bf16[4,128,128]{2,1,0:T(8,128)(2,1)S(1)}, bf16[4,128,128]{2,1,0:T(8,128)(2,1)S(1)}, u32[]{:S(2)}, u32[]{:S(2)}) %collective-permute-start.14) | collective-permute-done | bytes 131104 | tf_op jit(solution)/shard_map/ppermute | solution.py:25
  59.4 2.3 %finish.1 = (bf16[128,32,128]{2,1,0:T(8,128)(2,1)}, bf16[128,8,128]{2,1,0:T(8,128)(2,1)}, bf16[128,8,128]{2,1,0:T(8,128)(2,1)}) custom-call(s32[2]{0:T(128)S(1)} %pad_add_fusion.place_ref, bf16[128,16,128]{2,1,0:T(8,128)(2,1)S(1)} %get-tuple-element.43.refs_0_, bf16[64,16,128]{2,1,0:T(8,128)(2,1)S(1)} %collective-permute-done.10.refs_1_, ...), custom_call_target="tpu_custom_call" | custom-call | tf_op jit(solution)/shard_map/finish/pallas_call | solution.py:38
  (16 shorter events, 0.0 us)
Async XLA Ops:
  0.6 3.2 %copy-start.1 = (bf16[128,32,128]{2,1,0:T(8,128)(2,1)S(1)}, bf16[128,32,128]{2,1,0:T(8,128)(2,1)}, u32[]{:S(2)}) copy-start(bf16[128,32,128]{2,1,0:T(8,128)(2,1)} %do_ref) | copy-start | bytes 3145732
  0.6 3.1 %copy-start = (bf16[128,32,128]{2,1,0:T(8,128)(2,1)S(1)}, bf16[128,32,128]{2,1,0:T(8,128)(2,1)}, u32[]{:S(2)}) copy-start(bf16[128,32,128]{2,1,0:T(8,128)(2,1)} %q_ref) | copy-start | bytes 3145732
  0.6 2.4 %collective-permute-start = (bf16[128,8,128]{2,1,0:T(8,128)(2,1)}, bf16[128,8,128]{2,1,0:T(8,128)(2,1)S(1)}, u32[]{:S(2)}, u32[]{:S(2)}) collective-permute-start(bf16[128,8,128]{2,1,0:T(8,128)(2,1)} %key_ref.1), channel_id=1, source_target_pairs={{0,1},{1,0},{2,3},{3,2},{4,5},{5,4},{6,7},{7,6},{8,9},{9,8},{10,11... | collective-permute-start | bytes 786440 | tf_op jit(solution)/shard_map/ppermute | solution.py:25
  3.7 14.8 %copy-start.2 = (s32[16]{0:T(128)S(1)}, s32[16]{0:T(128)}, u32[]{:S(2)}) copy-start(s32[16]{0:T(128)} %lengths_ref.1) | copy-start | bytes 196
  3.7 6.9 %collective-permute-start.1 = (bf16[128,32,128]{2,1,0:T(8,128)(2,1)S(1)}, bf16[128,32,128]{2,1,0:T(8,128)(2,1)S(1)}, u32[]{:S(2)}, u32[]{:S(2)}) collective-permute-start(bf16[128,32,128]{2,1,0:T(8,128)(2,1)S(1)} %copy-done), channel_id=1, source_target_pairs={{0,1},{1,0},{2,3},{3,2},{4,5},{5,4},{6,7},{7,6},{8,9},{9,8},{10,11... | collective-permute-start | bytes 3145736 | tf_op jit(solution)/shard_map/ppermute | solution.py:25
  3.9 6.8 %collective-permute-start.2 = (bf16[128,32,128]{2,1,0:T(8,128)(2,1)S(1)}, bf16[128,32,128]{2,1,0:T(8,128)(2,1)S(1)}, u32[]{:S(2)}, u32[]{:S(2)}) collective-permute-start(bf16[128,32,128]{2,1,0:T(8,128)(2,1)S(1)} %copy-done.1), channel_id=1, source_target_pairs={{0,1},{1,0},{2,3},{3,2},{4,5},{5,4},{6,7},{7,6},{8,9},{9,8},{10,11... | collective-permute-start | bytes 3145736 | tf_op jit(solution)/shard_map/ppermute | solution.py:25
  4.3 8.4 %collective-permute-start.3 = (bf16[128,8,128]{2,1,0:T(8,128)(2,1)S(1)}, bf16[128,8,128]{2,1,0:T(8,128)(2,1)S(1)}, u32[]{:S(2)}, u32[]{:S(2)}) collective-permute-start(bf16[128,8,128]{2,1,0:T(8,128)(2,1)S(1)} %get-tuple-element.38.own_ref), channel_id=1, source_target_pairs={{0,1},{1,0},{2,3},{3,2},{4,5},{5,4},{6,7},{7,6},{8,9},{9,8},{10,11... | collective-permute-start | bytes 786440 | tf_op jit(solution)/shard_map/ppermute | solution.py:25
  4.4 14.1 %collective-permute-start.5 = (bf16[4,2,128,128]{3,2,1,0:T(8,128)(2,1)S(1)}, bf16[4,2,128,128]{3,2,1,0:T(8,128)(2,1)S(1)}, u32[]{:S(2)}, u32[]{:S(2)}) collective-permute-start(bf16[4,2,128,128]{3,2,1,0:T(8,128)(2,1)S(1)} %pack_other.1.refs_0_), channel_id=1, source_target_pairs={{0,4},{1,5},{2,6},{3,7},{4,8},{5,9},{6,10},{7,11},{8,12},{9,13},{1... | collective-permute-start | bytes 786440 | tf_op jit(solution)/shard_map/ppermute | solution.py:21
  7.5 11.0 %collective-permute-start.4 = (bf16[4,2,128,128]{3,2,1,0:T(8,128)(2,1)S(1)}, bf16[4,2,128,128]{3,2,1,0:T(8,128)(2,1)S(1)}, u32[]{:S(2)}, u32[]{:S(2)}) collective-permute-start(bf16[4,2,128,128]{3,2,1,0:T(8,128)(2,1)S(1)} %pack_other.1.refs_0_), channel_id=1, source_target_pairs={{0,2},{1,3},{2,4},{3,5},{4,6},{5,7},{6,8},{7,9},{8,10},{9,11},{10,... | collective-permute-start | bytes 786440 | tf_op jit(solution)/shard_map/ppermute | solution.py:21
  13.4 20.3 %collective-permute-start.7 = (bf16[4,2,128,128]{3,2,1,0:T(8,128)(2,1)S(1)}, bf16[4,2,128,128]{3,2,1,0:T(8,128)(2,1)S(1)}, u32[]{:S(2)}, u32[]{:S(2)}) collective-permute-start(bf16[4,2,128,128]{3,2,1,0:T(8,128)(2,1)S(1)} %pack_both.1.refs_0_), channel_id=1, source_target_pairs={{0,4},{1,5},{2,6},{3,7},{4,8},{5,9},{6,10},{7,11},{8,12},{9,13},{1... | collective-permute-start | bytes 786440 | tf_op jit(solution)/shard_map/ppermute | solution.py:21
  15.4 18.3 %collective-permute-start.6 = (bf16[4,2,128,128]{3,2,1,0:T(8,128)(2,1)S(1)}, bf16[4,2,128,128]{3,2,1,0:T(8,128)(2,1)S(1)}, u32[]{:S(2)}, u32[]{:S(2)}) collective-permute-start(bf16[4,2,128,128]{3,2,1,0:T(8,128)(2,1)S(1)} %pack_both.1.refs_0_), channel_id=1, source_target_pairs={{0,2},{1,3},{2,4},{3,5},{4,6},{5,7},{6,8},{7,9},{8,10},{9,11},{10,... | collective-permute-start | bytes 786440 | tf_op jit(solution)/shard_map/ppermute | solution.py:21
  25.1 18.5 %collective-permute-start.8 = (bf16[4,2,128,128]{3,2,1,0:T(8,128)(2,1)S(1)}, bf16[4,2,128,128]{3,2,1,0:T(8,128)(2,1)S(1)}, u32[]{:S(2)}, u32[]{:S(2)}) collective-permute-start(bf16[4,2,128,128]{3,2,1,0:T(8,128)(2,1)S(1)} %get-tuple-element.41), channel_id=1, source_target_pairs={{4,0},{5,1},{6,2},{7,3},{8,4},{9,5},{10,6},{11,7},{12,8},{13,9},{1... | collective-permute-start | bytes 786440 | tf_op jit(solution)/shard_map/ppermute | solution.py:21
  28.5 15.2 %collective-permute-start.9 = (bf16[4,2,128,128]{3,2,1,0:T(8,128)(2,1)S(1)}, bf16[4,2,128,128]{3,2,1,0:T(8,128)(2,1)S(1)}, u32[]{:S(2)}, u32[]{:S(2)}) collective-permute-start(bf16[4,2,128,128]{3,2,1,0:T(8,128)(2,1)S(1)} %get-tuple-element.42), channel_id=1, source_target_pairs={{2,0},{3,1},{4,2},{5,3},{6,4},{7,5},{8,6},{9,7},{10,8},{11,9},{12,... | collective-permute-start | bytes 786440 | tf_op jit(solution)/shard_map/ppermute | solution.py:21
  39.8 12.2 %collective-permute-start.12 = (bf16[4,2,128,128]{3,2,1,0:T(8,128)(2,1)S(1)}, bf16[4,2,128,128]{3,2,1,0:T(8,128)(2,1)S(1)}, u32[]{:S(2)}, u32[]{:S(2)}) collective-permute-start(bf16[4,2,128,128]{3,2,1,0:T(8,128)(2,1)S(1)} %get-tuple-element.47), channel_id=1, source_target_pairs={{4,0},{5,1},{6,2},{7,3},{8,4},{9,5},{10,6},{11,7},{12,8},{13,9},{1... | collective-permute-start | bytes 786440 | tf_op jit(solution)/shard_map/ppermute | solution.py:21
  41.7 13.5 %collective-permute-start.13 = (bf16[4,2,128,128]{3,2,1,0:T(8,128)(2,1)S(1)}, bf16[4,2,128,128]{3,2,1,0:T(8,128)(2,1)S(1)}, u32[]{:S(2)}, u32[]{:S(2)}) collective-permute-start(bf16[4,2,128,128]{3,2,1,0:T(8,128)(2,1)S(1)} %get-tuple-element.48), channel_id=1, source_target_pairs={{2,0},{3,1},{4,2},{5,3},{6,4},{7,5},{8,6},{9,7},{10,8},{11,9},{12,... | collective-permute-start | bytes 786440 | tf_op jit(solution)/shard_map/ppermute | solution.py:21
  47.0 11.5 %collective-permute-start.10 = (bf16[64,16,128]{2,1,0:T(8,128)(2,1)S(1)}, bf16[64,16,128]{2,1,0:T(8,128)(2,1)S(1)}, u32[]{:S(2)}, u32[]{:S(2)}) collective-permute-start(bf16[64,16,128]{2,1,0:T(8,128)(2,1)S(1)} %get-tuple-element.44), channel_id=1, source_target_pairs={{0,1},{1,0},{2,3},{3,2},{4,5},{5,4},{6,7},{7,6},{8,9},{9,8},{10,11... | collective-permute-start | bytes 786440 | tf_op jit(solution)/shard_map/ppermute | solution.py:25
  51.4 7.0 %collective-permute-start.11 = (bf16[64,16,128]{2,1,0:T(8,128)(2,1)S(1)}, bf16[64,16,128]{2,1,0:T(8,128)(2,1)S(1)}, u32[]{:S(2)}, u32[]{:S(2)}) collective-permute-start(bf16[64,16,128]{2,1,0:T(8,128)(2,1)S(1)} %get-tuple-element.45), channel_id=1, source_target_pairs={{0,1},{1,0},{2,3},{3,2},{4,5},{5,4},{6,7},{7,6},{8,9},{9,8},{10,11... | collective-permute-start | bytes 786440 | tf_op jit(solution)/shard_map/ppermute | solution.py:25
  51.5 7.0 %collective-permute-start.15 = (bf16[4,128,128]{2,1,0:T(8,128)(2,1)S(1)}, bf16[4,128,128]{2,1,0:T(8,128)(2,1)S(1)}, u32[]{:S(2)}, u32[]{:S(2)}) collective-permute-start(bf16[4,128,128]{2,1,0:T(8,128)(2,1)S(1)} %get-tuple-element.52), channel_id=1, source_target_pairs={{0,1},{1,0},{2,3},{3,2},{4,5},{5,4},{6,7},{7,6},{8,9},{9,8},{10,11... | collective-permute-start | bytes 393224 | tf_op jit(solution)/shard_map/ppermute | solution.py:25
  55.9 3.6 %collective-permute-start.14 = (bf16[4,128,128]{2,1,0:T(8,128)(2,1)S(1)}, bf16[4,128,128]{2,1,0:T(8,128)(2,1)S(1)}, u32[]{:S(2)}, u32[]{:S(2)}) collective-permute-start(bf16[4,128,128]{2,1,0:T(8,128)(2,1)S(1)} %get-tuple-element.50), channel_id=1, source_target_pairs={{0,1},{1,0},{2,3},{3,2},{4,5},{5,4},{6,7},{7,6},{8,9},{9,8},{10,11... | collective-permute-start | bytes 393224 | tf_op jit(solution)/shard_map/ppermute | solution.py:25

commit v12 on v7

--- a/solution.py
+++ b/solution.py
@@ -8,8 +8,9 @@
 from jax.sharding import PartitionSpec as P
 
 AXES = ("ctx", "uly")
+MASKED = -1e30
 LOG2E = 1.4426950408889634
-MASKED = -1e30
+HEADS_AT_ONCE = 2
 BF16, F32 = jnp.bfloat16, jnp.float32
 NT = (((1,), (1,)), ((), ()))
 VMEM_BYTES = 16 * 2**20
@@ -26,6 +27,10 @@
 
 def in_vmem(array):
     return pltpu.with_memory_space_constraint(array, pltpu.VMEM)
+
+
+def in_hbm(array):
+    return pltpu.with_memory_space_constraint(array, pltpu.HBM)
 
 
 def call(kernel, name, grid, place, inputs, in_specs, outs, out_specs, scratch, flops, aliases={}):
@@ -49,31 +54,34 @@
 
 def arrange_kernel(group, place_ref, q_ref, do_ref, q_other_ref, do_other_ref, out_ref, scr):
     core = place_ref[0]
-    rows, heads, dim = q_ref.shape
+    tokens, heads, dim = q_ref.shape
+    half = heads // 2
+    mine = pl.ds(pl.multiple_of(core * half, half), half)
+    turn = 0
     for kind, (own, other) in enumerate([(q_ref, q_other_ref), (do_ref, do_other_ref)]):
         for which, ref in enumerate([own, other]):
             block = 1 - core if which else core
-            scr[...] = ref[...].astype(F32).reshape(rows * heads, dim)
-            for h in range(heads):
-                out_ref[h // group, block, kind, h % group] = scr[pl.ds(h, rows, stride=heads), :].astype(BF16)
+            wide = scr.at[turn % 2]
+            wide[...] = ref[:, mine].astype(F32).reshape(tokens * half, dim)
+            for h in range(half):
+                out_ref[h // group, block, kind, h % group] = wide[pl.ds(h, tokens, stride=half), :].astype(BF16)
+            turn += 1
 
 
 def arrange(place, queries, grad_out, q_other, do_other, key_heads):
     tokens, heads, dim = queries.shape
     half, group = heads // 2, heads // key_heads
-    rows = 32
-    in_spec = pl.BlockSpec((rows, half, dim), lambda i, place: (i, place[0], 0))
-    out = (key_heads // 2, 2, 2, group, tokens, dim)
+    whole = pl.BlockSpec(memory_space=pltpu.VMEM)
     return call(
         functools.partial(arrange_kernel, group),
         "arrange",
-        (tokens // rows,),
-        place,
-        (queries, grad_out, q_other, do_other),
-        [in_spec] * 4,
-        pltpu.VMEM(out, BF16),
-        pl.BlockSpec(out[:4] + (rows, dim), lambda i, place: (0, 0, 0, 0, i, 0)),
-        [pltpu.VMEM((rows * half, dim), F32)],
+        (1,),
+        place,
+        [in_vmem(x) for x in (queries, grad_out, q_other, do_other)],
+        [whole] * 4,
+        pltpu.VMEM((key_heads // 2, 2, 2, group, tokens, dim), BF16),
+        whole,
+        [pltpu.VMEM((2, tokens * half, dim), F32)],
         10**9,
     )
 
@@ -109,7 +117,7 @@
         "fetch",
         (1,),
         place,
-        [pltpu.with_memory_space_constraint(x, pltpu.HBM) for x in (keys, *arrays)],
+        [in_hbm(x) for x in (keys, *arrays)],
         [pl.BlockSpec(memory_space=pltpu.HBM)] * (1 + len(arrays)),
         [pltpu.VMEM(out, BF16)] + [pltpu.VMEM(x.shape, x.dtype) for x in arrays],
         [pl.BlockSpec(memory_space=pltpu.VMEM)] * (1 + len(arrays)),
@@ -215,8 +223,8 @@
     k_scr, acc, firsts = refs[-3:]
     _, _, _, group, tokens, dim = qd_ref.shape
     count = 2 * halo + 1
-    pair = 2 * tokens
-    row, lane = on_diagonal(tokens, 2)
+    pair = HEADS_AT_ONCE * tokens
+    row, lane = on_diagonal(tokens, HEADS_AT_ONCE)
     diagonal = row <= lane
 
     @pl.when(pl.program_id(0) == 0)
@@ -260,9 +268,9 @@
     v_scr, acc = refs[-2:]
     _, _, _, group, tokens, dim = qd_ref.shape
     count = 2 * halo + 1
-    pair = 2 * tokens
+    pair = HEADS_AT_ONCE * tokens
     window_of(v_refs, v_scr)
-    row, lane = on_diagonal(tokens, 2)
+    row, lane = on_diagonal(tokens, HEADS_AT_ONCE)
     diagonal = row <= lane
     for e in range(2):
         v = v_scr[pl.ds(e, count)].reshape(count * tokens, dim)
@@ -289,7 +297,7 @@
 
 def own_kernel(halo, place_ref, qd_ref, p_ref, ds_ref, *refs):
     k_refs, back_refs = refs[: halo + 1], refs[halo + 1 : 2 * halo + 1]
-    dq_ref, dq_other_ref, dk_ref, dv_ref, dv_other_ref, k_scr, dq_scr, dv_scr = refs[2 * halo + 1 :]
+    dq_ref, *other_refs, dk_ref, dv_ref, k_scr, dq_scr, dv_scr, far_scr = refs[2 * halo + 1 :]
     core, head = place_ref[0], pl.program_id(0)
     _, _, _, group, tokens, dim = qd_ref.shape
     rows = dq_ref.shape[1]
@@ -315,16 +323,23 @@
     for ref in back_refs:
         dv_scr[...] += ref[0].astype(F32)
     dv_ref[0] = dv_scr[core].astype(BF16)
-    dv_other_ref[0] = dv_scr[1 - core].astype(BF16)
+    dq_rows = tokens * rows
+    at = dq_rows + head * tokens
+    far_scr[pl.ds(pl.multiple_of(at, tokens), tokens)] = dv_scr[1 - core].astype(BF16)
 
     @pl.when(head == pl.num_programs(0) - 1)
     def _():
         dq_ref[...] = dq_scr[core].astype(BF16).reshape(dq_ref.shape)
-        dq_other_ref[...] = dq_scr[1 - core].astype(BF16).reshape(dq_ref.shape)
-
-
-def sum_kernel(place_ref, own_ref, *refs):
-    back_refs, (mine_ref, other_ref) = refs[:-2], refs[-2:]
+        far_scr[:dq_rows] = dq_scr[1 - core].astype(BF16)
+        start = 0
+        for ref in other_refs:
+            part = ref.shape[0] * rows
+            ref[...] = far_scr[start : start + part].reshape(ref.shape)
+            start += part
+
+
+def sum_kernel(count, place_ref, own_ref, *refs):
+    back_refs, (mine_ref, other_ref) = refs[:count], refs[-2:]
     core = place_ref[0]
     for block, ref in [(1 - core, other_ref), (core, mine_ref)]:
         total = own_ref[:, block]
@@ -333,51 +348,57 @@
         ref[...] = total.astype(BF16)
 
 
-def summed(place, own, backs):
+def summed(place, own, backs, before):
     half, _, tokens, dim = own.shape
     pair_spec = pl.BlockSpec(own.shape, lambda i, place: (0, 0, 0, 0))
     one = (half, tokens, dim)
     return call(
-        sum_kernel,
+        functools.partial(sum_kernel, len(backs)),
         "sum_dk",
         (1,),
         place,
-        (own, *backs),
-        [pair_spec] * (1 + len(backs)),
+        (own, *backs, *(in_hbm(x) for x in before)),
+        [pair_spec] * (1 + len(backs)) + [pl.BlockSpec(memory_space=pltpu.HBM)] * len(before),
         [jax.ShapeDtypeStruct(one, BF16)] * 2,
         [pl.BlockSpec(one, lambda i, place: (0, 0, 0))] * 2,
         [],
-        10**8,
-    )
-
-
-def join_kernel(place_ref, own_ref, other_ref, out_ref, sems):
+        0,
+    )
+
+
+def join_kernel(parts, place_ref, own_ref, *refs):
+    others, out_ref, sems = refs[:parts], refs[-2], refs[-1]
     core = place_ref[0]
-    half = own_ref.shape[1]
-    copies = []
-    for which, ref in enumerate([own_ref, other_ref]):
-        side = 1 - core if which else core
-        at = pl.multiple_of(side * half, half)
-        copies.append(pltpu.make_async_copy(ref, out_ref.at[:, pl.ds(at, half)], sems.at[which]))
-        copies[-1].start()
+    tokens, half, _ = own_ref.shape
+    at = pl.multiple_of(core * half, half)
+    copies = [pltpu.make_async_copy(own_ref, out_ref.at[:, pl.ds(at, half)], sems.at[0])]
+    at = pl.multiple_of((1 - core) * half, half)
+    first = 0
+    for i, part in enumerate(others):
+        count = min(part.shape[0], tokens - first)
+        to = out_ref.at[pl.ds(first, count), pl.ds(at, half)]
+        copies.append(pltpu.make_async_copy(part.at[pl.ds(0, count)], to, sems.at[1 + i]))
+        first += count
+    for copy in copies:
+        copy.start()
     for copy in copies:
         copy.wait()
 
 
-def join(place, own, other):
+def join(place, own, others):
     tokens, half, dim = own.shape
     anywhere = pl.BlockSpec(memory_space=pl.ANY)
     return call(
-        join_kernel,
+        functools.partial(join_kernel, len(others)),
         "join",
         (1,),
         place,
-        (own, other),
-        [anywhere] * 2,
+        (own, *others),
+        [anywhere] * (1 + len(others)),
         jax.ShapeDtypeStruct((tokens, 2 * half, dim), BF16),
         anywhere,
-        [pltpu.SemaphoreType.DMA((2,))],
-        10**9,
+        [pltpu.SemaphoreType.DMA((1 + len(others),))],
+        0,
     )
 
 
@@ -385,16 +406,17 @@
     core = place_ref[0]
     rows, heads, dim = out_ref.shape
     half = heads // 2
-    for which, ref in enumerate([own_ref, other_ref]):
-        side = 1 - core if which else core
-        for h in range(half):
-            scr[pl.ds(side * half + h, rows, stride=heads), :] = ref[h].astype(F32)
+    other = other_ref[...].reshape(-1, dim)
+    skip = other.shape[0] - half * rows
+    for h in range(half):
+        scr[pl.ds(core * half + h, rows, stride=heads), :] = own_ref[h].astype(F32)
+        rest = other[skip + h * rows : skip + (h + 1) * rows]
+        scr[pl.ds((1 - core) * half + h, rows, stride=heads), :] = rest.astype(F32)
     out_ref[...] = scr[...].astype(BF16).reshape(rows, heads, dim)
 
 
 def merge(place, own, other, name):
     half, tokens, dim = own.shape
-    spec = pl.BlockSpec(own.shape, lambda i, place: (0, 0, 0))
     out = (tokens, 2 * half, dim)
     return call(
         merge_kernel,
@@ -402,11 +424,11 @@
         (1,),
         place,
         (own, other),
-        [spec] * 2,
+        [pl.BlockSpec(x.shape, lambda i, place: (0, 0, 0)) for x in (own, other)],
         jax.ShapeDtypeStruct(out, BF16),
         pl.BlockSpec(out, lambda i, place: (0, 0, 0)),
         [pltpu.VMEM((tokens * 2 * half, dim), F32)],
-        4 * 10**9,
+        0,
     )
 
 
@@ -425,11 +447,11 @@
 
     far_first = range(halo, 0, -1)
     k_other = swapped(keys, device_count)
-    k_mine, v_mine, q_mine, do_mine = fetch(place, keys, (values, queries, grad_out))
+    k_mine, v_mine = fetch(place, keys, (values,))
     k_own = pack_other(place, k_other, k_mine)
-    k_own, q_mine, do_mine, v_mine = lax.optimization_barrier((k_own, q_mine, do_mine, v_mine))
-    q_other, do_other, v_other = (swapped(x, device_count) for x in (q_mine, do_mine, v_mine))
-    qd = arrange(place, in_vmem(q_mine), in_vmem(do_mine), q_other, do_other, key_heads)
+    k_own, queries, grad_out, v_mine = lax.optimization_barrier((k_own, queries, grad_out, v_mine))
+    q_other, do_other, v_other = (swapped(x, device_count) for x in (queries, grad_out, v_mine))
+    qd = arrange(place, queries, grad_out, q_other, do_other, key_heads)
     qd, v_mine, v_other = lax.optimization_barrier((qd, v_mine, v_other))
     v_own = pack_both(place, v_mine, v_other)
 
@@ -452,6 +474,12 @@
     one_shape = jax.ShapeDtypeStruct((half, tokens, dim), BF16)
     dq_shape = jax.ShapeDtypeStruct((tokens, heads // 2, dim), BF16)
     dq_spec = pl.BlockSpec(dq_shape.shape, lambda h, *_: (0, 0, 0))
+    far_rows = tokens + half * tokens // (heads // 2)
+    step = (far_rows // 3 + 7) // 8 * 8
+    parts = [
+        jax.ShapeDtypeStruct((rows, heads // 2, dim), BF16) for rows in (step, step, far_rows - 2 * step)
+    ]
+    part_specs = [pl.BlockSpec(part.shape, lambda h, *_: (0, 0, 0)) for part in parts]
     run = pltpu.VMEM((window, tokens, dim), BF16)
     acc = pltpu.VMEM((2 * halo, tokens, dim), F32)
     product = 2 * half * 2 * count * tokens * group * tokens * dim
@@ -467,7 +495,7 @@
         [qd_spec] + [pair_spec] * (halo + 1),
         [p_shape] + [jax.ShapeDtypeStruct(pair, BF16)] * halo,
         [p_spec] + [pair_spec] * halo,
-        [run, acc, pltpu.VMEM((2, 1, 2 * tokens), jnp.int32)],
+        [run, acc, pltpu.VMEM((2, 1, HEADS_AT_ONCE * tokens), jnp.int32)],
         4 * product,
     )
     dv_back = sent_back(dv_halo)
@@ -484,27 +512,27 @@
         4 * product,
     )
     dk_back = sent_back(dk_halo)
-    dq, dq_other, dk_own, dv, dv_other = call(
+    dq, *others, dk_own, dv = call(
         functools.partial(own_kernel, halo),
         "own",
         (half,),
         place,
         (in_vmem(qd), in_vmem(prob), in_vmem(dscore), *k_pairs, *dv_back),
         [qd_spec, p_spec, p_spec] + [pair_spec] * (2 * halo + 1),
-        [dq_shape] * 2 + [jax.ShapeDtypeStruct(pair, F32)] + [one_shape] * 2,
-        [dq_spec] * 2 + [pair_spec] + [one_spec] * 2,
+        [dq_shape, *parts, jax.ShapeDtypeStruct(pair, F32), one_shape],
+        [dq_spec, *part_specs, pair_spec, one_spec],
         [
             run,
             pltpu.VMEM((2, tokens * heads // 2, dim), F32),
             pltpu.VMEM((2, tokens, dim), F32),
+            pltpu.VMEM((far_rows * heads // 2, dim), BF16),
         ],
         0,
     )
-    dq_other = swapped(dq_other, device_count)
-    dv_other = swapped(dv_other, device_count)
-    dk, dk_other = summed(place, dk_own, dk_back)
-    grad_queries = join(place, dq, dq_other)
-    grad_values = merge(place, dv, dv_other, "merge_dv")
+    others = [swapped(part, device_count) for part in others]
+    grad_queries = join(place, dq, others)
+    grad_values = merge(place, dv, others[-1], "merge_dv")
+    dk, dk_other = summed(place, dk_own, dk_back, (grad_queries, grad_values))
     grad_keys = merge(place, dk, swapped(dk_other, device_count), "merge_dk")
     return grad_queries, grad_keys, grad_values
 

time: 62.7 us -> 61.2 us (0.976)
  waiting for transfers between devices: 3.71 us -> 2.28 us
  Pallas kernels: 26.9 us -> 25.8 us
  starting transfers between devices: 30.8 us -> 31.7 us
    ppermute x8, waiting for transfers between devices: 3.69 us -> 0.02 us  [moved(): return lax.ppermute(array, AXES, pairs)]
    ppermute x7 -> x8, waiting for transfers between devices: 0.02 us -> 2.26 us  [swapped(): return lax.ppermute(array, AXES, [(d, d ^ 1) for d in range(device_count)])]
    pallas_call x11, Pallas kernels: 26.9 us -> 25.8 us  [call(): pl.pallas_call(kernel, out_shape=outs, grid_spec=pltpu.PrefetchScalarGrid...]
    ppermute x8, starting transfers between devices: 22.9 us -> 23.7 us  [moved(): return lax.ppermute(array, AXES, pairs)]
    ppermute x7 -> x8, starting transfers between devices: 7.89 us -> 7.96 us  [swapped(): return lax.ppermute(array, AXES, [(d, d ^ 1) for d in range(device_count)])]
  transfers between devices with their start and end apart: 15 -> 16, of which waited for: 1 -> 2; matrix products, arithmetic and copies ran while one was open for 0% -> 0% of each run, Pallas kernels for 40% -> 38%
where the time goes in v12:
time: 61.2 us; the launch traced here: 60.8 us
  starting transfers between devices  31.7 us (52%)
  Pallas kernels  25.8 us (42%)
  waiting for transfers between devices  2.28 us (4%)
  between operations  0.9 us (1%)
    pallas_call x11, Pallas kernels, call(): pl.pallas_call(kernel, out_shape=outs, grid_spec=pltpu.PrefetchScalarGrid...  25.8 us
    ppermute x8, starting transfers between devices, moved(): return lax.ppermute(array, AXES, pairs)  23.7 us
    ppermute x8, starting transfers between devices, swapped(): return lax.ppermute(array, AXES, [(d, d ^ 1) for d in range(device_count)])  7.96 us
    ppermute x8, waiting for transfers between devices, swapped(): return lax.ppermute(array, AXES, [(d, d ^ 1) for d in range(device_count)])  2.26 us
  transfers between devices with their start and end apart: 16, of which 2 were waited for; matrix products, arithmetic and copies ran while one was open for 0% of the time, Pallas kernels for 38%

profile of v12, /device:TPU:23, one launch (start us, length us, event | category | flops | bytes accessed | tf_op | source)
XLA Modules:
  0.0 60.8 jit_solution(15027471932733078280)
XLA Ops:
  0.6 0.7 %collective-permute-start = (bf16[128,8,128]{2,1,0:T(8,128)(2,1)}, bf16[128,8,128]{2,1,0:T(8,128)(2,1)S(1)}, u32[]{:S(2)}, u32[]{:S(2)}) collective-permute-start(bf16[128,8,128]{2,1,0:T(8,128)(2,1)} %key_ref.1), channel_id=1, source_target_pairs={{0,1},{1,0},{2,3},{3,2},{4,5},{5,4},{6,7},{7,6},{8,9},{9,8},{10,11... | collective-permute-start | bytes 786440 | tf_op jit(solution)/shard_map/ppermute | solution.py:25
  1.4 0.1 pad_add_fusion.place_ref
  1.5 1.6 %fetch.1 = (bf16[4,2,128,128]{3,2,1,0:T(8,128)(2,1)S(1)}, bf16[128,8,128]{2,1,0:T(8,128)(2,1)S(1)}) custom-call(s32[2]{0:T(128)S(1)} %pad_add_fusion.place_ref, bf16[128,8,128]{2,1,0:T(8,128)(2,1)} %key_ref.1, bf16[128,8,128]{2,1,0:T(8,128)(2,1)} %refs_0_.1), custom_call_target="tpu_custom_call" | custom-call | flops 1000000000 | tf_op jit(solution)/shard_map/fetch/pallas_call | solution.py:38
  3.1 0.0 collective-permute-done.other_ref
  3.1 0.6 %pack_other.1.refs_0_ = bf16[4,2,128,128]{3,2,1,0:T(8,128)(2,1)S(1)} custom-call(s32[2]{0:T(128)S(1)} %pad_add_fusion.place_ref, bf16[128,8,128]{2,1,0:T(8,128)(2,1)S(1)} %collective-permute-done.other_ref, bf16[4,2,128,128]{3,2,1,0:T(8,128)(2,1)S(1)} %get-tuple-element.26._), custom_call_target="tpu_custom_call", output_to_operand_aliasing={{}: (2, {})} | custom-call | flops 1000000000 | tf_op jit(solution)/shard_map/pack_other/pallas_call | solution.py:38
  3.7 0.0 copy-start.2
  3.7 0.1 collective-permute-start.1
  3.9 0.4 collective-permute-start.2
  4.3 0.1 collective-permute-start.3
  4.4 3.1 %collective-permute-start.5 = (bf16[4,2,128,128]{3,2,1,0:T(8,128)(2,1)S(1)}, bf16[4,2,128,128]{3,2,1,0:T(8,128)(2,1)S(1)}, u32[]{:S(2)}, u32[]{:S(2)}) collective-permute-start(bf16[4,2,128,128]{3,2,1,0:T(8,128)(2,1)S(1)} %pack_other.1.refs_0_), channel_id=1, source_target_pairs={{0,4},{1,5},{2,6},{3,7},{4,8},{5,9},{6,10},{7,11},{8,12},{9,13},{1... | collective-permute-start | bytes 786440 | tf_op jit(solution)/shard_map/ppermute | solution.py:21
  7.5 3.1 %collective-permute-start.4 = (bf16[4,2,128,128]{3,2,1,0:T(8,128)(2,1)S(1)}, bf16[4,2,128,128]{3,2,1,0:T(8,128)(2,1)S(1)}, u32[]{:S(2)}, u32[]{:S(2)}) collective-permute-start(bf16[4,2,128,128]{3,2,1,0:T(8,128)(2,1)S(1)} %pack_other.1.refs_0_), channel_id=1, source_target_pairs={{0,2},{1,3},{2,4},{3,5},{4,6},{5,7},{6,8},{7,9},{8,10},{9,11},{10,... | collective-permute-start | bytes 786440 | tf_op jit(solution)/shard_map/ppermute | solution.py:21
  10.7 2.0 %arrange.1.qd_ref = bf16[4,2,2,4,128,128]{5,4,3,2,1,0:T(8,128)(2,1)S(1)} custom-call(s32[2]{0:T(128)S(1)} %pad_add_fusion.place_ref, bf16[128,32,128]{2,1,0:T(8,128)(2,1)S(1)} %copy-done, bf16[128,32,128]{2,1,0:T(8,128)(2,1)S(1)} %copy-done.1, bf16[128,32,128]{2,1,0:T(8,128)(2,1)S(1)} %collective-permute-done.1.q_other_ref, ...), custom_call_target="tpu_custom_call" | custom-call | flops 1000000000 | tf_op jit(solution)/shard_map/arrange/pallas_call | solution.py:38
  12.7 0.7 %pack_both.1.refs_0_ = bf16[4,2,128,128]{3,2,1,0:T(8,128)(2,1)S(1)} custom-call(s32[2]{0:T(128)S(1)} %pad_add_fusion.place_ref, bf16[128,8,128]{2,1,0:T(8,128)(2,1)S(1)} %get-tuple-element.34.own_ref, bf16[128,8,128]{2,1,0:T(8,128)(2,1)S(1)} %collective-permute-done.3.other_ref), custom_call_target="tpu_custom_call" | custom-call | flops 1000000000 | tf_op jit(solution)/shard_map/pack_both/pallas_call | solution.py:38
  13.4 1.9 %collective-permute-start.7 = (bf16[4,2,128,128]{3,2,1,0:T(8,128)(2,1)S(1)}, bf16[4,2,128,128]{3,2,1,0:T(8,128)(2,1)S(1)}, u32[]{:S(2)}, u32[]{:S(2)}) collective-permute-start(bf16[4,2,128,128]{3,2,1,0:T(8,128)(2,1)S(1)} %pack_both.1.refs_0_), channel_id=1, source_target_pairs={{0,4},{1,5},{2,6},{3,7},{4,8},{5,9},{6,10},{7,11},{8,12},{9,13},{1... | collective-permute-start | bytes 786440 | tf_op jit(solution)/shard_map/ppermute | solution.py:21
  15.4 3.1 %collective-permute-start.6 = (bf16[4,2,128,128]{3,2,1,0:T(8,128)(2,1)S(1)}, bf16[4,2,128,128]{3,2,1,0:T(8,128)(2,1)S(1)}, u32[]{:S(2)}, u32[]{:S(2)}) collective-permute-start(bf16[4,2,128,128]{3,2,1,0:T(8,128)(2,1)S(1)} %pack_both.1.refs_0_), channel_id=1, source_target_pairs={{0,2},{1,3},{2,4},{3,5},{4,6},{5,7},{6,8},{7,9},{8,10},{9,11},{10,... | collective-permute-start | bytes 786440 | tf_op jit(solution)/shard_map/ppermute | solution.py:21
  18.5 6.5 %prob.1 = (bf16[4,2,640,512]{3,2,1,0:T(8,128)(2,1)S(1)}, bf16[4,2,128,128]{3,2,1,0:T(8,128)(2,1)S(1)}, bf16[4,2,128,128]{3,2,1,0:T(8,128)(2,1)S(1)}) custom-call(s32[2]{0:T(128)S(1)} %pad_add_fusion.place_ref, s32[16]{0:T(128)S(1)} %copy-done.2, bf16[4,2,2,4,128,128]{5,4,3,2,1,0:T(8,128)(2,1)S(1)} %arrange.1.qd_ref, ...), custom_call_target="tpu_custom_call" | custom-call | flops 2684354560 | tf_op jit(solution)/shard_map/prob/pallas_call | solution.py:38
  25.1 3.4 %collective-permute-start.8 = (bf16[4,2,128,128]{3,2,1,0:T(8,128)(2,1)S(1)}, bf16[4,2,128,128]{3,2,1,0:T(8,128)(2,1)S(1)}, u32[]{:S(2)}, u32[]{:S(2)}) collective-permute-start(bf16[4,2,128,128]{3,2,1,0:T(8,128)(2,1)S(1)} %get-tuple-element.37), channel_id=1, source_target_pairs={{4,0},{5,1},{6,2},{7,3},{8,4},{9,5},{10,6},{11,7},{12,8},{13,9},{1... | collective-permute-start | bytes 786440 | tf_op jit(solution)/shard_map/ppermute | solution.py:21
  28.4 5.2 %collective-permute-start.9 = (bf16[4,2,128,128]{3,2,1,0:T(8,128)(2,1)S(1)}, bf16[4,2,128,128]{3,2,1,0:T(8,128)(2,1)S(1)}, u32[]{:S(2)}, u32[]{:S(2)}) collective-permute-start(bf16[4,2,128,128]{3,2,1,0:T(8,128)(2,1)S(1)} %get-tuple-element.38), channel_id=1, source_target_pairs={{2,0},{3,1},{4,2},{5,3},{6,4},{7,5},{8,6},{9,7},{10,8},{11,9},{12,... | collective-permute-start | bytes 786440 | tf_op jit(solution)/shard_map/ppermute | solution.py:21
  33.7 6.0 %dscore.1 = (bf16[4,2,640,512]{3,2,1,0:T(8,128)(2,1)S(1)}, bf16[4,2,128,128]{3,2,1,0:T(8,128)(2,1)S(1)}, bf16[4,2,128,128]{3,2,1,0:T(8,128)(2,1)S(1)}) custom-call(s32[2]{0:T(128)S(1)} %pad_add_fusion.place_ref, bf16[4,2,2,4,128,128]{5,4,3,2,1,0:T(8,128)(2,1)S(1)} %arrange.1.qd_ref, bf16[4,2,640,512]{3,2,1,0:T(8,128)(2,1)S(1)} %get-tuple-element.33.p_ref, ...), custom_call_target="tpu_custom_call" | custom-call | flops 2684354560 | tf_op jit(solution)/shard_map/dscore/pallas_call | solution.py:38
  39.7 1.9 %collective-permute-start.13 = (bf16[4,2,128,128]{3,2,1,0:T(8,128)(2,1)S(1)}, bf16[4,2,128,128]{3,2,1,0:T(8,128)(2,1)S(1)}, u32[]{:S(2)}, u32[]{:S(2)}) collective-permute-start(bf16[4,2,128,128]{3,2,1,0:T(8,128)(2,1)S(1)} %get-tuple-element.44), channel_id=1, source_target_pairs={{4,0},{5,1},{6,2},{7,3},{8,4},{9,5},{10,6},{11,7},{12,8},{13,9},{1... | collective-permute-start | bytes 786440 | tf_op jit(solution)/shard_map/ppermute | solution.py:21
  41.6 1.9 %collective-permute-start.14 = (bf16[4,2,128,128]{3,2,1,0:T(8,128)(2,1)S(1)}, bf16[4,2,128,128]{3,2,1,0:T(8,128)(2,1)S(1)}, u32[]{:S(2)}, u32[]{:S(2)}) collective-permute-start(bf16[4,2,128,128]{3,2,1,0:T(8,128)(2,1)S(1)} %get-tuple-element.45), channel_id=1, source_target_pairs={{2,0},{3,1},{4,2},{5,3},{6,4},{7,5},{8,6},{9,7},{10,8},{11,9},{12,... | collective-permute-start | bytes 786440 | tf_op jit(solution)/shard_map/ppermute | solution.py:21
  43.6 3.4 %own.1 = (bf16[128,16,128]{2,1,0:T(8,128)(2,1)S(1)}, bf16[56,16,128]{2,1,0:T(8,128)(2,1)S(1)}, bf16[56,16,128]{2,1,0:T(8,128)(2,1)S(1)}, bf16[48,16,128]{2,1,0:T...) custom-call(s32[2]{0:T(128)S(1)} %pad_add_fusion.place_ref, ...), custom_call_target="tpu_custom_call" | custom-call | tf_op jit(solution)/shard_map/own/pallas_call | solution.py:38
  47.0 4.5 %collective-permute-start.10 = (bf16[56,16,128]{2,1,0:T(8,128)(2,1)S(1)}, bf16[56,16,128]{2,1,0:T(8,128)(2,1)S(1)}, u32[]{:S(2)}, u32[]{:S(2)}) collective-permute-start(bf16[56,16,128]{2,1,0:T(8,128)(2,1)S(1)} %get-tuple-element.40), channel_id=1, source_target_pairs={{0,1},{1,0},{2,3},{3,2},{4,5},{5,4},{6,7},{7,6},{8,9},{9,8},{10,11... | collective-permute-start | bytes 688136 | tf_op jit(solution)/shard_map/ppermute | solution.py:25
  51.4 0.1 collective-permute-start.11
  51.5 0.4 collective-permute-start.12
  51.9 1.3 %collective-permute-done.12.refs_2_.other_ref = bf16[48,16,128]{2,1,0:T(8,128)(2,1)S(1)} collective-permute-done((bf16[48,16,128]{2,1,0:T(8,128)(2,1)S(1)}, bf16[48,16,128]{2,1,0:T(8,128)(2,1)S(1)}, u32[]{:S(2)}, u32[]{:S(2)}) %collective-permute-start.12) | collective-permute-done | bytes 196640 | tf_op jit(solution)/shard_map/ppermute | solution.py:25
  53.2 1.4 %merge_dv.1.refs_3_ = bf16[128,8,128]{2,1,0:T(8,128)(2,1)} custom-call(s32[2]{0:T(128)S(1)} %pad_add_fusion.place_ref, bf16[4,128,128]{2,1,0:T(8,128)(2,1)S(1)} %get-tuple-element.46.own_ref, bf16[48,16,128]{2,1,0:T(8,128)(2,1)S(1)} %collective-permute-done.12.refs_2_.other_ref), custom_call_target="tpu_custom_call" | custom-call | tf_op jit(solution)/shard_map/merge_dv/pallas_call | solution.py:38
  54.6 1.5 %join.1.refs_2_ = bf16[128,32,128]{2,1,0:T(8,128)(2,1)} custom-call(s32[2]{0:T(128)S(1)} %pad_add_fusion.place_ref, bf16[128,16,128]{2,1,0:T(8,128)(2,1)S(1)} %get-tuple-element.39.own_ref, bf16[56,16,128]{2,1,0:T(8,128)(2,1)S(1)} %collective-permute-done.10.refs_0_, bf16[56,16,128]{2,1,0:T(8,128)(2,1)S(1)} %collective-permute-done.11.refs_1_, ...), custom_call_target="tpu_custom_call" | custom-call | tf_op jit(solution)/shard_map/join/pallas_call | solution.py:38
  56.2 0.6 %sum_dk.1 = (bf16[4,128,128]{2,1,0:T(8,128)(2,1)S(1)}, bf16[4,128,128]{2,1,0:T(8,128)(2,1)S(1)}) custom-call(s32[2]{0:T(128)S(1)} %pad_add_fusion.place_ref, f32[4,2,128,128]{3,2,1,0:T(8,128)S(1)} %get-tuple-element.43.own_ref, bf16[4,2,128,128]{3,2,1,0:T(8,128)(2,1)S(1)} %collective-permute-done.13.refs_0_, ...), custom_call_target="tpu_custom_call" | custom-call | tf_op jit(solution)/shard_map/sum_dk/pallas_call | solution.py:38
  56.8 1.6 %collective-permute-start.15 = (bf16[4,128,128]{2,1,0:T(8,128)(2,1)S(1)}, bf16[4,128,128]{2,1,0:T(8,128)(2,1)S(1)}, u32[]{:S(2)}, u32[]{:S(2)}) collective-permute-start(bf16[4,128,128]{2,1,0:T(8,128)(2,1)S(1)} %get-tuple-element.48), channel_id=1, source_target_pairs={{0,1},{1,0},{2,3},{3,2},{4,5},{5,4},{6,7},{7,6},{8,9},{9,8},{10,11... | collective-permute-start | bytes 393224 | tf_op jit(solution)/shard_map/ppermute | solution.py:25
  58.4 1.0 %collective-permute-done.15.other_ref = bf16[4,128,128]{2,1,0:T(8,128)(2,1)S(1)} collective-permute-done((bf16[4,128,128]{2,1,0:T(8,128)(2,1)S(1)}, bf16[4,128,128]{2,1,0:T(8,128)(2,1)S(1)}, u32[]{:S(2)}, u32[]{:S(2)}) %collective-permute-start.15) | collective-permute-done | bytes 131104 | tf_op jit(solution)/shard_map/ppermute | solution.py:25
  59.4 1.4 %merge_dk.1 = bf16[128,8,128]{2,1,0:T(8,128)(2,1)} custom-call(s32[2]{0:T(128)S(1)} %pad_add_fusion.place_ref, bf16[4,128,128]{2,1,0:T(8,128)(2,1)S(1)} %get-tuple-element.47.own_ref, bf16[4,128,128]{2,1,0:T(8,128)(2,1)S(1)} %collective-permute-done.15.other_ref), custom_call_target="tpu_custom_call" | custom-call | tf_op jit(solution)/shard_map/merge_dk/pallas_call | solution.py:38
  (18 shorter events, 0.0 us)
Async XLA Ops:
  0.6 3.2 %copy-start.1 = (bf16[128,32,128]{2,1,0:T(8,128)(2,1)S(1)}, bf16[128,32,128]{2,1,0:T(8,128)(2,1)}, u32[]{:S(2)}) copy-start(bf16[128,32,128]{2,1,0:T(8,128)(2,1)} %do_ref) | copy-start | bytes 3145732
  0.6 3.1 %copy-start = (bf16[128,32,128]{2,1,0:T(8,128)(2,1)S(1)}, bf16[128,32,128]{2,1,0:T(8,128)(2,1)}, u32[]{:S(2)}) copy-start(bf16[128,32,128]{2,1,0:T(8,128)(2,1)} %q_ref) | copy-start | bytes 3145732
  0.6 2.4 %collective-permute-start = (bf16[128,8,128]{2,1,0:T(8,128)(2,1)}, bf16[128,8,128]{2,1,0:T(8,128)(2,1)S(1)}, u32[]{:S(2)}, u32[]{:S(2)}) collective-permute-start(bf16[128,8,128]{2,1,0:T(8,128)(2,1)} %key_ref.1), channel_id=1, source_target_pairs={{0,1},{1,0},{2,3},{3,2},{4,5},{5,4},{6,7},{7,6},{8,9},{9,8},{10,11... | collective-permute-start | bytes 786440 | tf_op jit(solution)/shard_map/ppermute | solution.py:25
  3.7 14.8 %copy-start.2 = (s32[16]{0:T(128)S(1)}, s32[16]{0:T(128)}, u32[]{:S(2)}) copy-start(s32[16]{0:T(128)} %lengths_ref.1) | copy-start | bytes 196
  3.7 6.9 %collective-permute-start.1 = (bf16[128,32,128]{2,1,0:T(8,128)(2,1)S(1)}, bf16[128,32,128]{2,1,0:T(8,128)(2,1)S(1)}, u32[]{:S(2)}, u32[]{:S(2)}) collective-permute-start(bf16[128,32,128]{2,1,0:T(8,128)(2,1)S(1)} %copy-done), channel_id=1, source_target_pairs={{0,1},{1,0},{2,3},{3,2},{4,5},{5,4},{6,7},{7,6},{8,9},{9,8},{10,11... | collective-permute-start | bytes 3145736 | tf_op jit(solution)/shard_map/ppermute | solution.py:25
  3.9 6.8 %collective-permute-start.2 = (bf16[128,32,128]{2,1,0:T(8,128)(2,1)S(1)}, bf16[128,32,128]{2,1,0:T(8,128)(2,1)S(1)}, u32[]{:S(2)}, u32[]{:S(2)}) collective-permute-start(bf16[128,32,128]{2,1,0:T(8,128)(2,1)S(1)} %copy-done.1), channel_id=1, source_target_pairs={{0,1},{1,0},{2,3},{3,2},{4,5},{5,4},{6,7},{7,6},{8,9},{9,8},{10,11... | collective-permute-start | bytes 3145736 | tf_op jit(solution)/shard_map/ppermute | solution.py:25
  4.3 8.4 %collective-permute-start.3 = (bf16[128,8,128]{2,1,0:T(8,128)(2,1)S(1)}, bf16[128,8,128]{2,1,0:T(8,128)(2,1)S(1)}, u32[]{:S(2)}, u32[]{:S(2)}) collective-permute-start(bf16[128,8,128]{2,1,0:T(8,128)(2,1)S(1)} %get-tuple-element.34.own_ref), channel_id=1, source_target_pairs={{0,1},{1,0},{2,3},{3,2},{4,5},{5,4},{6,7},{7,6},{8,9},{9,8},{10,11... | collective-permute-start | bytes 786440 | tf_op jit(solution)/shard_map/ppermute | solution.py:25
  4.4 14.1 %collective-permute-start.5 = (bf16[4,2,128,128]{3,2,1,0:T(8,128)(2,1)S(1)}, bf16[4,2,128,128]{3,2,1,0:T(8,128)(2,1)S(1)}, u32[]{:S(2)}, u32[]{:S(2)}) collective-permute-start(bf16[4,2,128,128]{3,2,1,0:T(8,128)(2,1)S(1)} %pack_other.1.refs_0_), channel_id=1, source_target_pairs={{0,4},{1,5},{2,6},{3,7},{4,8},{5,9},{6,10},{7,11},{8,12},{9,13},{1... | collective-permute-start | bytes 786440 | tf_op jit(solution)/shard_map/ppermute | solution.py:21
  7.5 11.0 %collective-permute-start.4 = (bf16[4,2,128,128]{3,2,1,0:T(8,128)(2,1)S(1)}, bf16[4,2,128,128]{3,2,1,0:T(8,128)(2,1)S(1)}, u32[]{:S(2)}, u32[]{:S(2)}) collective-permute-start(bf16[4,2,128,128]{3,2,1,0:T(8,128)(2,1)S(1)} %pack_other.1.refs_0_), channel_id=1, source_target_pairs={{0,2},{1,3},{2,4},{3,5},{4,6},{5,7},{6,8},{7,9},{8,10},{9,11},{10,... | collective-permute-start | bytes 786440 | tf_op jit(solution)/shard_map/ppermute | solution.py:21
  13.4 20.2 %collective-permute-start.7 = (bf16[4,2,128,128]{3,2,1,0:T(8,128)(2,1)S(1)}, bf16[4,2,128,128]{3,2,1,0:T(8,128)(2,1)S(1)}, u32[]{:S(2)}, u32[]{:S(2)}) collective-permute-start(bf16[4,2,128,128]{3,2,1,0:T(8,128)(2,1)S(1)} %pack_both.1.refs_0_), channel_id=1, source_target_pairs={{0,4},{1,5},{2,6},{3,7},{4,8},{5,9},{6,10},{7,11},{8,12},{9,13},{1... | collective-permute-start | bytes 786440 | tf_op jit(solution)/shard_map/ppermute | solution.py:21
  15.4 18.3 %collective-permute-start.6 = (bf16[4,2,128,128]{3,2,1,0:T(8,128)(2,1)S(1)}, bf16[4,2,128,128]{3,2,1,0:T(8,128)(2,1)S(1)}, u32[]{:S(2)}, u32[]{:S(2)}) collective-permute-start(bf16[4,2,128,128]{3,2,1,0:T(8,128)(2,1)S(1)} %pack_both.1.refs_0_), channel_id=1, source_target_pairs={{0,2},{1,3},{2,4},{3,5},{4,6},{5,7},{6,8},{7,9},{8,10},{9,11},{10,... | collective-permute-start | bytes 786440 | tf_op jit(solution)/shard_map/ppermute | solution.py:21
  25.1 18.5 %collective-permute-start.8 = (bf16[4,2,128,128]{3,2,1,0:T(8,128)(2,1)S(1)}, bf16[4,2,128,128]{3,2,1,0:T(8,128)(2,1)S(1)}, u32[]{:S(2)}, u32[]{:S(2)}) collective-permute-start(bf16[4,2,128,128]{3,2,1,0:T(8,128)(2,1)S(1)} %get-tuple-element.37), channel_id=1, source_target_pairs={{4,0},{5,1},{6,2},{7,3},{8,4},{9,5},{10,6},{11,7},{12,8},{13,9},{1... | collective-permute-start | bytes 786440 | tf_op jit(solution)/shard_map/ppermute | solution.py:21
  28.4 15.2 %collective-permute-start.9 = (bf16[4,2,128,128]{3,2,1,0:T(8,128)(2,1)S(1)}, bf16[4,2,128,128]{3,2,1,0:T(8,128)(2,1)S(1)}, u32[]{:S(2)}, u32[]{:S(2)}) collective-permute-start(bf16[4,2,128,128]{3,2,1,0:T(8,128)(2,1)S(1)} %get-tuple-element.38), channel_id=1, source_target_pairs={{2,0},{3,1},{4,2},{5,3},{6,4},{7,5},{8,6},{9,7},{10,8},{11,9},{12,... | collective-permute-start | bytes 786440 | tf_op jit(solution)/shard_map/ppermute | solution.py:21
  39.7 16.5 %collective-permute-start.13 = (bf16[4,2,128,128]{3,2,1,0:T(8,128)(2,1)S(1)}, bf16[4,2,128,128]{3,2,1,0:T(8,128)(2,1)S(1)}, u32[]{:S(2)}, u32[]{:S(2)}) collective-permute-start(bf16[4,2,128,128]{3,2,1,0:T(8,128)(2,1)S(1)} %get-tuple-element.44), channel_id=1, source_target_pairs={{4,0},{5,1},{6,2},{7,3},{8,4},{9,5},{10,6},{11,7},{12,8},{13,9},{1... | collective-permute-start | bytes 786440 | tf_op jit(solution)/shard_map/ppermute | solution.py:21
  41.6 14.5 %collective-permute-start.14 = (bf16[4,2,128,128]{3,2,1,0:T(8,128)(2,1)S(1)}, bf16[4,2,128,128]{3,2,1,0:T(8,128)(2,1)S(1)}, u32[]{:S(2)}, u32[]{:S(2)}) collective-permute-start(bf16[4,2,128,128]{3,2,1,0:T(8,128)(2,1)S(1)} %get-tuple-element.45), channel_id=1, source_target_pairs={{2,0},{3,1},{4,2},{5,3},{6,4},{7,5},{8,6},{9,7},{10,8},{11,9},{12,... | collective-permute-start | bytes 786440 | tf_op jit(solution)/shard_map/ppermute | solution.py:21
  47.0 7.6 %collective-permute-start.10 = (bf16[56,16,128]{2,1,0:T(8,128)(2,1)S(1)}, bf16[56,16,128]{2,1,0:T(8,128)(2,1)S(1)}, u32[]{:S(2)}, u32[]{:S(2)}) collective-permute-start(bf16[56,16,128]{2,1,0:T(8,128)(2,1)S(1)} %get-tuple-element.40), channel_id=1, source_target_pairs={{0,1},{1,0},{2,3},{3,2},{4,5},{5,4},{6,7},{7,6},{8,9},{9,8},{10,11... | collective-permute-start | bytes 688136 | tf_op jit(solution)/shard_map/ppermute | solution.py:25
  51.4 3.2 %collective-permute-start.11 = (bf16[56,16,128]{2,1,0:T(8,128)(2,1)S(1)}, bf16[56,16,128]{2,1,0:T(8,128)(2,1)S(1)}, u32[]{:S(2)}, u32[]{:S(2)}) collective-permute-start(bf16[56,16,128]{2,1,0:T(8,128)(2,1)S(1)} %get-tuple-element.41), channel_id=1, source_target_pairs={{0,1},{1,0},{2,3},{3,2},{4,5},{5,4},{6,7},{7,6},{8,9},{9,8},{10,11... | collective-permute-start | bytes 688136 | tf_op jit(solution)/shard_map/ppermute | solution.py:25
  51.5 1.7 %collective-permute-start.12 = (bf16[48,16,128]{2,1,0:T(8,128)(2,1)S(1)}, bf16[48,16,128]{2,1,0:T(8,128)(2,1)S(1)}, u32[]{:S(2)}, u32[]{:S(2)}) collective-permute-start(bf16[48,16,128]{2,1,0:T(8,128)(2,1)S(1)} %get-tuple-element.42), channel_id=1, source_target_pairs={{0,1},{1,0},{2,3},{3,2},{4,5},{5,4},{6,7},{7,6},{8,9},{9,8},{10,11... | collective-permute-start | bytes 589832 | tf_op jit(solution)/shard_map/ppermute | solution.py:25
  56.8 2.6 %collective-permute-start.15 = (bf16[4,128,128]{2,1,0:T(8,128)(2,1)S(1)}, bf16[4,128,128]{2,1,0:T(8,128)(2,1)S(1)}, u32[]{:S(2)}, u32[]{:S(2)}) collective-permute-start(bf16[4,128,128]{2,1,0:T(8,128)(2,1)S(1)} %get-tuple-element.48), channel_id=1, source_target_pairs={{0,1},{1,0},{2,3},{3,2},{4,5},{5,4},{6,7},{7,6},{8,9},{9,8},{10,11... | collective-permute-start | bytes 393224 | tf_op jit(solution)/shard_map/ppermute | solution.py:25

commit v13 on v12

--- a/solution.py
+++ b/solution.py
@@ -10,7 +10,7 @@
 AXES = ("ctx", "uly")
 MASKED = -1e30
 LOG2E = 1.4426950408889634
-HEADS_AT_ONCE = 2
+HEADS_AT_ONCE = 1
 BF16, F32 = jnp.bfloat16, jnp.float32
 NT = (((1,), (1,)), ((), ()))
 VMEM_BYTES = 16 * 2**20
@@ -297,7 +297,7 @@
 
 def own_kernel(halo, place_ref, qd_ref, p_ref, ds_ref, *refs):
     k_refs, back_refs = refs[: halo + 1], refs[halo + 1 : 2 * halo + 1]
-    dq_ref, *other_refs, dk_ref, dv_ref, k_scr, dq_scr, dv_scr, far_scr = refs[2 * halo + 1 :]
+    dq_ref, *other_refs, dk_ref, dv_ref, k_scr, dq_scr, dv_scr, far_dv = refs[2 * halo + 1 :]
     core, head = place_ref[0], pl.program_id(0)
     _, _, _, group, tokens, dim = qd_ref.shape
     rows = dq_ref.shape[1]
@@ -323,18 +323,18 @@
     for ref in back_refs:
         dv_scr[...] += ref[0].astype(F32)
     dv_ref[0] = dv_scr[core].astype(BF16)
-    dq_rows = tokens * rows
-    at = dq_rows + head * tokens
-    far_scr[pl.ds(pl.multiple_of(at, tokens), tokens)] = dv_scr[1 - core].astype(BF16)
+    far_dv[pl.ds(pl.multiple_of(head * tokens, tokens), tokens)] = dv_scr[1 - core].astype(BF16)
 
     @pl.when(head == pl.num_programs(0) - 1)
     def _():
         dq_ref[...] = dq_scr[core].astype(BF16).reshape(dq_ref.shape)
-        far_scr[:dq_rows] = dq_scr[1 - core].astype(BF16)
-        start = 0
+        dq_rows, start = tokens * rows, 0
         for ref in other_refs:
             part = ref.shape[0] * rows
-            ref[...] = far_scr[start : start + part].reshape(ref.shape)
+            here = min(part, dq_rows - start)
+            ref[: here // rows] = dq_scr[1 - core, start : start + here].astype(BF16).reshape(-1, rows, dim)
+            if here < part:
+                ref[here // rows :] = far_dv[...].reshape(-1, rows, dim)
             start += part
 
 
@@ -366,47 +366,9 @@
     )
 
 
-def join_kernel(parts, place_ref, own_ref, *refs):
-    others, out_ref, sems = refs[:parts], refs[-2], refs[-1]
-    core = place_ref[0]
-    tokens, half, _ = own_ref.shape
-    at = pl.multiple_of(core * half, half)
-    copies = [pltpu.make_async_copy(own_ref, out_ref.at[:, pl.ds(at, half)], sems.at[0])]
-    at = pl.multiple_of((1 - core) * half, half)
-    first = 0
-    for i, part in enumerate(others):
-        count = min(part.shape[0], tokens - first)
-        to = out_ref.at[pl.ds(first, count), pl.ds(at, half)]
-        copies.append(pltpu.make_async_copy(part.at[pl.ds(0, count)], to, sems.at[1 + i]))
-        first += count
-    for copy in copies:
-        copy.start()
-    for copy in copies:
-        copy.wait()
-
-
-def join(place, own, others):
-    tokens, half, dim = own.shape
-    anywhere = pl.BlockSpec(memory_space=pl.ANY)
-    return call(
-        functools.partial(join_kernel, len(others)),
-        "join",
-        (1,),
-        place,
-        (own, *others),
-        [anywhere] * (1 + len(others)),
-        jax.ShapeDtypeStruct((tokens, 2 * half, dim), BF16),
-        anywhere,
-        [pltpu.SemaphoreType.DMA((1 + len(others),))],
-        0,
-    )
-
-
-def merge_kernel(place_ref, own_ref, other_ref, out_ref, scr):
-    core = place_ref[0]
+def merge_half(core, own_ref, other, out_ref, scr):
     rows, heads, dim = out_ref.shape
     half = heads // 2
-    other = other_ref[...].reshape(-1, dim)
     skip = other.shape[0] - half * rows
     for h in range(half):
         scr[pl.ds(core * half + h, rows, stride=heads), :] = own_ref[h].astype(F32)
@@ -415,16 +377,60 @@
     out_ref[...] = scr[...].astype(BF16).reshape(rows, heads, dim)
 
 
+def join_kernel(parts, place_ref, dq_ref, dv_ref, *refs):
+    others, (dq_out, dv_out, scr, sems) = refs[:parts], refs[parts:]
+    core = place_ref[0]
+    tokens, half, dim = dq_ref.shape
+    at = pl.multiple_of(core * half, half)
+    copies = [pltpu.make_async_copy(dq_ref, dq_out.at[:, pl.ds(at, half)], sems.at[0])]
+    at = pl.multiple_of((1 - core) * half, half)
+    first = 0
+    for i, part in enumerate(others):
+        count = min(part.shape[0], tokens - first)
+        to = dq_out.at[pl.ds(first, count), pl.ds(at, half)]
+        copies.append(pltpu.make_async_copy(part.at[pl.ds(0, count)], to, sems.at[1 + i]))
+        first += count
+    for copy in copies:
+        copy.start()
+    merge_half(core, dv_ref, others[-1][...].reshape(-1, dim), dv_out, scr)
+    for copy in copies:
+        copy.wait()
+
+
+def join(place, dq, dv, others):
+    tokens, half, dim = dq.shape
+    out = (tokens, 2 * dv.shape[0], dim)
+    vmem = pl.BlockSpec(memory_space=pltpu.VMEM)
+    parts = len(others)
+    return call(
+        functools.partial(join_kernel, parts),
+        "join",
+        (1,),
+        place,
+        [in_vmem(x) for x in (dq, dv, *others)],
+        [vmem] * (2 + parts),
+        [jax.ShapeDtypeStruct((tokens, 2 * half, dim), BF16), jax.ShapeDtypeStruct(out, BF16)],
+        [pl.BlockSpec(memory_space=pl.ANY), pl.BlockSpec(out, lambda i, place: (0, 0, 0))],
+        [pltpu.VMEM((tokens * out[1], dim), F32), pltpu.SemaphoreType.DMA((1 + parts,))],
+        0,
+    )
+
+
+def merge_kernel(place_ref, own_ref, other_ref, out_ref, scr):
+    merge_half(place_ref[0], own_ref, other_ref[...].reshape(-1, own_ref.shape[2]), out_ref, scr)
+
+
 def merge(place, own, other, name):
     half, tokens, dim = own.shape
     out = (tokens, 2 * half, dim)
+    vmem = pl.BlockSpec(memory_space=pltpu.VMEM)
     return call(
         merge_kernel,
         name,
         (1,),
         place,
-        (own, other),
-        [pl.BlockSpec(x.shape, lambda i, place: (0, 0, 0)) for x in (own, other)],
+        (in_vmem(own), in_vmem(other)),
+        [vmem] * 2,
         jax.ShapeDtypeStruct(out, BF16),
         pl.BlockSpec(out, lambda i, place: (0, 0, 0)),
         [pltpu.VMEM((tokens * 2 * half, dim), F32)],
@@ -525,13 +531,12 @@
             run,
             pltpu.VMEM((2, tokens * heads // 2, dim), F32),
             pltpu.VMEM((2, tokens, dim), F32),
-            pltpu.VMEM((far_rows * heads // 2, dim), BF16),
+            pltpu.VMEM((half * tokens, dim), BF16),
         ],
         0,
     )
     others = [swapped(part, device_count) for part in others]
-    grad_queries = join(place, dq, others)
-    grad_values = merge(place, dv, others[-1], "merge_dv")
+    grad_queries, grad_values = join(place, dq, dv, others)
     dk, dk_other = summed(place, dk_own, dk_back, (grad_queries, grad_values))
     grad_keys = merge(place, dk, swapped(dk_other, device_count), "merge_dk")
     return grad_queries, grad_keys, grad_values

time: 61.2 us -> 61.6 us (level)
    pallas_call x11 -> x10, Pallas kernels: 25.8 us -> 26 us  [call(): pl.pallas_call(kernel, out_shape=outs, grid_spec=pltpu.PrefetchScalarGrid...]
where the time goes in v13:
time: 61.6 us; the launch traced here: 61.3 us
  starting transfers between devices  32 us (52%)
  Pallas kernels  26 us (42%)
  waiting for transfers between devices  2.28 us (4%)
  between operations  0.89 us (1%)
    pallas_call x10, Pallas kernels, call(): pl.pallas_call(kernel, out_shape=outs, grid_spec=pltpu.PrefetchScalarGrid...  26 us
    ppermute x8, starting transfers between devices, moved(): return lax.ppermute(array, AXES, pairs)  23.7 us
    ppermute x8, starting transfers between devices, swapped(): return lax.ppermute(array, AXES, [(d, d ^ 1) for d in range(device_count)])  8.32 us
    ppermute x8, waiting for transfers between devices, swapped(): return lax.ppermute(array, AXES, [(d, d ^ 1) for d in range(device_count)])  2.26 us
  transfers between devices with their start and end apart: 16, of which 2 were waited for; matrix products, arithmetic and copies ran while one was open for 0% of the time, Pallas kernels for 38%

profile of v13, /device:TPU:23, one launch (start us, length us, event | category | flops | bytes accessed | tf_op | source)
XLA Modules:
  0.0 61.3 jit_solution(10223896404315450775)
XLA Ops:
  0.6 0.7 %collective-permute-start = (bf16[128,8,128]{2,1,0:T(8,128)(2,1)}, bf16[128,8,128]{2,1,0:T(8,128)(2,1)S(1)}, u32[]{:S(2)}, u32[]{:S(2)}) collective-permute-start(bf16[128,8,128]{2,1,0:T(8,128)(2,1)} %key_ref.1), channel_id=1, source_target_pairs={{0,1},{1,0},{2,3},{3,2},{4,5},{5,4},{6,7},{7,6},{8,9},{9,8},{10,11... | collective-permute-start | bytes 786440 | tf_op jit(solution)/shard_map/ppermute | solution.py:25
  1.4 0.1 pad_add_fusion.place_ref
  1.5 1.6 %fetch.1 = (bf16[4,2,128,128]{3,2,1,0:T(8,128)(2,1)S(1)}, bf16[128,8,128]{2,1,0:T(8,128)(2,1)S(1)}) custom-call(s32[2]{0:T(128)S(1)} %pad_add_fusion.place_ref, bf16[128,8,128]{2,1,0:T(8,128)(2,1)} %key_ref.1, bf16[128,8,128]{2,1,0:T(8,128)(2,1)} %refs_0_.1), custom_call_target="tpu_custom_call" | custom-call | flops 1000000000 | tf_op jit(solution)/shard_map/fetch/pallas_call | solution.py:38
  3.1 0.6 %pack_other.1.refs_0_ = bf16[4,2,128,128]{3,2,1,0:T(8,128)(2,1)S(1)} custom-call(s32[2]{0:T(128)S(1)} %pad_add_fusion.place_ref, bf16[128,8,128]{2,1,0:T(8,128)(2,1)S(1)} %collective-permute-done.other_ref, bf16[4,2,128,128]{3,2,1,0:T(8,128)(2,1)S(1)} %get-tuple-element.28._), custom_call_target="tpu_custom_call", output_to_operand_aliasing={{}: (2, {})} | custom-call | flops 1000000000 | tf_op jit(solution)/shard_map/pack_other/pallas_call | solution.py:38
  3.7 0.0 copy-start.2
  3.7 0.1 collective-permute-start.1
  3.9 0.4 collective-permute-start.2
  4.3 0.1 collective-permute-start.3
  4.4 3.1 %collective-permute-start.5 = (bf16[4,2,128,128]{3,2,1,0:T(8,128)(2,1)S(1)}, bf16[4,2,128,128]{3,2,1,0:T(8,128)(2,1)S(1)}, u32[]{:S(2)}, u32[]{:S(2)}) collective-permute-start(bf16[4,2,128,128]{3,2,1,0:T(8,128)(2,1)S(1)} %pack_other.1.refs_0_), channel_id=1, source_target_pairs={{0,4},{1,5},{2,6},{3,7},{4,8},{5,9},{6,10},{7,11},{8,12},{9,13},{1... | collective-permute-start | bytes 786440 | tf_op jit(solution)/shard_map/ppermute | solution.py:21
  7.5 3.1 %collective-permute-start.4 = (bf16[4,2,128,128]{3,2,1,0:T(8,128)(2,1)S(1)}, bf16[4,2,128,128]{3,2,1,0:T(8,128)(2,1)S(1)}, u32[]{:S(2)}, u32[]{:S(2)}) collective-permute-start(bf16[4,2,128,128]{3,2,1,0:T(8,128)(2,1)S(1)} %pack_other.1.refs_0_), channel_id=1, source_target_pairs={{0,2},{1,3},{2,4},{3,5},{4,6},{5,7},{6,8},{7,9},{8,10},{9,11},{10,... | collective-permute-start | bytes 786440 | tf_op jit(solution)/shard_map/ppermute | solution.py:21
  10.7 2.0 %arrange.1.qd_ref = bf16[4,2,2,4,128,128]{5,4,3,2,1,0:T(8,128)(2,1)S(1)} custom-call(s32[2]{0:T(128)S(1)} %pad_add_fusion.place_ref, bf16[128,32,128]{2,1,0:T(8,128)(2,1)S(1)} %copy-done, bf16[128,32,128]{2,1,0:T(8,128)(2,1)S(1)} %copy-done.1, bf16[128,32,128]{2,1,0:T(8,128)(2,1)S(1)} %collective-permute-done.1.q_other_ref, ...), custom_call_target="tpu_custom_call" | custom-call | flops 1000000000 | tf_op jit(solution)/shard_map/arrange/pallas_call | solution.py:38
  12.7 0.7 %pack_both.1.refs_0_ = bf16[4,2,128,128]{3,2,1,0:T(8,128)(2,1)S(1)} custom-call(s32[2]{0:T(128)S(1)} %pad_add_fusion.place_ref, bf16[128,8,128]{2,1,0:T(8,128)(2,1)S(1)} %get-tuple-element.36.own_ref, bf16[128,8,128]{2,1,0:T(8,128)(2,1)S(1)} %collective-permute-done.3.other_ref), custom_call_target="tpu_custom_call" | custom-call | flops 1000000000 | tf_op jit(solution)/shard_map/pack_both/pallas_call | solution.py:38
  13.4 1.9 %collective-permute-start.7 = (bf16[4,2,128,128]{3,2,1,0:T(8,128)(2,1)S(1)}, bf16[4,2,128,128]{3,2,1,0:T(8,128)(2,1)S(1)}, u32[]{:S(2)}, u32[]{:S(2)}) collective-permute-start(bf16[4,2,128,128]{3,2,1,0:T(8,128)(2,1)S(1)} %pack_both.1.refs_0_), channel_id=1, source_target_pairs={{0,4},{1,5},{2,6},{3,7},{4,8},{5,9},{6,10},{7,11},{8,12},{9,13},{1... | collective-permute-start | bytes 786440 | tf_op jit(solution)/shard_map/ppermute | solution.py:21
  15.4 3.1 %collective-permute-start.6 = (bf16[4,2,128,128]{3,2,1,0:T(8,128)(2,1)S(1)}, bf16[4,2,128,128]{3,2,1,0:T(8,128)(2,1)S(1)}, u32[]{:S(2)}, u32[]{:S(2)}) collective-permute-start(bf16[4,2,128,128]{3,2,1,0:T(8,128)(2,1)S(1)} %pack_both.1.refs_0_), channel_id=1, source_target_pairs={{0,2},{1,3},{2,4},{3,5},{4,6},{5,7},{6,8},{7,9},{8,10},{9,11},{10,... | collective-permute-start | bytes 786440 | tf_op jit(solution)/shard_map/ppermute | solution.py:21
  18.5 0.0 collective-permute-done.5.refs_2_
  18.5 0.0 collective-permute-done.4.refs_1_
  18.5 7.1 %prob.1 = (bf16[4,2,640,512]{3,2,1,0:T(8,128)(2,1)S(1)}, bf16[4,2,128,128]{3,2,1,0:T(8,128)(2,1)S(1)}, bf16[4,2,128,128]{3,2,1,0:T(8,128)(2,1)S(1)}) custom-call(s32[2]{0:T(128)S(1)} %pad_add_fusion.place_ref, s32[16]{0:T(128)S(1)} %copy-done.2, bf16[4,2,2,4,128,128]{5,4,3,2,1,0:T(8,128)(2,1)S(1)} %arrange.1.qd_ref, ...), custom_call_target="tpu_custom_call" | custom-call | flops 2684354560 | tf_op jit(solution)/shard_map/prob/pallas_call | solution.py:38
  25.6 3.4 %collective-permute-start.8 = (bf16[4,2,128,128]{3,2,1,0:T(8,128)(2,1)S(1)}, bf16[4,2,128,128]{3,2,1,0:T(8,128)(2,1)S(1)}, u32[]{:S(2)}, u32[]{:S(2)}) collective-permute-start(bf16[4,2,128,128]{3,2,1,0:T(8,128)(2,1)S(1)} %get-tuple-element.39), channel_id=1, source_target_pairs={{4,0},{5,1},{6,2},{7,3},{8,4},{9,5},{10,6},{11,7},{12,8},{13,9},{1... | collective-permute-start | bytes 786440 | tf_op jit(solution)/shard_map/ppermute | solution.py:21
  29.0 5.2 %collective-permute-start.9 = (bf16[4,2,128,128]{3,2,1,0:T(8,128)(2,1)S(1)}, bf16[4,2,128,128]{3,2,1,0:T(8,128)(2,1)S(1)}, u32[]{:S(2)}, u32[]{:S(2)}) collective-permute-start(bf16[4,2,128,128]{3,2,1,0:T(8,128)(2,1)S(1)} %get-tuple-element.40), channel_id=1, source_target_pairs={{2,0},{3,1},{4,2},{5,3},{6,4},{7,5},{8,6},{9,7},{10,8},{11,9},{12,... | collective-permute-start | bytes 786440 | tf_op jit(solution)/shard_map/ppermute | solution.py:21
  34.2 6.4 %dscore.1 = (bf16[4,2,640,512]{3,2,1,0:T(8,128)(2,1)S(1)}, bf16[4,2,128,128]{3,2,1,0:T(8,128)(2,1)S(1)}, bf16[4,2,128,128]{3,2,1,0:T(8,128)(2,1)S(1)}) custom-call(s32[2]{0:T(128)S(1)} %pad_add_fusion.place_ref, bf16[4,2,2,4,128,128]{5,4,3,2,1,0:T(8,128)(2,1)S(1)} %arrange.1.qd_ref, bf16[4,2,640,512]{3,2,1,0:T(8,128)(2,1)S(1)} %get-tuple-element.35.p_ref, ...), custom_call_target="tpu_custom_call" | custom-call | flops 2684354560 | tf_op jit(solution)/shard_map/dscore/pallas_call | solution.py:38
  40.6 1.9 %collective-permute-start.13 = (bf16[4,2,128,128]{3,2,1,0:T(8,128)(2,1)S(1)}, bf16[4,2,128,128]{3,2,1,0:T(8,128)(2,1)S(1)}, u32[]{:S(2)}, u32[]{:S(2)}) collective-permute-start(bf16[4,2,128,128]{3,2,1,0:T(8,128)(2,1)S(1)} %get-tuple-element.48), channel_id=1, source_target_pairs={{4,0},{5,1},{6,2},{7,3},{8,4},{9,5},{10,6},{11,7},{12,8},{13,9},{1... | collective-permute-start | bytes 786440 | tf_op jit(solution)/shard_map/ppermute | solution.py:21
  42.6 1.9 %collective-permute-start.14 = (bf16[4,2,128,128]{3,2,1,0:T(8,128)(2,1)S(1)}, bf16[4,2,128,128]{3,2,1,0:T(8,128)(2,1)S(1)}, u32[]{:S(2)}, u32[]{:S(2)}) collective-permute-start(bf16[4,2,128,128]{3,2,1,0:T(8,128)(2,1)S(1)} %get-tuple-element.49), channel_id=1, source_target_pairs={{2,0},{3,1},{4,2},{5,3},{6,4},{7,5},{8,6},{9,7},{10,8},{11,9},{12,... | collective-permute-start | bytes 786440 | tf_op jit(solution)/shard_map/ppermute | solution.py:21
  44.5 3.4 %own.1 = (bf16[128,16,128]{2,1,0:T(8,128)(2,1)S(1)}, bf16[56,16,128]{2,1,0:T(8,128)(2,1)S(1)}, bf16[56,16,128]{2,1,0:T(8,128)(2,1)S(1)}, bf16[48,16,128]{2,1,0:T...) custom-call(s32[2]{0:T(128)S(1)} %pad_add_fusion.place_ref, ...), custom_call_target="tpu_custom_call" | custom-call | tf_op jit(solution)/shard_map/own/pallas_call | solution.py:38
  47.9 3.5 %collective-permute-start.10 = (bf16[56,16,128]{2,1,0:T(8,128)(2,1)S(1)}, bf16[56,16,128]{2,1,0:T(8,128)(2,1)S(1)}, u32[]{:S(2)}, u32[]{:S(2)}) collective-permute-start(bf16[56,16,128]{2,1,0:T(8,128)(2,1)S(1)} %get-tuple-element.43), channel_id=1, source_target_pairs={{0,1},{1,0},{2,3},{3,2},{4,5},{5,4},{6,7},{7,6},{8,9},{9,8},{10,11... | collective-permute-start | bytes 688136 | tf_op jit(solution)/shard_map/ppermute | solution.py:25
  51.4 0.1 collective-permute-start.11
  51.5 0.4 collective-permute-start.12
  51.9 1.3 %collective-permute-done.12.refs_2_ = bf16[48,16,128]{2,1,0:T(8,128)(2,1)S(1)} collective-permute-done((bf16[48,16,128]{2,1,0:T(8,128)(2,1)S(1)}, bf16[48,16,128]{2,1,0:T(8,128)(2,1)S(1)}, u32[]{:S(2)}, u32[]{:S(2)}) %collective-permute-start.12) | collective-permute-done | bytes 196640 | tf_op jit(solution)/shard_map/ppermute | solution.py:25
  53.2 2.2 %join.1 = (bf16[128,32,128]{2,1,0:T(8,128)(2,1)}, bf16[128,8,128]{2,1,0:T(8,128)(2,1)}) custom-call(s32[2]{0:T(128)S(1)} %pad_add_fusion.place_ref, bf16[128,16,128]{2,1,0:T(8,128)(2,1)S(1)} %get-tuple-element.41.dq_ref, bf16[4,128,128]{2,1,0:T(8,128)(2,1)S(1)} %get-tuple-element.42.dv_ref, bf16[56,16,128]{2,1,0:T(8,128)(2,1)S(1)} %collective-permute-done.10.refs_0_, ...), custom_call_target="tpu_custom_call" | custom-call | tf_op jit(solution)/shard_map/join/pallas_call | solution.py:38
  55.4 0.6 %sum_dk.1 = (bf16[4,128,128]{2,1,0:T(8,128)(2,1)S(1)}, bf16[4,128,128]{2,1,0:T(8,128)(2,1)S(1)}) custom-call(s32[2]{0:T(128)S(1)} %pad_add_fusion.place_ref, f32[4,2,128,128]{3,2,1,0:T(8,128)S(1)} %get-tuple-element.47.own_ref, bf16[4,2,128,128]{3,2,1,0:T(8,128)(2,1)S(1)} %collective-permute-done.13.refs_0_, ...), custom_call_target="tpu_custom_call" | custom-call | tf_op jit(solution)/shard_map/sum_dk/pallas_call | solution.py:38
  56.1 2.9 %collective-permute-start.15 = (bf16[4,128,128]{2,1,0:T(8,128)(2,1)S(1)}, bf16[4,128,128]{2,1,0:T(8,128)(2,1)S(1)}, u32[]{:S(2)}, u32[]{:S(2)}) collective-permute-start(bf16[4,128,128]{2,1,0:T(8,128)(2,1)S(1)} %get-tuple-element.52), channel_id=1, source_target_pairs={{0,1},{1,0},{2,3},{3,2},{4,5},{5,4},{6,7},{7,6},{8,9},{9,8},{10,11... | collective-permute-start | bytes 393224 | tf_op jit(solution)/shard_map/ppermute | solution.py:25
  58.9 1.0 %collective-permute-done.15.other_ref = bf16[4,128,128]{2,1,0:T(8,128)(2,1)S(1)} collective-permute-done((bf16[4,128,128]{2,1,0:T(8,128)(2,1)S(1)}, bf16[4,128,128]{2,1,0:T(8,128)(2,1)S(1)}, u32[]{:S(2)}, u32[]{:S(2)}) %collective-permute-start.15) | collective-permute-done | bytes 131104 | tf_op jit(solution)/shard_map/ppermute | solution.py:25
  59.9 1.4 %merge_dk.1 = bf16[128,8,128]{2,1,0:T(8,128)(2,1)} custom-call(s32[2]{0:T(128)S(1)} %pad_add_fusion.place_ref, bf16[4,128,128]{2,1,0:T(8,128)(2,1)S(1)} %get-tuple-element.51.own_ref, bf16[4,128,128]{2,1,0:T(8,128)(2,1)S(1)} %collective-permute-done.15.other_ref), custom_call_target="tpu_custom_call" | custom-call | tf_op jit(solution)/shard_map/merge_dk/pallas_call | solution.py:38
  (17 shorter events, 0.0 us)
Async XLA Ops:
  0.6 3.2 %copy-start.1 = (bf16[128,32,128]{2,1,0:T(8,128)(2,1)S(1)}, bf16[128,32,128]{2,1,0:T(8,128)(2,1)}, u32[]{:S(2)}) copy-start(bf16[128,32,128]{2,1,0:T(8,128)(2,1)} %do_ref) | copy-start | bytes 3145732
  0.6 3.1 %copy-start = (bf16[128,32,128]{2,1,0:T(8,128)(2,1)S(1)}, bf16[128,32,128]{2,1,0:T(8,128)(2,1)}, u32[]{:S(2)}) copy-start(bf16[128,32,128]{2,1,0:T(8,128)(2,1)} %q_ref) | copy-start | bytes 3145732
  0.6 2.4 %collective-permute-start = (bf16[128,8,128]{2,1,0:T(8,128)(2,1)}, bf16[128,8,128]{2,1,0:T(8,128)(2,1)S(1)}, u32[]{:S(2)}, u32[]{:S(2)}) collective-permute-start(bf16[128,8,128]{2,1,0:T(8,128)(2,1)} %key_ref.1), channel_id=1, source_target_pairs={{0,1},{1,0},{2,3},{3,2},{4,5},{5,4},{6,7},{7,6},{8,9},{9,8},{10,11... | collective-permute-start | bytes 786440 | tf_op jit(solution)/shard_map/ppermute | solution.py:25
  3.7 14.8 %copy-start.2 = (s32[16]{0:T(128)S(1)}, s32[16]{0:T(128)}, u32[]{:S(2)}) copy-start(s32[16]{0:T(128)} %lengths_ref.1) | copy-start | bytes 196
  3.7 6.9 %collective-permute-start.1 = (bf16[128,32,128]{2,1,0:T(8,128)(2,1)S(1)}, bf16[128,32,128]{2,1,0:T(8,128)(2,1)S(1)}, u32[]{:S(2)}, u32[]{:S(2)}) collective-permute-start(bf16[128,32,128]{2,1,0:T(8,128)(2,1)S(1)} %copy-done), channel_id=1, source_target_pairs={{0,1},{1,0},{2,3},{3,2},{4,5},{5,4},{6,7},{7,6},{8,9},{9,8},{10,11... | collective-permute-start | bytes 3145736 | tf_op jit(solution)/shard_map/ppermute | solution.py:25
  3.9 6.8 %collective-permute-start.2 = (bf16[128,32,128]{2,1,0:T(8,128)(2,1)S(1)}, bf16[128,32,128]{2,1,0:T(8,128)(2,1)S(1)}, u32[]{:S(2)}, u32[]{:S(2)}) collective-permute-start(bf16[128,32,128]{2,1,0:T(8,128)(2,1)S(1)} %copy-done.1), channel_id=1, source_target_pairs={{0,1},{1,0},{2,3},{3,2},{4,5},{5,4},{6,7},{7,6},{8,9},{9,8},{10,11... | collective-permute-start | bytes 3145736 | tf_op jit(solution)/shard_map/ppermute | solution.py:25
  4.3 8.4 %collective-permute-start.3 = (bf16[128,8,128]{2,1,0:T(8,128)(2,1)S(1)}, bf16[128,8,128]{2,1,0:T(8,128)(2,1)S(1)}, u32[]{:S(2)}, u32[]{:S(2)}) collective-permute-start(bf16[128,8,128]{2,1,0:T(8,128)(2,1)S(1)} %get-tuple-element.36.own_ref), channel_id=1, source_target_pairs={{0,1},{1,0},{2,3},{3,2},{4,5},{5,4},{6,7},{7,6},{8,9},{9,8},{10,11... | collective-permute-start | bytes 786440 | tf_op jit(solution)/shard_map/ppermute | solution.py:25
  4.4 14.1 %collective-permute-start.5 = (bf16[4,2,128,128]{3,2,1,0:T(8,128)(2,1)S(1)}, bf16[4,2,128,128]{3,2,1,0:T(8,128)(2,1)S(1)}, u32[]{:S(2)}, u32[]{:S(2)}) collective-permute-start(bf16[4,2,128,128]{3,2,1,0:T(8,128)(2,1)S(1)} %pack_other.1.refs_0_), channel_id=1, source_target_pairs={{0,4},{1,5},{2,6},{3,7},{4,8},{5,9},{6,10},{7,11},{8,12},{9,13},{1... | collective-permute-start | bytes 786440 | tf_op jit(solution)/shard_map/ppermute | solution.py:21
  7.5 11.0 %collective-permute-start.4 = (bf16[4,2,128,128]{3,2,1,0:T(8,128)(2,1)S(1)}, bf16[4,2,128,128]{3,2,1,0:T(8,128)(2,1)S(1)}, u32[]{:S(2)}, u32[]{:S(2)}) collective-permute-start(bf16[4,2,128,128]{3,2,1,0:T(8,128)(2,1)S(1)} %pack_other.1.refs_0_), channel_id=1, source_target_pairs={{0,2},{1,3},{2,4},{3,5},{4,6},{5,7},{6,8},{7,9},{8,10},{9,11},{10,... | collective-permute-start | bytes 786440 | tf_op jit(solution)/shard_map/ppermute | solution.py:21
  13.4 20.8 %collective-permute-start.7 = (bf16[4,2,128,128]{3,2,1,0:T(8,128)(2,1)S(1)}, bf16[4,2,128,128]{3,2,1,0:T(8,128)(2,1)S(1)}, u32[]{:S(2)}, u32[]{:S(2)}) collective-permute-start(bf16[4,2,128,128]{3,2,1,0:T(8,128)(2,1)S(1)} %pack_both.1.refs_0_), channel_id=1, source_target_pairs={{0,4},{1,5},{2,6},{3,7},{4,8},{5,9},{6,10},{7,11},{8,12},{9,13},{1... | collective-permute-start | bytes 786440 | tf_op jit(solution)/shard_map/ppermute | solution.py:21
  15.4 18.8 %collective-permute-start.6 = (bf16[4,2,128,128]{3,2,1,0:T(8,128)(2,1)S(1)}, bf16[4,2,128,128]{3,2,1,0:T(8,128)(2,1)S(1)}, u32[]{:S(2)}, u32[]{:S(2)}) collective-permute-start(bf16[4,2,128,128]{3,2,1,0:T(8,128)(2,1)S(1)} %pack_both.1.refs_0_), channel_id=1, source_target_pairs={{0,2},{1,3},{2,4},{3,5},{4,6},{5,7},{6,8},{7,9},{8,10},{9,11},{10,... | collective-permute-start | bytes 786440 | tf_op jit(solution)/shard_map/ppermute | solution.py:21
  25.6 18.9 %collective-permute-start.8 = (bf16[4,2,128,128]{3,2,1,0:T(8,128)(2,1)S(1)}, bf16[4,2,128,128]{3,2,1,0:T(8,128)(2,1)S(1)}, u32[]{:S(2)}, u32[]{:S(2)}) collective-permute-start(bf16[4,2,128,128]{3,2,1,0:T(8,128)(2,1)S(1)} %get-tuple-element.39), channel_id=1, source_target_pairs={{4,0},{5,1},{6,2},{7,3},{8,4},{9,5},{10,6},{11,7},{12,8},{13,9},{1... | collective-permute-start | bytes 786440 | tf_op jit(solution)/shard_map/ppermute | solution.py:21
  29.0 15.5 %collective-permute-start.9 = (bf16[4,2,128,128]{3,2,1,0:T(8,128)(2,1)S(1)}, bf16[4,2,128,128]{3,2,1,0:T(8,128)(2,1)S(1)}, u32[]{:S(2)}, u32[]{:S(2)}) collective-permute-start(bf16[4,2,128,128]{3,2,1,0:T(8,128)(2,1)S(1)} %get-tuple-element.40), channel_id=1, source_target_pairs={{2,0},{3,1},{4,2},{5,3},{6,4},{7,5},{8,6},{9,7},{10,8},{11,9},{12,... | collective-permute-start | bytes 786440 | tf_op jit(solution)/shard_map/ppermute | solution.py:21
  40.6 14.8 %collective-permute-start.13 = (bf16[4,2,128,128]{3,2,1,0:T(8,128)(2,1)S(1)}, bf16[4,2,128,128]{3,2,1,0:T(8,128)(2,1)S(1)}, u32[]{:S(2)}, u32[]{:S(2)}) collective-permute-start(bf16[4,2,128,128]{3,2,1,0:T(8,128)(2,1)S(1)} %get-tuple-element.48), channel_id=1, source_target_pairs={{4,0},{5,1},{6,2},{7,3},{8,4},{9,5},{10,6},{11,7},{12,8},{13,9},{1... | collective-permute-start | bytes 786440 | tf_op jit(solution)/shard_map/ppermute | solution.py:21
  42.6 12.9 %collective-permute-start.14 = (bf16[4,2,128,128]{3,2,1,0:T(8,128)(2,1)S(1)}, bf16[4,2,128,128]{3,2,1,0:T(8,128)(2,1)S(1)}, u32[]{:S(2)}, u32[]{:S(2)}) collective-permute-start(bf16[4,2,128,128]{3,2,1,0:T(8,128)(2,1)S(1)} %get-tuple-element.49), channel_id=1, source_target_pairs={{2,0},{3,1},{4,2},{5,3},{6,4},{7,5},{8,6},{9,7},{10,8},{11,9},{12,... | collective-permute-start | bytes 786440 | tf_op jit(solution)/shard_map/ppermute | solution.py:21
  47.9 5.3 %collective-permute-start.10 = (bf16[56,16,128]{2,1,0:T(8,128)(2,1)S(1)}, bf16[56,16,128]{2,1,0:T(8,128)(2,1)S(1)}, u32[]{:S(2)}, u32[]{:S(2)}) collective-permute-start(bf16[56,16,128]{2,1,0:T(8,128)(2,1)S(1)} %get-tuple-element.43), channel_id=1, source_target_pairs={{0,1},{1,0},{2,3},{3,2},{4,5},{5,4},{6,7},{7,6},{8,9},{9,8},{10,11... | collective-permute-start | bytes 688136 | tf_op jit(solution)/shard_map/ppermute | solution.py:25
  51.4 1.8 %collective-permute-start.11 = (bf16[56,16,128]{2,1,0:T(8,128)(2,1)S(1)}, bf16[56,16,128]{2,1,0:T(8,128)(2,1)S(1)}, u32[]{:S(2)}, u32[]{:S(2)}) collective-permute-start(bf16[56,16,128]{2,1,0:T(8,128)(2,1)S(1)} %get-tuple-element.44), channel_id=1, source_target_pairs={{0,1},{1,0},{2,3},{3,2},{4,5},{5,4},{6,7},{7,6},{8,9},{9,8},{10,11... | collective-permute-start | bytes 688136 | tf_op jit(solution)/shard_map/ppermute | solution.py:25
  51.5 1.7 %collective-permute-start.12 = (bf16[48,16,128]{2,1,0:T(8,128)(2,1)S(1)}, bf16[48,16,128]{2,1,0:T(8,128)(2,1)S(1)}, u32[]{:S(2)}, u32[]{:S(2)}) collective-permute-start(bf16[48,16,128]{2,1,0:T(8,128)(2,1)S(1)} %get-tuple-element.45), channel_id=1, source_target_pairs={{0,1},{1,0},{2,3},{3,2},{4,5},{5,4},{6,7},{7,6},{8,9},{9,8},{10,11... | collective-permute-start | bytes 589832 | tf_op jit(solution)/shard_map/ppermute | solution.py:25
  56.1 3.9 %collective-permute-start.15 = (bf16[4,128,128]{2,1,0:T(8,128)(2,1)S(1)}, bf16[4,128,128]{2,1,0:T(8,128)(2,1)S(1)}, u32[]{:S(2)}, u32[]{:S(2)}) collective-permute-start(bf16[4,128,128]{2,1,0:T(8,128)(2,1)S(1)} %get-tuple-element.52), channel_id=1, source_target_pairs={{0,1},{1,0},{2,3},{3,2},{4,5},{5,4},{6,7},{7,6},{8,9},{9,8},{10,11... | collective-permute-start | bytes 393224 | tf_op jit(solution)/shard_map/ppermute | solution.py:25

commit v14 on v13

--- a/solution.py
+++ b/solution.py
@@ -10,7 +10,7 @@
 AXES = ("ctx", "uly")
 MASKED = -1e30
 LOG2E = 1.4426950408889634
-HEADS_AT_ONCE = 1
+HEADS_AT_ONCE = 2
 BF16, F32 = jnp.bfloat16, jnp.float32
 NT = (((1,), (1,)), ((), ()))
 VMEM_BYTES = 16 * 2**20
@@ -216,11 +216,15 @@
     ref[0, e, -tokens:, lanes] = jnp.where(diagonal, tiles[0], 0.0).astype(BF16)
 
 
+def chunks_of(lanes, pair):
+    return [(e, at) for e in range(2) for at in range(0, lanes, pair)]
+
+
 def prob_kernel(halo, place_ref, lengths_ref, qd_ref, *refs):
     k_refs = refs[: halo + 1]
     p_ref = refs[halo + 1]
-    dv_refs = refs[halo + 2 : -3]
-    k_scr, acc, firsts = refs[-3:]
+    dv_refs = refs[halo + 2 : -4]
+    k_scr, acc, bias, s_scr = refs[-4:]
     _, _, _, group, tokens, dim = qd_ref.shape
     count = 2 * halo + 1
     pair = HEADS_AT_ONCE * tokens
@@ -230,33 +234,42 @@
     @pl.when(pl.program_id(0) == 0)
     def _():
         for e in range(2):
-            query_pos = lane[:1] + (2 * halo + e) * tokens
-            firsts[e] = first_allowed(lengths_ref, query_pos, place_ref[1])
+            query_pos = lane[:1, :tokens] + (2 * halo + e) * tokens
+            first = first_allowed(lengths_ref, query_pos, place_ref[1]) - row[:, :tokens]
+            last = (e + count - 1) * tokens
+            bound = jnp.where(diagonal[:, :tokens], last, e * tokens)
+            bias[e, 0] = jnp.where(first <= bound, 0.0, MASKED)
+            for j in range(1, count - 1):
+                bias[e, j] = jnp.where(first <= (e + j) * tokens, 0.0, MASKED)
 
     window_of(k_refs, k_scr)
-    for e in range(2):
-        first = firsts[e] - row
+    chunks = chunks_of(group * tokens, pair)
+
+    def scores(i):
+        e, at = chunks[i]
         k = k_scr[pl.ds(e, count)].reshape(count * tokens, dim)
-        q = qd_ref[0, e, 0].reshape(group * tokens, dim)
-        do = qd_ref[0, e, 1].reshape(group * tokens, dim)
-        for at in range(0, group * tokens, pair):
-            s = lax.dot_general(k, q[at : at + pair], NT, preferred_element_type=F32)
-            tiles = [s[j * tokens : (j + 1) * tokens] for j in range(count)]
-            last = (e + count - 1) * tokens
-            bound = jnp.where(diagonal, last, e * tokens)
-            tiles[0] = jnp.where(first <= bound, jnp.where(diagonal, tiles.pop(), tiles[0]), MASKED)
-            for j in range(1, count - 1):
-                tiles[j] = jnp.where(first <= (e + j) * tokens, tiles[j], MASKED)
-            top = folded(jnp.maximum, functools.reduce(jnp.maximum, tiles))
-            tiles = [jnp.exp2((tile - top) * (dim**-0.5 * LOG2E)) for tile in tiles]
-            inv = 1.0 / folded(jnp.add, functools.reduce(jnp.add, tiles))
-            store_tiles(p_ref, e, at, [tile * inv for tile in tiles], diagonal)
-        keep = (2 * halo - e) * tokens
-        dv = jnp.dot(p_ref[0, e, :keep], do, preferred_element_type=F32).reshape(2 * halo - e, tokens, dim)
-        if e == 0:
-            acc[...] = dv
-        else:
-            acc[1:] += dv
+        q = qd_ref[0, e, 0].reshape(group * tokens, dim)[at : at + pair]
+        s_scr[i % 2] = lax.dot_general(k, q, NT, preferred_element_type=F32)
+
+    scores(0)
+    for i, (e, at) in enumerate(chunks):
+        if i + 1 < len(chunks):
+            scores(i + 1)
+        tiles = [s_scr[i % 2, j * tokens : (j + 1) * tokens] for j in range(count)]
+        tiles[0] = jnp.where(diagonal, tiles.pop(), tiles[0])
+        tiles = [t + jnp.concatenate([bias[e, j]] * HEADS_AT_ONCE, axis=1) for j, t in enumerate(tiles)]
+        top = folded(jnp.maximum, functools.reduce(jnp.maximum, tiles))
+        tiles = [jnp.exp2((tile - top) * (dim**-0.5 * LOG2E)) for tile in tiles]
+        inv = 1.0 / folded(jnp.add, functools.reduce(jnp.add, tiles))
+        store_tiles(p_ref, e, at, [tile * inv for tile in tiles], diagonal)
+        if at + pair == group * tokens:
+            do = qd_ref[0, e, 1].reshape(group * tokens, dim)
+            keep = (2 * halo - e) * tokens
+            dv = jnp.dot(p_ref[0, e, :keep], do, preferred_element_type=F32).reshape(2 * halo - e, tokens, dim)
+            if e == 0:
+                acc[...] = dv
+            else:
+                acc[1:] += dv
     for back, ref in zip(range(1, halo + 1), dv_refs):
         ref[0] = acc[pl.ds(2 * (halo - back), 2)].astype(BF16)
 
@@ -264,33 +277,41 @@
 def dscore_kernel(halo, place_ref, qd_ref, p_ref, *refs):
     v_refs = refs[: halo + 1]
     ds_ref = refs[halo + 1]
-    dk_refs = refs[halo + 2 : -2]
-    v_scr, acc = refs[-2:]
+    dk_refs = refs[halo + 2 : -3]
+    v_scr, acc, dp_scr = refs[-3:]
     _, _, _, group, tokens, dim = qd_ref.shape
     count = 2 * halo + 1
     pair = HEADS_AT_ONCE * tokens
-    window_of(v_refs, v_scr)
     row, lane = on_diagonal(tokens, HEADS_AT_ONCE)
     diagonal = row <= lane
-    for e in range(2):
+    window_of(v_refs, v_scr)
+    chunks = chunks_of(group * tokens, pair)
+
+    def dprobs(i):
+        e, at = chunks[i]
         v = v_scr[pl.ds(e, count)].reshape(count * tokens, dim)
-        q = qd_ref[0, e, 0].reshape(group * tokens, dim)
-        do = qd_ref[0, e, 1].reshape(group * tokens, dim)
-        for at in range(0, group * tokens, pair):
-            dp = lax.dot_general(v, do[at : at + pair], NT, preferred_element_type=F32)
-            dps = [dp[j * tokens : (j + 1) * tokens] for j in range(count)]
-            dps[0] = jnp.where(diagonal, dps.pop(), dps[0])
-            ps = [p_ref[0, e, j * tokens : (j + 1) * tokens, at : at + pair] for j in range(count)]
-            ps[0] += ps.pop()
-            ps = [p.astype(F32) for p in ps]
-            delta = folded(jnp.add, functools.reduce(jnp.add, [p * dp for p, dp in zip(ps, dps)]))
-            store_tiles(ds_ref, e, at, [p * (dp - delta) for p, dp in zip(ps, dps)], diagonal)
-        keep = (2 * halo - e) * tokens
-        dk = jnp.dot(ds_ref[0, e, :keep], q, preferred_element_type=F32).reshape(2 * halo - e, tokens, dim)
-        if e == 0:
-            acc[...] = dk
-        else:
-            acc[1:] += dk
+        do = qd_ref[0, e, 1].reshape(group * tokens, dim)[at : at + pair]
+        dp_scr[i % 2] = lax.dot_general(v, do, NT, preferred_element_type=F32)
+
+    dprobs(0)
+    for i, (e, at) in enumerate(chunks):
+        if i + 1 < len(chunks):
+            dprobs(i + 1)
+        dps = [dp_scr[i % 2, j * tokens : (j + 1) * tokens] for j in range(count)]
+        dps[0] = jnp.where(diagonal, dps.pop(), dps[0])
+        ps = [p_ref[0, e, j * tokens : (j + 1) * tokens, at : at + pair] for j in range(count)]
+        ps[0] += ps.pop()
+        ps = [p.astype(F32) for p in ps]
+        delta = folded(jnp.add, functools.reduce(jnp.add, [p * dp for p, dp in zip(ps, dps)]))
+        store_tiles(ds_ref, e, at, [p * (dp - delta) for p, dp in zip(ps, dps)], diagonal)
+        if at + pair == group * tokens:
+            q = qd_ref[0, e, 0].reshape(group * tokens, dim)
+            keep = (2 * halo - e) * tokens
+            dk = jnp.dot(ds_ref[0, e, :keep], q, preferred_element_type=F32).reshape(2 * halo - e, tokens, dim)
+            if e == 0:
+                acc[...] = dk
+            else:
+                acc[1:] += dk
     for back, ref in zip(range(1, halo + 1), dk_refs):
         ref[0] = (acc[pl.ds(2 * (halo - back), 2)] * dim**-0.5).astype(BF16)
 
@@ -488,6 +509,7 @@
     part_specs = [pl.BlockSpec(part.shape, lambda h, *_: (0, 0, 0)) for part in parts]
     run = pltpu.VMEM((window, tokens, dim), BF16)
     acc = pltpu.VMEM((2 * halo, tokens, dim), F32)
+    products = pltpu.VMEM((2, count * tokens, HEADS_AT_ONCE * tokens), F32)
     product = 2 * half * 2 * count * tokens * group * tokens * dim
 
     k_pairs = halo_of(k_own)
@@ -501,7 +523,7 @@
         [qd_spec] + [pair_spec] * (halo + 1),
         [p_shape] + [jax.ShapeDtypeStruct(pair, BF16)] * halo,
         [p_spec] + [pair_spec] * halo,
-        [run, acc, pltpu.VMEM((2, 1, HEADS_AT_ONCE * tokens), jnp.int32)],
+        [run, acc, pltpu.VMEM((2, count - 1, tokens, tokens), F32), products],
         4 * product,
     )
     dv_back = sent_back(dv_halo)
@@ -514,7 +536,7 @@
         [qd_spec, p_spec] + [pair_spec] * (halo + 1),
         [p_shape] + [jax.ShapeDtypeStruct(pair, BF16)] * halo,
         [p_spec] + [pair_spec] * halo,
-        [run, acc],
+        [run, acc, products],
         4 * product,
     )
     dk_back = sent_back(dk_halo)

time: 61.6 us -> 61.2 us (level)
    pallas_call x10, Pallas kernels: 26 us -> 25.4 us  [call(): pl.pallas_call(kernel, out_shape=outs, grid_spec=pltpu.PrefetchScalarGrid...]
  transfers between devices with their start and end apart: 16 -> 16, of which waited for: 2 -> 2; matrix products, arithmetic and copies ran while one was open for 0% -> 0% of each run, Pallas kernels for 38% -> 37%
where the time goes in v14:
time: 61.2 us; the launch traced here: 60.9 us
  starting transfers between devices  32.2 us (53%)
  Pallas kernels  25.4 us (42%)
  waiting for transfers between devices  2.28 us (4%)
  between operations  0.89 us (1%)
    pallas_call x10, Pallas kernels, call(): pl.pallas_call(kernel, out_shape=outs, grid_spec=pltpu.PrefetchScalarGrid...  25.4 us
    ppermute x8, starting transfers between devices, moved(): return lax.ppermute(array, AXES, pairs)  23.7 us
    ppermute x8, starting transfers between devices, swapped(): return lax.ppermute(array, AXES, [(d, d ^ 1) for d in range(device_count)])  8.5 us
    ppermute x8, waiting for transfers between devices, swapped(): return lax.ppermute(array, AXES, [(d, d ^ 1) for d in range(device_count)])  2.26 us
  transfers between devices with their start and end apart: 16, of which 2 were waited for; matrix products, arithmetic and copies ran while one was open for 0% of the time, Pallas kernels for 37%

profile of v14, /device:TPU:23, one launch (start us, length us, event | category | flops | bytes accessed | tf_op | source)
XLA Modules:
  0.0 60.9 jit_solution(16485158206151521645)
XLA Ops:
  0.6 0.7 %collective-permute-start = (bf16[128,8,128]{2,1,0:T(8,128)(2,1)}, bf16[128,8,128]{2,1,0:T(8,128)(2,1)S(1)}, u32[]{:S(2)}, u32[]{:S(2)}) collective-permute-start(bf16[128,8,128]{2,1,0:T(8,128)(2,1)} %key_ref.1), channel_id=1, source_target_pairs={{0,1},{1,0},{2,3},{3,2},{4,5},{5,4},{6,7},{7,6},{8,9},{9,8},{10,11... | collective-permute-start | bytes 786440 | tf_op jit(solution)/shard_map/ppermute | solution.py:25
  1.4 0.1 pad_add_fusion.place_ref
  1.5 1.6 %fetch.1 = (bf16[4,2,128,128]{3,2,1,0:T(8,128)(2,1)S(1)}, bf16[128,8,128]{2,1,0:T(8,128)(2,1)S(1)}) custom-call(s32[2]{0:T(128)S(1)} %pad_add_fusion.place_ref, bf16[128,8,128]{2,1,0:T(8,128)(2,1)} %key_ref.1, bf16[128,8,128]{2,1,0:T(8,128)(2,1)} %refs_0_.1), custom_call_target="tpu_custom_call" | custom-call | flops 1000000000 | tf_op jit(solution)/shard_map/fetch/pallas_call | solution.py:38
  3.1 0.6 %pack_other.1.refs_0_ = bf16[4,2,128,128]{3,2,1,0:T(8,128)(2,1)S(1)} custom-call(s32[2]{0:T(128)S(1)} %pad_add_fusion.place_ref, bf16[128,8,128]{2,1,0:T(8,128)(2,1)S(1)} %collective-permute-done.other_ref, bf16[4,2,128,128]{3,2,1,0:T(8,128)(2,1)S(1)} %get-tuple-element.28._), custom_call_target="tpu_custom_call", output_to_operand_aliasing={{}: (2, {})} | custom-call | flops 1000000000 | tf_op jit(solution)/shard_map/pack_other/pallas_call | solution.py:38
  3.7 0.0 copy-start.2
  3.7 0.1 collective-permute-start.1
  3.9 0.4 collective-permute-start.2
  4.3 0.1 collective-permute-start.3
  4.4 3.1 %collective-permute-start.5 = (bf16[4,2,128,128]{3,2,1,0:T(8,128)(2,1)S(1)}, bf16[4,2,128,128]{3,2,1,0:T(8,128)(2,1)S(1)}, u32[]{:S(2)}, u32[]{:S(2)}) collective-permute-start(bf16[4,2,128,128]{3,2,1,0:T(8,128)(2,1)S(1)} %pack_other.1.refs_0_), channel_id=1, source_target_pairs={{0,4},{1,5},{2,6},{3,7},{4,8},{5,9},{6,10},{7,11},{8,12},{9,13},{1... | collective-permute-start | bytes 786440 | tf_op jit(solution)/shard_map/ppermute | solution.py:21
  7.5 3.1 %collective-permute-start.4 = (bf16[4,2,128,128]{3,2,1,0:T(8,128)(2,1)S(1)}, bf16[4,2,128,128]{3,2,1,0:T(8,128)(2,1)S(1)}, u32[]{:S(2)}, u32[]{:S(2)}) collective-permute-start(bf16[4,2,128,128]{3,2,1,0:T(8,128)(2,1)S(1)} %pack_other.1.refs_0_), channel_id=1, source_target_pairs={{0,2},{1,3},{2,4},{3,5},{4,6},{5,7},{6,8},{7,9},{8,10},{9,11},{10,... | collective-permute-start | bytes 786440 | tf_op jit(solution)/shard_map/ppermute | solution.py:21
  10.7 2.0 %arrange.1.qd_ref = bf16[4,2,2,4,128,128]{5,4,3,2,1,0:T(8,128)(2,1)S(1)} custom-call(s32[2]{0:T(128)S(1)} %pad_add_fusion.place_ref, bf16[128,32,128]{2,1,0:T(8,128)(2,1)S(1)} %copy-done, bf16[128,32,128]{2,1,0:T(8,128)(2,1)S(1)} %copy-done.1, bf16[128,32,128]{2,1,0:T(8,128)(2,1)S(1)} %collective-permute-done.1.q_other_ref, ...), custom_call_target="tpu_custom_call" | custom-call | flops 1000000000 | tf_op jit(solution)/shard_map/arrange/pallas_call | solution.py:38
  12.7 0.7 %pack_both.1.refs_0_ = bf16[4,2,128,128]{3,2,1,0:T(8,128)(2,1)S(1)} custom-call(s32[2]{0:T(128)S(1)} %pad_add_fusion.place_ref, bf16[128,8,128]{2,1,0:T(8,128)(2,1)S(1)} %get-tuple-element.36.own_ref, bf16[128,8,128]{2,1,0:T(8,128)(2,1)S(1)} %collective-permute-done.3.other_ref), custom_call_target="tpu_custom_call" | custom-call | flops 1000000000 | tf_op jit(solution)/shard_map/pack_both/pallas_call | solution.py:38
  13.4 1.9 %collective-permute-start.7 = (bf16[4,2,128,128]{3,2,1,0:T(8,128)(2,1)S(1)}, bf16[4,2,128,128]{3,2,1,0:T(8,128)(2,1)S(1)}, u32[]{:S(2)}, u32[]{:S(2)}) collective-permute-start(bf16[4,2,128,128]{3,2,1,0:T(8,128)(2,1)S(1)} %pack_both.1.refs_0_), channel_id=1, source_target_pairs={{0,4},{1,5},{2,6},{3,7},{4,8},{5,9},{6,10},{7,11},{8,12},{9,13},{1... | collective-permute-start | bytes 786440 | tf_op jit(solution)/shard_map/ppermute | solution.py:21
  15.4 3.1 %collective-permute-start.6 = (bf16[4,2,128,128]{3,2,1,0:T(8,128)(2,1)S(1)}, bf16[4,2,128,128]{3,2,1,0:T(8,128)(2,1)S(1)}, u32[]{:S(2)}, u32[]{:S(2)}) collective-permute-start(bf16[4,2,128,128]{3,2,1,0:T(8,128)(2,1)S(1)} %pack_both.1.refs_0_), channel_id=1, source_target_pairs={{0,2},{1,3},{2,4},{3,5},{4,6},{5,7},{6,8},{7,9},{8,10},{9,11},{10,... | collective-permute-start | bytes 786440 | tf_op jit(solution)/shard_map/ppermute | solution.py:21
  18.5 0.0 collective-permute-done.5.refs_2_
  18.5 0.0 collective-permute-done.4.refs_1_
  18.5 6.6 %prob.1 = (bf16[4,2,640,512]{3,2,1,0:T(8,128)(2,1)S(1)}, bf16[4,2,128,128]{3,2,1,0:T(8,128)(2,1)S(1)}, bf16[4,2,128,128]{3,2,1,0:T(8,128)(2,1)S(1)}) custom-call(s32[2]{0:T(128)S(1)} %pad_add_fusion.place_ref, s32[16]{0:T(128)S(1)} %copy-done.2, bf16[4,2,2,4,128,128]{5,4,3,2,1,0:T(8,128)(2,1)S(1)} %arrange.1.qd_ref, ...), custom_call_target="tpu_custom_call" | custom-call | flops 2684354560 | tf_op jit(solution)/shard_map/prob/pallas_call | solution.py:38
  25.1 3.4 %collective-permute-start.8 = (bf16[4,2,128,128]{3,2,1,0:T(8,128)(2,1)S(1)}, bf16[4,2,128,128]{3,2,1,0:T(8,128)(2,1)S(1)}, u32[]{:S(2)}, u32[]{:S(2)}) collective-permute-start(bf16[4,2,128,128]{3,2,1,0:T(8,128)(2,1)S(1)} %get-tuple-element.39), channel_id=1, source_target_pairs={{4,0},{5,1},{6,2},{7,3},{8,4},{9,5},{10,6},{11,7},{12,8},{13,9},{1... | collective-permute-start | bytes 786440 | tf_op jit(solution)/shard_map/ppermute | solution.py:21
  28.5 5.2 %collective-permute-start.9 = (bf16[4,2,128,128]{3,2,1,0:T(8,128)(2,1)S(1)}, bf16[4,2,128,128]{3,2,1,0:T(8,128)(2,1)S(1)}, u32[]{:S(2)}, u32[]{:S(2)}) collective-permute-start(bf16[4,2,128,128]{3,2,1,0:T(8,128)(2,1)S(1)} %get-tuple-element.40), channel_id=1, source_target_pairs={{2,0},{3,1},{4,2},{5,3},{6,4},{7,5},{8,6},{9,7},{10,8},{11,9},{12,... | collective-permute-start | bytes 786440 | tf_op jit(solution)/shard_map/ppermute | solution.py:21
  33.8 6.2 %dscore.1 = (bf16[4,2,640,512]{3,2,1,0:T(8,128)(2,1)S(1)}, bf16[4,2,128,128]{3,2,1,0:T(8,128)(2,1)S(1)}, bf16[4,2,128,128]{3,2,1,0:T(8,128)(2,1)S(1)}) custom-call(s32[2]{0:T(128)S(1)} %pad_add_fusion.place_ref, bf16[4,2,2,4,128,128]{5,4,3,2,1,0:T(8,128)(2,1)S(1)} %arrange.1.qd_ref, bf16[4,2,640,512]{3,2,1,0:T(8,128)(2,1)S(1)} %get-tuple-element.35.p_ref, ...), custom_call_target="tpu_custom_call" | custom-call | flops 2684354560 | tf_op jit(solution)/shard_map/dscore/pallas_call | solution.py:38
  40.0 1.9 %collective-permute-start.13 = (bf16[4,2,128,128]{3,2,1,0:T(8,128)(2,1)S(1)}, bf16[4,2,128,128]{3,2,1,0:T(8,128)(2,1)S(1)}, u32[]{:S(2)}, u32[]{:S(2)}) collective-permute-start(bf16[4,2,128,128]{3,2,1,0:T(8,128)(2,1)S(1)} %get-tuple-element.48), channel_id=1, source_target_pairs={{4,0},{5,1},{6,2},{7,3},{8,4},{9,5},{10,6},{11,7},{12,8},{13,9},{1... | collective-permute-start | bytes 786440 | tf_op jit(solution)/shard_map/ppermute | solution.py:21
  41.9 1.9 %collective-permute-start.14 = (bf16[4,2,128,128]{3,2,1,0:T(8,128)(2,1)S(1)}, bf16[4,2,128,128]{3,2,1,0:T(8,128)(2,1)S(1)}, u32[]{:S(2)}, u32[]{:S(2)}) collective-permute-start(bf16[4,2,128,128]{3,2,1,0:T(8,128)(2,1)S(1)} %get-tuple-element.49), channel_id=1, source_target_pairs={{2,0},{3,1},{4,2},{5,3},{6,4},{7,5},{8,6},{9,7},{10,8},{11,9},{12,... | collective-permute-start | bytes 786440 | tf_op jit(solution)/shard_map/ppermute | solution.py:21
  43.9 3.4 %own.1 = (bf16[128,16,128]{2,1,0:T(8,128)(2,1)S(1)}, bf16[56,16,128]{2,1,0:T(8,128)(2,1)S(1)}, bf16[56,16,128]{2,1,0:T(8,128)(2,1)S(1)}, bf16[48,16,128]{2,1,0:T...) custom-call(s32[2]{0:T(128)S(1)} %pad_add_fusion.place_ref, ...), custom_call_target="tpu_custom_call" | custom-call | tf_op jit(solution)/shard_map/own/pallas_call | solution.py:38
  47.2 4.0 %collective-permute-start.10 = (bf16[56,16,128]{2,1,0:T(8,128)(2,1)S(1)}, bf16[56,16,128]{2,1,0:T(8,128)(2,1)S(1)}, u32[]{:S(2)}, u32[]{:S(2)}) collective-permute-start(bf16[56,16,128]{2,1,0:T(8,128)(2,1)S(1)} %get-tuple-element.43), channel_id=1, source_target_pairs={{0,1},{1,0},{2,3},{3,2},{4,5},{5,4},{6,7},{7,6},{8,9},{9,8},{10,11... | collective-permute-start | bytes 688136 | tf_op jit(solution)/shard_map/ppermute | solution.py:25
  51.2 0.1 collective-permute-start.11
  51.3 0.4 collective-permute-start.12
  51.7 1.3 %collective-permute-done.12.refs_2_ = bf16[48,16,128]{2,1,0:T(8,128)(2,1)S(1)} collective-permute-done((bf16[48,16,128]{2,1,0:T(8,128)(2,1)S(1)}, bf16[48,16,128]{2,1,0:T(8,128)(2,1)S(1)}, u32[]{:S(2)}, u32[]{:S(2)}) %collective-permute-start.12) | collective-permute-done | bytes 196640 | tf_op jit(solution)/shard_map/ppermute | solution.py:25
  53.0 2.2 %join.1 = (bf16[128,32,128]{2,1,0:T(8,128)(2,1)}, bf16[128,8,128]{2,1,0:T(8,128)(2,1)}) custom-call(s32[2]{0:T(128)S(1)} %pad_add_fusion.place_ref, bf16[128,16,128]{2,1,0:T(8,128)(2,1)S(1)} %get-tuple-element.41.dq_ref, bf16[4,128,128]{2,1,0:T(8,128)(2,1)S(1)} %get-tuple-element.42.dv_ref, bf16[56,16,128]{2,1,0:T(8,128)(2,1)S(1)} %collective-permute-done.10.refs_0_, ...), custom_call_target="tpu_custom_call" | custom-call | tf_op jit(solution)/shard_map/join/pallas_call | solution.py:38
  55.3 0.6 %sum_dk.1 = (bf16[4,128,128]{2,1,0:T(8,128)(2,1)S(1)}, bf16[4,128,128]{2,1,0:T(8,128)(2,1)S(1)}) custom-call(s32[2]{0:T(128)S(1)} %pad_add_fusion.place_ref, f32[4,2,128,128]{3,2,1,0:T(8,128)S(1)} %get-tuple-element.47.own_ref, bf16[4,2,128,128]{3,2,1,0:T(8,128)(2,1)S(1)} %collective-permute-done.13.refs_0_, ...), custom_call_target="tpu_custom_call" | custom-call | tf_op jit(solution)/shard_map/sum_dk/pallas_call | solution.py:38
  55.9 2.6 %collective-permute-start.15 = (bf16[4,128,128]{2,1,0:T(8,128)(2,1)S(1)}, bf16[4,128,128]{2,1,0:T(8,128)(2,1)S(1)}, u32[]{:S(2)}, u32[]{:S(2)}) collective-permute-start(bf16[4,128,128]{2,1,0:T(8,128)(2,1)S(1)} %get-tuple-element.52), channel_id=1, source_target_pairs={{0,1},{1,0},{2,3},{3,2},{4,5},{5,4},{6,7},{7,6},{8,9},{9,8},{10,11... | collective-permute-start | bytes 393224 | tf_op jit(solution)/shard_map/ppermute | solution.py:25
  58.5 1.0 %collective-permute-done.15.other_ref = bf16[4,128,128]{2,1,0:T(8,128)(2,1)S(1)} collective-permute-done((bf16[4,128,128]{2,1,0:T(8,128)(2,1)S(1)}, bf16[4,128,128]{2,1,0:T(8,128)(2,1)S(1)}, u32[]{:S(2)}, u32[]{:S(2)}) %collective-permute-start.15) | collective-permute-done | bytes 131104 | tf_op jit(solution)/shard_map/ppermute | solution.py:25
  59.5 1.4 %merge_dk.1 = bf16[128,8,128]{2,1,0:T(8,128)(2,1)} custom-call(s32[2]{0:T(128)S(1)} %pad_add_fusion.place_ref, bf16[4,128,128]{2,1,0:T(8,128)(2,1)S(1)} %get-tuple-element.51.own_ref, bf16[4,128,128]{2,1,0:T(8,128)(2,1)S(1)} %collective-permute-done.15.other_ref), custom_call_target="tpu_custom_call" | custom-call | tf_op jit(solution)/shard_map/merge_dk/pallas_call | solution.py:38
  (17 shorter events, 0.0 us)
Async XLA Ops:
  0.6 3.2 %copy-start.1 = (bf16[128,32,128]{2,1,0:T(8,128)(2,1)S(1)}, bf16[128,32,128]{2,1,0:T(8,128)(2,1)}, u32[]{:S(2)}) copy-start(bf16[128,32,128]{2,1,0:T(8,128)(2,1)} %do_ref) | copy-start | bytes 3145732
  0.6 3.1 %copy-start = (bf16[128,32,128]{2,1,0:T(8,128)(2,1)S(1)}, bf16[128,32,128]{2,1,0:T(8,128)(2,1)}, u32[]{:S(2)}) copy-start(bf16[128,32,128]{2,1,0:T(8,128)(2,1)} %q_ref) | copy-start | bytes 3145732
  0.6 2.4 %collective-permute-start = (bf16[128,8,128]{2,1,0:T(8,128)(2,1)}, bf16[128,8,128]{2,1,0:T(8,128)(2,1)S(1)}, u32[]{:S(2)}, u32[]{:S(2)}) collective-permute-start(bf16[128,8,128]{2,1,0:T(8,128)(2,1)} %key_ref.1), channel_id=1, source_target_pairs={{0,1},{1,0},{2,3},{3,2},{4,5},{5,4},{6,7},{7,6},{8,9},{9,8},{10,11... | collective-permute-start | bytes 786440 | tf_op jit(solution)/shard_map/ppermute | solution.py:25
  3.7 14.8 %copy-start.2 = (s32[16]{0:T(128)S(1)}, s32[16]{0:T(128)}, u32[]{:S(2)}) copy-start(s32[16]{0:T(128)} %lengths_ref.1) | copy-start | bytes 196
  3.7 6.9 %collective-permute-start.1 = (bf16[128,32,128]{2,1,0:T(8,128)(2,1)S(1)}, bf16[128,32,128]{2,1,0:T(8,128)(2,1)S(1)}, u32[]{:S(2)}, u32[]{:S(2)}) collective-permute-start(bf16[128,32,128]{2,1,0:T(8,128)(2,1)S(1)} %copy-done), channel_id=1, source_target_pairs={{0,1},{1,0},{2,3},{3,2},{4,5},{5,4},{6,7},{7,6},{8,9},{9,8},{10,11... | collective-permute-start | bytes 3145736 | tf_op jit(solution)/shard_map/ppermute | solution.py:25
  3.9 6.8 %collective-permute-start.2 = (bf16[128,32,128]{2,1,0:T(8,128)(2,1)S(1)}, bf16[128,32,128]{2,1,0:T(8,128)(2,1)S(1)}, u32[]{:S(2)}, u32[]{:S(2)}) collective-permute-start(bf16[128,32,128]{2,1,0:T(8,128)(2,1)S(1)} %copy-done.1), channel_id=1, source_target_pairs={{0,1},{1,0},{2,3},{3,2},{4,5},{5,4},{6,7},{7,6},{8,9},{9,8},{10,11... | collective-permute-start | bytes 3145736 | tf_op jit(solution)/shard_map/ppermute | solution.py:25
  4.3 8.4 %collective-permute-start.3 = (bf16[128,8,128]{2,1,0:T(8,128)(2,1)S(1)}, bf16[128,8,128]{2,1,0:T(8,128)(2,1)S(1)}, u32[]{:S(2)}, u32[]{:S(2)}) collective-permute-start(bf16[128,8,128]{2,1,0:T(8,128)(2,1)S(1)} %get-tuple-element.36.own_ref), channel_id=1, source_target_pairs={{0,1},{1,0},{2,3},{3,2},{4,5},{5,4},{6,7},{7,6},{8,9},{9,8},{10,11... | collective-permute-start | bytes 786440 | tf_op jit(solution)/shard_map/ppermute | solution.py:25
  4.4 14.1 %collective-permute-start.5 = (bf16[4,2,128,128]{3,2,1,0:T(8,128)(2,1)S(1)}, bf16[4,2,128,128]{3,2,1,0:T(8,128)(2,1)S(1)}, u32[]{:S(2)}, u32[]{:S(2)}) collective-permute-start(bf16[4,2,128,128]{3,2,1,0:T(8,128)(2,1)S(1)} %pack_other.1.refs_0_), channel_id=1, source_target_pairs={{0,4},{1,5},{2,6},{3,7},{4,8},{5,9},{6,10},{7,11},{8,12},{9,13},{1... | collective-permute-start | bytes 786440 | tf_op jit(solution)/shard_map/ppermute | solution.py:21
  7.5 11.0 %collective-permute-start.4 = (bf16[4,2,128,128]{3,2,1,0:T(8,128)(2,1)S(1)}, bf16[4,2,128,128]{3,2,1,0:T(8,128)(2,1)S(1)}, u32[]{:S(2)}, u32[]{:S(2)}) collective-permute-start(bf16[4,2,128,128]{3,2,1,0:T(8,128)(2,1)S(1)} %pack_other.1.refs_0_), channel_id=1, source_target_pairs={{0,2},{1,3},{2,4},{3,5},{4,6},{5,7},{6,8},{7,9},{8,10},{9,11},{10,... | collective-permute-start | bytes 786440 | tf_op jit(solution)/shard_map/ppermute | solution.py:21
  13.4 20.3 %collective-permute-start.7 = (bf16[4,2,128,128]{3,2,1,0:T(8,128)(2,1)S(1)}, bf16[4,2,128,128]{3,2,1,0:T(8,128)(2,1)S(1)}, u32[]{:S(2)}, u32[]{:S(2)}) collective-permute-start(bf16[4,2,128,128]{3,2,1,0:T(8,128)(2,1)S(1)} %pack_both.1.refs_0_), channel_id=1, source_target_pairs={{0,4},{1,5},{2,6},{3,7},{4,8},{5,9},{6,10},{7,11},{8,12},{9,13},{1... | collective-permute-start | bytes 786440 | tf_op jit(solution)/shard_map/ppermute | solution.py:21
  15.4 18.4 %collective-permute-start.6 = (bf16[4,2,128,128]{3,2,1,0:T(8,128)(2,1)S(1)}, bf16[4,2,128,128]{3,2,1,0:T(8,128)(2,1)S(1)}, u32[]{:S(2)}, u32[]{:S(2)}) collective-permute-start(bf16[4,2,128,128]{3,2,1,0:T(8,128)(2,1)S(1)} %pack_both.1.refs_0_), channel_id=1, source_target_pairs={{0,2},{1,3},{2,4},{3,5},{4,6},{5,7},{6,8},{7,9},{8,10},{9,11},{10,... | collective-permute-start | bytes 786440 | tf_op jit(solution)/shard_map/ppermute | solution.py:21
  25.1 18.7 %collective-permute-start.8 = (bf16[4,2,128,128]{3,2,1,0:T(8,128)(2,1)S(1)}, bf16[4,2,128,128]{3,2,1,0:T(8,128)(2,1)S(1)}, u32[]{:S(2)}, u32[]{:S(2)}) collective-permute-start(bf16[4,2,128,128]{3,2,1,0:T(8,128)(2,1)S(1)} %get-tuple-element.39), channel_id=1, source_target_pairs={{4,0},{5,1},{6,2},{7,3},{8,4},{9,5},{10,6},{11,7},{12,8},{13,9},{1... | collective-permute-start | bytes 786440 | tf_op jit(solution)/shard_map/ppermute | solution.py:21
  28.5 15.4 %collective-permute-start.9 = (bf16[4,2,128,128]{3,2,1,0:T(8,128)(2,1)S(1)}, bf16[4,2,128,128]{3,2,1,0:T(8,128)(2,1)S(1)}, u32[]{:S(2)}, u32[]{:S(2)}) collective-permute-start(bf16[4,2,128,128]{3,2,1,0:T(8,128)(2,1)S(1)} %get-tuple-element.40), channel_id=1, source_target_pairs={{2,0},{3,1},{4,2},{5,3},{6,4},{7,5},{8,6},{9,7},{10,8},{11,9},{12,... | collective-permute-start | bytes 786440 | tf_op jit(solution)/shard_map/ppermute | solution.py:21
  40.0 15.3 %collective-permute-start.13 = (bf16[4,2,128,128]{3,2,1,0:T(8,128)(2,1)S(1)}, bf16[4,2,128,128]{3,2,1,0:T(8,128)(2,1)S(1)}, u32[]{:S(2)}, u32[]{:S(2)}) collective-permute-start(bf16[4,2,128,128]{3,2,1,0:T(8,128)(2,1)S(1)} %get-tuple-element.48), channel_id=1, source_target_pairs={{4,0},{5,1},{6,2},{7,3},{8,4},{9,5},{10,6},{11,7},{12,8},{13,9},{1... | collective-permute-start | bytes 786440 | tf_op jit(solution)/shard_map/ppermute | solution.py:21
  41.9 13.3 %collective-permute-start.14 = (bf16[4,2,128,128]{3,2,1,0:T(8,128)(2,1)S(1)}, bf16[4,2,128,128]{3,2,1,0:T(8,128)(2,1)S(1)}, u32[]{:S(2)}, u32[]{:S(2)}) collective-permute-start(bf16[4,2,128,128]{3,2,1,0:T(8,128)(2,1)S(1)} %get-tuple-element.49), channel_id=1, source_target_pairs={{2,0},{3,1},{4,2},{5,3},{6,4},{7,5},{8,6},{9,7},{10,8},{11,9},{12,... | collective-permute-start | bytes 786440 | tf_op jit(solution)/shard_map/ppermute | solution.py:21
  47.2 5.8 %collective-permute-start.10 = (bf16[56,16,128]{2,1,0:T(8,128)(2,1)S(1)}, bf16[56,16,128]{2,1,0:T(8,128)(2,1)S(1)}, u32[]{:S(2)}, u32[]{:S(2)}) collective-permute-start(bf16[56,16,128]{2,1,0:T(8,128)(2,1)S(1)} %get-tuple-element.43), channel_id=1, source_target_pairs={{0,1},{1,0},{2,3},{3,2},{4,5},{5,4},{6,7},{7,6},{8,9},{9,8},{10,11... | collective-permute-start | bytes 688136 | tf_op jit(solution)/shard_map/ppermute | solution.py:25
  51.2 1.8 %collective-permute-start.11 = (bf16[56,16,128]{2,1,0:T(8,128)(2,1)S(1)}, bf16[56,16,128]{2,1,0:T(8,128)(2,1)S(1)}, u32[]{:S(2)}, u32[]{:S(2)}) collective-permute-start(bf16[56,16,128]{2,1,0:T(8,128)(2,1)S(1)} %get-tuple-element.44), channel_id=1, source_target_pairs={{0,1},{1,0},{2,3},{3,2},{4,5},{5,4},{6,7},{7,6},{8,9},{9,8},{10,11... | collective-permute-start | bytes 688136 | tf_op jit(solution)/shard_map/ppermute | solution.py:25
  51.3 1.7 %collective-permute-start.12 = (bf16[48,16,128]{2,1,0:T(8,128)(2,1)S(1)}, bf16[48,16,128]{2,1,0:T(8,128)(2,1)S(1)}, u32[]{:S(2)}, u32[]{:S(2)}) collective-permute-start(bf16[48,16,128]{2,1,0:T(8,128)(2,1)S(1)} %get-tuple-element.45), channel_id=1, source_target_pairs={{0,1},{1,0},{2,3},{3,2},{4,5},{5,4},{6,7},{7,6},{8,9},{9,8},{10,11... | collective-permute-start | bytes 589832 | tf_op jit(solution)/shard_map/ppermute | solution.py:25
  55.9 3.6 %collective-permute-start.15 = (bf16[4,128,128]{2,1,0:T(8,128)(2,1)S(1)}, bf16[4,128,128]{2,1,0:T(8,128)(2,1)S(1)}, u32[]{:S(2)}, u32[]{:S(2)}) collective-permute-start(bf16[4,128,128]{2,1,0:T(8,128)(2,1)S(1)} %get-tuple-element.52), channel_id=1, source_target_pairs={{0,1},{1,0},{2,3},{3,2},{4,5},{5,4},{6,7},{7,6},{8,9},{9,8},{10,11... | collective-permute-start | bytes 393224 | tf_op jit(solution)/shard_map/ppermute | solution.py:25

commit v15 on v13

--- a/solution.py
+++ b/solution.py
@@ -10,7 +10,7 @@
 AXES = ("ctx", "uly")
 MASKED = -1e30
 LOG2E = 1.4426950408889634
-HEADS_AT_ONCE = 1
+HEADS_AT_ONCE = 2
 BF16, F32 = jnp.bfloat16, jnp.float32
 NT = (((1,), (1,)), ((), ()))
 VMEM_BYTES = 16 * 2**20

time: 61.6 us -> 61.1 us (level)
  Pallas kernels: 26 us -> 25.1 us
    pallas_call x10, Pallas kernels: 26 us -> 25.1 us  [call(): pl.pallas_call(kernel, out_shape=outs, grid_spec=pltpu.PrefetchScalarGrid...]
  transfers between devices with their start and end apart: 16 -> 16, of which waited for: 2 -> 2; matrix products, arithmetic and copies ran while one was open for 0% -> 0% of each run, Pallas kernels for 38% -> 37%
where the time goes in v15:
time: 61.1 us; the launch traced here: 60.8 us
  starting transfers between devices  32.4 us (53%)
  Pallas kernels  25.1 us (41%)
  waiting for transfers between devices  2.28 us (4%)
  between operations  0.89 us (1%)
    pallas_call x10, Pallas kernels, call(): pl.pallas_call(kernel, out_shape=outs, grid_spec=pltpu.PrefetchScalarGrid...  25.1 us
    ppermute x8, starting transfers between devices, moved(): return lax.ppermute(array, AXES, pairs)  23.8 us
    ppermute x8, starting transfers between devices, swapped(): return lax.ppermute(array, AXES, [(d, d ^ 1) for d in range(device_count)])  8.69 us
    ppermute x8, waiting for transfers between devices, swapped(): return lax.ppermute(array, AXES, [(d, d ^ 1) for d in range(device_count)])  2.26 us
  transfers between devices with their start and end apart: 16, of which 2 were waited for; matrix products, arithmetic and copies ran while one was open for 0% of the time, Pallas kernels for 37%

profile of v15, /device:TPU:23, one launch (start us, length us, event | category | flops | bytes accessed | tf_op | source)
XLA Modules:
  0.0 60.8 jit_solution(6204198571660981773)
XLA Ops:
  0.6 0.7 %collective-permute-start = (bf16[128,8,128]{2,1,0:T(8,128)(2,1)}, bf16[128,8,128]{2,1,0:T(8,128)(2,1)S(1)}, u32[]{:S(2)}, u32[]{:S(2)}) collective-permute-start(bf16[128,8,128]{2,1,0:T(8,128)(2,1)} %key_ref.1), channel_id=1, source_target_pairs={{0,1},{1,0},{2,3},{3,2},{4,5},{5,4},{6,7},{7,6},{8,9},{9,8},{10,11... | collective-permute-start | bytes 786440 | tf_op jit(solution)/shard_map/ppermute | solution.py:25
  1.4 0.1 pad_add_fusion.place_ref
  1.5 1.6 %fetch.1 = (bf16[4,2,128,128]{3,2,1,0:T(8,128)(2,1)S(1)}, bf16[128,8,128]{2,1,0:T(8,128)(2,1)S(1)}) custom-call(s32[2]{0:T(128)S(1)} %pad_add_fusion.place_ref, bf16[128,8,128]{2,1,0:T(8,128)(2,1)} %key_ref.1, bf16[128,8,128]{2,1,0:T(8,128)(2,1)} %refs_0_.1), custom_call_target="tpu_custom_call" | custom-call | flops 1000000000 | tf_op jit(solution)/shard_map/fetch/pallas_call | solution.py:38
  3.1 0.6 %pack_other.1.refs_0_ = bf16[4,2,128,128]{3,2,1,0:T(8,128)(2,1)S(1)} custom-call(s32[2]{0:T(128)S(1)} %pad_add_fusion.place_ref, bf16[128,8,128]{2,1,0:T(8,128)(2,1)S(1)} %collective-permute-done.other_ref, bf16[4,2,128,128]{3,2,1,0:T(8,128)(2,1)S(1)} %get-tuple-element.28._), custom_call_target="tpu_custom_call", output_to_operand_aliasing={{}: (2, {})} | custom-call | flops 1000000000 | tf_op jit(solution)/shard_map/pack_other/pallas_call | solution.py:38
  3.7 0.0 copy-start.2
  3.7 0.1 collective-permute-start.1
  3.9 0.4 collective-permute-start.2
  4.3 0.1 collective-permute-start.3
  4.4 3.1 %collective-permute-start.5 = (bf16[4,2,128,128]{3,2,1,0:T(8,128)(2,1)S(1)}, bf16[4,2,128,128]{3,2,1,0:T(8,128)(2,1)S(1)}, u32[]{:S(2)}, u32[]{:S(2)}) collective-permute-start(bf16[4,2,128,128]{3,2,1,0:T(8,128)(2,1)S(1)} %pack_other.1.refs_0_), channel_id=1, source_target_pairs={{0,4},{1,5},{2,6},{3,7},{4,8},{5,9},{6,10},{7,11},{8,12},{9,13},{1... | collective-permute-start | bytes 786440 | tf_op jit(solution)/shard_map/ppermute | solution.py:21
  7.5 3.1 %collective-permute-start.4 = (bf16[4,2,128,128]{3,2,1,0:T(8,128)(2,1)S(1)}, bf16[4,2,128,128]{3,2,1,0:T(8,128)(2,1)S(1)}, u32[]{:S(2)}, u32[]{:S(2)}) collective-permute-start(bf16[4,2,128,128]{3,2,1,0:T(8,128)(2,1)S(1)} %pack_other.1.refs_0_), channel_id=1, source_target_pairs={{0,2},{1,3},{2,4},{3,5},{4,6},{5,7},{6,8},{7,9},{8,10},{9,11},{10,... | collective-permute-start | bytes 786440 | tf_op jit(solution)/shard_map/ppermute | solution.py:21
  10.7 2.0 %arrange.1.qd_ref = bf16[4,2,2,4,128,128]{5,4,3,2,1,0:T(8,128)(2,1)S(1)} custom-call(s32[2]{0:T(128)S(1)} %pad_add_fusion.place_ref, bf16[128,32,128]{2,1,0:T(8,128)(2,1)S(1)} %copy-done, bf16[128,32,128]{2,1,0:T(8,128)(2,1)S(1)} %copy-done.1, bf16[128,32,128]{2,1,0:T(8,128)(2,1)S(1)} %collective-permute-done.1.q_other_ref, ...), custom_call_target="tpu_custom_call" | custom-call | flops 1000000000 | tf_op jit(solution)/shard_map/arrange/pallas_call | solution.py:38
  12.7 0.7 %pack_both.1.refs_0_ = bf16[4,2,128,128]{3,2,1,0:T(8,128)(2,1)S(1)} custom-call(s32[2]{0:T(128)S(1)} %pad_add_fusion.place_ref, bf16[128,8,128]{2,1,0:T(8,128)(2,1)S(1)} %get-tuple-element.36.own_ref, bf16[128,8,128]{2,1,0:T(8,128)(2,1)S(1)} %collective-permute-done.3.other_ref), custom_call_target="tpu_custom_call" | custom-call | flops 1000000000 | tf_op jit(solution)/shard_map/pack_both/pallas_call | solution.py:38
  13.4 1.9 %collective-permute-start.7 = (bf16[4,2,128,128]{3,2,1,0:T(8,128)(2,1)S(1)}, bf16[4,2,128,128]{3,2,1,0:T(8,128)(2,1)S(1)}, u32[]{:S(2)}, u32[]{:S(2)}) collective-permute-start(bf16[4,2,128,128]{3,2,1,0:T(8,128)(2,1)S(1)} %pack_both.1.refs_0_), channel_id=1, source_target_pairs={{0,4},{1,5},{2,6},{3,7},{4,8},{5,9},{6,10},{7,11},{8,12},{9,13},{1... | collective-permute-start | bytes 786440 | tf_op jit(solution)/shard_map/ppermute | solution.py:21
  15.4 3.1 %collective-permute-start.6 = (bf16[4,2,128,128]{3,2,1,0:T(8,128)(2,1)S(1)}, bf16[4,2,128,128]{3,2,1,0:T(8,128)(2,1)S(1)}, u32[]{:S(2)}, u32[]{:S(2)}) collective-permute-start(bf16[4,2,128,128]{3,2,1,0:T(8,128)(2,1)S(1)} %pack_both.1.refs_0_), channel_id=1, source_target_pairs={{0,2},{1,3},{2,4},{3,5},{4,6},{5,7},{6,8},{7,9},{8,10},{9,11},{10,... | collective-permute-start | bytes 786440 | tf_op jit(solution)/shard_map/ppermute | solution.py:21
  18.5 0.0 collective-permute-done.5.refs_2_
  18.5 0.0 collective-permute-done.4.refs_1_
  18.5 6.5 %prob.1 = (bf16[4,2,640,512]{3,2,1,0:T(8,128)(2,1)S(1)}, bf16[4,2,128,128]{3,2,1,0:T(8,128)(2,1)S(1)}, bf16[4,2,128,128]{3,2,1,0:T(8,128)(2,1)S(1)}) custom-call(s32[2]{0:T(128)S(1)} %pad_add_fusion.place_ref, s32[16]{0:T(128)S(1)} %copy-done.2, bf16[4,2,2,4,128,128]{5,4,3,2,1,0:T(8,128)(2,1)S(1)} %arrange.1.qd_ref, ...), custom_call_target="tpu_custom_call" | custom-call | flops 2684354560 | tf_op jit(solution)/shard_map/prob/pallas_call | solution.py:38
  25.0 3.4 %collective-permute-start.8 = (bf16[4,2,128,128]{3,2,1,0:T(8,128)(2,1)S(1)}, bf16[4,2,128,128]{3,2,1,0:T(8,128)(2,1)S(1)}, u32[]{:S(2)}, u32[]{:S(2)}) collective-permute-start(bf16[4,2,128,128]{3,2,1,0:T(8,128)(2,1)S(1)} %get-tuple-element.39), channel_id=1, source_target_pairs={{4,0},{5,1},{6,2},{7,3},{8,4},{9,5},{10,6},{11,7},{12,8},{13,9},{1... | collective-permute-start | bytes 786440 | tf_op jit(solution)/shard_map/ppermute | solution.py:21
  28.4 5.2 %collective-permute-start.9 = (bf16[4,2,128,128]{3,2,1,0:T(8,128)(2,1)S(1)}, bf16[4,2,128,128]{3,2,1,0:T(8,128)(2,1)S(1)}, u32[]{:S(2)}, u32[]{:S(2)}) collective-permute-start(bf16[4,2,128,128]{3,2,1,0:T(8,128)(2,1)S(1)} %get-tuple-element.40), channel_id=1, source_target_pairs={{2,0},{3,1},{4,2},{5,3},{6,4},{7,5},{8,6},{9,7},{10,8},{11,9},{12,... | collective-permute-start | bytes 786440 | tf_op jit(solution)/shard_map/ppermute | solution.py:21
  33.7 6.0 %dscore.1 = (bf16[4,2,640,512]{3,2,1,0:T(8,128)(2,1)S(1)}, bf16[4,2,128,128]{3,2,1,0:T(8,128)(2,1)S(1)}, bf16[4,2,128,128]{3,2,1,0:T(8,128)(2,1)S(1)}) custom-call(s32[2]{0:T(128)S(1)} %pad_add_fusion.place_ref, bf16[4,2,2,4,128,128]{5,4,3,2,1,0:T(8,128)(2,1)S(1)} %arrange.1.qd_ref, bf16[4,2,640,512]{3,2,1,0:T(8,128)(2,1)S(1)} %get-tuple-element.35.p_ref, ...), custom_call_target="tpu_custom_call" | custom-call | flops 2684354560 | tf_op jit(solution)/shard_map/dscore/pallas_call | solution.py:38
  39.7 1.9 %collective-permute-start.13 = (bf16[4,2,128,128]{3,2,1,0:T(8,128)(2,1)S(1)}, bf16[4,2,128,128]{3,2,1,0:T(8,128)(2,1)S(1)}, u32[]{:S(2)}, u32[]{:S(2)}) collective-permute-start(bf16[4,2,128,128]{3,2,1,0:T(8,128)(2,1)S(1)} %get-tuple-element.48), channel_id=1, source_target_pairs={{4,0},{5,1},{6,2},{7,3},{8,4},{9,5},{10,6},{11,7},{12,8},{13,9},{1... | collective-permute-start | bytes 786440 | tf_op jit(solution)/shard_map/ppermute | solution.py:21
  41.6 1.9 %collective-permute-start.14 = (bf16[4,2,128,128]{3,2,1,0:T(8,128)(2,1)S(1)}, bf16[4,2,128,128]{3,2,1,0:T(8,128)(2,1)S(1)}, u32[]{:S(2)}, u32[]{:S(2)}) collective-permute-start(bf16[4,2,128,128]{3,2,1,0:T(8,128)(2,1)S(1)} %get-tuple-element.49), channel_id=1, source_target_pairs={{2,0},{3,1},{4,2},{5,3},{6,4},{7,5},{8,6},{9,7},{10,8},{11,9},{12,... | collective-permute-start | bytes 786440 | tf_op jit(solution)/shard_map/ppermute | solution.py:21
  43.6 3.3 %own.1 = (bf16[128,16,128]{2,1,0:T(8,128)(2,1)S(1)}, bf16[56,16,128]{2,1,0:T(8,128)(2,1)S(1)}, bf16[56,16,128]{2,1,0:T(8,128)(2,1)S(1)}, bf16[48,16,128]{2,1,0:T...) custom-call(s32[2]{0:T(128)S(1)} %pad_add_fusion.place_ref, ...), custom_call_target="tpu_custom_call" | custom-call | tf_op jit(solution)/shard_map/own/pallas_call | solution.py:38
  46.9 4.5 %collective-permute-start.10 = (bf16[56,16,128]{2,1,0:T(8,128)(2,1)S(1)}, bf16[56,16,128]{2,1,0:T(8,128)(2,1)S(1)}, u32[]{:S(2)}, u32[]{:S(2)}) collective-permute-start(bf16[56,16,128]{2,1,0:T(8,128)(2,1)S(1)} %get-tuple-element.43), channel_id=1, source_target_pairs={{0,1},{1,0},{2,3},{3,2},{4,5},{5,4},{6,7},{7,6},{8,9},{9,8},{10,11... | collective-permute-start | bytes 688136 | tf_op jit(solution)/shard_map/ppermute | solution.py:25
  51.4 0.1 collective-permute-start.11
  51.5 0.4 collective-permute-start.12
  51.9 1.3 %collective-permute-done.12.refs_2_ = bf16[48,16,128]{2,1,0:T(8,128)(2,1)S(1)} collective-permute-done((bf16[48,16,128]{2,1,0:T(8,128)(2,1)S(1)}, bf16[48,16,128]{2,1,0:T(8,128)(2,1)S(1)}, u32[]{:S(2)}, u32[]{:S(2)}) %collective-permute-start.12) | collective-permute-done | bytes 196640 | tf_op jit(solution)/shard_map/ppermute | solution.py:25
  53.2 2.2 %join.1 = (bf16[128,32,128]{2,1,0:T(8,128)(2,1)}, bf16[128,8,128]{2,1,0:T(8,128)(2,1)}) custom-call(s32[2]{0:T(128)S(1)} %pad_add_fusion.place_ref, bf16[128,16,128]{2,1,0:T(8,128)(2,1)S(1)} %get-tuple-element.41.dq_ref, bf16[4,128,128]{2,1,0:T(8,128)(2,1)S(1)} %get-tuple-element.42.dv_ref, bf16[56,16,128]{2,1,0:T(8,128)(2,1)S(1)} %collective-permute-done.10.refs_0_, ...), custom_call_target="tpu_custom_call" | custom-call | tf_op jit(solution)/shard_map/join/pallas_call | solution.py:38
  55.4 0.6 %sum_dk.1 = (bf16[4,128,128]{2,1,0:T(8,128)(2,1)S(1)}, bf16[4,128,128]{2,1,0:T(8,128)(2,1)S(1)}) custom-call(s32[2]{0:T(128)S(1)} %pad_add_fusion.place_ref, f32[4,2,128,128]{3,2,1,0:T(8,128)S(1)} %get-tuple-element.47.own_ref, bf16[4,2,128,128]{3,2,1,0:T(8,128)(2,1)S(1)} %collective-permute-done.13.refs_0_, ...), custom_call_target="tpu_custom_call" | custom-call | tf_op jit(solution)/shard_map/sum_dk/pallas_call | solution.py:38
  56.1 2.3 %collective-permute-start.15 = (bf16[4,128,128]{2,1,0:T(8,128)(2,1)S(1)}, bf16[4,128,128]{2,1,0:T(8,128)(2,1)S(1)}, u32[]{:S(2)}, u32[]{:S(2)}) collective-permute-start(bf16[4,128,128]{2,1,0:T(8,128)(2,1)S(1)} %get-tuple-element.52), channel_id=1, source_target_pairs={{0,1},{1,0},{2,3},{3,2},{4,5},{5,4},{6,7},{7,6},{8,9},{9,8},{10,11... | collective-permute-start | bytes 393224 | tf_op jit(solution)/shard_map/ppermute | solution.py:25
  58.4 1.0 %collective-permute-done.15.other_ref = bf16[4,128,128]{2,1,0:T(8,128)(2,1)S(1)} collective-permute-done((bf16[4,128,128]{2,1,0:T(8,128)(2,1)S(1)}, bf16[4,128,128]{2,1,0:T(8,128)(2,1)S(1)}, u32[]{:S(2)}, u32[]{:S(2)}) %collective-permute-start.15) | collective-permute-done | bytes 131104 | tf_op jit(solution)/shard_map/ppermute | solution.py:25
  59.4 1.4 %merge_dk.1 = bf16[128,8,128]{2,1,0:T(8,128)(2,1)} custom-call(s32[2]{0:T(128)S(1)} %pad_add_fusion.place_ref, bf16[4,128,128]{2,1,0:T(8,128)(2,1)S(1)} %get-tuple-element.51.own_ref, bf16[4,128,128]{2,1,0:T(8,128)(2,1)S(1)} %collective-permute-done.15.other_ref), custom_call_target="tpu_custom_call" | custom-call | tf_op jit(solution)/shard_map/merge_dk/pallas_call | solution.py:38
  (17 shorter events, 0.0 us)
Async XLA Ops:
  0.6 3.2 %copy-start.1 = (bf16[128,32,128]{2,1,0:T(8,128)(2,1)S(1)}, bf16[128,32,128]{2,1,0:T(8,128)(2,1)}, u32[]{:S(2)}) copy-start(bf16[128,32,128]{2,1,0:T(8,128)(2,1)} %do_ref) | copy-start | bytes 3145732
  0.6 3.1 %copy-start = (bf16[128,32,128]{2,1,0:T(8,128)(2,1)S(1)}, bf16[128,32,128]{2,1,0:T(8,128)(2,1)}, u32[]{:S(2)}) copy-start(bf16[128,32,128]{2,1,0:T(8,128)(2,1)} %q_ref) | copy-start | bytes 3145732
  0.6 2.4 %collective-permute-start = (bf16[128,8,128]{2,1,0:T(8,128)(2,1)}, bf16[128,8,128]{2,1,0:T(8,128)(2,1)S(1)}, u32[]{:S(2)}, u32[]{:S(2)}) collective-permute-start(bf16[128,8,128]{2,1,0:T(8,128)(2,1)} %key_ref.1), channel_id=1, source_target_pairs={{0,1},{1,0},{2,3},{3,2},{4,5},{5,4},{6,7},{7,6},{8,9},{9,8},{10,11... | collective-permute-start | bytes 786440 | tf_op jit(solution)/shard_map/ppermute | solution.py:25
  3.7 14.8 %copy-start.2 = (s32[16]{0:T(128)S(1)}, s32[16]{0:T(128)}, u32[]{:S(2)}) copy-start(s32[16]{0:T(128)} %lengths_ref.1) | copy-start | bytes 196
  3.7 6.9 %collective-permute-start.1 = (bf16[128,32,128]{2,1,0:T(8,128)(2,1)S(1)}, bf16[128,32,128]{2,1,0:T(8,128)(2,1)S(1)}, u32[]{:S(2)}, u32[]{:S(2)}) collective-permute-start(bf16[128,32,128]{2,1,0:T(8,128)(2,1)S(1)} %copy-done), channel_id=1, source_target_pairs={{0,1},{1,0},{2,3},{3,2},{4,5},{5,4},{6,7},{7,6},{8,9},{9,8},{10,11... | collective-permute-start | bytes 3145736 | tf_op jit(solution)/shard_map/ppermute | solution.py:25
  3.9 6.8 %collective-permute-start.2 = (bf16[128,32,128]{2,1,0:T(8,128)(2,1)S(1)}, bf16[128,32,128]{2,1,0:T(8,128)(2,1)S(1)}, u32[]{:S(2)}, u32[]{:S(2)}) collective-permute-start(bf16[128,32,128]{2,1,0:T(8,128)(2,1)S(1)} %copy-done.1), channel_id=1, source_target_pairs={{0,1},{1,0},{2,3},{3,2},{4,5},{5,4},{6,7},{7,6},{8,9},{9,8},{10,11... | collective-permute-start | bytes 3145736 | tf_op jit(solution)/shard_map/ppermute | solution.py:25
  4.3 8.4 %collective-permute-start.3 = (bf16[128,8,128]{2,1,0:T(8,128)(2,1)S(1)}, bf16[128,8,128]{2,1,0:T(8,128)(2,1)S(1)}, u32[]{:S(2)}, u32[]{:S(2)}) collective-permute-start(bf16[128,8,128]{2,1,0:T(8,128)(2,1)S(1)} %get-tuple-element.36.own_ref), channel_id=1, source_target_pairs={{0,1},{1,0},{2,3},{3,2},{4,5},{5,4},{6,7},{7,6},{8,9},{9,8},{10,11... | collective-permute-start | bytes 786440 | tf_op jit(solution)/shard_map/ppermute | solution.py:25
  4.4 14.1 %collective-permute-start.5 = (bf16[4,2,128,128]{3,2,1,0:T(8,128)(2,1)S(1)}, bf16[4,2,128,128]{3,2,1,0:T(8,128)(2,1)S(1)}, u32[]{:S(2)}, u32[]{:S(2)}) collective-permute-start(bf16[4,2,128,128]{3,2,1,0:T(8,128)(2,1)S(1)} %pack_other.1.refs_0_), channel_id=1, source_target_pairs={{0,4},{1,5},{2,6},{3,7},{4,8},{5,9},{6,10},{7,11},{8,12},{9,13},{1... | collective-permute-start | bytes 786440 | tf_op jit(solution)/shard_map/ppermute | solution.py:21
  7.5 11.0 %collective-permute-start.4 = (bf16[4,2,128,128]{3,2,1,0:T(8,128)(2,1)S(1)}, bf16[4,2,128,128]{3,2,1,0:T(8,128)(2,1)S(1)}, u32[]{:S(2)}, u32[]{:S(2)}) collective-permute-start(bf16[4,2,128,128]{3,2,1,0:T(8,128)(2,1)S(1)} %pack_other.1.refs_0_), channel_id=1, source_target_pairs={{0,2},{1,3},{2,4},{3,5},{4,6},{5,7},{6,8},{7,9},{8,10},{9,11},{10,... | collective-permute-start | bytes 786440 | tf_op jit(solution)/shard_map/ppermute | solution.py:21
  13.4 20.2 %collective-permute-start.7 = (bf16[4,2,128,128]{3,2,1,0:T(8,128)(2,1)S(1)}, bf16[4,2,128,128]{3,2,1,0:T(8,128)(2,1)S(1)}, u32[]{:S(2)}, u32[]{:S(2)}) collective-permute-start(bf16[4,2,128,128]{3,2,1,0:T(8,128)(2,1)S(1)} %pack_both.1.refs_0_), channel_id=1, source_target_pairs={{0,4},{1,5},{2,6},{3,7},{4,8},{5,9},{6,10},{7,11},{8,12},{9,13},{1... | collective-permute-start | bytes 786440 | tf_op jit(solution)/shard_map/ppermute | solution.py:21
  15.4 18.3 %collective-permute-start.6 = (bf16[4,2,128,128]{3,2,1,0:T(8,128)(2,1)S(1)}, bf16[4,2,128,128]{3,2,1,0:T(8,128)(2,1)S(1)}, u32[]{:S(2)}, u32[]{:S(2)}) collective-permute-start(bf16[4,2,128,128]{3,2,1,0:T(8,128)(2,1)S(1)} %pack_both.1.refs_0_), channel_id=1, source_target_pairs={{0,2},{1,3},{2,4},{3,5},{4,6},{5,7},{6,8},{7,9},{8,10},{9,11},{10,... | collective-permute-start | bytes 786440 | tf_op jit(solution)/shard_map/ppermute | solution.py:21
  25.0 18.5 %collective-permute-start.8 = (bf16[4,2,128,128]{3,2,1,0:T(8,128)(2,1)S(1)}, bf16[4,2,128,128]{3,2,1,0:T(8,128)(2,1)S(1)}, u32[]{:S(2)}, u32[]{:S(2)}) collective-permute-start(bf16[4,2,128,128]{3,2,1,0:T(8,128)(2,1)S(1)} %get-tuple-element.39), channel_id=1, source_target_pairs={{4,0},{5,1},{6,2},{7,3},{8,4},{9,5},{10,6},{11,7},{12,8},{13,9},{1... | collective-permute-start | bytes 786440 | tf_op jit(solution)/shard_map/ppermute | solution.py:21
  28.4 15.2 %collective-permute-start.9 = (bf16[4,2,128,128]{3,2,1,0:T(8,128)(2,1)S(1)}, bf16[4,2,128,128]{3,2,1,0:T(8,128)(2,1)S(1)}, u32[]{:S(2)}, u32[]{:S(2)}) collective-permute-start(bf16[4,2,128,128]{3,2,1,0:T(8,128)(2,1)S(1)} %get-tuple-element.40), channel_id=1, source_target_pairs={{2,0},{3,1},{4,2},{5,3},{6,4},{7,5},{8,6},{9,7},{10,8},{11,9},{12,... | collective-permute-start | bytes 786440 | tf_op jit(solution)/shard_map/ppermute | solution.py:21
  39.7 15.7 %collective-permute-start.13 = (bf16[4,2,128,128]{3,2,1,0:T(8,128)(2,1)S(1)}, bf16[4,2,128,128]{3,2,1,0:T(8,128)(2,1)S(1)}, u32[]{:S(2)}, u32[]{:S(2)}) collective-permute-start(bf16[4,2,128,128]{3,2,1,0:T(8,128)(2,1)S(1)} %get-tuple-element.48), channel_id=1, source_target_pairs={{4,0},{5,1},{6,2},{7,3},{8,4},{9,5},{10,6},{11,7},{12,8},{13,9},{1... | collective-permute-start | bytes 786440 | tf_op jit(solution)/shard_map/ppermute | solution.py:21
  41.6 13.8 %collective-permute-start.14 = (bf16[4,2,128,128]{3,2,1,0:T(8,128)(2,1)S(1)}, bf16[4,2,128,128]{3,2,1,0:T(8,128)(2,1)S(1)}, u32[]{:S(2)}, u32[]{:S(2)}) collective-permute-start(bf16[4,2,128,128]{3,2,1,0:T(8,128)(2,1)S(1)} %get-tuple-element.49), channel_id=1, source_target_pairs={{2,0},{3,1},{4,2},{5,3},{6,4},{7,5},{8,6},{9,7},{10,8},{11,9},{12,... | collective-permute-start | bytes 786440 | tf_op jit(solution)/shard_map/ppermute | solution.py:21
  46.9 6.2 %collective-permute-start.10 = (bf16[56,16,128]{2,1,0:T(8,128)(2,1)S(1)}, bf16[56,16,128]{2,1,0:T(8,128)(2,1)S(1)}, u32[]{:S(2)}, u32[]{:S(2)}) collective-permute-start(bf16[56,16,128]{2,1,0:T(8,128)(2,1)S(1)} %get-tuple-element.43), channel_id=1, source_target_pairs={{0,1},{1,0},{2,3},{3,2},{4,5},{5,4},{6,7},{7,6},{8,9},{9,8},{10,11... | collective-permute-start | bytes 688136 | tf_op jit(solution)/shard_map/ppermute | solution.py:25
  51.4 1.8 %collective-permute-start.11 = (bf16[56,16,128]{2,1,0:T(8,128)(2,1)S(1)}, bf16[56,16,128]{2,1,0:T(8,128)(2,1)S(1)}, u32[]{:S(2)}, u32[]{:S(2)}) collective-permute-start(bf16[56,16,128]{2,1,0:T(8,128)(2,1)S(1)} %get-tuple-element.44), channel_id=1, source_target_pairs={{0,1},{1,0},{2,3},{3,2},{4,5},{5,4},{6,7},{7,6},{8,9},{9,8},{10,11... | collective-permute-start | bytes 688136 | tf_op jit(solution)/shard_map/ppermute | solution.py:25
  51.5 1.7 %collective-permute-start.12 = (bf16[48,16,128]{2,1,0:T(8,128)(2,1)S(1)}, bf16[48,16,128]{2,1,0:T(8,128)(2,1)S(1)}, u32[]{:S(2)}, u32[]{:S(2)}) collective-permute-start(bf16[48,16,128]{2,1,0:T(8,128)(2,1)S(1)} %get-tuple-element.45), channel_id=1, source_target_pairs={{0,1},{1,0},{2,3},{3,2},{4,5},{5,4},{6,7},{7,6},{8,9},{9,8},{10,11... | collective-permute-start | bytes 589832 | tf_op jit(solution)/shard_map/ppermute | solution.py:25
  56.1 3.3 %collective-permute-start.15 = (bf16[4,128,128]{2,1,0:T(8,128)(2,1)S(1)}, bf16[4,128,128]{2,1,0:T(8,128)(2,1)S(1)}, u32[]{:S(2)}, u32[]{:S(2)}) collective-permute-start(bf16[4,128,128]{2,1,0:T(8,128)(2,1)S(1)} %get-tuple-element.52), channel_id=1, source_target_pairs={{0,1},{1,0},{2,3},{3,2},{4,5},{5,4},{6,7},{7,6},{8,9},{9,8},{10,11... | collective-permute-start | bytes 393224 | tf_op jit(solution)/shard_map/ppermute | solution.py:25

commit v16 on v15

--- a/solution.py
+++ b/solution.py
@@ -207,20 +207,28 @@
     return jnp.concatenate([row] * copies, axis=1), jnp.concatenate([lane] * copies, axis=1)
 
 
-def store_tiles(ref, e, at, tiles, diagonal):
+def store_tile(ref, e, j, at, tile, diagonal):
     tokens, pair = diagonal.shape
     lanes = slice(at, at + pair)
-    ref[0, e, :tokens, lanes] = jnp.where(diagonal, 0.0, tiles[0]).astype(BF16)
-    for j, tile in enumerate(tiles[1:], 1):
+    if j:
         ref[0, e, j * tokens : (j + 1) * tokens, lanes] = tile.astype(BF16)
-    ref[0, e, -tokens:, lanes] = jnp.where(diagonal, tiles[0], 0.0).astype(BF16)
+    else:
+        ref[0, e, :tokens, lanes] = jnp.where(diagonal, 0.0, tile).astype(BF16)
+        ref[0, e, -tokens:, lanes] = jnp.where(diagonal, tile, 0.0).astype(BF16)
+
+
+def load_tile(ref, e, j, at, pair, tokens):
+    tile = ref[0, e, j * tokens : (j + 1) * tokens, at : at + pair]
+    if j == 0:
+        tile += ref[0, e, -tokens:, at : at + pair]
+    return tile.astype(F32)
 
 
 def prob_kernel(halo, place_ref, lengths_ref, qd_ref, *refs):
     k_refs = refs[: halo + 1]
-    p_ref = refs[halo + 1]
-    dv_refs = refs[halo + 2 : -3]
-    k_scr, acc, firsts = refs[-3:]
+    w_ref, inv_ref, do_ref = refs[halo + 1 : halo + 4]
+    dv_refs = refs[halo + 4 : -4]
+    k_scr, acc, bias, tiles = refs[-4:]
     _, _, _, group, tokens, dim = qd_ref.shape
     count = 2 * halo + 1
     pair = HEADS_AT_ONCE * tokens
@@ -231,28 +239,44 @@
     def _():
         for e in range(2):
             query_pos = lane[:1] + (2 * halo + e) * tokens
-            firsts[e] = first_allowed(lengths_ref, query_pos, place_ref[1])
+            first = first_allowed(lengths_ref, query_pos, place_ref[1]) - row
+            last = (e + count - 1) * tokens
+            bias[e, 0] = jnp.where(first <= jnp.where(diagonal, last, e * tokens), 0.0, MASKED)
+            for j in range(1, count - 1):
+                bias[e, j] = jnp.where(first <= (e + j) * tokens, 0.0, MASKED)
 
     window_of(k_refs, k_scr)
+    scale = dim**-0.5 * LOG2E
+    turn = 0
     for e in range(2):
-        first = firsts[e] - row
         k = k_scr[pl.ds(e, count)].reshape(count * tokens, dim)
         q = qd_ref[0, e, 0].reshape(group * tokens, dim)
-        do = qd_ref[0, e, 1].reshape(group * tokens, dim)
         for at in range(0, group * tokens, pair):
+            scr = tiles.at[turn % 2]
+            turn += 1
             s = lax.dot_general(k, q[at : at + pair], NT, preferred_element_type=F32)
-            tiles = [s[j * tokens : (j + 1) * tokens] for j in range(count)]
-            last = (e + count - 1) * tokens
-            bound = jnp.where(diagonal, last, e * tokens)
-            tiles[0] = jnp.where(first <= bound, jnp.where(diagonal, tiles.pop(), tiles[0]), MASKED)
-            for j in range(1, count - 1):
-                tiles[j] = jnp.where(first <= (e + j) * tokens, tiles[j], MASKED)
-            top = folded(jnp.maximum, functools.reduce(jnp.maximum, tiles))
-            tiles = [jnp.exp2((tile - top) * (dim**-0.5 * LOG2E)) for tile in tiles]
-            inv = 1.0 / folded(jnp.add, functools.reduce(jnp.add, tiles))
-            store_tiles(p_ref, e, at, [tile * inv for tile in tiles], diagonal)
+            top = None
+            for j in range(count - 1):
+                tile = s[j * tokens : (j + 1) * tokens]
+                if j == 0:
+                    tile = jnp.where(diagonal, s[(count - 1) * tokens :], tile)
+                tile += bias[e, j]
+                scr[j] = tile
+                top = tile if top is None else jnp.maximum(top, tile)
+            top = folded(jnp.maximum, top) * scale
+            total = None
+            for j in range(count - 1):
+                w = jnp.exp2(scr[j] * scale - top)
+                store_tile(w_ref, e, j, at, w, diagonal)
+                total = w if total is None else total + w
+            inv = 1.0 / folded(jnp.add, total)
+            inv_ref[0, e, :, at : at + pair] = inv
+            for g in range(at // tokens, (at + pair) // tokens):
+                of_row = jnp.broadcast_to(inv[:, g * tokens - at : (g + 1) * tokens - at], (8, tokens)).T
+                do_ref[0, e, g] = (qd_ref[0, e, 1, g].astype(F32) * of_row[:, :1]).astype(BF16)
+        do = do_ref[0, e].reshape(group * tokens, dim)
         keep = (2 * halo - e) * tokens
-        dv = jnp.dot(p_ref[0, e, :keep], do, preferred_element_type=F32).reshape(2 * halo - e, tokens, dim)
+        dv = jnp.dot(w_ref[0, e, :keep], do, preferred_element_type=F32).reshape(2 * halo - e, tokens, dim)
         if e == 0:
             acc[...] = dv
         else:
@@ -261,30 +285,38 @@
         ref[0] = acc[pl.ds(2 * (halo - back), 2)].astype(BF16)
 
 
-def dscore_kernel(halo, place_ref, qd_ref, p_ref, *refs):
+def dscore_kernel(halo, place_ref, qd_ref, w_ref, inv_ref, do_ref, *refs):
     v_refs = refs[: halo + 1]
     ds_ref = refs[halo + 1]
-    dk_refs = refs[halo + 2 : -2]
-    v_scr, acc = refs[-2:]
+    dk_refs = refs[halo + 2 : -3]
+    v_scr, acc, tiles = refs[-3:]
     _, _, _, group, tokens, dim = qd_ref.shape
     count = 2 * halo + 1
     pair = HEADS_AT_ONCE * tokens
-    window_of(v_refs, v_scr)
     row, lane = on_diagonal(tokens, HEADS_AT_ONCE)
     diagonal = row <= lane
+    window_of(v_refs, v_scr)
+    turn = 0
     for e in range(2):
         v = v_scr[pl.ds(e, count)].reshape(count * tokens, dim)
         q = qd_ref[0, e, 0].reshape(group * tokens, dim)
-        do = qd_ref[0, e, 1].reshape(group * tokens, dim)
+        do = do_ref[0, e].reshape(group * tokens, dim)
         for at in range(0, group * tokens, pair):
+            scr = tiles.at[turn % 2]
+            turn += 1
             dp = lax.dot_general(v, do[at : at + pair], NT, preferred_element_type=F32)
-            dps = [dp[j * tokens : (j + 1) * tokens] for j in range(count)]
-            dps[0] = jnp.where(diagonal, dps.pop(), dps[0])
-            ps = [p_ref[0, e, j * tokens : (j + 1) * tokens, at : at + pair] for j in range(count)]
-            ps[0] += ps.pop()
-            ps = [p.astype(F32) for p in ps]
-            delta = folded(jnp.add, functools.reduce(jnp.add, [p * dp for p, dp in zip(ps, dps)]))
-            store_tiles(ds_ref, e, at, [p * (dp - delta) for p, dp in zip(ps, dps)], diagonal)
+            delta = None
+            for j in range(count - 1):
+                tile = dp[j * tokens : (j + 1) * tokens]
+                if j == 0:
+                    tile = jnp.where(diagonal, dp[(count - 1) * tokens :], tile)
+                scr[j] = tile
+                term = load_tile(w_ref, e, j, at, pair, tokens) * tile
+                delta = term if delta is None else delta + term
+            delta = folded(jnp.add, delta) * inv_ref[0, e, :, at : at + pair]
+            for j in range(count - 1):
+                w = load_tile(w_ref, e, j, at, pair, tokens)
+                store_tile(ds_ref, e, j, at, w * (scr[j] - delta), diagonal)
         keep = (2 * halo - e) * tokens
         dk = jnp.dot(ds_ref[0, e, :keep], q, preferred_element_type=F32).reshape(2 * halo - e, tokens, dim)
         if e == 0:
@@ -295,7 +327,7 @@
         ref[0] = (acc[pl.ds(2 * (halo - back), 2)] * dim**-0.5).astype(BF16)
 
 
-def own_kernel(halo, place_ref, qd_ref, p_ref, ds_ref, *refs):
+def own_kernel(halo, place_ref, qd_ref, w_ref, do_ref, ds_ref, *refs):
     k_refs, back_refs = refs[: halo + 1], refs[halo + 1 : 2 * halo + 1]
     dq_ref, *other_refs, dk_ref, dv_ref, k_scr, dq_scr, dv_scr, far_dv = refs[2 * halo + 1 :]
     core, head = place_ref[0], pl.program_id(0)
@@ -306,14 +338,14 @@
     window_of(k_refs, k_scr)
     for e in range(2):
         q = qd_ref[0, e, 0].reshape(group * tokens, dim)
-        do = qd_ref[0, e, 1].reshape(group * tokens, dim)
+        do = do_ref[0, e].reshape(group * tokens, dim)
         k = k_scr[pl.ds(e, count)].reshape(count * tokens, dim)
         dqt = jnp.dot(k.T, ds_ref[0, e], preferred_element_type=F32) * scale
         for g in range(group):
             dq_scr[e, pl.ds(head * group + g, tokens, stride=rows), :] = dqt[:, g * tokens : (g + 1) * tokens].T
         keep = (2 * halo - e) * tokens
         dk = jnp.dot(ds_ref[0, e, keep:], q, preferred_element_type=F32) * scale
-        dv = jnp.dot(p_ref[0, e, keep:], do, preferred_element_type=F32)
+        dv = jnp.dot(w_ref[0, e, keep:], do, preferred_element_type=F32)
         if e == 0:
             dk_ref[0, 0], dv_scr[0] = dk, dv
         else:
@@ -474,6 +506,11 @@
     qd_spec = per_head(2, 2, group, tokens, dim)
     p_spec = per_head(2, count * tokens, group * tokens)
     p_shape = pltpu.VMEM((half, 2, count * tokens, group * tokens), BF16)
+    inv_shape = pltpu.VMEM((half, 2, 1, group * tokens), F32)
+    inv_spec = per_head(2, 1, group * tokens)
+    do_shape = pltpu.VMEM((half, 2, group, tokens, dim), BF16)
+    do_spec = per_head(2, group, tokens, dim)
+    tiles = pltpu.VMEM((2, count - 1, tokens, HEADS_AT_ONCE * tokens), F32)
     pair_spec = per_head(2, tokens, dim)
     pair = (half, 2, tokens, dim)
     one_spec = per_head(tokens, dim)
@@ -492,16 +529,16 @@
 
     k_pairs = halo_of(k_own)
     v_pairs = halo_of(v_own)
-    prob, *dv_halo = call(
+    prob, inverse, scaled, *dv_halo = call(
         functools.partial(prob_kernel, halo),
         "prob",
         (half,),
         (place, doc_lengths),
         (in_vmem(qd), *k_pairs),
         [qd_spec] + [pair_spec] * (halo + 1),
-        [p_shape] + [jax.ShapeDtypeStruct(pair, BF16)] * halo,
-        [p_spec] + [pair_spec] * halo,
-        [run, acc, pltpu.VMEM((2, 1, HEADS_AT_ONCE * tokens), jnp.int32)],
+        [p_shape, inv_shape, do_shape] + [jax.ShapeDtypeStruct(pair, BF16)] * halo,
+        [p_spec, inv_spec, do_spec] + [pair_spec] * halo,
+        [run, acc, tiles, tiles],
         4 * product,
     )
     dv_back = sent_back(dv_halo)
@@ -510,11 +547,11 @@
         "dscore",
         (half,),
         place,
-        (in_vmem(qd), in_vmem(prob), *v_pairs),
-        [qd_spec, p_spec] + [pair_spec] * (halo + 1),
+        (in_vmem(qd), in_vmem(prob), in_vmem(inverse), in_vmem(scaled), *v_pairs),
+        [qd_spec, p_spec, inv_spec, do_spec] + [pair_spec] * (halo + 1),
         [p_shape] + [jax.ShapeDtypeStruct(pair, BF16)] * halo,
         [p_spec] + [pair_spec] * halo,
-        [run, acc],
+        [run, acc, tiles],
         4 * product,
     )
     dk_back = sent_back(dk_halo)
@@ -523,8 +560,8 @@
         "own",
         (half,),
         place,
-        (in_vmem(qd), in_vmem(prob), in_vmem(dscore), *k_pairs, *dv_back),
-        [qd_spec, p_spec, p_spec] + [pair_spec] * (2 * halo + 1),
+        (in_vmem(qd), in_vmem(prob), in_vmem(scaled), in_vmem(dscore), *k_pairs, *dv_back),
+        [qd_spec, p_spec, do_spec, p_spec] + [pair_spec] * (2 * halo + 1),
         [dq_shape, *parts, jax.ShapeDtypeStruct(pair, F32), one_shape],
         [dq_spec, *part_specs, pair_spec, one_spec],
         [

time: 61.1 us -> 61.7 us (level)
  no operation moved by 1% of the time
where the time goes in v16:
time: 61.7 us; the launch traced here: 61.4 us
  starting transfers between devices  32.5 us (53%)
  Pallas kernels  25.7 us (42%)
  waiting for transfers between devices  2.28 us (4%)
  between operations  0.89 us (1%)
    pallas_call x10, Pallas kernels, call(): pl.pallas_call(kernel, out_shape=outs, grid_spec=pltpu.PrefetchScalarGrid...  25.7 us
    ppermute x8, starting transfers between devices, moved(): return lax.ppermute(array, AXES, pairs)  23.7 us
    ppermute x8, starting transfers between devices, swapped(): return lax.ppermute(array, AXES, [(d, d ^ 1) for d in range(device_count)])  8.76 us
    ppermute x8, waiting for transfers between devices, swapped(): return lax.ppermute(array, AXES, [(d, d ^ 1) for d in range(device_count)])  2.26 us
  transfers between devices with their start and end apart: 16, of which 2 were waited for; matrix products, arithmetic and copies ran while one was open for 0% of the time, Pallas kernels for 37%

profile of v16, /device:TPU:23, one launch (start us, length us, event | category | flops | bytes accessed | tf_op | source)
XLA Modules:
  0.0 61.4 jit_solution(437126705926445291)
XLA Ops:
  0.6 0.7 %collective-permute-start = (bf16[128,8,128]{2,1,0:T(8,128)(2,1)}, bf16[128,8,128]{2,1,0:T(8,128)(2,1)S(1)}, u32[]{:S(2)}, u32[]{:S(2)}) collective-permute-start(bf16[128,8,128]{2,1,0:T(8,128)(2,1)} %key_ref.1), channel_id=1, source_target_pairs={{0,1},{1,0},{2,3},{3,2},{4,5},{5,4},{6,7},{7,6},{8,9},{9,8},{10,11... | collective-permute-start | bytes 786440 | tf_op jit(solution)/shard_map/ppermute | solution.py:25
  1.4 0.1 pad_add_fusion.place_ref
  1.5 1.6 %fetch.1 = (bf16[4,2,128,128]{3,2,1,0:T(8,128)(2,1)S(1)}, bf16[128,8,128]{2,1,0:T(8,128)(2,1)S(1)}) custom-call(s32[2]{0:T(128)S(1)} %pad_add_fusion.place_ref, bf16[128,8,128]{2,1,0:T(8,128)(2,1)} %key_ref.1, bf16[128,8,128]{2,1,0:T(8,128)(2,1)} %refs_0_.1), custom_call_target="tpu_custom_call" | custom-call | flops 1000000000 | tf_op jit(solution)/shard_map/fetch/pallas_call | solution.py:38
  3.1 0.6 %pack_other.1.refs_0_ = bf16[4,2,128,128]{3,2,1,0:T(8,128)(2,1)S(1)} custom-call(s32[2]{0:T(128)S(1)} %pad_add_fusion.place_ref, bf16[128,8,128]{2,1,0:T(8,128)(2,1)S(1)} %collective-permute-done.other_ref, bf16[4,2,128,128]{3,2,1,0:T(8,128)(2,1)S(1)} %get-tuple-element.30._), custom_call_target="tpu_custom_call", output_to_operand_aliasing={{}: (2, {})} | custom-call | flops 1000000000 | tf_op jit(solution)/shard_map/pack_other/pallas_call | solution.py:38
  3.7 0.0 copy-start.2
  3.7 0.1 collective-permute-start.1
  3.9 0.4 collective-permute-start.2
  4.3 0.1 collective-permute-start.3
  4.4 3.1 %collective-permute-start.5 = (bf16[4,2,128,128]{3,2,1,0:T(8,128)(2,1)S(1)}, bf16[4,2,128,128]{3,2,1,0:T(8,128)(2,1)S(1)}, u32[]{:S(2)}, u32[]{:S(2)}) collective-permute-start(bf16[4,2,128,128]{3,2,1,0:T(8,128)(2,1)S(1)} %pack_other.1.refs_0_), channel_id=1, source_target_pairs={{0,4},{1,5},{2,6},{3,7},{4,8},{5,9},{6,10},{7,11},{8,12},{9,13},{1... | collective-permute-start | bytes 786440 | tf_op jit(solution)/shard_map/ppermute | solution.py:21
  7.5 3.1 %collective-permute-start.4 = (bf16[4,2,128,128]{3,2,1,0:T(8,128)(2,1)S(1)}, bf16[4,2,128,128]{3,2,1,0:T(8,128)(2,1)S(1)}, u32[]{:S(2)}, u32[]{:S(2)}) collective-permute-start(bf16[4,2,128,128]{3,2,1,0:T(8,128)(2,1)S(1)} %pack_other.1.refs_0_), channel_id=1, source_target_pairs={{0,2},{1,3},{2,4},{3,5},{4,6},{5,7},{6,8},{7,9},{8,10},{9,11},{10,... | collective-permute-start | bytes 786440 | tf_op jit(solution)/shard_map/ppermute | solution.py:21
  10.7 2.0 %arrange.1.qd_ref = bf16[4,2,2,4,128,128]{5,4,3,2,1,0:T(8,128)(2,1)S(1)} custom-call(s32[2]{0:T(128)S(1)} %pad_add_fusion.place_ref, bf16[128,32,128]{2,1,0:T(8,128)(2,1)S(1)} %copy-done, bf16[128,32,128]{2,1,0:T(8,128)(2,1)S(1)} %copy-done.1, bf16[128,32,128]{2,1,0:T(8,128)(2,1)S(1)} %collective-permute-done.1.q_other_ref, ...), custom_call_target="tpu_custom_call" | custom-call | flops 1000000000 | tf_op jit(solution)/shard_map/arrange/pallas_call | solution.py:38
  12.7 0.7 %pack_both.1.refs_0_ = bf16[4,2,128,128]{3,2,1,0:T(8,128)(2,1)S(1)} custom-call(s32[2]{0:T(128)S(1)} %pad_add_fusion.place_ref, bf16[128,8,128]{2,1,0:T(8,128)(2,1)S(1)} %get-tuple-element.40.own_ref, bf16[128,8,128]{2,1,0:T(8,128)(2,1)S(1)} %collective-permute-done.3.other_ref), custom_call_target="tpu_custom_call" | custom-call | flops 1000000000 | tf_op jit(solution)/shard_map/pack_both/pallas_call | solution.py:38
  13.4 1.9 %collective-permute-start.7 = (bf16[4,2,128,128]{3,2,1,0:T(8,128)(2,1)S(1)}, bf16[4,2,128,128]{3,2,1,0:T(8,128)(2,1)S(1)}, u32[]{:S(2)}, u32[]{:S(2)}) collective-permute-start(bf16[4,2,128,128]{3,2,1,0:T(8,128)(2,1)S(1)} %pack_both.1.refs_0_), channel_id=1, source_target_pairs={{0,4},{1,5},{2,6},{3,7},{4,8},{5,9},{6,10},{7,11},{8,12},{9,13},{1... | collective-permute-start | bytes 786440 | tf_op jit(solution)/shard_map/ppermute | solution.py:21
  15.4 3.1 %collective-permute-start.6 = (bf16[4,2,128,128]{3,2,1,0:T(8,128)(2,1)S(1)}, bf16[4,2,128,128]{3,2,1,0:T(8,128)(2,1)S(1)}, u32[]{:S(2)}, u32[]{:S(2)}) collective-permute-start(bf16[4,2,128,128]{3,2,1,0:T(8,128)(2,1)S(1)} %pack_both.1.refs_0_), channel_id=1, source_target_pairs={{0,2},{1,3},{2,4},{3,5},{4,6},{5,7},{6,8},{7,9},{8,10},{9,11},{10,... | collective-permute-start | bytes 786440 | tf_op jit(solution)/shard_map/ppermute | solution.py:21
  18.5 0.0 collective-permute-done.5.refs_2_
  18.5 0.0 collective-permute-done.4.refs_1_
  18.5 7.1 %prob.1 = (bf16[4,2,640,512]{3,2,1,0:T(8,128)(2,1)S(1)}, f32[4,2,1,512]{3,2,1,0:T(1,128)S(1)}, bf16[4,2,4,128,128]{4,3,2,1,0:T(8,128)(2,1)S(1)}, bf16[4,2,128,12...) custom-call(s32[2]{0:T(128)S(1)} %pad_add_fusion.place_ref, s32[16]{0:T(128)S(1)} %copy-done.2, ...), custom_call_target="tpu_custom_call" | custom-call | flops 2684354560 | tf_op jit(solution)/shard_map/prob/pallas_call | solution.py:38
  25.7 3.4 %collective-permute-start.8 = (bf16[4,2,128,128]{3,2,1,0:T(8,128)(2,1)S(1)}, bf16[4,2,128,128]{3,2,1,0:T(8,128)(2,1)S(1)}, u32[]{:S(2)}, u32[]{:S(2)}) collective-permute-start(bf16[4,2,128,128]{3,2,1,0:T(8,128)(2,1)S(1)} %get-tuple-element.43), channel_id=1, source_target_pairs={{4,0},{5,1},{6,2},{7,3},{8,4},{9,5},{10,6},{11,7},{12,8},{13,9},{1... | collective-permute-start | bytes 786440 | tf_op jit(solution)/shard_map/ppermute | solution.py:21
  29.1 5.2 %collective-permute-start.9 = (bf16[4,2,128,128]{3,2,1,0:T(8,128)(2,1)S(1)}, bf16[4,2,128,128]{3,2,1,0:T(8,128)(2,1)S(1)}, u32[]{:S(2)}, u32[]{:S(2)}) collective-permute-start(bf16[4,2,128,128]{3,2,1,0:T(8,128)(2,1)S(1)} %get-tuple-element.44), channel_id=1, source_target_pairs={{2,0},{3,1},{4,2},{5,3},{6,4},{7,5},{8,6},{9,7},{10,8},{11,9},{12,... | collective-permute-start | bytes 786440 | tf_op jit(solution)/shard_map/ppermute | solution.py:21
  34.3 6.0 %dscore.1 = (bf16[4,2,640,512]{3,2,1,0:T(8,128)(2,1)S(1)}, bf16[4,2,128,128]{3,2,1,0:T(8,128)(2,1)S(1)}, bf16[4,2,128,128]{3,2,1,0:T(8,128)(2,1)S(1)}) custom-call(s32[2]{0:T(128)S(1)} %pad_add_fusion.place_ref, bf16[4,2,2,4,128,128]{5,4,3,2,1,0:T(8,128)(2,1)S(1)} %arrange.1.qd_ref, bf16[4,2,640,512]{3,2,1,0:T(8,128)(2,1)S(1)} %get-tuple-element.37.w_ref, ...), custom_call_target="tpu_custom_call" | custom-call | flops 2684354560 | tf_op jit(solution)/shard_map/dscore/pallas_call | solution.py:38
  40.3 1.9 %collective-permute-start.13 = (bf16[4,2,128,128]{3,2,1,0:T(8,128)(2,1)S(1)}, bf16[4,2,128,128]{3,2,1,0:T(8,128)(2,1)S(1)}, u32[]{:S(2)}, u32[]{:S(2)}) collective-permute-start(bf16[4,2,128,128]{3,2,1,0:T(8,128)(2,1)S(1)} %get-tuple-element.52), channel_id=1, source_target_pairs={{4,0},{5,1},{6,2},{7,3},{8,4},{9,5},{10,6},{11,7},{12,8},{13,9},{1... | collective-permute-start | bytes 786440 | tf_op jit(solution)/shard_map/ppermute | solution.py:21
  42.2 1.9 %collective-permute-start.14 = (bf16[4,2,128,128]{3,2,1,0:T(8,128)(2,1)S(1)}, bf16[4,2,128,128]{3,2,1,0:T(8,128)(2,1)S(1)}, u32[]{:S(2)}, u32[]{:S(2)}) collective-permute-start(bf16[4,2,128,128]{3,2,1,0:T(8,128)(2,1)S(1)} %get-tuple-element.53), channel_id=1, source_target_pairs={{2,0},{3,1},{4,2},{5,3},{6,4},{7,5},{8,6},{9,7},{10,8},{11,9},{12,... | collective-permute-start | bytes 786440 | tf_op jit(solution)/shard_map/ppermute | solution.py:21
  44.2 3.3 %own.1 = (bf16[128,16,128]{2,1,0:T(8,128)(2,1)S(1)}, bf16[56,16,128]{2,1,0:T(8,128)(2,1)S(1)}, bf16[56,16,128]{2,1,0:T(8,128)(2,1)S(1)}, bf16[48,16,128]{2,1,0:T...) custom-call(s32[2]{0:T(128)S(1)} %pad_add_fusion.place_ref, ...), custom_call_target="tpu_custom_call" | custom-call | tf_op jit(solution)/shard_map/own/pallas_call | solution.py:38
  47.5 4.6 %collective-permute-start.10 = (bf16[56,16,128]{2,1,0:T(8,128)(2,1)S(1)}, bf16[56,16,128]{2,1,0:T(8,128)(2,1)S(1)}, u32[]{:S(2)}, u32[]{:S(2)}) collective-permute-start(bf16[56,16,128]{2,1,0:T(8,128)(2,1)S(1)} %get-tuple-element.47), channel_id=1, source_target_pairs={{0,1},{1,0},{2,3},{3,2},{4,5},{5,4},{6,7},{7,6},{8,9},{9,8},{10,11... | collective-permute-start | bytes 688136 | tf_op jit(solution)/shard_map/ppermute | solution.py:25
  52.1 0.1 collective-permute-start.11
  52.2 0.4 collective-permute-start.12
  52.6 1.3 %collective-permute-done.12.refs_2_ = bf16[48,16,128]{2,1,0:T(8,128)(2,1)S(1)} collective-permute-done((bf16[48,16,128]{2,1,0:T(8,128)(2,1)S(1)}, bf16[48,16,128]{2,1,0:T(8,128)(2,1)S(1)}, u32[]{:S(2)}, u32[]{:S(2)}) %collective-permute-start.12) | collective-permute-done | bytes 196640 | tf_op jit(solution)/shard_map/ppermute | solution.py:25
  53.9 2.2 %join.1 = (bf16[128,32,128]{2,1,0:T(8,128)(2,1)}, bf16[128,8,128]{2,1,0:T(8,128)(2,1)}) custom-call(s32[2]{0:T(128)S(1)} %pad_add_fusion.place_ref, bf16[128,16,128]{2,1,0:T(8,128)(2,1)S(1)} %get-tuple-element.45.dq_ref, bf16[4,128,128]{2,1,0:T(8,128)(2,1)S(1)} %get-tuple-element.46.dv_ref, bf16[56,16,128]{2,1,0:T(8,128)(2,1)S(1)} %collective-permute-done.10.refs_0_, ...), custom_call_target="tpu_custom_call" | custom-call | tf_op jit(solution)/shard_map/join/pallas_call | solution.py:38
  56.1 0.6 %sum_dk.1 = (bf16[4,128,128]{2,1,0:T(8,128)(2,1)S(1)}, bf16[4,128,128]{2,1,0:T(8,128)(2,1)S(1)}) custom-call(s32[2]{0:T(128)S(1)} %pad_add_fusion.place_ref, f32[4,2,128,128]{3,2,1,0:T(8,128)S(1)} %get-tuple-element.51.own_ref, bf16[4,2,128,128]{3,2,1,0:T(8,128)(2,1)S(1)} %collective-permute-done.13.refs_0_, ...), custom_call_target="tpu_custom_call" | custom-call | tf_op jit(solution)/shard_map/sum_dk/pallas_call | solution.py:38
  56.8 2.3 %collective-permute-start.15 = (bf16[4,128,128]{2,1,0:T(8,128)(2,1)S(1)}, bf16[4,128,128]{2,1,0:T(8,128)(2,1)S(1)}, u32[]{:S(2)}, u32[]{:S(2)}) collective-permute-start(bf16[4,128,128]{2,1,0:T(8,128)(2,1)S(1)} %get-tuple-element.56), channel_id=1, source_target_pairs={{0,1},{1,0},{2,3},{3,2},{4,5},{5,4},{6,7},{7,6},{8,9},{9,8},{10,11... | collective-permute-start | bytes 393224 | tf_op jit(solution)/shard_map/ppermute | solution.py:25
  59.0 1.0 %collective-permute-done.15.other_ref = bf16[4,128,128]{2,1,0:T(8,128)(2,1)S(1)} collective-permute-done((bf16[4,128,128]{2,1,0:T(8,128)(2,1)S(1)}, bf16[4,128,128]{2,1,0:T(8,128)(2,1)S(1)}, u32[]{:S(2)}, u32[]{:S(2)}) %collective-permute-start.15) | collective-permute-done | bytes 131104 | tf_op jit(solution)/shard_map/ppermute | solution.py:25
  60.0 1.4 %merge_dk.1 = bf16[128,8,128]{2,1,0:T(8,128)(2,1)} custom-call(s32[2]{0:T(128)S(1)} %pad_add_fusion.place_ref, bf16[4,128,128]{2,1,0:T(8,128)(2,1)S(1)} %get-tuple-element.55.own_ref, bf16[4,128,128]{2,1,0:T(8,128)(2,1)S(1)} %collective-permute-done.15.other_ref), custom_call_target="tpu_custom_call" | custom-call | tf_op jit(solution)/shard_map/merge_dk/pallas_call | solution.py:38
  (17 shorter events, 0.0 us)
Async XLA Ops:
  0.6 3.2 %copy-start.1 = (bf16[128,32,128]{2,1,0:T(8,128)(2,1)S(1)}, bf16[128,32,128]{2,1,0:T(8,128)(2,1)}, u32[]{:S(2)}) copy-start(bf16[128,32,128]{2,1,0:T(8,128)(2,1)} %do_ref) | copy-start | bytes 3145732
  0.6 3.1 %copy-start = (bf16[128,32,128]{2,1,0:T(8,128)(2,1)S(1)}, bf16[128,32,128]{2,1,0:T(8,128)(2,1)}, u32[]{:S(2)}) copy-start(bf16[128,32,128]{2,1,0:T(8,128)(2,1)} %q_ref) | copy-start | bytes 3145732
  0.6 2.4 %collective-permute-start = (bf16[128,8,128]{2,1,0:T(8,128)(2,1)}, bf16[128,8,128]{2,1,0:T(8,128)(2,1)S(1)}, u32[]{:S(2)}, u32[]{:S(2)}) collective-permute-start(bf16[128,8,128]{2,1,0:T(8,128)(2,1)} %key_ref.1), channel_id=1, source_target_pairs={{0,1},{1,0},{2,3},{3,2},{4,5},{5,4},{6,7},{7,6},{8,9},{9,8},{10,11... | collective-permute-start | bytes 786440 | tf_op jit(solution)/shard_map/ppermute | solution.py:25
  3.7 14.8 %copy-start.2 = (s32[16]{0:T(128)S(1)}, s32[16]{0:T(128)}, u32[]{:S(2)}) copy-start(s32[16]{0:T(128)} %lengths_ref.1) | copy-start | bytes 196
  3.7 6.9 %collective-permute-start.1 = (bf16[128,32,128]{2,1,0:T(8,128)(2,1)S(1)}, bf16[128,32,128]{2,1,0:T(8,128)(2,1)S(1)}, u32[]{:S(2)}, u32[]{:S(2)}) collective-permute-start(bf16[128,32,128]{2,1,0:T(8,128)(2,1)S(1)} %copy-done), channel_id=1, source_target_pairs={{0,1},{1,0},{2,3},{3,2},{4,5},{5,4},{6,7},{7,6},{8,9},{9,8},{10,11... | collective-permute-start | bytes 3145736 | tf_op jit(solution)/shard_map/ppermute | solution.py:25
  3.9 6.8 %collective-permute-start.2 = (bf16[128,32,128]{2,1,0:T(8,128)(2,1)S(1)}, bf16[128,32,128]{2,1,0:T(8,128)(2,1)S(1)}, u32[]{:S(2)}, u32[]{:S(2)}) collective-permute-start(bf16[128,32,128]{2,1,0:T(8,128)(2,1)S(1)} %copy-done.1), channel_id=1, source_target_pairs={{0,1},{1,0},{2,3},{3,2},{4,5},{5,4},{6,7},{7,6},{8,9},{9,8},{10,11... | collective-permute-start | bytes 3145736 | tf_op jit(solution)/shard_map/ppermute | solution.py:25
  4.3 8.4 %collective-permute-start.3 = (bf16[128,8,128]{2,1,0:T(8,128)(2,1)S(1)}, bf16[128,8,128]{2,1,0:T(8,128)(2,1)S(1)}, u32[]{:S(2)}, u32[]{:S(2)}) collective-permute-start(bf16[128,8,128]{2,1,0:T(8,128)(2,1)S(1)} %get-tuple-element.40.own_ref), channel_id=1, source_target_pairs={{0,1},{1,0},{2,3},{3,2},{4,5},{5,4},{6,7},{7,6},{8,9},{9,8},{10,11... | collective-permute-start | bytes 786440 | tf_op jit(solution)/shard_map/ppermute | solution.py:25
  4.4 14.1 %collective-permute-start.5 = (bf16[4,2,128,128]{3,2,1,0:T(8,128)(2,1)S(1)}, bf16[4,2,128,128]{3,2,1,0:T(8,128)(2,1)S(1)}, u32[]{:S(2)}, u32[]{:S(2)}) collective-permute-start(bf16[4,2,128,128]{3,2,1,0:T(8,128)(2,1)S(1)} %pack_other.1.refs_0_), channel_id=1, source_target_pairs={{0,4},{1,5},{2,6},{3,7},{4,8},{5,9},{6,10},{7,11},{8,12},{9,13},{1... | collective-permute-start | bytes 786440 | tf_op jit(solution)/shard_map/ppermute | solution.py:21
  7.5 11.0 %collective-permute-start.4 = (bf16[4,2,128,128]{3,2,1,0:T(8,128)(2,1)S(1)}, bf16[4,2,128,128]{3,2,1,0:T(8,128)(2,1)S(1)}, u32[]{:S(2)}, u32[]{:S(2)}) collective-permute-start(bf16[4,2,128,128]{3,2,1,0:T(8,128)(2,1)S(1)} %pack_other.1.refs_0_), channel_id=1, source_target_pairs={{0,2},{1,3},{2,4},{3,5},{4,6},{5,7},{6,8},{7,9},{8,10},{9,11},{10,... | collective-permute-start | bytes 786440 | tf_op jit(solution)/shard_map/ppermute | solution.py:21
  13.4 20.8 %collective-permute-start.7 = (bf16[4,2,128,128]{3,2,1,0:T(8,128)(2,1)S(1)}, bf16[4,2,128,128]{3,2,1,0:T(8,128)(2,1)S(1)}, u32[]{:S(2)}, u32[]{:S(2)}) collective-permute-start(bf16[4,2,128,128]{3,2,1,0:T(8,128)(2,1)S(1)} %pack_both.1.refs_0_), channel_id=1, source_target_pairs={{0,4},{1,5},{2,6},{3,7},{4,8},{5,9},{6,10},{7,11},{8,12},{9,13},{1... | collective-permute-start | bytes 786440 | tf_op jit(solution)/shard_map/ppermute | solution.py:21
  15.4 18.9 %collective-permute-start.6 = (bf16[4,2,128,128]{3,2,1,0:T(8,128)(2,1)S(1)}, bf16[4,2,128,128]{3,2,1,0:T(8,128)(2,1)S(1)}, u32[]{:S(2)}, u32[]{:S(2)}) collective-permute-start(bf16[4,2,128,128]{3,2,1,0:T(8,128)(2,1)S(1)} %pack_both.1.refs_0_), channel_id=1, source_target_pairs={{0,2},{1,3},{2,4},{3,5},{4,6},{5,7},{6,8},{7,9},{8,10},{9,11},{10,... | collective-permute-start | bytes 786440 | tf_op jit(solution)/shard_map/ppermute | solution.py:21
  25.7 18.5 %collective-permute-start.8 = (bf16[4,2,128,128]{3,2,1,0:T(8,128)(2,1)S(1)}, bf16[4,2,128,128]{3,2,1,0:T(8,128)(2,1)S(1)}, u32[]{:S(2)}, u32[]{:S(2)}) collective-permute-start(bf16[4,2,128,128]{3,2,1,0:T(8,128)(2,1)S(1)} %get-tuple-element.43), channel_id=1, source_target_pairs={{4,0},{5,1},{6,2},{7,3},{8,4},{9,5},{10,6},{11,7},{12,8},{13,9},{1... | collective-permute-start | bytes 786440 | tf_op jit(solution)/shard_map/ppermute | solution.py:21
  29.1 15.1 %collective-permute-start.9 = (bf16[4,2,128,128]{3,2,1,0:T(8,128)(2,1)S(1)}, bf16[4,2,128,128]{3,2,1,0:T(8,128)(2,1)S(1)}, u32[]{:S(2)}, u32[]{:S(2)}) collective-permute-start(bf16[4,2,128,128]{3,2,1,0:T(8,128)(2,1)S(1)} %get-tuple-element.44), channel_id=1, source_target_pairs={{2,0},{3,1},{4,2},{5,3},{6,4},{7,5},{8,6},{9,7},{10,8},{11,9},{12,... | collective-permute-start | bytes 786440 | tf_op jit(solution)/shard_map/ppermute | solution.py:21
  40.3 15.8 %collective-permute-start.13 = (bf16[4,2,128,128]{3,2,1,0:T(8,128)(2,1)S(1)}, bf16[4,2,128,128]{3,2,1,0:T(8,128)(2,1)S(1)}, u32[]{:S(2)}, u32[]{:S(2)}) collective-permute-start(bf16[4,2,128,128]{3,2,1,0:T(8,128)(2,1)S(1)} %get-tuple-element.52), channel_id=1, source_target_pairs={{4,0},{5,1},{6,2},{7,3},{8,4},{9,5},{10,6},{11,7},{12,8},{13,9},{1... | collective-permute-start | bytes 786440 | tf_op jit(solution)/shard_map/ppermute | solution.py:21
  42.2 13.9 %collective-permute-start.14 = (bf16[4,2,128,128]{3,2,1,0:T(8,128)(2,1)S(1)}, bf16[4,2,128,128]{3,2,1,0:T(8,128)(2,1)S(1)}, u32[]{:S(2)}, u32[]{:S(2)}) collective-permute-start(bf16[4,2,128,128]{3,2,1,0:T(8,128)(2,1)S(1)} %get-tuple-element.53), channel_id=1, source_target_pairs={{2,0},{3,1},{4,2},{5,3},{6,4},{7,5},{8,6},{9,7},{10,8},{11,9},{12,... | collective-permute-start | bytes 786440 | tf_op jit(solution)/shard_map/ppermute | solution.py:21
  47.5 6.4 %collective-permute-start.10 = (bf16[56,16,128]{2,1,0:T(8,128)(2,1)S(1)}, bf16[56,16,128]{2,1,0:T(8,128)(2,1)S(1)}, u32[]{:S(2)}, u32[]{:S(2)}) collective-permute-start(bf16[56,16,128]{2,1,0:T(8,128)(2,1)S(1)} %get-tuple-element.47), channel_id=1, source_target_pairs={{0,1},{1,0},{2,3},{3,2},{4,5},{5,4},{6,7},{7,6},{8,9},{9,8},{10,11... | collective-permute-start | bytes 688136 | tf_op jit(solution)/shard_map/ppermute | solution.py:25
  52.1 1.8 %collective-permute-start.11 = (bf16[56,16,128]{2,1,0:T(8,128)(2,1)S(1)}, bf16[56,16,128]{2,1,0:T(8,128)(2,1)S(1)}, u32[]{:S(2)}, u32[]{:S(2)}) collective-permute-start(bf16[56,16,128]{2,1,0:T(8,128)(2,1)S(1)} %get-tuple-element.48), channel_id=1, source_target_pairs={{0,1},{1,0},{2,3},{3,2},{4,5},{5,4},{6,7},{7,6},{8,9},{9,8},{10,11... | collective-permute-start | bytes 688136 | tf_op jit(solution)/shard_map/ppermute | solution.py:25
  52.2 1.7 %collective-permute-start.12 = (bf16[48,16,128]{2,1,0:T(8,128)(2,1)S(1)}, bf16[48,16,128]{2,1,0:T(8,128)(2,1)S(1)}, u32[]{:S(2)}, u32[]{:S(2)}) collective-permute-start(bf16[48,16,128]{2,1,0:T(8,128)(2,1)S(1)} %get-tuple-element.49), channel_id=1, source_target_pairs={{0,1},{1,0},{2,3},{3,2},{4,5},{5,4},{6,7},{7,6},{8,9},{9,8},{10,11... | collective-permute-start | bytes 589832 | tf_op jit(solution)/shard_map/ppermute | solution.py:25
  56.8 3.2 %collective-permute-start.15 = (bf16[4,128,128]{2,1,0:T(8,128)(2,1)S(1)}, bf16[4,128,128]{2,1,0:T(8,128)(2,1)S(1)}, u32[]{:S(2)}, u32[]{:S(2)}) collective-permute-start(bf16[4,128,128]{2,1,0:T(8,128)(2,1)S(1)} %get-tuple-element.56), channel_id=1, source_target_pairs={{0,1},{1,0},{2,3},{3,2},{4,5},{5,4},{6,7},{7,6},{8,9},{9,8},{10,11... | collective-permute-start | bytes 393224 | tf_op jit(solution)/shard_map/ppermute | solution.py:25

commit v17 on v15

--- a/solution.py
+++ b/solution.py
@@ -210,17 +210,18 @@
 def store_tiles(ref, e, at, tiles, diagonal):
     tokens, pair = diagonal.shape
     lanes = slice(at, at + pair)
-    ref[0, e, :tokens, lanes] = jnp.where(diagonal, 0.0, tiles[0]).astype(BF16)
+    shared = tiles[0].astype(F32)
+    ref[0, e, :tokens, lanes] = jnp.where(diagonal, 0.0, shared).astype(BF16)
     for j, tile in enumerate(tiles[1:], 1):
         ref[0, e, j * tokens : (j + 1) * tokens, lanes] = tile.astype(BF16)
-    ref[0, e, -tokens:, lanes] = jnp.where(diagonal, tiles[0], 0.0).astype(BF16)
+    ref[0, e, -tokens:, lanes] = jnp.where(diagonal, shared, 0.0).astype(BF16)
 
 
 def prob_kernel(halo, place_ref, lengths_ref, qd_ref, *refs):
     k_refs = refs[: halo + 1]
     p_ref = refs[halo + 1]
     dv_refs = refs[halo + 2 : -3]
-    k_scr, acc, firsts = refs[-3:]
+    k_scr, acc, bias = refs[-3:]
     _, _, _, group, tokens, dim = qd_ref.shape
     count = 2 * halo + 1
     pair = HEADS_AT_ONCE * tokens
@@ -231,22 +232,22 @@
     def _():
         for e in range(2):
             query_pos = lane[:1] + (2 * halo + e) * tokens
-            firsts[e] = first_allowed(lengths_ref, query_pos, place_ref[1])
+            first = first_allowed(lengths_ref, query_pos, place_ref[1]) - row
+            last = (e + count - 1) * tokens
+            bias[e, 0] = jnp.where(first <= jnp.where(diagonal, last, e * tokens), 0.0, MASKED)
+            for j in range(1, count - 1):
+                bias[e, j] = jnp.where(first <= (e + j) * tokens, 0.0, MASKED)
 
     window_of(k_refs, k_scr)
     for e in range(2):
-        first = firsts[e] - row
         k = k_scr[pl.ds(e, count)].reshape(count * tokens, dim)
         q = qd_ref[0, e, 0].reshape(group * tokens, dim)
         do = qd_ref[0, e, 1].reshape(group * tokens, dim)
         for at in range(0, group * tokens, pair):
             s = lax.dot_general(k, q[at : at + pair], NT, preferred_element_type=F32)
             tiles = [s[j * tokens : (j + 1) * tokens] for j in range(count)]
-            last = (e + count - 1) * tokens
-            bound = jnp.where(diagonal, last, e * tokens)
-            tiles[0] = jnp.where(first <= bound, jnp.where(diagonal, tiles.pop(), tiles[0]), MASKED)
-            for j in range(1, count - 1):
-                tiles[j] = jnp.where(first <= (e + j) * tokens, tiles[j], MASKED)
+            tiles[0] = jnp.where(diagonal, tiles.pop(), tiles[0])
+            tiles = [tile + bias[e, j] for j, tile in enumerate(tiles)]
             top = folded(jnp.maximum, functools.reduce(jnp.maximum, tiles))
             tiles = [jnp.exp2((tile - top) * (dim**-0.5 * LOG2E)) for tile in tiles]
             inv = 1.0 / folded(jnp.add, functools.reduce(jnp.add, tiles))
@@ -282,9 +283,8 @@
             dps[0] = jnp.where(diagonal, dps.pop(), dps[0])
             ps = [p_ref[0, e, j * tokens : (j + 1) * tokens, at : at + pair] for j in range(count)]
             ps[0] += ps.pop()
-            ps = [p.astype(F32) for p in ps]
-            delta = folded(jnp.add, functools.reduce(jnp.add, [p * dp for p, dp in zip(ps, dps)]))
-            store_tiles(ds_ref, e, at, [p * (dp - delta) for p, dp in zip(ps, dps)], diagonal)
+            delta = folded(jnp.add, functools.reduce(jnp.add, [p.astype(F32) * dp for p, dp in zip(ps, dps)]))
+            store_tiles(ds_ref, e, at, [p * (dp - delta).astype(BF16) for p, dp in zip(ps, dps)], diagonal)
         keep = (2 * halo - e) * tokens
         dk = jnp.dot(ds_ref[0, e, :keep], q, preferred_element_type=F32).reshape(2 * halo - e, tokens, dim)
         if e == 0:
@@ -501,7 +501,7 @@
         [qd_spec] + [pair_spec] * (halo + 1),
         [p_shape] + [jax.ShapeDtypeStruct(pair, BF16)] * halo,
         [p_spec] + [pair_spec] * halo,
-        [run, acc, pltpu.VMEM((2, 1, HEADS_AT_ONCE * tokens), jnp.int32)],
+        [run, acc, pltpu.VMEM((2, count - 1, tokens, HEADS_AT_ONCE * tokens), F32)],
         4 * product,
     )
     dv_back = sent_back(dv_halo)

time: 61.1 us -> 61 us (level)
  transfers between devices with their start and end apart: 16 -> 16, of which waited for: 2 -> 3; matrix products, arithmetic and copies ran while one was open for 0% -> 0% of each run, Pallas kernels for 37% -> 36%
where the time goes in v17:
time: 61 us; the launch traced here: 60.7 us
  starting transfers between devices  32.6 us (53%)
  Pallas kernels  24.6 us (40%)
  waiting for transfers between devices  2.57 us (4%)
  between operations  0.89 us (1%)
    pallas_call x10, Pallas kernels, call(): pl.pallas_call(kernel, out_shape=outs, grid_spec=pltpu.PrefetchScalarGrid...  24.6 us
    ppermute x8, starting transfers between devices, moved(): return lax.ppermute(array, AXES, pairs)  23.7 us
    ppermute x8, starting transfers between devices, swapped(): return lax.ppermute(array, AXES, [(d, d ^ 1) for d in range(device_count)])  8.85 us
    ppermute x8, waiting for transfers between devices, swapped(): return lax.ppermute(array, AXES, [(d, d ^ 1) for d in range(device_count)])  2.26 us
  transfers between devices with their start and end apart: 16, of which 3 were waited for; matrix products, arithmetic and copies ran while one was open for 0% of the time, Pallas kernels for 36%

profile of v17, /device:TPU:23, one launch (start us, length us, event | category | flops | bytes accessed | tf_op | source)
XLA Modules:
  0.0 60.7 jit_solution(6241999257982375832)
XLA Ops:
  0.6 0.7 %collective-permute-start = (bf16[128,8,128]{2,1,0:T(8,128)(2,1)}, bf16[128,8,128]{2,1,0:T(8,128)(2,1)S(1)}, u32[]{:S(2)}, u32[]{:S(2)}) collective-permute-start(bf16[128,8,128]{2,1,0:T(8,128)(2,1)} %key_ref.1), channel_id=1, source_target_pairs={{0,1},{1,0},{2,3},{3,2},{4,5},{5,4},{6,7},{7,6},{8,9},{9,8},{10,11... | collective-permute-start | bytes 786440 | tf_op jit(solution)/shard_map/ppermute | solution.py:25
  1.4 0.1 pad_add_fusion.place_ref
  1.5 1.6 %fetch.1 = (bf16[4,2,128,128]{3,2,1,0:T(8,128)(2,1)S(1)}, bf16[128,8,128]{2,1,0:T(8,128)(2,1)S(1)}) custom-call(s32[2]{0:T(128)S(1)} %pad_add_fusion.place_ref, bf16[128,8,128]{2,1,0:T(8,128)(2,1)} %key_ref.1, bf16[128,8,128]{2,1,0:T(8,128)(2,1)} %refs_0_.1), custom_call_target="tpu_custom_call" | custom-call | flops 1000000000 | tf_op jit(solution)/shard_map/fetch/pallas_call | solution.py:38
  3.1 0.6 %pack_other.1.refs_0_ = bf16[4,2,128,128]{3,2,1,0:T(8,128)(2,1)S(1)} custom-call(s32[2]{0:T(128)S(1)} %pad_add_fusion.place_ref, bf16[128,8,128]{2,1,0:T(8,128)(2,1)S(1)} %collective-permute-done.other_ref, bf16[4,2,128,128]{3,2,1,0:T(8,128)(2,1)S(1)} %get-tuple-element.28._), custom_call_target="tpu_custom_call", output_to_operand_aliasing={{}: (2, {})} | custom-call | flops 1000000000 | tf_op jit(solution)/shard_map/pack_other/pallas_call | solution.py:38
  3.7 0.0 copy-start.2
  3.7 0.1 collective-permute-start.1
  3.9 0.4 collective-permute-start.2
  4.3 0.1 collective-permute-start.3
  4.4 3.1 %collective-permute-start.5 = (bf16[4,2,128,128]{3,2,1,0:T(8,128)(2,1)S(1)}, bf16[4,2,128,128]{3,2,1,0:T(8,128)(2,1)S(1)}, u32[]{:S(2)}, u32[]{:S(2)}) collective-permute-start(bf16[4,2,128,128]{3,2,1,0:T(8,128)(2,1)S(1)} %pack_other.1.refs_0_), channel_id=1, source_target_pairs={{0,4},{1,5},{2,6},{3,7},{4,8},{5,9},{6,10},{7,11},{8,12},{9,13},{1... | collective-permute-start | bytes 786440 | tf_op jit(solution)/shard_map/ppermute | solution.py:21
  7.5 3.1 %collective-permute-start.4 = (bf16[4,2,128,128]{3,2,1,0:T(8,128)(2,1)S(1)}, bf16[4,2,128,128]{3,2,1,0:T(8,128)(2,1)S(1)}, u32[]{:S(2)}, u32[]{:S(2)}) collective-permute-start(bf16[4,2,128,128]{3,2,1,0:T(8,128)(2,1)S(1)} %pack_other.1.refs_0_), channel_id=1, source_target_pairs={{0,2},{1,3},{2,4},{3,5},{4,6},{5,7},{6,8},{7,9},{8,10},{9,11},{10,... | collective-permute-start | bytes 786440 | tf_op jit(solution)/shard_map/ppermute | solution.py:21
  10.7 2.0 %arrange.1.qd_ref = bf16[4,2,2,4,128,128]{5,4,3,2,1,0:T(8,128)(2,1)S(1)} custom-call(s32[2]{0:T(128)S(1)} %pad_add_fusion.place_ref, bf16[128,32,128]{2,1,0:T(8,128)(2,1)S(1)} %copy-done, bf16[128,32,128]{2,1,0:T(8,128)(2,1)S(1)} %copy-done.1, bf16[128,32,128]{2,1,0:T(8,128)(2,1)S(1)} %collective-permute-done.1.q_other_ref, ...), custom_call_target="tpu_custom_call" | custom-call | flops 1000000000 | tf_op jit(solution)/shard_map/arrange/pallas_call | solution.py:38
  12.7 0.7 %pack_both.1.refs_0_ = bf16[4,2,128,128]{3,2,1,0:T(8,128)(2,1)S(1)} custom-call(s32[2]{0:T(128)S(1)} %pad_add_fusion.place_ref, bf16[128,8,128]{2,1,0:T(8,128)(2,1)S(1)} %get-tuple-element.36.own_ref, bf16[128,8,128]{2,1,0:T(8,128)(2,1)S(1)} %collective-permute-done.3.other_ref), custom_call_target="tpu_custom_call" | custom-call | flops 1000000000 | tf_op jit(solution)/shard_map/pack_both/pallas_call | solution.py:38
  13.4 1.9 %collective-permute-start.7 = (bf16[4,2,128,128]{3,2,1,0:T(8,128)(2,1)S(1)}, bf16[4,2,128,128]{3,2,1,0:T(8,128)(2,1)S(1)}, u32[]{:S(2)}, u32[]{:S(2)}) collective-permute-start(bf16[4,2,128,128]{3,2,1,0:T(8,128)(2,1)S(1)} %pack_both.1.refs_0_), channel_id=1, source_target_pairs={{0,4},{1,5},{2,6},{3,7},{4,8},{5,9},{6,10},{7,11},{8,12},{9,13},{1... | collective-permute-start | bytes 786440 | tf_op jit(solution)/shard_map/ppermute | solution.py:21
  15.4 3.1 %collective-permute-start.6 = (bf16[4,2,128,128]{3,2,1,0:T(8,128)(2,1)S(1)}, bf16[4,2,128,128]{3,2,1,0:T(8,128)(2,1)S(1)}, u32[]{:S(2)}, u32[]{:S(2)}) collective-permute-start(bf16[4,2,128,128]{3,2,1,0:T(8,128)(2,1)S(1)} %pack_both.1.refs_0_), channel_id=1, source_target_pairs={{0,2},{1,3},{2,4},{3,5},{4,6},{5,7},{6,8},{7,9},{8,10},{9,11},{10,... | collective-permute-start | bytes 786440 | tf_op jit(solution)/shard_map/ppermute | solution.py:21
  18.5 0.0 collective-permute-done.5.refs_2_
  18.5 6.5 %prob.1 = (bf16[4,2,640,512]{3,2,1,0:T(8,128)(2,1)S(1)}, bf16[4,2,128,128]{3,2,1,0:T(8,128)(2,1)S(1)}, bf16[4,2,128,128]{3,2,1,0:T(8,128)(2,1)S(1)}) custom-call(s32[2]{0:T(128)S(1)} %pad_add_fusion.place_ref, s32[16]{0:T(128)S(1)} %copy-done.2, bf16[4,2,2,4,128,128]{5,4,3,2,1,0:T(8,128)(2,1)S(1)} %arrange.1.qd_ref, ...), custom_call_target="tpu_custom_call" | custom-call | flops 2684354560 | tf_op jit(solution)/shard_map/prob/pallas_call | solution.py:38
  25.0 3.4 %collective-permute-start.8 = (bf16[4,2,128,128]{3,2,1,0:T(8,128)(2,1)S(1)}, bf16[4,2,128,128]{3,2,1,0:T(8,128)(2,1)S(1)}, u32[]{:S(2)}, u32[]{:S(2)}) collective-permute-start(bf16[4,2,128,128]{3,2,1,0:T(8,128)(2,1)S(1)} %get-tuple-element.39), channel_id=1, source_target_pairs={{4,0},{5,1},{6,2},{7,3},{8,4},{9,5},{10,6},{11,7},{12,8},{13,9},{1... | collective-permute-start | bytes 786440 | tf_op jit(solution)/shard_map/ppermute | solution.py:21
  28.4 5.2 %collective-permute-start.9 = (bf16[4,2,128,128]{3,2,1,0:T(8,128)(2,1)S(1)}, bf16[4,2,128,128]{3,2,1,0:T(8,128)(2,1)S(1)}, u32[]{:S(2)}, u32[]{:S(2)}) collective-permute-start(bf16[4,2,128,128]{3,2,1,0:T(8,128)(2,1)S(1)} %get-tuple-element.40), channel_id=1, source_target_pairs={{2,0},{3,1},{4,2},{5,3},{6,4},{7,5},{8,6},{9,7},{10,8},{11,9},{12,... | collective-permute-start | bytes 786440 | tf_op jit(solution)/shard_map/ppermute | solution.py:21
  33.6 5.6 %dscore.1 = (bf16[4,2,640,512]{3,2,1,0:T(8,128)(2,1)S(1)}, bf16[4,2,128,128]{3,2,1,0:T(8,128)(2,1)S(1)}, bf16[4,2,128,128]{3,2,1,0:T(8,128)(2,1)S(1)}) custom-call(s32[2]{0:T(128)S(1)} %pad_add_fusion.place_ref, bf16[4,2,2,4,128,128]{5,4,3,2,1,0:T(8,128)(2,1)S(1)} %arrange.1.qd_ref, bf16[4,2,640,512]{3,2,1,0:T(8,128)(2,1)S(1)} %get-tuple-element.35.p_ref, ...), custom_call_target="tpu_custom_call" | custom-call | flops 2684354560 | tf_op jit(solution)/shard_map/dscore/pallas_call | solution.py:38
  39.2 1.9 %collective-permute-start.13 = (bf16[4,2,128,128]{3,2,1,0:T(8,128)(2,1)S(1)}, bf16[4,2,128,128]{3,2,1,0:T(8,128)(2,1)S(1)}, u32[]{:S(2)}, u32[]{:S(2)}) collective-permute-start(bf16[4,2,128,128]{3,2,1,0:T(8,128)(2,1)S(1)} %get-tuple-element.48), channel_id=1, source_target_pairs={{4,0},{5,1},{6,2},{7,3},{8,4},{9,5},{10,6},{11,7},{12,8},{13,9},{1... | collective-permute-start | bytes 786440 | tf_op jit(solution)/shard_map/ppermute | solution.py:21
  41.2 1.9 %collective-permute-start.14 = (bf16[4,2,128,128]{3,2,1,0:T(8,128)(2,1)S(1)}, bf16[4,2,128,128]{3,2,1,0:T(8,128)(2,1)S(1)}, u32[]{:S(2)}, u32[]{:S(2)}) collective-permute-start(bf16[4,2,128,128]{3,2,1,0:T(8,128)(2,1)S(1)} %get-tuple-element.49), channel_id=1, source_target_pairs={{2,0},{3,1},{4,2},{5,3},{6,4},{7,5},{8,6},{9,7},{10,8},{11,9},{12,... | collective-permute-start | bytes 786440 | tf_op jit(solution)/shard_map/ppermute | solution.py:21
  43.1 0.3 collective-permute-done.9.refs_4_
  43.4 3.3 %own.1 = (bf16[128,16,128]{2,1,0:T(8,128)(2,1)S(1)}, bf16[56,16,128]{2,1,0:T(8,128)(2,1)S(1)}, bf16[56,16,128]{2,1,0:T(8,128)(2,1)S(1)}, bf16[48,16,128]{2,1,0:T...) custom-call(s32[2]{0:T(128)S(1)} %pad_add_fusion.place_ref, ...), custom_call_target="tpu_custom_call" | custom-call | tf_op jit(solution)/shard_map/own/pallas_call | solution.py:38
  46.7 5.2 %collective-permute-start.10 = (bf16[56,16,128]{2,1,0:T(8,128)(2,1)S(1)}, bf16[56,16,128]{2,1,0:T(8,128)(2,1)S(1)}, u32[]{:S(2)}, u32[]{:S(2)}) collective-permute-start(bf16[56,16,128]{2,1,0:T(8,128)(2,1)S(1)} %get-tuple-element.43), channel_id=1, source_target_pairs={{0,1},{1,0},{2,3},{3,2},{4,5},{5,4},{6,7},{7,6},{8,9},{9,8},{10,11... | collective-permute-start | bytes 688136 | tf_op jit(solution)/shard_map/ppermute | solution.py:25
  51.9 0.1 collective-permute-start.11
  52.0 0.4 collective-permute-start.12
  52.4 1.3 %collective-permute-done.12.refs_2_ = bf16[48,16,128]{2,1,0:T(8,128)(2,1)S(1)} collective-permute-done((bf16[48,16,128]{2,1,0:T(8,128)(2,1)S(1)}, bf16[48,16,128]{2,1,0:T(8,128)(2,1)S(1)}, u32[]{:S(2)}, u32[]{:S(2)}) %collective-permute-start.12) | collective-permute-done | bytes 196640 | tf_op jit(solution)/shard_map/ppermute | solution.py:25
  53.7 2.2 %join.1 = (bf16[128,32,128]{2,1,0:T(8,128)(2,1)}, bf16[128,8,128]{2,1,0:T(8,128)(2,1)}) custom-call(s32[2]{0:T(128)S(1)} %pad_add_fusion.place_ref, bf16[128,16,128]{2,1,0:T(8,128)(2,1)S(1)} %get-tuple-element.41.dq_ref, bf16[4,128,128]{2,1,0:T(8,128)(2,1)S(1)} %get-tuple-element.42.dv_ref, bf16[56,16,128]{2,1,0:T(8,128)(2,1)S(1)} %collective-permute-done.10.refs_0_, ...), custom_call_target="tpu_custom_call" | custom-call | tf_op jit(solution)/shard_map/join/pallas_call | solution.py:38
  55.9 0.6 %sum_dk.1 = (bf16[4,128,128]{2,1,0:T(8,128)(2,1)S(1)}, bf16[4,128,128]{2,1,0:T(8,128)(2,1)S(1)}) custom-call(s32[2]{0:T(128)S(1)} %pad_add_fusion.place_ref, f32[4,2,128,128]{3,2,1,0:T(8,128)S(1)} %get-tuple-element.47.own_ref, bf16[4,2,128,128]{3,2,1,0:T(8,128)(2,1)S(1)} %collective-permute-done.13.refs_0_, ...), custom_call_target="tpu_custom_call" | custom-call | tf_op jit(solution)/shard_map/sum_dk/pallas_call | solution.py:38
  56.6 1.8 %collective-permute-start.15 = (bf16[4,128,128]{2,1,0:T(8,128)(2,1)S(1)}, bf16[4,128,128]{2,1,0:T(8,128)(2,1)S(1)}, u32[]{:S(2)}, u32[]{:S(2)}) collective-permute-start(bf16[4,128,128]{2,1,0:T(8,128)(2,1)S(1)} %get-tuple-element.52), channel_id=1, source_target_pairs={{0,1},{1,0},{2,3},{3,2},{4,5},{5,4},{6,7},{7,6},{8,9},{9,8},{10,11... | collective-permute-start | bytes 393224 | tf_op jit(solution)/shard_map/ppermute | solution.py:25
  58.3 1.0 %collective-permute-done.15.other_ref = bf16[4,128,128]{2,1,0:T(8,128)(2,1)S(1)} collective-permute-done((bf16[4,128,128]{2,1,0:T(8,128)(2,1)S(1)}, bf16[4,128,128]{2,1,0:T(8,128)(2,1)S(1)}, u32[]{:S(2)}, u32[]{:S(2)}) %collective-permute-start.15) | collective-permute-done | bytes 131104 | tf_op jit(solution)/shard_map/ppermute | solution.py:25
  59.3 1.4 %merge_dk.1 = bf16[128,8,128]{2,1,0:T(8,128)(2,1)} custom-call(s32[2]{0:T(128)S(1)} %pad_add_fusion.place_ref, bf16[4,128,128]{2,1,0:T(8,128)(2,1)S(1)} %get-tuple-element.51.own_ref, bf16[4,128,128]{2,1,0:T(8,128)(2,1)S(1)} %collective-permute-done.15.other_ref), custom_call_target="tpu_custom_call" | custom-call | tf_op jit(solution)/shard_map/merge_dk/pallas_call | solution.py:38
  (17 shorter events, 0.0 us)
Async XLA Ops:
  0.6 3.2 %copy-start.1 = (bf16[128,32,128]{2,1,0:T(8,128)(2,1)S(1)}, bf16[128,32,128]{2,1,0:T(8,128)(2,1)}, u32[]{:S(2)}) copy-start(bf16[128,32,128]{2,1,0:T(8,128)(2,1)} %do_ref) | copy-start | bytes 3145732
  0.6 3.1 %copy-start = (bf16[128,32,128]{2,1,0:T(8,128)(2,1)S(1)}, bf16[128,32,128]{2,1,0:T(8,128)(2,1)}, u32[]{:S(2)}) copy-start(bf16[128,32,128]{2,1,0:T(8,128)(2,1)} %q_ref) | copy-start | bytes 3145732
  0.6 2.4 %collective-permute-start = (bf16[128,8,128]{2,1,0:T(8,128)(2,1)}, bf16[128,8,128]{2,1,0:T(8,128)(2,1)S(1)}, u32[]{:S(2)}, u32[]{:S(2)}) collective-permute-start(bf16[128,8,128]{2,1,0:T(8,128)(2,1)} %key_ref.1), channel_id=1, source_target_pairs={{0,1},{1,0},{2,3},{3,2},{4,5},{5,4},{6,7},{7,6},{8,9},{9,8},{10,11... | collective-permute-start | bytes 786440 | tf_op jit(solution)/shard_map/ppermute | solution.py:25
  3.7 14.8 %copy-start.2 = (s32[16]{0:T(128)S(1)}, s32[16]{0:T(128)}, u32[]{:S(2)}) copy-start(s32[16]{0:T(128)} %lengths_ref.1) | copy-start | bytes 196
  3.7 6.9 %collective-permute-start.1 = (bf16[128,32,128]{2,1,0:T(8,128)(2,1)S(1)}, bf16[128,32,128]{2,1,0:T(8,128)(2,1)S(1)}, u32[]{:S(2)}, u32[]{:S(2)}) collective-permute-start(bf16[128,32,128]{2,1,0:T(8,128)(2,1)S(1)} %copy-done), channel_id=1, source_target_pairs={{0,1},{1,0},{2,3},{3,2},{4,5},{5,4},{6,7},{7,6},{8,9},{9,8},{10,11... | collective-permute-start | bytes 3145736 | tf_op jit(solution)/shard_map/ppermute | solution.py:25
  3.9 6.8 %collective-permute-start.2 = (bf16[128,32,128]{2,1,0:T(8,128)(2,1)S(1)}, bf16[128,32,128]{2,1,0:T(8,128)(2,1)S(1)}, u32[]{:S(2)}, u32[]{:S(2)}) collective-permute-start(bf16[128,32,128]{2,1,0:T(8,128)(2,1)S(1)} %copy-done.1), channel_id=1, source_target_pairs={{0,1},{1,0},{2,3},{3,2},{4,5},{5,4},{6,7},{7,6},{8,9},{9,8},{10,11... | collective-permute-start | bytes 3145736 | tf_op jit(solution)/shard_map/ppermute | solution.py:25
  4.3 8.4 %collective-permute-start.3 = (bf16[128,8,128]{2,1,0:T(8,128)(2,1)S(1)}, bf16[128,8,128]{2,1,0:T(8,128)(2,1)S(1)}, u32[]{:S(2)}, u32[]{:S(2)}) collective-permute-start(bf16[128,8,128]{2,1,0:T(8,128)(2,1)S(1)} %get-tuple-element.36.own_ref), channel_id=1, source_target_pairs={{0,1},{1,0},{2,3},{3,2},{4,5},{5,4},{6,7},{7,6},{8,9},{9,8},{10,11... | collective-permute-start | bytes 786440 | tf_op jit(solution)/shard_map/ppermute | solution.py:25
  4.4 14.1 %collective-permute-start.5 = (bf16[4,2,128,128]{3,2,1,0:T(8,128)(2,1)S(1)}, bf16[4,2,128,128]{3,2,1,0:T(8,128)(2,1)S(1)}, u32[]{:S(2)}, u32[]{:S(2)}) collective-permute-start(bf16[4,2,128,128]{3,2,1,0:T(8,128)(2,1)S(1)} %pack_other.1.refs_0_), channel_id=1, source_target_pairs={{0,4},{1,5},{2,6},{3,7},{4,8},{5,9},{6,10},{7,11},{8,12},{9,13},{1... | collective-permute-start | bytes 786440 | tf_op jit(solution)/shard_map/ppermute | solution.py:21
  7.5 11.0 %collective-permute-start.4 = (bf16[4,2,128,128]{3,2,1,0:T(8,128)(2,1)S(1)}, bf16[4,2,128,128]{3,2,1,0:T(8,128)(2,1)S(1)}, u32[]{:S(2)}, u32[]{:S(2)}) collective-permute-start(bf16[4,2,128,128]{3,2,1,0:T(8,128)(2,1)S(1)} %pack_other.1.refs_0_), channel_id=1, source_target_pairs={{0,2},{1,3},{2,4},{3,5},{4,6},{5,7},{6,8},{7,9},{8,10},{9,11},{10,... | collective-permute-start | bytes 786440 | tf_op jit(solution)/shard_map/ppermute | solution.py:21
  13.4 20.2 %collective-permute-start.7 = (bf16[4,2,128,128]{3,2,1,0:T(8,128)(2,1)S(1)}, bf16[4,2,128,128]{3,2,1,0:T(8,128)(2,1)S(1)}, u32[]{:S(2)}, u32[]{:S(2)}) collective-permute-start(bf16[4,2,128,128]{3,2,1,0:T(8,128)(2,1)S(1)} %pack_both.1.refs_0_), channel_id=1, source_target_pairs={{0,4},{1,5},{2,6},{3,7},{4,8},{5,9},{6,10},{7,11},{8,12},{9,13},{1... | collective-permute-start | bytes 786440 | tf_op jit(solution)/shard_map/ppermute | solution.py:21
  15.4 18.2 %collective-permute-start.6 = (bf16[4,2,128,128]{3,2,1,0:T(8,128)(2,1)S(1)}, bf16[4,2,128,128]{3,2,1,0:T(8,128)(2,1)S(1)}, u32[]{:S(2)}, u32[]{:S(2)}) collective-permute-start(bf16[4,2,128,128]{3,2,1,0:T(8,128)(2,1)S(1)} %pack_both.1.refs_0_), channel_id=1, source_target_pairs={{0,2},{1,3},{2,4},{3,5},{4,6},{5,7},{6,8},{7,9},{8,10},{9,11},{10,... | collective-permute-start | bytes 786440 | tf_op jit(solution)/shard_map/ppermute | solution.py:21
  25.0 18.1 %collective-permute-start.8 = (bf16[4,2,128,128]{3,2,1,0:T(8,128)(2,1)S(1)}, bf16[4,2,128,128]{3,2,1,0:T(8,128)(2,1)S(1)}, u32[]{:S(2)}, u32[]{:S(2)}) collective-permute-start(bf16[4,2,128,128]{3,2,1,0:T(8,128)(2,1)S(1)} %get-tuple-element.39), channel_id=1, source_target_pairs={{4,0},{5,1},{6,2},{7,3},{8,4},{9,5},{10,6},{11,7},{12,8},{13,9},{1... | collective-permute-start | bytes 786440 | tf_op jit(solution)/shard_map/ppermute | solution.py:21
  28.4 15.0 %collective-permute-start.9 = (bf16[4,2,128,128]{3,2,1,0:T(8,128)(2,1)S(1)}, bf16[4,2,128,128]{3,2,1,0:T(8,128)(2,1)S(1)}, u32[]{:S(2)}, u32[]{:S(2)}) collective-permute-start(bf16[4,2,128,128]{3,2,1,0:T(8,128)(2,1)S(1)} %get-tuple-element.40), channel_id=1, source_target_pairs={{2,0},{3,1},{4,2},{5,3},{6,4},{7,5},{8,6},{9,7},{10,8},{11,9},{12,... | collective-permute-start | bytes 786440 | tf_op jit(solution)/shard_map/ppermute | solution.py:21
  39.2 16.7 %collective-permute-start.13 = (bf16[4,2,128,128]{3,2,1,0:T(8,128)(2,1)S(1)}, bf16[4,2,128,128]{3,2,1,0:T(8,128)(2,1)S(1)}, u32[]{:S(2)}, u32[]{:S(2)}) collective-permute-start(bf16[4,2,128,128]{3,2,1,0:T(8,128)(2,1)S(1)} %get-tuple-element.48), channel_id=1, source_target_pairs={{4,0},{5,1},{6,2},{7,3},{8,4},{9,5},{10,6},{11,7},{12,8},{13,9},{1... | collective-permute-start | bytes 786440 | tf_op jit(solution)/shard_map/ppermute | solution.py:21
  41.2 14.8 %collective-permute-start.14 = (bf16[4,2,128,128]{3,2,1,0:T(8,128)(2,1)S(1)}, bf16[4,2,128,128]{3,2,1,0:T(8,128)(2,1)S(1)}, u32[]{:S(2)}, u32[]{:S(2)}) collective-permute-start(bf16[4,2,128,128]{3,2,1,0:T(8,128)(2,1)S(1)} %get-tuple-element.49), channel_id=1, source_target_pairs={{2,0},{3,1},{4,2},{5,3},{6,4},{7,5},{8,6},{9,7},{10,8},{11,9},{12,... | collective-permute-start | bytes 786440 | tf_op jit(solution)/shard_map/ppermute | solution.py:21
  46.7 6.9 %collective-permute-start.10 = (bf16[56,16,128]{2,1,0:T(8,128)(2,1)S(1)}, bf16[56,16,128]{2,1,0:T(8,128)(2,1)S(1)}, u32[]{:S(2)}, u32[]{:S(2)}) collective-permute-start(bf16[56,16,128]{2,1,0:T(8,128)(2,1)S(1)} %get-tuple-element.43), channel_id=1, source_target_pairs={{0,1},{1,0},{2,3},{3,2},{4,5},{5,4},{6,7},{7,6},{8,9},{9,8},{10,11... | collective-permute-start | bytes 688136 | tf_op jit(solution)/shard_map/ppermute | solution.py:25
  51.9 1.8 %collective-permute-start.11 = (bf16[56,16,128]{2,1,0:T(8,128)(2,1)S(1)}, bf16[56,16,128]{2,1,0:T(8,128)(2,1)S(1)}, u32[]{:S(2)}, u32[]{:S(2)}) collective-permute-start(bf16[56,16,128]{2,1,0:T(8,128)(2,1)S(1)} %get-tuple-element.44), channel_id=1, source_target_pairs={{0,1},{1,0},{2,3},{3,2},{4,5},{5,4},{6,7},{7,6},{8,9},{9,8},{10,11... | collective-permute-start | bytes 688136 | tf_op jit(solution)/shard_map/ppermute | solution.py:25
  52.0 1.7 %collective-permute-start.12 = (bf16[48,16,128]{2,1,0:T(8,128)(2,1)S(1)}, bf16[48,16,128]{2,1,0:T(8,128)(2,1)S(1)}, u32[]{:S(2)}, u32[]{:S(2)}) collective-permute-start(bf16[48,16,128]{2,1,0:T(8,128)(2,1)S(1)} %get-tuple-element.45), channel_id=1, source_target_pairs={{0,1},{1,0},{2,3},{3,2},{4,5},{5,4},{6,7},{7,6},{8,9},{9,8},{10,11... | collective-permute-start | bytes 589832 | tf_op jit(solution)/shard_map/ppermute | solution.py:25
  56.6 2.8 %collective-permute-start.15 = (bf16[4,128,128]{2,1,0:T(8,128)(2,1)S(1)}, bf16[4,128,128]{2,1,0:T(8,128)(2,1)S(1)}, u32[]{:S(2)}, u32[]{:S(2)}) collective-permute-start(bf16[4,128,128]{2,1,0:T(8,128)(2,1)S(1)} %get-tuple-element.52), channel_id=1, source_target_pairs={{0,1},{1,0},{2,3},{3,2},{4,5},{5,4},{6,7},{7,6},{8,9},{9,8},{10,11... | collective-permute-start | bytes 393224 | tf_op jit(solution)/shard_map/ppermute | solution.py:25

commit v18 on v17

--- a/solution.py
+++ b/solution.py
@@ -196,9 +196,8 @@
 
 
 def window_of(pair_refs, scr):
-    halo = len(pair_refs) - 1
-    for back, ref in enumerate(pair_refs):
-        scr[pl.ds(2 * (halo - back), 2)] = ref[0]
+    for i, ref in enumerate(pair_refs):
+        scr[pl.ds(2 * i, 2)] = ref[0]
 
 
 def on_diagonal(tokens, copies):
@@ -451,7 +450,7 @@
     window, count = 2 * halo + 2, 2 * halo + 1
     place = jnp.stack([core, (device // 2 - halo) * (2 * tokens)]).astype(jnp.int32)
 
-    far_first = range(halo, 0, -1)
+    near_first = range(1, halo + 1)
     k_other = swapped(keys, device_count)
     k_mine, v_mine = fetch(place, keys, (values,))
     k_own = pack_other(place, k_other, k_mine)
@@ -462,11 +461,11 @@
     v_own = pack_both(place, v_mine, v_other)
 
     def halo_of(own):
-        received = {back: moved(own, device_count, 2 * back) for back in far_first}
-        return [own] + [received[back] for back in range(1, halo + 1)]
+        received = {back: moved(own, device_count, 2 * back) for back in near_first}
+        return [received[back] for back in range(halo, 0, -1)] + [own]
 
     def sent_back(partials):
-        return [moved(partials[back - 1], device_count, -2 * back) for back in far_first]
+        return [moved(partials[back - 1], device_count, -2 * back) for back in near_first]
 
     def per_head(*shape):
         return pl.BlockSpec((1,) + shape, lambda h, *_: (h,) + (0,) * len(shape))

time: 61 us -> 66 us (1.082)
  the two profiles are of different devices: /device:TPU:23 before, /device:TPU:3 now
where the time goes in v18:
time: 66 us; the launch traced here: 65.7 us
  starting transfers between devices  28.1 us (43%)
  Pallas kernels  24.6 us (37%)
  waiting for transfers between devices  12.1 us (18%)
  between operations  0.89 us (1%)
    ppermute x8, starting transfers between devices, moved(): return lax.ppermute(array, AXES, pairs)  25.1 us
    pallas_call x10, Pallas kernels, call(): pl.pallas_call(kernel, out_shape=outs, grid_spec=pltpu.PrefetchScalarGrid...  24.6 us
    ppermute x8, waiting for transfers between devices, moved(): return lax.ppermute(array, AXES, pairs)  9.76 us
    ppermute x8, starting transfers between devices, swapped(): return lax.ppermute(array, AXES, [(d, d ^ 1) for d in range(device_count)])  2.97 us
    ppermute x8, waiting for transfers between devices, swapped(): return lax.ppermute(array, AXES, [(d, d ^ 1) for d in range(device_count)])  2.3 us
  transfers between devices with their start and end apart: 16, of which 3 were waited for; matrix products, arithmetic and copies ran while one was open for 0% of the time, Pallas kernels for 33%

profile of v18, /device:TPU:3, one launch (start us, length us, event | category | flops | bytes accessed | tf_op | source)
XLA Modules:
  0.0 65.7 jit_solution(12490915502579839998)
XLA Ops:
  0.6 0.7 %collective-permute-start = (bf16[128,8,128]{2,1,0:T(8,128)(2,1)}, bf16[128,8,128]{2,1,0:T(8,128)(2,1)S(1)}, u32[]{:S(2)}, u32[]{:S(2)}) collective-permute-start(bf16[128,8,128]{2,1,0:T(8,128)(2,1)} %key_ref.1), channel_id=1, source_target_pairs={{0,1},{1,0},{2,3},{3,2},{4,5},{5,4},{6,7},{7,6},{8,9},{9,8},{10,11... | collective-permute-start | bytes 786440 | tf_op jit(solution)/shard_map/ppermute | solution.py:25
  1.4 0.1 pad_add_fusion.place_ref
  1.5 1.6 %fetch.1 = (bf16[4,2,128,128]{3,2,1,0:T(8,128)(2,1)S(1)}, bf16[128,8,128]{2,1,0:T(8,128)(2,1)S(1)}) custom-call(s32[2]{0:T(128)S(1)} %pad_add_fusion.place_ref, bf16[128,8,128]{2,1,0:T(8,128)(2,1)} %key_ref.1, bf16[128,8,128]{2,1,0:T(8,128)(2,1)} %refs_0_.1), custom_call_target="tpu_custom_call" | custom-call | flops 1000000000 | tf_op jit(solution)/shard_map/fetch/pallas_call | solution.py:38
  3.1 0.0 collective-permute-done.other_ref
  3.1 0.6 pack_other.1.refs_2_
  3.7 0.0 copy-start.2
  3.7 0.1 collective-permute-start.1
  3.9 0.4 collective-permute-start.2
  4.3 0.1 collective-permute-start.3
  4.4 3.1 %collective-permute-start.5 = (bf16[4,2,128,128]{3,2,1,0:T(8,128)(2,1)S(1)}, bf16[4,2,128,128]{3,2,1,0:T(8,128)(2,1)S(1)}, u32[]{:S(2)}, u32[]{:S(2)}) collective-permute-start(bf16[4,2,128,128]{3,2,1,0:T(8,128)(2,1)S(1)} %pack_other.1.refs_2_), channel_id=1, source_target_pairs={{0,2},{1,3},{2,4},{3,5},{4,6},{5,7},{6,8},{7,9},{8,10},{9,11},{10,... | collective-permute-start | bytes 786440 | tf_op jit(solution)/shard_map/ppermute | solution.py:21
  7.5 3.2 %collective-permute-start.4 = (bf16[4,2,128,128]{3,2,1,0:T(8,128)(2,1)S(1)}, bf16[4,2,128,128]{3,2,1,0:T(8,128)(2,1)S(1)}, u32[]{:S(2)}, u32[]{:S(2)}) collective-permute-start(bf16[4,2,128,128]{3,2,1,0:T(8,128)(2,1)S(1)} %pack_other.1.refs_2_), channel_id=1, source_target_pairs={{0,4},{1,5},{2,6},{3,7},{4,8},{5,9},{6,10},{7,11},{8,12},{9,13},{1... | collective-permute-start | bytes 786440 | tf_op jit(solution)/shard_map/ppermute | solution.py:21
  10.7 2.0 %arrange.1.qd_ref = bf16[4,2,2,4,128,128]{5,4,3,2,1,0:T(8,128)(2,1)S(1)} custom-call(s32[2]{0:T(128)S(1)} %pad_add_fusion.place_ref, bf16[128,32,128]{2,1,0:T(8,128)(2,1)S(1)} %copy-done, bf16[128,32,128]{2,1,0:T(8,128)(2,1)S(1)} %copy-done.1, bf16[128,32,128]{2,1,0:T(8,128)(2,1)S(1)} %collective-permute-done.1.q_other_ref, ...), custom_call_target="tpu_custom_call" | custom-call | flops 1000000000 | tf_op jit(solution)/shard_map/arrange/pallas_call | solution.py:38
  12.7 0.7 %pack_both.1.refs_2_ = bf16[4,2,128,128]{3,2,1,0:T(8,128)(2,1)S(1)} custom-call(s32[2]{0:T(128)S(1)} %pad_add_fusion.place_ref, bf16[128,8,128]{2,1,0:T(8,128)(2,1)S(1)} %get-tuple-element.36.own_ref, bf16[128,8,128]{2,1,0:T(8,128)(2,1)S(1)} %collective-permute-done.3.other_ref), custom_call_target="tpu_custom_call" | custom-call | flops 1000000000 | tf_op jit(solution)/shard_map/pack_both/pallas_call | solution.py:38
  13.5 3.1 %collective-permute-start.7 = (bf16[4,2,128,128]{3,2,1,0:T(8,128)(2,1)S(1)}, bf16[4,2,128,128]{3,2,1,0:T(8,128)(2,1)S(1)}, u32[]{:S(2)}, u32[]{:S(2)}) collective-permute-start(bf16[4,2,128,128]{3,2,1,0:T(8,128)(2,1)S(1)} %pack_both.1.refs_2_), channel_id=1, source_target_pairs={{0,2},{1,3},{2,4},{3,5},{4,6},{5,7},{6,8},{7,9},{8,10},{9,11},{10,... | collective-permute-start | bytes 786440 | tf_op jit(solution)/shard_map/ppermute | solution.py:21
  16.6 3.2 %collective-permute-start.6 = (bf16[4,2,128,128]{3,2,1,0:T(8,128)(2,1)S(1)}, bf16[4,2,128,128]{3,2,1,0:T(8,128)(2,1)S(1)}, u32[]{:S(2)}, u32[]{:S(2)}) collective-permute-start(bf16[4,2,128,128]{3,2,1,0:T(8,128)(2,1)S(1)} %pack_both.1.refs_2_), channel_id=1, source_target_pairs={{0,4},{1,5},{2,6},{3,7},{4,8},{5,9},{6,10},{7,11},{8,12},{9,13},{1... | collective-permute-start | bytes 786440 | tf_op jit(solution)/shard_map/ppermute | solution.py:21
  19.8 6.5 %prob.1 = (bf16[4,2,640,512]{3,2,1,0:T(8,128)(2,1)S(1)}, bf16[4,2,128,128]{3,2,1,0:T(8,128)(2,1)S(1)}, bf16[4,2,128,128]{3,2,1,0:T(8,128)(2,1)S(1)}) custom-call(s32[2]{0:T(128)S(1)} %pad_add_fusion.place_ref, s32[16]{0:T(128)S(1)} %copy-done.2, bf16[4,2,2,4,128,128]{5,4,3,2,1,0:T(8,128)(2,1)S(1)} %arrange.1.qd_ref, ...), custom_call_target="tpu_custom_call" | custom-call | flops 2684354560 | tf_op jit(solution)/shard_map/prob/pallas_call | solution.py:38
  26.2 8.1 %collective-permute-start.8 = (bf16[4,2,128,128]{3,2,1,0:T(8,128)(2,1)S(1)}, bf16[4,2,128,128]{3,2,1,0:T(8,128)(2,1)S(1)}, u32[]{:S(2)}, u32[]{:S(2)}) collective-permute-start(bf16[4,2,128,128]{3,2,1,0:T(8,128)(2,1)S(1)} %get-tuple-element.39), channel_id=1, source_target_pairs={{2,0},{3,1},{4,2},{5,3},{6,4},{7,5},{8,6},{9,7},{10,8},{11,9},{12,... | collective-permute-start | bytes 786440 | tf_op jit(solution)/shard_map/ppermute | solution.py:21
  34.3 1.3 %collective-permute-start.9 = (bf16[4,2,128,128]{3,2,1,0:T(8,128)(2,1)S(1)}, bf16[4,2,128,128]{3,2,1,0:T(8,128)(2,1)S(1)}, u32[]{:S(2)}, u32[]{:S(2)}) collective-permute-start(bf16[4,2,128,128]{3,2,1,0:T(8,128)(2,1)S(1)} %get-tuple-element.40), channel_id=1, source_target_pairs={{4,0},{5,1},{6,2},{7,3},{8,4},{9,5},{10,6},{11,7},{12,8},{13,9},{1... | collective-permute-start | bytes 786440 | tf_op jit(solution)/shard_map/ppermute | solution.py:21
  35.6 5.6 %dscore.1 = (bf16[4,2,640,512]{3,2,1,0:T(8,128)(2,1)S(1)}, bf16[4,2,128,128]{3,2,1,0:T(8,128)(2,1)S(1)}, bf16[4,2,128,128]{3,2,1,0:T(8,128)(2,1)S(1)}) custom-call(s32[2]{0:T(128)S(1)} %pad_add_fusion.place_ref, bf16[4,2,2,4,128,128]{5,4,3,2,1,0:T(8,128)(2,1)S(1)} %arrange.1.qd_ref, bf16[4,2,640,512]{3,2,1,0:T(8,128)(2,1)S(1)} %get-tuple-element.35.p_ref, ...), custom_call_target="tpu_custom_call" | custom-call | flops 2684354560 | tf_op jit(solution)/shard_map/dscore/pallas_call | solution.py:38
  41.2 1.9 %collective-permute-start.13 = (bf16[4,2,128,128]{3,2,1,0:T(8,128)(2,1)S(1)}, bf16[4,2,128,128]{3,2,1,0:T(8,128)(2,1)S(1)}, u32[]{:S(2)}, u32[]{:S(2)}) collective-permute-start(bf16[4,2,128,128]{3,2,1,0:T(8,128)(2,1)S(1)} %get-tuple-element.48), channel_id=1, source_target_pairs={{2,0},{3,1},{4,2},{5,3},{6,4},{7,5},{8,6},{9,7},{10,8},{11,9},{12,... | collective-permute-start | bytes 786440 | tf_op jit(solution)/shard_map/ppermute | solution.py:21
  43.2 1.3 %collective-permute-start.14 = (bf16[4,2,128,128]{3,2,1,0:T(8,128)(2,1)S(1)}, bf16[4,2,128,128]{3,2,1,0:T(8,128)(2,1)S(1)}, u32[]{:S(2)}, u32[]{:S(2)}) collective-permute-start(bf16[4,2,128,128]{3,2,1,0:T(8,128)(2,1)S(1)} %get-tuple-element.49), channel_id=1, source_target_pairs={{4,0},{5,1},{6,2},{7,3},{8,4},{9,5},{10,6},{11,7},{12,8},{13,9},{1... | collective-permute-start | bytes 786440 | tf_op jit(solution)/shard_map/ppermute | solution.py:21
  44.5 9.7 %collective-permute-done.9.refs_4_ = bf16[4,2,128,128]{3,2,1,0:T(8,128)(2,1)S(1)} collective-permute-done((bf16[4,2,128,128]{3,2,1,0:T(8,128)(2,1)S(1)}, bf16[4,2,128,128]{3,2,1,0:T(8,128)(2,1)S(1)}, u32[]{:S(2)}, u32[]{:S(2)}) %collective-permute-start.9) | collective-permute-done | bytes 262176 | tf_op jit(solution)/shard_map/ppermute | solution.py:21
  54.2 3.3 %own.1 = (bf16[128,16,128]{2,1,0:T(8,128)(2,1)S(1)}, bf16[56,16,128]{2,1,0:T(8,128)(2,1)S(1)}, bf16[56,16,128]{2,1,0:T(8,128)(2,1)S(1)}, bf16[48,16,128]{2,1,0:T...) custom-call(s32[2]{0:T(128)S(1)} %pad_add_fusion.place_ref, ...), custom_call_target="tpu_custom_call" | custom-call | tf_op jit(solution)/shard_map/own/pallas_call | solution.py:38
  57.6 0.7 %collective-permute-start.10 = (bf16[56,16,128]{2,1,0:T(8,128)(2,1)S(1)}, bf16[56,16,128]{2,1,0:T(8,128)(2,1)S(1)}, u32[]{:S(2)}, u32[]{:S(2)}) collective-permute-start(bf16[56,16,128]{2,1,0:T(8,128)(2,1)S(1)} %get-tuple-element.43), channel_id=1, source_target_pairs={{0,1},{1,0},{2,3},{3,2},{4,5},{5,4},{6,7},{7,6},{8,9},{9,8},{10,11... | collective-permute-start | bytes 688136 | tf_op jit(solution)/shard_map/ppermute | solution.py:25
  58.2 0.1 collective-permute-start.11
  58.3 0.4 collective-permute-start.12
  58.7 1.3 %collective-permute-done.12.refs_2_ = bf16[48,16,128]{2,1,0:T(8,128)(2,1)S(1)} collective-permute-done((bf16[48,16,128]{2,1,0:T(8,128)(2,1)S(1)}, bf16[48,16,128]{2,1,0:T(8,128)(2,1)S(1)}, u32[]{:S(2)}, u32[]{:S(2)}) %collective-permute-start.12) | collective-permute-done | bytes 196640 | tf_op jit(solution)/shard_map/ppermute | solution.py:25
  60.0 2.2 %join.1 = (bf16[128,32,128]{2,1,0:T(8,128)(2,1)}, bf16[128,8,128]{2,1,0:T(8,128)(2,1)}) custom-call(s32[2]{0:T(128)S(1)} %pad_add_fusion.place_ref, bf16[128,16,128]{2,1,0:T(8,128)(2,1)S(1)} %get-tuple-element.41.dq_ref, bf16[4,128,128]{2,1,0:T(8,128)(2,1)S(1)} %get-tuple-element.42.dv_ref, bf16[56,16,128]{2,1,0:T(8,128)(2,1)S(1)} %collective-permute-done.10.refs_0_, ...), custom_call_target="tpu_custom_call" | custom-call | tf_op jit(solution)/shard_map/join/pallas_call | solution.py:38
  62.3 0.6 sum_dk.1
  62.9 0.4 collective-permute-start.15
  63.3 1.0 %collective-permute-done.15.other_ref = bf16[4,128,128]{2,1,0:T(8,128)(2,1)S(1)} collective-permute-done((bf16[4,128,128]{2,1,0:T(8,128)(2,1)S(1)}, bf16[4,128,128]{2,1,0:T(8,128)(2,1)S(1)}, u32[]{:S(2)}, u32[]{:S(2)}) %collective-permute-start.15) | collective-permute-done | bytes 131104 | tf_op jit(solution)/shard_map/ppermute | solution.py:25
  64.3 1.4 %merge_dk.1 = bf16[128,8,128]{2,1,0:T(8,128)(2,1)} custom-call(s32[2]{0:T(128)S(1)} %pad_add_fusion.place_ref, bf16[4,128,128]{2,1,0:T(8,128)(2,1)S(1)} %get-tuple-element.51.own_ref, bf16[4,128,128]{2,1,0:T(8,128)(2,1)S(1)} %collective-permute-done.15.other_ref), custom_call_target="tpu_custom_call" | custom-call | tf_op jit(solution)/shard_map/merge_dk/pallas_call | solution.py:38
  (17 shorter events, 0.0 us)
Async XLA Ops:
  0.6 3.2 %copy-start.1 = (bf16[128,32,128]{2,1,0:T(8,128)(2,1)S(1)}, bf16[128,32,128]{2,1,0:T(8,128)(2,1)}, u32[]{:S(2)}) copy-start(bf16[128,32,128]{2,1,0:T(8,128)(2,1)} %do_ref) | copy-start | bytes 3145732
  0.6 3.1 %copy-start = (bf16[128,32,128]{2,1,0:T(8,128)(2,1)S(1)}, bf16[128,32,128]{2,1,0:T(8,128)(2,1)}, u32[]{:S(2)}) copy-start(bf16[128,32,128]{2,1,0:T(8,128)(2,1)} %q_ref) | copy-start | bytes 3145732
  0.6 2.4 %collective-permute-start = (bf16[128,8,128]{2,1,0:T(8,128)(2,1)}, bf16[128,8,128]{2,1,0:T(8,128)(2,1)S(1)}, u32[]{:S(2)}, u32[]{:S(2)}) collective-permute-start(bf16[128,8,128]{2,1,0:T(8,128)(2,1)} %key_ref.1), channel_id=1, source_target_pairs={{0,1},{1,0},{2,3},{3,2},{4,5},{5,4},{6,7},{7,6},{8,9},{9,8},{10,11... | collective-permute-start | bytes 786440 | tf_op jit(solution)/shard_map/ppermute | solution.py:25
  3.7 16.1 %copy-start.2 = (s32[16]{0:T(128)S(1)}, s32[16]{0:T(128)}, u32[]{:S(2)}) copy-start(s32[16]{0:T(128)} %lengths_ref.1) | copy-start | bytes 196
  3.7 7.0 %collective-permute-start.1 = (bf16[128,32,128]{2,1,0:T(8,128)(2,1)S(1)}, bf16[128,32,128]{2,1,0:T(8,128)(2,1)S(1)}, u32[]{:S(2)}, u32[]{:S(2)}) collective-permute-start(bf16[128,32,128]{2,1,0:T(8,128)(2,1)S(1)} %copy-done), channel_id=1, source_target_pairs={{0,1},{1,0},{2,3},{3,2},{4,5},{5,4},{6,7},{7,6},{8,9},{9,8},{10,11... | collective-permute-start | bytes 3145736 | tf_op jit(solution)/shard_map/ppermute | solution.py:25
  3.9 6.8 %collective-permute-start.2 = (bf16[128,32,128]{2,1,0:T(8,128)(2,1)S(1)}, bf16[128,32,128]{2,1,0:T(8,128)(2,1)S(1)}, u32[]{:S(2)}, u32[]{:S(2)}) collective-permute-start(bf16[128,32,128]{2,1,0:T(8,128)(2,1)S(1)} %copy-done.1), channel_id=1, source_target_pairs={{0,1},{1,0},{2,3},{3,2},{4,5},{5,4},{6,7},{7,6},{8,9},{9,8},{10,11... | collective-permute-start | bytes 3145736 | tf_op jit(solution)/shard_map/ppermute | solution.py:25
  4.3 8.4 %collective-permute-start.3 = (bf16[128,8,128]{2,1,0:T(8,128)(2,1)S(1)}, bf16[128,8,128]{2,1,0:T(8,128)(2,1)S(1)}, u32[]{:S(2)}, u32[]{:S(2)}) collective-permute-start(bf16[128,8,128]{2,1,0:T(8,128)(2,1)S(1)} %get-tuple-element.36.own_ref), channel_id=1, source_target_pairs={{0,1},{1,0},{2,3},{3,2},{4,5},{5,4},{6,7},{7,6},{8,9},{9,8},{10,11... | collective-permute-start | bytes 786440 | tf_op jit(solution)/shard_map/ppermute | solution.py:25
  4.4 15.4 %collective-permute-start.5 = (bf16[4,2,128,128]{3,2,1,0:T(8,128)(2,1)S(1)}, bf16[4,2,128,128]{3,2,1,0:T(8,128)(2,1)S(1)}, u32[]{:S(2)}, u32[]{:S(2)}) collective-permute-start(bf16[4,2,128,128]{3,2,1,0:T(8,128)(2,1)S(1)} %pack_other.1.refs_2_), channel_id=1, source_target_pairs={{0,2},{1,3},{2,4},{3,5},{4,6},{5,7},{6,8},{7,9},{8,10},{9,11},{10,... | collective-permute-start | bytes 786440 | tf_op jit(solution)/shard_map/ppermute | solution.py:21
  7.5 12.3 %collective-permute-start.4 = (bf16[4,2,128,128]{3,2,1,0:T(8,128)(2,1)S(1)}, bf16[4,2,128,128]{3,2,1,0:T(8,128)(2,1)S(1)}, u32[]{:S(2)}, u32[]{:S(2)}) collective-permute-start(bf16[4,2,128,128]{3,2,1,0:T(8,128)(2,1)S(1)} %pack_other.1.refs_2_), channel_id=1, source_target_pairs={{0,4},{1,5},{2,6},{3,7},{4,8},{5,9},{6,10},{7,11},{8,12},{9,13},{1... | collective-permute-start | bytes 786440 | tf_op jit(solution)/shard_map/ppermute | solution.py:21
  13.5 22.2 %collective-permute-start.7 = (bf16[4,2,128,128]{3,2,1,0:T(8,128)(2,1)S(1)}, bf16[4,2,128,128]{3,2,1,0:T(8,128)(2,1)S(1)}, u32[]{:S(2)}, u32[]{:S(2)}) collective-permute-start(bf16[4,2,128,128]{3,2,1,0:T(8,128)(2,1)S(1)} %pack_both.1.refs_2_), channel_id=1, source_target_pairs={{0,2},{1,3},{2,4},{3,5},{4,6},{5,7},{6,8},{7,9},{8,10},{9,11},{10,... | collective-permute-start | bytes 786440 | tf_op jit(solution)/shard_map/ppermute | solution.py:21
  16.6 19.0 %collective-permute-start.6 = (bf16[4,2,128,128]{3,2,1,0:T(8,128)(2,1)S(1)}, bf16[4,2,128,128]{3,2,1,0:T(8,128)(2,1)S(1)}, u32[]{:S(2)}, u32[]{:S(2)}) collective-permute-start(bf16[4,2,128,128]{3,2,1,0:T(8,128)(2,1)S(1)} %pack_both.1.refs_2_), channel_id=1, source_target_pairs={{0,4},{1,5},{2,6},{3,7},{4,8},{5,9},{6,10},{7,11},{8,12},{9,13},{1... | collective-permute-start | bytes 786440 | tf_op jit(solution)/shard_map/ppermute | solution.py:21
  26.2 18.2 %collective-permute-start.8 = (bf16[4,2,128,128]{3,2,1,0:T(8,128)(2,1)S(1)}, bf16[4,2,128,128]{3,2,1,0:T(8,128)(2,1)S(1)}, u32[]{:S(2)}, u32[]{:S(2)}) collective-permute-start(bf16[4,2,128,128]{3,2,1,0:T(8,128)(2,1)S(1)} %get-tuple-element.39), channel_id=1, source_target_pairs={{2,0},{3,1},{4,2},{5,3},{6,4},{7,5},{8,6},{9,7},{10,8},{11,9},{12,... | collective-permute-start | bytes 786440 | tf_op jit(solution)/shard_map/ppermute | solution.py:21
  34.3 19.9 %collective-permute-start.9 = (bf16[4,2,128,128]{3,2,1,0:T(8,128)(2,1)S(1)}, bf16[4,2,128,128]{3,2,1,0:T(8,128)(2,1)S(1)}, u32[]{:S(2)}, u32[]{:S(2)}) collective-permute-start(bf16[4,2,128,128]{3,2,1,0:T(8,128)(2,1)S(1)} %get-tuple-element.40), channel_id=1, source_target_pairs={{4,0},{5,1},{6,2},{7,3},{8,4},{9,5},{10,6},{11,7},{12,8},{13,9},{1... | collective-permute-start | bytes 786440 | tf_op jit(solution)/shard_map/ppermute | solution.py:21
  41.2 21.0 %collective-permute-start.13 = (bf16[4,2,128,128]{3,2,1,0:T(8,128)(2,1)S(1)}, bf16[4,2,128,128]{3,2,1,0:T(8,128)(2,1)S(1)}, u32[]{:S(2)}, u32[]{:S(2)}) collective-permute-start(bf16[4,2,128,128]{3,2,1,0:T(8,128)(2,1)S(1)} %get-tuple-element.48), channel_id=1, source_target_pairs={{2,0},{3,1},{4,2},{5,3},{6,4},{7,5},{8,6},{9,7},{10,8},{11,9},{12,... | collective-permute-start | bytes 786440 | tf_op jit(solution)/shard_map/ppermute | solution.py:21
  43.2 19.1 %collective-permute-start.14 = (bf16[4,2,128,128]{3,2,1,0:T(8,128)(2,1)S(1)}, bf16[4,2,128,128]{3,2,1,0:T(8,128)(2,1)S(1)}, u32[]{:S(2)}, u32[]{:S(2)}) collective-permute-start(bf16[4,2,128,128]{3,2,1,0:T(8,128)(2,1)S(1)} %get-tuple-element.49), channel_id=1, source_target_pairs={{4,0},{5,1},{6,2},{7,3},{8,4},{9,5},{10,6},{11,7},{12,8},{13,9},{1... | collective-permute-start | bytes 786440 | tf_op jit(solution)/shard_map/ppermute | solution.py:21
  57.6 2.4 %collective-permute-start.10 = (bf16[56,16,128]{2,1,0:T(8,128)(2,1)S(1)}, bf16[56,16,128]{2,1,0:T(8,128)(2,1)S(1)}, u32[]{:S(2)}, u32[]{:S(2)}) collective-permute-start(bf16[56,16,128]{2,1,0:T(8,128)(2,1)S(1)} %get-tuple-element.43), channel_id=1, source_target_pairs={{0,1},{1,0},{2,3},{3,2},{4,5},{5,4},{6,7},{7,6},{8,9},{9,8},{10,11... | collective-permute-start | bytes 688136 | tf_op jit(solution)/shard_map/ppermute | solution.py:25
  58.2 1.8 %collective-permute-start.11 = (bf16[56,16,128]{2,1,0:T(8,128)(2,1)S(1)}, bf16[56,16,128]{2,1,0:T(8,128)(2,1)S(1)}, u32[]{:S(2)}, u32[]{:S(2)}) collective-permute-start(bf16[56,16,128]{2,1,0:T(8,128)(2,1)S(1)} %get-tuple-element.44), channel_id=1, source_target_pairs={{0,1},{1,0},{2,3},{3,2},{4,5},{5,4},{6,7},{7,6},{8,9},{9,8},{10,11... | collective-permute-start | bytes 688136 | tf_op jit(solution)/shard_map/ppermute | solution.py:25
  58.3 1.7 %collective-permute-start.12 = (bf16[48,16,128]{2,1,0:T(8,128)(2,1)S(1)}, bf16[48,16,128]{2,1,0:T(8,128)(2,1)S(1)}, u32[]{:S(2)}, u32[]{:S(2)}) collective-permute-start(bf16[48,16,128]{2,1,0:T(8,128)(2,1)S(1)} %get-tuple-element.45), channel_id=1, source_target_pairs={{0,1},{1,0},{2,3},{3,2},{4,5},{5,4},{6,7},{7,6},{8,9},{9,8},{10,11... | collective-permute-start | bytes 589832 | tf_op jit(solution)/shard_map/ppermute | solution.py:25
  62.9 1.4 %collective-permute-start.15 = (bf16[4,128,128]{2,1,0:T(8,128)(2,1)S(1)}, bf16[4,128,128]{2,1,0:T(8,128)(2,1)S(1)}, u32[]{:S(2)}, u32[]{:S(2)}) collective-permute-start(bf16[4,128,128]{2,1,0:T(8,128)(2,1)S(1)} %get-tuple-element.52), channel_id=1, source_target_pairs={{0,1},{1,0},{2,3},{3,2},{4,5},{5,4},{6,7},{7,6},{8,9},{9,8},{10,11... | collective-permute-start | bytes 393224 | tf_op jit(solution)/shard_map/ppermute | solution.py:25

commit v19 on v17

--- a/solution.py
+++ b/solution.py
@@ -16,9 +16,11 @@
 VMEM_BYTES = 16 * 2**20
 
 
-def moved(array, device_count, by):
-    pairs = [(d, d + by) for d in range(device_count) if 0 <= d + by < device_count]
-    return lax.ppermute(array, AXES, pairs)
+def moved(array, device_count, by, ring=False):
+    pairs = [(d, d + by) for d in range(device_count)]
+    if ring:
+        return lax.ppermute(array, AXES, [(d, to % device_count) for d, to in pairs])
+    return lax.ppermute(array, AXES, [(d, to) for d, to in pairs if 0 <= to < device_count])
 
 
 def swapped(array, device_count):
@@ -461,8 +463,8 @@
     qd, v_mine, v_other = lax.optimization_barrier((qd, v_mine, v_other))
     v_own = pack_both(place, v_mine, v_other)
 
-    def halo_of(own):
-        received = {back: moved(own, device_count, 2 * back) for back in far_first}
+    def halo_of(own, ring=False):
+        received = {back: moved(own, device_count, 2 * back, ring) for back in far_first}
         return [own] + [received[back] for back in range(1, halo + 1)]
 
     def sent_back(partials):
@@ -490,7 +492,7 @@
     acc = pltpu.VMEM((2 * halo, tokens, dim), F32)
     product = 2 * half * 2 * count * tokens * group * tokens * dim
 
-    k_pairs = halo_of(k_own)
+    k_pairs = halo_of(k_own, ring=True)
     v_pairs = halo_of(v_own)
     prob, *dv_halo = call(
         functools.partial(prob_kernel, halo),

time: 61 us -> 58.9 us (0.966)
  starting transfers between devices: 32.6 us -> 29.2 us
  waiting for transfers between devices: 2.57 us -> 3.9 us
    ppermute x8, starting transfers between devices: 23.7 us -> 21 us  [the longest x6 18.5 us: moved(): lax.ppermute(array, AXES, [(d, to) for d, to in pairs if 0 <= to < device...]
    ppermute x8, waiting for transfers between devices: 2.26 us -> 3.36 us  [swapped(): return lax.ppermute(array, AXES, [(d, d ^ 1) for d in range(device_count)])]
    ppermute x8, starting transfers between devices: 8.85 us -> 8.22 us  [swapped(): return lax.ppermute(array, AXES, [(d, d ^ 1) for d in range(device_count)])]
  transfers between devices with their start and end apart: 16 -> 16, of which waited for: 3 -> 4; matrix products, arithmetic and copies ran while one was open for 0% -> 0% of each run, Pallas kernels for 36% -> 37%
where the time goes in v19:
time: 58.9 us; the launch traced here: 58.6 us
  starting transfers between devices  29.2 us (50%)
  Pallas kernels  24.6 us (42%)
  waiting for transfers between devices  3.9 us (7%)
  between operations  0.84 us (1%)
    pallas_call x10, Pallas kernels, call(): pl.pallas_call(kernel, out_shape=outs, grid_spec=pltpu.PrefetchScalarGrid...  24.6 us
    ppermute x6, starting transfers between devices, moved(): lax.ppermute(array, AXES, [(d, to) for d, to in pairs if 0 <= to < device...  18.5 us
    ppermute x8, starting transfers between devices, swapped(): return lax.ppermute(array, AXES, [(d, d ^ 1) for d in range(device_count)])  8.22 us
    ppermute x8, waiting for transfers between devices, swapped(): return lax.ppermute(array, AXES, [(d, d ^ 1) for d in range(device_count)])  3.36 us
    ppermute x2, starting transfers between devices, moved(): lax.ppermute(array, AXES, [(d, to % device_count) for d, to in pairs])  2.45 us
  transfers between devices with their start and end apart: 16, of which 4 were waited for; matrix products, arithmetic and copies ran while one was open for 0% of the time, Pallas kernels for 37%

profile of v19, /device:TPU:23, one launch (start us, length us, event | category | flops | bytes accessed | tf_op | source)
XLA Modules:
  0.0 58.6 jit_solution(17253362946708475373)
XLA Ops:
  0.6 0.7 %collective-permute-start = (bf16[128,8,128]{2,1,0:T(8,128)(2,1)}, bf16[128,8,128]{2,1,0:T(8,128)(2,1)S(1)}, u32[]{:S(2)}, u32[]{:S(2)}) collective-permute-start(bf16[128,8,128]{2,1,0:T(8,128)(2,1)} %key_ref.1), channel_id=1, source_target_pairs={{0,1},{1,0},{2,3},{3,2},{4,5},{5,4},{6,7},{7,6},{8,9},{9,8},{10,11... | collective-permute-start | bytes 786440 | tf_op jit(solution)/shard_map/ppermute | solution.py:27
  1.4 0.1 pad_add_fusion.place_ref
  1.5 1.6 %fetch.1 = (bf16[4,2,128,128]{3,2,1,0:T(8,128)(2,1)S(1)}, bf16[128,8,128]{2,1,0:T(8,128)(2,1)S(1)}) custom-call(s32[2]{0:T(128)S(1)} %pad_add_fusion.place_ref, bf16[128,8,128]{2,1,0:T(8,128)(2,1)} %key_ref.1, bf16[128,8,128]{2,1,0:T(8,128)(2,1)} %refs_0_.1), custom_call_target="tpu_custom_call" | custom-call | flops 1000000000 | tf_op jit(solution)/shard_map/fetch/pallas_call | solution.py:40
  3.1 0.6 %pack_other.1.refs_0_ = bf16[4,2,128,128]{3,2,1,0:T(8,128)(2,1)S(1)} custom-call(s32[2]{0:T(128)S(1)} %pad_add_fusion.place_ref, bf16[128,8,128]{2,1,0:T(8,128)(2,1)S(1)} %collective-permute-done.other_ref, bf16[4,2,128,128]{3,2,1,0:T(8,128)(2,1)S(1)} %get-tuple-element.28._), custom_call_target="tpu_custom_call", output_to_operand_aliasing={{}: (2, {})} | custom-call | flops 1000000000 | tf_op jit(solution)/shard_map/pack_other/pallas_call | solution.py:40
  3.7 0.1 collective-permute-start.1
  3.9 0.4 collective-permute-start.2
  4.3 0.1 collective-permute-start.3
  4.4 1.2 %collective-permute-start.5 = (bf16[4,2,128,128]{3,2,1,0:T(8,128)(2,1)S(1)}, bf16[4,2,128,128]{3,2,1,0:T(8,128)(2,1)S(1)}, u32[]{:S(2)}, u32[]{:S(2)}) collective-permute-start(bf16[4,2,128,128]{3,2,1,0:T(8,128)(2,1)S(1)} %pack_other.1.refs_0_), channel_id=1, source_target_pairs={{0,4},{1,5},{2,6},{3,7},{4,8},{5,9},{6,10},{7,11},{8,12},{9,13},{1... | collective-permute-start | bytes 786440 | tf_op jit(solution)/shard_map/ppermute | solution.py:22
  5.6 1.2 %collective-permute-start.4 = (bf16[4,2,128,128]{3,2,1,0:T(8,128)(2,1)S(1)}, bf16[4,2,128,128]{3,2,1,0:T(8,128)(2,1)S(1)}, u32[]{:S(2)}, u32[]{:S(2)}) collective-permute-start(bf16[4,2,128,128]{3,2,1,0:T(8,128)(2,1)S(1)} %pack_other.1.refs_0_), channel_id=1, source_target_pairs={{0,2},{1,3},{2,4},{3,5},{4,6},{5,7},{6,8},{7,9},{8,10},{9,11},{10,... | collective-permute-start | bytes 786440 | tf_op jit(solution)/shard_map/ppermute | solution.py:22
  6.8 1.1 %collective-permute-done.2.do_other_ref = bf16[128,32,128]{2,1,0:T(8,128)(2,1)S(1)} collective-permute-done((bf16[128,32,128]{2,1,0:T(8,128)(2,1)S(1)}, bf16[128,32,128]{2,1,0:T(8,128)(2,1)S(1)}, u32[]{:S(2)}, u32[]{:S(2)}) %collective-permute-start.2) | collective-permute-done | bytes 1048608 | tf_op jit(solution)/shard_map/ppermute | solution.py:27
  7.9 2.0 %arrange.1.qd_ref = bf16[4,2,2,4,128,128]{5,4,3,2,1,0:T(8,128)(2,1)S(1)} custom-call(s32[2]{0:T(128)S(1)} %pad_add_fusion.place_ref, bf16[128,32,128]{2,1,0:T(8,128)(2,1)S(1)} %copy-done, bf16[128,32,128]{2,1,0:T(8,128)(2,1)S(1)} %copy-done.1, bf16[128,32,128]{2,1,0:T(8,128)(2,1)S(1)} %collective-permute-done.1.q_other_ref, ...), custom_call_target="tpu_custom_call" | custom-call | flops 1000000000 | tf_op jit(solution)/shard_map/arrange/pallas_call | solution.py:40
  10.0 0.7 %pack_both.1.refs_0_ = bf16[4,2,128,128]{3,2,1,0:T(8,128)(2,1)S(1)} custom-call(s32[2]{0:T(128)S(1)} %pad_add_fusion.place_ref, bf16[128,8,128]{2,1,0:T(8,128)(2,1)S(1)} %get-tuple-element.36.own_ref, bf16[128,8,128]{2,1,0:T(8,128)(2,1)S(1)} %collective-permute-done.3.other_ref), custom_call_target="tpu_custom_call" | custom-call | flops 1000000000 | tf_op jit(solution)/shard_map/pack_both/pallas_call | solution.py:40
  10.7 3.1 %collective-permute-start.7 = (bf16[4,2,128,128]{3,2,1,0:T(8,128)(2,1)S(1)}, bf16[4,2,128,128]{3,2,1,0:T(8,128)(2,1)S(1)}, u32[]{:S(2)}, u32[]{:S(2)}) collective-permute-start(bf16[4,2,128,128]{3,2,1,0:T(8,128)(2,1)S(1)} %pack_both.1.refs_0_), channel_id=1, source_target_pairs={{0,4},{1,5},{2,6},{3,7},{4,8},{5,9},{6,10},{7,11},{8,12},{9,13},{1... | collective-permute-start | bytes 786440 | tf_op jit(solution)/shard_map/ppermute | solution.py:23
  13.9 3.1 %collective-permute-start.6 = (bf16[4,2,128,128]{3,2,1,0:T(8,128)(2,1)S(1)}, bf16[4,2,128,128]{3,2,1,0:T(8,128)(2,1)S(1)}, u32[]{:S(2)}, u32[]{:S(2)}) collective-permute-start(bf16[4,2,128,128]{3,2,1,0:T(8,128)(2,1)S(1)} %pack_both.1.refs_0_), channel_id=1, source_target_pairs={{0,2},{1,3},{2,4},{3,5},{4,6},{5,7},{6,8},{7,9},{8,10},{9,11},{10,... | collective-permute-start | bytes 786440 | tf_op jit(solution)/shard_map/ppermute | solution.py:23
  17.0 0.5 collective-permute-done.4.refs_1_
  17.5 6.5 %prob.1 = (bf16[4,2,640,512]{3,2,1,0:T(8,128)(2,1)S(1)}, bf16[4,2,128,128]{3,2,1,0:T(8,128)(2,1)S(1)}, bf16[4,2,128,128]{3,2,1,0:T(8,128)(2,1)S(1)}) custom-call(s32[2]{0:T(128)S(1)} %pad_add_fusion.place_ref, s32[16]{0:T(128)S(1)} %copy-done.2, bf16[4,2,2,4,128,128]{5,4,3,2,1,0:T(8,128)(2,1)S(1)} %arrange.1.qd_ref, ...), custom_call_target="tpu_custom_call" | custom-call | flops 2684354560 | tf_op jit(solution)/shard_map/prob/pallas_call | solution.py:40
  24.0 1.9 %collective-permute-start.8 = (bf16[4,2,128,128]{3,2,1,0:T(8,128)(2,1)S(1)}, bf16[4,2,128,128]{3,2,1,0:T(8,128)(2,1)S(1)}, u32[]{:S(2)}, u32[]{:S(2)}) collective-permute-start(bf16[4,2,128,128]{3,2,1,0:T(8,128)(2,1)S(1)} %get-tuple-element.39), channel_id=1, source_target_pairs={{4,0},{5,1},{6,2},{7,3},{8,4},{9,5},{10,6},{11,7},{12,8},{13,9},{1... | collective-permute-start | bytes 786440 | tf_op jit(solution)/shard_map/ppermute | solution.py:23
  25.9 6.5 %collective-permute-start.9 = (bf16[4,2,128,128]{3,2,1,0:T(8,128)(2,1)S(1)}, bf16[4,2,128,128]{3,2,1,0:T(8,128)(2,1)S(1)}, u32[]{:S(2)}, u32[]{:S(2)}) collective-permute-start(bf16[4,2,128,128]{3,2,1,0:T(8,128)(2,1)S(1)} %get-tuple-element.40), channel_id=1, source_target_pairs={{2,0},{3,1},{4,2},{5,3},{6,4},{7,5},{8,6},{9,7},{10,8},{11,9},{12,... | collective-permute-start | bytes 786440 | tf_op jit(solution)/shard_map/ppermute | solution.py:23
  32.4 5.6 %dscore.1 = (bf16[4,2,640,512]{3,2,1,0:T(8,128)(2,1)S(1)}, bf16[4,2,128,128]{3,2,1,0:T(8,128)(2,1)S(1)}, bf16[4,2,128,128]{3,2,1,0:T(8,128)(2,1)S(1)}) custom-call(s32[2]{0:T(128)S(1)} %pad_add_fusion.place_ref, bf16[4,2,2,4,128,128]{5,4,3,2,1,0:T(8,128)(2,1)S(1)} %arrange.1.qd_ref, bf16[4,2,640,512]{3,2,1,0:T(8,128)(2,1)S(1)} %get-tuple-element.35.p_ref, ...), custom_call_target="tpu_custom_call" | custom-call | flops 2684354560 | tf_op jit(solution)/shard_map/dscore/pallas_call | solution.py:40
  38.0 1.9 %collective-permute-start.13 = (bf16[4,2,128,128]{3,2,1,0:T(8,128)(2,1)S(1)}, bf16[4,2,128,128]{3,2,1,0:T(8,128)(2,1)S(1)}, u32[]{:S(2)}, u32[]{:S(2)}) collective-permute-start(bf16[4,2,128,128]{3,2,1,0:T(8,128)(2,1)S(1)} %get-tuple-element.48), channel_id=1, source_target_pairs={{4,0},{5,1},{6,2},{7,3},{8,4},{9,5},{10,6},{11,7},{12,8},{13,9},{1... | collective-permute-start | bytes 786440 | tf_op jit(solution)/shard_map/ppermute | solution.py:23
  39.9 1.9 %collective-permute-start.14 = (bf16[4,2,128,128]{3,2,1,0:T(8,128)(2,1)S(1)}, bf16[4,2,128,128]{3,2,1,0:T(8,128)(2,1)S(1)}, u32[]{:S(2)}, u32[]{:S(2)}) collective-permute-start(bf16[4,2,128,128]{3,2,1,0:T(8,128)(2,1)S(1)} %get-tuple-element.49), channel_id=1, source_target_pairs={{2,0},{3,1},{4,2},{5,3},{6,4},{7,5},{8,6},{9,7},{10,8},{11,9},{12,... | collective-permute-start | bytes 786440 | tf_op jit(solution)/shard_map/ppermute | solution.py:23
  41.9 3.3 %own.1 = (bf16[128,16,128]{2,1,0:T(8,128)(2,1)S(1)}, bf16[56,16,128]{2,1,0:T(8,128)(2,1)S(1)}, bf16[56,16,128]{2,1,0:T(8,128)(2,1)S(1)}, bf16[48,16,128]{2,1,0:T...) custom-call(s32[2]{0:T(128)S(1)} %pad_add_fusion.place_ref, ...), custom_call_target="tpu_custom_call" | custom-call | tf_op jit(solution)/shard_map/own/pallas_call | solution.py:40
  45.3 2.9 %collective-permute-start.10 = (bf16[56,16,128]{2,1,0:T(8,128)(2,1)S(1)}, bf16[56,16,128]{2,1,0:T(8,128)(2,1)S(1)}, u32[]{:S(2)}, u32[]{:S(2)}) collective-permute-start(bf16[56,16,128]{2,1,0:T(8,128)(2,1)S(1)} %get-tuple-element.43), channel_id=1, source_target_pairs={{0,1},{1,0},{2,3},{3,2},{4,5},{5,4},{6,7},{7,6},{8,9},{9,8},{10,11... | collective-permute-start | bytes 688136 | tf_op jit(solution)/shard_map/ppermute | solution.py:27
  48.2 0.1 collective-permute-start.11
  48.3 0.4 collective-permute-start.12
  48.7 1.3 %collective-permute-done.12.refs_2_ = bf16[48,16,128]{2,1,0:T(8,128)(2,1)S(1)} collective-permute-done((bf16[48,16,128]{2,1,0:T(8,128)(2,1)S(1)}, bf16[48,16,128]{2,1,0:T(8,128)(2,1)S(1)}, u32[]{:S(2)}, u32[]{:S(2)}) %collective-permute-start.12) | collective-permute-done | bytes 196640 | tf_op jit(solution)/shard_map/ppermute | solution.py:27
  50.0 2.2 %join.1 = (bf16[128,32,128]{2,1,0:T(8,128)(2,1)}, bf16[128,8,128]{2,1,0:T(8,128)(2,1)}) custom-call(s32[2]{0:T(128)S(1)} %pad_add_fusion.place_ref, bf16[128,16,128]{2,1,0:T(8,128)(2,1)S(1)} %get-tuple-element.41.dq_ref, bf16[4,128,128]{2,1,0:T(8,128)(2,1)S(1)} %get-tuple-element.42.dv_ref, bf16[56,16,128]{2,1,0:T(8,128)(2,1)S(1)} %collective-permute-done.10.refs_0_, ...), custom_call_target="tpu_custom_call" | custom-call | tf_op jit(solution)/shard_map/join/pallas_call | solution.py:40
  52.2 0.0 collective-permute-done.14.refs_1_
  52.2 0.6 %sum_dk.1 = (bf16[4,128,128]{2,1,0:T(8,128)(2,1)S(1)}, bf16[4,128,128]{2,1,0:T(8,128)(2,1)S(1)}) custom-call(s32[2]{0:T(128)S(1)} %pad_add_fusion.place_ref, f32[4,2,128,128]{3,2,1,0:T(8,128)S(1)} %get-tuple-element.47.own_ref, bf16[4,2,128,128]{3,2,1,0:T(8,128)(2,1)S(1)} %collective-permute-done.13.refs_0_, ...), custom_call_target="tpu_custom_call" | custom-call | tf_op jit(solution)/shard_map/sum_dk/pallas_call | solution.py:40
  52.9 3.4 %collective-permute-start.15 = (bf16[4,128,128]{2,1,0:T(8,128)(2,1)S(1)}, bf16[4,128,128]{2,1,0:T(8,128)(2,1)S(1)}, u32[]{:S(2)}, u32[]{:S(2)}) collective-permute-start(bf16[4,128,128]{2,1,0:T(8,128)(2,1)S(1)} %get-tuple-element.52), channel_id=1, source_target_pairs={{0,1},{1,0},{2,3},{3,2},{4,5},{5,4},{6,7},{7,6},{8,9},{9,8},{10,11... | collective-permute-start | bytes 393224 | tf_op jit(solution)/shard_map/ppermute | solution.py:27
  56.2 1.0 %collective-permute-done.15.other_ref = bf16[4,128,128]{2,1,0:T(8,128)(2,1)S(1)} collective-permute-done((bf16[4,128,128]{2,1,0:T(8,128)(2,1)S(1)}, bf16[4,128,128]{2,1,0:T(8,128)(2,1)S(1)}, u32[]{:S(2)}, u32[]{:S(2)}) %collective-permute-start.15) | collective-permute-done | bytes 131104 | tf_op jit(solution)/shard_map/ppermute | solution.py:27
  57.2 1.4 %merge_dk.1 = bf16[128,8,128]{2,1,0:T(8,128)(2,1)} custom-call(s32[2]{0:T(128)S(1)} %pad_add_fusion.place_ref, bf16[4,128,128]{2,1,0:T(8,128)(2,1)S(1)} %get-tuple-element.51.own_ref, bf16[4,128,128]{2,1,0:T(8,128)(2,1)S(1)} %collective-permute-done.15.other_ref), custom_call_target="tpu_custom_call" | custom-call | tf_op jit(solution)/shard_map/merge_dk/pallas_call | solution.py:40
  (17 shorter events, 0.0 us)
Async XLA Ops:
  0.6 3.2 %copy-start.1 = (bf16[128,32,128]{2,1,0:T(8,128)(2,1)S(1)}, bf16[128,32,128]{2,1,0:T(8,128)(2,1)}, u32[]{:S(2)}) copy-start(bf16[128,32,128]{2,1,0:T(8,128)(2,1)} %do_ref) | copy-start | bytes 3145732
  0.6 3.1 %copy-start = (bf16[128,32,128]{2,1,0:T(8,128)(2,1)S(1)}, bf16[128,32,128]{2,1,0:T(8,128)(2,1)}, u32[]{:S(2)}) copy-start(bf16[128,32,128]{2,1,0:T(8,128)(2,1)} %q_ref) | copy-start | bytes 3145732
  0.6 2.4 %collective-permute-start = (bf16[128,8,128]{2,1,0:T(8,128)(2,1)}, bf16[128,8,128]{2,1,0:T(8,128)(2,1)S(1)}, u32[]{:S(2)}, u32[]{:S(2)}) collective-permute-start(bf16[128,8,128]{2,1,0:T(8,128)(2,1)} %key_ref.1), channel_id=1, source_target_pairs={{0,1},{1,0},{2,3},{3,2},{4,5},{5,4},{6,7},{7,6},{8,9},{9,8},{10,11... | collective-permute-start | bytes 786440 | tf_op jit(solution)/shard_map/ppermute | solution.py:27
  3.7 13.8 %copy-start.2 = (s32[16]{0:T(128)S(1)}, s32[16]{0:T(128)}, u32[]{:S(2)}) copy-start(s32[16]{0:T(128)} %lengths_ref.1) | copy-start | bytes 196
  3.7 3.1 %collective-permute-start.1 = (bf16[128,32,128]{2,1,0:T(8,128)(2,1)S(1)}, bf16[128,32,128]{2,1,0:T(8,128)(2,1)S(1)}, u32[]{:S(2)}, u32[]{:S(2)}) collective-permute-start(bf16[128,32,128]{2,1,0:T(8,128)(2,1)S(1)} %copy-done), channel_id=1, source_target_pairs={{0,1},{1,0},{2,3},{3,2},{4,5},{5,4},{6,7},{7,6},{8,9},{9,8},{10,11... | collective-permute-start | bytes 3145736 | tf_op jit(solution)/shard_map/ppermute | solution.py:27
  3.9 4.1 %collective-permute-start.2 = (bf16[128,32,128]{2,1,0:T(8,128)(2,1)S(1)}, bf16[128,32,128]{2,1,0:T(8,128)(2,1)S(1)}, u32[]{:S(2)}, u32[]{:S(2)}) collective-permute-start(bf16[128,32,128]{2,1,0:T(8,128)(2,1)S(1)} %copy-done.1), channel_id=1, source_target_pairs={{0,1},{1,0},{2,3},{3,2},{4,5},{5,4},{6,7},{7,6},{8,9},{9,8},{10,11... | collective-permute-start | bytes 3145736 | tf_op jit(solution)/shard_map/ppermute | solution.py:27
  4.3 5.7 %collective-permute-start.3 = (bf16[128,8,128]{2,1,0:T(8,128)(2,1)S(1)}, bf16[128,8,128]{2,1,0:T(8,128)(2,1)S(1)}, u32[]{:S(2)}, u32[]{:S(2)}) collective-permute-start(bf16[128,8,128]{2,1,0:T(8,128)(2,1)S(1)} %get-tuple-element.36.own_ref), channel_id=1, source_target_pairs={{0,1},{1,0},{2,3},{3,2},{4,5},{5,4},{6,7},{7,6},{8,9},{9,8},{10,11... | collective-permute-start | bytes 786440 | tf_op jit(solution)/shard_map/ppermute | solution.py:27
  4.4 12.6 %collective-permute-start.5 = (bf16[4,2,128,128]{3,2,1,0:T(8,128)(2,1)S(1)}, bf16[4,2,128,128]{3,2,1,0:T(8,128)(2,1)S(1)}, u32[]{:S(2)}, u32[]{:S(2)}) collective-permute-start(bf16[4,2,128,128]{3,2,1,0:T(8,128)(2,1)S(1)} %pack_other.1.refs_0_), channel_id=1, source_target_pairs={{0,4},{1,5},{2,6},{3,7},{4,8},{5,9},{6,10},{7,11},{8,12},{9,13},{1... | collective-permute-start | bytes 786440 | tf_op jit(solution)/shard_map/ppermute | solution.py:22
  5.6 11.9 %collective-permute-start.4 = (bf16[4,2,128,128]{3,2,1,0:T(8,128)(2,1)S(1)}, bf16[4,2,128,128]{3,2,1,0:T(8,128)(2,1)S(1)}, u32[]{:S(2)}, u32[]{:S(2)}) collective-permute-start(bf16[4,2,128,128]{3,2,1,0:T(8,128)(2,1)S(1)} %pack_other.1.refs_0_), channel_id=1, source_target_pairs={{0,2},{1,3},{2,4},{3,5},{4,6},{5,7},{6,8},{7,9},{8,10},{9,11},{10,... | collective-permute-start | bytes 786440 | tf_op jit(solution)/shard_map/ppermute | solution.py:22
  10.7 21.7 %collective-permute-start.7 = (bf16[4,2,128,128]{3,2,1,0:T(8,128)(2,1)S(1)}, bf16[4,2,128,128]{3,2,1,0:T(8,128)(2,1)S(1)}, u32[]{:S(2)}, u32[]{:S(2)}) collective-permute-start(bf16[4,2,128,128]{3,2,1,0:T(8,128)(2,1)S(1)} %pack_both.1.refs_0_), channel_id=1, source_target_pairs={{0,4},{1,5},{2,6},{3,7},{4,8},{5,9},{6,10},{7,11},{8,12},{9,13},{1... | collective-permute-start | bytes 786440 | tf_op jit(solution)/shard_map/ppermute | solution.py:23
  13.9 18.6 %collective-permute-start.6 = (bf16[4,2,128,128]{3,2,1,0:T(8,128)(2,1)S(1)}, bf16[4,2,128,128]{3,2,1,0:T(8,128)(2,1)S(1)}, u32[]{:S(2)}, u32[]{:S(2)}) collective-permute-start(bf16[4,2,128,128]{3,2,1,0:T(8,128)(2,1)S(1)} %pack_both.1.refs_0_), channel_id=1, source_target_pairs={{0,2},{1,3},{2,4},{3,5},{4,6},{5,7},{6,8},{7,9},{8,10},{9,11},{10,... | collective-permute-start | bytes 786440 | tf_op jit(solution)/shard_map/ppermute | solution.py:23
  24.0 17.9 %collective-permute-start.8 = (bf16[4,2,128,128]{3,2,1,0:T(8,128)(2,1)S(1)}, bf16[4,2,128,128]{3,2,1,0:T(8,128)(2,1)S(1)}, u32[]{:S(2)}, u32[]{:S(2)}) collective-permute-start(bf16[4,2,128,128]{3,2,1,0:T(8,128)(2,1)S(1)} %get-tuple-element.39), channel_id=1, source_target_pairs={{4,0},{5,1},{6,2},{7,3},{8,4},{9,5},{10,6},{11,7},{12,8},{13,9},{1... | collective-permute-start | bytes 786440 | tf_op jit(solution)/shard_map/ppermute | solution.py:23
  25.9 16.0 %collective-permute-start.9 = (bf16[4,2,128,128]{3,2,1,0:T(8,128)(2,1)S(1)}, bf16[4,2,128,128]{3,2,1,0:T(8,128)(2,1)S(1)}, u32[]{:S(2)}, u32[]{:S(2)}) collective-permute-start(bf16[4,2,128,128]{3,2,1,0:T(8,128)(2,1)S(1)} %get-tuple-element.40), channel_id=1, source_target_pairs={{2,0},{3,1},{4,2},{5,3},{6,4},{7,5},{8,6},{9,7},{10,8},{11,9},{12,... | collective-permute-start | bytes 786440 | tf_op jit(solution)/shard_map/ppermute | solution.py:23
  38.0 14.2 %collective-permute-start.13 = (bf16[4,2,128,128]{3,2,1,0:T(8,128)(2,1)S(1)}, bf16[4,2,128,128]{3,2,1,0:T(8,128)(2,1)S(1)}, u32[]{:S(2)}, u32[]{:S(2)}) collective-permute-start(bf16[4,2,128,128]{3,2,1,0:T(8,128)(2,1)S(1)} %get-tuple-element.48), channel_id=1, source_target_pairs={{4,0},{5,1},{6,2},{7,3},{8,4},{9,5},{10,6},{11,7},{12,8},{13,9},{1... | collective-permute-start | bytes 786440 | tf_op jit(solution)/shard_map/ppermute | solution.py:23
  39.9 12.3 %collective-permute-start.14 = (bf16[4,2,128,128]{3,2,1,0:T(8,128)(2,1)S(1)}, bf16[4,2,128,128]{3,2,1,0:T(8,128)(2,1)S(1)}, u32[]{:S(2)}, u32[]{:S(2)}) collective-permute-start(bf16[4,2,128,128]{3,2,1,0:T(8,128)(2,1)S(1)} %get-tuple-element.49), channel_id=1, source_target_pairs={{2,0},{3,1},{4,2},{5,3},{6,4},{7,5},{8,6},{9,7},{10,8},{11,9},{12,... | collective-permute-start | bytes 786440 | tf_op jit(solution)/shard_map/ppermute | solution.py:23
  45.3 4.7 %collective-permute-start.10 = (bf16[56,16,128]{2,1,0:T(8,128)(2,1)S(1)}, bf16[56,16,128]{2,1,0:T(8,128)(2,1)S(1)}, u32[]{:S(2)}, u32[]{:S(2)}) collective-permute-start(bf16[56,16,128]{2,1,0:T(8,128)(2,1)S(1)} %get-tuple-element.43), channel_id=1, source_target_pairs={{0,1},{1,0},{2,3},{3,2},{4,5},{5,4},{6,7},{7,6},{8,9},{9,8},{10,11... | collective-permute-start | bytes 688136 | tf_op jit(solution)/shard_map/ppermute | solution.py:27
  48.2 1.8 %collective-permute-start.11 = (bf16[56,16,128]{2,1,0:T(8,128)(2,1)S(1)}, bf16[56,16,128]{2,1,0:T(8,128)(2,1)S(1)}, u32[]{:S(2)}, u32[]{:S(2)}) collective-permute-start(bf16[56,16,128]{2,1,0:T(8,128)(2,1)S(1)} %get-tuple-element.44), channel_id=1, source_target_pairs={{0,1},{1,0},{2,3},{3,2},{4,5},{5,4},{6,7},{7,6},{8,9},{9,8},{10,11... | collective-permute-start | bytes 688136 | tf_op jit(solution)/shard_map/ppermute | solution.py:27
  48.3 1.7 %collective-permute-start.12 = (bf16[48,16,128]{2,1,0:T(8,128)(2,1)S(1)}, bf16[48,16,128]{2,1,0:T(8,128)(2,1)S(1)}, u32[]{:S(2)}, u32[]{:S(2)}) collective-permute-start(bf16[48,16,128]{2,1,0:T(8,128)(2,1)S(1)} %get-tuple-element.45), channel_id=1, source_target_pairs={{0,1},{1,0},{2,3},{3,2},{4,5},{5,4},{6,7},{7,6},{8,9},{9,8},{10,11... | collective-permute-start | bytes 589832 | tf_op jit(solution)/shard_map/ppermute | solution.py:27
  52.9 4.4 %collective-permute-start.15 = (bf16[4,128,128]{2,1,0:T(8,128)(2,1)S(1)}, bf16[4,128,128]{2,1,0:T(8,128)(2,1)S(1)}, u32[]{:S(2)}, u32[]{:S(2)}) collective-permute-start(bf16[4,128,128]{2,1,0:T(8,128)(2,1)S(1)} %get-tuple-element.52), channel_id=1, source_target_pairs={{0,1},{1,0},{2,3},{3,2},{4,5},{5,4},{6,7},{7,6},{8,9},{9,8},{10,11... | collective-permute-start | bytes 393224 | tf_op jit(solution)/shard_map/ppermute | solution.py:27

commit v20 on v19

--- a/solution.py
+++ b/solution.py
@@ -16,7 +16,7 @@
 VMEM_BYTES = 16 * 2**20
 
 
-def moved(array, device_count, by, ring=False):
+def moved(array, device_count, by, ring):
     pairs = [(d, d + by) for d in range(device_count)]
     if ring:
         return lax.ppermute(array, AXES, [(d, to % device_count) for d, to in pairs])
@@ -463,12 +463,12 @@
     qd, v_mine, v_other = lax.optimization_barrier((qd, v_mine, v_other))
     v_own = pack_both(place, v_mine, v_other)
 
-    def halo_of(own, ring=False):
+    def halo_of(own, ring):
         received = {back: moved(own, device_count, 2 * back, ring) for back in far_first}
         return [own] + [received[back] for back in range(1, halo + 1)]
 
-    def sent_back(partials):
-        return [moved(partials[back - 1], device_count, -2 * back) for back in far_first]
+    def sent_back(partials, ring):
+        return [moved(partials[back - 1], device_count, -2 * back, ring) for back in far_first]
 
     def per_head(*shape):
         return pl.BlockSpec((1,) + shape, lambda h, *_: (h,) + (0,) * len(shape))
@@ -493,7 +493,7 @@
     product = 2 * half * 2 * count * tokens * group * tokens * dim
 
     k_pairs = halo_of(k_own, ring=True)
-    v_pairs = halo_of(v_own)
+    v_pairs = halo_of(v_own, ring=False)
     prob, *dv_halo = call(
         functools.partial(prob_kernel, halo),
         "prob",
@@ -506,7 +506,7 @@
         [run, acc, pltpu.VMEM((2, count - 1, tokens, HEADS_AT_ONCE * tokens), F32)],
         4 * product,
     )
-    dv_back = sent_back(dv_halo)
+    dv_back = sent_back(dv_halo, ring=False)
     dscore, *dk_halo = call(
         functools.partial(dscore_kernel, halo),
         "dscore",
@@ -519,7 +519,7 @@
         [run, acc],
         4 * product,
     )
-    dk_back = sent_back(dk_halo)
+    dk_back = sent_back(dk_halo, ring=True)
     dq, *others, dk_own, dv = call(
         functools.partial(own_kernel, halo),
         "own",

time: 58.9 us -> 59.1 us (level)
  starting transfers between devices: 29.2 us -> 26.8 us
  waiting for transfers between devices: 3.9 us -> 6.21 us
    ppermute x6 -> x4, starting transfers between devices: 18.5 us -> 14.7 us  [moved(): lax.ppermute(array, AXES, [(d, to) for d, to in pairs if 0 <= to < device...]
    ppermute x6 -> x4, waiting for transfers between devices: 0.03 us -> 2.34 us  [moved(): lax.ppermute(array, AXES, [(d, to) for d, to in pairs if 0 <= to < device...]
    ppermute x8, starting transfers between devices: 8.22 us -> 9.5 us  [swapped(): return lax.ppermute(array, AXES, [(d, d ^ 1) for d in range(device_count)])]
    ppermute x2 -> x4, starting transfers between devices: 2.45 us -> 2.58 us  [moved(): lax.ppermute(array, AXES, [(d, to % device_count) for d, to in pairs])]
  transfers between devices with their start and end apart: 16 -> 16, of which waited for: 4 -> 5; matrix products, arithmetic and copies ran while one was open for 0% -> 0% of each run, Pallas kernels for 37% -> 38%
where the time goes in v20:
time: 59.1 us; the launch traced here: 58.5 us
  starting transfers between devices  26.8 us (45%)
  Pallas kernels  24.6 us (42%)
  waiting for transfers between devices  6.21 us (11%)
  between operations  0.83 us (1%)
    pallas_call x10, Pallas kernels, call(): pl.pallas_call(kernel, out_shape=outs, grid_spec=pltpu.PrefetchScalarGrid...  24.6 us
    ppermute x4, starting transfers between devices, moved(): lax.ppermute(array, AXES, [(d, to) for d, to in pairs if 0 <= to < device...  14.7 us
    ppermute x8, starting transfers between devices, swapped(): return lax.ppermute(array, AXES, [(d, d ^ 1) for d in range(device_count)])  9.5 us
    ppermute x8, waiting for transfers between devices, swapped(): return lax.ppermute(array, AXES, [(d, d ^ 1) for d in range(device_count)])  3.36 us
    ppermute x4, starting transfers between devices, moved(): lax.ppermute(array, AXES, [(d, to % device_count) for d, to in pairs])  2.58 us
    ppermute x4, waiting for transfers between devices, moved(): lax.ppermute(array, AXES, [(d, to) for d, to in pairs if 0 <= to < device...  2.34 us
  transfers between devices with their start and end apart: 16, of which 5 were waited for; matrix products, arithmetic and copies ran while one was open for 0% of the time, Pallas kernels for 38%

profile of v20, /device:TPU:23, one launch (start us, length us, event | category | flops | bytes accessed | tf_op | source)
XLA Modules:
  0.0 58.5 jit_solution(514511232761218060)
XLA Ops:
  0.6 0.7 %collective-permute-start = (bf16[128,8,128]{2,1,0:T(8,128)(2,1)}, bf16[128,8,128]{2,1,0:T(8,128)(2,1)S(1)}, u32[]{:S(2)}, u32[]{:S(2)}) collective-permute-start(bf16[128,8,128]{2,1,0:T(8,128)(2,1)} %key_ref.1), channel_id=1, source_target_pairs={{0,1},{1,0},{2,3},{3,2},{4,5},{5,4},{6,7},{7,6},{8,9},{9,8},{10,11... | collective-permute-start | bytes 786440 | tf_op jit(solution)/shard_map/ppermute | solution.py:27
  1.4 0.1 pad_add_fusion.place_ref
  1.5 1.6 %fetch.1 = (bf16[4,2,128,128]{3,2,1,0:T(8,128)(2,1)S(1)}, bf16[128,8,128]{2,1,0:T(8,128)(2,1)S(1)}) custom-call(s32[2]{0:T(128)S(1)} %pad_add_fusion.place_ref, bf16[128,8,128]{2,1,0:T(8,128)(2,1)} %key_ref.1, bf16[128,8,128]{2,1,0:T(8,128)(2,1)} %refs_0_.1), custom_call_target="tpu_custom_call" | custom-call | flops 1000000000 | tf_op jit(solution)/shard_map/fetch/pallas_call | solution.py:40
  3.1 0.6 %pack_other.1.refs_0_ = bf16[4,2,128,128]{3,2,1,0:T(8,128)(2,1)S(1)} custom-call(s32[2]{0:T(128)S(1)} %pad_add_fusion.place_ref, bf16[128,8,128]{2,1,0:T(8,128)(2,1)S(1)} %collective-permute-done.other_ref, bf16[4,2,128,128]{3,2,1,0:T(8,128)(2,1)S(1)} %get-tuple-element.28._), custom_call_target="tpu_custom_call", output_to_operand_aliasing={{}: (2, {})} | custom-call | flops 1000000000 | tf_op jit(solution)/shard_map/pack_other/pallas_call | solution.py:40
  3.7 0.1 collective-permute-start.1
  3.9 0.4 collective-permute-start.2
  4.3 0.1 collective-permute-start.3
  4.4 1.2 %collective-permute-start.5 = (bf16[4,2,128,128]{3,2,1,0:T(8,128)(2,1)S(1)}, bf16[4,2,128,128]{3,2,1,0:T(8,128)(2,1)S(1)}, u32[]{:S(2)}, u32[]{:S(2)}) collective-permute-start(bf16[4,2,128,128]{3,2,1,0:T(8,128)(2,1)S(1)} %pack_other.1.refs_0_), channel_id=1, source_target_pairs={{0,4},{1,5},{2,6},{3,7},{4,8},{5,9},{6,10},{7,11},{8,12},{9,13},{1... | collective-permute-start | bytes 786440 | tf_op jit(solution)/shard_map/ppermute | solution.py:22
  5.6 1.2 %collective-permute-start.4 = (bf16[4,2,128,128]{3,2,1,0:T(8,128)(2,1)S(1)}, bf16[4,2,128,128]{3,2,1,0:T(8,128)(2,1)S(1)}, u32[]{:S(2)}, u32[]{:S(2)}) collective-permute-start(bf16[4,2,128,128]{3,2,1,0:T(8,128)(2,1)S(1)} %pack_other.1.refs_0_), channel_id=1, source_target_pairs={{0,2},{1,3},{2,4},{3,5},{4,6},{5,7},{6,8},{7,9},{8,10},{9,11},{10,... | collective-permute-start | bytes 786440 | tf_op jit(solution)/shard_map/ppermute | solution.py:22
  6.8 1.1 %collective-permute-done.2.do_other_ref = bf16[128,32,128]{2,1,0:T(8,128)(2,1)S(1)} collective-permute-done((bf16[128,32,128]{2,1,0:T(8,128)(2,1)S(1)}, bf16[128,32,128]{2,1,0:T(8,128)(2,1)S(1)}, u32[]{:S(2)}, u32[]{:S(2)}) %collective-permute-start.2) | collective-permute-done | bytes 1048608 | tf_op jit(solution)/shard_map/ppermute | solution.py:27
  7.9 2.0 %arrange.1.qd_ref = bf16[4,2,2,4,128,128]{5,4,3,2,1,0:T(8,128)(2,1)S(1)} custom-call(s32[2]{0:T(128)S(1)} %pad_add_fusion.place_ref, bf16[128,32,128]{2,1,0:T(8,128)(2,1)S(1)} %copy-done, bf16[128,32,128]{2,1,0:T(8,128)(2,1)S(1)} %copy-done.1, bf16[128,32,128]{2,1,0:T(8,128)(2,1)S(1)} %collective-permute-done.1.q_other_ref, ...), custom_call_target="tpu_custom_call" | custom-call | flops 1000000000 | tf_op jit(solution)/shard_map/arrange/pallas_call | solution.py:40
  10.0 0.7 %pack_both.1.refs_0_ = bf16[4,2,128,128]{3,2,1,0:T(8,128)(2,1)S(1)} custom-call(s32[2]{0:T(128)S(1)} %pad_add_fusion.place_ref, bf16[128,8,128]{2,1,0:T(8,128)(2,1)S(1)} %get-tuple-element.36.own_ref, bf16[128,8,128]{2,1,0:T(8,128)(2,1)S(1)} %collective-permute-done.3.other_ref), custom_call_target="tpu_custom_call" | custom-call | flops 1000000000 | tf_op jit(solution)/shard_map/pack_both/pallas_call | solution.py:40
  10.7 3.1 %collective-permute-start.7 = (bf16[4,2,128,128]{3,2,1,0:T(8,128)(2,1)S(1)}, bf16[4,2,128,128]{3,2,1,0:T(8,128)(2,1)S(1)}, u32[]{:S(2)}, u32[]{:S(2)}) collective-permute-start(bf16[4,2,128,128]{3,2,1,0:T(8,128)(2,1)S(1)} %pack_both.1.refs_0_), channel_id=1, source_target_pairs={{0,4},{1,5},{2,6},{3,7},{4,8},{5,9},{6,10},{7,11},{8,12},{9,13},{1... | collective-permute-start | bytes 786440 | tf_op jit(solution)/shard_map/ppermute | solution.py:23
  13.9 3.1 %collective-permute-start.6 = (bf16[4,2,128,128]{3,2,1,0:T(8,128)(2,1)S(1)}, bf16[4,2,128,128]{3,2,1,0:T(8,128)(2,1)S(1)}, u32[]{:S(2)}, u32[]{:S(2)}) collective-permute-start(bf16[4,2,128,128]{3,2,1,0:T(8,128)(2,1)S(1)} %pack_both.1.refs_0_), channel_id=1, source_target_pairs={{0,2},{1,3},{2,4},{3,5},{4,6},{5,7},{6,8},{7,9},{8,10},{9,11},{10,... | collective-permute-start | bytes 786440 | tf_op jit(solution)/shard_map/ppermute | solution.py:23
  17.0 0.5 collective-permute-done.4.refs_1_
  17.5 6.5 %prob.1 = (bf16[4,2,640,512]{3,2,1,0:T(8,128)(2,1)S(1)}, bf16[4,2,128,128]{3,2,1,0:T(8,128)(2,1)S(1)}, bf16[4,2,128,128]{3,2,1,0:T(8,128)(2,1)S(1)}) custom-call(s32[2]{0:T(128)S(1)} %pad_add_fusion.place_ref, s32[16]{0:T(128)S(1)} %copy-done.2, bf16[4,2,2,4,128,128]{5,4,3,2,1,0:T(8,128)(2,1)S(1)} %arrange.1.qd_ref, ...), custom_call_target="tpu_custom_call" | custom-call | flops 2684354560 | tf_op jit(solution)/shard_map/prob/pallas_call | solution.py:40
  24.0 1.9 %collective-permute-start.8 = (bf16[4,2,128,128]{3,2,1,0:T(8,128)(2,1)S(1)}, bf16[4,2,128,128]{3,2,1,0:T(8,128)(2,1)S(1)}, u32[]{:S(2)}, u32[]{:S(2)}) collective-permute-start(bf16[4,2,128,128]{3,2,1,0:T(8,128)(2,1)S(1)} %get-tuple-element.39), channel_id=1, source_target_pairs={{4,0},{5,1},{6,2},{7,3},{8,4},{9,5},{10,6},{11,7},{12,8},{13,9},{1... | collective-permute-start | bytes 786440 | tf_op jit(solution)/shard_map/ppermute | solution.py:23
  25.9 6.5 %collective-permute-start.9 = (bf16[4,2,128,128]{3,2,1,0:T(8,128)(2,1)S(1)}, bf16[4,2,128,128]{3,2,1,0:T(8,128)(2,1)S(1)}, u32[]{:S(2)}, u32[]{:S(2)}) collective-permute-start(bf16[4,2,128,128]{3,2,1,0:T(8,128)(2,1)S(1)} %get-tuple-element.40), channel_id=1, source_target_pairs={{2,0},{3,1},{4,2},{5,3},{6,4},{7,5},{8,6},{9,7},{10,8},{11,9},{12,... | collective-permute-start | bytes 786440 | tf_op jit(solution)/shard_map/ppermute | solution.py:23
  32.4 5.6 %dscore.1 = (bf16[4,2,640,512]{3,2,1,0:T(8,128)(2,1)S(1)}, bf16[4,2,128,128]{3,2,1,0:T(8,128)(2,1)S(1)}, bf16[4,2,128,128]{3,2,1,0:T(8,128)(2,1)S(1)}) custom-call(s32[2]{0:T(128)S(1)} %pad_add_fusion.place_ref, bf16[4,2,2,4,128,128]{5,4,3,2,1,0:T(8,128)(2,1)S(1)} %arrange.1.qd_ref, bf16[4,2,640,512]{3,2,1,0:T(8,128)(2,1)S(1)} %get-tuple-element.35.p_ref, ...), custom_call_target="tpu_custom_call" | custom-call | flops 2684354560 | tf_op jit(solution)/shard_map/dscore/pallas_call | solution.py:40
  38.0 0.1 collective-permute-start.13
  38.1 0.1 collective-permute-start.14
  38.2 2.3 %collective-permute-done.9.refs_4_ = bf16[4,2,128,128]{3,2,1,0:T(8,128)(2,1)S(1)} collective-permute-done((bf16[4,2,128,128]{3,2,1,0:T(8,128)(2,1)S(1)}, bf16[4,2,128,128]{3,2,1,0:T(8,128)(2,1)S(1)}, u32[]{:S(2)}, u32[]{:S(2)}) %collective-permute-start.9) | collective-permute-done | bytes 262176 | tf_op jit(solution)/shard_map/ppermute | solution.py:23
  40.5 3.3 %own.1 = (bf16[128,16,128]{2,1,0:T(8,128)(2,1)S(1)}, bf16[56,16,128]{2,1,0:T(8,128)(2,1)S(1)}, bf16[56,16,128]{2,1,0:T(8,128)(2,1)S(1)}, bf16[48,16,128]{2,1,0:T...) custom-call(s32[2]{0:T(128)S(1)} %pad_add_fusion.place_ref, ...), custom_call_target="tpu_custom_call" | custom-call | tf_op jit(solution)/shard_map/own/pallas_call | solution.py:40
  43.8 6.7 %collective-permute-start.10 = (bf16[56,16,128]{2,1,0:T(8,128)(2,1)S(1)}, bf16[56,16,128]{2,1,0:T(8,128)(2,1)S(1)}, u32[]{:S(2)}, u32[]{:S(2)}) collective-permute-start(bf16[56,16,128]{2,1,0:T(8,128)(2,1)S(1)} %get-tuple-element.43), channel_id=1, source_target_pairs={{0,1},{1,0},{2,3},{3,2},{4,5},{5,4},{6,7},{7,6},{8,9},{9,8},{10,11... | collective-permute-start | bytes 688136 | tf_op jit(solution)/shard_map/ppermute | solution.py:27
  50.6 0.1 collective-permute-start.11
  50.7 0.4 collective-permute-start.12
  51.1 1.3 %collective-permute-done.12.refs_2_ = bf16[48,16,128]{2,1,0:T(8,128)(2,1)S(1)} collective-permute-done((bf16[48,16,128]{2,1,0:T(8,128)(2,1)S(1)}, bf16[48,16,128]{2,1,0:T(8,128)(2,1)S(1)}, u32[]{:S(2)}, u32[]{:S(2)}) %collective-permute-start.12) | collective-permute-done | bytes 196640 | tf_op jit(solution)/shard_map/ppermute | solution.py:27
  52.4 2.2 %join.1 = (bf16[128,32,128]{2,1,0:T(8,128)(2,1)}, bf16[128,8,128]{2,1,0:T(8,128)(2,1)}) custom-call(s32[2]{0:T(128)S(1)} %pad_add_fusion.place_ref, bf16[128,16,128]{2,1,0:T(8,128)(2,1)S(1)} %get-tuple-element.41.dq_ref, bf16[4,128,128]{2,1,0:T(8,128)(2,1)S(1)} %get-tuple-element.42.dv_ref, bf16[56,16,128]{2,1,0:T(8,128)(2,1)S(1)} %collective-permute-done.10.refs_0_, ...), custom_call_target="tpu_custom_call" | custom-call | tf_op jit(solution)/shard_map/join/pallas_call | solution.py:40
  54.6 0.6 %sum_dk.1 = (bf16[4,128,128]{2,1,0:T(8,128)(2,1)S(1)}, bf16[4,128,128]{2,1,0:T(8,128)(2,1)S(1)}) custom-call(s32[2]{0:T(128)S(1)} %pad_add_fusion.place_ref, f32[4,2,128,128]{3,2,1,0:T(8,128)S(1)} %get-tuple-element.47.own_ref, bf16[4,2,128,128]{3,2,1,0:T(8,128)(2,1)S(1)} %collective-permute-done.13.refs_0_, ...), custom_call_target="tpu_custom_call" | custom-call | tf_op jit(solution)/shard_map/sum_dk/pallas_call | solution.py:40
  55.3 0.9 %collective-permute-start.15 = (bf16[4,128,128]{2,1,0:T(8,128)(2,1)S(1)}, bf16[4,128,128]{2,1,0:T(8,128)(2,1)S(1)}, u32[]{:S(2)}, u32[]{:S(2)}) collective-permute-start(bf16[4,128,128]{2,1,0:T(8,128)(2,1)S(1)} %get-tuple-element.52), channel_id=1, source_target_pairs={{0,1},{1,0},{2,3},{3,2},{4,5},{5,4},{6,7},{7,6},{8,9},{9,8},{10,11... | collective-permute-start | bytes 393224 | tf_op jit(solution)/shard_map/ppermute | solution.py:27
  56.1 1.0 %collective-permute-done.15.other_ref = bf16[4,128,128]{2,1,0:T(8,128)(2,1)S(1)} collective-permute-done((bf16[4,128,128]{2,1,0:T(8,128)(2,1)S(1)}, bf16[4,128,128]{2,1,0:T(8,128)(2,1)S(1)}, u32[]{:S(2)}, u32[]{:S(2)}) %collective-permute-start.15) | collective-permute-done | bytes 131104 | tf_op jit(solution)/shard_map/ppermute | solution.py:27
  57.1 1.4 %merge_dk.1 = bf16[128,8,128]{2,1,0:T(8,128)(2,1)} custom-call(s32[2]{0:T(128)S(1)} %pad_add_fusion.place_ref, bf16[4,128,128]{2,1,0:T(8,128)(2,1)S(1)} %get-tuple-element.51.own_ref, bf16[4,128,128]{2,1,0:T(8,128)(2,1)S(1)} %collective-permute-done.15.other_ref), custom_call_target="tpu_custom_call" | custom-call | tf_op jit(solution)/shard_map/merge_dk/pallas_call | solution.py:40
  (17 shorter events, 0.0 us)
Async XLA Ops:
  0.6 3.2 %copy-start.1 = (bf16[128,32,128]{2,1,0:T(8,128)(2,1)S(1)}, bf16[128,32,128]{2,1,0:T(8,128)(2,1)}, u32[]{:S(2)}) copy-start(bf16[128,32,128]{2,1,0:T(8,128)(2,1)} %do_ref) | copy-start | bytes 3145732
  0.6 3.1 %copy-start = (bf16[128,32,128]{2,1,0:T(8,128)(2,1)S(1)}, bf16[128,32,128]{2,1,0:T(8,128)(2,1)}, u32[]{:S(2)}) copy-start(bf16[128,32,128]{2,1,0:T(8,128)(2,1)} %q_ref) | copy-start | bytes 3145732
  0.6 2.4 %collective-permute-start = (bf16[128,8,128]{2,1,0:T(8,128)(2,1)}, bf16[128,8,128]{2,1,0:T(8,128)(2,1)S(1)}, u32[]{:S(2)}, u32[]{:S(2)}) collective-permute-start(bf16[128,8,128]{2,1,0:T(8,128)(2,1)} %key_ref.1), channel_id=1, source_target_pairs={{0,1},{1,0},{2,3},{3,2},{4,5},{5,4},{6,7},{7,6},{8,9},{9,8},{10,11... | collective-permute-start | bytes 786440 | tf_op jit(solution)/shard_map/ppermute | solution.py:27
  3.7 13.8 %copy-start.2 = (s32[16]{0:T(128)S(1)}, s32[16]{0:T(128)}, u32[]{:S(2)}) copy-start(s32[16]{0:T(128)} %lengths_ref.1) | copy-start | bytes 196
  3.7 3.1 %collective-permute-start.1 = (bf16[128,32,128]{2,1,0:T(8,128)(2,1)S(1)}, bf16[128,32,128]{2,1,0:T(8,128)(2,1)S(1)}, u32[]{:S(2)}, u32[]{:S(2)}) collective-permute-start(bf16[128,32,128]{2,1,0:T(8,128)(2,1)S(1)} %copy-done), channel_id=1, source_target_pairs={{0,1},{1,0},{2,3},{3,2},{4,5},{5,4},{6,7},{7,6},{8,9},{9,8},{10,11... | collective-permute-start | bytes 3145736 | tf_op jit(solution)/shard_map/ppermute | solution.py:27
  3.9 4.1 %collective-permute-start.2 = (bf16[128,32,128]{2,1,0:T(8,128)(2,1)S(1)}, bf16[128,32,128]{2,1,0:T(8,128)(2,1)S(1)}, u32[]{:S(2)}, u32[]{:S(2)}) collective-permute-start(bf16[128,32,128]{2,1,0:T(8,128)(2,1)S(1)} %copy-done.1), channel_id=1, source_target_pairs={{0,1},{1,0},{2,3},{3,2},{4,5},{5,4},{6,7},{7,6},{8,9},{9,8},{10,11... | collective-permute-start | bytes 3145736 | tf_op jit(solution)/shard_map/ppermute | solution.py:27
  4.3 5.7 %collective-permute-start.3 = (bf16[128,8,128]{2,1,0:T(8,128)(2,1)S(1)}, bf16[128,8,128]{2,1,0:T(8,128)(2,1)S(1)}, u32[]{:S(2)}, u32[]{:S(2)}) collective-permute-start(bf16[128,8,128]{2,1,0:T(8,128)(2,1)S(1)} %get-tuple-element.36.own_ref), channel_id=1, source_target_pairs={{0,1},{1,0},{2,3},{3,2},{4,5},{5,4},{6,7},{7,6},{8,9},{9,8},{10,11... | collective-permute-start | bytes 786440 | tf_op jit(solution)/shard_map/ppermute | solution.py:27
  4.4 12.6 %collective-permute-start.5 = (bf16[4,2,128,128]{3,2,1,0:T(8,128)(2,1)S(1)}, bf16[4,2,128,128]{3,2,1,0:T(8,128)(2,1)S(1)}, u32[]{:S(2)}, u32[]{:S(2)}) collective-permute-start(bf16[4,2,128,128]{3,2,1,0:T(8,128)(2,1)S(1)} %pack_other.1.refs_0_), channel_id=1, source_target_pairs={{0,4},{1,5},{2,6},{3,7},{4,8},{5,9},{6,10},{7,11},{8,12},{9,13},{1... | collective-permute-start | bytes 786440 | tf_op jit(solution)/shard_map/ppermute | solution.py:22
  5.6 11.9 %collective-permute-start.4 = (bf16[4,2,128,128]{3,2,1,0:T(8,128)(2,1)S(1)}, bf16[4,2,128,128]{3,2,1,0:T(8,128)(2,1)S(1)}, u32[]{:S(2)}, u32[]{:S(2)}) collective-permute-start(bf16[4,2,128,128]{3,2,1,0:T(8,128)(2,1)S(1)} %pack_other.1.refs_0_), channel_id=1, source_target_pairs={{0,2},{1,3},{2,4},{3,5},{4,6},{5,7},{6,8},{7,9},{8,10},{9,11},{10,... | collective-permute-start | bytes 786440 | tf_op jit(solution)/shard_map/ppermute | solution.py:22
  10.7 21.7 %collective-permute-start.7 = (bf16[4,2,128,128]{3,2,1,0:T(8,128)(2,1)S(1)}, bf16[4,2,128,128]{3,2,1,0:T(8,128)(2,1)S(1)}, u32[]{:S(2)}, u32[]{:S(2)}) collective-permute-start(bf16[4,2,128,128]{3,2,1,0:T(8,128)(2,1)S(1)} %pack_both.1.refs_0_), channel_id=1, source_target_pairs={{0,4},{1,5},{2,6},{3,7},{4,8},{5,9},{6,10},{7,11},{8,12},{9,13},{1... | collective-permute-start | bytes 786440 | tf_op jit(solution)/shard_map/ppermute | solution.py:23
  13.9 18.6 %collective-permute-start.6 = (bf16[4,2,128,128]{3,2,1,0:T(8,128)(2,1)S(1)}, bf16[4,2,128,128]{3,2,1,0:T(8,128)(2,1)S(1)}, u32[]{:S(2)}, u32[]{:S(2)}) collective-permute-start(bf16[4,2,128,128]{3,2,1,0:T(8,128)(2,1)S(1)} %pack_both.1.refs_0_), channel_id=1, source_target_pairs={{0,2},{1,3},{2,4},{3,5},{4,6},{5,7},{6,8},{7,9},{8,10},{9,11},{10,... | collective-permute-start | bytes 786440 | tf_op jit(solution)/shard_map/ppermute | solution.py:23
  24.0 14.2 %collective-permute-start.8 = (bf16[4,2,128,128]{3,2,1,0:T(8,128)(2,1)S(1)}, bf16[4,2,128,128]{3,2,1,0:T(8,128)(2,1)S(1)}, u32[]{:S(2)}, u32[]{:S(2)}) collective-permute-start(bf16[4,2,128,128]{3,2,1,0:T(8,128)(2,1)S(1)} %get-tuple-element.39), channel_id=1, source_target_pairs={{4,0},{5,1},{6,2},{7,3},{8,4},{9,5},{10,6},{11,7},{12,8},{13,9},{1... | collective-permute-start | bytes 786440 | tf_op jit(solution)/shard_map/ppermute | solution.py:23
  25.9 14.6 %collective-permute-start.9 = (bf16[4,2,128,128]{3,2,1,0:T(8,128)(2,1)S(1)}, bf16[4,2,128,128]{3,2,1,0:T(8,128)(2,1)S(1)}, u32[]{:S(2)}, u32[]{:S(2)}) collective-permute-start(bf16[4,2,128,128]{3,2,1,0:T(8,128)(2,1)S(1)} %get-tuple-element.40), channel_id=1, source_target_pairs={{2,0},{3,1},{4,2},{5,3},{6,4},{7,5},{8,6},{9,7},{10,8},{11,9},{12,... | collective-permute-start | bytes 786440 | tf_op jit(solution)/shard_map/ppermute | solution.py:23
  38.0 16.6 %collective-permute-start.13 = (bf16[4,2,128,128]{3,2,1,0:T(8,128)(2,1)S(1)}, bf16[4,2,128,128]{3,2,1,0:T(8,128)(2,1)S(1)}, u32[]{:S(2)}, u32[]{:S(2)}) collective-permute-start(bf16[4,2,128,128]{3,2,1,0:T(8,128)(2,1)S(1)} %get-tuple-element.48), channel_id=1, source_target_pairs={{0,28},{1,29},{2,30},{3,31},{4,0},{5,1},{6,2},{7,3},{8,4},{9,5},{1... | collective-permute-start | bytes 786440 | tf_op jit(solution)/shard_map/ppermute | solution.py:22
  38.1 16.5 %collective-permute-start.14 = (bf16[4,2,128,128]{3,2,1,0:T(8,128)(2,1)S(1)}, bf16[4,2,128,128]{3,2,1,0:T(8,128)(2,1)S(1)}, u32[]{:S(2)}, u32[]{:S(2)}) collective-permute-start(bf16[4,2,128,128]{3,2,1,0:T(8,128)(2,1)S(1)} %get-tuple-element.49), channel_id=1, source_target_pairs={{0,30},{1,31},{2,0},{3,1},{4,2},{5,3},{6,4},{7,5},{8,6},{9,7},{10,... | collective-permute-start | bytes 786440 | tf_op jit(solution)/shard_map/ppermute | solution.py:22
  43.8 8.5 %collective-permute-start.10 = (bf16[56,16,128]{2,1,0:T(8,128)(2,1)S(1)}, bf16[56,16,128]{2,1,0:T(8,128)(2,1)S(1)}, u32[]{:S(2)}, u32[]{:S(2)}) collective-permute-start(bf16[56,16,128]{2,1,0:T(8,128)(2,1)S(1)} %get-tuple-element.43), channel_id=1, source_target_pairs={{0,1},{1,0},{2,3},{3,2},{4,5},{5,4},{6,7},{7,6},{8,9},{9,8},{10,11... | collective-permute-start | bytes 688136 | tf_op jit(solution)/shard_map/ppermute | solution.py:27
  50.6 1.8 %collective-permute-start.11 = (bf16[56,16,128]{2,1,0:T(8,128)(2,1)S(1)}, bf16[56,16,128]{2,1,0:T(8,128)(2,1)S(1)}, u32[]{:S(2)}, u32[]{:S(2)}) collective-permute-start(bf16[56,16,128]{2,1,0:T(8,128)(2,1)S(1)} %get-tuple-element.44), channel_id=1, source_target_pairs={{0,1},{1,0},{2,3},{3,2},{4,5},{5,4},{6,7},{7,6},{8,9},{9,8},{10,11... | collective-permute-start | bytes 688136 | tf_op jit(solution)/shard_map/ppermute | solution.py:27
  50.7 1.7 %collective-permute-start.12 = (bf16[48,16,128]{2,1,0:T(8,128)(2,1)S(1)}, bf16[48,16,128]{2,1,0:T(8,128)(2,1)S(1)}, u32[]{:S(2)}, u32[]{:S(2)}) collective-permute-start(bf16[48,16,128]{2,1,0:T(8,128)(2,1)S(1)} %get-tuple-element.45), channel_id=1, source_target_pairs={{0,1},{1,0},{2,3},{3,2},{4,5},{5,4},{6,7},{7,6},{8,9},{9,8},{10,11... | collective-permute-start | bytes 589832 | tf_op jit(solution)/shard_map/ppermute | solution.py:27
  55.3 1.8 %collective-permute-start.15 = (bf16[4,128,128]{2,1,0:T(8,128)(2,1)S(1)}, bf16[4,128,128]{2,1,0:T(8,128)(2,1)S(1)}, u32[]{:S(2)}, u32[]{:S(2)}) collective-permute-start(bf16[4,128,128]{2,1,0:T(8,128)(2,1)S(1)} %get-tuple-element.52), channel_id=1, source_target_pairs={{0,1},{1,0},{2,3},{3,2},{4,5},{5,4},{6,7},{7,6},{8,9},{9,8},{10,11... | collective-permute-start | bytes 393224 | tf_op jit(solution)/shard_map/ppermute | solution.py:27

commit v21 on v20

--- a/solution.py
+++ b/solution.py
@@ -493,7 +493,8 @@
     product = 2 * half * 2 * count * tokens * group * tokens * dim
 
     k_pairs = halo_of(k_own, ring=True)
-    v_pairs = halo_of(v_own, ring=False)
+    k_pairs[-1], v_own = lax.optimization_barrier((k_pairs[-1], v_own))
+    v_pairs = halo_of(v_own, ring=True)
     prob, *dv_halo = call(
         functools.partial(prob_kernel, halo),
         "prob",

time: 59.1 us -> 60.4 us (1.022)
  the two profiles are of different devices: /device:TPU:23 before, /device:TPU:19 now
where the time goes in v21:
time: 60.4 us; the launch traced here: 60.2 us
  starting transfers between devices  29.3 us (49%)
  Pallas kernels  24.6 us (41%)
  waiting for transfers between devices  5.44 us (9%)
  between operations  0.8 us (1%)
    pallas_call x10, Pallas kernels, call(): pl.pallas_call(kernel, out_shape=outs, grid_spec=pltpu.PrefetchScalarGrid...  24.6 us
    ppermute x8, starting transfers between devices, swapped(): return lax.ppermute(array, AXES, [(d, d ^ 1) for d in range(device_count)])  12.1 us
    ppermute x6, starting transfers between devices, moved(): lax.ppermute(array, AXES, [(d, to % device_count) for d, to in pairs])  11.3 us
    ppermute x2, starting transfers between devices, moved(): lax.ppermute(array, AXES, [(d, to) for d, to in pairs if 0 <= to < device...  5.92 us
    ppermute x8, waiting for transfers between devices, swapped(): return lax.ppermute(array, AXES, [(d, d ^ 1) for d in range(device_count)])  3.4 us
    ppermute x6, waiting for transfers between devices, moved(): lax.ppermute(array, AXES, [(d, to % device_count) for d, to in pairs])  2.04 us
  transfers between devices with their start and end apart: 16, of which 4 were waited for; matrix products, arithmetic and copies ran while one was open for 0% of the time, Pallas kernels for 36%

profile of v21, /device:TPU:19, one launch (start us, length us, event | category | flops | bytes accessed | tf_op | source)
XLA Modules:
  0.0 60.2 jit_solution(3816965002415888059)
XLA Ops:
  0.6 0.7 %collective-permute-start = (bf16[128,8,128]{2,1,0:T(8,128)(2,1)}, bf16[128,8,128]{2,1,0:T(8,128)(2,1)S(1)}, u32[]{:S(2)}, u32[]{:S(2)}) collective-permute-start(bf16[128,8,128]{2,1,0:T(8,128)(2,1)} %key_ref.1), channel_id=1, source_target_pairs={{0,1},{1,0},{2,3},{3,2},{4,5},{5,4},{6,7},{7,6},{8,9},{9,8},{10,11... | collective-permute-start | bytes 786440 | tf_op jit(solution)/shard_map/ppermute | solution.py:27
  1.4 0.1 pad_add_fusion.place_ref
  1.5 1.6 %fetch.1 = (bf16[4,2,128,128]{3,2,1,0:T(8,128)(2,1)S(1)}, bf16[128,8,128]{2,1,0:T(8,128)(2,1)S(1)}) custom-call(s32[2]{0:T(128)S(1)} %pad_add_fusion.place_ref, bf16[128,8,128]{2,1,0:T(8,128)(2,1)} %key_ref.1, bf16[128,8,128]{2,1,0:T(8,128)(2,1)} %refs_0_.1), custom_call_target="tpu_custom_call" | custom-call | flops 1000000000 | tf_op jit(solution)/shard_map/fetch/pallas_call | solution.py:40
  3.1 0.6 %pack_other.1.refs_0_ = bf16[4,2,128,128]{3,2,1,0:T(8,128)(2,1)S(1)} custom-call(s32[2]{0:T(128)S(1)} %pad_add_fusion.place_ref, bf16[128,8,128]{2,1,0:T(8,128)(2,1)S(1)} %collective-permute-done.other_ref, bf16[4,2,128,128]{3,2,1,0:T(8,128)(2,1)S(1)} %get-tuple-element.30._), custom_call_target="tpu_custom_call", output_to_operand_aliasing={{}: (2, {})} | custom-call | flops 1000000000 | tf_op jit(solution)/shard_map/pack_other/pallas_call | solution.py:40
  3.7 0.0 copy-start.2
  3.7 0.1 collective-permute-start.1
  3.9 0.4 collective-permute-start.2
  4.3 0.1 collective-permute-start.3
  4.4 1.2 %collective-permute-start.5 = (bf16[4,2,128,128]{3,2,1,0:T(8,128)(2,1)S(1)}, bf16[4,2,128,128]{3,2,1,0:T(8,128)(2,1)S(1)}, u32[]{:S(2)}, u32[]{:S(2)}) collective-permute-start(bf16[4,2,128,128]{3,2,1,0:T(8,128)(2,1)S(1)} %pack_other.1.refs_0_), channel_id=1, source_target_pairs={{0,4},{1,5},{2,6},{3,7},{4,8},{5,9},{6,10},{7,11},{8,12},{9,13},{1... | collective-permute-start | bytes 786440 | tf_op jit(solution)/shard_map/ppermute | solution.py:22
  5.6 1.2 %collective-permute-start.4 = (bf16[4,2,128,128]{3,2,1,0:T(8,128)(2,1)S(1)}, bf16[4,2,128,128]{3,2,1,0:T(8,128)(2,1)S(1)}, u32[]{:S(2)}, u32[]{:S(2)}) collective-permute-start(bf16[4,2,128,128]{3,2,1,0:T(8,128)(2,1)S(1)} %pack_other.1.refs_0_), channel_id=1, source_target_pairs={{0,2},{1,3},{2,4},{3,5},{4,6},{5,7},{6,8},{7,9},{8,10},{9,11},{10,... | collective-permute-start | bytes 786440 | tf_op jit(solution)/shard_map/ppermute | solution.py:22
  6.8 1.1 %collective-permute-done.2.do_other_ref = bf16[128,32,128]{2,1,0:T(8,128)(2,1)S(1)} collective-permute-done((bf16[128,32,128]{2,1,0:T(8,128)(2,1)S(1)}, bf16[128,32,128]{2,1,0:T(8,128)(2,1)S(1)}, u32[]{:S(2)}, u32[]{:S(2)}) %collective-permute-start.2) | collective-permute-done | bytes 1048608 | tf_op jit(solution)/shard_map/ppermute | solution.py:27
  7.9 2.0 %arrange.1.qd_ref = bf16[4,2,2,4,128,128]{5,4,3,2,1,0:T(8,128)(2,1)S(1)} custom-call(s32[2]{0:T(128)S(1)} %pad_add_fusion.place_ref, bf16[128,32,128]{2,1,0:T(8,128)(2,1)S(1)} %copy-done, bf16[128,32,128]{2,1,0:T(8,128)(2,1)S(1)} %copy-done.1, bf16[128,32,128]{2,1,0:T(8,128)(2,1)S(1)} %collective-permute-done.1.q_other_ref, ...), custom_call_target="tpu_custom_call" | custom-call | flops 1000000000 | tf_op jit(solution)/shard_map/arrange/pallas_call | solution.py:40
  10.0 0.7 %pack_both.1.refs_0_ = bf16[4,2,128,128]{3,2,1,0:T(8,128)(2,1)S(1)} custom-call(s32[2]{0:T(128)S(1)} %pad_add_fusion.place_ref, bf16[128,8,128]{2,1,0:T(8,128)(2,1)S(1)} %get-tuple-element.37.own_ref, bf16[128,8,128]{2,1,0:T(8,128)(2,1)S(1)} %collective-permute-done.3.other_ref), custom_call_target="tpu_custom_call" | custom-call | flops 1000000000 | tf_op jit(solution)/shard_map/pack_both/pallas_call | solution.py:40
  10.7 2.0 %collective-permute-done.5.refs_2_ = bf16[4,2,128,128]{3,2,1,0:T(8,128)(2,1)S(1)} collective-permute-done((bf16[4,2,128,128]{3,2,1,0:T(8,128)(2,1)S(1)}, bf16[4,2,128,128]{3,2,1,0:T(8,128)(2,1)S(1)}, u32[]{:S(2)}, u32[]{:S(2)}) %collective-permute-start.5) | collective-permute-done | bytes 262176 | tf_op jit(solution)/shard_map/ppermute | solution.py:22
  12.7 0.3 collective-permute-start.7
  13.1 5.9 %collective-permute-start.6 = (bf16[4,2,128,128]{3,2,1,0:T(8,128)(2,1)S(1)}, bf16[4,2,128,128]{3,2,1,0:T(8,128)(2,1)S(1)}, u32[]{:S(2)}, u32[]{:S(2)}) collective-permute-start(bf16[4,2,128,128]{3,2,1,0:T(8,128)(2,1)S(1)} %pack_both.1.refs_0_), channel_id=1, source_target_pairs={{0,2},{1,3},{2,4},{3,5},{4,6},{5,7},{6,8},{7,9},{8,10},{9,11},{10,... | collective-permute-start | bytes 786440 | tf_op jit(solution)/shard_map/ppermute | solution.py:22
  19.0 6.4 %prob.1 = (bf16[4,2,640,512]{3,2,1,0:T(8,128)(2,1)S(1)}, bf16[4,2,128,128]{3,2,1,0:T(8,128)(2,1)S(1)}, bf16[4,2,128,128]{3,2,1,0:T(8,128)(2,1)S(1)}) custom-call(s32[2]{0:T(128)S(1)} %pad_add_fusion.place_ref, s32[16]{0:T(128)S(1)} %copy-done.2, bf16[4,2,2,4,128,128]{5,4,3,2,1,0:T(8,128)(2,1)S(1)} %arrange.1.qd_ref, ...), custom_call_target="tpu_custom_call" | custom-call | flops 2684354560 | tf_op jit(solution)/shard_map/prob/pallas_call | solution.py:40
  25.4 4.0 %collective-permute-start.8 = (bf16[4,2,128,128]{3,2,1,0:T(8,128)(2,1)S(1)}, bf16[4,2,128,128]{3,2,1,0:T(8,128)(2,1)S(1)}, u32[]{:S(2)}, u32[]{:S(2)}) collective-permute-start(bf16[4,2,128,128]{3,2,1,0:T(8,128)(2,1)S(1)} %get-tuple-element.43), channel_id=1, source_target_pairs={{4,0},{5,1},{6,2},{7,3},{8,4},{9,5},{10,6},{11,7},{12,8},{13,9},{1... | collective-permute-start | bytes 786440 | tf_op jit(solution)/shard_map/ppermute | solution.py:23
  29.4 1.9 %collective-permute-start.9 = (bf16[4,2,128,128]{3,2,1,0:T(8,128)(2,1)S(1)}, bf16[4,2,128,128]{3,2,1,0:T(8,128)(2,1)S(1)}, u32[]{:S(2)}, u32[]{:S(2)}) collective-permute-start(bf16[4,2,128,128]{3,2,1,0:T(8,128)(2,1)S(1)} %get-tuple-element.44), channel_id=1, source_target_pairs={{2,0},{3,1},{4,2},{5,3},{6,4},{7,5},{8,6},{9,7},{10,8},{11,9},{12,... | collective-permute-start | bytes 786440 | tf_op jit(solution)/shard_map/ppermute | solution.py:23
  31.4 5.6 %dscore.1 = (bf16[4,2,640,512]{3,2,1,0:T(8,128)(2,1)S(1)}, bf16[4,2,128,128]{3,2,1,0:T(8,128)(2,1)S(1)}, bf16[4,2,128,128]{3,2,1,0:T(8,128)(2,1)S(1)}) custom-call(s32[2]{0:T(128)S(1)} %pad_add_fusion.place_ref, bf16[4,2,2,4,128,128]{5,4,3,2,1,0:T(8,128)(2,1)S(1)} %arrange.1.qd_ref, bf16[4,2,640,512]{3,2,1,0:T(8,128)(2,1)S(1)} %get-tuple-element.40.p_ref, ...), custom_call_target="tpu_custom_call" | custom-call | flops 2684354560 | tf_op jit(solution)/shard_map/dscore/pallas_call | solution.py:40
  37.0 0.1 collective-permute-start.13
  37.0 2.5 %collective-permute-start.14 = (bf16[4,2,128,128]{3,2,1,0:T(8,128)(2,1)S(1)}, bf16[4,2,128,128]{3,2,1,0:T(8,128)(2,1)S(1)}, u32[]{:S(2)}, u32[]{:S(2)}) collective-permute-start(bf16[4,2,128,128]{3,2,1,0:T(8,128)(2,1)S(1)} %get-tuple-element.53), channel_id=1, source_target_pairs={{0,30},{1,31},{2,0},{3,1},{4,2},{5,3},{6,4},{7,5},{8,6},{9,7},{10,... | collective-permute-start | bytes 786440 | tf_op jit(solution)/shard_map/ppermute | solution.py:22
  39.6 3.3 %own.1 = (bf16[128,16,128]{2,1,0:T(8,128)(2,1)S(1)}, bf16[56,16,128]{2,1,0:T(8,128)(2,1)S(1)}, bf16[56,16,128]{2,1,0:T(8,128)(2,1)S(1)}, bf16[48,16,128]{2,1,0:T...) custom-call(s32[2]{0:T(128)S(1)} %pad_add_fusion.place_ref, ...), custom_call_target="tpu_custom_call" | custom-call | tf_op jit(solution)/shard_map/own/pallas_call | solution.py:40
  42.9 9.8 %collective-permute-start.10 = (bf16[56,16,128]{2,1,0:T(8,128)(2,1)S(1)}, bf16[56,16,128]{2,1,0:T(8,128)(2,1)S(1)}, u32[]{:S(2)}, u32[]{:S(2)}) collective-permute-start(bf16[56,16,128]{2,1,0:T(8,128)(2,1)S(1)} %get-tuple-element.47), channel_id=1, source_target_pairs={{0,1},{1,0},{2,3},{3,2},{4,5},{5,4},{6,7},{7,6},{8,9},{9,8},{10,11... | collective-permute-start | bytes 688136 | tf_op jit(solution)/shard_map/ppermute | solution.py:27
  52.7 0.1 collective-permute-start.11
  52.8 0.4 collective-permute-start.12
  53.3 1.3 %collective-permute-done.12.refs_2_ = bf16[48,16,128]{2,1,0:T(8,128)(2,1)S(1)} collective-permute-done((bf16[48,16,128]{2,1,0:T(8,128)(2,1)S(1)}, bf16[48,16,128]{2,1,0:T(8,128)(2,1)S(1)}, u32[]{:S(2)}, u32[]{:S(2)}) %collective-permute-start.12) | collective-permute-done | bytes 196640 | tf_op jit(solution)/shard_map/ppermute | solution.py:27
  54.5 2.2 %join.1 = (bf16[128,32,128]{2,1,0:T(8,128)(2,1)}, bf16[128,8,128]{2,1,0:T(8,128)(2,1)}) custom-call(s32[2]{0:T(128)S(1)} %pad_add_fusion.place_ref, bf16[128,16,128]{2,1,0:T(8,128)(2,1)S(1)} %get-tuple-element.45.dq_ref, bf16[4,128,128]{2,1,0:T(8,128)(2,1)S(1)} %get-tuple-element.46.dv_ref, bf16[56,16,128]{2,1,0:T(8,128)(2,1)S(1)} %collective-permute-done.10.refs_0_, ...), custom_call_target="tpu_custom_call" | custom-call | tf_op jit(solution)/shard_map/join/pallas_call | solution.py:40
  56.8 0.6 %sum_dk.1 = (bf16[4,128,128]{2,1,0:T(8,128)(2,1)S(1)}, bf16[4,128,128]{2,1,0:T(8,128)(2,1)S(1)}) custom-call(s32[2]{0:T(128)S(1)} %pad_add_fusion.place_ref, f32[4,2,128,128]{3,2,1,0:T(8,128)S(1)} %get-tuple-element.51.own_ref, bf16[4,2,128,128]{3,2,1,0:T(8,128)(2,1)S(1)} %collective-permute-done.13.refs_0_, ...), custom_call_target="tpu_custom_call" | custom-call | tf_op jit(solution)/shard_map/sum_dk/pallas_call | solution.py:40
  57.4 0.4 collective-permute-start.15
  57.8 1.0 %collective-permute-done.15.other_ref = bf16[4,128,128]{2,1,0:T(8,128)(2,1)S(1)} collective-permute-done((bf16[4,128,128]{2,1,0:T(8,128)(2,1)S(1)}, bf16[4,128,128]{2,1,0:T(8,128)(2,1)S(1)}, u32[]{:S(2)}, u32[]{:S(2)}) %collective-permute-start.15) | collective-permute-done | bytes 131104 | tf_op jit(solution)/shard_map/ppermute | solution.py:27
  58.8 1.4 %merge_dk.1 = bf16[128,8,128]{2,1,0:T(8,128)(2,1)} custom-call(s32[2]{0:T(128)S(1)} %pad_add_fusion.place_ref, bf16[4,128,128]{2,1,0:T(8,128)(2,1)S(1)} %get-tuple-element.55.own_ref, bf16[4,128,128]{2,1,0:T(8,128)(2,1)S(1)} %collective-permute-done.15.other_ref), custom_call_target="tpu_custom_call" | custom-call | tf_op jit(solution)/shard_map/merge_dk/pallas_call | solution.py:40
  (17 shorter events, 0.0 us)
Async XLA Ops:
  0.6 3.2 %copy-start.1 = (bf16[128,32,128]{2,1,0:T(8,128)(2,1)S(1)}, bf16[128,32,128]{2,1,0:T(8,128)(2,1)}, u32[]{:S(2)}) copy-start(bf16[128,32,128]{2,1,0:T(8,128)(2,1)} %do_ref) | copy-start | bytes 3145732
  0.6 3.1 %copy-start = (bf16[128,32,128]{2,1,0:T(8,128)(2,1)S(1)}, bf16[128,32,128]{2,1,0:T(8,128)(2,1)}, u32[]{:S(2)}) copy-start(bf16[128,32,128]{2,1,0:T(8,128)(2,1)} %q_ref) | copy-start | bytes 3145732
  0.6 2.4 %collective-permute-start = (bf16[128,8,128]{2,1,0:T(8,128)(2,1)}, bf16[128,8,128]{2,1,0:T(8,128)(2,1)S(1)}, u32[]{:S(2)}, u32[]{:S(2)}) collective-permute-start(bf16[128,8,128]{2,1,0:T(8,128)(2,1)} %key_ref.1), channel_id=1, source_target_pairs={{0,1},{1,0},{2,3},{3,2},{4,5},{5,4},{6,7},{7,6},{8,9},{9,8},{10,11... | collective-permute-start | bytes 786440 | tf_op jit(solution)/shard_map/ppermute | solution.py:27
  3.7 15.3 %copy-start.2 = (s32[16]{0:T(128)S(1)}, s32[16]{0:T(128)}, u32[]{:S(2)}) copy-start(s32[16]{0:T(128)} %lengths_ref.1) | copy-start | bytes 196
  3.7 3.1 %collective-permute-start.1 = (bf16[128,32,128]{2,1,0:T(8,128)(2,1)S(1)}, bf16[128,32,128]{2,1,0:T(8,128)(2,1)S(1)}, u32[]{:S(2)}, u32[]{:S(2)}) collective-permute-start(bf16[128,32,128]{2,1,0:T(8,128)(2,1)S(1)} %copy-done), channel_id=1, source_target_pairs={{0,1},{1,0},{2,3},{3,2},{4,5},{5,4},{6,7},{7,6},{8,9},{9,8},{10,11... | collective-permute-start | bytes 3145736 | tf_op jit(solution)/shard_map/ppermute | solution.py:27
  3.9 4.1 %collective-permute-start.2 = (bf16[128,32,128]{2,1,0:T(8,128)(2,1)S(1)}, bf16[128,32,128]{2,1,0:T(8,128)(2,1)S(1)}, u32[]{:S(2)}, u32[]{:S(2)}) collective-permute-start(bf16[128,32,128]{2,1,0:T(8,128)(2,1)S(1)} %copy-done.1), channel_id=1, source_target_pairs={{0,1},{1,0},{2,3},{3,2},{4,5},{5,4},{6,7},{7,6},{8,9},{9,8},{10,11... | collective-permute-start | bytes 3145736 | tf_op jit(solution)/shard_map/ppermute | solution.py:27
  4.3 5.7 %collective-permute-start.3 = (bf16[128,8,128]{2,1,0:T(8,128)(2,1)S(1)}, bf16[128,8,128]{2,1,0:T(8,128)(2,1)S(1)}, u32[]{:S(2)}, u32[]{:S(2)}) collective-permute-start(bf16[128,8,128]{2,1,0:T(8,128)(2,1)S(1)} %get-tuple-element.37.own_ref), channel_id=1, source_target_pairs={{0,1},{1,0},{2,3},{3,2},{4,5},{5,4},{6,7},{7,6},{8,9},{9,8},{10,11... | collective-permute-start | bytes 786440 | tf_op jit(solution)/shard_map/ppermute | solution.py:27
  4.4 8.4 %collective-permute-start.5 = (bf16[4,2,128,128]{3,2,1,0:T(8,128)(2,1)S(1)}, bf16[4,2,128,128]{3,2,1,0:T(8,128)(2,1)S(1)}, u32[]{:S(2)}, u32[]{:S(2)}) collective-permute-start(bf16[4,2,128,128]{3,2,1,0:T(8,128)(2,1)S(1)} %pack_other.1.refs_0_), channel_id=1, source_target_pairs={{0,4},{1,5},{2,6},{3,7},{4,8},{5,9},{6,10},{7,11},{8,12},{9,13},{1... | collective-permute-start | bytes 786440 | tf_op jit(solution)/shard_map/ppermute | solution.py:22
  5.6 13.3 %collective-permute-start.4 = (bf16[4,2,128,128]{3,2,1,0:T(8,128)(2,1)S(1)}, bf16[4,2,128,128]{3,2,1,0:T(8,128)(2,1)S(1)}, u32[]{:S(2)}, u32[]{:S(2)}) collective-permute-start(bf16[4,2,128,128]{3,2,1,0:T(8,128)(2,1)S(1)} %pack_other.1.refs_0_), channel_id=1, source_target_pairs={{0,2},{1,3},{2,4},{3,5},{4,6},{5,7},{6,8},{7,9},{8,10},{9,11},{10,... | collective-permute-start | bytes 786440 | tf_op jit(solution)/shard_map/ppermute | solution.py:22
  12.7 18.6 %collective-permute-start.7 = (bf16[4,2,128,128]{3,2,1,0:T(8,128)(2,1)S(1)}, bf16[4,2,128,128]{3,2,1,0:T(8,128)(2,1)S(1)}, u32[]{:S(2)}, u32[]{:S(2)}) collective-permute-start(bf16[4,2,128,128]{3,2,1,0:T(8,128)(2,1)S(1)} %pack_both.1.refs_0_), channel_id=1, source_target_pairs={{0,4},{1,5},{2,6},{3,7},{4,8},{5,9},{6,10},{7,11},{8,12},{9,13},{1... | collective-permute-start | bytes 786440 | tf_op jit(solution)/shard_map/ppermute | solution.py:22
  13.1 18.3 %collective-permute-start.6 = (bf16[4,2,128,128]{3,2,1,0:T(8,128)(2,1)S(1)}, bf16[4,2,128,128]{3,2,1,0:T(8,128)(2,1)S(1)}, u32[]{:S(2)}, u32[]{:S(2)}) collective-permute-start(bf16[4,2,128,128]{3,2,1,0:T(8,128)(2,1)S(1)} %pack_both.1.refs_0_), channel_id=1, source_target_pairs={{0,2},{1,3},{2,4},{3,5},{4,6},{5,7},{6,8},{7,9},{8,10},{9,11},{10,... | collective-permute-start | bytes 786440 | tf_op jit(solution)/shard_map/ppermute | solution.py:22
  25.4 14.1 %collective-permute-start.8 = (bf16[4,2,128,128]{3,2,1,0:T(8,128)(2,1)S(1)}, bf16[4,2,128,128]{3,2,1,0:T(8,128)(2,1)S(1)}, u32[]{:S(2)}, u32[]{:S(2)}) collective-permute-start(bf16[4,2,128,128]{3,2,1,0:T(8,128)(2,1)S(1)} %get-tuple-element.43), channel_id=1, source_target_pairs={{4,0},{5,1},{6,2},{7,3},{8,4},{9,5},{10,6},{11,7},{12,8},{13,9},{1... | collective-permute-start | bytes 786440 | tf_op jit(solution)/shard_map/ppermute | solution.py:23
  29.4 10.1 %collective-permute-start.9 = (bf16[4,2,128,128]{3,2,1,0:T(8,128)(2,1)S(1)}, bf16[4,2,128,128]{3,2,1,0:T(8,128)(2,1)S(1)}, u32[]{:S(2)}, u32[]{:S(2)}) collective-permute-start(bf16[4,2,128,128]{3,2,1,0:T(8,128)(2,1)S(1)} %get-tuple-element.44), channel_id=1, source_target_pairs={{2,0},{3,1},{4,2},{5,3},{6,4},{7,5},{8,6},{9,7},{10,8},{11,9},{12,... | collective-permute-start | bytes 786440 | tf_op jit(solution)/shard_map/ppermute | solution.py:23
  37.0 19.8 %collective-permute-start.13 = (bf16[4,2,128,128]{3,2,1,0:T(8,128)(2,1)S(1)}, bf16[4,2,128,128]{3,2,1,0:T(8,128)(2,1)S(1)}, u32[]{:S(2)}, u32[]{:S(2)}) collective-permute-start(bf16[4,2,128,128]{3,2,1,0:T(8,128)(2,1)S(1)} %get-tuple-element.52), channel_id=1, source_target_pairs={{0,28},{1,29},{2,30},{3,31},{4,0},{5,1},{6,2},{7,3},{8,4},{9,5},{1... | collective-permute-start | bytes 786440 | tf_op jit(solution)/shard_map/ppermute | solution.py:22
  37.0 19.8 %collective-permute-start.14 = (bf16[4,2,128,128]{3,2,1,0:T(8,128)(2,1)S(1)}, bf16[4,2,128,128]{3,2,1,0:T(8,128)(2,1)S(1)}, u32[]{:S(2)}, u32[]{:S(2)}) collective-permute-start(bf16[4,2,128,128]{3,2,1,0:T(8,128)(2,1)S(1)} %get-tuple-element.53), channel_id=1, source_target_pairs={{0,30},{1,31},{2,0},{3,1},{4,2},{5,3},{6,4},{7,5},{8,6},{9,7},{10,... | collective-permute-start | bytes 786440 | tf_op jit(solution)/shard_map/ppermute | solution.py:22
  42.9 11.6 %collective-permute-start.10 = (bf16[56,16,128]{2,1,0:T(8,128)(2,1)S(1)}, bf16[56,16,128]{2,1,0:T(8,128)(2,1)S(1)}, u32[]{:S(2)}, u32[]{:S(2)}) collective-permute-start(bf16[56,16,128]{2,1,0:T(8,128)(2,1)S(1)} %get-tuple-element.47), channel_id=1, source_target_pairs={{0,1},{1,0},{2,3},{3,2},{4,5},{5,4},{6,7},{7,6},{8,9},{9,8},{10,11... | collective-permute-start | bytes 688136 | tf_op jit(solution)/shard_map/ppermute | solution.py:27
  52.7 1.8 %collective-permute-start.11 = (bf16[56,16,128]{2,1,0:T(8,128)(2,1)S(1)}, bf16[56,16,128]{2,1,0:T(8,128)(2,1)S(1)}, u32[]{:S(2)}, u32[]{:S(2)}) collective-permute-start(bf16[56,16,128]{2,1,0:T(8,128)(2,1)S(1)} %get-tuple-element.48), channel_id=1, source_target_pairs={{0,1},{1,0},{2,3},{3,2},{4,5},{5,4},{6,7},{7,6},{8,9},{9,8},{10,11... | collective-permute-start | bytes 688136 | tf_op jit(solution)/shard_map/ppermute | solution.py:27
  52.8 1.7 %collective-permute-start.12 = (bf16[48,16,128]{2,1,0:T(8,128)(2,1)S(1)}, bf16[48,16,128]{2,1,0:T(8,128)(2,1)S(1)}, u32[]{:S(2)}, u32[]{:S(2)}) collective-permute-start(bf16[48,16,128]{2,1,0:T(8,128)(2,1)S(1)} %get-tuple-element.49), channel_id=1, source_target_pairs={{0,1},{1,0},{2,3},{3,2},{4,5},{5,4},{6,7},{7,6},{8,9},{9,8},{10,11... | collective-permute-start | bytes 589832 | tf_op jit(solution)/shard_map/ppermute | solution.py:27
  57.4 1.4 %collective-permute-start.15 = (bf16[4,128,128]{2,1,0:T(8,128)(2,1)S(1)}, bf16[4,128,128]{2,1,0:T(8,128)(2,1)S(1)}, u32[]{:S(2)}, u32[]{:S(2)}) collective-permute-start(bf16[4,128,128]{2,1,0:T(8,128)(2,1)S(1)} %get-tuple-element.56), channel_id=1, source_target_pairs={{0,1},{1,0},{2,3},{3,2},{4,5},{5,4},{6,7},{7,6},{8,9},{9,8},{10,11... | collective-permute-start | bytes 393224 | tf_op jit(solution)/shard_map/ppermute | solution.py:27

commit v22 on v20

--- a/solution.py
+++ b/solution.py
@@ -464,11 +464,11 @@
     v_own = pack_both(place, v_mine, v_other)
 
     def halo_of(own, ring):
-        received = {back: moved(own, device_count, 2 * back, ring) for back in far_first}
+        received = {back: moved(own, device_count, 2 * back, ring[back == halo]) for back in far_first}
         return [own] + [received[back] for back in range(1, halo + 1)]
 
     def sent_back(partials, ring):
-        return [moved(partials[back - 1], device_count, -2 * back, ring) for back in far_first]
+        return [moved(partials[back - 1], device_count, -2 * back, ring[back == halo]) for back in far_first]
 
     def per_head(*shape):
         return pl.BlockSpec((1,) + shape, lambda h, *_: (h,) + (0,) * len(shape))
@@ -492,8 +492,8 @@
     acc = pltpu.VMEM((2 * halo, tokens, dim), F32)
     product = 2 * half * 2 * count * tokens * group * tokens * dim
 
-    k_pairs = halo_of(k_own, ring=True)
-    v_pairs = halo_of(v_own, ring=False)
+    k_pairs = halo_of(k_own, ring=(True, True))
+    v_pairs = halo_of(v_own, ring=(False, False))
     prob, *dv_halo = call(
         functools.partial(prob_kernel, halo),
         "prob",
@@ -506,7 +506,7 @@
         [run, acc, pltpu.VMEM((2, count - 1, tokens, HEADS_AT_ONCE * tokens), F32)],
         4 * product,
     )
-    dv_back = sent_back(dv_halo, ring=False)
+    dv_back = sent_back(dv_halo, ring=(True, False))
     dscore, *dk_halo = call(
         functools.partial(dscore_kernel, halo),
         "dscore",
@@ -519,7 +519,7 @@
         [run, acc],
         4 * product,
     )
-    dk_back = sent_back(dk_halo, ring=True)
+    dk_back = sent_back(dk_halo, ring=(True, False))
     dq, *others, dk_own, dv = call(
         functools.partial(own_kernel, halo),
         "own",

time: 59.1 us -> 59 us (level)
  waiting for transfers between devices: 6.21 us -> 4.79 us
  starting transfers between devices: 26.8 us -> 28.1 us
    ppermute x4, starting transfers between devices: 2.58 us -> 8.59 us  [moved(): lax.ppermute(array, AXES, [(d, to % device_count) for d, to in pairs])]
    ppermute x4, starting transfers between devices: 14.7 us -> 10.1 us  [moved(): lax.ppermute(array, AXES, [(d, to) for d, to in pairs if 0 <= to < device...]
    ppermute x4, waiting for transfers between devices: 2.34 us -> 0.01 us  [moved(): lax.ppermute(array, AXES, [(d, to) for d, to in pairs if 0 <= to < device...]
    ppermute x4, waiting for transfers between devices: 0.51 us -> 1.42 us  [moved(): lax.ppermute(array, AXES, [(d, to % device_count) for d, to in pairs])]
where the time goes in v22:
time: 59 us; the launch traced here: 58.4 us
  starting transfers between devices  28.1 us (48%)
  Pallas kernels  24.6 us (42%)
  waiting for transfers between devices  4.79 us (8%)
  between operations  0.81 us (1%)
    pallas_call x10, Pallas kernels, call(): pl.pallas_call(kernel, out_shape=outs, grid_spec=pltpu.PrefetchScalarGrid...  24.6 us
    ppermute x4, starting transfers between devices, moved(): lax.ppermute(array, AXES, [(d, to) for d, to in pairs if 0 <= to < device...  10.1 us
    ppermute x8, starting transfers between devices, swapped(): return lax.ppermute(array, AXES, [(d, d ^ 1) for d in range(device_count)])  9.44 us
    ppermute x4, starting transfers between devices, moved(): lax.ppermute(array, AXES, [(d, to % device_count) for d, to in pairs])  8.59 us
    ppermute x8, waiting for transfers between devices, swapped(): return lax.ppermute(array, AXES, [(d, d ^ 1) for d in range(device_count)])  3.36 us
    ppermute x4, waiting for transfers between devices, moved(): lax.ppermute(array, AXES, [(d, to % device_count) for d, to in pairs])  1.42 us
  transfers between devices with their start and end apart: 16, of which 5 were waited for; matrix products, arithmetic and copies ran while one was open for 0% of the time, Pallas kernels for 38%

profile of v22, /device:TPU:23, one launch (start us, length us, event | category | flops | bytes accessed | tf_op | source)
XLA Modules:
  0.0 58.4 jit_solution(9060797909548270360)
XLA Ops:
  0.6 0.7 %collective-permute-start = (bf16[128,8,128]{2,1,0:T(8,128)(2,1)}, bf16[128,8,128]{2,1,0:T(8,128)(2,1)S(1)}, u32[]{:S(2)}, u32[]{:S(2)}) collective-permute-start(bf16[128,8,128]{2,1,0:T(8,128)(2,1)} %key_ref.1), channel_id=1, source_target_pairs={{0,1},{1,0},{2,3},{3,2},{4,5},{5,4},{6,7},{7,6},{8,9},{9,8},{10,11... | collective-permute-start | bytes 786440 | tf_op jit(solution)/shard_map/ppermute | solution.py:27
  1.4 0.1 pad_add_fusion.place_ref
  1.5 1.6 %fetch.1 = (bf16[4,2,128,128]{3,2,1,0:T(8,128)(2,1)S(1)}, bf16[128,8,128]{2,1,0:T(8,128)(2,1)S(1)}) custom-call(s32[2]{0:T(128)S(1)} %pad_add_fusion.place_ref, bf16[128,8,128]{2,1,0:T(8,128)(2,1)} %key_ref.1, bf16[128,8,128]{2,1,0:T(8,128)(2,1)} %refs_0_.1), custom_call_target="tpu_custom_call" | custom-call | flops 1000000000 | tf_op jit(solution)/shard_map/fetch/pallas_call | solution.py:40
  3.1 0.6 %pack_other.1.refs_0_ = bf16[4,2,128,128]{3,2,1,0:T(8,128)(2,1)S(1)} custom-call(s32[2]{0:T(128)S(1)} %pad_add_fusion.place_ref, bf16[128,8,128]{2,1,0:T(8,128)(2,1)S(1)} %collective-permute-done.other_ref, bf16[4,2,128,128]{3,2,1,0:T(8,128)(2,1)S(1)} %get-tuple-element.28._), custom_call_target="tpu_custom_call", output_to_operand_aliasing={{}: (2, {})} | custom-call | flops 1000000000 | tf_op jit(solution)/shard_map/pack_other/pallas_call | solution.py:40
  3.7 0.1 collective-permute-start.1
  3.9 0.4 collective-permute-start.2
  4.3 0.1 collective-permute-start.3
  4.4 1.2 %collective-permute-start.5 = (bf16[4,2,128,128]{3,2,1,0:T(8,128)(2,1)S(1)}, bf16[4,2,128,128]{3,2,1,0:T(8,128)(2,1)S(1)}, u32[]{:S(2)}, u32[]{:S(2)}) collective-permute-start(bf16[4,2,128,128]{3,2,1,0:T(8,128)(2,1)S(1)} %pack_other.1.refs_0_), channel_id=1, source_target_pairs={{0,4},{1,5},{2,6},{3,7},{4,8},{5,9},{6,10},{7,11},{8,12},{9,13},{1... | collective-permute-start | bytes 786440 | tf_op jit(solution)/shard_map/ppermute | solution.py:22
  5.6 1.2 %collective-permute-start.4 = (bf16[4,2,128,128]{3,2,1,0:T(8,128)(2,1)S(1)}, bf16[4,2,128,128]{3,2,1,0:T(8,128)(2,1)S(1)}, u32[]{:S(2)}, u32[]{:S(2)}) collective-permute-start(bf16[4,2,128,128]{3,2,1,0:T(8,128)(2,1)S(1)} %pack_other.1.refs_0_), channel_id=1, source_target_pairs={{0,2},{1,3},{2,4},{3,5},{4,6},{5,7},{6,8},{7,9},{8,10},{9,11},{10,... | collective-permute-start | bytes 786440 | tf_op jit(solution)/shard_map/ppermute | solution.py:22
  6.8 1.1 %collective-permute-done.2.do_other_ref = bf16[128,32,128]{2,1,0:T(8,128)(2,1)S(1)} collective-permute-done((bf16[128,32,128]{2,1,0:T(8,128)(2,1)S(1)}, bf16[128,32,128]{2,1,0:T(8,128)(2,1)S(1)}, u32[]{:S(2)}, u32[]{:S(2)}) %collective-permute-start.2) | collective-permute-done | bytes 1048608 | tf_op jit(solution)/shard_map/ppermute | solution.py:27
  7.9 2.0 %arrange.1.qd_ref = bf16[4,2,2,4,128,128]{5,4,3,2,1,0:T(8,128)(2,1)S(1)} custom-call(s32[2]{0:T(128)S(1)} %pad_add_fusion.place_ref, bf16[128,32,128]{2,1,0:T(8,128)(2,1)S(1)} %copy-done, bf16[128,32,128]{2,1,0:T(8,128)(2,1)S(1)} %copy-done.1, bf16[128,32,128]{2,1,0:T(8,128)(2,1)S(1)} %collective-permute-done.1.q_other_ref, ...), custom_call_target="tpu_custom_call" | custom-call | flops 1000000000 | tf_op jit(solution)/shard_map/arrange/pallas_call | solution.py:40
  10.0 0.7 %pack_both.1.refs_0_ = bf16[4,2,128,128]{3,2,1,0:T(8,128)(2,1)S(1)} custom-call(s32[2]{0:T(128)S(1)} %pad_add_fusion.place_ref, bf16[128,8,128]{2,1,0:T(8,128)(2,1)S(1)} %get-tuple-element.36.own_ref, bf16[128,8,128]{2,1,0:T(8,128)(2,1)S(1)} %collective-permute-done.3.other_ref), custom_call_target="tpu_custom_call" | custom-call | flops 1000000000 | tf_op jit(solution)/shard_map/pack_both/pallas_call | solution.py:40
  10.7 3.1 %collective-permute-start.7 = (bf16[4,2,128,128]{3,2,1,0:T(8,128)(2,1)S(1)}, bf16[4,2,128,128]{3,2,1,0:T(8,128)(2,1)S(1)}, u32[]{:S(2)}, u32[]{:S(2)}) collective-permute-start(bf16[4,2,128,128]{3,2,1,0:T(8,128)(2,1)S(1)} %pack_both.1.refs_0_), channel_id=1, source_target_pairs={{0,4},{1,5},{2,6},{3,7},{4,8},{5,9},{6,10},{7,11},{8,12},{9,13},{1... | collective-permute-start | bytes 786440 | tf_op jit(solution)/shard_map/ppermute | solution.py:23
  13.9 3.1 %collective-permute-start.6 = (bf16[4,2,128,128]{3,2,1,0:T(8,128)(2,1)S(1)}, bf16[4,2,128,128]{3,2,1,0:T(8,128)(2,1)S(1)}, u32[]{:S(2)}, u32[]{:S(2)}) collective-permute-start(bf16[4,2,128,128]{3,2,1,0:T(8,128)(2,1)S(1)} %pack_both.1.refs_0_), channel_id=1, source_target_pairs={{0,2},{1,3},{2,4},{3,5},{4,6},{5,7},{6,8},{7,9},{8,10},{9,11},{10,... | collective-permute-start | bytes 786440 | tf_op jit(solution)/shard_map/ppermute | solution.py:23
  17.0 0.5 collective-permute-done.4.refs_1_
  17.5 6.5 %prob.1 = (bf16[4,2,640,512]{3,2,1,0:T(8,128)(2,1)S(1)}, bf16[4,2,128,128]{3,2,1,0:T(8,128)(2,1)S(1)}, bf16[4,2,128,128]{3,2,1,0:T(8,128)(2,1)S(1)}) custom-call(s32[2]{0:T(128)S(1)} %pad_add_fusion.place_ref, s32[16]{0:T(128)S(1)} %copy-done.2, bf16[4,2,2,4,128,128]{5,4,3,2,1,0:T(8,128)(2,1)S(1)} %arrange.1.qd_ref, ...), custom_call_target="tpu_custom_call" | custom-call | flops 2684354560 | tf_op jit(solution)/shard_map/prob/pallas_call | solution.py:40
  24.0 1.9 %collective-permute-start.8 = (bf16[4,2,128,128]{3,2,1,0:T(8,128)(2,1)S(1)}, bf16[4,2,128,128]{3,2,1,0:T(8,128)(2,1)S(1)}, u32[]{:S(2)}, u32[]{:S(2)}) collective-permute-start(bf16[4,2,128,128]{3,2,1,0:T(8,128)(2,1)S(1)} %get-tuple-element.39), channel_id=1, source_target_pairs={{4,0},{5,1},{6,2},{7,3},{8,4},{9,5},{10,6},{11,7},{12,8},{13,9},{1... | collective-permute-start | bytes 786440 | tf_op jit(solution)/shard_map/ppermute | solution.py:23
  25.9 4.6 %collective-permute-start.9 = (bf16[4,2,128,128]{3,2,1,0:T(8,128)(2,1)S(1)}, bf16[4,2,128,128]{3,2,1,0:T(8,128)(2,1)S(1)}, u32[]{:S(2)}, u32[]{:S(2)}) collective-permute-start(bf16[4,2,128,128]{3,2,1,0:T(8,128)(2,1)S(1)} %get-tuple-element.40), channel_id=1, source_target_pairs={{0,30},{1,31},{2,0},{3,1},{4,2},{5,3},{6,4},{7,5},{8,6},{9,7},{10,... | collective-permute-start | bytes 786440 | tf_op jit(solution)/shard_map/ppermute | solution.py:22
  30.5 5.6 %dscore.1 = (bf16[4,2,640,512]{3,2,1,0:T(8,128)(2,1)S(1)}, bf16[4,2,128,128]{3,2,1,0:T(8,128)(2,1)S(1)}, bf16[4,2,128,128]{3,2,1,0:T(8,128)(2,1)S(1)}) custom-call(s32[2]{0:T(128)S(1)} %pad_add_fusion.place_ref, bf16[4,2,2,4,128,128]{5,4,3,2,1,0:T(8,128)(2,1)S(1)} %arrange.1.qd_ref, bf16[4,2,640,512]{3,2,1,0:T(8,128)(2,1)S(1)} %get-tuple-element.35.p_ref, ...), custom_call_target="tpu_custom_call" | custom-call | flops 2684354560 | tf_op jit(solution)/shard_map/dscore/pallas_call | solution.py:40
  36.1 1.9 %collective-permute-start.13 = (bf16[4,2,128,128]{3,2,1,0:T(8,128)(2,1)S(1)}, bf16[4,2,128,128]{3,2,1,0:T(8,128)(2,1)S(1)}, u32[]{:S(2)}, u32[]{:S(2)}) collective-permute-start(bf16[4,2,128,128]{3,2,1,0:T(8,128)(2,1)S(1)} %get-tuple-element.48), channel_id=1, source_target_pairs={{4,0},{5,1},{6,2},{7,3},{8,4},{9,5},{10,6},{11,7},{12,8},{13,9},{1... | collective-permute-start | bytes 786440 | tf_op jit(solution)/shard_map/ppermute | solution.py:23
  38.1 1.5 %collective-permute-start.14 = (bf16[4,2,128,128]{3,2,1,0:T(8,128)(2,1)S(1)}, bf16[4,2,128,128]{3,2,1,0:T(8,128)(2,1)S(1)}, u32[]{:S(2)}, u32[]{:S(2)}) collective-permute-start(bf16[4,2,128,128]{3,2,1,0:T(8,128)(2,1)S(1)} %get-tuple-element.49), channel_id=1, source_target_pairs={{0,30},{1,31},{2,0},{3,1},{4,2},{5,3},{6,4},{7,5},{8,6},{9,7},{10,... | collective-permute-start | bytes 786440 | tf_op jit(solution)/shard_map/ppermute | solution.py:22
  39.6 0.9 %collective-permute-done.9.refs_4_ = bf16[4,2,128,128]{3,2,1,0:T(8,128)(2,1)S(1)} collective-permute-done((bf16[4,2,128,128]{3,2,1,0:T(8,128)(2,1)S(1)}, bf16[4,2,128,128]{3,2,1,0:T(8,128)(2,1)S(1)}, u32[]{:S(2)}, u32[]{:S(2)}) %collective-permute-start.9) | collective-permute-done | bytes 262176 | tf_op jit(solution)/shard_map/ppermute | solution.py:22
  40.5 3.3 %own.1 = (bf16[128,16,128]{2,1,0:T(8,128)(2,1)S(1)}, bf16[56,16,128]{2,1,0:T(8,128)(2,1)S(1)}, bf16[56,16,128]{2,1,0:T(8,128)(2,1)S(1)}, bf16[48,16,128]{2,1,0:T...) custom-call(s32[2]{0:T(128)S(1)} %pad_add_fusion.place_ref, ...), custom_call_target="tpu_custom_call" | custom-call | tf_op jit(solution)/shard_map/own/pallas_call | solution.py:40
  43.8 6.7 %collective-permute-start.10 = (bf16[56,16,128]{2,1,0:T(8,128)(2,1)S(1)}, bf16[56,16,128]{2,1,0:T(8,128)(2,1)S(1)}, u32[]{:S(2)}, u32[]{:S(2)}) collective-permute-start(bf16[56,16,128]{2,1,0:T(8,128)(2,1)S(1)} %get-tuple-element.43), channel_id=1, source_target_pairs={{0,1},{1,0},{2,3},{3,2},{4,5},{5,4},{6,7},{7,6},{8,9},{9,8},{10,11... | collective-permute-start | bytes 688136 | tf_op jit(solution)/shard_map/ppermute | solution.py:27
  50.5 0.1 collective-permute-start.11
  50.6 0.4 collective-permute-start.12
  51.0 1.3 %collective-permute-done.12.refs_2_ = bf16[48,16,128]{2,1,0:T(8,128)(2,1)S(1)} collective-permute-done((bf16[48,16,128]{2,1,0:T(8,128)(2,1)S(1)}, bf16[48,16,128]{2,1,0:T(8,128)(2,1)S(1)}, u32[]{:S(2)}, u32[]{:S(2)}) %collective-permute-start.12) | collective-permute-done | bytes 196640 | tf_op jit(solution)/shard_map/ppermute | solution.py:27
  52.3 2.2 %join.1 = (bf16[128,32,128]{2,1,0:T(8,128)(2,1)}, bf16[128,8,128]{2,1,0:T(8,128)(2,1)}) custom-call(s32[2]{0:T(128)S(1)} %pad_add_fusion.place_ref, bf16[128,16,128]{2,1,0:T(8,128)(2,1)S(1)} %get-tuple-element.41.dq_ref, bf16[4,128,128]{2,1,0:T(8,128)(2,1)S(1)} %get-tuple-element.42.dv_ref, bf16[56,16,128]{2,1,0:T(8,128)(2,1)S(1)} %collective-permute-done.10.refs_0_, ...), custom_call_target="tpu_custom_call" | custom-call | tf_op jit(solution)/shard_map/join/pallas_call | solution.py:40
  54.5 0.6 %sum_dk.1 = (bf16[4,128,128]{2,1,0:T(8,128)(2,1)S(1)}, bf16[4,128,128]{2,1,0:T(8,128)(2,1)S(1)}) custom-call(s32[2]{0:T(128)S(1)} %pad_add_fusion.place_ref, f32[4,2,128,128]{3,2,1,0:T(8,128)S(1)} %get-tuple-element.47.own_ref, bf16[4,2,128,128]{3,2,1,0:T(8,128)(2,1)S(1)} %collective-permute-done.13.refs_0_, ...), custom_call_target="tpu_custom_call" | custom-call | tf_op jit(solution)/shard_map/sum_dk/pallas_call | solution.py:40
  55.2 0.9 %collective-permute-start.15 = (bf16[4,128,128]{2,1,0:T(8,128)(2,1)S(1)}, bf16[4,128,128]{2,1,0:T(8,128)(2,1)S(1)}, u32[]{:S(2)}, u32[]{:S(2)}) collective-permute-start(bf16[4,128,128]{2,1,0:T(8,128)(2,1)S(1)} %get-tuple-element.52), channel_id=1, source_target_pairs={{0,1},{1,0},{2,3},{3,2},{4,5},{5,4},{6,7},{7,6},{8,9},{9,8},{10,11... | collective-permute-start | bytes 393224 | tf_op jit(solution)/shard_map/ppermute | solution.py:27
  56.0 1.0 %collective-permute-done.15.other_ref = bf16[4,128,128]{2,1,0:T(8,128)(2,1)S(1)} collective-permute-done((bf16[4,128,128]{2,1,0:T(8,128)(2,1)S(1)}, bf16[4,128,128]{2,1,0:T(8,128)(2,1)S(1)}, u32[]{:S(2)}, u32[]{:S(2)}) %collective-permute-start.15) | collective-permute-done | bytes 131104 | tf_op jit(solution)/shard_map/ppermute | solution.py:27
  57.0 1.4 %merge_dk.1 = bf16[128,8,128]{2,1,0:T(8,128)(2,1)} custom-call(s32[2]{0:T(128)S(1)} %pad_add_fusion.place_ref, bf16[4,128,128]{2,1,0:T(8,128)(2,1)S(1)} %get-tuple-element.51.own_ref, bf16[4,128,128]{2,1,0:T(8,128)(2,1)S(1)} %collective-permute-done.15.other_ref), custom_call_target="tpu_custom_call" | custom-call | tf_op jit(solution)/shard_map/merge_dk/pallas_call | solution.py:40
  (17 shorter events, 0.0 us)
Async XLA Ops:
  0.6 3.2 %copy-start.1 = (bf16[128,32,128]{2,1,0:T(8,128)(2,1)S(1)}, bf16[128,32,128]{2,1,0:T(8,128)(2,1)}, u32[]{:S(2)}) copy-start(bf16[128,32,128]{2,1,0:T(8,128)(2,1)} %do_ref) | copy-start | bytes 3145732
  0.6 3.1 %copy-start = (bf16[128,32,128]{2,1,0:T(8,128)(2,1)S(1)}, bf16[128,32,128]{2,1,0:T(8,128)(2,1)}, u32[]{:S(2)}) copy-start(bf16[128,32,128]{2,1,0:T(8,128)(2,1)} %q_ref) | copy-start | bytes 3145732
  0.6 2.4 %collective-permute-start = (bf16[128,8,128]{2,1,0:T(8,128)(2,1)}, bf16[128,8,128]{2,1,0:T(8,128)(2,1)S(1)}, u32[]{:S(2)}, u32[]{:S(2)}) collective-permute-start(bf16[128,8,128]{2,1,0:T(8,128)(2,1)} %key_ref.1), channel_id=1, source_target_pairs={{0,1},{1,0},{2,3},{3,2},{4,5},{5,4},{6,7},{7,6},{8,9},{9,8},{10,11... | collective-permute-start | bytes 786440 | tf_op jit(solution)/shard_map/ppermute | solution.py:27
  3.7 13.8 %copy-start.2 = (s32[16]{0:T(128)S(1)}, s32[16]{0:T(128)}, u32[]{:S(2)}) copy-start(s32[16]{0:T(128)} %lengths_ref.1) | copy-start | bytes 196
  3.7 3.1 %collective-permute-start.1 = (bf16[128,32,128]{2,1,0:T(8,128)(2,1)S(1)}, bf16[128,32,128]{2,1,0:T(8,128)(2,1)S(1)}, u32[]{:S(2)}, u32[]{:S(2)}) collective-permute-start(bf16[128,32,128]{2,1,0:T(8,128)(2,1)S(1)} %copy-done), channel_id=1, source_target_pairs={{0,1},{1,0},{2,3},{3,2},{4,5},{5,4},{6,7},{7,6},{8,9},{9,8},{10,11... | collective-permute-start | bytes 3145736 | tf_op jit(solution)/shard_map/ppermute | solution.py:27
  3.9 4.1 %collective-permute-start.2 = (bf16[128,32,128]{2,1,0:T(8,128)(2,1)S(1)}, bf16[128,32,128]{2,1,0:T(8,128)(2,1)S(1)}, u32[]{:S(2)}, u32[]{:S(2)}) collective-permute-start(bf16[128,32,128]{2,1,0:T(8,128)(2,1)S(1)} %copy-done.1), channel_id=1, source_target_pairs={{0,1},{1,0},{2,3},{3,2},{4,5},{5,4},{6,7},{7,6},{8,9},{9,8},{10,11... | collective-permute-start | bytes 3145736 | tf_op jit(solution)/shard_map/ppermute | solution.py:27
  4.3 5.7 %collective-permute-start.3 = (bf16[128,8,128]{2,1,0:T(8,128)(2,1)S(1)}, bf16[128,8,128]{2,1,0:T(8,128)(2,1)S(1)}, u32[]{:S(2)}, u32[]{:S(2)}) collective-permute-start(bf16[128,8,128]{2,1,0:T(8,128)(2,1)S(1)} %get-tuple-element.36.own_ref), channel_id=1, source_target_pairs={{0,1},{1,0},{2,3},{3,2},{4,5},{5,4},{6,7},{7,6},{8,9},{9,8},{10,11... | collective-permute-start | bytes 786440 | tf_op jit(solution)/shard_map/ppermute | solution.py:27
  4.4 12.6 %collective-permute-start.5 = (bf16[4,2,128,128]{3,2,1,0:T(8,128)(2,1)S(1)}, bf16[4,2,128,128]{3,2,1,0:T(8,128)(2,1)S(1)}, u32[]{:S(2)}, u32[]{:S(2)}) collective-permute-start(bf16[4,2,128,128]{3,2,1,0:T(8,128)(2,1)S(1)} %pack_other.1.refs_0_), channel_id=1, source_target_pairs={{0,4},{1,5},{2,6},{3,7},{4,8},{5,9},{6,10},{7,11},{8,12},{9,13},{1... | collective-permute-start | bytes 786440 | tf_op jit(solution)/shard_map/ppermute | solution.py:22
  5.6 11.9 %collective-permute-start.4 = (bf16[4,2,128,128]{3,2,1,0:T(8,128)(2,1)S(1)}, bf16[4,2,128,128]{3,2,1,0:T(8,128)(2,1)S(1)}, u32[]{:S(2)}, u32[]{:S(2)}) collective-permute-start(bf16[4,2,128,128]{3,2,1,0:T(8,128)(2,1)S(1)} %pack_other.1.refs_0_), channel_id=1, source_target_pairs={{0,2},{1,3},{2,4},{3,5},{4,6},{5,7},{6,8},{7,9},{8,10},{9,11},{10,... | collective-permute-start | bytes 786440 | tf_op jit(solution)/shard_map/ppermute | solution.py:22
  10.7 19.8 %collective-permute-start.7 = (bf16[4,2,128,128]{3,2,1,0:T(8,128)(2,1)S(1)}, bf16[4,2,128,128]{3,2,1,0:T(8,128)(2,1)S(1)}, u32[]{:S(2)}, u32[]{:S(2)}) collective-permute-start(bf16[4,2,128,128]{3,2,1,0:T(8,128)(2,1)S(1)} %pack_both.1.refs_0_), channel_id=1, source_target_pairs={{0,4},{1,5},{2,6},{3,7},{4,8},{5,9},{6,10},{7,11},{8,12},{9,13},{1... | collective-permute-start | bytes 786440 | tf_op jit(solution)/shard_map/ppermute | solution.py:23
  13.9 16.7 %collective-permute-start.6 = (bf16[4,2,128,128]{3,2,1,0:T(8,128)(2,1)S(1)}, bf16[4,2,128,128]{3,2,1,0:T(8,128)(2,1)S(1)}, u32[]{:S(2)}, u32[]{:S(2)}) collective-permute-start(bf16[4,2,128,128]{3,2,1,0:T(8,128)(2,1)S(1)} %pack_both.1.refs_0_), channel_id=1, source_target_pairs={{0,2},{1,3},{2,4},{3,5},{4,6},{5,7},{6,8},{7,9},{8,10},{9,11},{10,... | collective-permute-start | bytes 786440 | tf_op jit(solution)/shard_map/ppermute | solution.py:23
  24.0 15.6 %collective-permute-start.8 = (bf16[4,2,128,128]{3,2,1,0:T(8,128)(2,1)S(1)}, bf16[4,2,128,128]{3,2,1,0:T(8,128)(2,1)S(1)}, u32[]{:S(2)}, u32[]{:S(2)}) collective-permute-start(bf16[4,2,128,128]{3,2,1,0:T(8,128)(2,1)S(1)} %get-tuple-element.39), channel_id=1, source_target_pairs={{4,0},{5,1},{6,2},{7,3},{8,4},{9,5},{10,6},{11,7},{12,8},{13,9},{1... | collective-permute-start | bytes 786440 | tf_op jit(solution)/shard_map/ppermute | solution.py:23
  25.9 14.6 %collective-permute-start.9 = (bf16[4,2,128,128]{3,2,1,0:T(8,128)(2,1)S(1)}, bf16[4,2,128,128]{3,2,1,0:T(8,128)(2,1)S(1)}, u32[]{:S(2)}, u32[]{:S(2)}) collective-permute-start(bf16[4,2,128,128]{3,2,1,0:T(8,128)(2,1)S(1)} %get-tuple-element.40), channel_id=1, source_target_pairs={{0,30},{1,31},{2,0},{3,1},{4,2},{5,3},{6,4},{7,5},{8,6},{9,7},{10,... | collective-permute-start | bytes 786440 | tf_op jit(solution)/shard_map/ppermute | solution.py:22
  36.1 18.4 %collective-permute-start.13 = (bf16[4,2,128,128]{3,2,1,0:T(8,128)(2,1)S(1)}, bf16[4,2,128,128]{3,2,1,0:T(8,128)(2,1)S(1)}, u32[]{:S(2)}, u32[]{:S(2)}) collective-permute-start(bf16[4,2,128,128]{3,2,1,0:T(8,128)(2,1)S(1)} %get-tuple-element.48), channel_id=1, source_target_pairs={{4,0},{5,1},{6,2},{7,3},{8,4},{9,5},{10,6},{11,7},{12,8},{13,9},{1... | collective-permute-start | bytes 786440 | tf_op jit(solution)/shard_map/ppermute | solution.py:23
  38.1 16.5 %collective-permute-start.14 = (bf16[4,2,128,128]{3,2,1,0:T(8,128)(2,1)S(1)}, bf16[4,2,128,128]{3,2,1,0:T(8,128)(2,1)S(1)}, u32[]{:S(2)}, u32[]{:S(2)}) collective-permute-start(bf16[4,2,128,128]{3,2,1,0:T(8,128)(2,1)S(1)} %get-tuple-element.49), channel_id=1, source_target_pairs={{0,30},{1,31},{2,0},{3,1},{4,2},{5,3},{6,4},{7,5},{8,6},{9,7},{10,... | collective-permute-start | bytes 786440 | tf_op jit(solution)/shard_map/ppermute | solution.py:22
  43.8 8.4 %collective-permute-start.10 = (bf16[56,16,128]{2,1,0:T(8,128)(2,1)S(1)}, bf16[56,16,128]{2,1,0:T(8,128)(2,1)S(1)}, u32[]{:S(2)}, u32[]{:S(2)}) collective-permute-start(bf16[56,16,128]{2,1,0:T(8,128)(2,1)S(1)} %get-tuple-element.43), channel_id=1, source_target_pairs={{0,1},{1,0},{2,3},{3,2},{4,5},{5,4},{6,7},{7,6},{8,9},{9,8},{10,11... | collective-permute-start | bytes 688136 | tf_op jit(solution)/shard_map/ppermute | solution.py:27
  50.5 1.8 %collective-permute-start.11 = (bf16[56,16,128]{2,1,0:T(8,128)(2,1)S(1)}, bf16[56,16,128]{2,1,0:T(8,128)(2,1)S(1)}, u32[]{:S(2)}, u32[]{:S(2)}) collective-permute-start(bf16[56,16,128]{2,1,0:T(8,128)(2,1)S(1)} %get-tuple-element.44), channel_id=1, source_target_pairs={{0,1},{1,0},{2,3},{3,2},{4,5},{5,4},{6,7},{7,6},{8,9},{9,8},{10,11... | collective-permute-start | bytes 688136 | tf_op jit(solution)/shard_map/ppermute | solution.py:27
  50.6 1.7 %collective-permute-start.12 = (bf16[48,16,128]{2,1,0:T(8,128)(2,1)S(1)}, bf16[48,16,128]{2,1,0:T(8,128)(2,1)S(1)}, u32[]{:S(2)}, u32[]{:S(2)}) collective-permute-start(bf16[48,16,128]{2,1,0:T(8,128)(2,1)S(1)} %get-tuple-element.45), channel_id=1, source_target_pairs={{0,1},{1,0},{2,3},{3,2},{4,5},{5,4},{6,7},{7,6},{8,9},{9,8},{10,11... | collective-permute-start | bytes 589832 | tf_op jit(solution)/shard_map/ppermute | solution.py:27
  55.2 1.9 %collective-permute-start.15 = (bf16[4,128,128]{2,1,0:T(8,128)(2,1)S(1)}, bf16[4,128,128]{2,1,0:T(8,128)(2,1)S(1)}, u32[]{:S(2)}, u32[]{:S(2)}) collective-permute-start(bf16[4,128,128]{2,1,0:T(8,128)(2,1)S(1)} %get-tuple-element.52), channel_id=1, source_target_pairs={{0,1},{1,0},{2,3},{3,2},{4,5},{5,4},{6,7},{7,6},{8,9},{9,8},{10,11... | collective-permute-start | bytes 393224 | tf_op jit(solution)/shard_map/ppermute | solution.py:27

commit v23 on v22

--- a/solution.py
+++ b/solution.py
@@ -467,8 +467,8 @@
         received = {back: moved(own, device_count, 2 * back, ring[back == halo]) for back in far_first}
         return [own] + [received[back] for back in range(1, halo + 1)]
 
-    def sent_back(partials, ring):
-        return [moved(partials[back - 1], device_count, -2 * back, ring[back == halo]) for back in far_first]
+    def sent_back(partials, ring, order):
+        return [moved(partials[back - 1], device_count, -2 * back, ring[back == halo]) for back in order]
 
     def per_head(*shape):
         return pl.BlockSpec((1,) + shape, lambda h, *_: (h,) + (0,) * len(shape))
@@ -506,7 +506,7 @@
         [run, acc, pltpu.VMEM((2, count - 1, tokens, HEADS_AT_ONCE * tokens), F32)],
         4 * product,
     )
-    dv_back = sent_back(dv_halo, ring=(True, False))
+    dv_back = sent_back(dv_halo, (True, False), range(1, halo + 1))
     dscore, *dk_halo = call(
         functools.partial(dscore_kernel, halo),
         "dscore",
@@ -519,7 +519,7 @@
         [run, acc],
         4 * product,
     )
-    dk_back = sent_back(dk_halo, ring=(True, False))
+    dk_back = sent_back(dk_halo, (True, False), range(1, halo + 1))
     dq, *others, dk_own, dv = call(
         functools.partial(own_kernel, halo),
         "own",

time: 59 us -> 60.1 us (1.019)
  the two profiles are of different devices: /device:TPU:23 before, /device:TPU:27 now
where the time goes in v23:
time: 60.1 us; the launch traced here: 59.9 us
  starting transfers between devices  26.5 us (44%)
  Pallas kernels  24.6 us (41%)
  waiting for transfers between devices  7.87 us (13%)
  between operations  0.84 us (1%)
    pallas_call x10, Pallas kernels, call(): pl.pallas_call(kernel, out_shape=outs, grid_spec=pltpu.PrefetchScalarGrid...  24.6 us
    ppermute x4, starting transfers between devices, moved(): lax.ppermute(array, AXES, [(d, to % device_count) for d, to in pairs])  8.9 us
    ppermute x4, starting transfers between devices, moved(): lax.ppermute(array, AXES, [(d, to) for d, to in pairs if 0 <= to < device...  8.89 us
    ppermute x8, starting transfers between devices, swapped(): return lax.ppermute(array, AXES, [(d, d ^ 1) for d in range(device_count)])  8.69 us
    ppermute x8, waiting for transfers between devices, swapped(): return lax.ppermute(array, AXES, [(d, d ^ 1) for d in range(device_count)])  4.61 us
    ppermute x4, waiting for transfers between devices, moved(): lax.ppermute(array, AXES, [(d, to) for d, to in pairs if 0 <= to < device...  3.26 us
  transfers between devices with their start and end apart: 16, of which 5 were waited for; matrix products, arithmetic and copies ran while one was open for 0% of the time, Pallas kernels for 37%

profile of v23, /device:TPU:27, one launch (start us, length us, event | category | flops | bytes accessed | tf_op | source)
XLA Modules:
  0.0 59.9 jit_solution(18402107470402224995)
XLA Ops:
  0.6 0.7 %collective-permute-start = (bf16[128,8,128]{2,1,0:T(8,128)(2,1)}, bf16[128,8,128]{2,1,0:T(8,128)(2,1)S(1)}, u32[]{:S(2)}, u32[]{:S(2)}) collective-permute-start(bf16[128,8,128]{2,1,0:T(8,128)(2,1)} %key_ref.1), channel_id=1, source_target_pairs={{0,1},{1,0},{2,3},{3,2},{4,5},{5,4},{6,7},{7,6},{8,9},{9,8},{10,11... | collective-permute-start | bytes 786440 | tf_op jit(solution)/shard_map/ppermute | solution.py:27
  1.4 0.1 pad_add_fusion.place_ref
  1.5 1.6 %fetch.1 = (bf16[4,2,128,128]{3,2,1,0:T(8,128)(2,1)S(1)}, bf16[128,8,128]{2,1,0:T(8,128)(2,1)S(1)}) custom-call(s32[2]{0:T(128)S(1)} %pad_add_fusion.place_ref, bf16[128,8,128]{2,1,0:T(8,128)(2,1)} %key_ref.1, bf16[128,8,128]{2,1,0:T(8,128)(2,1)} %refs_0_.1), custom_call_target="tpu_custom_call" | custom-call | flops 1000000000 | tf_op jit(solution)/shard_map/fetch/pallas_call | solution.py:40
  3.1 0.6 %pack_other.1.refs_0_ = bf16[4,2,128,128]{3,2,1,0:T(8,128)(2,1)S(1)} custom-call(s32[2]{0:T(128)S(1)} %pad_add_fusion.place_ref, bf16[128,8,128]{2,1,0:T(8,128)(2,1)S(1)} %collective-permute-done.other_ref, bf16[4,2,128,128]{3,2,1,0:T(8,128)(2,1)S(1)} %get-tuple-element.28._), custom_call_target="tpu_custom_call", output_to_operand_aliasing={{}: (2, {})} | custom-call | flops 1000000000 | tf_op jit(solution)/shard_map/pack_other/pallas_call | solution.py:40
  3.7 0.0 copy-start.2
  3.7 0.1 collective-permute-start.1
  3.9 0.4 collective-permute-start.2
  4.3 0.1 collective-permute-start.3
  4.4 1.2 %collective-permute-start.5 = (bf16[4,2,128,128]{3,2,1,0:T(8,128)(2,1)S(1)}, bf16[4,2,128,128]{3,2,1,0:T(8,128)(2,1)S(1)}, u32[]{:S(2)}, u32[]{:S(2)}) collective-permute-start(bf16[4,2,128,128]{3,2,1,0:T(8,128)(2,1)S(1)} %pack_other.1.refs_0_), channel_id=1, source_target_pairs={{0,4},{1,5},{2,6},{3,7},{4,8},{5,9},{6,10},{7,11},{8,12},{9,13},{1... | collective-permute-start | bytes 786440 | tf_op jit(solution)/shard_map/ppermute | solution.py:22
  5.6 0.8 %collective-permute-done.1.q_other_ref = bf16[128,32,128]{2,1,0:T(8,128)(2,1)S(1)} collective-permute-done((bf16[128,32,128]{2,1,0:T(8,128)(2,1)S(1)}, bf16[128,32,128]{2,1,0:T(8,128)(2,1)S(1)}, u32[]{:S(2)}, u32[]{:S(2)}) %collective-permute-start.1) | collective-permute-done | bytes 1048608 | tf_op jit(solution)/shard_map/ppermute | solution.py:27
  6.4 1.5 %collective-permute-done.2.do_other_ref = bf16[128,32,128]{2,1,0:T(8,128)(2,1)S(1)} collective-permute-done((bf16[128,32,128]{2,1,0:T(8,128)(2,1)S(1)}, bf16[128,32,128]{2,1,0:T(8,128)(2,1)S(1)}, u32[]{:S(2)}, u32[]{:S(2)}) %collective-permute-start.2) | collective-permute-done | bytes 1048608 | tf_op jit(solution)/shard_map/ppermute | solution.py:27
  7.9 2.0 %arrange.1.qd_ref = bf16[4,2,2,4,128,128]{5,4,3,2,1,0:T(8,128)(2,1)S(1)} custom-call(s32[2]{0:T(128)S(1)} %pad_add_fusion.place_ref, bf16[128,32,128]{2,1,0:T(8,128)(2,1)S(1)} %copy-done, bf16[128,32,128]{2,1,0:T(8,128)(2,1)S(1)} %copy-done.1, bf16[128,32,128]{2,1,0:T(8,128)(2,1)S(1)} %collective-permute-done.1.q_other_ref, ...), custom_call_target="tpu_custom_call" | custom-call | flops 1000000000 | tf_op jit(solution)/shard_map/arrange/pallas_call | solution.py:40
  10.0 0.7 %pack_both.1.refs_0_ = bf16[4,2,128,128]{3,2,1,0:T(8,128)(2,1)S(1)} custom-call(s32[2]{0:T(128)S(1)} %pad_add_fusion.place_ref, bf16[128,8,128]{2,1,0:T(8,128)(2,1)S(1)} %get-tuple-element.36.own_ref, bf16[128,8,128]{2,1,0:T(8,128)(2,1)S(1)} %collective-permute-done.3.other_ref), custom_call_target="tpu_custom_call" | custom-call | flops 1000000000 | tf_op jit(solution)/shard_map/pack_both/pallas_call | solution.py:40
  10.7 3.1 %collective-permute-start.7 = (bf16[4,2,128,128]{3,2,1,0:T(8,128)(2,1)S(1)}, bf16[4,2,128,128]{3,2,1,0:T(8,128)(2,1)S(1)}, u32[]{:S(2)}, u32[]{:S(2)}) collective-permute-start(bf16[4,2,128,128]{3,2,1,0:T(8,128)(2,1)S(1)} %pack_both.1.refs_0_), channel_id=1, source_target_pairs={{0,4},{1,5},{2,6},{3,7},{4,8},{5,9},{6,10},{7,11},{8,12},{9,13},{1... | collective-permute-start | bytes 786440 | tf_op jit(solution)/shard_map/ppermute | solution.py:23
  13.9 1.9 %collective-permute-start.6 = (bf16[4,2,128,128]{3,2,1,0:T(8,128)(2,1)S(1)}, bf16[4,2,128,128]{3,2,1,0:T(8,128)(2,1)S(1)}, u32[]{:S(2)}, u32[]{:S(2)}) collective-permute-start(bf16[4,2,128,128]{3,2,1,0:T(8,128)(2,1)S(1)} %pack_both.1.refs_0_), channel_id=1, source_target_pairs={{0,2},{1,3},{2,4},{3,5},{4,6},{5,7},{6,8},{7,9},{8,10},{9,11},{10,... | collective-permute-start | bytes 786440 | tf_op jit(solution)/shard_map/ppermute | solution.py:23
  15.8 6.5 %prob.1 = (bf16[4,2,640,512]{3,2,1,0:T(8,128)(2,1)S(1)}, bf16[4,2,128,128]{3,2,1,0:T(8,128)(2,1)S(1)}, bf16[4,2,128,128]{3,2,1,0:T(8,128)(2,1)S(1)}) custom-call(s32[2]{0:T(128)S(1)} %pad_add_fusion.place_ref, s32[16]{0:T(128)S(1)} %copy-done.2, bf16[4,2,2,4,128,128]{5,4,3,2,1,0:T(8,128)(2,1)S(1)} %arrange.1.qd_ref, ...), custom_call_target="tpu_custom_call" | custom-call | flops 2684354560 | tf_op jit(solution)/shard_map/prob/pallas_call | solution.py:40
  22.3 6.1 %collective-permute-start.8 = (bf16[4,2,128,128]{3,2,1,0:T(8,128)(2,1)S(1)}, bf16[4,2,128,128]{3,2,1,0:T(8,128)(2,1)S(1)}, u32[]{:S(2)}, u32[]{:S(2)}) collective-permute-start(bf16[4,2,128,128]{3,2,1,0:T(8,128)(2,1)S(1)} %get-tuple-element.39), channel_id=1, source_target_pairs={{0,30},{1,31},{2,0},{3,1},{4,2},{5,3},{6,4},{7,5},{8,6},{9,7},{10,... | collective-permute-start | bytes 786440 | tf_op jit(solution)/shard_map/ppermute | solution.py:22
  28.4 1.9 %collective-permute-start.9 = (bf16[4,2,128,128]{3,2,1,0:T(8,128)(2,1)S(1)}, bf16[4,2,128,128]{3,2,1,0:T(8,128)(2,1)S(1)}, u32[]{:S(2)}, u32[]{:S(2)}) collective-permute-start(bf16[4,2,128,128]{3,2,1,0:T(8,128)(2,1)S(1)} %get-tuple-element.40), channel_id=1, source_target_pairs={{4,0},{5,1},{6,2},{7,3},{8,4},{9,5},{10,6},{11,7},{12,8},{13,9},{1... | collective-permute-start | bytes 786440 | tf_op jit(solution)/shard_map/ppermute | solution.py:23
  30.3 5.6 %dscore.1 = (bf16[4,2,640,512]{3,2,1,0:T(8,128)(2,1)S(1)}, bf16[4,2,128,128]{3,2,1,0:T(8,128)(2,1)S(1)}, bf16[4,2,128,128]{3,2,1,0:T(8,128)(2,1)S(1)}) custom-call(s32[2]{0:T(128)S(1)} %pad_add_fusion.place_ref, bf16[4,2,2,4,128,128]{5,4,3,2,1,0:T(8,128)(2,1)S(1)} %arrange.1.qd_ref, bf16[4,2,640,512]{3,2,1,0:T(8,128)(2,1)S(1)} %get-tuple-element.35.p_ref, ...), custom_call_target="tpu_custom_call" | custom-call | flops 2684354560 | tf_op jit(solution)/shard_map/dscore/pallas_call | solution.py:40
  35.9 1.6 %collective-permute-start.13 = (bf16[4,2,128,128]{3,2,1,0:T(8,128)(2,1)S(1)}, bf16[4,2,128,128]{3,2,1,0:T(8,128)(2,1)S(1)}, u32[]{:S(2)}, u32[]{:S(2)}) collective-permute-start(bf16[4,2,128,128]{3,2,1,0:T(8,128)(2,1)S(1)} %get-tuple-element.48), channel_id=1, source_target_pairs={{0,30},{1,31},{2,0},{3,1},{4,2},{5,3},{6,4},{7,5},{8,6},{9,7},{10,... | collective-permute-start | bytes 786440 | tf_op jit(solution)/shard_map/ppermute | solution.py:22
  37.5 1.9 %collective-permute-start.14 = (bf16[4,2,128,128]{3,2,1,0:T(8,128)(2,1)S(1)}, bf16[4,2,128,128]{3,2,1,0:T(8,128)(2,1)S(1)}, u32[]{:S(2)}, u32[]{:S(2)}) collective-permute-start(bf16[4,2,128,128]{3,2,1,0:T(8,128)(2,1)S(1)} %get-tuple-element.49), channel_id=1, source_target_pairs={{4,0},{5,1},{6,2},{7,3},{8,4},{9,5},{10,6},{11,7},{12,8},{13,9},{1... | collective-permute-start | bytes 786440 | tf_op jit(solution)/shard_map/ppermute | solution.py:23
  39.4 3.2 %collective-permute-done.9.refs_4_ = bf16[4,2,128,128]{3,2,1,0:T(8,128)(2,1)S(1)} collective-permute-done((bf16[4,2,128,128]{3,2,1,0:T(8,128)(2,1)S(1)}, bf16[4,2,128,128]{3,2,1,0:T(8,128)(2,1)S(1)}, u32[]{:S(2)}, u32[]{:S(2)}) %collective-permute-start.9) | collective-permute-done | bytes 262176 | tf_op jit(solution)/shard_map/ppermute | solution.py:23
  42.7 3.3 %own.1 = (bf16[128,16,128]{2,1,0:T(8,128)(2,1)S(1)}, bf16[56,16,128]{2,1,0:T(8,128)(2,1)S(1)}, bf16[56,16,128]{2,1,0:T(8,128)(2,1)S(1)}, bf16[48,16,128]{2,1,0:T...) custom-call(s32[2]{0:T(128)S(1)} %pad_add_fusion.place_ref, ...), custom_call_target="tpu_custom_call" | custom-call | tf_op jit(solution)/shard_map/own/pallas_call | solution.py:40
  46.0 6.4 %collective-permute-start.10 = (bf16[56,16,128]{2,1,0:T(8,128)(2,1)S(1)}, bf16[56,16,128]{2,1,0:T(8,128)(2,1)S(1)}, u32[]{:S(2)}, u32[]{:S(2)}) collective-permute-start(bf16[56,16,128]{2,1,0:T(8,128)(2,1)S(1)} %get-tuple-element.43), channel_id=1, source_target_pairs={{0,1},{1,0},{2,3},{3,2},{4,5},{5,4},{6,7},{7,6},{8,9},{9,8},{10,11... | collective-permute-start | bytes 688136 | tf_op jit(solution)/shard_map/ppermute | solution.py:27
  52.4 0.1 collective-permute-start.11
  52.5 0.4 collective-permute-start.12
  52.9 1.3 %collective-permute-done.12.refs_2_ = bf16[48,16,128]{2,1,0:T(8,128)(2,1)S(1)} collective-permute-done((bf16[48,16,128]{2,1,0:T(8,128)(2,1)S(1)}, bf16[48,16,128]{2,1,0:T(8,128)(2,1)S(1)}, u32[]{:S(2)}, u32[]{:S(2)}) %collective-permute-start.12) | collective-permute-done | bytes 196640 | tf_op jit(solution)/shard_map/ppermute | solution.py:27
  54.2 2.2 %join.1 = (bf16[128,32,128]{2,1,0:T(8,128)(2,1)}, bf16[128,8,128]{2,1,0:T(8,128)(2,1)}) custom-call(s32[2]{0:T(128)S(1)} %pad_add_fusion.place_ref, bf16[128,16,128]{2,1,0:T(8,128)(2,1)S(1)} %get-tuple-element.41.dq_ref, bf16[4,128,128]{2,1,0:T(8,128)(2,1)S(1)} %get-tuple-element.42.dv_ref, bf16[56,16,128]{2,1,0:T(8,128)(2,1)S(1)} %collective-permute-done.10.refs_0_, ...), custom_call_target="tpu_custom_call" | custom-call | tf_op jit(solution)/shard_map/join/pallas_call | solution.py:40
  56.4 0.6 %sum_dk.1 = (bf16[4,128,128]{2,1,0:T(8,128)(2,1)S(1)}, bf16[4,128,128]{2,1,0:T(8,128)(2,1)S(1)}) custom-call(s32[2]{0:T(128)S(1)} %pad_add_fusion.place_ref, f32[4,2,128,128]{3,2,1,0:T(8,128)S(1)} %get-tuple-element.47.own_ref, bf16[4,2,128,128]{3,2,1,0:T(8,128)(2,1)S(1)} %collective-permute-done.13.refs_0_, ...), custom_call_target="tpu_custom_call" | custom-call | tf_op jit(solution)/shard_map/sum_dk/pallas_call | solution.py:40
  57.1 0.4 collective-permute-start.15
  57.5 1.0 %collective-permute-done.15.other_ref = bf16[4,128,128]{2,1,0:T(8,128)(2,1)S(1)} collective-permute-done((bf16[4,128,128]{2,1,0:T(8,128)(2,1)S(1)}, bf16[4,128,128]{2,1,0:T(8,128)(2,1)S(1)}, u32[]{:S(2)}, u32[]{:S(2)}) %collective-permute-start.15) | collective-permute-done | bytes 131104 | tf_op jit(solution)/shard_map/ppermute | solution.py:27
  58.5 1.4 %merge_dk.1 = bf16[128,8,128]{2,1,0:T(8,128)(2,1)} custom-call(s32[2]{0:T(128)S(1)} %pad_add_fusion.place_ref, bf16[4,128,128]{2,1,0:T(8,128)(2,1)S(1)} %get-tuple-element.51.own_ref, bf16[4,128,128]{2,1,0:T(8,128)(2,1)S(1)} %collective-permute-done.15.other_ref), custom_call_target="tpu_custom_call" | custom-call | tf_op jit(solution)/shard_map/merge_dk/pallas_call | solution.py:40
  (17 shorter events, 0.0 us)
Async XLA Ops:
  0.6 3.2 %copy-start.1 = (bf16[128,32,128]{2,1,0:T(8,128)(2,1)S(1)}, bf16[128,32,128]{2,1,0:T(8,128)(2,1)}, u32[]{:S(2)}) copy-start(bf16[128,32,128]{2,1,0:T(8,128)(2,1)} %do_ref) | copy-start | bytes 3145732
  0.6 3.1 %copy-start = (bf16[128,32,128]{2,1,0:T(8,128)(2,1)S(1)}, bf16[128,32,128]{2,1,0:T(8,128)(2,1)}, u32[]{:S(2)}) copy-start(bf16[128,32,128]{2,1,0:T(8,128)(2,1)} %q_ref) | copy-start | bytes 3145732
  0.6 2.4 %collective-permute-start = (bf16[128,8,128]{2,1,0:T(8,128)(2,1)}, bf16[128,8,128]{2,1,0:T(8,128)(2,1)S(1)}, u32[]{:S(2)}, u32[]{:S(2)}) collective-permute-start(bf16[128,8,128]{2,1,0:T(8,128)(2,1)} %key_ref.1), channel_id=1, source_target_pairs={{0,1},{1,0},{2,3},{3,2},{4,5},{5,4},{6,7},{7,6},{8,9},{9,8},{10,11... | collective-permute-start | bytes 786440 | tf_op jit(solution)/shard_map/ppermute | solution.py:27
  3.7 12.1 %copy-start.2 = (s32[16]{0:T(128)S(1)}, s32[16]{0:T(128)}, u32[]{:S(2)}) copy-start(s32[16]{0:T(128)} %lengths_ref.1) | copy-start | bytes 196
  3.7 2.7 %collective-permute-start.1 = (bf16[128,32,128]{2,1,0:T(8,128)(2,1)S(1)}, bf16[128,32,128]{2,1,0:T(8,128)(2,1)S(1)}, u32[]{:S(2)}, u32[]{:S(2)}) collective-permute-start(bf16[128,32,128]{2,1,0:T(8,128)(2,1)S(1)} %copy-done), channel_id=1, source_target_pairs={{0,1},{1,0},{2,3},{3,2},{4,5},{5,4},{6,7},{7,6},{8,9},{9,8},{10,11... | collective-permute-start | bytes 3145736 | tf_op jit(solution)/shard_map/ppermute | solution.py:27
  3.9 4.1 %collective-permute-start.2 = (bf16[128,32,128]{2,1,0:T(8,128)(2,1)S(1)}, bf16[128,32,128]{2,1,0:T(8,128)(2,1)S(1)}, u32[]{:S(2)}, u32[]{:S(2)}) collective-permute-start(bf16[128,32,128]{2,1,0:T(8,128)(2,1)S(1)} %copy-done.1), channel_id=1, source_target_pairs={{0,1},{1,0},{2,3},{3,2},{4,5},{5,4},{6,7},{7,6},{8,9},{9,8},{10,11... | collective-permute-start | bytes 3145736 | tf_op jit(solution)/shard_map/ppermute | solution.py:27
  4.3 5.7 %collective-permute-start.3 = (bf16[128,8,128]{2,1,0:T(8,128)(2,1)S(1)}, bf16[128,8,128]{2,1,0:T(8,128)(2,1)S(1)}, u32[]{:S(2)}, u32[]{:S(2)}) collective-permute-start(bf16[128,8,128]{2,1,0:T(8,128)(2,1)S(1)} %get-tuple-element.36.own_ref), channel_id=1, source_target_pairs={{0,1},{1,0},{2,3},{3,2},{4,5},{5,4},{6,7},{7,6},{8,9},{9,8},{10,11... | collective-permute-start | bytes 786440 | tf_op jit(solution)/shard_map/ppermute | solution.py:27
  4.4 11.4 %collective-permute-start.5 = (bf16[4,2,128,128]{3,2,1,0:T(8,128)(2,1)S(1)}, bf16[4,2,128,128]{3,2,1,0:T(8,128)(2,1)S(1)}, u32[]{:S(2)}, u32[]{:S(2)}) collective-permute-start(bf16[4,2,128,128]{3,2,1,0:T(8,128)(2,1)S(1)} %pack_other.1.refs_0_), channel_id=1, source_target_pairs={{0,4},{1,5},{2,6},{3,7},{4,8},{5,9},{6,10},{7,11},{8,12},{9,13},{1... | collective-permute-start | bytes 786440 | tf_op jit(solution)/shard_map/ppermute | solution.py:22
  5.6 10.2 %collective-permute-start.4 = (bf16[4,2,128,128]{3,2,1,0:T(8,128)(2,1)S(1)}, bf16[4,2,128,128]{3,2,1,0:T(8,128)(2,1)S(1)}, u32[]{:S(2)}, u32[]{:S(2)}) collective-permute-start(bf16[4,2,128,128]{3,2,1,0:T(8,128)(2,1)S(1)} %pack_other.1.refs_0_), channel_id=1, source_target_pairs={{0,2},{1,3},{2,4},{3,5},{4,6},{5,7},{6,8},{7,9},{8,10},{9,11},{10,... | collective-permute-start | bytes 786440 | tf_op jit(solution)/shard_map/ppermute | solution.py:22
  10.7 19.6 %collective-permute-start.7 = (bf16[4,2,128,128]{3,2,1,0:T(8,128)(2,1)S(1)}, bf16[4,2,128,128]{3,2,1,0:T(8,128)(2,1)S(1)}, u32[]{:S(2)}, u32[]{:S(2)}) collective-permute-start(bf16[4,2,128,128]{3,2,1,0:T(8,128)(2,1)S(1)} %pack_both.1.refs_0_), channel_id=1, source_target_pairs={{0,4},{1,5},{2,6},{3,7},{4,8},{5,9},{6,10},{7,11},{8,12},{9,13},{1... | collective-permute-start | bytes 786440 | tf_op jit(solution)/shard_map/ppermute | solution.py:23
  13.9 16.5 %collective-permute-start.6 = (bf16[4,2,128,128]{3,2,1,0:T(8,128)(2,1)S(1)}, bf16[4,2,128,128]{3,2,1,0:T(8,128)(2,1)S(1)}, u32[]{:S(2)}, u32[]{:S(2)}) collective-permute-start(bf16[4,2,128,128]{3,2,1,0:T(8,128)(2,1)S(1)} %pack_both.1.refs_0_), channel_id=1, source_target_pairs={{0,2},{1,3},{2,4},{3,5},{4,6},{5,7},{6,8},{7,9},{8,10},{9,11},{10,... | collective-permute-start | bytes 786440 | tf_op jit(solution)/shard_map/ppermute | solution.py:23
  22.3 17.1 %collective-permute-start.8 = (bf16[4,2,128,128]{3,2,1,0:T(8,128)(2,1)S(1)}, bf16[4,2,128,128]{3,2,1,0:T(8,128)(2,1)S(1)}, u32[]{:S(2)}, u32[]{:S(2)}) collective-permute-start(bf16[4,2,128,128]{3,2,1,0:T(8,128)(2,1)S(1)} %get-tuple-element.39), channel_id=1, source_target_pairs={{0,30},{1,31},{2,0},{3,1},{4,2},{5,3},{6,4},{7,5},{8,6},{9,7},{10,... | collective-permute-start | bytes 786440 | tf_op jit(solution)/shard_map/ppermute | solution.py:22
  28.4 14.3 %collective-permute-start.9 = (bf16[4,2,128,128]{3,2,1,0:T(8,128)(2,1)S(1)}, bf16[4,2,128,128]{3,2,1,0:T(8,128)(2,1)S(1)}, u32[]{:S(2)}, u32[]{:S(2)}) collective-permute-start(bf16[4,2,128,128]{3,2,1,0:T(8,128)(2,1)S(1)} %get-tuple-element.40), channel_id=1, source_target_pairs={{4,0},{5,1},{6,2},{7,3},{8,4},{9,5},{10,6},{11,7},{12,8},{13,9},{1... | collective-permute-start | bytes 786440 | tf_op jit(solution)/shard_map/ppermute | solution.py:23
  35.9 20.5 %collective-permute-start.13 = (bf16[4,2,128,128]{3,2,1,0:T(8,128)(2,1)S(1)}, bf16[4,2,128,128]{3,2,1,0:T(8,128)(2,1)S(1)}, u32[]{:S(2)}, u32[]{:S(2)}) collective-permute-start(bf16[4,2,128,128]{3,2,1,0:T(8,128)(2,1)S(1)} %get-tuple-element.48), channel_id=1, source_target_pairs={{0,30},{1,31},{2,0},{3,1},{4,2},{5,3},{6,4},{7,5},{8,6},{9,7},{10,... | collective-permute-start | bytes 786440 | tf_op jit(solution)/shard_map/ppermute | solution.py:22
  37.5 18.9 %collective-permute-start.14 = (bf16[4,2,128,128]{3,2,1,0:T(8,128)(2,1)S(1)}, bf16[4,2,128,128]{3,2,1,0:T(8,128)(2,1)S(1)}, u32[]{:S(2)}, u32[]{:S(2)}) collective-permute-start(bf16[4,2,128,128]{3,2,1,0:T(8,128)(2,1)S(1)} %get-tuple-element.49), channel_id=1, source_target_pairs={{4,0},{5,1},{6,2},{7,3},{8,4},{9,5},{10,6},{11,7},{12,8},{13,9},{1... | collective-permute-start | bytes 786440 | tf_op jit(solution)/shard_map/ppermute | solution.py:23
  46.0 8.2 %collective-permute-start.10 = (bf16[56,16,128]{2,1,0:T(8,128)(2,1)S(1)}, bf16[56,16,128]{2,1,0:T(8,128)(2,1)S(1)}, u32[]{:S(2)}, u32[]{:S(2)}) collective-permute-start(bf16[56,16,128]{2,1,0:T(8,128)(2,1)S(1)} %get-tuple-element.43), channel_id=1, source_target_pairs={{0,1},{1,0},{2,3},{3,2},{4,5},{5,4},{6,7},{7,6},{8,9},{9,8},{10,11... | collective-permute-start | bytes 688136 | tf_op jit(solution)/shard_map/ppermute | solution.py:27
  52.4 1.8 %collective-permute-start.11 = (bf16[56,16,128]{2,1,0:T(8,128)(2,1)S(1)}, bf16[56,16,128]{2,1,0:T(8,128)(2,1)S(1)}, u32[]{:S(2)}, u32[]{:S(2)}) collective-permute-start(bf16[56,16,128]{2,1,0:T(8,128)(2,1)S(1)} %get-tuple-element.44), channel_id=1, source_target_pairs={{0,1},{1,0},{2,3},{3,2},{4,5},{5,4},{6,7},{7,6},{8,9},{9,8},{10,11... | collective-permute-start | bytes 688136 | tf_op jit(solution)/shard_map/ppermute | solution.py:27
  52.5 1.7 %collective-permute-start.12 = (bf16[48,16,128]{2,1,0:T(8,128)(2,1)S(1)}, bf16[48,16,128]{2,1,0:T(8,128)(2,1)S(1)}, u32[]{:S(2)}, u32[]{:S(2)}) collective-permute-start(bf16[48,16,128]{2,1,0:T(8,128)(2,1)S(1)} %get-tuple-element.45), channel_id=1, source_target_pairs={{0,1},{1,0},{2,3},{3,2},{4,5},{5,4},{6,7},{7,6},{8,9},{9,8},{10,11... | collective-permute-start | bytes 589832 | tf_op jit(solution)/shard_map/ppermute | solution.py:27
  57.1 1.4 %collective-permute-start.15 = (bf16[4,128,128]{2,1,0:T(8,128)(2,1)S(1)}, bf16[4,128,128]{2,1,0:T(8,128)(2,1)S(1)}, u32[]{:S(2)}, u32[]{:S(2)}) collective-permute-start(bf16[4,128,128]{2,1,0:T(8,128)(2,1)S(1)} %get-tuple-element.52), channel_id=1, source_target_pairs={{0,1},{1,0},{2,3},{3,2},{4,5},{5,4},{6,7},{7,6},{8,9},{9,8},{10,11... | collective-permute-start | bytes 393224 | tf_op jit(solution)/shard_map/ppermute | solution.py:27
